TPU v7x, 32 devices: a whole 2x2x4 slice. The times are simulated.
32 devices in a mesh: field: 2 (over x), row: 4 (over z), col: 4 (over y, core).
Axes of the slice: x: 2, y: 2, z: 4, core: 2. Of those that a mesh axis runs over, the one named last changes fastest.
Arguments:
- field: float32 [128, 128, 512], P(('field', 'row'), 'col'), parts along dimension 0, may hold values from -6 to 6
- w_expand: bfloat16 [512, 2048], replicated, may hold values from -0.25 to 0.25
- depth_kernel: float32 [3, 3, 2048], replicated, may hold values from -2 to 2
- w_project: bfloat16 [2048, 512], replicated, may hold values from -0.125 to 0.125
- w_qkv: bfloat16 [512, 1536], replicated, may hold values from -8 to 8
- w_out: bfloat16 [512, 512], replicated, may hold values from -0.25 to 0.25
Outputs:
- output: float32 [128, 128, 512], P(('field', 'row'), 'col'), parts along dimension 0
There are 2 independent parts, one for each index of `field`. A program takes and returns all parts, laid end to end along the dimension named above; an argument that names none is the same for every part. Nothing has to cross between parts.
All inputs are finite; a program needn't handle non-finite values.
Results may differ from a plain program's by a relative error of at most 0.006.
Values may be sent and summed in bfloat16 or wider, within the bound.
No kernel may reach another device: no remote copies, remote signals or barrier semaphores. Data moves between devices by JAX's collectives and lax.ppermute only.
A program may use at most 64 MiB of HBM per device.

v0:
```python
import math

import jax
import jax.numpy as jnp
from jax import lax
from jax.sharding import PartitionSpec as P

HEADS = 16
GRID = 16


def extended(block, sides, width):
    for axis, dim in sides:
        count = lax.axis_size(axis)
        forward = [(i, i + 1) for i in range(count - 1)]
        backward = [(target, source) for source, target in forward]
        low = lax.ppermute(
            lax.slice_in_dim(block, block.shape[dim] - width, None, axis=dim), axis, forward
        )
        high = lax.ppermute(lax.slice_in_dim(block, 0, width, axis=dim), axis, backward)
        block = jnp.concatenate([low, block, high], axis=dim)
    return block


def layer_norm(inputs):
    average = jnp.mean(inputs, axis=-1, keepdims=True)
    centred = inputs - average
    variance = jnp.mean(centred * centred, axis=-1, keepdims=True)
    return centred * lax.rsqrt(variance + 1e-05)


def depthwise(padded, kernel, tile_rows, tile_cols):
    summed = jnp.zeros((tile_rows, tile_cols, padded.shape[2]), jnp.float32)
    for offset_row in range(3):
        for offset_col in range(3):
            window = padded[
                offset_row : offset_row + tile_rows, offset_col : offset_col + tile_cols
            ].astype(jnp.float32)
            summed = summed + kernel[offset_row, offset_col] * window
    return summed


def attend(set_block):
    set_count, token_count, triple = set_block.shape
    channels = triple // 3
    head_width = channels // HEADS
    pieces = set_block.reshape(set_count, token_count, 3, HEADS, head_width)
    queries = pieces[:, :, 0]
    key_rows = pieces[:, :, 1]
    values = pieces[:, :, 2]
    scores = jnp.einsum(
        "snhd,smhd->shnm", queries, key_rows, preferred_element_type=jnp.float32
    ) * (1.0 / math.sqrt(head_width))
    row_max = jnp.max(scores, axis=-1, keepdims=True)
    raised = jnp.exp(scores - row_max)
    attn_weights = (raised / jnp.sum(raised, axis=-1, keepdims=True)).astype(jnp.bfloat16)
    attended = jnp.einsum(
        "shnm,smhd->snhd", attn_weights, values, preferred_element_type=jnp.float32
    )
    return attended.astype(jnp.bfloat16).reshape(set_count, token_count, channels)


def shards(field, w_expand, depth_kernel, w_project, w_qkv, w_out):
    tile_rows, tile_cols, channels = field.shape
    expand_width = w_expand.shape[1]
    normed = layer_norm(field).astype(jnp.bfloat16)
    expanded = jax.nn.gelu(
        jnp.dot(
            normed.reshape(tile_rows * tile_cols, channels),
            w_expand,
            preferred_element_type=jnp.float32,
        ),
        approximate=True,
    ).astype(jnp.bfloat16)
    expanded = expanded.reshape(tile_rows, tile_cols, expand_width)
    padded = extended(expanded, (("row", 0), ("col", 1)), 1)
    activated = jax.nn.gelu(
        depthwise(padded, depth_kernel, tile_rows, tile_cols), approximate=True
    ).astype(jnp.bfloat16)
    branch = jnp.dot(
        activated.reshape(tile_rows * tile_cols, expand_width),
        w_project,
        preferred_element_type=jnp.float32,
    )
    mixed = field + branch.reshape(tile_rows, tile_cols, channels)
    normed_two = layer_norm(mixed).astype(jnp.bfloat16)
    row_devices = lax.axis_size("row")
    col_devices = lax.axis_size("col")
    blocks_rows = GRID // row_devices
    blocks_cols = GRID // col_devices
    stride_rows = tile_rows // blocks_rows
    stride_cols = tile_cols // blocks_cols
    sets_total = stride_rows * stride_cols
    sets_local = sets_total // (row_devices * col_devices)
    members = blocks_rows * blocks_cols
    width_out = normed_two.shape[2]
    grouped = normed_two.reshape(
        blocks_rows, stride_rows, blocks_cols, stride_cols, width_out
    ).transpose(1, 3, 0, 2, 4)
    shaped = grouped.reshape(sets_total, 1, members, width_out)
    arrived = lax.all_to_all(shaped, ("row", "col"), split_axis=0, concat_axis=1, tiled=True)
    set_tokens = arrived.reshape(sets_local, row_devices * col_devices * members, width_out)
    projected = jnp.dot(set_tokens.reshape(-1, channels), w_qkv, preferred_element_type=jnp.float32)
    set_qkv = projected.astype(jnp.bfloat16).reshape(sets_local, -1, 3 * channels)
    attended = attend(set_qkv)
    leaving = attended.reshape(sets_local, row_devices * col_devices, members, channels)
    returned = lax.all_to_all(leaving, ("row", "col"), split_axis=1, concat_axis=0, tiled=True)
    restored = returned.reshape(
        stride_rows, stride_cols, blocks_rows, blocks_cols, channels
    ).transpose(2, 0, 3, 1, 4)
    restored = restored.reshape(tile_rows * tile_cols, channels)
    final = jnp.dot(restored, w_out, preferred_element_type=jnp.float32)
    return mixed + final.reshape(tile_rows, tile_cols, channels)


def solution(mesh):
    return jax.shard_map(
        shards,
        mesh=mesh,
        in_specs=(P(("field", "row"), "col", None), P(), P(), P(), P(), P()),
        out_specs=P(("field", "row"), "col", None),
        check_vma=False,
    )
```

profile of v0, /device:TPU:0, one launch (start us, length us, event | category | flops | bytes accessed | tf_op | source)
XLA Modules:
  0.0 114.1 jit_solution(10917877575753339104)
XLA Ops:
  0.0 1.5 %reduce_sum.45 = f32[16,32]{1,0:T(8,128)S(1)} reduce(f32[16,32,512]{2,1,0:T(8,128)} %param.6, f32[]{:T(128)} %constant.9.clone.1), dimensions={2}, to_apply=%region_0.0 | reduce | flops 261632 | bytes 1050628 | tf_op jit(solution)/shard_map/reduce_sum | solution.py:26
  1.5 1.5 %multiply_reduce_fusion.2 = f32[16,32]{1,0:T(8,128)S(1)} fusion(f32[16,32,512]{2,1,0:T(8,128)} %param.6, f32[16,32]{1,0:T(8,128)S(1)} %broadcast_multiply_fusion.1), kind=kLoop, calls=%fused_computation.40 | loop fusion | flops 785920 | bytes 1052672 | tf_op jit(solution)/shard_map/reduce_sum | solution.py:28
  3.0 1.4 %multiply_convert_fusion.1 = bf16[16,32,512]{2,1,0:T(8,128)(2,1)S(1)} fusion(f32[16,32,512]{2,1,0:T(8,128)} %param.6, f32[16,32]{1,0:T(8,128)S(1)} %add_rsqrt_fusion.1, f32[16,32]{1,0:T(8,128)S(1)} %broadcast_multiply_fusion.1), kind=kLoop, calls=%fused_computation.39 | loop fusion | flops 786432 | bytes 1576960 | tf_op jit(solution)/shard_map/convert_element_type | solution.py:66
  4.5 2.0 %fusion.11 = bf16[512,2048]{1,0:T(8,128)(2,1)S(1)} fusion(bf16[512,512]{1,0:T(8,128)(2,1)S(1)} %bitcast.87, bf16[512,2048]{1,0:T(8,128)(2,1)S(1)} %copy-done), kind=kOutput, calls=%fused_computation.14 | convolution fusion | flops 1083179008 | bytes 4718592 | tf_op jit(solution)/shard_map/dot_general | solution.py:68
  6.6 4.9 %collective-permute-start = (bf16[1,32,2048]{2,1,0:T(8,128)(2,1)S(1)}, bf16[1,32,2048]{2,1,0:T(8,128)(2,1)S(1)}, u32[]{:S(2)}, u32[]{:S(2)}) collective-permute-start(bf16[1,32,2048]{2,1,0:T(8,128)(2,1)S(1)} %get-tuple-element.9), channel_id=1, source_target_pairs={{0,4},{4,8},{8,12},{1,5},{5,9},{9,13},{2,6},{6,10},{10,14},{3,7},{... | collective-permute-start | bytes 393224 | tf_op jit(solution)/shard_map/ppermute | solution.py:17
  12.8 1.4 %collective-permute-done = bf16[1,32,2048]{2,1,0:T(8,128)(2,1)S(1)} collective-permute-done((bf16[1,32,2048]{2,1,0:T(8,128)(2,1)S(1)}, bf16[1,32,2048]{2,1,0:T(8,128)(2,1)S(1)}, u32[]{:S(2)}, u32[]{:S(2)}) %collective-permute-start) | collective-permute-done | bytes 131104 | tf_op jit(solution)/shard_map/ppermute | solution.py:17
  14.2 4.1 %collective-permute-done.1 = bf16[1,32,2048]{2,1,0:T(8,128)(2,1)S(1)} collective-permute-done((bf16[1,32,2048]{2,1,0:T(8,128)(2,1)S(1)}, bf16[1,32,2048]{2,1,0:T(8,128)(2,1)S(1)}, u32[]{:S(2)}, u32[]{:S(2)}) %collective-permute-start.1) | collective-permute-done | bytes 131104 | tf_op jit(solution)/shard_map/ppermute | solution.py:20
  18.6 1.3 %collective-permute-start.2 = (bf16[18,1,2048]{2,1,0:T(2,128)(2,1)S(1)}, bf16[18,1,2048]{2,1,0:T(2,128)(2,1)S(1)}, u32[]{:S(2)}, u32[]{:S(2)}) collective-permute-start(bf16[18,1,2048]{2,1,0:T(2,128)(2,1)S(1)} %get-tuple-element.7), channel_id=1, source_target_pairs={{0,1},{1,2},{2,3},{4,5},{5,6},{6,7},{8,9},{9,10},{10,11},{12,13},{... | collective-permute-start | bytes 221192 | tf_op jit(solution)/shard_map/ppermute | solution.py:17
  21.3 3.6 %collective-permute-done.3 = bf16[18,1,2048]{2,1,0:T(2,128)(2,1)S(1)} collective-permute-done((bf16[18,1,2048]{2,1,0:T(2,128)(2,1)S(1)}, bf16[18,1,2048]{2,1,0:T(2,128)(2,1)S(1)}, u32[]{:S(2)}, u32[]{:S(2)}) %collective-permute-start.3) | collective-permute-done | bytes 73760 | tf_op jit(solution)/shard_map/ppermute | solution.py:20
  24.9 2.8 %maximum_maximum_fusion = (bf16[18,33,2048]{2,1,0:T(8,128)(2,1)S(1)}, bf16[18,33,2048]{2,1,0:T(8,128)(2,1)S(1)}) fusion(bf16[1,32,2048]{2,1,0:T(8,128)(2,1)S(1)} %collective-permute-done.1, bf16[16,32,2048]{2,1,0:T(8,128)(2,1)S(1)} %bitcast.79, bf16[1,32,2048]{2,1,0:T(8,128)(2,1)S(1)} %collective-permute-done, ...), kind=kLoop, calls=%fused_computation.26 | loop fusion | flops 19464192 | bytes 7372800 | tf_op jit(solution)/shard_map/concatenate | solution.py:21
  27.8 5.9 %fusion.44 = (f32[16,32]{1,0:T(8,128)S(1)}, f32[16,32,512]{2,1,0:T(8,128)S(1)}) fusion(f32[16,32,512]{2,1,0:T(8,128)S(1)} %copy-done.1, bf16[2048,512]{1,0:T(8,128)(2,1)S(1)} %copy-done.3, bf16[16,32,2048]{2,1,0:T(8,128)(2,1)S(1)} %bitcast.80, bf16[18,33,2048]{2,1,0:T(8,128)(2,1)S(1)} %get-tuple-element.6, ...), kind=kOutput, calls=%fused_computation.63 | convolution fusion | flops 1113062912 | bytes 19212288 | tf_op jit(solution)/shard_map/dot_general | solution.py:80
  34.5 21.5 %all_to_all.30 = bf16[32,1,16,512]{3,2,1,0:T(8,128)(2,1)S(1)} all-to-all(bf16[32,1,16,512]{3,2,1,0:T(8,128)(2,1)S(1)} %copy.32), channel_id=1, replica_groups=mesh['field'=2,'row'=4,'col'=4] {'row','col'}, dimensions={0} | all-to-all | bytes 1048576 | tf_op jit(solution)/shard_map/all_to_all | solution.py:101
  56.1 2.1 %convolution_convert_fusion = bf16[512,1536]{1,0:T(8,128)(2,1)} fusion(bf16[512,512]{1,0:T(8,128)(2,1)S(1)} %bitcast.88, bf16[512,1536]{1,0:T(8,128)(2,1)S(1)} %copy-done.4), kind=kOutput, calls=%fused_computation.25 | convolution fusion | flops 806092800 | bytes 3670016 | tf_op jit(solution)/shard_map/dot_general | solution.py:103
  58.2 2.6 %copy.34 = bf16[512,1536]{0,1:T(8,128)(2,1)} copy(bf16[512,1536]{1,0:T(8,128)(2,1)} %convolution_convert_fusion) | data formatting | bytes 3145728 | tf_op jit(solution)/shard_map/convert_element_type | solution.py:104
  60.9 3.5 %reshape_reshape.10 = bf16[2,256,3,16,32]{1,0,4,3,2:T(2,128)(2,1)} reshape(bf16[512,1536]{0,1:T(8,128)(2,1)} %copy.34) | data formatting | bytes 3145728 | tf_op jit(solution)/shard_map/reshape;reshape | solution.py:47
  64.4 4.0 %fusion.42 = (bf16[2,256,1,16,32]{1,0,4,3,2:T(2,128)(2,1)}, bf16[2,256,1,16,32]{1,0,4,3,2:T(2,128)(2,1)}, bf16[2,256,1,16,32]{1,0,4,3,2:T(2,128)(2,1)}) fusion(bf16[2,256,3,16,32]{1,0,4,3,2:T(2,128)(2,1)} %reshape_reshape.10), kind=kLoop, calls=%fused_computation.61 | loop fusion | bytes 3145728 | tf_op jit(solution)/shard_map/slice | solution.py:50
  68.4 7.4 %fusion.45 = (f32[2,16,256]{2,1,0:T(8,128)S(1)}, f32[2,16,256,256]{2,3,1,0:T(8,128)}) fusion(bf16[2,256,1,16,32]{1,0,4,3,2:T(2,128)(2,1)} %get-tuple-element.12, bf16[2,256,1,16,32]{1,0,4,3,2:T(2,128)(2,1)} %get-tuple-element.13), kind=kOutput, calls=%fused_computation.64 | convolution fusion | flops 140509440 | bytes 9469952 | tf_op jit(solution)/shard_map/sub | solution.py:55
  75.8 5.2 %fusion.33 = bf16[2,256,16,32]{1,3,2,0:T(8,128)(2,1)} fusion(f32[2,16,256,256]{2,3,1,0:T(8,128)} %get-tuple-element.26, f32[2,16,256]{2,1,0:T(8,128)S(1)} %get-tuple-element.25, bf16[2,256,1,16,32]{1,0,4,3,2:T(2,128)(2,1)} %get-tuple-element.11), kind=kOutput, calls=%fused_computation.36 | convolution fusion | flops 138674176 | bytes 9469952 | tf_op jit(solution)/shard_map/shnm,smhd->snhd/dot_general | solution.py:57
  81.0 3.8 %copy.39 = bf16[2,256,16,32]{3,2,1,0:T(8,128)(2,1)} copy(bf16[2,256,16,32]{1,3,2,0:T(8,128)(2,1)} %fusion.33) | data formatting | bytes 1048576 | tf_op jit(solution)/shard_map/convert_element_type | solution.py:60
  84.7 4.1 %reshape_reshape.11 = bf16[2,16,16,512]{3,2,1,0:T(8,128)(2,1)} reshape(bf16[2,256,16,32]{3,2,1,0:T(8,128)(2,1)} %copy.39) | data formatting | bytes 1048576 | tf_op jit(solution)/shard_map/reshape;reshape | solution.py:106
  89.9 18.5 %all_to_all.31 = bf16[2,16,16,512]{3,2,0,1:T(8,128)(2,1)} all-to-all(bf16[2,16,16,512]{3,2,0,1:T(8,128)(2,1)S(1)} %copy.40), channel_id=1, replica_groups=mesh['field'=2,'row'=4,'col'=4] {'row','col'}, dimensions={1} | all-to-all | bytes 1048576 | tf_op jit(solution)/shard_map/all_to_all | solution.py:107
  108.4 2.0 %reshape.57 = bf16[4,8,4,4,512]{4,3,2,1,0:T(4,128)(2,1)} reshape(bf16[16,2,1,16,512]{4,3,1,0,2:T(8,128)(2,1)} %bitcast.84) | data formatting | bytes 1048576 | tf_op jit(solution)/shard_map/reshape | solution.py:108
  110.3 1.3 %copy.41 = bf16[4,4,4,8,512]{4,3,2,1,0:T(8,128)(2,1)S(1)} copy(bf16[4,4,4,8,512]{4,2,0,3,1:T(4,128)(2,1)} %bitcast.85) | data formatting | bytes 1048576 | tf_op jit(solution)/shard_map/transpose | solution.py:110
  111.7 2.5 %convolution_add_fusion = f32[16,32,512]{2,1,0:T(8,128)} fusion(f32[16,32,512]{2,1,0:T(8,128)S(1)} %get-tuple-element.24, bf16[16,32,512]{2,1,0:T(8,128)(2,1)S(1)} %bitcast.86, bf16[512,512]{1,0:T(8,128)(2,1)} %param.11), kind=kOutput, calls=%fused_computation.33 | convolution fusion | flops 268697600 | bytes 3145728 | tf_op jit(solution)/shard_map/dot_general | solution.py:112
  (26 shorter events, 4.9 us)
Async XLA Ops:
  0.0 4.5 %copy-start = (bf16[512,2048]{1,0:T(8,128)(2,1)S(1)}, bf16[512,2048]{1,0:T(8,128)(2,1)}, u32[]{:S(2)}) copy-start(bf16[512,2048]{1,0:T(8,128)(2,1)} %param.7) | copy-start | bytes 6291460
  4.5 16.7 %copy-start.2 = (f32[3,3,2048]{2,1,0:T(4,128)S(1)}, f32[3,3,2048]{2,1,0:T(4,128)}, u32[]{:S(2)}) copy-start(f32[3,3,2048]{2,1,0:T(4,128)} %param.8) | copy-start | bytes 221188
  6.6 7.7 %collective-permute-start = (bf16[1,32,2048]{2,1,0:T(8,128)(2,1)S(1)}, bf16[1,32,2048]{2,1,0:T(8,128)(2,1)S(1)}, u32[]{:S(2)}, u32[]{:S(2)}) collective-permute-start(bf16[1,32,2048]{2,1,0:T(8,128)(2,1)S(1)} %get-tuple-element.9), channel_id=1, source_target_pairs={{0,4},{4,8},{8,12},{1,5},{5,9},{9,13},{2,6},{6,10},{10,14},{3,7},{... | collective-permute-start | bytes 393224 | tf_op jit(solution)/shard_map/ppermute | solution.py:17
  11.5 6.9 %collective-permute-start.1 = (bf16[1,32,2048]{2,1,0:T(8,128)(2,1)S(1)}, bf16[1,32,2048]{2,1,0:T(8,128)(2,1)S(1)}, u32[]{:S(2)}, u32[]{:S(2)}) collective-permute-start(bf16[1,32,2048]{2,1,0:T(8,128)(2,1)S(1)} %get-tuple-element.10), channel_id=1, source_target_pairs={{4,0},{8,4},{12,8},{5,1},{9,5},{13,9},{6,2},{10,6},{14,10},{7,3},{... | collective-permute-start | bytes 393224 | tf_op jit(solution)/shard_map/ppermute | solution.py:20
  18.6 2.7 %collective-permute-start.2 = (bf16[18,1,2048]{2,1,0:T(2,128)(2,1)S(1)}, bf16[18,1,2048]{2,1,0:T(2,128)(2,1)S(1)}, u32[]{:S(2)}, u32[]{:S(2)}) collective-permute-start(bf16[18,1,2048]{2,1,0:T(2,128)(2,1)S(1)} %get-tuple-element.7), channel_id=1, source_target_pairs={{0,1},{1,2},{2,3},{4,5},{5,6},{6,7},{8,9},{9,10},{10,11},{12,13},{... | collective-permute-start | bytes 221192 | tf_op jit(solution)/shard_map/ppermute | solution.py:17
  19.9 5.0 %collective-permute-start.3 = (bf16[18,1,2048]{2,1,0:T(2,128)(2,1)S(1)}, bf16[18,1,2048]{2,1,0:T(2,128)(2,1)S(1)}, u32[]{:S(2)}, u32[]{:S(2)}) collective-permute-start(bf16[18,1,2048]{2,1,0:T(2,128)(2,1)S(1)} %get-tuple-element.8), channel_id=1, source_target_pairs={{1,0},{2,1},{3,2},{5,4},{6,5},{7,6},{9,8},{10,9},{11,10},{13,12},{... | collective-permute-start | bytes 221192 | tf_op jit(solution)/shard_map/ppermute | solution.py:20
  21.3 6.5 %copy-start.1 = (f32[16,32,512]{2,1,0:T(8,128)S(1)}, f32[16,32,512]{2,1,0:T(8,128)}, u32[]{:S(2)}) copy-start(f32[16,32,512]{2,1,0:T(8,128)} %param.6) | copy-start | bytes 3145732
  21.3 6.5 %copy-start.3 = (bf16[2048,512]{1,0:T(8,128)(2,1)S(1)}, bf16[2048,512]{1,0:T(8,128)(2,1)}, u32[]{:S(2)}) copy-start(bf16[2048,512]{1,0:T(8,128)(2,1)} %param.9) | copy-start | bytes 6291460
  33.7 22.4 %copy-start.4 = (bf16[512,1536]{1,0:T(8,128)(2,1)S(1)}, bf16[512,1536]{1,0:T(8,128)(2,1)}, u32[]{:S(2)}) copy-start(bf16[512,1536]{1,0:T(8,128)(2,1)} %param.10) | copy-start | bytes 4718596
where the time goes:
time: 115 us; the launch traced here: 114 us
  blocking collectives  40 us (35%)
  matrix products  25.1 us (22%)
  local copies, waits for them, and re-layouts  22.8 us (20%)
  waiting for transfers between devices  9.17 us (8%)
  starting transfers between devices  8.82 us (8%)
  other arithmetic  7.97 us (7%)
    all_to_all x1, blocking collectives, shards(): lax.all_to_all(shaped, ('row', 'col'), split_axis=0, concat_axis=1, tiled...  21.5 us
    all_to_all x1, blocking collectives, shards(): lax.all_to_all(leaving, ('row', 'col'), split_axis=1, concat_axis=0, tile...  18.5 us
    ppermute x2, waiting for transfers between devices, extended(): lax.ppermute(lax.slice_in_dim(block, 0, width, axis=dim), axis, backward)  7.73 us
    sub x1, matrix products, attend(): raised = jnp.exp(scores - row_max)  7.35 us
    ppermute x2, starting transfers between devices, extended(): lax.ppermute(lax.slice_in_dim(block, block.shape[dim] - width, None, axis...  6.24 us
    dot_general x1, matrix products, shards(): jnp.dot(activated.reshape(tile_rows * tile_cols, expand_width), w_project...  5.9 us
    dot_general x1, matrix products, attend(): jnp.einsum('shnm,smhd->snhd', attn_weights, values, preferred_element_typ...  5.21 us
    another operation x2, local copies, waits for them, and re-layouts, shards(): attended.reshape(sets_local, row_devices * col_devices, members, channels)  5.16 us
  transfers between devices with their start and end apart: 4, of which 3 were waited for; matrix products, arithmetic and copies ran while one was open for 0% of the time, Pallas kernels for 0%

commit v1 on v0

v1 whole, which is shorter than its diff:
```python
import functools
import math

import jax
import jax.numpy as jnp
import numpy as np
from jax import lax
from jax.experimental import pallas as pl
from jax.experimental.pallas import tpu as pltpu
from jax.sharding import PartitionSpec as P

HEADS = 16
GRID = 16
LANES = 128
MIB = 1024 * 1024
NT = (((1,), (1,)), ((), ()))


def layer_norm(inputs):
    average = jnp.mean(inputs, axis=-1, keepdims=True)
    centred = inputs - average
    variance = jnp.mean(centred * centred, axis=-1, keepdims=True)
    return centred * lax.rsqrt(variance + 1e-05)


def gelu(x):
    scale = math.sqrt(2.0 / math.pi)
    half = 0.5 * x
    return half + half * jnp.tanh(x * (scale + (scale * 0.044715) * (x * x)))


def matmul(a, b):
    return jnp.dot(a, b, preferred_element_type=jnp.float32)


def matmul_nt(a, b):
    return lax.dot_general(a, b, NT, preferred_element_type=jnp.float32)


def divisor(size, most, unit):
    best = size
    for piece in range(unit, most + 1, unit):
        if size % piece == 0:
            best = piece
    return best


def expand_kernel(field_ref, weight_ref, out_ref, normed_ref):
    @pl.when(pl.program_id(0) == 0)
    def _():
        normed_ref[...] = layer_norm(field_ref[...]).astype(jnp.bfloat16)

    tokens = out_ref.shape[0]
    step = divisor(tokens, 128, 16)
    for start in range(0, tokens, step):
        rows = slice(start, start + step)
        out_ref[rows, :] = gelu(matmul(normed_ref[rows, :], weight_ref[...])).astype(jnp.bfloat16)


def expand(field, w_expand):
    tokens, channels = field.shape
    width = w_expand.shape[1]
    tile = divisor(width, 512, LANES)
    return pl.pallas_call(
        expand_kernel,
        grid=(width // tile,),
        in_specs=[
            pl.BlockSpec((tokens, channels), lambda j: (0, 0)),
            pl.BlockSpec((channels, tile), lambda j: (0, j)),
        ],
        out_specs=pl.BlockSpec((tokens, tile), lambda j: (0, j)),
        out_shape=jax.ShapeDtypeStruct((tokens, width), jnp.bfloat16),
        scratch_shapes=[pltpu.VMEM((tokens, channels), jnp.bfloat16)],
        compiler_params=pltpu.CompilerParams(vmem_limit_bytes=24 * MIB),
        cost_estimate=pl.CostEstimate(
            flops=2 * tokens * channels * width,
            bytes_accessed=tokens * channels * 4 + channels * width * 2 + tokens * width * 2,
            transcendentals=tokens * width,
        ),
        name="expand",
    )(field, w_expand)


def round_up(size, unit):
    return -(-size // unit) * unit


def mix_kernel(
    expanded_ref, field_ref, up_ref, down_ref, left_ref, right_ref, w_expand_ref, depth_ref,
    w_project_ref, perm_ref, mixed_ref, grouped_ref, halo_ref, total_ref, *, rows, cols,
):
    step = pl.program_id(0)
    tile = expanded_ref.shape[1]
    slot = round_up(rows + 2, 16)

    @pl.when(step == 0)
    def _():
        halo_ref[...] = jnp.zeros_like(halo_ref)
        halo_ref[:cols, :] = layer_norm(up_ref[...]).astype(jnp.bfloat16)
        halo_ref[cols : 2 * cols, :] = layer_norm(down_ref[...]).astype(jnp.bfloat16)
        for index, ref in ((0, left_ref), (1, right_ref)):
            strip = layer_norm(ref[...])
            strip = jnp.concatenate(
                [strip, jnp.zeros((slot - rows - 2, strip.shape[1]), jnp.float32)], axis=0
            )
            start = 2 * cols + index * slot
            halo_ref[start : start + slot, :] = strip.astype(jnp.bfloat16)
        total_ref[...] = jnp.zeros_like(total_ref)

    halo = gelu(matmul(halo_ref[...], w_expand_ref[...])).astype(jnp.bfloat16).astype(jnp.float32)
    position = lax.broadcasted_iota(jnp.int32, (cols, LANES), 0)
    at_first = position == 0
    at_last = position == cols - 1
    half = rows // 2
    parts = [[], []]
    for chunk in range(tile // LANES):
        lanes = slice(chunk * LANES, (chunk + 1) * LANES)
        taps = [[depth_ref[p, q : q + 1, lanes] for q in range(3)] for p in range(3)]
        sides = []
        for q, start in ((0, 2 * cols), (2, 2 * cols + slot)):
            sides.append(
                sum(taps[p][q] * halo[start + p : start + p + rows, lanes] for p in range(3))
            )

        def row_of(y):
            if y < 0:
                return halo[:cols, lanes]
            if y == rows:
                return halo[cols : 2 * cols, lanes]
            return expanded_ref[y * cols : (y + 1) * cols, lanes].astype(jnp.float32)

        window = [row_of(-1), row_of(0), None]
        made = []
        for y in range(rows):
            window[2] = row_of(y + 1)
            summed = [
                taps[0][q] * window[0] + taps[1][q] * window[1] + taps[2][q] * window[2]
                for q in range(3)
            ]
            before = jnp.where(at_first, sides[0][y : y + 1], pltpu.roll(summed[0], 1, 0))
            after = jnp.where(at_last, sides[1][y : y + 1], pltpu.roll(summed[2], cols - 1, 0))
            made.append(gelu(before + summed[1] + after).astype(jnp.bfloat16))
            window = [window[1], window[2], None]
        for index in range(2):
            parts[index].append(jnp.concatenate(made[index * half : (index + 1) * half], axis=0))
    for index in range(2):
        place = slice(index * half * cols, (index + 1) * half * cols)
        total_ref[place, :] += matmul(jnp.concatenate(parts[index], axis=1), w_project_ref[...])

    @pl.when(step == pl.num_programs(0) - 1)
    def _():
        mixed = field_ref[...] + total_ref[...]
        mixed_ref[...] = mixed
        normed = layer_norm(mixed).astype(jnp.bfloat16)
        grouped_ref[...] = matmul(perm_ref[...], normed).astype(jnp.bfloat16)


def mix(expanded, field, up, down, left, right, w_expand, depth_kernel, w_project, perm, rows, cols):
    tokens, channels = field.shape
    width = expanded.shape[1]
    tile = divisor(width, 256, LANES)
    slot = round_up(rows + 2, 16)

    def whole(array):
        return pl.BlockSpec(array.shape, lambda j: (0,) * array.ndim)

    return pl.pallas_call(
        functools.partial(mix_kernel, rows=rows, cols=cols),
        grid=(width // tile,),
        in_specs=[
            pl.BlockSpec((tokens, tile), lambda j: (0, j)),
            whole(field),
            whole(up),
            whole(down),
            whole(left),
            whole(right),
            pl.BlockSpec((channels, tile), lambda j: (0, j)),
            pl.BlockSpec((3, 3, tile), lambda j: (0, 0, j)),
            pl.BlockSpec((tile, channels), lambda j: (j, 0)),
            whole(perm),
        ],
        out_specs=[
            pl.BlockSpec((tokens, channels), lambda j: (0, 0)),
            pl.BlockSpec((tokens, channels), lambda j: (0, 0)),
        ],
        out_shape=[
            jax.ShapeDtypeStruct((tokens, channels), jnp.float32),
            jax.ShapeDtypeStruct((tokens, channels), jnp.bfloat16),
        ],
        scratch_shapes=[
            pltpu.VMEM((2 * cols + 2 * slot, channels), jnp.bfloat16),
            pltpu.VMEM((tokens, channels), jnp.float32),
        ],
        compiler_params=pltpu.CompilerParams(vmem_limit_bytes=32 * MIB),
        cost_estimate=pl.CostEstimate(
            flops=2 * tokens * channels * width,
            bytes_accessed=tokens * channels * 10 + 4 * channels * width + tokens * width * 2,
            transcendentals=tokens * width,
        ),
        name="mix",
    )(expanded, field, up, down, left, right, w_expand, depth_kernel, w_project, perm)


def identity(size):
    row = lax.broadcasted_iota(jnp.int32, (size, size), 0)
    column = lax.broadcasted_iota(jnp.int32, (size, size), 1)
    return jnp.where(row == column, 1.0, 0.0).astype(jnp.bfloat16)


def attend_kernel(tokens_ref, weight_ref, out_ref):
    devices, sets, members, channels = tokens_ref.shape
    count = devices * members
    head_width = channels // HEADS
    group_heads = LANES // head_width
    factor = math.log2(math.e) / math.sqrt(head_width)
    lane = lax.broadcasted_iota(jnp.int32, (1, LANES), 1)
    masks = [
        jnp.where((lane >= j * head_width) & (lane < (j + 1) * head_width), 1.0, 0.0).astype(
            jnp.bfloat16
        )
        for j in range(group_heads)
    ]
    ones = jnp.ones((16, count), jnp.bfloat16)
    turn_values = identity(channels)
    turn_tokens = identity(count)
    for s in range(sets):
        block = tokens_ref[:, s].reshape(count, channels)
        qkv = matmul(block, weight_ref[...]).astype(jnp.bfloat16)
        values = matmul_nt(turn_values, qkv[:, 2 * channels :]).astype(jnp.bfloat16)
        heads = []
        for group in range(channels // LANES):
            lanes = slice(group * LANES, (group + 1) * LANES)
            queries = qkv[:, lanes]
            keys = qkv[:, channels + group * LANES : channels + (group + 1) * LANES]
            for j in range(group_heads):
                scores = matmul_nt(keys * masks[j], queries)
                highest = jnp.max(scores, axis=0, keepdims=True)
                raised = jnp.exp2((scores - highest) * factor).astype(jnp.bfloat16)
                head = (group * group_heads + j) * head_width
                left = jnp.concatenate([values[head : head + head_width], ones], axis=0)
                product = matmul(left, raised)
                scale = 1.0 / product[head_width : head_width + 1]
                heads.append((product[:head_width] * scale).astype(jnp.bfloat16))
        turned = jnp.concatenate(heads, axis=0)
        attended = matmul_nt(turn_tokens, turned).astype(jnp.bfloat16)
        out_ref[:, s] = attended.reshape(devices, members, channels)


def attend(blocks, w_qkv):
    devices, sets, members, channels = blocks.shape
    apart = members % 16 != 0
    if apart:
        count = devices * members
        blocks = blocks.transpose(1, 0, 2, 3).reshape(1, sets, count, channels)
    whole = pl.BlockSpec(blocks.shape, lambda: (0, 0, 0, 0))
    count = devices * members
    result = pl.pallas_call(
        attend_kernel,
        in_specs=[whole, pl.BlockSpec(w_qkv.shape, lambda: (0, 0))],
        out_specs=whole,
        out_shape=jax.ShapeDtypeStruct(blocks.shape, jnp.bfloat16),
        compiler_params=pltpu.CompilerParams(vmem_limit_bytes=32 * MIB),
        cost_estimate=pl.CostEstimate(
            flops=sets * (2 * count * channels * channels * 3 + 4 * count * count * channels),
            bytes_accessed=4 * sets * count * channels + 6 * channels * channels,
            transcendentals=sets * HEADS * count * count,
        ),
        name="attend",
    )(blocks, w_qkv)
    if apart:
        result = result.reshape(sets, devices, members, channels).transpose(1, 0, 2, 3)
    return result


def finish_kernel(attended_ref, back_ref, weight_ref, mixed_ref, out_ref):
    restored = matmul(back_ref[...], attended_ref[...]).astype(jnp.bfloat16)
    out_ref[...] = mixed_ref[...] + matmul(restored, weight_ref[...])


def finish(attended, back, w_out, mixed):
    tokens, channels = mixed.shape
    step = divisor(tokens, 128, 16)
    return pl.pallas_call(
        finish_kernel,
        grid=(tokens // step,),
        in_specs=[
            pl.BlockSpec((tokens, channels), lambda i: (0, 0)),
            pl.BlockSpec((step, tokens), lambda i: (i, 0)),
            pl.BlockSpec(w_out.shape, lambda i: (0, 0)),
            pl.BlockSpec((step, channels), lambda i: (i, 0)),
        ],
        out_specs=pl.BlockSpec((step, channels), lambda i: (i, 0)),
        out_shape=jax.ShapeDtypeStruct((tokens, channels), jnp.float32),
        compiler_params=pltpu.CompilerParams(vmem_limit_bytes=24 * MIB),
        name="finish",
    )(attended, back, w_out, mixed)


def exchange(low_edge, high_edge, axis):
    count = lax.axis_size(axis)
    forward = [(i, i + 1) for i in range(count - 1)]
    backward = [(target, source) for source, target in forward]
    return lax.ppermute(high_edge, axis, forward), lax.ppermute(low_edge, axis, backward)


def grouping(rows, cols, blocks_rows, blocks_cols):
    order = np.arange(rows * cols).reshape(
        blocks_rows, rows // blocks_rows, blocks_cols, cols // blocks_cols
    )
    order = order.transpose(1, 3, 0, 2).reshape(-1)
    matrix = np.zeros((order.size, order.size), np.float32)
    matrix[np.arange(order.size), order] = 1.0
    return matrix


def shards(field, w_expand, depth_kernel, w_project, w_qkv, w_out):
    rows, cols, channels = field.shape
    tokens = rows * cols
    row_devices = lax.axis_size("row")
    col_devices = lax.axis_size("col")
    devices = row_devices * col_devices
    blocks_rows = GRID // row_devices
    blocks_cols = GRID // col_devices
    members = blocks_rows * blocks_cols
    sets_local = tokens // members // devices
    matrix = grouping(rows, cols, blocks_rows, blocks_cols)
    perm = jnp.asarray(matrix, jnp.bfloat16)
    back = jnp.asarray(matrix.T, jnp.bfloat16)

    flat = field.reshape(tokens, channels)
    up, down = exchange(field[0], field[rows - 1], "row")
    expanded = expand(flat, w_expand)
    first = jnp.concatenate([up[:1], field[:, 0], down[:1]], axis=0)
    last = jnp.concatenate([up[cols - 1 :], field[:, cols - 1], down[cols - 1 :]], axis=0)
    left, right = exchange(first, last, "col")
    mixed, grouped = mix(
        expanded, flat, up, down, left, right, w_expand, depth_kernel, w_project, perm, rows, cols
    )
    arrived = lax.all_to_all(
        grouped.reshape(devices, sets_local * members, channels), ("row", "col"), 0, 0, tiled=True
    )
    attended = attend(arrived.reshape(devices, sets_local, members, channels), w_qkv)
    returned = lax.all_to_all(
        attended.reshape(devices, sets_local * members, channels), ("row", "col"), 0, 0, tiled=True
    )
    final = finish(returned.reshape(tokens, channels), back, w_out, mixed)
    return final.reshape(rows, cols, channels)


def solution(mesh):
    return jax.shard_map(
        shards,
        mesh=mesh,
        in_specs=(P(("field", "row"), "col", None), P(), P(), P(), P(), P()),
        out_specs=P(("field", "row"), "col", None),
        check_vma=False,
    )
```

time: 115 us -> 83.1 us (0.72)
  matrix products: 25.1 us -> 0 us
  Pallas kernels: 0 us -> 24.6 us
  local copies, waits for them, and re-layouts: 22.8 us -> 4.89 us
  waiting for transfers between devices: 9.17 us -> 0.76 us
  other arithmetic: 7.97 us -> 0.02 us
  blocking collectives: 40 us -> 42.8 us
    pallas_call x0 -> x4, Pallas kernels: none -> 24.6 us  [the longest x1 9.94 us: attend(): pl.pallas_call(attend_kernel, in_specs=[whole, pl.BlockSpec(w_qkv.shape,...]
    dot_general x5 -> x0, matrix products: 17.7 us -> none  [the longest x1 5.9 us: shards(): jnp.dot(activated.reshape(tile_rows * tile_cols, expand_width), w_project...]
    another operation x3 -> x0, local copies, waits for them, and re-layouts: 8.68 us -> none  [the longest x2 5.16 us: shards(): attended.reshape(sets_local, row_devices * col_devices, members, channels)]
    ppermute x4, waiting for transfers between devices: 9.17 us -> 0.76 us  [the longest x2 0.75 us: exchange(): lax.ppermute(high_edge, axis, forward)]
    sub x1 -> x0, matrix products: 7.35 us -> none  [attend(): raised = jnp.exp(scores - row_max)]
    convert_element_type x2 -> x0, local copies, waits for them, and re-layouts: 6.36 us -> none  [the longest x1 3.76 us: attend(): attended.astype(jnp.bfloat16).reshape(set_count, token_count, channels)]
    reduce_sum x3 -> x0, other arithmetic: 3.27 us -> none  [the longest x2 1.76 us: layer_norm(): variance = jnp.mean(centred * centred, axis=-1, keepdims=True)]
    slice x3, local copies, waits for them, and re-layouts: 4.11 us -> 1.1 us  [shards(): first = jnp.concatenate([up[:1], field[:, 0], down[:1]], axis=0)]
  transfers between devices with their start and end apart: 4 -> 4, of which waited for: 3 -> 1; matrix products, arithmetic and copies ran while one was open for 0% -> 1% of each run, Pallas kernels for 0% -> 3%
where the time goes in v1:
time: 83.1 us; the launch traced here: 82.8 us
  blocking collectives  42.8 us (52%)
  Pallas kernels  24.6 us (30%)
  starting transfers between devices  9.57 us (12%)
  local copies, waits for them, and re-layouts  4.89 us (6%)
    all_to_all x1, blocking collectives, shards(): lax.all_to_all(grouped.reshape(devices, sets_local * members, channels),...  24.4 us
    all_to_all x1, blocking collectives, shards(): lax.all_to_all(attended.reshape(devices, sets_local * members, channels),...  18.4 us
    pallas_call x1, Pallas kernels, attend(): pl.pallas_call(attend_kernel, in_specs=[whole, pl.BlockSpec(w_qkv.shape,...  9.94 us
    pallas_call x1, Pallas kernels, mix(): pl.pallas_call(functools.partial(mix_kernel, rows=rows, cols=cols), grid=...  9.34 us
    ppermute x2, starting transfers between devices, exchange(): lax.ppermute(high_edge, axis, forward)  6.98 us
    unnamed x22, local copies, waits for them, and re-layouts  2.85 us
    pallas_call x1, Pallas kernels, expand(): pl.pallas_call(expand_kernel, grid=(width // tile,), in_specs=[pl.BlockSp...  2.66 us
    pallas_call x1, Pallas kernels, finish(): pl.pallas_call(finish_kernel, grid=(tokens // step,), in_specs=[pl.BlockS...  2.63 us
  transfers between devices with their start and end apart: 4, of which 1 were waited for; matrix products, arithmetic and copies ran while one was open for 1% of the time, Pallas kernels for 3%

profile of v1, /device:TPU:0, one launch (start us, length us, event | category | flops | bytes accessed | tf_op | source)
XLA Modules:
  0.0 82.8 jit_solution(20762458546001190)
XLA Ops:
  0.0 0.9 %slice_bitcast_fusion = (f32[32,512]{1,0:T(8,128)S(1)}, f32[32,512]{1,0:T(8,128)S(1)}) fusion(f32[16,32,512]{2,1,0:T(8,128)} %param.8), kind=kLoop, calls=%fused_computation | loop fusion | bytes 262144 | tf_op jit(solution)/shard_map/squeeze | solution.py:331
  0.9 1.3 %collective-permute-start.1 = (f32[32,512]{1,0:T(8,128)S(1)}, f32[32,512]{1,0:T(8,128)S(1)}, u32[]{:S(2)}, u32[]{:S(2)}) collective-permute-start(f32[32,512]{1,0:T(8,128)S(1)} %get-tuple-element.11), channel_id=1, source_target_pairs={{4,0},{8,4},{12,8},{5,1},{9,5},{13,9},{6,2},{10,6},{14,10},{7,3},{... | collective-permute-start | bytes 196616 | tf_op jit(solution)/shard_map/ppermute | solution.py:303
  2.2 5.6 %collective-permute-start = (f32[32,512]{1,0:T(8,128)S(1)}, f32[32,512]{1,0:T(8,128)S(1)}, u32[]{:S(2)}, u32[]{:S(2)}) collective-permute-start(f32[32,512]{1,0:T(8,128)S(1)} %get-tuple-element.12), channel_id=1, source_target_pairs={{0,4},{4,8},{8,12},{1,5},{5,9},{9,13},{2,6},{6,10},{10,14},{3,7},{... | collective-permute-start | bytes 196616 | tf_op jit(solution)/shard_map/ppermute | solution.py:303
  7.8 1.1 %fusion = (f32[16,1,512]{2,1,0:T(1,128)S(1)}, f32[16,1,512]{2,1,0:T(1,128)S(1)}) fusion(f32[16,32,512]{2,1,0:T(8,128)} %param.8), kind=kLoop, calls=%fused_computation.6 | loop fusion | bytes 131072 | tf_op jit(solution)/shard_map/slice | solution.py:333
  8.9 0.0 collective-permute-done.1.down_ref
  8.9 0.7 collective-permute-done.up_ref
  9.7 1.4 %collective-permute-start.2 = (f32[18,512]{1,0:T(8,128)S(1)}, f32[18,512]{1,0:T(8,128)S(1)}, u32[]{:S(2)}, u32[]{:S(2)}) collective-permute-start(f32[18,512]{1,0:T(8,128)S(1)} %pad_maximum_fusion), channel_id=1, source_target_pairs={{0,1},{1,2},{2,3},{4,5},{5,6},{6,7},{8,9},{9,10},{10,11},{12,13},{... | collective-permute-start | bytes 110600 | tf_op jit(solution)/shard_map/ppermute | solution.py:303
  11.2 1.3 %collective-permute-start.3 = (f32[18,512]{1,0:T(8,128)S(1)}, f32[18,512]{1,0:T(8,128)S(1)}, u32[]{:S(2)}, u32[]{:S(2)}) collective-permute-start(f32[18,512]{1,0:T(8,128)S(1)} %pad_maximum_fusion.1), channel_id=1, source_target_pairs={{1,0},{2,1},{3,2},{5,4},{6,5},{7,6},{9,8},{10,9},{11,10},{13,12},{... | collective-permute-start | bytes 110600 | tf_op jit(solution)/shard_map/ppermute | solution.py:303
  12.5 0.0 copy-start
  12.5 1.6 %copy-done = bf16[512,2048]{1,0:T(8,128)(2,1)S(1)} copy-done((bf16[512,2048]{1,0:T(8,128)(2,1)S(1)}, bf16[512,2048]{1,0:T(8,128)(2,1)}, u32[]{:S(2)}) %copy-start) | copy-done | bytes 2097176
  14.1 1.2 %copy-done.2 = f32[16,32,512]{2,1,0:T(8,128)S(1)} copy-done((f32[16,32,512]{2,1,0:T(8,128)S(1)}, f32[16,32,512]{2,1,0:T(8,128)}, u32[]{:S(2)}) %copy-start.2) | copy-done | bytes 1048600
  15.3 2.7 %expand.1.expanded_ref = bf16[512,2048]{1,0:T(8,128)(2,1)S(1)} custom-call(f32[512,512]{1,0:T(8,128)S(1)} %bitcast.16, bf16[512,2048]{1,0:T(8,128)(2,1)S(1)} %copy-done), custom_call_target="tpu_custom_call" | custom-call | flops 1073741824 | bytes 5242880 | tf_op jit(solution)/shard_map/expand/pallas_call | solution.py:64
  18.0 0.0 copy-start.9
  18.0 0.0 collective-permute-done.2.left_ref
  18.0 0.0 collective-permute-done.3.right_ref
  18.0 0.0 copy-done.7
  18.0 0.0 copy-done.8
  18.0 0.0 copy-done.1
  18.0 9.3 %mix.1 = (f32[512,512]{1,0:T(8,128)S(1)}, bf16[512,512]{1,0:T(8,128)(2,1)S(1)}) custom-call(bf16[512,2048]{1,0:T(8,128)(2,1)S(1)} %expand.1.expanded_ref, f32[512,512]{1,0:T(8,128)S(1)} %bitcast.17, f32[32,512]{1,0:T(8,128)S(1)} %collective-permute-done.up_ref, f32[32,512]{1,0:T(8,128)S(1)} %collective-permute-done.1.down_ref, ...), custom_call_target="tpu_custom_call" | custom-call | flops 1073741824 | bytes 8912896 | tf_op jit(solution)/shard_map/mix/pallas_call | solution.py:167
  27.4 24.4 %all_to_all.10 = bf16[16,32,512]{2,1,0:T(8,128)(2,1)S(1)} all-to-all(bf16[16,32,512]{2,1,0:T(8,128)(2,1)S(1)} %bitcast.19), channel_id=1, replica_groups=mesh['field'=2,'row'=4,'col'=4] {'row','col'}, dimensions={0} | all-to-all | bytes 1048576 | tf_op jit(solution)/shard_map/all_to_all | solution.py:339
  51.8 9.9 %attend.1 = bf16[16,2,16,512]{3,2,1,0:T(8,128)(2,1)S(1)} custom-call(bf16[16,2,16,512]{3,2,1,0:T(8,128)(2,1)S(1)} %bitcast.20, bf16[512,1536]{1,0:T(8,128)(2,1)S(1)} %copy-done.9), custom_call_target="tpu_custom_call" | custom-call | flops 1073741824 | bytes 2621440 | tf_op jit(solution)/shard_map/attend/pallas_call | solution.py:257
  61.8 18.4 %all_to_all.11 = bf16[16,32,512]{2,1,0:T(8,128)(2,1)S(1)} all-to-all(bf16[16,32,512]{2,1,0:T(8,128)(2,1)S(1)} %bitcast.21), channel_id=1, replica_groups=mesh['field'=2,'row'=4,'col'=4] {'row','col'}, dimensions={0} | all-to-all | bytes 1048576 | tf_op jit(solution)/shard_map/all_to_all | solution.py:343
  80.1 0.0 copy-done.5
  80.1 2.6 %finish.1 = f32[512,512]{1,0:T(8,128)} custom-call(bf16[512,512]{1,0:T(8,128)(2,1)S(1)} %bitcast.18, bf16[512,512]{1,0:T(8,128)(2,1)S(1)} %copy-done.6, bf16[512,512]{1,0:T(8,128)(2,1)S(1)} %copy-done.5, f32[512,512]{1,0:T(8,128)S(1)} %get-tuple-element.8.mixed_ref), custom_call_target="tpu_custom_call" | custom-call | tf_op jit(solution)/shard_map/finish/pallas_call | solution.py:283
  (18 shorter events, 0.1 us)
Async XLA Ops:
  0.0 18.0 %copy-start.7 = (bf16[512,512]{1,0:T(8,128)(2,1)S(1)}, bf16[512,512]{1,0:T(8,128)(2,1)}, u32[]{:S(2)}) copy-start(bf16[512,512]{1,0:T(8,128)(2,1)} %constant.4.clone.perm_ref) | copy-start | bytes 1572868
  0.9 8.0 %collective-permute-start.1 = (f32[32,512]{1,0:T(8,128)S(1)}, f32[32,512]{1,0:T(8,128)S(1)}, u32[]{:S(2)}, u32[]{:S(2)}) collective-permute-start(f32[32,512]{1,0:T(8,128)S(1)} %get-tuple-element.11), channel_id=1, source_target_pairs={{4,0},{8,4},{12,8},{5,1},{9,5},{13,9},{6,2},{10,6},{14,10},{7,3},{... | collective-permute-start | bytes 196616 | tf_op jit(solution)/shard_map/ppermute | solution.py:303
  2.2 7.5 %collective-permute-start = (f32[32,512]{1,0:T(8,128)S(1)}, f32[32,512]{1,0:T(8,128)S(1)}, u32[]{:S(2)}, u32[]{:S(2)}) collective-permute-start(f32[32,512]{1,0:T(8,128)S(1)} %get-tuple-element.12), channel_id=1, source_target_pairs={{0,4},{4,8},{8,12},{1,5},{5,9},{9,13},{2,6},{6,10},{10,14},{3,7},{... | collective-permute-start | bytes 196616 | tf_op jit(solution)/shard_map/ppermute | solution.py:303
  9.7 8.3 %copy-start.8 = (f32[3,3,2048]{2,1,0:T(4,128)S(1)}, f32[3,3,2048]{2,1,0:T(4,128)}, u32[]{:S(2)}) copy-start(f32[3,3,2048]{2,1,0:T(4,128)} %depth_ref.1) | copy-start | bytes 221188
  9.7 8.3 %collective-permute-start.2 = (f32[18,512]{1,0:T(8,128)S(1)}, f32[18,512]{1,0:T(8,128)S(1)}, u32[]{:S(2)}, u32[]{:S(2)}) collective-permute-start(f32[18,512]{1,0:T(8,128)S(1)} %pad_maximum_fusion), channel_id=1, source_target_pairs={{0,1},{1,2},{2,3},{4,5},{5,6},{6,7},{8,9},{9,10},{10,11},{12,13},{... | collective-permute-start | bytes 110600 | tf_op jit(solution)/shard_map/ppermute | solution.py:303
  11.2 6.8 %collective-permute-start.3 = (f32[18,512]{1,0:T(8,128)S(1)}, f32[18,512]{1,0:T(8,128)S(1)}, u32[]{:S(2)}, u32[]{:S(2)}) collective-permute-start(f32[18,512]{1,0:T(8,128)S(1)} %pad_maximum_fusion.1), channel_id=1, source_target_pairs={{1,0},{2,1},{3,2},{5,4},{6,5},{7,6},{9,8},{10,9},{11,10},{13,12},{... | collective-permute-start | bytes 110600 | tf_op jit(solution)/shard_map/ppermute | solution.py:303
  12.5 1.6 %copy-start = (bf16[512,2048]{1,0:T(8,128)(2,1)S(1)}, bf16[512,2048]{1,0:T(8,128)(2,1)}, u32[]{:S(2)}) copy-start(bf16[512,2048]{1,0:T(8,128)(2,1)} %w_expand_ref.1) | copy-start | bytes 6291460
  14.1 1.2 %copy-start.2 = (f32[16,32,512]{2,1,0:T(8,128)S(1)}, f32[16,32,512]{2,1,0:T(8,128)}, u32[]{:S(2)}) copy-start(f32[16,32,512]{2,1,0:T(8,128)} %param.8) | copy-start | bytes 3145732
  15.3 2.7 %copy-start.1 = (bf16[512,2048]{1,0:T(8,128)(2,1)S(1)}, bf16[512,2048]{1,0:T(8,128)(2,1)}, u32[]{:S(2)}) copy-start(bf16[512,2048]{1,0:T(8,128)(2,1)} %w_expand_ref.1) | copy-start | bytes 6291460
  15.3 2.7 %copy-start.3 = (f32[16,32,512]{2,1,0:T(8,128)S(1)}, f32[16,32,512]{2,1,0:T(8,128)}, u32[]{:S(2)}) copy-start(f32[16,32,512]{2,1,0:T(8,128)} %param.8) | copy-start | bytes 3145732
  15.3 2.7 %copy-start.4 = (bf16[2048,512]{1,0:T(8,128)(2,1)S(1)}, bf16[2048,512]{1,0:T(8,128)(2,1)}, u32[]{:S(2)}) copy-start(bf16[2048,512]{1,0:T(8,128)(2,1)} %w_project_ref.1) | copy-start | bytes 6291460
  18.0 33.8 %copy-start.9 = (bf16[512,1536]{1,0:T(8,128)(2,1)S(1)}, bf16[512,1536]{1,0:T(8,128)(2,1)}, u32[]{:S(2)}) copy-start(bf16[512,1536]{1,0:T(8,128)(2,1)} %weight_ref.4) | copy-start | bytes 4718596
  51.8 28.3 %copy-start.5 = (bf16[512,512]{1,0:T(8,128)(2,1)S(1)}, bf16[512,512]{1,0:T(8,128)(2,1)}, u32[]{:S(2)}) copy-start(bf16[512,512]{1,0:T(8,128)(2,1)} %weight_ref.5) | copy-start | bytes 1572868
  51.8 28.3 %copy-start.6 = (bf16[512,512]{1,0:T(8,128)(2,1)S(1)}, bf16[512,512]{1,0:T(8,128)(2,1)}, u32[]{:S(2)}) copy-start(bf16[512,512]{1,0:T(8,128)(2,1)} %constant.5.clone.back_ref) | copy-start | bytes 1572868

commit v2 on v1

v2 whole, which is shorter than its diff:
```python
import functools
import math

import jax
import jax.numpy as jnp
import numpy as np
from jax import lax
from jax.experimental import pallas as pl
from jax.experimental.pallas import tpu as pltpu
from jax.sharding import PartitionSpec as P

HEADS = 16
GRID = 16
LANES = 128
MIB = 1024 * 1024
NT = (((1,), (1,)), ((), ()))


def layer_norm(inputs):
    average = jnp.mean(inputs, axis=-1, keepdims=True)
    centred = inputs - average
    variance = jnp.mean(centred * centred, axis=-1, keepdims=True)
    return centred * lax.rsqrt(variance + 1e-05)


def gelu(x):
    scale = math.sqrt(2.0 / math.pi)
    half = 0.5 * x
    return half + half * jnp.tanh(x * (scale + (scale * 0.044715) * (x * x)))


def matmul(a, b):
    return jnp.dot(a, b, preferred_element_type=jnp.float32)


def matmul_nt(a, b):
    return lax.dot_general(a, b, NT, preferred_element_type=jnp.float32)


def divisor(size, most, unit):
    best = size
    for piece in range(unit, most + 1, unit):
        if size % piece == 0:
            best = piece
    return best


def round_up(size, unit):
    return -(-size // unit) * unit


def vmem():
    return pl.BlockSpec(memory_space=pltpu.VMEM)


def norm_kernel(field_ref, normed_ref):
    normed_ref[...] = layer_norm(field_ref[...]).astype(jnp.bfloat16)


def norm(field):
    tokens, channels = field.shape
    step = divisor(tokens, 128, 16)
    return pl.pallas_call(
        norm_kernel,
        grid=(tokens // step,),
        in_specs=[pl.BlockSpec((step, channels), lambda i: (i, 0))],
        out_specs=pl.BlockSpec((step, channels), lambda i: (i, 0)),
        out_shape=jax.ShapeDtypeStruct((tokens, channels), jnp.bfloat16),
        compiler_params=pltpu.CompilerParams(vmem_limit_bytes=16 * MIB),
        cost_estimate=pl.CostEstimate(
            flops=8 * tokens * channels, bytes_accessed=6 * tokens * channels, transcendentals=tokens
        ),
        name="norm",
    )(field)


def expand_kernel(normed_ref, weight_ref, out_ref):
    tokens = out_ref.shape[0]
    step = divisor(tokens, 128, 16)
    for start in range(0, tokens, step):
        rows = slice(start, start + step)
        out_ref[rows, :] = gelu(matmul(normed_ref[rows, :], weight_ref[...])).astype(jnp.bfloat16)


def expand(normed, w_expand):
    tokens, channels = normed.shape
    width = w_expand.shape[1]
    tile = divisor(width, 512, LANES)
    return pl.pallas_call(
        expand_kernel,
        grid=(width // tile,),
        in_specs=[vmem(), pl.BlockSpec((channels, tile), lambda j: (0, j))],
        out_specs=pl.BlockSpec((tokens, tile), lambda j: (0, j)),
        out_shape=jax.ShapeDtypeStruct((tokens, width), jnp.bfloat16),
        compiler_params=pltpu.CompilerParams(vmem_limit_bytes=16 * MIB),
        cost_estimate=pl.CostEstimate(
            flops=2 * tokens * channels * width,
            bytes_accessed=tokens * channels * 2 + channels * width * 2 + tokens * width * 2,
            transcendentals=tokens * width,
        ),
        name="expand",
    )(normed, w_expand)


def mix_kernel(
    expanded_ref, field_ref, up_ref, down_ref, left_ref, right_ref, w_expand_ref, depth_ref,
    w_project_ref, perm_ref, mixed_ref, grouped_ref, halo_ref, total_ref, even_ref, odd_ref,
    *, rows, cols,
):
    width = expanded_ref.shape[1]
    tile = even_ref.shape[1]
    slot = left_ref.shape[0]
    left_start, right_start = 2 * cols, 2 * cols + slot

    edges = jnp.concatenate(
        [up_ref[...], down_ref[...], left_ref[...], right_ref[...]], axis=0
    )

    def halo_body(index, carry):
        lanes = pl.ds(pl.multiple_of(index * tile, tile), tile)
        made = gelu(matmul(edges, w_expand_ref[:, lanes]))
        halo_ref[:, lanes] = made.astype(jnp.bfloat16).astype(jnp.float32)
        return carry

    lax.fori_loop(0, width // tile, halo_body, 0)

    position = lax.broadcasted_iota(jnp.int32, (8, LANES), 0)
    at_first = position == 0
    at_last = position == 7

    def convolve(index, out_ref):
        for sub in range(tile // LANES):
            lanes = pl.ds(pl.multiple_of(index * tile + sub * LANES, LANES), LANES)
            taps = [[depth_ref[p, q : q + 1, lanes] for q in range(3)] for p in range(3)]
            sides = []
            for q, start in ((0, left_start), (2, right_start)):
                sides.append(
                    sum(taps[p][q] * halo_ref[start + p : start + p + rows, lanes] for p in range(3))
                )

            def row_of(y):
                if y < 0:
                    return halo_ref[:cols, lanes]
                if y == rows:
                    return halo_ref[cols : 2 * cols, lanes]
                return expanded_ref[y * cols : (y + 1) * cols, lanes].astype(jnp.float32)

            window = [row_of(-1), row_of(0), None]
            for y in range(rows):
                window[2] = row_of(y + 1)
                summed = [
                    taps[0][q] * window[0] + taps[1][q] * window[1] + taps[2][q] * window[2]
                    for q in range(3)
                ]
                before = pltpu.roll(summed[0], 1, 0)
                before = jnp.concatenate(
                    [jnp.where(at_first, sides[0][y : y + 1], before[:8]), before[8:]], axis=0
                )
                after = pltpu.roll(summed[2], cols - 1, 0)
                after = jnp.concatenate(
                    [after[:-8], jnp.where(at_last, sides[1][y : y + 1], after[-8:])], axis=0
                )
                made = gelu(before + summed[1] + after).astype(jnp.bfloat16)
                out_ref[y * cols : (y + 1) * cols, sub * LANES : (sub + 1) * LANES] = made
                window = [window[1], window[2], None]

    def project(index, in_ref):
        piece = pl.ds(pl.multiple_of(index * tile, tile), tile)
        total_ref[...] += matmul(in_ref[...], w_project_ref[piece, :])

    total_ref[...] = field_ref[...]
    convolve(0, even_ref)

    def body(index, carry):
        project(2 * index, even_ref)
        convolve(2 * index + 1, odd_ref)
        project(2 * index + 1, odd_ref)
        convolve(2 * index + 2, even_ref)
        return carry

    pairs = width // tile // 2
    lax.fori_loop(0, pairs - 1, body, 0)
    project(2 * pairs - 2, even_ref)
    convolve(2 * pairs - 1, odd_ref)
    project(2 * pairs - 1, odd_ref)

    mixed = total_ref[...]
    mixed_ref[...] = mixed
    normed = layer_norm(mixed).astype(jnp.bfloat16)
    grouped_ref[...] = matmul(perm_ref[...], normed).astype(jnp.bfloat16)


def mix(expanded, field, up, down, left, right, w_expand, depth_kernel, w_project, perm, rows, cols):
    tokens, channels = field.shape
    width = expanded.shape[1]
    tile = divisor(width // 2, 256, LANES)
    slot = left.shape[0]
    return pl.pallas_call(
        functools.partial(mix_kernel, rows=rows, cols=cols),
        in_specs=[vmem()] * 10,
        out_specs=[vmem()] * 2,
        out_shape=[
            jax.ShapeDtypeStruct((tokens, channels), jnp.float32),
            jax.ShapeDtypeStruct((tokens, channels), jnp.bfloat16),
        ],
        scratch_shapes=[
            pltpu.VMEM((2 * cols + 2 * slot, width), jnp.float32),
            pltpu.VMEM((tokens, channels), jnp.float32),
            pltpu.VMEM((tokens, tile), jnp.bfloat16),
            pltpu.VMEM((tokens, tile), jnp.bfloat16),
        ],
        compiler_params=pltpu.CompilerParams(vmem_limit_bytes=16 * MIB),
        cost_estimate=pl.CostEstimate(
            flops=2 * tokens * channels * width,
            bytes_accessed=tokens * channels * 10 + 4 * channels * width + tokens * width * 2,
            transcendentals=tokens * width,
        ),
        name="mix",
    )(expanded, field, up, down, left, right, w_expand, depth_kernel, w_project, perm)


def identity(size):
    row = lax.broadcasted_iota(jnp.int32, (size, size), 0)
    column = lax.broadcasted_iota(jnp.int32, (size, size), 1)
    return jnp.where(row == column, 1.0, 0.0).astype(jnp.bfloat16)


def attend_kernel(
    tokens_ref, weight_ref, out_ref, query_ref, key_ref, value_ref, turned_ref, even_ref, odd_ref
):
    devices, sets, members, channels = tokens_ref.shape
    count = devices * members
    head_width = channels // HEADS
    group_heads = LANES // head_width
    groups = channels // LANES
    factor = math.log2(math.e) / math.sqrt(head_width)
    lane = lax.broadcasted_iota(jnp.int32, (1, LANES), 1)
    masks = [
        jnp.where((lane >= j * head_width) & (lane < (j + 1) * head_width), 1.0, 0.0).astype(
            jnp.bfloat16
        )
        for j in range(group_heads)
    ]
    turn_values = identity(channels)
    for s in range(sets):
        block = tokens_ref[:, s].reshape(count, channels)
        qkv = matmul(block, weight_ref[...]).astype(jnp.bfloat16)
        values = matmul_nt(turn_values, qkv[:, 2 * channels :]).astype(jnp.bfloat16)
        for group in range(groups):
            lanes = slice(group * LANES, (group + 1) * LANES)
            query_ref[s * groups + group] = qkv[:, lanes]
            key_ref[s * groups + group] = qkv[:, channels + group * LANES : channels + (group + 1) * LANES]
            for j in range(group_heads):
                head = (group * group_heads + j) * head_width
                value_ref[s * groups + group, j, :head_width] = values[head : head + head_width]
                value_ref[s * groups + group, j, head_width:] = jnp.ones((16, count), jnp.bfloat16)

    def scores(index, out):
        keys = key_ref[index]
        stacked = jnp.concatenate([keys * mask for mask in masks], axis=0)
        out[...] = matmul_nt(stacked, query_ref[index])

    def weigh(index, scores_ref):
        for j in range(group_heads):
            part = scores_ref[j * count : (j + 1) * count]
            highest = jnp.max(part, axis=0, keepdims=True)
            raised = jnp.exp2((part - highest) * factor).astype(jnp.bfloat16)
            product = matmul(value_ref[index, j], raised)
            scale = 1.0 / product[head_width : head_width + 1]
            turned_ref[index, j * head_width : (j + 1) * head_width] = (
                product[:head_width] * scale
            ).astype(jnp.bfloat16)

    total = sets * groups
    scores(0, even_ref)

    def body(pair, carry):
        scores(2 * pair + 1, odd_ref)
        weigh(2 * pair, even_ref)
        scores(jnp.minimum(2 * pair + 2, total - 1), even_ref)
        weigh(2 * pair + 1, odd_ref)
        return carry

    lax.fori_loop(0, total // 2, body, 0)
    turn_tokens = identity(count)
    for s in range(sets):
        turned = turned_ref[s * groups : (s + 1) * groups].reshape(channels, count)
        attended = matmul_nt(turn_tokens, turned).astype(jnp.bfloat16)
        out_ref[:, s] = attended.reshape(devices, members, channels)


def attend(blocks, w_qkv):
    devices, sets, members, channels = blocks.shape
    count = devices * members
    apart = members % 16 != 0
    if apart:
        blocks = blocks.transpose(1, 0, 2, 3).reshape(1, sets, count, channels)
    head_width = channels // HEADS
    group_heads = LANES // head_width
    total = sets * channels // LANES
    result = pl.pallas_call(
        attend_kernel,
        in_specs=[vmem()] * 2,
        out_specs=vmem(),
        out_shape=jax.ShapeDtypeStruct(blocks.shape, jnp.bfloat16),
        scratch_shapes=[
            pltpu.VMEM((total, count, LANES), jnp.bfloat16),
            pltpu.VMEM((total, count, LANES), jnp.bfloat16),
            pltpu.VMEM((total, group_heads, head_width + 16, count), jnp.bfloat16),
            pltpu.VMEM((total, LANES, count), jnp.bfloat16),
            pltpu.VMEM((group_heads * count, count), jnp.float32),
            pltpu.VMEM((group_heads * count, count), jnp.float32),
        ],
        compiler_params=pltpu.CompilerParams(vmem_limit_bytes=24 * MIB),
        cost_estimate=pl.CostEstimate(
            flops=sets * (2 * count * channels * channels * 3 + 4 * count * count * channels),
            bytes_accessed=4 * sets * count * channels + 6 * channels * channels,
            transcendentals=sets * HEADS * count * count,
        ),
        name="attend",
    )(blocks, w_qkv)
    if apart:
        result = result.reshape(sets, devices, members, channels).transpose(1, 0, 2, 3)
    return result


def finish_kernel(attended_ref, back_ref, weight_ref, mixed_ref, out_ref):
    step = out_ref.shape[0]
    rows = pl.ds(pl.multiple_of(pl.program_id(0) * step, step), step)
    restored = matmul(back_ref[rows, :], attended_ref[...]).astype(jnp.bfloat16)
    out_ref[...] = mixed_ref[rows, :] + matmul(restored, weight_ref[...])


def finish(attended, back, w_out, mixed):
    tokens, channels = mixed.shape
    step = divisor(tokens, 128, 16)
    return pl.pallas_call(
        finish_kernel,
        grid=(tokens // step,),
        in_specs=[vmem()] * 4,
        out_specs=pl.BlockSpec((step, channels), lambda i: (i, 0)),
        out_shape=jax.ShapeDtypeStruct((tokens, channels), jnp.float32),
        compiler_params=pltpu.CompilerParams(vmem_limit_bytes=16 * MIB),
        name="finish",
    )(attended, back, w_out, mixed)


def exchange(low_edge, high_edge, axis):
    count = lax.axis_size(axis)
    even = lax.axis_index(axis) % 2 == 0

    def swap(edge, start):
        pairs = [(i, i + 1) for i in range(start, count - 1, 2)]
        return lax.ppermute(edge, axis, pairs + [(b, a) for a, b in pairs])

    one = swap(jnp.where(even, high_edge, low_edge), 0)
    two = swap(jnp.where(even, low_edge, high_edge), 1)
    return jnp.where(even, two, one), jnp.where(even, one, two)


def grouping(rows, cols, blocks_rows, blocks_cols):
    order = np.arange(rows * cols).reshape(
        blocks_rows, rows // blocks_rows, blocks_cols, cols // blocks_cols
    )
    order = order.transpose(1, 3, 0, 2).reshape(-1)
    matrix = np.zeros((order.size, order.size), np.float32)
    matrix[np.arange(order.size), order] = 1.0
    return matrix


def shards(field, w_expand, depth_kernel, w_project, w_qkv, w_out):
    rows, cols, channels = field.shape
    tokens = rows * cols
    row_devices = lax.axis_size("row")
    col_devices = lax.axis_size("col")
    devices = row_devices * col_devices
    blocks_rows = GRID // row_devices
    blocks_cols = GRID // col_devices
    members = blocks_rows * blocks_cols
    sets_local = tokens // members // devices
    matrix = grouping(rows, cols, blocks_rows, blocks_cols)
    perm = jnp.asarray(matrix, jnp.bfloat16)
    back = jnp.asarray(matrix.T, jnp.bfloat16)

    flat = field.reshape(tokens, channels)
    normed = norm(flat)
    up, down = exchange(normed[:cols], normed[tokens - cols :], "row")
    expanded = expand(normed, w_expand)
    tile = normed.reshape(rows, cols, channels)
    spare = jnp.zeros((round_up(rows + 2, 16) - rows - 2, channels), jnp.bfloat16)
    first = jnp.concatenate([up[:1], tile[:, 0], down[:1], spare], axis=0)
    last = jnp.concatenate([up[cols - 1 :], tile[:, cols - 1], down[cols - 1 :], spare], axis=0)
    left, right = exchange(first, last, "col")
    mixed, grouped = mix(
        expanded, flat, up, down, left, right, w_expand, depth_kernel, w_project, perm, rows, cols
    )
    arrived = lax.all_to_all(
        grouped.reshape(devices, sets_local * members, channels), ("row", "col"), 0, 0, tiled=True
    )
    attended = attend(arrived.reshape(devices, sets_local, members, channels), w_qkv)
    returned = lax.all_to_all(
        attended.reshape(devices, sets_local * members, channels), ("row", "col"), 0, 0, tiled=True
    )
    final = finish(returned.reshape(tokens, channels), back, w_out, mixed)
    return final.reshape(rows, cols, channels)


def solution(mesh):
    return jax.shard_map(
        shards,
        mesh=mesh,
        in_specs=(P(("field", "row"), "col", None), P(), P(), P(), P(), P()),
        out_specs=P(("field", "row"), "col", None),
        check_vma=False,
    )
```

time: 83.1 us -> 70.2 us (0.84)
  Pallas kernels: 24.6 us -> 18.7 us
  starting transfers between devices: 9.57 us -> 4.61 us
  local copies, waits for them, and re-layouts: 4.89 us -> 1.57 us
  blocking collectives: 42.8 us -> 43.7 us
    pallas_call x4 -> x5, Pallas kernels: 24.6 us -> 18.7 us  [the longest x1 8.35 us: mix(): pl.pallas_call(functools.partial(mix_kernel, rows=rows, cols=cols), in_sp...]
    ppermute x4, starting transfers between devices: 9.57 us -> 4.61 us  [swap(): return lax.ppermute(edge, axis, pairs + [(b, a) for a, b in pairs])]
    unnamed x22 -> x18, local copies, waits for them, and re-layouts: 2.85 us -> 1.42 us
    slice x3 -> x2, local copies, waits for them, and re-layouts: 1.1 us -> 0.07 us  [shards(): first = jnp.concatenate([up[:1], tile[:, 0], down[:1], spare], axis=0)]
    all_to_all x1, blocking collectives: 24.4 us -> 25.4 us  [shards(): lax.all_to_all(grouped.reshape(devices, sets_local * members, channels),...]
    squeeze x1, local copies, waits for them, and re-layouts: 0.94 us -> 0.01 us  [shards(): tile[:, cols - 1]]
  transfers between devices with their start and end apart: 4 -> 4, of which waited for: 1 -> 1; matrix products, arithmetic and copies ran while one was open for 1% -> 0% of each run, Pallas kernels for 3% -> 3%
where the time goes in v2:
time: 70.2 us; the launch traced here: 70 us
  blocking collectives  43.7 us (62%)
  Pallas kernels  18.7 us (27%)
  starting transfers between devices  4.61 us (7%)
  local copies, waits for them, and re-layouts  1.57 us (2%)
  waiting for transfers between devices  1.06 us (2%)
    all_to_all x1, blocking collectives, shards(): lax.all_to_all(grouped.reshape(devices, sets_local * members, channels),...  25.4 us
    all_to_all x1, blocking collectives, shards(): lax.all_to_all(attended.reshape(devices, sets_local * members, channels),...  18.4 us
    pallas_call x1, Pallas kernels, mix(): pl.pallas_call(functools.partial(mix_kernel, rows=rows, cols=cols), in_sp...  8.35 us
    ppermute x4, starting transfers between devices, swap(): return lax.ppermute(edge, axis, pairs + [(b, a) for a, b in pairs])  4.61 us
    pallas_call x1, Pallas kernels, attend(): pl.pallas_call(attend_kernel, in_specs=[vmem()] * 2, out_specs=vmem(), ou...  4.56 us
    pallas_call x1, Pallas kernels, finish(): pl.pallas_call(finish_kernel, grid=(tokens // step,), in_specs=[vmem()] *...  2.63 us
    pallas_call x1, Pallas kernels, expand(): pl.pallas_call(expand_kernel, grid=(width // tile,), in_specs=[vmem(), pl...  2.35 us
    unnamed x18, local copies, waits for them, and re-layouts  1.42 us
  transfers between devices with their start and end apart: 4, of which 1 were waited for; matrix products, arithmetic and copies ran while one was open for 0% of the time, Pallas kernels for 3%

profile of v2, /device:TPU:0, one launch (start us, length us, event | category | flops | bytes accessed | tf_op | source)
XLA Modules:
  0.0 70.0 jit_solution(4970907048679674637)
XLA Ops:
  0.0 1.4 %copy-done.1 = f32[16,32,512]{2,1,0:T(8,128)S(1)} copy-done((f32[16,32,512]{2,1,0:T(8,128)S(1)}, f32[16,32,512]{2,1,0:T(8,128)}, u32[]{:S(2)}) %copy-start.1) | copy-done | bytes 1048600
  1.4 0.8 %norm.1.normed_ref = bf16[512,512]{1,0:T(8,128)(2,1)S(1)} custom-call(f32[512,512]{1,0:T(8,128)S(1)} %bitcast.11), custom_call_target="tpu_custom_call" | custom-call | flops 2097152 | bytes 1572864 | tf_op jit(solution)/shard_map/norm/pallas_call | solution.py:63
  2.2 3.1 %collective-permute-start.1 = (bf16[32,512]{1,0:T(8,128)(2,1)S(1)}, bf16[32,512]{1,0:T(8,128)(2,1)S(1)}, u32[]{:S(2)}, u32[]{:S(2)}) collective-permute-start(bf16[32,512]{1,0:T(8,128)(2,1)S(1)} %get-tuple-element.11), channel_id=1, source_target_pairs={{0,4},{8,12},{4,0},{12,8},{1,5},{9,13},{5,1},{13,9},{2,6},{10,14},... | collective-permute-start | bytes 98312 | tf_op jit(solution)/shard_map/ppermute | solution.py:354
  5.3 0.7 collective-permute-start
  6.0 0.1 fusion
  6.1 0.1 pad.7.clone
  6.2 1.1 %collective-permute-done.1 = bf16[32,512]{1,0:T(8,128)(2,1)S(1)} collective-permute-done((bf16[32,512]{1,0:T(8,128)(2,1)S(1)}, bf16[32,512]{1,0:T(8,128)(2,1)S(1)}, u32[]{:S(2)}, u32[]{:S(2)}) %collective-permute-start.1) | collective-permute-done | bytes 32800 | tf_op jit(solution)/shard_map/ppermute | solution.py:354
  7.2 0.0 collective-permute-done
  7.2 0.1 broadcast_select_fusion.2
  7.3 0.1 collective-permute-start.3
  7.4 0.0 copy-start.2
  7.4 0.0 copy-start.3
  7.4 0.0 copy-start.6
  7.4 0.0 copy-start.7
  7.5 0.8 %collective-permute-start.2 = (bf16[32,512]{1,0:T(8,128)(2,1)S(1)}, bf16[32,512]{1,0:T(8,128)(2,1)S(1)}, u32[]{:S(2)}, u32[]{:S(2)}) collective-permute-start(bf16[32,512]{1,0:T(8,128)(2,1)S(1)} %get-tuple-element.18), channel_id=1, source_target_pairs={{1,2},{2,1},{5,6},{6,5},{9,10},{10,9},{13,14},{14,13},{17,18},{18,... | collective-permute-start | bytes 98312 | tf_op jit(solution)/shard_map/ppermute | solution.py:354
  8.3 2.4 %expand.1.expanded_ref = bf16[512,2048]{1,0:T(8,128)(2,1)S(1)} custom-call(bf16[512,512]{1,0:T(8,128)(2,1)S(1)} %norm.1.normed_ref, bf16[512,2048]{1,0:T(8,128)(2,1)S(1)} %copy-done), custom_call_target="tpu_custom_call" | custom-call | flops 1073741824 | bytes 4718592 | tf_op jit(solution)/shard_map/expand/pallas_call | solution.py:89
  10.6 0.0 collective-permute-done.3
  10.6 0.0 collective-permute-done.2
  10.7 0.0 copy-start.8
  10.7 8.3 %mix.1 = (f32[512,512]{1,0:T(8,128)S(1)}, bf16[512,512]{1,0:T(8,128)(2,1)S(1)}) custom-call(bf16[512,2048]{1,0:T(8,128)(2,1)S(1)} %expand.1.expanded_ref, f32[512,512]{1,0:T(8,128)S(1)} %bitcast.12, bf16[32,512]{1,0:T(8,128)(2,1)S(1)} %get-tuple-element.16.up_ref, bf16[32,512]{1,0:T(8,128)(2,1)S(1)} %get-tuple-element.15.down_ref, ...), custom_call_target="tpu_custom_call" | custom-call | flops 1073741824 | bytes 8912896 | tf_op jit(solution)/shard_map/mix/pallas_call | solution.py:198
  19.1 25.4 %all_to_all.10 = bf16[16,32,512]{2,1,0:T(8,128)(2,1)S(1)} all-to-all(bf16[16,32,512]{2,1,0:T(8,128)(2,1)S(1)} %bitcast.15), channel_id=1, replica_groups=mesh['field'=2,'row'=4,'col'=4] {'row','col'}, dimensions={0} | all-to-all | bytes 1048576 | tf_op jit(solution)/shard_map/all_to_all | solution.py:397
  44.5 4.6 %attend.1 = bf16[16,2,16,512]{3,2,1,0:T(8,128)(2,1)S(1)} custom-call(bf16[16,2,16,512]{3,2,1,0:T(8,128)(2,1)S(1)} %bitcast.16, bf16[512,1536]{1,0:T(8,128)(2,1)S(1)} %copy-done.8), custom_call_target="tpu_custom_call" | custom-call | flops 1073741824 | bytes 2621440 | tf_op jit(solution)/shard_map/attend/pallas_call | solution.py:301
  49.0 18.4 %all_to_all.11 = bf16[16,32,512]{2,1,0:T(8,128)(2,1)S(1)} all-to-all(bf16[16,32,512]{2,1,0:T(8,128)(2,1)S(1)} %bitcast.17), channel_id=1, replica_groups=mesh['field'=2,'row'=4,'col'=4] {'row','col'}, dimensions={0} | all-to-all | bytes 1048576 | tf_op jit(solution)/shard_map/all_to_all | solution.py:401
  67.4 2.6 %finish.1 = f32[512,512]{1,0:T(8,128)} custom-call(bf16[512,512]{1,0:T(8,128)(2,1)S(1)} %bitcast.14, bf16[512,512]{1,0:T(8,128)(2,1)S(1)} %copy-done.5, bf16[512,512]{1,0:T(8,128)(2,1)S(1)} %copy-done.4, f32[512,512]{1,0:T(8,128)S(1)} %get-tuple-element.8.mixed_ref), custom_call_target="tpu_custom_call" | custom-call | tf_op jit(solution)/shard_map/finish/pallas_call | solution.py:337
  (18 shorter events, 0.1 us)
Async XLA Ops:
  0.0 8.3 %copy-start = (bf16[512,2048]{1,0:T(8,128)(2,1)S(1)}, bf16[512,2048]{1,0:T(8,128)(2,1)}, u32[]{:S(2)}) copy-start(bf16[512,2048]{1,0:T(8,128)(2,1)} %w_expand_ref.1) | copy-start | bytes 6291460
  0.0 1.4 %copy-start.1 = (f32[16,32,512]{2,1,0:T(8,128)S(1)}, f32[16,32,512]{2,1,0:T(8,128)}, u32[]{:S(2)}) copy-start(f32[16,32,512]{2,1,0:T(8,128)} %param.8) | copy-start | bytes 3145732
  2.2 5.0 %collective-permute-start.1 = (bf16[32,512]{1,0:T(8,128)(2,1)S(1)}, bf16[32,512]{1,0:T(8,128)(2,1)S(1)}, u32[]{:S(2)}, u32[]{:S(2)}) collective-permute-start(bf16[32,512]{1,0:T(8,128)(2,1)S(1)} %get-tuple-element.11), channel_id=1, source_target_pairs={{0,4},{8,12},{4,0},{12,8},{1,5},{9,13},{5,1},{13,9},{2,6},{10,14},... | collective-permute-start | bytes 98312 | tf_op jit(solution)/shard_map/ppermute | solution.py:354
  5.3 1.9 %collective-permute-start = (bf16[32,512]{1,0:T(8,128)(2,1)S(1)}, bf16[32,512]{1,0:T(8,128)(2,1)S(1)}, u32[]{:S(2)}, u32[]{:S(2)}) collective-permute-start(bf16[32,512]{1,0:T(8,128)(2,1)S(1)} %get-tuple-element.12), channel_id=1, source_target_pairs={{4,8},{8,4},{5,9},{9,5},{6,10},{10,6},{7,11},{11,7},{20,24},{24,20... | collective-permute-start | bytes 98312 | tf_op jit(solution)/shard_map/ppermute | solution.py:354
  7.3 3.3 %collective-permute-start.3 = (bf16[32,512]{1,0:T(8,128)(2,1)S(1)}, bf16[32,512]{1,0:T(8,128)(2,1)S(1)}, u32[]{:S(2)}, u32[]{:S(2)}) collective-permute-start(bf16[32,512]{1,0:T(8,128)(2,1)S(1)} %get-tuple-element.17), channel_id=1, source_target_pairs={{0,1},{2,3},{1,0},{3,2},{4,5},{6,7},{5,4},{7,6},{8,9},{10,11},{9,8... | collective-permute-start | bytes 98312 | tf_op jit(solution)/shard_map/ppermute | solution.py:354
  7.4 3.3 %copy-start.2 = (f32[16,32,512]{2,1,0:T(8,128)S(1)}, f32[16,32,512]{2,1,0:T(8,128)}, u32[]{:S(2)}) copy-start(f32[16,32,512]{2,1,0:T(8,128)} %param.8) | copy-start | bytes 3145732
  7.4 3.3 %copy-start.3 = (bf16[2048,512]{1,0:T(8,128)(2,1)S(1)}, bf16[2048,512]{1,0:T(8,128)(2,1)}, u32[]{:S(2)}) copy-start(bf16[2048,512]{1,0:T(8,128)(2,1)} %w_project_ref.1) | copy-start | bytes 6291460
  7.4 3.3 %copy-start.6 = (bf16[512,512]{1,0:T(8,128)(2,1)S(1)}, bf16[512,512]{1,0:T(8,128)(2,1)}, u32[]{:S(2)}) copy-start(bf16[512,512]{1,0:T(8,128)(2,1)} %constant.31.clone.perm_ref) | copy-start | bytes 1572868
  7.4 3.3 %copy-start.7 = (f32[3,3,2048]{2,1,0:T(4,128)S(1)}, f32[3,3,2048]{2,1,0:T(4,128)}, u32[]{:S(2)}) copy-start(f32[3,3,2048]{2,1,0:T(4,128)} %depth_ref.1) | copy-start | bytes 221188
  7.5 3.2 %collective-permute-start.2 = (bf16[32,512]{1,0:T(8,128)(2,1)S(1)}, bf16[32,512]{1,0:T(8,128)(2,1)S(1)}, u32[]{:S(2)}, u32[]{:S(2)}) collective-permute-start(bf16[32,512]{1,0:T(8,128)(2,1)S(1)} %get-tuple-element.18), channel_id=1, source_target_pairs={{1,2},{2,1},{5,6},{6,5},{9,10},{10,9},{13,14},{14,13},{17,18},{18,... | collective-permute-start | bytes 98312 | tf_op jit(solution)/shard_map/ppermute | solution.py:354
  10.7 33.8 %copy-start.8 = (bf16[512,1536]{1,0:T(8,128)(2,1)S(1)}, bf16[512,1536]{1,0:T(8,128)(2,1)}, u32[]{:S(2)}) copy-start(bf16[512,1536]{1,0:T(8,128)(2,1)} %weight_ref.4) | copy-start | bytes 4718596
  44.5 22.9 %copy-start.4 = (bf16[512,512]{1,0:T(8,128)(2,1)S(1)}, bf16[512,512]{1,0:T(8,128)(2,1)}, u32[]{:S(2)}) copy-start(bf16[512,512]{1,0:T(8,128)(2,1)} %weight_ref.5) | copy-start | bytes 1572868
  44.5 22.9 %copy-start.5 = (bf16[512,512]{1,0:T(8,128)(2,1)S(1)}, bf16[512,512]{1,0:T(8,128)(2,1)}, u32[]{:S(2)}) copy-start(bf16[512,512]{1,0:T(8,128)(2,1)} %constant.32.clone.back_ref) | copy-start | bytes 1572868

commit v3 on v2

--- a/solution.py
+++ b/solution.py
@@ -23,10 +23,10 @@
     return centred * lax.rsqrt(variance + 1e-05)
 
 
-def gelu(x):
+def gelu_of_half(half):
     scale = math.sqrt(2.0 / math.pi)
-    half = 0.5 * x
-    return half + half * jnp.tanh(x * (scale + (scale * 0.044715) * (x * x)))
+    inner = half * (2.0 * scale + (8.0 * scale * 0.044715) * (half * half))
+    return half + half * jnp.tanh(inner)
 
 
 def matmul(a, b):
@@ -53,148 +53,182 @@
     return pl.BlockSpec(memory_space=pltpu.VMEM)
 
 
-def norm_kernel(field_ref, normed_ref):
-    normed_ref[...] = layer_norm(field_ref[...]).astype(jnp.bfloat16)
-
-
-def norm(field):
+def half_norm(inputs):
+    return (layer_norm(inputs) * 0.5).astype(jnp.bfloat16)
+
+
+def edge_kernel(edge_ref, out_ref):
+    out_ref[...] = half_norm(edge_ref[...])
+
+
+def norm_edges(edges):
+    return pl.pallas_call(
+        edge_kernel,
+        in_specs=[vmem()],
+        out_specs=vmem(),
+        out_shape=jax.ShapeDtypeStruct(edges.shape, jnp.bfloat16),
+        compiler_params=pltpu.CompilerParams(vmem_limit_bytes=8 * MIB),
+        cost_estimate=pl.CostEstimate(
+            flops=8 * edges.size, bytes_accessed=6 * edges.size, transcendentals=edges.shape[0]
+        ),
+        name="norm_edges",
+    )(edges)
+
+
+def padded_rows(tokens):
+    return tokens + 16
+
+
+def expand_kernel(field_ref, weight_ref, normed_ref, out_ref):
+    tokens = normed_ref.shape[0]
+    width = weight_ref.shape[1]
+    tile = divisor(width, 512, LANES)
+    step = divisor(tokens, 128, 16)
+    starts = range(0, tokens, step)
+    for start in starts:
+        normed_ref[start : start + step, :] = half_norm(field_ref[start : start + step, :])
+
+    def body(index, carry):
+        lanes = pl.ds(pl.multiple_of(index * tile, tile), tile)
+        for start in starts:
+            made = gelu_of_half(
+                matmul(normed_ref[start : start + step, :], weight_ref[:, lanes])
+            )
+            for sub in range(tile // LANES):
+                row = (index * (tile // LANES) + sub) * padded_rows(tokens) + 8 + start
+                out_ref[pl.ds(pl.multiple_of(row, 8), step), :] = made[
+                    :, sub * LANES : (sub + 1) * LANES
+                ]
+        return carry
+
+    lax.fori_loop(0, width // tile, body, 0)
+
+
+def expand(field, w_expand):
     tokens, channels = field.shape
-    step = divisor(tokens, 128, 16)
-    return pl.pallas_call(
-        norm_kernel,
-        grid=(tokens // step,),
-        in_specs=[pl.BlockSpec((step, channels), lambda i: (i, 0))],
-        out_specs=pl.BlockSpec((step, channels), lambda i: (i, 0)),
-        out_shape=jax.ShapeDtypeStruct((tokens, channels), jnp.bfloat16),
-        compiler_params=pltpu.CompilerParams(vmem_limit_bytes=16 * MIB),
-        cost_estimate=pl.CostEstimate(
-            flops=8 * tokens * channels, bytes_accessed=6 * tokens * channels, transcendentals=tokens
-        ),
-        name="norm",
-    )(field)
-
-
-def expand_kernel(normed_ref, weight_ref, out_ref):
-    tokens = out_ref.shape[0]
-    step = divisor(tokens, 128, 16)
-    for start in range(0, tokens, step):
-        rows = slice(start, start + step)
-        out_ref[rows, :] = gelu(matmul(normed_ref[rows, :], weight_ref[...])).astype(jnp.bfloat16)
-
-
-def expand(normed, w_expand):
-    tokens, channels = normed.shape
     width = w_expand.shape[1]
-    tile = divisor(width, 512, LANES)
     return pl.pallas_call(
         expand_kernel,
-        grid=(width // tile,),
-        in_specs=[vmem(), pl.BlockSpec((channels, tile), lambda j: (0, j))],
-        out_specs=pl.BlockSpec((tokens, tile), lambda j: (0, j)),
-        out_shape=jax.ShapeDtypeStruct((tokens, width), jnp.bfloat16),
+        in_specs=[vmem()] * 2,
+        out_specs=[vmem()] * 2,
+        out_shape=[
+            jax.ShapeDtypeStruct((tokens, channels), jnp.bfloat16),
+            jax.ShapeDtypeStruct((width // LANES * padded_rows(tokens), LANES), jnp.float32),
+        ],
         compiler_params=pltpu.CompilerParams(vmem_limit_bytes=16 * MIB),
         cost_estimate=pl.CostEstimate(
             flops=2 * tokens * channels * width,
-            bytes_accessed=tokens * channels * 2 + channels * width * 2 + tokens * width * 2,
+            bytes_accessed=tokens * channels * 6 + channels * width * 2 + tokens * width * 4,
             transcendentals=tokens * width,
         ),
         name="expand",
-    )(normed, w_expand)
+    )(field, w_expand)
 
 
 def mix_kernel(
     expanded_ref, field_ref, up_ref, down_ref, left_ref, right_ref, w_expand_ref, depth_ref,
-    w_project_ref, perm_ref, mixed_ref, grouped_ref, halo_ref, total_ref, even_ref, odd_ref,
-    *, rows, cols,
+    w_project_ref, perm_ref, mixed_ref, grouped_ref, total_ref, normed_ref,
+    even_ref, odd_ref, even_halo_ref, odd_halo_ref, *, rows, cols,
 ):
-    width = expanded_ref.shape[1]
+    tokens = rows * cols
+    width = w_expand_ref.shape[1]
     tile = even_ref.shape[1]
     slot = left_ref.shape[0]
-    left_start, right_start = 2 * cols, 2 * cols + slot
+    up_start, down_start, left_start = 8, 16 + cols, 24 + 2 * cols
+    right_start = left_start + slot
 
     edges = jnp.concatenate(
         [up_ref[...], down_ref[...], left_ref[...], right_ref[...]], axis=0
     )
 
-    def halo_body(index, carry):
+    def expand_halo(index, out_ref):
         lanes = pl.ds(pl.multiple_of(index * tile, tile), tile)
-        made = gelu(matmul(edges, w_expand_ref[:, lanes]))
-        halo_ref[:, lanes] = made.astype(jnp.bfloat16).astype(jnp.float32)
-        return carry
-
-    lax.fori_loop(0, width // tile, halo_body, 0)
+        made = gelu_of_half(matmul(edges, w_expand_ref[:, lanes]))
+        for sub in range(tile // LANES):
+            part = made[:, sub * LANES : (sub + 1) * LANES]
+            out_ref[sub, up_start : up_start + cols] = part[:cols]
+            out_ref[sub, down_start : down_start + cols] = part[cols : 2 * cols]
+            out_ref[sub, left_start : left_start + 2 * slot] = part[2 * cols :]
 
     position = lax.broadcasted_iota(jnp.int32, (8, LANES), 0)
     at_first = position == 0
     at_last = position == 7
 
-    def convolve(index, out_ref):
+    def convolve(index, out_ref, halo_ref):
         for sub in range(tile // LANES):
             lanes = pl.ds(pl.multiple_of(index * tile + sub * LANES, LANES), LANES)
-            taps = [[depth_ref[p, q : q + 1, lanes] for q in range(3)] for p in range(3)]
-            sides = []
-            for q, start in ((0, left_start), (2, right_start)):
-                sides.append(
-                    sum(taps[p][q] * halo_ref[start + p : start + p + rows, lanes] for p in range(3))
+            base = (index * (tile // LANES) + sub) * padded_rows(tokens) + 8
+            taps = [[0.5 * depth_ref[p, q : q + 1, lanes] for q in range(3)] for p in range(3)]
+            sums = {}
+            for y in range(-1, rows + 1):
+                if y < 0:
+                    parts = [halo_ref[sub, up_start + q : up_start + q + cols] for q in (-1, 0, 1)]
+                elif y == rows:
+                    parts = [
+                        halo_ref[sub, down_start + q : down_start + q + cols] for q in (-1, 0, 1)
+                    ]
+                else:
+                    parts = [
+                        expanded_ref[pl.ds(base + (y * cols + q), cols), :] for q in (-1, 0, 1)
+                    ]
+                left = halo_ref[sub, left_start + y + 1 : left_start + y + 2]
+                right = halo_ref[sub, right_start + y + 1 : right_start + y + 2]
+                parts[0] = jnp.concatenate(
+                    [jnp.where(at_first, left, parts[0][:8]), parts[0][8:]], axis=0
                 )
-
-            def row_of(y):
-                if y < 0:
-                    return halo_ref[:cols, lanes]
-                if y == rows:
-                    return halo_ref[cols : 2 * cols, lanes]
-                return expanded_ref[y * cols : (y + 1) * cols, lanes].astype(jnp.float32)
-
-            window = [row_of(-1), row_of(0), None]
-            for y in range(rows):
-                window[2] = row_of(y + 1)
-                summed = [
-                    taps[0][q] * window[0] + taps[1][q] * window[1] + taps[2][q] * window[2]
-                    for q in range(3)
-                ]
-                before = pltpu.roll(summed[0], 1, 0)
-                before = jnp.concatenate(
-                    [jnp.where(at_first, sides[0][y : y + 1], before[:8]), before[8:]], axis=0
+                parts[2] = jnp.concatenate(
+                    [parts[2][:-8], jnp.where(at_last, right, parts[2][-8:])], axis=0
                 )
-                after = pltpu.roll(summed[2], cols - 1, 0)
-                after = jnp.concatenate(
-                    [after[:-8], jnp.where(at_last, sides[1][y : y + 1], after[-8:])], axis=0
-                )
-                made = gelu(before + summed[1] + after).astype(jnp.bfloat16)
-                out_ref[y * cols : (y + 1) * cols, sub * LANES : (sub + 1) * LANES] = made
-                window = [window[1], window[2], None]
+                for p in range(3):
+                    target = y + 1 - p
+                    if 0 <= target < rows:
+                        for q in range(3):
+                            term = taps[p][q] * parts[q]
+                            sums[target] = sums[target] + term if target in sums else term
+                if y > 0:
+                    out_ref[
+                        (y - 1) * cols : y * cols, sub * LANES : (sub + 1) * LANES
+                    ] = gelu_of_half(sums.pop(y - 1)).astype(jnp.bfloat16)
 
     def project(index, in_ref):
         piece = pl.ds(pl.multiple_of(index * tile, tile), tile)
         total_ref[...] += matmul(in_ref[...], w_project_ref[piece, :])
 
     total_ref[...] = field_ref[...]
-    convolve(0, even_ref)
+    expand_halo(0, even_halo_ref)
+    expand_halo(1, odd_halo_ref)
+    convolve(0, even_ref, even_halo_ref)
 
     def body(index, carry):
         project(2 * index, even_ref)
-        convolve(2 * index + 1, odd_ref)
+        convolve(2 * index + 1, odd_ref, odd_halo_ref)
+        expand_halo(2 * index + 2, even_halo_ref)
         project(2 * index + 1, odd_ref)
-        convolve(2 * index + 2, even_ref)
+        convolve(2 * index + 2, even_ref, even_halo_ref)
+        expand_halo(2 * index + 3, odd_halo_ref)
         return carry
 
     pairs = width // tile // 2
     lax.fori_loop(0, pairs - 1, body, 0)
     project(2 * pairs - 2, even_ref)
-    convolve(2 * pairs - 1, odd_ref)
+    convolve(2 * pairs - 1, odd_ref, odd_halo_ref)
     project(2 * pairs - 1, odd_ref)
 
-    mixed = total_ref[...]
-    mixed_ref[...] = mixed
-    normed = layer_norm(mixed).astype(jnp.bfloat16)
-    grouped_ref[...] = matmul(perm_ref[...], normed).astype(jnp.bfloat16)
+    step = divisor(tokens, 128, 16)
+    for start in range(0, tokens, step):
+        piece = slice(start, start + step)
+        mixed = total_ref[piece, :]
+        mixed_ref[piece, :] = mixed
+        normed_ref[piece, :] = layer_norm(mixed).astype(jnp.bfloat16)
+    grouped_ref[...] = matmul(perm_ref[...], normed_ref[...]).astype(jnp.bfloat16)
 
 
 def mix(expanded, field, up, down, left, right, w_expand, depth_kernel, w_project, perm, rows, cols):
     tokens, channels = field.shape
-    width = expanded.shape[1]
+    width = w_expand.shape[1]
     tile = divisor(width // 2, 256, LANES)
     slot = left.shape[0]
+    halo = pltpu.VMEM((tile // LANES, 24 + 2 * cols + 2 * slot, LANES), jnp.float32)
     return pl.pallas_call(
         functools.partial(mix_kernel, rows=rows, cols=cols),
         in_specs=[vmem()] * 10,
@@ -204,15 +238,17 @@
             jax.ShapeDtypeStruct((tokens, channels), jnp.bfloat16),
         ],
         scratch_shapes=[
-            pltpu.VMEM((2 * cols + 2 * slot, width), jnp.float32),
             pltpu.VMEM((tokens, channels), jnp.float32),
+            pltpu.VMEM((tokens, channels), jnp.bfloat16),
             pltpu.VMEM((tokens, tile), jnp.bfloat16),
             pltpu.VMEM((tokens, tile), jnp.bfloat16),
+            halo,
+            halo,
         ],
         compiler_params=pltpu.CompilerParams(vmem_limit_bytes=16 * MIB),
         cost_estimate=pl.CostEstimate(
             flops=2 * tokens * channels * width,
-            bytes_accessed=tokens * channels * 10 + 4 * channels * width + tokens * width * 2,
+            bytes_accessed=tokens * channels * 10 + 4 * channels * width + tokens * width * 4,
             transcendentals=tokens * width,
         ),
         name="mix",
@@ -324,11 +360,21 @@
     return result
 
 
-def finish_kernel(attended_ref, back_ref, weight_ref, mixed_ref, out_ref):
-    step = out_ref.shape[0]
-    rows = pl.ds(pl.multiple_of(pl.program_id(0) * step, step), step)
-    restored = matmul(back_ref[rows, :], attended_ref[...]).astype(jnp.bfloat16)
-    out_ref[...] = mixed_ref[rows, :] + matmul(restored, weight_ref[...])
+def finish_kernel(attended_ref, back_ref, weight_ref, mixed_ref, out_ref, made_ref, sent):
+    tokens = mixed_ref.shape[0]
+    step = made_ref.shape[1]
+    copies = []
+    for index, start in enumerate(range(0, tokens, step)):
+        rows = slice(start, start + step)
+        restored = matmul(back_ref[rows, :], attended_ref[...]).astype(jnp.bfloat16)
+        made_ref[index] = mixed_ref[rows, :] + matmul(restored, weight_ref[...])
+        copy = pltpu.make_async_copy(
+            made_ref.at[index], out_ref.at[pl.ds(start, step)], sent.at[index]
+        )
+        copy.start()
+        copies.append(copy)
+    for copy in copies:
+        copy.wait()
 
 
 def finish(attended, back, w_out, mixed):
@@ -336,10 +382,13 @@
     step = divisor(tokens, 128, 16)
     return pl.pallas_call(
         finish_kernel,
-        grid=(tokens // step,),
         in_specs=[vmem()] * 4,
-        out_specs=pl.BlockSpec((step, channels), lambda i: (i, 0)),
+        out_specs=pl.BlockSpec(memory_space=pltpu.HBM),
         out_shape=jax.ShapeDtypeStruct((tokens, channels), jnp.float32),
+        scratch_shapes=[
+            pltpu.VMEM((tokens // step, step, channels), jnp.float32),
+            pltpu.SemaphoreType.DMA((tokens // step,)),
+        ],
         compiler_params=pltpu.CompilerParams(vmem_limit_bytes=16 * MIB),
         name="finish",
     )(attended, back, w_out, mixed)
@@ -383,9 +432,10 @@
     back = jnp.asarray(matrix.T, jnp.bfloat16)
 
     flat = field.reshape(tokens, channels)
-    normed = norm(flat)
-    up, down = exchange(normed[:cols], normed[tokens - cols :], "row")
-    expanded = expand(normed, w_expand)
+    edges = norm_edges(jnp.concatenate([field[0], field[rows - 1]], axis=0))
+    up, down = exchange(edges[:cols], edges[cols:], "row")
+    normed, expanded = expand(flat, w_expand)
+    up, down, normed = lax.optimization_barrier((up, down, normed))
     tile = normed.reshape(rows, cols, channels)
     spare = jnp.zeros((round_up(rows + 2, 16) - rows - 2, channels), jnp.bfloat16)
     first = jnp.concatenate([up[:1], tile[:, 0], down[:1], spare], axis=0)

time: 70.2 us -> 76.5 us (1.090)
  local copies, waits for them, and re-layouts: 1.57 us -> 12.5 us
  Pallas kernels: 18.7 us -> 14.8 us
    unnamed x18 -> x26, local copies, waits for them, and re-layouts: 1.42 us -> 10.5 us
    pallas_call x1, Pallas kernels: 8.35 us -> 5.69 us  [mix(): pl.pallas_call(functools.partial(mix_kernel, rows=rows, cols=cols), in_sp...]
    pallas_call x3, Pallas kernels: 5.8 us -> 4.58 us  [the longest x1 2.5 us: expand(): pl.pallas_call(expand_kernel, in_specs=[vmem()] * 2, out_specs=[vmem()] *...]
    slice x2, local copies, waits for them, and re-layouts: 0.07 us -> 1.04 us  [shards(): first = jnp.concatenate([up[:1], tile[:, 0], down[:1], spare], axis=0)]
    squeeze x0 -> x1, local copies, waits for them, and re-layouts: none -> 0.88 us  [shards(): edges = norm_edges(jnp.concatenate([field[0], field[rows - 1]], axis=0))]
where the time goes in v3:
time: 76.5 us; the launch traced here: 76 us
  blocking collectives  43.4 us (57%)
  Pallas kernels  14.8 us (19%)
  local copies, waits for them, and re-layouts  12.5 us (16%)
  starting transfers between devices  4.47 us (6%)
    all_to_all x1, blocking collectives, shards(): lax.all_to_all(grouped.reshape(devices, sets_local * members, channels),...  25 us
    all_to_all x1, blocking collectives, shards(): lax.all_to_all(attended.reshape(devices, sets_local * members, channels),...  18.4 us
    unnamed x26, local copies, waits for them, and re-layouts  10.5 us
    pallas_call x1, Pallas kernels, mix(): pl.pallas_call(functools.partial(mix_kernel, rows=rows, cols=cols), in_sp...  5.69 us
    pallas_call x1, Pallas kernels, attend(): pl.pallas_call(attend_kernel, in_specs=[vmem()] * 2, out_specs=vmem(), ou...  4.56 us
    ppermute x4, starting transfers between devices, swap(): return lax.ppermute(edge, axis, pairs + [(b, a) for a, b in pairs])  4.47 us
    pallas_call x1, Pallas kernels, expand(): pl.pallas_call(expand_kernel, in_specs=[vmem()] * 2, out_specs=[vmem()] *...  2.5 us
    pallas_call x1, Pallas kernels, finish(): pl.pallas_call(finish_kernel, in_specs=[vmem()] * 4, out_specs=pl.BlockSp...  1.89 us
  transfers between devices with their start and end apart: 4, of which 1 were waited for; matrix products, arithmetic and copies ran while one was open for 0% of the time, Pallas kernels for 3%

profile of v3, /device:TPU:0, one launch (start us, length us, event | category | flops | bytes accessed | tf_op | source)
XLA Modules:
  0.0 76.0 jit_solution(9975130343518208098)
XLA Ops:
  0.0 0.9 %slice_bitcast_fusion.1 = (f32[32,512]{1,0:T(8,128)S(1)}, f32[32,512]{1,0:T(8,128)S(1)}) fusion(f32[16,32,512]{2,1,0:T(8,128)} %param.8), kind=kLoop, calls=%fused_computation.2 | loop fusion | bytes 262144 | tf_op jit(solution)/shard_map/squeeze | solution.py:435
  0.9 0.2 norm_edges.1
  1.1 3.1 %collective-permute-start.1 = (bf16[32,512]{1,0:T(8,128)(2,1)S(1)}, bf16[32,512]{1,0:T(8,128)(2,1)S(1)}, u32[]{:S(2)}, u32[]{:S(2)}) collective-permute-start(bf16[32,512]{1,0:T(8,128)(2,1)S(1)} %get-tuple-element.27), channel_id=1, source_target_pairs={{0,4},{8,12},{4,0},{12,8},{1,5},{9,13},{5,1},{13,9},{2,6},{10,14},... | collective-permute-start | bytes 98312 | tf_op jit(solution)/shard_map/ppermute | solution.py:403
  4.2 0.7 collective-permute-start
  4.9 0.0 copy-start.2
  4.9 1.6 %copy-done.2 = bf16[512,2048]{1,0:T(8,128)(2,1)S(1)} copy-done((bf16[512,2048]{1,0:T(8,128)(2,1)S(1)}, bf16[512,2048]{1,0:T(8,128)(2,1)}, u32[]{:S(2)}) %copy-start.2) | copy-done | bytes 2097176
  6.5 1.2 %copy-done.5 = f32[16,32,512]{2,1,0:T(8,128)S(1)} copy-done((f32[16,32,512]{2,1,0:T(8,128)S(1)}, f32[16,32,512]{2,1,0:T(8,128)}, u32[]{:S(2)}) %copy-start.5) | copy-done | bytes 1048600
  7.7 2.5 %expand.1 = (bf16[512,512]{1,0:T(8,128)(2,1)S(1)}, f32[8448,128]{1,0:T(8,128)S(1)}) custom-call(f32[512,512]{1,0:T(8,128)S(1)} %bitcast.16, bf16[512,2048]{1,0:T(8,128)(2,1)S(1)} %copy-done.2), custom_call_target="tpu_custom_call" | custom-call | flops 1073741824 | bytes 7864320 | tf_op jit(solution)/shard_map/expand/pallas_call | solution.py:110
  10.2 2.0 %copy-done = f32[8448,128]{1,0:T(8,128)} copy-done((f32[8448,128]{1,0:T(8,128)}, f32[8448,128]{1,0:T(8,128)S(1)}, u32[]{:S(2)}) %copy-start) | copy-done | bytes 4325400
  12.2 0.8 %copy-done.11 = bf16[512,512]{1,0:T(8,128)(2,1)} copy-done((bf16[512,512]{1,0:T(8,128)(2,1)}, bf16[512,512]{1,0:T(8,128)(2,1)S(1)}, u32[]{:S(2)}) %copy-start.11) | copy-done | bytes 524312
  13.0 0.1 pad.7.clone
  13.1 1.0 %fusion = (bf16[16,1,512]{2,1,0:T(2,128)(2,1)S(1)}, bf16[16,1,512]{2,1,0:T(2,128)(2,1)S(1)}) fusion(bf16[16,32,512]{2,1,0:T(8,128)(2,1)} %bitcast.21), kind=kLoop, calls=%fused_computation.15 | loop fusion | bytes 65536 | tf_op jit(solution)/shard_map/slice | solution.py:441
  14.2 0.1 broadcast_select_fusion.2
  14.3 0.1 collective-permute-start.3
  14.3 0.7 collective-permute-start.2
  15.0 0.5 collective-permute-done.3
  15.6 2.2 %copy-done.1 = f32[8448,128]{1,0:T(8,128)S(1)} copy-done((f32[8448,128]{1,0:T(8,128)S(1)}, f32[8448,128]{1,0:T(8,128)}, u32[]{:S(2)}) %copy-start.1) | copy-done | bytes 4325400
  17.8 1.6 %copy-done.4 = bf16[2048,512]{1,0:T(8,128)(2,1)S(1)} copy-done((bf16[2048,512]{1,0:T(8,128)(2,1)S(1)}, bf16[2048,512]{1,0:T(8,128)(2,1)}, u32[]{:S(2)}) %copy-start.4) | copy-done | bytes 2097176
  19.4 1.0 %copy-done.9 = bf16[512,512]{1,0:T(8,128)(2,1)S(1)} copy-done((bf16[512,512]{1,0:T(8,128)(2,1)S(1)}, bf16[512,512]{1,0:T(8,128)(2,1)}, u32[]{:S(2)}) %copy-start.9) | copy-done | bytes 524312
  20.4 5.7 %mix.1 = (f32[512,512]{1,0:T(8,128)S(1)}, bf16[512,512]{1,0:T(8,128)(2,1)S(1)}) custom-call(f32[8448,128]{1,0:T(8,128)S(1)} %copy-done.1, f32[512,512]{1,0:T(8,128)S(1)} %bitcast.17, bf16[32,512]{1,0:T(8,128)(2,1)S(1)} %get-tuple-element.14.up_ref, bf16[32,512]{1,0:T(8,128)(2,1)S(1)} %get-tuple-element.15.down_ref, ...), custom_call_target="tpu_custom_call" | custom-call | flops 1073741824 | bytes 11010048 | tf_op jit(solution)/shard_map/mix/pallas_call | solution.py:232
  26.1 25.0 %all_to_all.10 = bf16[16,32,512]{2,1,0:T(8,128)(2,1)S(1)} all-to-all(bf16[16,32,512]{2,1,0:T(8,128)(2,1)S(1)} %bitcast.18), channel_id=1, replica_groups=mesh['field'=2,'row'=4,'col'=4] {'row','col'}, dimensions={0} | all-to-all | bytes 1048576 | tf_op jit(solution)/shard_map/all_to_all | solution.py:447
  51.2 4.6 %attend.1 = bf16[16,2,16,512]{3,2,1,0:T(8,128)(2,1)S(1)} custom-call(bf16[16,2,16,512]{3,2,1,0:T(8,128)(2,1)S(1)} %bitcast.19, bf16[512,1536]{1,0:T(8,128)(2,1)S(1)} %copy-done.12), custom_call_target="tpu_custom_call" | custom-call | flops 1073741824 | bytes 2621440 | tf_op jit(solution)/shard_map/attend/pallas_call | solution.py:337
  55.7 18.4 %all_to_all.11 = bf16[16,32,512]{2,1,0:T(8,128)(2,1)S(1)} all-to-all(bf16[16,32,512]{2,1,0:T(8,128)(2,1)S(1)} %bitcast.20), channel_id=1, replica_groups=mesh['field'=2,'row'=4,'col'=4] {'row','col'}, dimensions={0} | all-to-all | bytes 1048576 | tf_op jit(solution)/shard_map/all_to_all | solution.py:451
  74.1 1.9 %finish.1 = f32[512,512]{1,0:T(8,128)} custom-call(bf16[512,512]{1,0:T(8,128)(2,1)S(1)} %bitcast.15, bf16[512,512]{1,0:T(8,128)(2,1)S(1)} %copy-done.8, bf16[512,512]{1,0:T(8,128)(2,1)S(1)} %copy-done.7, f32[512,512]{1,0:T(8,128)S(1)} %get-tuple-element.18.mixed_ref), custom_call_target="tpu_custom_call" | custom-call | tf_op jit(solution)/shard_map/finish/pallas_call | solution.py:383
  (28 shorter events, 0.1 us)
Async XLA Ops:
  1.1 12.0 %collective-permute-start.1 = (bf16[32,512]{1,0:T(8,128)(2,1)S(1)}, bf16[32,512]{1,0:T(8,128)(2,1)S(1)}, u32[]{:S(2)}, u32[]{:S(2)}) collective-permute-start(bf16[32,512]{1,0:T(8,128)(2,1)S(1)} %get-tuple-element.27), channel_id=1, source_target_pairs={{0,4},{8,12},{4,0},{12,8},{1,5},{9,13},{5,1},{13,9},{2,6},{10,14},... | collective-permute-start | bytes 98312 | tf_op jit(solution)/shard_map/ppermute | solution.py:403
  4.2 8.9 %collective-permute-start = (bf16[32,512]{1,0:T(8,128)(2,1)S(1)}, bf16[32,512]{1,0:T(8,128)(2,1)S(1)}, u32[]{:S(2)}, u32[]{:S(2)}) collective-permute-start(bf16[32,512]{1,0:T(8,128)(2,1)S(1)} %get-tuple-element.28), channel_id=1, source_target_pairs={{4,8},{8,4},{5,9},{9,5},{6,10},{10,6},{7,11},{11,7},{20,24},{24,20... | collective-permute-start | bytes 98312 | tf_op jit(solution)/shard_map/ppermute | solution.py:403
  4.9 1.6 %copy-start.2 = (bf16[512,2048]{1,0:T(8,128)(2,1)S(1)}, bf16[512,2048]{1,0:T(8,128)(2,1)}, u32[]{:S(2)}) copy-start(bf16[512,2048]{1,0:T(8,128)(2,1)} %w_expand_ref.1) | copy-start | bytes 6291460
  6.5 1.2 %copy-start.5 = (f32[16,32,512]{2,1,0:T(8,128)S(1)}, f32[16,32,512]{2,1,0:T(8,128)}, u32[]{:S(2)}) copy-start(f32[16,32,512]{2,1,0:T(8,128)} %param.8) | copy-start | bytes 3145732
  7.7 7.9 %copy-start.3 = (bf16[512,2048]{1,0:T(8,128)(2,1)S(1)}, bf16[512,2048]{1,0:T(8,128)(2,1)}, u32[]{:S(2)}) copy-start(bf16[512,2048]{1,0:T(8,128)(2,1)} %w_expand_ref.1) | copy-start | bytes 6291460
  7.7 7.9 %copy-start.6 = (f32[16,32,512]{2,1,0:T(8,128)S(1)}, f32[16,32,512]{2,1,0:T(8,128)}, u32[]{:S(2)}) copy-start(f32[16,32,512]{2,1,0:T(8,128)} %param.8) | copy-start | bytes 3145732
  7.7 7.9 %copy-start.10 = (f32[3,3,2048]{2,1,0:T(4,128)S(1)}, f32[3,3,2048]{2,1,0:T(4,128)}, u32[]{:S(2)}) copy-start(f32[3,3,2048]{2,1,0:T(4,128)} %depth_ref.1) | copy-start | bytes 221188
  10.2 2.0 %copy-start = (f32[8448,128]{1,0:T(8,128)}, f32[8448,128]{1,0:T(8,128)S(1)}, u32[]{:S(2)}) copy-start(f32[8448,128]{1,0:T(8,128)S(1)} %get-tuple-element.12.expanded_ref) | copy-start | bytes 12976132
  12.2 0.8 %copy-start.11 = (bf16[512,512]{1,0:T(8,128)(2,1)}, bf16[512,512]{1,0:T(8,128)(2,1)S(1)}, u32[]{:S(2)}) copy-start(bf16[512,512]{1,0:T(8,128)(2,1)S(1)} %get-tuple-element.16) | copy-start | bytes 1572868
  14.3 1.3 %collective-permute-start.3 = (bf16[32,512]{1,0:T(8,128)(2,1)S(1)}, bf16[32,512]{1,0:T(8,128)(2,1)S(1)}, u32[]{:S(2)}, u32[]{:S(2)}) collective-permute-start(bf16[32,512]{1,0:T(8,128)(2,1)S(1)} %get-tuple-element.29), channel_id=1, source_target_pairs={{0,1},{2,3},{1,0},{3,2},{4,5},{6,7},{5,4},{7,6},{8,9},{10,11},{9,8... | collective-permute-start | bytes 98312 | tf_op jit(solution)/shard_map/ppermute | solution.py:403
  14.3 1.2 %collective-permute-start.2 = (bf16[32,512]{1,0:T(8,128)(2,1)S(1)}, bf16[32,512]{1,0:T(8,128)(2,1)S(1)}, u32[]{:S(2)}, u32[]{:S(2)}) collective-permute-start(bf16[32,512]{1,0:T(8,128)(2,1)S(1)} %get-tuple-element.30), channel_id=1, source_target_pairs={{1,2},{2,1},{5,6},{6,5},{9,10},{10,9},{13,14},{14,13},{17,18},{18,... | collective-permute-start | bytes 98312 | tf_op jit(solution)/shard_map/ppermute | solution.py:403
  15.6 2.2 %copy-start.1 = (f32[8448,128]{1,0:T(8,128)S(1)}, f32[8448,128]{1,0:T(8,128)}, u32[]{:S(2)}) copy-start(f32[8448,128]{1,0:T(8,128)} %copy-done) | copy-start | bytes 12976132
  17.8 1.6 %copy-start.4 = (bf16[2048,512]{1,0:T(8,128)(2,1)S(1)}, bf16[2048,512]{1,0:T(8,128)(2,1)}, u32[]{:S(2)}) copy-start(bf16[2048,512]{1,0:T(8,128)(2,1)} %w_project_ref.1) | copy-start | bytes 6291460
  19.4 1.0 %copy-start.9 = (bf16[512,512]{1,0:T(8,128)(2,1)S(1)}, bf16[512,512]{1,0:T(8,128)(2,1)}, u32[]{:S(2)}) copy-start(bf16[512,512]{1,0:T(8,128)(2,1)} %constant.31.clone.perm_ref) | copy-start | bytes 1572868
  20.4 30.7 %copy-start.12 = (bf16[512,1536]{1,0:T(8,128)(2,1)S(1)}, bf16[512,1536]{1,0:T(8,128)(2,1)}, u32[]{:S(2)}) copy-start(bf16[512,1536]{1,0:T(8,128)(2,1)} %weight_ref.4) | copy-start | bytes 4718596
  51.2 22.9 %copy-start.7 = (bf16[512,512]{1,0:T(8,128)(2,1)S(1)}, bf16[512,512]{1,0:T(8,128)(2,1)}, u32[]{:S(2)}) copy-start(bf16[512,512]{1,0:T(8,128)(2,1)} %weight_ref.5) | copy-start | bytes 1572868
  51.2 22.9 %copy-start.8 = (bf16[512,512]{1,0:T(8,128)(2,1)S(1)}, bf16[512,512]{1,0:T(8,128)(2,1)}, u32[]{:S(2)}) copy-start(bf16[512,512]{1,0:T(8,128)(2,1)} %constant.32.clone.back_ref) | copy-start | bytes 1572868

commit v4 on v3

--- a/solution.py
+++ b/solution.py
@@ -69,7 +69,7 @@
         out_shape=jax.ShapeDtypeStruct(edges.shape, jnp.bfloat16),
         compiler_params=pltpu.CompilerParams(vmem_limit_bytes=8 * MIB),
         cost_estimate=pl.CostEstimate(
-            flops=8 * edges.size, bytes_accessed=6 * edges.size, transcendentals=edges.shape[0]
+            flops=10**10, bytes_accessed=6 * edges.size, transcendentals=edges.shape[0]
         ),
         name="norm_edges",
     )(edges)

time: 76.5 us -> 73.6 us (0.962)
  local copies, waits for them, and re-layouts: 12.5 us -> 9.67 us
    unnamed x26 -> x22, local copies, waits for them, and re-layouts: 10.5 us -> 7.67 us
where the time goes in v4:
time: 73.6 us; the launch traced here: 73.2 us
  blocking collectives  43.4 us (59%)
  Pallas kernels  14.8 us (20%)
  local copies, waits for them, and re-layouts  9.67 us (13%)
  starting transfers between devices  4.47 us (6%)
    all_to_all x1, blocking collectives, shards(): lax.all_to_all(grouped.reshape(devices, sets_local * members, channels),...  25 us
    all_to_all x1, blocking collectives, shards(): lax.all_to_all(attended.reshape(devices, sets_local * members, channels),...  18.4 us
    unnamed x22, local copies, waits for them, and re-layouts  7.67 us
    pallas_call x1, Pallas kernels, mix(): pl.pallas_call(functools.partial(mix_kernel, rows=rows, cols=cols), in_sp...  5.7 us
    pallas_call x1, Pallas kernels, attend(): pl.pallas_call(attend_kernel, in_specs=[vmem()] * 2, out_specs=vmem(), ou...  4.56 us
    ppermute x4, starting transfers between devices, swap(): return lax.ppermute(edge, axis, pairs + [(b, a) for a, b in pairs])  4.47 us
    pallas_call x1, Pallas kernels, expand(): pl.pallas_call(expand_kernel, in_specs=[vmem()] * 2, out_specs=[vmem()] *...  2.5 us
    pallas_call x1, Pallas kernels, finish(): pl.pallas_call(finish_kernel, in_specs=[vmem()] * 4, out_specs=pl.BlockSp...  1.89 us
  transfers between devices with their start and end apart: 4, of which 1 were waited for; matrix products, arithmetic and copies ran while one was open for 0% of the time, Pallas kernels for 3%

profile of v4, /device:TPU:0, one launch (start us, length us, event | category | flops | bytes accessed | tf_op | source)
XLA Modules:
  0.0 73.2 jit_solution(12087061025501631071)
XLA Ops:
  0.0 0.9 %slice_bitcast_fusion.1 = (f32[32,512]{1,0:T(8,128)S(1)}, f32[32,512]{1,0:T(8,128)S(1)}) fusion(f32[16,32,512]{2,1,0:T(8,128)} %param.8), kind=kLoop, calls=%fused_computation.2 | loop fusion | bytes 262144 | tf_op jit(solution)/shard_map/squeeze | solution.py:435
  0.9 0.0 copy-start.2
  0.9 0.0 copy-start.4
  0.9 0.2 norm_edges.1
  1.1 3.1 %collective-permute-start.1 = (bf16[32,512]{1,0:T(8,128)(2,1)S(1)}, bf16[32,512]{1,0:T(8,128)(2,1)S(1)}, u32[]{:S(2)}, u32[]{:S(2)}) collective-permute-start(bf16[32,512]{1,0:T(8,128)(2,1)S(1)} %get-tuple-element.27), channel_id=1, source_target_pairs={{0,4},{8,12},{4,0},{12,8},{1,5},{9,13},{5,1},{13,9},{2,6},{10,14},... | collective-permute-start | bytes 98312 | tf_op jit(solution)/shard_map/ppermute | solution.py:403
  4.2 0.7 collective-permute-start
  4.9 0.0 copy-start.8
  4.9 2.5 %expand.1 = (bf16[512,512]{1,0:T(8,128)(2,1)S(1)}, f32[8448,128]{1,0:T(8,128)S(1)}) custom-call(f32[512,512]{1,0:T(8,128)S(1)} %bitcast.16, bf16[512,2048]{1,0:T(8,128)(2,1)S(1)} %copy-done.2), custom_call_target="tpu_custom_call" | custom-call | flops 1073741824 | bytes 7864320 | tf_op jit(solution)/shard_map/expand/pallas_call | solution.py:110
  7.4 2.0 %copy-done = f32[8448,128]{1,0:T(8,128)} copy-done((f32[8448,128]{1,0:T(8,128)}, f32[8448,128]{1,0:T(8,128)S(1)}, u32[]{:S(2)}) %copy-start) | copy-done | bytes 4325400
  9.4 0.8 %copy-done.9 = bf16[512,512]{1,0:T(8,128)(2,1)} copy-done((bf16[512,512]{1,0:T(8,128)(2,1)}, bf16[512,512]{1,0:T(8,128)(2,1)S(1)}, u32[]{:S(2)}) %copy-start.9) | copy-done | bytes 524312
  10.2 0.1 pad.7.clone
  10.3 1.0 %fusion = (bf16[16,1,512]{2,1,0:T(2,128)(2,1)S(1)}, bf16[16,1,512]{2,1,0:T(2,128)(2,1)S(1)}) fusion(bf16[16,32,512]{2,1,0:T(8,128)(2,1)} %bitcast.21), kind=kLoop, calls=%fused_computation.15 | loop fusion | bytes 65536 | tf_op jit(solution)/shard_map/slice | solution.py:441
  11.4 0.1 broadcast_select_fusion.2
  11.5 0.1 collective-permute-start.3
  11.6 0.7 collective-permute-start.2
  12.2 0.5 collective-permute-done.3
  12.8 2.2 %copy-done.1 = f32[8448,128]{1,0:T(8,128)S(1)} copy-done((f32[8448,128]{1,0:T(8,128)S(1)}, f32[8448,128]{1,0:T(8,128)}, u32[]{:S(2)}) %copy-start.1) | copy-done | bytes 4325400
  15.0 1.6 %copy-done.3 = bf16[2048,512]{1,0:T(8,128)(2,1)S(1)} copy-done((bf16[2048,512]{1,0:T(8,128)(2,1)S(1)}, bf16[2048,512]{1,0:T(8,128)(2,1)}, u32[]{:S(2)}) %copy-start.3) | copy-done | bytes 2097176
  16.6 1.0 %copy-done.7 = bf16[512,512]{1,0:T(8,128)(2,1)S(1)} copy-done((bf16[512,512]{1,0:T(8,128)(2,1)S(1)}, bf16[512,512]{1,0:T(8,128)(2,1)}, u32[]{:S(2)}) %copy-start.7) | copy-done | bytes 524312
  17.6 5.7 %mix.1 = (f32[512,512]{1,0:T(8,128)S(1)}, bf16[512,512]{1,0:T(8,128)(2,1)S(1)}) custom-call(f32[8448,128]{1,0:T(8,128)S(1)} %copy-done.1, f32[512,512]{1,0:T(8,128)S(1)} %bitcast.17, bf16[32,512]{1,0:T(8,128)(2,1)S(1)} %get-tuple-element.14.up_ref, bf16[32,512]{1,0:T(8,128)(2,1)S(1)} %get-tuple-element.15.down_ref, ...), custom_call_target="tpu_custom_call" | custom-call | flops 1073741824 | bytes 11010048 | tf_op jit(solution)/shard_map/mix/pallas_call | solution.py:232
  23.3 25.0 %all_to_all.10 = bf16[16,32,512]{2,1,0:T(8,128)(2,1)S(1)} all-to-all(bf16[16,32,512]{2,1,0:T(8,128)(2,1)S(1)} %bitcast.18), channel_id=1, replica_groups=mesh['field'=2,'row'=4,'col'=4] {'row','col'}, dimensions={0} | all-to-all | bytes 1048576 | tf_op jit(solution)/shard_map/all_to_all | solution.py:447
  48.4 4.6 %attend.1 = bf16[16,2,16,512]{3,2,1,0:T(8,128)(2,1)S(1)} custom-call(bf16[16,2,16,512]{3,2,1,0:T(8,128)(2,1)S(1)} %bitcast.19, bf16[512,1536]{1,0:T(8,128)(2,1)S(1)} %copy-done.10), custom_call_target="tpu_custom_call" | custom-call | flops 1073741824 | bytes 2621440 | tf_op jit(solution)/shard_map/attend/pallas_call | solution.py:337
  53.0 18.4 %all_to_all.11 = bf16[16,32,512]{2,1,0:T(8,128)(2,1)S(1)} all-to-all(bf16[16,32,512]{2,1,0:T(8,128)(2,1)S(1)} %bitcast.20), channel_id=1, replica_groups=mesh['field'=2,'row'=4,'col'=4] {'row','col'}, dimensions={0} | all-to-all | bytes 1048576 | tf_op jit(solution)/shard_map/all_to_all | solution.py:451
  71.3 1.9 %finish.1 = f32[512,512]{1,0:T(8,128)} custom-call(bf16[512,512]{1,0:T(8,128)(2,1)S(1)} %bitcast.15, bf16[512,512]{1,0:T(8,128)(2,1)S(1)} %copy-done.6, bf16[512,512]{1,0:T(8,128)(2,1)S(1)} %copy-done.5, f32[512,512]{1,0:T(8,128)S(1)} %get-tuple-element.18.mixed_ref), custom_call_target="tpu_custom_call" | custom-call | tf_op jit(solution)/shard_map/finish/pallas_call | solution.py:383
  (24 shorter events, 0.1 us)
Async XLA Ops:
  0.9 4.0 %copy-start.2 = (bf16[512,2048]{1,0:T(8,128)(2,1)S(1)}, bf16[512,2048]{1,0:T(8,128)(2,1)}, u32[]{:S(2)}) copy-start(bf16[512,2048]{1,0:T(8,128)(2,1)} %w_expand_ref.1) | copy-start | bytes 6291460
  0.9 4.0 %copy-start.4 = (f32[16,32,512]{2,1,0:T(8,128)S(1)}, f32[16,32,512]{2,1,0:T(8,128)}, u32[]{:S(2)}) copy-start(f32[16,32,512]{2,1,0:T(8,128)} %param.8) | copy-start | bytes 3145732
  1.1 9.2 %collective-permute-start.1 = (bf16[32,512]{1,0:T(8,128)(2,1)S(1)}, bf16[32,512]{1,0:T(8,128)(2,1)S(1)}, u32[]{:S(2)}, u32[]{:S(2)}) collective-permute-start(bf16[32,512]{1,0:T(8,128)(2,1)S(1)} %get-tuple-element.27), channel_id=1, source_target_pairs={{0,4},{8,12},{4,0},{12,8},{1,5},{9,13},{5,1},{13,9},{2,6},{10,14},... | collective-permute-start | bytes 98312 | tf_op jit(solution)/shard_map/ppermute | solution.py:403
  4.2 6.1 %collective-permute-start = (bf16[32,512]{1,0:T(8,128)(2,1)S(1)}, bf16[32,512]{1,0:T(8,128)(2,1)S(1)}, u32[]{:S(2)}, u32[]{:S(2)}) collective-permute-start(bf16[32,512]{1,0:T(8,128)(2,1)S(1)} %get-tuple-element.28), channel_id=1, source_target_pairs={{4,8},{8,4},{5,9},{9,5},{6,10},{10,6},{7,11},{11,7},{20,24},{24,20... | collective-permute-start | bytes 98312 | tf_op jit(solution)/shard_map/ppermute | solution.py:403
  4.9 7.9 %copy-start.8 = (f32[3,3,2048]{2,1,0:T(4,128)S(1)}, f32[3,3,2048]{2,1,0:T(4,128)}, u32[]{:S(2)}) copy-start(f32[3,3,2048]{2,1,0:T(4,128)} %depth_ref.1) | copy-start | bytes 221188
  7.4 2.0 %copy-start = (f32[8448,128]{1,0:T(8,128)}, f32[8448,128]{1,0:T(8,128)S(1)}, u32[]{:S(2)}) copy-start(f32[8448,128]{1,0:T(8,128)S(1)} %get-tuple-element.12.expanded_ref) | copy-start | bytes 12976132
  9.4 0.8 %copy-start.9 = (bf16[512,512]{1,0:T(8,128)(2,1)}, bf16[512,512]{1,0:T(8,128)(2,1)S(1)}, u32[]{:S(2)}) copy-start(bf16[512,512]{1,0:T(8,128)(2,1)S(1)} %get-tuple-element.16) | copy-start | bytes 1572868
  11.5 1.3 %collective-permute-start.3 = (bf16[32,512]{1,0:T(8,128)(2,1)S(1)}, bf16[32,512]{1,0:T(8,128)(2,1)S(1)}, u32[]{:S(2)}, u32[]{:S(2)}) collective-permute-start(bf16[32,512]{1,0:T(8,128)(2,1)S(1)} %get-tuple-element.29), channel_id=1, source_target_pairs={{0,1},{2,3},{1,0},{3,2},{4,5},{6,7},{5,4},{7,6},{8,9},{10,11},{9,8... | collective-permute-start | bytes 98312 | tf_op jit(solution)/shard_map/ppermute | solution.py:403
  11.6 1.2 %collective-permute-start.2 = (bf16[32,512]{1,0:T(8,128)(2,1)S(1)}, bf16[32,512]{1,0:T(8,128)(2,1)S(1)}, u32[]{:S(2)}, u32[]{:S(2)}) collective-permute-start(bf16[32,512]{1,0:T(8,128)(2,1)S(1)} %get-tuple-element.30), channel_id=1, source_target_pairs={{1,2},{2,1},{5,6},{6,5},{9,10},{10,9},{13,14},{14,13},{17,18},{18,... | collective-permute-start | bytes 98312 | tf_op jit(solution)/shard_map/ppermute | solution.py:403
  12.8 2.2 %copy-start.1 = (f32[8448,128]{1,0:T(8,128)S(1)}, f32[8448,128]{1,0:T(8,128)}, u32[]{:S(2)}) copy-start(f32[8448,128]{1,0:T(8,128)} %copy-done) | copy-start | bytes 12976132
  15.0 1.6 %copy-start.3 = (bf16[2048,512]{1,0:T(8,128)(2,1)S(1)}, bf16[2048,512]{1,0:T(8,128)(2,1)}, u32[]{:S(2)}) copy-start(bf16[2048,512]{1,0:T(8,128)(2,1)} %w_project_ref.1) | copy-start | bytes 6291460
  16.6 1.0 %copy-start.7 = (bf16[512,512]{1,0:T(8,128)(2,1)S(1)}, bf16[512,512]{1,0:T(8,128)(2,1)}, u32[]{:S(2)}) copy-start(bf16[512,512]{1,0:T(8,128)(2,1)} %constant.31.clone.perm_ref) | copy-start | bytes 1572868
  17.6 30.7 %copy-start.10 = (bf16[512,1536]{1,0:T(8,128)(2,1)S(1)}, bf16[512,1536]{1,0:T(8,128)(2,1)}, u32[]{:S(2)}) copy-start(bf16[512,1536]{1,0:T(8,128)(2,1)} %weight_ref.4) | copy-start | bytes 4718596
  48.4 22.9 %copy-start.5 = (bf16[512,512]{1,0:T(8,128)(2,1)S(1)}, bf16[512,512]{1,0:T(8,128)(2,1)}, u32[]{:S(2)}) copy-start(bf16[512,512]{1,0:T(8,128)(2,1)} %weight_ref.5) | copy-start | bytes 1572868
  48.4 22.9 %copy-start.6 = (bf16[512,512]{1,0:T(8,128)(2,1)S(1)}, bf16[512,512]{1,0:T(8,128)(2,1)}, u32[]{:S(2)}) copy-start(bf16[512,512]{1,0:T(8,128)(2,1)} %constant.32.clone.back_ref) | copy-start | bytes 1572868

commit v5 on v4

--- a/solution.py
+++ b/solution.py
@@ -57,36 +57,37 @@
     return (layer_norm(inputs) * 0.5).astype(jnp.bfloat16)
 
 
-def edge_kernel(edge_ref, out_ref):
-    out_ref[...] = half_norm(edge_ref[...])
-
-
-def norm_edges(edges):
+def half_norm_kernel(in_ref, out_ref):
+    rows = in_ref.shape[0]
+    step = divisor(rows, 128, 16)
+    for start in range(0, rows, step):
+        out_ref[start : start + step, :] = half_norm(in_ref[start : start + step, :])
+
+
+def half_norm_of(inputs, work):
     return pl.pallas_call(
-        edge_kernel,
+        half_norm_kernel,
         in_specs=[vmem()],
         out_specs=vmem(),
-        out_shape=jax.ShapeDtypeStruct(edges.shape, jnp.bfloat16),
+        out_shape=jax.ShapeDtypeStruct(inputs.shape, jnp.bfloat16),
         compiler_params=pltpu.CompilerParams(vmem_limit_bytes=8 * MIB),
         cost_estimate=pl.CostEstimate(
-            flops=10**10, bytes_accessed=6 * edges.size, transcendentals=edges.shape[0]
+            flops=work, bytes_accessed=6 * inputs.size, transcendentals=inputs.shape[0]
         ),
-        name="norm_edges",
-    )(edges)
+        name="half_norm",
+    )(inputs)
 
 
 def padded_rows(tokens):
     return tokens + 16
 
 
-def expand_kernel(field_ref, weight_ref, normed_ref, out_ref):
+def expand_kernel(normed_ref, weight_ref, out_ref):
     tokens = normed_ref.shape[0]
     width = weight_ref.shape[1]
     tile = divisor(width, 512, LANES)
     step = divisor(tokens, 128, 16)
     starts = range(0, tokens, step)
-    for start in starts:
-        normed_ref[start : start + step, :] = half_norm(field_ref[start : start + step, :])
 
     def body(index, carry):
         lanes = pl.ds(pl.multiple_of(index * tile, tile), tile)
@@ -104,25 +105,22 @@
     lax.fori_loop(0, width // tile, body, 0)
 
 
-def expand(field, w_expand):
-    tokens, channels = field.shape
+def expand(normed, w_expand):
+    tokens, channels = normed.shape
     width = w_expand.shape[1]
     return pl.pallas_call(
         expand_kernel,
         in_specs=[vmem()] * 2,
-        out_specs=[vmem()] * 2,
-        out_shape=[
-            jax.ShapeDtypeStruct((tokens, channels), jnp.bfloat16),
-            jax.ShapeDtypeStruct((width // LANES * padded_rows(tokens), LANES), jnp.float32),
-        ],
+        out_specs=vmem(),
+        out_shape=jax.ShapeDtypeStruct((width // LANES * padded_rows(tokens), LANES), jnp.float32),
         compiler_params=pltpu.CompilerParams(vmem_limit_bytes=16 * MIB),
         cost_estimate=pl.CostEstimate(
-            flops=2 * tokens * channels * width,
-            bytes_accessed=tokens * channels * 6 + channels * width * 2 + tokens * width * 4,
+            flops=10**10,
+            bytes_accessed=tokens * channels * 2 + channels * width * 2 + tokens * width * 4,
             transcendentals=tokens * width,
         ),
         name="expand",
-    )(field, w_expand)
+    )(normed, w_expand)
 
 
 def mix_kernel(
@@ -432,14 +430,15 @@
     back = jnp.asarray(matrix.T, jnp.bfloat16)
 
     flat = field.reshape(tokens, channels)
-    edges = norm_edges(jnp.concatenate([field[0], field[rows - 1]], axis=0))
+    edges = half_norm_of(jnp.concatenate([field[0], field[rows - 1]], axis=0), 10**10)
     up, down = exchange(edges[:cols], edges[cols:], "row")
-    normed, expanded = expand(flat, w_expand)
-    up, down, normed = lax.optimization_barrier((up, down, normed))
+    normed = half_norm_of(flat, 10**9)
     tile = normed.reshape(rows, cols, channels)
     spare = jnp.zeros((round_up(rows + 2, 16) - rows - 2, channels), jnp.bfloat16)
     first = jnp.concatenate([up[:1], tile[:, 0], down[:1], spare], axis=0)
     last = jnp.concatenate([up[cols - 1 :], tile[:, cols - 1], down[cols - 1 :], spare], axis=0)
+    normed, first, last = lax.optimization_barrier((normed, first, last))
+    expanded = expand(normed, w_expand)
     left, right = exchange(first, last, "col")
     mixed, grouped = mix(
         expanded, flat, up, down, left, right, w_expand, depth_kernel, w_project, perm, rows, cols

time: 73.6 us -> 65.5 us (0.89)
  local copies, waits for them, and re-layouts: 9.67 us -> 2.9 us
  blocking collectives: 43.4 us -> 38.9 us
  starting transfers between devices: 4.47 us -> 7.57 us
    unnamed x22 -> x20, local copies, waits for them, and re-layouts: 7.67 us -> 1.87 us
    all_to_all x1, blocking collectives: 25 us -> 20.6 us  [shards(): lax.all_to_all(grouped.reshape(devices, sets_local * members, channels),...]
    ppermute x4, starting transfers between devices: 4.47 us -> 7.57 us  [swap(): return lax.ppermute(edge, axis, pairs + [(b, a) for a, b in pairs])]
    slice x2, local copies, waits for them, and re-layouts: 1.04 us -> 0.07 us  [the longest x1 0.06 us: shards(): tile[:, cols - 1]]
    pallas_call x2 -> x3, Pallas kernels: 2.69 us -> 2.66 us  [the longest x1 2.15 us: expand(): pl.pallas_call(expand_kernel, in_specs=[vmem()] * 2, out_specs=vmem(), ou...]
  transfers between devices with their start and end apart: 4 -> 4, of which waited for: 1 -> 1; matrix products, arithmetic and copies ran while one was open for 0% -> 0% of each run, Pallas kernels for 3% -> 4%
where the time goes in v5:
time: 65.5 us; the launch traced here: 65.2 us
  blocking collectives  38.9 us (59%)
  Pallas kernels  14.8 us (23%)
  starting transfers between devices  7.57 us (12%)
  local copies, waits for them, and re-layouts  2.9 us (4%)
    all_to_all x1, blocking collectives, shards(): lax.all_to_all(grouped.reshape(devices, sets_local * members, channels),...  20.6 us
    all_to_all x1, blocking collectives, shards(): lax.all_to_all(attended.reshape(devices, sets_local * members, channels),...  18.4 us
    ppermute x4, starting transfers between devices, swap(): return lax.ppermute(edge, axis, pairs + [(b, a) for a, b in pairs])  7.57 us
    pallas_call x1, Pallas kernels, mix(): pl.pallas_call(functools.partial(mix_kernel, rows=rows, cols=cols), in_sp...  5.7 us
    pallas_call x1, Pallas kernels, attend(): pl.pallas_call(attend_kernel, in_specs=[vmem()] * 2, out_specs=vmem(), ou...  4.56 us
    pallas_call x1, Pallas kernels, expand(): pl.pallas_call(expand_kernel, in_specs=[vmem()] * 2, out_specs=vmem(), ou...  2.15 us
    pallas_call x1, Pallas kernels, finish(): pl.pallas_call(finish_kernel, in_specs=[vmem()] * 4, out_specs=pl.BlockSp...  1.9 us
    unnamed x20, local copies, waits for them, and re-layouts  1.87 us
  transfers between devices with their start and end apart: 4, of which 1 were waited for; matrix products, arithmetic and copies ran while one was open for 0% of the time, Pallas kernels for 4%

profile of v5, /device:TPU:0, one launch (start us, length us, event | category | flops | bytes accessed | tf_op | source)
XLA Modules:
  0.0 65.2 jit_solution(17078000960076292039)
XLA Ops:
  0.0 0.9 %slice_bitcast_fusion.1 = (f32[32,512]{1,0:T(8,128)S(1)}, f32[32,512]{1,0:T(8,128)S(1)}) fusion(f32[16,32,512]{2,1,0:T(8,128)} %param.8), kind=kLoop, calls=%fused_computation.2 | loop fusion | bytes 262144 | tf_op jit(solution)/shard_map/squeeze | solution.py:433
  0.9 0.0 copy-start.2
  0.9 0.2 half_norm.3
  1.1 0.8 %collective-permute-start = (bf16[32,512]{1,0:T(8,128)(2,1)S(1)}, bf16[32,512]{1,0:T(8,128)(2,1)S(1)}, u32[]{:S(2)}, u32[]{:S(2)}) collective-permute-start(bf16[32,512]{1,0:T(8,128)(2,1)S(1)} %get-tuple-element.25), channel_id=1, source_target_pairs={{4,8},{8,4},{5,9},{9,5},{6,10},{10,6},{7,11},{11,7},{20,24},{24,20... | collective-permute-start | bytes 98312 | tf_op jit(solution)/shard_map/ppermute | solution.py:401
  1.9 5.9 %collective-permute-start.1 = (bf16[32,512]{1,0:T(8,128)(2,1)S(1)}, bf16[32,512]{1,0:T(8,128)(2,1)S(1)}, u32[]{:S(2)}, u32[]{:S(2)}) collective-permute-start(bf16[32,512]{1,0:T(8,128)(2,1)S(1)} %get-tuple-element.26), channel_id=1, source_target_pairs={{0,4},{8,12},{4,0},{12,8},{1,5},{9,13},{5,1},{13,9},{2,6},{10,14},... | collective-permute-start | bytes 98312 | tf_op jit(solution)/shard_map/ppermute | solution.py:401
  7.8 0.3 half_norm.2.normed_ref
  8.2 0.1 fusion
  8.2 0.0 copy-start.7
  8.2 0.8 %copy-done.7 = bf16[512,512]{1,0:T(8,128)(2,1)} copy-done((bf16[512,512]{1,0:T(8,128)(2,1)}, bf16[512,512]{1,0:T(8,128)(2,1)S(1)}, u32[]{:S(2)}) %copy-start.7) | copy-done | bytes 524312
  9.0 0.1 pad.7.clone
  9.1 0.6 collective-permute-done.1
  9.8 0.1 maximum_maximum_fusion.1
  9.9 0.1 collective-permute-start.3
  9.9 0.0 copy-start.1
  9.9 0.0 copy-start.5
  10.0 0.0 copy-start.6
  10.0 0.8 %collective-permute-start.2 = (bf16[32,512]{1,0:T(8,128)(2,1)S(1)}, bf16[32,512]{1,0:T(8,128)(2,1)S(1)}, u32[]{:S(2)}, u32[]{:S(2)}) collective-permute-start(bf16[32,512]{1,0:T(8,128)(2,1)S(1)} %get-tuple-element.22), channel_id=1, source_target_pairs={{1,2},{2,1},{5,6},{6,5},{9,10},{10,9},{13,14},{14,13},{17,18},{18,... | collective-permute-start | bytes 98312 | tf_op jit(solution)/shard_map/ppermute | solution.py:401
  10.8 1.0 %copy-done.8 = bf16[512,512]{1,0:T(8,128)(2,1)S(1)} copy-done((bf16[512,512]{1,0:T(8,128)(2,1)S(1)}, bf16[512,512]{1,0:T(8,128)(2,1)}, u32[]{:S(2)}) %copy-start.8) | copy-done | bytes 524312
  11.8 2.1 %expand.1.expanded_ref = f32[8448,128]{1,0:T(8,128)S(1)} custom-call(bf16[512,512]{1,0:T(8,128)(2,1)S(1)} %copy-done.8, bf16[512,2048]{1,0:T(8,128)(2,1)S(1)} %copy-done), custom_call_target="tpu_custom_call" | custom-call | flops 10000000000 | bytes 6815744 | tf_op jit(solution)/shard_map/expand/pallas_call | solution.py:111
  14.1 5.7 %mix.1 = (f32[512,512]{1,0:T(8,128)S(1)}, bf16[512,512]{1,0:T(8,128)(2,1)S(1)}) custom-call(f32[8448,128]{1,0:T(8,128)S(1)} %expand.1.expanded_ref, f32[512,512]{1,0:T(8,128)S(1)} %bitcast.17, bf16[32,512]{1,0:T(8,128)(2,1)S(1)} %get-tuple-element.23.up_ref, bf16[32,512]{1,0:T(8,128)(2,1)S(1)} %get-tuple-element.24.down_ref, ...), custom_call_target="tpu_custom_call" | custom-call | flops 1073741824 | bytes 11010048 | tf_op jit(solution)/shard_map/mix/pallas_call | solution.py:230
  19.8 20.6 %all_to_all.10 = bf16[16,32,512]{2,1,0:T(8,128)(2,1)S(1)} all-to-all(bf16[16,32,512]{2,1,0:T(8,128)(2,1)S(1)} %bitcast.18), channel_id=1, replica_groups=mesh['field'=2,'row'=4,'col'=4] {'row','col'}, dimensions={0} | all-to-all | bytes 1048576 | tf_op jit(solution)/shard_map/all_to_all | solution.py:446
  40.4 4.6 %attend.1 = bf16[16,2,16,512]{3,2,1,0:T(8,128)(2,1)S(1)} custom-call(bf16[16,2,16,512]{3,2,1,0:T(8,128)(2,1)S(1)} %bitcast.19, bf16[512,1536]{1,0:T(8,128)(2,1)S(1)} %copy-done.9), custom_call_target="tpu_custom_call" | custom-call | flops 1073741824 | bytes 2621440 | tf_op jit(solution)/shard_map/attend/pallas_call | solution.py:335
  44.9 18.4 %all_to_all.11 = bf16[16,32,512]{2,1,0:T(8,128)(2,1)S(1)} all-to-all(bf16[16,32,512]{2,1,0:T(8,128)(2,1)S(1)} %bitcast.20), channel_id=1, replica_groups=mesh['field'=2,'row'=4,'col'=4] {'row','col'}, dimensions={0} | all-to-all | bytes 1048576 | tf_op jit(solution)/shard_map/all_to_all | solution.py:450
  63.3 1.9 %finish.1 = f32[512,512]{1,0:T(8,128)} custom-call(bf16[512,512]{1,0:T(8,128)(2,1)S(1)} %bitcast.15, bf16[512,512]{1,0:T(8,128)(2,1)S(1)} %copy-done.4, bf16[512,512]{1,0:T(8,128)(2,1)S(1)} %copy-done.3, f32[512,512]{1,0:T(8,128)S(1)} %get-tuple-element.14.mixed_ref), custom_call_target="tpu_custom_call" | custom-call | tf_op jit(solution)/shard_map/finish/pallas_call | solution.py:381
  (24 shorter events, 0.1 us)
Async XLA Ops:
  0.9 6.9 %copy-start.2 = (f32[16,32,512]{2,1,0:T(8,128)S(1)}, f32[16,32,512]{2,1,0:T(8,128)}, u32[]{:S(2)}) copy-start(f32[16,32,512]{2,1,0:T(8,128)} %param.8) | copy-start | bytes 3145732
  1.1 8.0 %collective-permute-start = (bf16[32,512]{1,0:T(8,128)(2,1)S(1)}, bf16[32,512]{1,0:T(8,128)(2,1)S(1)}, u32[]{:S(2)}, u32[]{:S(2)}) collective-permute-start(bf16[32,512]{1,0:T(8,128)(2,1)S(1)} %get-tuple-element.25), channel_id=1, source_target_pairs={{4,8},{8,4},{5,9},{9,5},{6,10},{10,6},{7,11},{11,7},{20,24},{24,20... | collective-permute-start | bytes 98312 | tf_op jit(solution)/shard_map/ppermute | solution.py:401
  1.9 7.8 %collective-permute-start.1 = (bf16[32,512]{1,0:T(8,128)(2,1)S(1)}, bf16[32,512]{1,0:T(8,128)(2,1)S(1)}, u32[]{:S(2)}, u32[]{:S(2)}) collective-permute-start(bf16[32,512]{1,0:T(8,128)(2,1)S(1)} %get-tuple-element.26), channel_id=1, source_target_pairs={{0,4},{8,12},{4,0},{12,8},{1,5},{9,13},{5,1},{13,9},{2,6},{10,14},... | collective-permute-start | bytes 98312 | tf_op jit(solution)/shard_map/ppermute | solution.py:401
  7.8 2.9 %copy-start = (bf16[512,2048]{1,0:T(8,128)(2,1)S(1)}, bf16[512,2048]{1,0:T(8,128)(2,1)}, u32[]{:S(2)}) copy-start(bf16[512,2048]{1,0:T(8,128)(2,1)} %w_expand_ref.1) | copy-start | bytes 6291460
  8.2 0.8 %copy-start.7 = (bf16[512,512]{1,0:T(8,128)(2,1)}, bf16[512,512]{1,0:T(8,128)(2,1)S(1)}, u32[]{:S(2)}) copy-start(bf16[512,512]{1,0:T(8,128)(2,1)S(1)} %half_norm.2.normed_ref) | copy-start | bytes 1572868
  9.9 4.1 %collective-permute-start.3 = (bf16[32,512]{1,0:T(8,128)(2,1)S(1)}, bf16[32,512]{1,0:T(8,128)(2,1)S(1)}, u32[]{:S(2)}, u32[]{:S(2)}) collective-permute-start(bf16[32,512]{1,0:T(8,128)(2,1)S(1)} %get-tuple-element.21), channel_id=1, source_target_pairs={{0,1},{2,3},{1,0},{3,2},{4,5},{6,7},{5,4},{7,6},{8,9},{10,11},{9,8... | collective-permute-start | bytes 98312 | tf_op jit(solution)/shard_map/ppermute | solution.py:401
  9.9 4.1 %copy-start.1 = (bf16[2048,512]{1,0:T(8,128)(2,1)S(1)}, bf16[2048,512]{1,0:T(8,128)(2,1)}, u32[]{:S(2)}) copy-start(bf16[2048,512]{1,0:T(8,128)(2,1)} %w_project_ref.1) | copy-start | bytes 6291460
  9.9 4.1 %copy-start.5 = (bf16[512,512]{1,0:T(8,128)(2,1)S(1)}, bf16[512,512]{1,0:T(8,128)(2,1)}, u32[]{:S(2)}) copy-start(bf16[512,512]{1,0:T(8,128)(2,1)} %constant.31.clone.perm_ref) | copy-start | bytes 1572868
  10.0 4.1 %copy-start.6 = (f32[3,3,2048]{2,1,0:T(4,128)S(1)}, f32[3,3,2048]{2,1,0:T(4,128)}, u32[]{:S(2)}) copy-start(f32[3,3,2048]{2,1,0:T(4,128)} %depth_ref.1) | copy-start | bytes 221188
  10.0 4.0 %collective-permute-start.2 = (bf16[32,512]{1,0:T(8,128)(2,1)S(1)}, bf16[32,512]{1,0:T(8,128)(2,1)S(1)}, u32[]{:S(2)}, u32[]{:S(2)}) collective-permute-start(bf16[32,512]{1,0:T(8,128)(2,1)S(1)} %get-tuple-element.22), channel_id=1, source_target_pairs={{1,2},{2,1},{5,6},{6,5},{9,10},{10,9},{13,14},{14,13},{17,18},{18,... | collective-permute-start | bytes 98312 | tf_op jit(solution)/shard_map/ppermute | solution.py:401
  10.8 1.0 %copy-start.8 = (bf16[512,512]{1,0:T(8,128)(2,1)S(1)}, bf16[512,512]{1,0:T(8,128)(2,1)}, u32[]{:S(2)}) copy-start(bf16[512,512]{1,0:T(8,128)(2,1)} %copy-done.7) | copy-start | bytes 1572868
  14.1 26.3 %copy-start.9 = (bf16[512,1536]{1,0:T(8,128)(2,1)S(1)}, bf16[512,1536]{1,0:T(8,128)(2,1)}, u32[]{:S(2)}) copy-start(bf16[512,1536]{1,0:T(8,128)(2,1)} %weight_ref.4) | copy-start | bytes 4718596
  40.3 22.9 %copy-start.3 = (bf16[512,512]{1,0:T(8,128)(2,1)S(1)}, bf16[512,512]{1,0:T(8,128)(2,1)}, u32[]{:S(2)}) copy-start(bf16[512,512]{1,0:T(8,128)(2,1)} %weight_ref.5) | copy-start | bytes 1572868
  40.3 22.9 %copy-start.4 = (bf16[512,512]{1,0:T(8,128)(2,1)S(1)}, bf16[512,512]{1,0:T(8,128)(2,1)}, u32[]{:S(2)}) copy-start(bf16[512,512]{1,0:T(8,128)(2,1)} %constant.32.clone.back_ref) | copy-start | bytes 1572868

commit v6 on v5

--- a/solution.py
+++ b/solution.py
@@ -124,10 +124,13 @@
 
 
 def mix_kernel(
-    expanded_ref, field_ref, up_ref, down_ref, left_ref, right_ref, w_expand_ref, depth_ref,
-    w_project_ref, perm_ref, mixed_ref, grouped_ref, total_ref, normed_ref,
-    even_ref, odd_ref, even_halo_ref, odd_halo_ref, *, rows, cols,
+    own_ref, expanded_ref, field_ref, up_ref, down_ref, left_ref, right_ref, w_expand_ref, depth_ref,
+    w_project_ref, perm_ref, mixed_ref, *refs, rows, cols, masks,
 ):
+    slab_refs = refs[: len(masks)]
+    total_ref, normed_ref, grouped_ref, even_ref, odd_ref, even_halo_ref, odd_halo_ref = refs[
+        len(masks) :
+    ]
     tokens = rows * cols
     width = w_expand_ref.shape[1]
     tile = even_ref.shape[1]
@@ -219,24 +222,31 @@
         mixed_ref[piece, :] = mixed
         normed_ref[piece, :] = layer_norm(mixed).astype(jnp.bfloat16)
     grouped_ref[...] = matmul(perm_ref[...], normed_ref[...]).astype(jnp.bfloat16)
-
-
-def mix(expanded, field, up, down, left, right, w_expand, depth_kernel, w_project, perm, rows, cols):
+    size = slab_refs[0].shape[1]
+    for mask, slab_ref in zip(masks, slab_refs):
+        for side in range(slab_ref.shape[0]):
+            start = pl.multiple_of((own_ref[0] ^ (mask | side)) * size, 16)
+            slab_ref[side] = grouped_ref[pl.ds(start, size), :]
+
+
+def mix(
+    own, masks, slab, expanded, field, up, down, left, right, w_expand, depth_kernel, w_project, perm,
+    rows, cols,
+):
     tokens, channels = field.shape
     width = w_expand.shape[1]
     tile = divisor(width // 2, 256, LANES)
     slot = left.shape[0]
     halo = pltpu.VMEM((tile // LANES, 24 + 2 * cols + 2 * slot, LANES), jnp.float32)
     return pl.pallas_call(
-        functools.partial(mix_kernel, rows=rows, cols=cols),
-        in_specs=[vmem()] * 10,
-        out_specs=[vmem()] * 2,
-        out_shape=[
-            jax.ShapeDtypeStruct((tokens, channels), jnp.float32),
-            jax.ShapeDtypeStruct((tokens, channels), jnp.bfloat16),
-        ],
+        functools.partial(mix_kernel, rows=rows, cols=cols, masks=masks),
+        in_specs=[pl.BlockSpec(memory_space=pltpu.SMEM)] + [vmem()] * 10,
+        out_specs=[vmem()] * (1 + len(masks)),
+        out_shape=[jax.ShapeDtypeStruct((tokens, channels), jnp.float32)]
+        + [jax.ShapeDtypeStruct(slab, jnp.bfloat16)] * len(masks),
         scratch_shapes=[
             pltpu.VMEM((tokens, channels), jnp.float32),
+            pltpu.VMEM((tokens, channels), jnp.bfloat16),
             pltpu.VMEM((tokens, channels), jnp.bfloat16),
             pltpu.VMEM((tokens, tile), jnp.bfloat16),
             pltpu.VMEM((tokens, tile), jnp.bfloat16),
@@ -250,7 +260,7 @@
             transcendentals=tokens * width,
         ),
         name="mix",
-    )(expanded, field, up, down, left, right, w_expand, depth_kernel, w_project, perm)
+    )(own, expanded, field, up, down, left, right, w_expand, depth_kernel, w_project, perm)
 
 
 def identity(size):
@@ -259,11 +269,13 @@
     return jnp.where(row == column, 1.0, 0.0).astype(jnp.bfloat16)
 
 
-def attend_kernel(
-    tokens_ref, weight_ref, out_ref, query_ref, key_ref, value_ref, turned_ref, even_ref, odd_ref
-):
-    devices, sets, members, channels = tokens_ref.shape
-    count = devices * members
+def attend_kernel(*refs, slabs, sets):
+    mine, others, weight_ref = refs[:slabs], refs[slabs : 2 * slabs], refs[2 * slabs]
+    out_refs = refs[2 * slabs + 1 : 3 * slabs + 1]
+    query_ref, key_ref, value_ref, turned_ref, even_ref, odd_ref = refs[3 * slabs + 1 :]
+    sides, size, channels = mine[0].shape
+    members = size // sets
+    count = slabs * sides * members
     head_width = channels // HEADS
     group_heads = LANES // head_width
     groups = channels // LANES
@@ -277,7 +289,15 @@
     ]
     turn_values = identity(channels)
     for s in range(sets):
-        block = tokens_ref[:, s].reshape(count, channels)
+        piece = slice(s * members, (s + 1) * members)
+        block = jnp.concatenate(
+            [
+                (mine, others)[side][index][side, piece]
+                for index in range(slabs)
+                for side in range(sides)
+            ],
+            axis=0,
+        )
         qkv = matmul(block, weight_ref[...]).astype(jnp.bfloat16)
         values = matmul_nt(turn_values, qkv[:, 2 * channels :]).astype(jnp.bfloat16)
         for group in range(groups):
@@ -320,23 +340,26 @@
     for s in range(sets):
         turned = turned_ref[s * groups : (s + 1) * groups].reshape(channels, count)
         attended = matmul_nt(turn_tokens, turned).astype(jnp.bfloat16)
-        out_ref[:, s] = attended.reshape(devices, members, channels)
-
-
-def attend(blocks, w_qkv):
-    devices, sets, members, channels = blocks.shape
-    count = devices * members
-    apart = members % 16 != 0
-    if apart:
-        blocks = blocks.transpose(1, 0, 2, 3).reshape(1, sets, count, channels)
+        for index in range(slabs):
+            for side in range(sides):
+                start = (index * sides + side) * members
+                out_refs[index][side, s * members : (s + 1) * members] = attended[
+                    start : start + members
+                ]
+
+
+def attend(mine, others, w_qkv, sets):
+    slabs = len(mine)
+    sides, size, channels = mine[0].shape
+    count = slabs * sides * size // sets
     head_width = channels // HEADS
     group_heads = LANES // head_width
     total = sets * channels // LANES
-    result = pl.pallas_call(
-        attend_kernel,
-        in_specs=[vmem()] * 2,
-        out_specs=vmem(),
-        out_shape=jax.ShapeDtypeStruct(blocks.shape, jnp.bfloat16),
+    return pl.pallas_call(
+        functools.partial(attend_kernel, slabs=slabs, sets=sets),
+        in_specs=[vmem()] * (2 * slabs + 1),
+        out_specs=[vmem()] * slabs,
+        out_shape=[jax.ShapeDtypeStruct(mine[0].shape, jnp.bfloat16)] * slabs,
         scratch_shapes=[
             pltpu.VMEM((total, count, LANES), jnp.bfloat16),
             pltpu.VMEM((total, count, LANES), jnp.bfloat16),
@@ -352,14 +375,19 @@
             transcendentals=sets * HEADS * count * count,
         ),
         name="attend",
-    )(blocks, w_qkv)
-    if apart:
-        result = result.reshape(sets, devices, members, channels).transpose(1, 0, 2, 3)
-    return result
-
-
-def finish_kernel(attended_ref, back_ref, weight_ref, mixed_ref, out_ref, made_ref, sent):
+    )(*mine, *others, w_qkv)
+
+
+def finish_kernel(own_ref, *refs, masks):
+    slabs = len(masks)
+    mine, others = refs[:slabs], refs[slabs : 2 * slabs]
+    back_ref, weight_ref, mixed_ref, out_ref, attended_ref, made_ref, sent = refs[2 * slabs :]
     tokens = mixed_ref.shape[0]
+    sides, size, _ = mine[0].shape
+    for index, mask in enumerate(masks):
+        for side in range(sides):
+            start = pl.multiple_of((own_ref[0] ^ (mask | side)) * size, 16)
+            attended_ref[pl.ds(start, size), :] = (mine, others)[side][index][side]
     step = made_ref.shape[1]
     copies = []
     for index, start in enumerate(range(0, tokens, step)):
@@ -375,21 +403,22 @@
         copy.wait()
 
 
-def finish(attended, back, w_out, mixed):
+def finish(own, masks, mine, others, back, w_out, mixed):
     tokens, channels = mixed.shape
     step = divisor(tokens, 128, 16)
     return pl.pallas_call(
-        finish_kernel,
-        in_specs=[vmem()] * 4,
+        functools.partial(finish_kernel, masks=masks),
+        in_specs=[pl.BlockSpec(memory_space=pltpu.SMEM)] + [vmem()] * (2 * len(masks) + 3),
         out_specs=pl.BlockSpec(memory_space=pltpu.HBM),
         out_shape=jax.ShapeDtypeStruct((tokens, channels), jnp.float32),
         scratch_shapes=[
+            pltpu.VMEM((tokens, channels), jnp.bfloat16),
             pltpu.VMEM((tokens // step, step, channels), jnp.float32),
             pltpu.SemaphoreType.DMA((tokens // step,)),
         ],
         compiler_params=pltpu.CompilerParams(vmem_limit_bytes=16 * MIB),
         name="finish",
-    )(attended, back, w_out, mixed)
+    )(own, *mine, *others, back, w_out, mixed)
 
 
 def exchange(low_edge, high_edge, axis):
@@ -403,6 +432,42 @@
     one = swap(jnp.where(even, high_edge, low_edge), 0)
     two = swap(jnp.where(even, low_edge, high_edge), 1)
     return jnp.where(even, two, one), jnp.where(even, one, two)
+
+
+def exchange_plan(row_devices, col_devices):
+    masks = [
+        row * col_devices + col for row in range(row_devices) for col in range(0, col_devices, 2)
+    ]
+    return masks, 2
+
+
+def trade(masks, slabs):
+    axes = ("row", "col")
+    devices = lax.axis_size("row") * lax.axis_size("col")
+
+    def swap(slab, mask):
+        return lax.ppermute(slab, axes, [(i, i ^ mask) for i in range(devices)])
+
+    mine = dict(zip(masks, slabs))
+    for mask in sorted(masks[1:], reverse=True):
+        mine[mask] = swap(mine[mask], mask)
+    mine = [mine[mask] for mask in masks]
+    return mine, [swap(slab, 1) for slab in mine]
+
+
+def trade_all(slabs, sets, members, outward):
+    axes = ("row", "col")
+    channels = slabs[0].shape[-1]
+    block = slabs[0].reshape(-1, channels)
+    devices = block.shape[0] // (sets * members)
+    if not outward:
+        block = block.reshape(sets, devices, members, channels).transpose(1, 0, 2, 3)
+    block = block.reshape(devices, sets * members, channels)
+    block = lax.all_to_all(block, axes, 0, 0, tiled=True)
+    if outward:
+        block = block.reshape(devices, sets, members, channels).transpose(1, 0, 2, 3)
+    block = [block.reshape(1, -1, channels)]
+    return block, block
 
 
 def grouping(rows, cols, blocks_rows, blocks_cols):
@@ -440,17 +505,28 @@
     normed, first, last = lax.optimization_barrier((normed, first, last))
     expanded = expand(normed, w_expand)
     left, right = exchange(first, last, "col")
-    mixed, grouped = mix(
-        expanded, flat, up, down, left, right, w_expand, depth_kernel, w_project, perm, rows, cols
+    pairwise = devices <= 16 and devices & (devices - 1) == 0 and col_devices % 2 == 0
+    if pairwise:
+        masks, sides = exchange_plan(row_devices, col_devices)
+        own = lax.axis_index(("row", "col")).reshape(1)
+    else:
+        masks, sides = [0], 1
+        own = jnp.zeros(1, jnp.int32)
+    slab = (sides, tokens // (sides * len(masks)), channels)
+    mixed, *slabs = mix(
+        own, masks, slab, expanded, flat, up, down, left, right, w_expand, depth_kernel, w_project,
+        perm, rows, cols,
     )
-    arrived = lax.all_to_all(
-        grouped.reshape(devices, sets_local * members, channels), ("row", "col"), 0, 0, tiled=True
-    )
-    attended = attend(arrived.reshape(devices, sets_local, members, channels), w_qkv)
-    returned = lax.all_to_all(
-        attended.reshape(devices, sets_local * members, channels), ("row", "col"), 0, 0, tiled=True
-    )
-    final = finish(returned.reshape(tokens, channels), back, w_out, mixed)
+
+    def route(slabs, outward):
+        if pairwise:
+            return trade(masks, slabs)
+        return trade_all(slabs, sets_local, members, outward)
+
+    mine, others = route(slabs, True)
+    slabs = attend(mine, others, w_qkv, sets_local)
+    mine, others = route(slabs, False)
+    final = finish(own, masks, mine, others, back, w_out, mixed)
     return final.reshape(rows, cols, channels)
 
 

time: 65.5 us -> 67.3 us (1.027)
  blocking collectives: 38.9 us -> 0 us
  starting transfers between devices: 7.57 us -> 35 us
  waiting for transfers between devices: 0.61 us -> 13.8 us
    all_to_all x2 -> x0, blocking collectives: 38.9 us -> none  [the longest x1 20.6 us: shards(): lax.all_to_all(grouped.reshape(devices, sets_local * members, channels),...]
    ppermute x0 -> x30, starting transfers between devices: none -> 27.4 us  [swap(): return lax.ppermute(slab, axes, [(i, i ^ mask) for i in range(devices)])]
    ppermute x0 -> x30, waiting for transfers between devices: none -> 13.2 us  [swap(): return lax.ppermute(slab, axes, [(i, i ^ mask) for i in range(devices)])]
  transfers between devices with their start and end apart: 4 -> 34, of which waited for: 1 -> 15; matrix products, arithmetic and copies ran while one was open for 0% -> 0% of each run, Pallas kernels for 4% -> 4%
where the time goes in v6:
time: 67.3 us; the launch traced here: 67 us
  starting transfers between devices  35 us (52%)
  Pallas kernels  14.9 us (22%)
  waiting for transfers between devices  13.8 us (21%)
  local copies, waits for them, and re-layouts  2.91 us (4%)
    ppermute x30, starting transfers between devices, swap(): return lax.ppermute(slab, axes, [(i, i ^ mask) for i in range(devices)])  27.4 us
    ppermute x30, waiting for transfers between devices, swap(): return lax.ppermute(slab, axes, [(i, i ^ mask) for i in range(devices)])  13.2 us
    ppermute x4, starting transfers between devices, swap(): return lax.ppermute(edge, axis, pairs + [(b, a) for a, b in pairs])  7.57 us
    pallas_call x1, Pallas kernels, mix(): pl.pallas_call(functools.partial(mix_kernel, rows=rows, cols=cols, masks=...  5.76 us
    pallas_call x1, Pallas kernels, attend(): pl.pallas_call(functools.partial(attend_kernel, slabs=slabs, sets=sets),...  4.56 us
    pallas_call x1, Pallas kernels, expand(): pl.pallas_call(expand_kernel, in_specs=[vmem()] * 2, out_specs=vmem(), ou...  2.15 us
    pallas_call x1, Pallas kernels, finish(): pl.pallas_call(functools.partial(finish_kernel, masks=masks), in_specs=[p...  1.94 us
    unnamed x20, local copies, waits for them, and re-layouts  1.87 us
  transfers between devices with their start and end apart: 34, of which 15 were waited for; matrix products, arithmetic and copies ran while one was open for 0% of the time, Pallas kernels for 4%

profile of v6, /device:TPU:0, one launch (start us, length us, event | category | flops | bytes accessed | tf_op | source)
XLA Modules:
  0.0 67.0 jit_solution(13063949959492866894)
XLA Ops:
  0.0 0.9 %slice_bitcast_fusion.1 = (f32[32,512]{1,0:T(8,128)S(1)}, f32[32,512]{1,0:T(8,128)S(1)}) fusion(f32[16,32,512]{2,1,0:T(8,128)} %param.8), kind=kLoop, calls=%fused_computation.2 | loop fusion | bytes 262144 | tf_op jit(solution)/shard_map/squeeze | solution.py:498
  1.1 0.8 %collective-permute-start = (bf16[32,512]{1,0:T(8,128)(2,1)S(1)}, bf16[32,512]{1,0:T(8,128)(2,1)S(1)}, u32[]{:S(2)}, u32[]{:S(2)}) collective-permute-start(bf16[32,512]{1,0:T(8,128)(2,1)S(1)} %get-tuple-element.55), channel_id=1, source_target_pairs={{4,8},{8,4},{5,9},{9,5},{6,10},{10,6},{7,11},{11,7},{20,24},{24,20... | collective-permute-start | bytes 98312 | tf_op jit(solution)/shard_map/ppermute | solution.py:430
  1.9 5.9 %collective-permute-start.1 = (bf16[32,512]{1,0:T(8,128)(2,1)S(1)}, bf16[32,512]{1,0:T(8,128)(2,1)S(1)}, u32[]{:S(2)}, u32[]{:S(2)}) collective-permute-start(bf16[32,512]{1,0:T(8,128)(2,1)S(1)} %get-tuple-element.56), channel_id=1, source_target_pairs={{0,4},{8,12},{4,0},{12,8},{1,5},{9,13},{5,1},{13,9},{2,6},{10,14},... | collective-permute-start | bytes 98312 | tf_op jit(solution)/shard_map/ppermute | solution.py:430
  10.8 1.0 %copy-done.8 = bf16[512,512]{1,0:T(8,128)(2,1)S(1)} copy-done((bf16[512,512]{1,0:T(8,128)(2,1)S(1)}, bf16[512,512]{1,0:T(8,128)(2,1)}, u32[]{:S(2)}) %copy-start.8) | copy-done | bytes 524312
  11.8 2.2 %expand.1.expanded_ref = f32[8448,128]{1,0:T(8,128)S(1)} custom-call(bf16[512,512]{1,0:T(8,128)(2,1)S(1)} %copy-done.8, bf16[512,2048]{1,0:T(8,128)(2,1)S(1)} %copy-done), custom_call_target="tpu_custom_call" | custom-call | flops 10000000000 | bytes 6815744 | tf_op jit(solution)/shard_map/expand/pallas_call | solution.py:111
  14.1 5.8 %mix.1 = (f32[512,512]{1,0:T(8,128)S(1)}, bf16[2,32,512]{2,1,0:T(8,128)(2,1)S(1)}, bf16[2,32,512]{2,1,0:T(8,128)(2,1)S(1)}, bf16[2,32,512]{2,1,0:T(8,128)(2,1)S(...) custom-call(s32[1]{0:T(128)} %bitcast.own_ref, ...), custom_call_target="tpu_custom_call" | custom-call | flops 1073741824 | bytes 11010048 | tf_op jit(solution)/shard_map/mix/pallas_call | solution.py:241
  19.9 3.5 %collective-permute-start.4 = (bf16[2,32,512]{2,1,0:T(8,128)(2,1)S(1)}, bf16[2,32,512]{2,1,0:T(8,128)(2,1)S(1)}, u32[]{:S(2)}, u32[]{:S(2)}) collective-permute-start(bf16[2,32,512]{2,1,0:T(8,128)(2,1)S(1)} %get-tuple-element.29), channel_id=1, source_target_pairs={{0,2},{1,3},{2,0},{3,1},{4,6},{5,7},{6,4},{7,5},{8,10},{9,11},{10,... | collective-permute-start | bytes 196616 | tf_op jit(solution)/shard_map/ppermute | solution.py:449
  23.4 2.0 %collective-permute-start.5 = (bf16[2,32,512]{2,1,0:T(8,128)(2,1)S(1)}, bf16[2,32,512]{2,1,0:T(8,128)(2,1)S(1)}, u32[]{:S(2)}, u32[]{:S(2)}) collective-permute-start(bf16[2,32,512]{2,1,0:T(8,128)(2,1)S(1)} %get-tuple-element.30), channel_id=1, source_target_pairs={{0,4},{1,5},{2,6},{3,7},{4,0},{5,1},{6,2},{7,3},{8,12},{9,13},{10,... | collective-permute-start | bytes 196616 | tf_op jit(solution)/shard_map/ppermute | solution.py:449
  25.4 1.4 %collective-permute-start.7 = (bf16[2,32,512]{2,1,0:T(8,128)(2,1)S(1)}, bf16[2,32,512]{2,1,0:T(8,128)(2,1)S(1)}, u32[]{:S(2)}, u32[]{:S(2)}) collective-permute-start(bf16[2,32,512]{2,1,0:T(8,128)(2,1)S(1)} %get-tuple-element.32), channel_id=1, source_target_pairs={{0,8},{1,9},{2,10},{3,11},{4,12},{5,13},{6,14},{7,15},{8,0},{9,1},... | collective-permute-start | bytes 196616 | tf_op jit(solution)/shard_map/ppermute | solution.py:449
  26.8 2.4 %collective-permute-start.8 = (bf16[2,32,512]{2,1,0:T(8,128)(2,1)S(1)}, bf16[2,32,512]{2,1,0:T(8,128)(2,1)S(1)}, u32[]{:S(2)}, u32[]{:S(2)}) collective-permute-start(bf16[2,32,512]{2,1,0:T(8,128)(2,1)S(1)} %get-tuple-element.33), channel_id=1, source_target_pairs={{0,10},{1,11},{2,8},{3,9},{4,14},{5,15},{6,12},{7,13},{8,2},{9,3},... | collective-permute-start | bytes 196616 | tf_op jit(solution)/shard_map/ppermute | solution.py:449
  29.2 1.5 %collective-permute-start.9 = (bf16[2,32,512]{2,1,0:T(8,128)(2,1)S(1)}, bf16[2,32,512]{2,1,0:T(8,128)(2,1)S(1)}, u32[]{:S(2)}, u32[]{:S(2)}) collective-permute-start(bf16[2,32,512]{2,1,0:T(8,128)(2,1)S(1)} %get-tuple-element.34), channel_id=1, source_target_pairs={{0,12},{1,13},{2,14},{3,15},{4,8},{5,9},{6,10},{7,11},{8,4},{9,5},... | collective-permute-start | bytes 196616 | tf_op jit(solution)/shard_map/ppermute | solution.py:449
  30.7 2.4 %collective-permute-start.10 = (bf16[2,32,512]{2,1,0:T(8,128)(2,1)S(1)}, bf16[2,32,512]{2,1,0:T(8,128)(2,1)S(1)}, u32[]{:S(2)}, u32[]{:S(2)}) collective-permute-start(bf16[2,32,512]{2,1,0:T(8,128)(2,1)S(1)} %get-tuple-element.35), channel_id=1, source_target_pairs={{0,14},{1,15},{2,12},{3,13},{4,10},{5,11},{6,8},{7,9},{8,6},{9,7},... | collective-permute-start | bytes 196616 | tf_op jit(solution)/shard_map/ppermute | solution.py:449
  33.1 1.6 %collective-permute-done.7.refs_4_ = bf16[2,32,512]{2,1,0:T(8,128)(2,1)S(1)} collective-permute-done((bf16[2,32,512]{2,1,0:T(8,128)(2,1)S(1)}, bf16[2,32,512]{2,1,0:T(8,128)(2,1)S(1)}, u32[]{:S(2)}, u32[]{:S(2)}) %collective-permute-start.7) | collective-permute-done | bytes 65568 | tf_op jit(solution)/shard_map/ppermute | solution.py:449
  34.7 4.2 %collective-permute-done.8.refs_5_ = bf16[2,32,512]{2,1,0:T(8,128)(2,1)S(1)} collective-permute-done((bf16[2,32,512]{2,1,0:T(8,128)(2,1)S(1)}, bf16[2,32,512]{2,1,0:T(8,128)(2,1)S(1)}, u32[]{:S(2)}, u32[]{:S(2)}) %collective-permute-start.8) | collective-permute-done | bytes 65568 | tf_op jit(solution)/shard_map/ppermute | solution.py:449
  41.4 4.6 %attend.1 = (bf16[2,32,512]{2,1,0:T(8,128)(2,1)S(1)}, bf16[2,32,512]{2,1,0:T(8,128)(2,1)S(1)}, bf16[2,32,512]{2,1,0:T(8,128)(2,1)S(1)}, bf16[2,32,512]{2,1,0:T(8...) custom-call(bf16[2,32,512]{2,1,0:T(8,128)(2,1)S(1)} %get-tuple-eleme, ...), custom_call_target="tpu_custom_call" | custom-call | flops 1073741824 | bytes 2621440 | tf_op jit(solution)/shard_map/attend/pallas_call | solution.py:358
  46.0 0.8 %collective-permute-start.19 = (bf16[2,32,512]{2,1,0:T(8,128)(2,1)S(1)}, bf16[2,32,512]{2,1,0:T(8,128)(2,1)S(1)}, u32[]{:S(2)}, u32[]{:S(2)}) collective-permute-start(bf16[2,32,512]{2,1,0:T(8,128)(2,1)S(1)} %get-tuple-element.37), channel_id=1, source_target_pairs={{0,2},{1,3},{2,0},{3,1},{4,6},{5,7},{6,4},{7,5},{8,10},{9,11},{10,... | collective-permute-start | bytes 196616 | tf_op jit(solution)/shard_map/ppermute | solution.py:449
  46.8 2.4 %collective-permute-start.20 = (bf16[2,32,512]{2,1,0:T(8,128)(2,1)S(1)}, bf16[2,32,512]{2,1,0:T(8,128)(2,1)S(1)}, u32[]{:S(2)}, u32[]{:S(2)}) collective-permute-start(bf16[2,32,512]{2,1,0:T(8,128)(2,1)S(1)} %get-tuple-element.38), channel_id=1, source_target_pairs={{0,4},{1,5},{2,6},{3,7},{4,0},{5,1},{6,2},{7,3},{8,12},{9,13},{10,... | collective-permute-start | bytes 196616 | tf_op jit(solution)/shard_map/ppermute | solution.py:449
  49.8 2.3 %collective-permute-start.22 = (bf16[2,32,512]{2,1,0:T(8,128)(2,1)S(1)}, bf16[2,32,512]{2,1,0:T(8,128)(2,1)S(1)}, u32[]{:S(2)}, u32[]{:S(2)}) collective-permute-start(bf16[2,32,512]{2,1,0:T(8,128)(2,1)S(1)} %get-tuple-element.40), channel_id=1, source_target_pairs={{0,8},{1,9},{2,10},{3,11},{4,12},{5,13},{6,14},{7,15},{8,0},{9,1},... | collective-permute-start | bytes 196616 | tf_op jit(solution)/shard_map/ppermute | solution.py:449
  52.1 1.0 %collective-permute-start.23 = (bf16[2,32,512]{2,1,0:T(8,128)(2,1)S(1)}, bf16[2,32,512]{2,1,0:T(8,128)(2,1)S(1)}, u32[]{:S(2)}, u32[]{:S(2)}) collective-permute-start(bf16[2,32,512]{2,1,0:T(8,128)(2,1)S(1)} %get-tuple-element.41), channel_id=1, source_target_pairs={{0,10},{1,11},{2,8},{3,9},{4,14},{5,15},{6,12},{7,13},{8,2},{9,3},... | collective-permute-start | bytes 196616 | tf_op jit(solution)/shard_map/ppermute | solution.py:449
  53.1 1.6 %collective-permute-start.24 = (bf16[2,32,512]{2,1,0:T(8,128)(2,1)S(1)}, bf16[2,32,512]{2,1,0:T(8,128)(2,1)S(1)}, u32[]{:S(2)}, u32[]{:S(2)}) collective-permute-start(bf16[2,32,512]{2,1,0:T(8,128)(2,1)S(1)} %get-tuple-element.42), channel_id=1, source_target_pairs={{0,12},{1,13},{2,14},{3,15},{4,8},{5,9},{6,10},{7,11},{8,4},{9,5},... | collective-permute-start | bytes 196616 | tf_op jit(solution)/shard_map/ppermute | solution.py:449
  54.7 2.7 %collective-permute-start.25 = (bf16[2,32,512]{2,1,0:T(8,128)(2,1)S(1)}, bf16[2,32,512]{2,1,0:T(8,128)(2,1)S(1)}, u32[]{:S(2)}, u32[]{:S(2)}) collective-permute-start(bf16[2,32,512]{2,1,0:T(8,128)(2,1)S(1)} %get-tuple-element.43), channel_id=1, source_target_pairs={{0,14},{1,15},{2,12},{3,13},{4,10},{5,11},{6,8},{7,9},{8,6},{9,7},... | collective-permute-start | bytes 196616 | tf_op jit(solution)/shard_map/ppermute | solution.py:449
  57.4 2.9 %collective-permute-done.22.refs_4_ = bf16[2,32,512]{2,1,0:T(8,128)(2,1)S(1)} collective-permute-done((bf16[2,32,512]{2,1,0:T(8,128)(2,1)S(1)}, bf16[2,32,512]{2,1,0:T(8,128)(2,1)S(1)}, u32[]{:S(2)}, u32[]{:S(2)}) %collective-permute-start.22) | collective-permute-done | bytes 65568 | tf_op jit(solution)/shard_map/ppermute | solution.py:449
  60.3 2.2 %collective-permute-done.23.refs_5_ = bf16[2,32,512]{2,1,0:T(8,128)(2,1)S(1)} collective-permute-done((bf16[2,32,512]{2,1,0:T(8,128)(2,1)S(1)}, bf16[2,32,512]{2,1,0:T(8,128)(2,1)S(1)}, u32[]{:S(2)}, u32[]{:S(2)}) %collective-permute-start.23) | collective-permute-done | bytes 65568 | tf_op jit(solution)/shard_map/ppermute | solution.py:449
  65.1 1.9 %finish.1 = f32[512,512]{1,0:T(8,128)} custom-call(s32[1]{0:T(128)} %bitcast.own_ref, bf16[2,32,512]{2,1,0:T(8,128)(2,1)S(1)} %get-tuple-element.36.refs_0_, bf16[2,32,512]{2,1,0:T(8,128)(2,1)S(1)} %collective-permute-done.19.refs_1_, bf16[2,32,512]{2,1,0:T(8,128)(2,1)S(1)} %collective-permute-done.20.refs_2_, ...), custom_call_target="tpu_custom_call" | custom-call | tf_op jit(solution)/shard_map/finish/pallas_call | solution.py:409
  (82 shorter events, 8.7 us)
Async XLA Ops:
  1.1 8.0 %collective-permute-start = (bf16[32,512]{1,0:T(8,128)(2,1)S(1)}, bf16[32,512]{1,0:T(8,128)(2,1)S(1)}, u32[]{:S(2)}, u32[]{:S(2)}) collective-permute-start(bf16[32,512]{1,0:T(8,128)(2,1)S(1)} %get-tuple-element.55), channel_id=1, source_target_pairs={{4,8},{8,4},{5,9},{9,5},{6,10},{10,6},{7,11},{11,7},{20,24},{24,20... | collective-permute-start | bytes 98312 | tf_op jit(solution)/shard_map/ppermute | solution.py:430
  1.9 7.8 %collective-permute-start.1 = (bf16[32,512]{1,0:T(8,128)(2,1)S(1)}, bf16[32,512]{1,0:T(8,128)(2,1)S(1)}, u32[]{:S(2)}, u32[]{:S(2)}) collective-permute-start(bf16[32,512]{1,0:T(8,128)(2,1)S(1)} %get-tuple-element.56), channel_id=1, source_target_pairs={{0,4},{8,12},{4,0},{12,8},{1,5},{9,13},{5,1},{13,9},{2,6},{10,14},... | collective-permute-start | bytes 98312 | tf_op jit(solution)/shard_map/ppermute | solution.py:430
  9.9 4.1 %collective-permute-start.3 = (bf16[32,512]{1,0:T(8,128)(2,1)S(1)}, bf16[32,512]{1,0:T(8,128)(2,1)S(1)}, u32[]{:S(2)}, u32[]{:S(2)}) collective-permute-start(bf16[32,512]{1,0:T(8,128)(2,1)S(1)} %get-tuple-element.51), channel_id=1, source_target_pairs={{0,1},{2,3},{1,0},{3,2},{4,5},{6,7},{5,4},{7,6},{8,9},{10,11},{9,8... | collective-permute-start | bytes 98312 | tf_op jit(solution)/shard_map/ppermute | solution.py:430
  10.0 4.0 %collective-permute-start.2 = (bf16[32,512]{1,0:T(8,128)(2,1)S(1)}, bf16[32,512]{1,0:T(8,128)(2,1)S(1)}, u32[]{:S(2)}, u32[]{:S(2)}) collective-permute-start(bf16[32,512]{1,0:T(8,128)(2,1)S(1)} %get-tuple-element.52), channel_id=1, source_target_pairs={{1,2},{2,1},{5,6},{6,5},{9,10},{10,9},{13,14},{14,13},{17,18},{18,... | collective-permute-start | bytes 98312 | tf_op jit(solution)/shard_map/ppermute | solution.py:430
  19.9 9.4 %collective-permute-start.4 = (bf16[2,32,512]{2,1,0:T(8,128)(2,1)S(1)}, bf16[2,32,512]{2,1,0:T(8,128)(2,1)S(1)}, u32[]{:S(2)}, u32[]{:S(2)}) collective-permute-start(bf16[2,32,512]{2,1,0:T(8,128)(2,1)S(1)} %get-tuple-element.29), channel_id=1, source_target_pairs={{0,2},{1,3},{2,0},{3,1},{4,6},{5,7},{6,4},{7,5},{8,10},{9,11},{10,... | collective-permute-start | bytes 196616 | tf_op jit(solution)/shard_map/ppermute | solution.py:449
  23.4 7.3 %collective-permute-start.5 = (bf16[2,32,512]{2,1,0:T(8,128)(2,1)S(1)}, bf16[2,32,512]{2,1,0:T(8,128)(2,1)S(1)}, u32[]{:S(2)}, u32[]{:S(2)}) collective-permute-start(bf16[2,32,512]{2,1,0:T(8,128)(2,1)S(1)} %get-tuple-element.30), channel_id=1, source_target_pairs={{0,4},{1,5},{2,6},{3,7},{4,0},{5,1},{6,2},{7,3},{8,12},{9,13},{10,... | collective-permute-start | bytes 196616 | tf_op jit(solution)/shard_map/ppermute | solution.py:449
  25.4 7.7 %collective-permute-start.6 = (bf16[2,32,512]{2,1,0:T(8,128)(2,1)S(1)}, bf16[2,32,512]{2,1,0:T(8,128)(2,1)S(1)}, u32[]{:S(2)}, u32[]{:S(2)}) collective-permute-start(bf16[2,32,512]{2,1,0:T(8,128)(2,1)S(1)} %get-tuple-element.31), channel_id=1, source_target_pairs={{0,6},{1,7},{2,4},{3,5},{4,2},{5,3},{6,0},{7,1},{8,14},{9,15},{10,... | collective-permute-start | bytes 196616 | tf_op jit(solution)/shard_map/ppermute | solution.py:449
  25.4 9.3 %collective-permute-start.7 = (bf16[2,32,512]{2,1,0:T(8,128)(2,1)S(1)}, bf16[2,32,512]{2,1,0:T(8,128)(2,1)S(1)}, u32[]{:S(2)}, u32[]{:S(2)}) collective-permute-start(bf16[2,32,512]{2,1,0:T(8,128)(2,1)S(1)} %get-tuple-element.32), channel_id=1, source_target_pairs={{0,8},{1,9},{2,10},{3,11},{4,12},{5,13},{6,14},{7,15},{8,0},{9,1},... | collective-permute-start | bytes 196616 | tf_op jit(solution)/shard_map/ppermute | solution.py:449
  26.8 12.1 %collective-permute-start.8 = (bf16[2,32,512]{2,1,0:T(8,128)(2,1)S(1)}, bf16[2,32,512]{2,1,0:T(8,128)(2,1)S(1)}, u32[]{:S(2)}, u32[]{:S(2)}) collective-permute-start(bf16[2,32,512]{2,1,0:T(8,128)(2,1)S(1)} %get-tuple-element.33), channel_id=1, source_target_pairs={{0,10},{1,11},{2,8},{3,9},{4,14},{5,15},{6,12},{7,13},{8,2},{9,3},... | collective-permute-start | bytes 196616 | tf_op jit(solution)/shard_map/ppermute | solution.py:449
  29.2 9.7 %collective-permute-start.9 = (bf16[2,32,512]{2,1,0:T(8,128)(2,1)S(1)}, bf16[2,32,512]{2,1,0:T(8,128)(2,1)S(1)}, u32[]{:S(2)}, u32[]{:S(2)}) collective-permute-start(bf16[2,32,512]{2,1,0:T(8,128)(2,1)S(1)} %get-tuple-element.34), channel_id=1, source_target_pairs={{0,12},{1,13},{2,14},{3,15},{4,8},{5,9},{6,10},{7,11},{8,4},{9,5},... | collective-permute-start | bytes 196616 | tf_op jit(solution)/shard_map/ppermute | solution.py:449
  30.7 8.7 %collective-permute-start.10 = (bf16[2,32,512]{2,1,0:T(8,128)(2,1)S(1)}, bf16[2,32,512]{2,1,0:T(8,128)(2,1)S(1)}, u32[]{:S(2)}, u32[]{:S(2)}) collective-permute-start(bf16[2,32,512]{2,1,0:T(8,128)(2,1)S(1)} %get-tuple-element.35), channel_id=1, source_target_pairs={{0,14},{1,15},{2,12},{3,13},{4,10},{5,11},{6,8},{7,9},{8,6},{9,7},... | collective-permute-start | bytes 196616 | tf_op jit(solution)/shard_map/ppermute | solution.py:449
  33.1 6.4 %collective-permute-start.11 = (bf16[2,32,512]{2,1,0:T(8,128)(2,1)S(1)}, bf16[2,32,512]{2,1,0:T(8,128)(2,1)S(1)}, u32[]{:S(2)}, u32[]{:S(2)}) collective-permute-start(bf16[2,32,512]{2,1,0:T(8,128)(2,1)S(1)} %get-tuple-element.28.refs_0_), channel_id=1, source_target_pairs={{0,1},{1,0},{2,3},{3,2},{4,5},{5,4},{6,7},{7,6},{8,9},{9,8},{10,11... | collective-permute-start | bytes 196616 | tf_op jit(solution)/shard_map/ppermute | solution.py:449
  34.7 5.3 %collective-permute-start.12 = (bf16[2,32,512]{2,1,0:T(8,128)(2,1)S(1)}, bf16[2,32,512]{2,1,0:T(8,128)(2,1)S(1)}, u32[]{:S(2)}, u32[]{:S(2)}) collective-permute-start(bf16[2,32,512]{2,1,0:T(8,128)(2,1)S(1)} %collective-permute-done.4.refs_1_), channel_id=1, source_target_pairs={{0,1},{1,0},{2,3},{3,2},{4,5},{5,4},{6,7},{7,6},{8,9},{9,8},{10,11... | collective-permute-start | bytes 196616 | tf_op jit(solution)/shard_map/ppermute | solution.py:449
  38.9 1.5 %collective-permute-start.14 = (bf16[2,32,512]{2,1,0:T(8,128)(2,1)S(1)}, bf16[2,32,512]{2,1,0:T(8,128)(2,1)S(1)}, u32[]{:S(2)}, u32[]{:S(2)}) collective-permute-start(bf16[2,32,512]{2,1,0:T(8,128)(2,1)S(1)} %collective-permute-done.6.refs_3_), channel_id=1, source_target_pairs={{0,1},{1,0},{2,3},{3,2},{4,5},{5,4},{6,7},{7,6},{8,9},{9,8},{10,11... | collective-permute-start | bytes 196616 | tf_op jit(solution)/shard_map/ppermute | solution.py:449
  46.0 7.1 %collective-permute-start.19 = (bf16[2,32,512]{2,1,0:T(8,128)(2,1)S(1)}, bf16[2,32,512]{2,1,0:T(8,128)(2,1)S(1)}, u32[]{:S(2)}, u32[]{:S(2)}) collective-permute-start(bf16[2,32,512]{2,1,0:T(8,128)(2,1)S(1)} %get-tuple-element.37), channel_id=1, source_target_pairs={{0,2},{1,3},{2,0},{3,1},{4,6},{5,7},{6,4},{7,5},{8,10},{9,11},{10,... | collective-permute-start | bytes 196616 | tf_op jit(solution)/shard_map/ppermute | solution.py:449
  46.8 7.9 %collective-permute-start.20 = (bf16[2,32,512]{2,1,0:T(8,128)(2,1)S(1)}, bf16[2,32,512]{2,1,0:T(8,128)(2,1)S(1)}, u32[]{:S(2)}, u32[]{:S(2)}) collective-permute-start(bf16[2,32,512]{2,1,0:T(8,128)(2,1)S(1)} %get-tuple-element.38), channel_id=1, source_target_pairs={{0,4},{1,5},{2,6},{3,7},{4,0},{5,1},{6,2},{7,3},{8,12},{9,13},{10,... | collective-permute-start | bytes 196616 | tf_op jit(solution)/shard_map/ppermute | solution.py:449
  49.2 8.2 %collective-permute-start.21 = (bf16[2,32,512]{2,1,0:T(8,128)(2,1)S(1)}, bf16[2,32,512]{2,1,0:T(8,128)(2,1)S(1)}, u32[]{:S(2)}, u32[]{:S(2)}) collective-permute-start(bf16[2,32,512]{2,1,0:T(8,128)(2,1)S(1)} %get-tuple-element.39), channel_id=1, source_target_pairs={{0,6},{1,7},{2,4},{3,5},{4,2},{5,3},{6,0},{7,1},{8,14},{9,15},{10,... | collective-permute-start | bytes 196616 | tf_op jit(solution)/shard_map/ppermute | solution.py:449
  49.8 10.6 %collective-permute-start.22 = (bf16[2,32,512]{2,1,0:T(8,128)(2,1)S(1)}, bf16[2,32,512]{2,1,0:T(8,128)(2,1)S(1)}, u32[]{:S(2)}, u32[]{:S(2)}) collective-permute-start(bf16[2,32,512]{2,1,0:T(8,128)(2,1)S(1)} %get-tuple-element.40), channel_id=1, source_target_pairs={{0,8},{1,9},{2,10},{3,11},{4,12},{5,13},{6,14},{7,15},{8,0},{9,1},... | collective-permute-start | bytes 196616 | tf_op jit(solution)/shard_map/ppermute | solution.py:449
  52.1 10.5 %collective-permute-start.23 = (bf16[2,32,512]{2,1,0:T(8,128)(2,1)S(1)}, bf16[2,32,512]{2,1,0:T(8,128)(2,1)S(1)}, u32[]{:S(2)}, u32[]{:S(2)}) collective-permute-start(bf16[2,32,512]{2,1,0:T(8,128)(2,1)S(1)} %get-tuple-element.41), channel_id=1, source_target_pairs={{0,10},{1,11},{2,8},{3,9},{4,14},{5,15},{6,12},{7,13},{8,2},{9,3},... | collective-permute-start | bytes 196616 | tf_op jit(solution)/shard_map/ppermute | solution.py:449
  53.1 9.5 %collective-permute-start.24 = (bf16[2,32,512]{2,1,0:T(8,128)(2,1)S(1)}, bf16[2,32,512]{2,1,0:T(8,128)(2,1)S(1)}, u32[]{:S(2)}, u32[]{:S(2)}) collective-permute-start(bf16[2,32,512]{2,1,0:T(8,128)(2,1)S(1)} %get-tuple-element.42), channel_id=1, source_target_pairs={{0,12},{1,13},{2,14},{3,15},{4,8},{5,9},{6,10},{7,11},{8,4},{9,5},... | collective-permute-start | bytes 196616 | tf_op jit(solution)/shard_map/ppermute | solution.py:449
  54.7 8.4 %collective-permute-start.25 = (bf16[2,32,512]{2,1,0:T(8,128)(2,1)S(1)}, bf16[2,32,512]{2,1,0:T(8,128)(2,1)S(1)}, u32[]{:S(2)}, u32[]{:S(2)}) collective-permute-start(bf16[2,32,512]{2,1,0:T(8,128)(2,1)S(1)} %get-tuple-element.43), channel_id=1, source_target_pairs={{0,14},{1,15},{2,12},{3,13},{4,10},{5,11},{6,8},{7,9},{8,6},{9,7},... | collective-permute-start | bytes 196616 | tf_op jit(solution)/shard_map/ppermute | solution.py:449
  57.4 5.7 %collective-permute-start.26 = (bf16[2,32,512]{2,1,0:T(8,128)(2,1)S(1)}, bf16[2,32,512]{2,1,0:T(8,128)(2,1)S(1)}, u32[]{:S(2)}, u32[]{:S(2)}) collective-permute-start(bf16[2,32,512]{2,1,0:T(8,128)(2,1)S(1)} %get-tuple-element.36.refs_0_), channel_id=1, source_target_pairs={{0,1},{1,0},{2,3},{3,2},{4,5},{5,4},{6,7},{7,6},{8,9},{9,8},{10,11... | collective-permute-start | bytes 196616 | tf_op jit(solution)/shard_map/ppermute | solution.py:449
  60.3 3.3 %collective-permute-start.27 = (bf16[2,32,512]{2,1,0:T(8,128)(2,1)S(1)}, bf16[2,32,512]{2,1,0:T(8,128)(2,1)S(1)}, u32[]{:S(2)}, u32[]{:S(2)}) collective-permute-start(bf16[2,32,512]{2,1,0:T(8,128)(2,1)S(1)} %collective-permute-done.19.refs_1_), channel_id=1, source_target_pairs={{0,1},{1,0},{2,3},{3,2},{4,5},{5,4},{6,7},{7,6},{8,9},{9,8},{10,11... | collective-permute-start | bytes 196616 | tf_op jit(solution)/shard_map/ppermute | solution.py:449
  62.6 1.5 %collective-permute-start.29 = (bf16[2,32,512]{2,1,0:T(8,128)(2,1)S(1)}, bf16[2,32,512]{2,1,0:T(8,128)(2,1)S(1)}, u32[]{:S(2)}, u32[]{:S(2)}) collective-permute-start(bf16[2,32,512]{2,1,0:T(8,128)(2,1)S(1)} %collective-permute-done.21.refs_3_), channel_id=1, source_target_pairs={{0,1},{1,0},{2,3},{3,2},{4,5},{5,4},{6,7},{7,6},{8,9},{9,8},{10,11... | collective-permute-start | bytes 196616 | tf_op jit(solution)/shard_map/ppermute | solution.py:449
  (20 other events, 154.5 us)

commit v7 on v6

--- a/solution.py
+++ b/solution.py
@@ -435,10 +435,7 @@
 
 
 def exchange_plan(row_devices, col_devices):
-    masks = [
-        row * col_devices + col for row in range(row_devices) for col in range(0, col_devices, 2)
-    ]
-    return masks, 2
+    return list(range(row_devices * col_devices - 2, -1, -2)), 2
 
 
 def trade(masks, slabs):
@@ -448,10 +445,7 @@
     def swap(slab, mask):
         return lax.ppermute(slab, axes, [(i, i ^ mask) for i in range(devices)])
 
-    mine = dict(zip(masks, slabs))
-    for mask in sorted(masks[1:], reverse=True):
-        mine[mask] = swap(mine[mask], mask)
-    mine = [mine[mask] for mask in masks]
+    mine = [swap(slab, mask) if mask else slab for mask, slab in zip(masks, slabs)]
     return mine, [swap(slab, 1) for slab in mine]
 
 

time: 67.3 us -> 65.7 us (0.976)
  waiting for transfers between devices: 13.8 us -> 7.67 us
  starting transfers between devices: 35 us -> 39.6 us
    ppermute x30, waiting for transfers between devices: 13.2 us -> 7.06 us  [swap(): return lax.ppermute(slab, axes, [(i, i ^ mask) for i in range(devices)])]
    ppermute x30, starting transfers between devices: 27.4 us -> 32 us  [swap(): return lax.ppermute(slab, axes, [(i, i ^ mask) for i in range(devices)])]
  transfers between devices with their start and end apart: 34 -> 34, of which waited for: 15 -> 16; matrix products, arithmetic and copies ran while one was open for 0% -> 0% of each run, Pallas kernels for 4% -> 4%
where the time goes in v7:
time: 65.7 us; the launch traced here: 65.5 us
  starting transfers between devices  39.6 us (60%)
  Pallas kernels  14.9 us (23%)
  waiting for transfers between devices  7.67 us (12%)
  local copies, waits for them, and re-layouts  2.91 us (4%)
    ppermute x30, starting transfers between devices, swap(): return lax.ppermute(slab, axes, [(i, i ^ mask) for i in range(devices)])  32 us
    ppermute x4, starting transfers between devices, swap(): return lax.ppermute(edge, axis, pairs + [(b, a) for a, b in pairs])  7.57 us
    ppermute x30, waiting for transfers between devices, swap(): return lax.ppermute(slab, axes, [(i, i ^ mask) for i in range(devices)])  7.06 us
    pallas_call x1, Pallas kernels, mix(): pl.pallas_call(functools.partial(mix_kernel, rows=rows, cols=cols, masks=...  5.76 us
    pallas_call x1, Pallas kernels, attend(): pl.pallas_call(functools.partial(attend_kernel, slabs=slabs, sets=sets),...  4.56 us
    pallas_call x1, Pallas kernels, expand(): pl.pallas_call(expand_kernel, in_specs=[vmem()] * 2, out_specs=vmem(), ou...  2.15 us
    pallas_call x1, Pallas kernels, finish(): pl.pallas_call(functools.partial(finish_kernel, masks=masks), in_specs=[p...  1.94 us
    unnamed x20, local copies, waits for them, and re-layouts  1.87 us
  transfers between devices with their start and end apart: 34, of which 16 were waited for; matrix products, arithmetic and copies ran while one was open for 0% of the time, Pallas kernels for 4%

profile of v7, /device:TPU:0, one launch (start us, length us, event | category | flops | bytes accessed | tf_op | source)
XLA Modules:
  0.0 65.5 jit_solution(13578576246181127787)
XLA Ops:
  0.0 0.9 %slice_bitcast_fusion.1 = (f32[32,512]{1,0:T(8,128)S(1)}, f32[32,512]{1,0:T(8,128)S(1)}) fusion(f32[16,32,512]{2,1,0:T(8,128)} %param.8), kind=kLoop, calls=%fused_computation.2 | loop fusion | bytes 262144 | tf_op jit(solution)/shard_map/squeeze | solution.py:492
  1.1 0.8 %collective-permute-start = (bf16[32,512]{1,0:T(8,128)(2,1)S(1)}, bf16[32,512]{1,0:T(8,128)(2,1)S(1)}, u32[]{:S(2)}, u32[]{:S(2)}) collective-permute-start(bf16[32,512]{1,0:T(8,128)(2,1)S(1)} %get-tuple-element.55), channel_id=1, source_target_pairs={{4,8},{8,4},{5,9},{9,5},{6,10},{10,6},{7,11},{11,7},{20,24},{24,20... | collective-permute-start | bytes 98312 | tf_op jit(solution)/shard_map/ppermute | solution.py:430
  1.9 5.9 %collective-permute-start.1 = (bf16[32,512]{1,0:T(8,128)(2,1)S(1)}, bf16[32,512]{1,0:T(8,128)(2,1)S(1)}, u32[]{:S(2)}, u32[]{:S(2)}) collective-permute-start(bf16[32,512]{1,0:T(8,128)(2,1)S(1)} %get-tuple-element.56), channel_id=1, source_target_pairs={{0,4},{8,12},{4,0},{12,8},{1,5},{9,13},{5,1},{13,9},{2,6},{10,14},... | collective-permute-start | bytes 98312 | tf_op jit(solution)/shard_map/ppermute | solution.py:430
  8.2 0.8 %copy-done.7 = bf16[512,512]{1,0:T(8,128)(2,1)} copy-done((bf16[512,512]{1,0:T(8,128)(2,1)}, bf16[512,512]{1,0:T(8,128)(2,1)S(1)}, u32[]{:S(2)}) %copy-start.7) | copy-done | bytes 524312
  9.1 0.6 collective-permute-done.1
  10.0 0.8 %collective-permute-start.2 = (bf16[32,512]{1,0:T(8,128)(2,1)S(1)}, bf16[32,512]{1,0:T(8,128)(2,1)S(1)}, u32[]{:S(2)}, u32[]{:S(2)}) collective-permute-start(bf16[32,512]{1,0:T(8,128)(2,1)S(1)} %get-tuple-element.52), channel_id=1, source_target_pairs={{1,2},{2,1},{5,6},{6,5},{9,10},{10,9},{13,14},{14,13},{17,18},{18,... | collective-permute-start | bytes 98312 | tf_op jit(solution)/shard_map/ppermute | solution.py:430
  10.8 1.0 %copy-done.8 = bf16[512,512]{1,0:T(8,128)(2,1)S(1)} copy-done((bf16[512,512]{1,0:T(8,128)(2,1)S(1)}, bf16[512,512]{1,0:T(8,128)(2,1)}, u32[]{:S(2)}) %copy-start.8) | copy-done | bytes 524312
  11.8 2.2 %expand.1.expanded_ref = f32[8448,128]{1,0:T(8,128)S(1)} custom-call(bf16[512,512]{1,0:T(8,128)(2,1)S(1)} %copy-done.8, bf16[512,2048]{1,0:T(8,128)(2,1)S(1)} %copy-done), custom_call_target="tpu_custom_call" | custom-call | flops 10000000000 | bytes 6815744 | tf_op jit(solution)/shard_map/expand/pallas_call | solution.py:111
  14.1 5.8 %mix.1 = (f32[512,512]{1,0:T(8,128)S(1)}, bf16[2,32,512]{2,1,0:T(8,128)(2,1)S(1)}, bf16[2,32,512]{2,1,0:T(8,128)(2,1)S(1)}, bf16[2,32,512]{2,1,0:T(8,128)(2,1)S(...) custom-call(s32[1]{0:T(128)} %bitcast.own_ref, ...), custom_call_target="tpu_custom_call" | custom-call | flops 1073741824 | bytes 11010048 | tf_op jit(solution)/shard_map/mix/pallas_call | solution.py:241
  19.9 4.3 %collective-permute-start.4 = (bf16[2,32,512]{2,1,0:T(8,128)(2,1)S(1)}, bf16[2,32,512]{2,1,0:T(8,128)(2,1)S(1)}, u32[]{:S(2)}, u32[]{:S(2)}) collective-permute-start(bf16[2,32,512]{2,1,0:T(8,128)(2,1)S(1)} %get-tuple-element.28), channel_id=1, source_target_pairs={{0,14},{1,15},{2,12},{3,13},{4,10},{5,11},{6,8},{7,9},{8,6},{9,7},... | collective-permute-start | bytes 196616 | tf_op jit(solution)/shard_map/ppermute | solution.py:446
  24.2 2.5 %collective-permute-start.5 = (bf16[2,32,512]{2,1,0:T(8,128)(2,1)S(1)}, bf16[2,32,512]{2,1,0:T(8,128)(2,1)S(1)}, u32[]{:S(2)}, u32[]{:S(2)}) collective-permute-start(bf16[2,32,512]{2,1,0:T(8,128)(2,1)S(1)} %get-tuple-element.29), channel_id=1, source_target_pairs={{0,12},{1,13},{2,14},{3,15},{4,8},{5,9},{6,10},{7,11},{8,4},{9,5},... | collective-permute-start | bytes 196616 | tf_op jit(solution)/shard_map/ppermute | solution.py:446
  26.7 0.9 %collective-permute-start.7 = (bf16[2,32,512]{2,1,0:T(8,128)(2,1)S(1)}, bf16[2,32,512]{2,1,0:T(8,128)(2,1)S(1)}, u32[]{:S(2)}, u32[]{:S(2)}) collective-permute-start(bf16[2,32,512]{2,1,0:T(8,128)(2,1)S(1)} %get-tuple-element.31), channel_id=1, source_target_pairs={{0,8},{1,9},{2,10},{3,11},{4,12},{5,13},{6,14},{7,15},{8,0},{9,1},... | collective-permute-start | bytes 196616 | tf_op jit(solution)/shard_map/ppermute | solution.py:446
  27.6 3.1 %collective-permute-start.8 = (bf16[2,32,512]{2,1,0:T(8,128)(2,1)S(1)}, bf16[2,32,512]{2,1,0:T(8,128)(2,1)S(1)}, u32[]{:S(2)}, u32[]{:S(2)}) collective-permute-start(bf16[2,32,512]{2,1,0:T(8,128)(2,1)S(1)} %get-tuple-element.32), channel_id=1, source_target_pairs={{0,6},{1,7},{2,4},{3,5},{4,2},{5,3},{6,0},{7,1},{8,14},{9,15},{10,... | collective-permute-start | bytes 196616 | tf_op jit(solution)/shard_map/ppermute | solution.py:446
  30.7 1.8 %collective-permute-start.9 = (bf16[2,32,512]{2,1,0:T(8,128)(2,1)S(1)}, bf16[2,32,512]{2,1,0:T(8,128)(2,1)S(1)}, u32[]{:S(2)}, u32[]{:S(2)}) collective-permute-start(bf16[2,32,512]{2,1,0:T(8,128)(2,1)S(1)} %get-tuple-element.33), channel_id=1, source_target_pairs={{0,4},{1,5},{2,6},{3,7},{4,0},{5,1},{6,2},{7,3},{8,12},{9,13},{10,... | collective-permute-start | bytes 196616 | tf_op jit(solution)/shard_map/ppermute | solution.py:446
  32.5 3.3 %collective-permute-start.10 = (bf16[2,32,512]{2,1,0:T(8,128)(2,1)S(1)}, bf16[2,32,512]{2,1,0:T(8,128)(2,1)S(1)}, u32[]{:S(2)}, u32[]{:S(2)}) collective-permute-start(bf16[2,32,512]{2,1,0:T(8,128)(2,1)S(1)} %get-tuple-element.34), channel_id=1, source_target_pairs={{0,2},{1,3},{2,0},{3,1},{4,6},{5,7},{6,4},{7,5},{8,10},{9,11},{10,... | collective-permute-start | bytes 196616 | tf_op jit(solution)/shard_map/ppermute | solution.py:446
  35.8 1.0 %collective-permute-start.18 = (bf16[2,32,512]{2,1,0:T(8,128)(2,1)S(1)}, bf16[2,32,512]{2,1,0:T(8,128)(2,1)S(1)}, u32[]{:S(2)}, u32[]{:S(2)}) collective-permute-start(bf16[2,32,512]{2,1,0:T(8,128)(2,1)S(1)} %get-tuple-element.35.refs_7_), channel_id=1, source_target_pairs={{0,1},{1,0},{2,3},{3,2},{4,5},{5,4},{6,7},{7,6},{8,9},{9,8},{10,11... | collective-permute-start | bytes 196616 | tf_op jit(solution)/shard_map/ppermute | solution.py:446
  37.6 1.0 %collective-permute-done.9.refs_5_ = bf16[2,32,512]{2,1,0:T(8,128)(2,1)S(1)} collective-permute-done((bf16[2,32,512]{2,1,0:T(8,128)(2,1)S(1)}, bf16[2,32,512]{2,1,0:T(8,128)(2,1)S(1)}, u32[]{:S(2)}, u32[]{:S(2)}) %collective-permute-start.9) | collective-permute-done | bytes 65568 | tf_op jit(solution)/shard_map/ppermute | solution.py:446
  40.8 4.6 %attend.1 = (bf16[2,32,512]{2,1,0:T(8,128)(2,1)S(1)}, bf16[2,32,512]{2,1,0:T(8,128)(2,1)S(1)}, bf16[2,32,512]{2,1,0:T(8,128)(2,1)S(1)}, bf16[2,32,512]{2,1,0:T(8...) custom-call(bf16[2,32,512]{2,1,0:T(8,128)(2,1)S(1)} %collective-perm, ...), custom_call_target="tpu_custom_call" | custom-call | flops 1073741824 | bytes 2621440 | tf_op jit(solution)/shard_map/attend/pallas_call | solution.py:358
  45.4 2.4 %collective-permute-start.19 = (bf16[2,32,512]{2,1,0:T(8,128)(2,1)S(1)}, bf16[2,32,512]{2,1,0:T(8,128)(2,1)S(1)}, u32[]{:S(2)}, u32[]{:S(2)}) collective-permute-start(bf16[2,32,512]{2,1,0:T(8,128)(2,1)S(1)} %get-tuple-element.36), channel_id=1, source_target_pairs={{0,14},{1,15},{2,12},{3,13},{4,10},{5,11},{6,8},{7,9},{8,6},{9,7},... | collective-permute-start | bytes 196616 | tf_op jit(solution)/shard_map/ppermute | solution.py:446
  47.8 2.1 %collective-permute-start.20 = (bf16[2,32,512]{2,1,0:T(8,128)(2,1)S(1)}, bf16[2,32,512]{2,1,0:T(8,128)(2,1)S(1)}, u32[]{:S(2)}, u32[]{:S(2)}) collective-permute-start(bf16[2,32,512]{2,1,0:T(8,128)(2,1)S(1)} %get-tuple-element.37), channel_id=1, source_target_pairs={{0,12},{1,13},{2,14},{3,15},{4,8},{5,9},{6,10},{7,11},{8,4},{9,5},... | collective-permute-start | bytes 196616 | tf_op jit(solution)/shard_map/ppermute | solution.py:446
  49.9 3.2 %collective-permute-start.22 = (bf16[2,32,512]{2,1,0:T(8,128)(2,1)S(1)}, bf16[2,32,512]{2,1,0:T(8,128)(2,1)S(1)}, u32[]{:S(2)}, u32[]{:S(2)}) collective-permute-start(bf16[2,32,512]{2,1,0:T(8,128)(2,1)S(1)} %get-tuple-element.39), channel_id=1, source_target_pairs={{0,8},{1,9},{2,10},{3,11},{4,12},{5,13},{6,14},{7,15},{8,0},{9,1},... | collective-permute-start | bytes 196616 | tf_op jit(solution)/shard_map/ppermute | solution.py:446
  53.1 4.2 %collective-permute-start.24 = (bf16[2,32,512]{2,1,0:T(8,128)(2,1)S(1)}, bf16[2,32,512]{2,1,0:T(8,128)(2,1)S(1)}, u32[]{:S(2)}, u32[]{:S(2)}) collective-permute-start(bf16[2,32,512]{2,1,0:T(8,128)(2,1)S(1)} %get-tuple-element.41), channel_id=1, source_target_pairs={{0,4},{1,5},{2,6},{3,7},{4,0},{5,1},{6,2},{7,3},{8,12},{9,13},{10,... | collective-permute-start | bytes 196616 | tf_op jit(solution)/shard_map/ppermute | solution.py:446
  57.4 2.8 %collective-permute-done.21.refs_2_ = bf16[2,32,512]{2,1,0:T(8,128)(2,1)S(1)} collective-permute-done((bf16[2,32,512]{2,1,0:T(8,128)(2,1)S(1)}, bf16[2,32,512]{2,1,0:T(8,128)(2,1)S(1)}, u32[]{:S(2)}, u32[]{:S(2)}) %collective-permute-start.21) | collective-permute-done | bytes 65568 | tf_op jit(solution)/shard_map/ppermute | solution.py:446
  63.6 1.9 %finish.1 = f32[512,512]{1,0:T(8,128)} custom-call(s32[1]{0:T(128)} %bitcast.own_ref, bf16[2,32,512]{2,1,0:T(8,128)(2,1)S(1)} %collective-permute-done.19.refs_0_, bf16[2,32,512]{2,1,0:T(8,128)(2,1)S(1)} %collective-permute-done.20.refs_1_, bf16[2,32,512]{2,1,0:T(8,128)(2,1)S(1)} %collective-permute-done.21.refs_2_, ...), custom_call_target="tpu_custom_call" | custom-call | tf_op jit(solution)/shard_map/finish/pallas_call | solution.py:409
  (82 shorter events, 7.3 us)
Async XLA Ops:
  1.1 8.0 %collective-permute-start = (bf16[32,512]{1,0:T(8,128)(2,1)S(1)}, bf16[32,512]{1,0:T(8,128)(2,1)S(1)}, u32[]{:S(2)}, u32[]{:S(2)}) collective-permute-start(bf16[32,512]{1,0:T(8,128)(2,1)S(1)} %get-tuple-element.55), channel_id=1, source_target_pairs={{4,8},{8,4},{5,9},{9,5},{6,10},{10,6},{7,11},{11,7},{20,24},{24,20... | collective-permute-start | bytes 98312 | tf_op jit(solution)/shard_map/ppermute | solution.py:430
  1.9 7.8 %collective-permute-start.1 = (bf16[32,512]{1,0:T(8,128)(2,1)S(1)}, bf16[32,512]{1,0:T(8,128)(2,1)S(1)}, u32[]{:S(2)}, u32[]{:S(2)}) collective-permute-start(bf16[32,512]{1,0:T(8,128)(2,1)S(1)} %get-tuple-element.56), channel_id=1, source_target_pairs={{0,4},{8,12},{4,0},{12,8},{1,5},{9,13},{5,1},{13,9},{2,6},{10,14},... | collective-permute-start | bytes 98312 | tf_op jit(solution)/shard_map/ppermute | solution.py:430
  9.9 4.1 %collective-permute-start.3 = (bf16[32,512]{1,0:T(8,128)(2,1)S(1)}, bf16[32,512]{1,0:T(8,128)(2,1)S(1)}, u32[]{:S(2)}, u32[]{:S(2)}) collective-permute-start(bf16[32,512]{1,0:T(8,128)(2,1)S(1)} %get-tuple-element.51), channel_id=1, source_target_pairs={{0,1},{2,3},{1,0},{3,2},{4,5},{6,7},{5,4},{7,6},{8,9},{10,11},{9,8... | collective-permute-start | bytes 98312 | tf_op jit(solution)/shard_map/ppermute | solution.py:430
  10.0 4.0 %collective-permute-start.2 = (bf16[32,512]{1,0:T(8,128)(2,1)S(1)}, bf16[32,512]{1,0:T(8,128)(2,1)S(1)}, u32[]{:S(2)}, u32[]{:S(2)}) collective-permute-start(bf16[32,512]{1,0:T(8,128)(2,1)S(1)} %get-tuple-element.52), channel_id=1, source_target_pairs={{1,2},{2,1},{5,6},{6,5},{9,10},{10,9},{13,14},{14,13},{17,18},{18,... | collective-permute-start | bytes 98312 | tf_op jit(solution)/shard_map/ppermute | solution.py:430
  19.9 10.8 %collective-permute-start.4 = (bf16[2,32,512]{2,1,0:T(8,128)(2,1)S(1)}, bf16[2,32,512]{2,1,0:T(8,128)(2,1)S(1)}, u32[]{:S(2)}, u32[]{:S(2)}) collective-permute-start(bf16[2,32,512]{2,1,0:T(8,128)(2,1)S(1)} %get-tuple-element.28), channel_id=1, source_target_pairs={{0,14},{1,15},{2,12},{3,13},{4,10},{5,11},{6,8},{7,9},{8,6},{9,7},... | collective-permute-start | bytes 196616 | tf_op jit(solution)/shard_map/ppermute | solution.py:446
  24.2 8.3 %collective-permute-start.5 = (bf16[2,32,512]{2,1,0:T(8,128)(2,1)S(1)}, bf16[2,32,512]{2,1,0:T(8,128)(2,1)S(1)}, u32[]{:S(2)}, u32[]{:S(2)}) collective-permute-start(bf16[2,32,512]{2,1,0:T(8,128)(2,1)S(1)} %get-tuple-element.29), channel_id=1, source_target_pairs={{0,12},{1,13},{2,14},{3,15},{4,8},{5,9},{6,10},{7,11},{8,4},{9,5},... | collective-permute-start | bytes 196616 | tf_op jit(solution)/shard_map/ppermute | solution.py:446
  26.7 9.2 %collective-permute-start.6 = (bf16[2,32,512]{2,1,0:T(8,128)(2,1)S(1)}, bf16[2,32,512]{2,1,0:T(8,128)(2,1)S(1)}, u32[]{:S(2)}, u32[]{:S(2)}) collective-permute-start(bf16[2,32,512]{2,1,0:T(8,128)(2,1)S(1)} %get-tuple-element.30), channel_id=1, source_target_pairs={{0,10},{1,11},{2,8},{3,9},{4,14},{5,15},{6,12},{7,13},{8,2},{9,3},... | collective-permute-start | bytes 196616 | tf_op jit(solution)/shard_map/ppermute | solution.py:446
  26.7 10.4 %collective-permute-start.7 = (bf16[2,32,512]{2,1,0:T(8,128)(2,1)S(1)}, bf16[2,32,512]{2,1,0:T(8,128)(2,1)S(1)}, u32[]{:S(2)}, u32[]{:S(2)}) collective-permute-start(bf16[2,32,512]{2,1,0:T(8,128)(2,1)S(1)} %get-tuple-element.31), channel_id=1, source_target_pairs={{0,8},{1,9},{2,10},{3,11},{4,12},{5,13},{6,14},{7,15},{8,0},{9,1},... | collective-permute-start | bytes 196616 | tf_op jit(solution)/shard_map/ppermute | solution.py:446
  27.6 9.5 %collective-permute-start.8 = (bf16[2,32,512]{2,1,0:T(8,128)(2,1)S(1)}, bf16[2,32,512]{2,1,0:T(8,128)(2,1)S(1)}, u32[]{:S(2)}, u32[]{:S(2)}) collective-permute-start(bf16[2,32,512]{2,1,0:T(8,128)(2,1)S(1)} %get-tuple-element.32), channel_id=1, source_target_pairs={{0,6},{1,7},{2,4},{3,5},{4,2},{5,3},{6,0},{7,1},{8,14},{9,15},{10,... | collective-permute-start | bytes 196616 | tf_op jit(solution)/shard_map/ppermute | solution.py:446
  30.7 7.8 %collective-permute-start.9 = (bf16[2,32,512]{2,1,0:T(8,128)(2,1)S(1)}, bf16[2,32,512]{2,1,0:T(8,128)(2,1)S(1)}, u32[]{:S(2)}, u32[]{:S(2)}) collective-permute-start(bf16[2,32,512]{2,1,0:T(8,128)(2,1)S(1)} %get-tuple-element.33), channel_id=1, source_target_pairs={{0,4},{1,5},{2,6},{3,7},{4,0},{5,1},{6,2},{7,3},{8,12},{9,13},{10,... | collective-permute-start | bytes 196616 | tf_op jit(solution)/shard_map/ppermute | solution.py:446
  32.5 6.1 %collective-permute-start.10 = (bf16[2,32,512]{2,1,0:T(8,128)(2,1)S(1)}, bf16[2,32,512]{2,1,0:T(8,128)(2,1)S(1)}, u32[]{:S(2)}, u32[]{:S(2)}) collective-permute-start(bf16[2,32,512]{2,1,0:T(8,128)(2,1)S(1)} %get-tuple-element.34), channel_id=1, source_target_pairs={{0,2},{1,3},{2,0},{3,1},{4,6},{5,7},{6,4},{7,5},{8,10},{9,11},{10,... | collective-permute-start | bytes 196616 | tf_op jit(solution)/shard_map/ppermute | solution.py:446
  35.8 3.2 %collective-permute-start.18 = (bf16[2,32,512]{2,1,0:T(8,128)(2,1)S(1)}, bf16[2,32,512]{2,1,0:T(8,128)(2,1)S(1)}, u32[]{:S(2)}, u32[]{:S(2)}) collective-permute-start(bf16[2,32,512]{2,1,0:T(8,128)(2,1)S(1)} %get-tuple-element.35.refs_7_), channel_id=1, source_target_pairs={{0,1},{1,0},{2,3},{3,2},{4,5},{5,4},{6,7},{7,6},{8,9},{9,8},{10,11... | collective-permute-start | bytes 196616 | tf_op jit(solution)/shard_map/ppermute | solution.py:446
  37.0 2.1 %collective-permute-start.11 = (bf16[2,32,512]{2,1,0:T(8,128)(2,1)S(1)}, bf16[2,32,512]{2,1,0:T(8,128)(2,1)S(1)}, u32[]{:S(2)}, u32[]{:S(2)}) collective-permute-start(bf16[2,32,512]{2,1,0:T(8,128)(2,1)S(1)} %collective-permute-done.4.refs_0_), channel_id=1, source_target_pairs={{0,1},{1,0},{2,3},{3,2},{4,5},{5,4},{6,7},{7,6},{8,9},{9,8},{10,11... | collective-permute-start | bytes 196616 | tf_op jit(solution)/shard_map/ppermute | solution.py:446
  37.0 2.5 %collective-permute-start.12 = (bf16[2,32,512]{2,1,0:T(8,128)(2,1)S(1)}, bf16[2,32,512]{2,1,0:T(8,128)(2,1)S(1)}, u32[]{:S(2)}, u32[]{:S(2)}) collective-permute-start(bf16[2,32,512]{2,1,0:T(8,128)(2,1)S(1)} %collective-permute-done.5.refs_1_), channel_id=1, source_target_pairs={{0,1},{1,0},{2,3},{3,2},{4,5},{5,4},{6,7},{7,6},{8,9},{9,8},{10,11... | collective-permute-start | bytes 196616 | tf_op jit(solution)/shard_map/ppermute | solution.py:446
  45.4 7.7 %collective-permute-start.19 = (bf16[2,32,512]{2,1,0:T(8,128)(2,1)S(1)}, bf16[2,32,512]{2,1,0:T(8,128)(2,1)S(1)}, u32[]{:S(2)}, u32[]{:S(2)}) collective-permute-start(bf16[2,32,512]{2,1,0:T(8,128)(2,1)S(1)} %get-tuple-element.36), channel_id=1, source_target_pairs={{0,14},{1,15},{2,12},{3,13},{4,10},{5,11},{6,8},{7,9},{8,6},{9,7},... | collective-permute-start | bytes 196616 | tf_op jit(solution)/shard_map/ppermute | solution.py:446
  47.8 9.5 %collective-permute-start.20 = (bf16[2,32,512]{2,1,0:T(8,128)(2,1)S(1)}, bf16[2,32,512]{2,1,0:T(8,128)(2,1)S(1)}, u32[]{:S(2)}, u32[]{:S(2)}) collective-permute-start(bf16[2,32,512]{2,1,0:T(8,128)(2,1)S(1)} %get-tuple-element.37), channel_id=1, source_target_pairs={{0,12},{1,13},{2,14},{3,15},{4,8},{5,9},{6,10},{7,11},{8,4},{9,5},... | collective-permute-start | bytes 196616 | tf_op jit(solution)/shard_map/ppermute | solution.py:446
  49.9 10.3 %collective-permute-start.21 = (bf16[2,32,512]{2,1,0:T(8,128)(2,1)S(1)}, bf16[2,32,512]{2,1,0:T(8,128)(2,1)S(1)}, u32[]{:S(2)}, u32[]{:S(2)}) collective-permute-start(bf16[2,32,512]{2,1,0:T(8,128)(2,1)S(1)} %get-tuple-element.38), channel_id=1, source_target_pairs={{0,10},{1,11},{2,8},{3,9},{4,14},{5,15},{6,12},{7,13},{8,2},{9,3},... | collective-permute-start | bytes 196616 | tf_op jit(solution)/shard_map/ppermute | solution.py:446
  49.9 10.3 %collective-permute-start.22 = (bf16[2,32,512]{2,1,0:T(8,128)(2,1)S(1)}, bf16[2,32,512]{2,1,0:T(8,128)(2,1)S(1)}, u32[]{:S(2)}, u32[]{:S(2)}) collective-permute-start(bf16[2,32,512]{2,1,0:T(8,128)(2,1)S(1)} %get-tuple-element.39), channel_id=1, source_target_pairs={{0,8},{1,9},{2,10},{3,11},{4,12},{5,13},{6,14},{7,15},{8,0},{9,1},... | collective-permute-start | bytes 196616 | tf_op jit(solution)/shard_map/ppermute | solution.py:446
  53.1 7.6 %collective-permute-start.23 = (bf16[2,32,512]{2,1,0:T(8,128)(2,1)S(1)}, bf16[2,32,512]{2,1,0:T(8,128)(2,1)S(1)}, u32[]{:S(2)}, u32[]{:S(2)}) collective-permute-start(bf16[2,32,512]{2,1,0:T(8,128)(2,1)S(1)} %get-tuple-element.40), channel_id=1, source_target_pairs={{0,6},{1,7},{2,4},{3,5},{4,2},{5,3},{6,0},{7,1},{8,14},{9,15},{10,... | collective-permute-start | bytes 196616 | tf_op jit(solution)/shard_map/ppermute | solution.py:446
  53.1 8.1 %collective-permute-start.24 = (bf16[2,32,512]{2,1,0:T(8,128)(2,1)S(1)}, bf16[2,32,512]{2,1,0:T(8,128)(2,1)S(1)}, u32[]{:S(2)}, u32[]{:S(2)}) collective-permute-start(bf16[2,32,512]{2,1,0:T(8,128)(2,1)S(1)} %get-tuple-element.41), channel_id=1, source_target_pairs={{0,4},{1,5},{2,6},{3,7},{4,0},{5,1},{6,2},{7,3},{8,12},{9,13},{10,... | collective-permute-start | bytes 196616 | tf_op jit(solution)/shard_map/ppermute | solution.py:446
  57.4 4.3 %collective-permute-start.25 = (bf16[2,32,512]{2,1,0:T(8,128)(2,1)S(1)}, bf16[2,32,512]{2,1,0:T(8,128)(2,1)S(1)}, u32[]{:S(2)}, u32[]{:S(2)}) collective-permute-start(bf16[2,32,512]{2,1,0:T(8,128)(2,1)S(1)} %get-tuple-element.42), channel_id=1, source_target_pairs={{0,2},{1,3},{2,0},{3,1},{4,6},{5,7},{6,4},{7,5},{8,10},{9,11},{10,... | collective-permute-start | bytes 196616 | tf_op jit(solution)/shard_map/ppermute | solution.py:446
  60.2 1.6 %collective-permute-start.33 = (bf16[2,32,512]{2,1,0:T(8,128)(2,1)S(1)}, bf16[2,32,512]{2,1,0:T(8,128)(2,1)S(1)}, u32[]{:S(2)}, u32[]{:S(2)}) collective-permute-start(bf16[2,32,512]{2,1,0:T(8,128)(2,1)S(1)} %get-tuple-element.43.refs_7_), channel_id=1, source_target_pairs={{0,1},{1,0},{2,3},{3,2},{4,5},{5,4},{6,7},{7,6},{8,9},{9,8},{10,11... | collective-permute-start | bytes 196616 | tf_op jit(solution)/shard_map/ppermute | solution.py:446
  60.3 1.9 %collective-permute-start.26 = (bf16[2,32,512]{2,1,0:T(8,128)(2,1)S(1)}, bf16[2,32,512]{2,1,0:T(8,128)(2,1)S(1)}, u32[]{:S(2)}, u32[]{:S(2)}) collective-permute-start(bf16[2,32,512]{2,1,0:T(8,128)(2,1)S(1)} %collective-permute-done.19.refs_0_), channel_id=1, source_target_pairs={{0,1},{1,0},{2,3},{3,2},{4,5},{5,4},{6,7},{7,6},{8,9},{9,8},{10,11... | collective-permute-start | bytes 196616 | tf_op jit(solution)/shard_map/ppermute | solution.py:446
  60.7 1.6 %collective-permute-start.27 = (bf16[2,32,512]{2,1,0:T(8,128)(2,1)S(1)}, bf16[2,32,512]{2,1,0:T(8,128)(2,1)S(1)}, u32[]{:S(2)}, u32[]{:S(2)}) collective-permute-start(bf16[2,32,512]{2,1,0:T(8,128)(2,1)S(1)} %collective-permute-done.20.refs_1_), channel_id=1, source_target_pairs={{0,1},{1,0},{2,3},{3,2},{4,5},{5,4},{6,7},{7,6},{8,9},{9,8},{10,11... | collective-permute-start | bytes 196616 | tf_op jit(solution)/shard_map/ppermute | solution.py:446
  (20 other events, 151.2 us)

commit v8 on v7

--- a/solution.py
+++ b/solution.py
@@ -435,7 +435,13 @@
 
 
 def exchange_plan(row_devices, col_devices):
-    return list(range(row_devices * col_devices - 2, -1, -2)), 2
+    devices = row_devices * col_devices
+    crossing = list(range(devices - 2, devices // 2 - 1, -2))
+    others = list(range(devices // 2 - 2, 0, -2))
+    masks = crossing[:1]
+    for index, mask in enumerate(crossing[1:]):
+        masks += [mask] + others[index : index + 1]
+    return masks + [0], 2
 
 
 def trade(masks, slabs):

time: 65.7 us -> 62.6 us (0.953)
  starting transfers between devices: 39.6 us -> 34.9 us
  waiting for transfers between devices: 7.67 us -> 9.22 us
    ppermute x30, starting transfers between devices: 32 us -> 27.3 us  [swap(): return lax.ppermute(slab, axes, [(i, i ^ mask) for i in range(devices)])]
    ppermute x30, waiting for transfers between devices: 7.06 us -> 8.61 us  [swap(): return lax.ppermute(slab, axes, [(i, i ^ mask) for i in range(devices)])]
where the time goes in v8:
time: 62.6 us; the launch traced here: 62.3 us
  starting transfers between devices  34.9 us (56%)
  Pallas kernels  14.9 us (24%)
  waiting for transfers between devices  9.22 us (15%)
  local copies, waits for them, and re-layouts  2.91 us (5%)
    ppermute x30, starting transfers between devices, swap(): return lax.ppermute(slab, axes, [(i, i ^ mask) for i in range(devices)])  27.3 us
    ppermute x30, waiting for transfers between devices, swap(): return lax.ppermute(slab, axes, [(i, i ^ mask) for i in range(devices)])  8.61 us
    ppermute x4, starting transfers between devices, swap(): return lax.ppermute(edge, axis, pairs + [(b, a) for a, b in pairs])  7.57 us
    pallas_call x1, Pallas kernels, mix(): pl.pallas_call(functools.partial(mix_kernel, rows=rows, cols=cols, masks=...  5.76 us
    pallas_call x1, Pallas kernels, attend(): pl.pallas_call(functools.partial(attend_kernel, slabs=slabs, sets=sets),...  4.56 us
    pallas_call x1, Pallas kernels, expand(): pl.pallas_call(expand_kernel, in_specs=[vmem()] * 2, out_specs=vmem(), ou...  2.15 us
    pallas_call x1, Pallas kernels, finish(): pl.pallas_call(functools.partial(finish_kernel, masks=masks), in_specs=[p...  1.94 us
    unnamed x20, local copies, waits for them, and re-layouts  1.87 us
  transfers between devices with their start and end apart: 34, of which 16 were waited for; matrix products, arithmetic and copies ran while one was open for 0% of the time, Pallas kernels for 4%

profile of v8, /device:TPU:0, one launch (start us, length us, event | category | flops | bytes accessed | tf_op | source)
XLA Modules:
  0.0 62.3 jit_solution(12937651065251059852)
XLA Ops:
  0.0 0.9 %slice_bitcast_fusion.1 = (f32[32,512]{1,0:T(8,128)S(1)}, f32[32,512]{1,0:T(8,128)S(1)}) fusion(f32[16,32,512]{2,1,0:T(8,128)} %param.8), kind=kLoop, calls=%fused_computation.2 | loop fusion | bytes 262144 | tf_op jit(solution)/shard_map/squeeze | solution.py:498
  1.1 0.8 %collective-permute-start = (bf16[32,512]{1,0:T(8,128)(2,1)S(1)}, bf16[32,512]{1,0:T(8,128)(2,1)S(1)}, u32[]{:S(2)}, u32[]{:S(2)}) collective-permute-start(bf16[32,512]{1,0:T(8,128)(2,1)S(1)} %get-tuple-element.55), channel_id=1, source_target_pairs={{4,8},{8,4},{5,9},{9,5},{6,10},{10,6},{7,11},{11,7},{20,24},{24,20... | collective-permute-start | bytes 98312 | tf_op jit(solution)/shard_map/ppermute | solution.py:430
  1.9 5.9 %collective-permute-start.1 = (bf16[32,512]{1,0:T(8,128)(2,1)S(1)}, bf16[32,512]{1,0:T(8,128)(2,1)S(1)}, u32[]{:S(2)}, u32[]{:S(2)}) collective-permute-start(bf16[32,512]{1,0:T(8,128)(2,1)S(1)} %get-tuple-element.56), channel_id=1, source_target_pairs={{0,4},{8,12},{4,0},{12,8},{1,5},{9,13},{5,1},{13,9},{2,6},{10,14},... | collective-permute-start | bytes 98312 | tf_op jit(solution)/shard_map/ppermute | solution.py:430
  8.2 0.8 %copy-done.7 = bf16[512,512]{1,0:T(8,128)(2,1)} copy-done((bf16[512,512]{1,0:T(8,128)(2,1)}, bf16[512,512]{1,0:T(8,128)(2,1)S(1)}, u32[]{:S(2)}) %copy-start.7) | copy-done | bytes 524312
  10.0 0.8 %collective-permute-start.2 = (bf16[32,512]{1,0:T(8,128)(2,1)S(1)}, bf16[32,512]{1,0:T(8,128)(2,1)S(1)}, u32[]{:S(2)}, u32[]{:S(2)}) collective-permute-start(bf16[32,512]{1,0:T(8,128)(2,1)S(1)} %get-tuple-element.52), channel_id=1, source_target_pairs={{1,2},{2,1},{5,6},{6,5},{9,10},{10,9},{13,14},{14,13},{17,18},{18,... | collective-permute-start | bytes 98312 | tf_op jit(solution)/shard_map/ppermute | solution.py:430
  10.8 1.0 %copy-done.8 = bf16[512,512]{1,0:T(8,128)(2,1)S(1)} copy-done((bf16[512,512]{1,0:T(8,128)(2,1)S(1)}, bf16[512,512]{1,0:T(8,128)(2,1)}, u32[]{:S(2)}) %copy-start.8) | copy-done | bytes 524312
  11.8 2.2 %expand.1.expanded_ref = f32[8448,128]{1,0:T(8,128)S(1)} custom-call(bf16[512,512]{1,0:T(8,128)(2,1)S(1)} %copy-done.8, bf16[512,2048]{1,0:T(8,128)(2,1)S(1)} %copy-done), custom_call_target="tpu_custom_call" | custom-call | flops 10000000000 | bytes 6815744 | tf_op jit(solution)/shard_map/expand/pallas_call | solution.py:111
  14.1 5.8 %mix.1 = (f32[512,512]{1,0:T(8,128)S(1)}, bf16[2,32,512]{2,1,0:T(8,128)(2,1)S(1)}, bf16[2,32,512]{2,1,0:T(8,128)(2,1)S(1)}, bf16[2,32,512]{2,1,0:T(8,128)(2,1)S(...) custom-call(s32[1]{0:T(128)} %bitcast.own_ref, ...), custom_call_target="tpu_custom_call" | custom-call | flops 1073741824 | bytes 11010048 | tf_op jit(solution)/shard_map/mix/pallas_call | solution.py:241
  19.9 4.3 %collective-permute-start.4 = (bf16[2,32,512]{2,1,0:T(8,128)(2,1)S(1)}, bf16[2,32,512]{2,1,0:T(8,128)(2,1)S(1)}, u32[]{:S(2)}, u32[]{:S(2)}) collective-permute-start(bf16[2,32,512]{2,1,0:T(8,128)(2,1)S(1)} %get-tuple-element.28), channel_id=1, source_target_pairs={{0,14},{1,15},{2,12},{3,13},{4,10},{5,11},{6,8},{7,9},{8,6},{9,7},... | collective-permute-start | bytes 196616 | tf_op jit(solution)/shard_map/ppermute | solution.py:452
  24.2 2.5 %collective-permute-start.5 = (bf16[2,32,512]{2,1,0:T(8,128)(2,1)S(1)}, bf16[2,32,512]{2,1,0:T(8,128)(2,1)S(1)}, u32[]{:S(2)}, u32[]{:S(2)}) collective-permute-start(bf16[2,32,512]{2,1,0:T(8,128)(2,1)S(1)} %get-tuple-element.29), channel_id=1, source_target_pairs={{0,12},{1,13},{2,14},{3,15},{4,8},{5,9},{6,10},{7,11},{8,4},{9,5},... | collective-permute-start | bytes 196616 | tf_op jit(solution)/shard_map/ppermute | solution.py:452
  26.7 2.8 %collective-permute-start.7 = (bf16[2,32,512]{2,1,0:T(8,128)(2,1)S(1)}, bf16[2,32,512]{2,1,0:T(8,128)(2,1)S(1)}, u32[]{:S(2)}, u32[]{:S(2)}) collective-permute-start(bf16[2,32,512]{2,1,0:T(8,128)(2,1)S(1)} %get-tuple-element.31), channel_id=1, source_target_pairs={{0,10},{1,11},{2,8},{3,9},{4,14},{5,15},{6,12},{7,13},{8,2},{9,3},... | collective-permute-start | bytes 196616 | tf_op jit(solution)/shard_map/ppermute | solution.py:452
  29.7 2.8 %collective-permute-start.9 = (bf16[2,32,512]{2,1,0:T(8,128)(2,1)S(1)}, bf16[2,32,512]{2,1,0:T(8,128)(2,1)S(1)}, u32[]{:S(2)}, u32[]{:S(2)}) collective-permute-start(bf16[2,32,512]{2,1,0:T(8,128)(2,1)S(1)} %get-tuple-element.33), channel_id=1, source_target_pairs={{0,8},{1,9},{2,10},{3,11},{4,12},{5,13},{6,14},{7,15},{8,0},{9,1},... | collective-permute-start | bytes 196616 | tf_op jit(solution)/shard_map/ppermute | solution.py:452
  32.6 2.2 %collective-permute-done.7.refs_3_ = bf16[2,32,512]{2,1,0:T(8,128)(2,1)S(1)} collective-permute-done((bf16[2,32,512]{2,1,0:T(8,128)(2,1)S(1)}, bf16[2,32,512]{2,1,0:T(8,128)(2,1)S(1)}, u32[]{:S(2)}, u32[]{:S(2)}) %collective-permute-start.7) | collective-permute-done | bytes 65568 | tf_op jit(solution)/shard_map/ppermute | solution.py:452
  34.8 0.8 %collective-permute-start.11 = (bf16[2,32,512]{2,1,0:T(8,128)(2,1)S(1)}, bf16[2,32,512]{2,1,0:T(8,128)(2,1)S(1)}, u32[]{:S(2)}, u32[]{:S(2)}) collective-permute-start(bf16[2,32,512]{2,1,0:T(8,128)(2,1)S(1)} %collective-permute-done.4.refs_0_), channel_id=1, source_target_pairs={{0,1},{1,0},{2,3},{3,2},{4,5},{5,4},{6,7},{7,6},{8,9},{9,8},{10,11... | collective-permute-start | bytes 196616 | tf_op jit(solution)/shard_map/ppermute | solution.py:452
  35.6 1.3 %collective-permute-done.9.refs_5_ = bf16[2,32,512]{2,1,0:T(8,128)(2,1)S(1)} collective-permute-done((bf16[2,32,512]{2,1,0:T(8,128)(2,1)S(1)}, bf16[2,32,512]{2,1,0:T(8,128)(2,1)S(1)}, u32[]{:S(2)}, u32[]{:S(2)}) %collective-permute-start.9) | collective-permute-done | bytes 65568 | tf_op jit(solution)/shard_map/ppermute | solution.py:452
  39.2 4.6 %attend.1 = (bf16[2,32,512]{2,1,0:T(8,128)(2,1)S(1)}, bf16[2,32,512]{2,1,0:T(8,128)(2,1)S(1)}, bf16[2,32,512]{2,1,0:T(8,128)(2,1)S(1)}, bf16[2,32,512]{2,1,0:T(8...) custom-call(bf16[2,32,512]{2,1,0:T(8,128)(2,1)S(1)} %collective-perm, ...), custom_call_target="tpu_custom_call" | custom-call | flops 1073741824 | bytes 2621440 | tf_op jit(solution)/shard_map/attend/pallas_call | solution.py:358
  43.8 2.4 %collective-permute-start.19 = (bf16[2,32,512]{2,1,0:T(8,128)(2,1)S(1)}, bf16[2,32,512]{2,1,0:T(8,128)(2,1)S(1)}, u32[]{:S(2)}, u32[]{:S(2)}) collective-permute-start(bf16[2,32,512]{2,1,0:T(8,128)(2,1)S(1)} %get-tuple-element.36), channel_id=1, source_target_pairs={{0,14},{1,15},{2,12},{3,13},{4,10},{5,11},{6,8},{7,9},{8,6},{9,7},... | collective-permute-start | bytes 196616 | tf_op jit(solution)/shard_map/ppermute | solution.py:452
  46.2 2.1 %collective-permute-start.20 = (bf16[2,32,512]{2,1,0:T(8,128)(2,1)S(1)}, bf16[2,32,512]{2,1,0:T(8,128)(2,1)S(1)}, u32[]{:S(2)}, u32[]{:S(2)}) collective-permute-start(bf16[2,32,512]{2,1,0:T(8,128)(2,1)S(1)} %get-tuple-element.37), channel_id=1, source_target_pairs={{0,12},{1,13},{2,14},{3,15},{4,8},{5,9},{6,10},{7,11},{8,4},{9,5},... | collective-permute-start | bytes 196616 | tf_op jit(solution)/shard_map/ppermute | solution.py:452
  48.3 3.2 %collective-permute-start.22 = (bf16[2,32,512]{2,1,0:T(8,128)(2,1)S(1)}, bf16[2,32,512]{2,1,0:T(8,128)(2,1)S(1)}, u32[]{:S(2)}, u32[]{:S(2)}) collective-permute-start(bf16[2,32,512]{2,1,0:T(8,128)(2,1)S(1)} %get-tuple-element.39), channel_id=1, source_target_pairs={{0,10},{1,11},{2,8},{3,9},{4,14},{5,15},{6,12},{7,13},{8,2},{9,3},... | collective-permute-start | bytes 196616 | tf_op jit(solution)/shard_map/ppermute | solution.py:452
  51.5 2.6 %collective-permute-start.24 = (bf16[2,32,512]{2,1,0:T(8,128)(2,1)S(1)}, bf16[2,32,512]{2,1,0:T(8,128)(2,1)S(1)}, u32[]{:S(2)}, u32[]{:S(2)}) collective-permute-start(bf16[2,32,512]{2,1,0:T(8,128)(2,1)S(1)} %get-tuple-element.41), channel_id=1, source_target_pairs={{0,8},{1,9},{2,10},{3,11},{4,12},{5,13},{6,14},{7,15},{8,0},{9,1},... | collective-permute-start | bytes 196616 | tf_op jit(solution)/shard_map/ppermute | solution.py:452
  54.2 0.8 %collective-permute-start.25 = (bf16[2,32,512]{2,1,0:T(8,128)(2,1)S(1)}, bf16[2,32,512]{2,1,0:T(8,128)(2,1)S(1)}, u32[]{:S(2)}, u32[]{:S(2)}) collective-permute-start(bf16[2,32,512]{2,1,0:T(8,128)(2,1)S(1)} %get-tuple-element.42), channel_id=1, source_target_pairs={{0,2},{1,3},{2,0},{3,1},{4,6},{5,7},{6,4},{7,5},{8,10},{9,11},{10,... | collective-permute-start | bytes 196616 | tf_op jit(solution)/shard_map/ppermute | solution.py:452
  55.0 1.2 %collective-permute-done.21.refs_2_ = bf16[2,32,512]{2,1,0:T(8,128)(2,1)S(1)} collective-permute-done((bf16[2,32,512]{2,1,0:T(8,128)(2,1)S(1)}, bf16[2,32,512]{2,1,0:T(8,128)(2,1)S(1)}, u32[]{:S(2)}, u32[]{:S(2)}) %collective-permute-start.21) | collective-permute-done | bytes 65568 | tf_op jit(solution)/shard_map/ppermute | solution.py:452
  56.9 0.7 %collective-permute-done.23.refs_4_ = bf16[2,32,512]{2,1,0:T(8,128)(2,1)S(1)} collective-permute-done((bf16[2,32,512]{2,1,0:T(8,128)(2,1)S(1)}, bf16[2,32,512]{2,1,0:T(8,128)(2,1)S(1)}, u32[]{:S(2)}, u32[]{:S(2)}) %collective-permute-start.23) | collective-permute-done | bytes 65568 | tf_op jit(solution)/shard_map/ppermute | solution.py:452
  60.4 1.9 %finish.1 = f32[512,512]{1,0:T(8,128)} custom-call(s32[1]{0:T(128)} %bitcast.own_ref, bf16[2,32,512]{2,1,0:T(8,128)(2,1)S(1)} %collective-permute-done.19.refs_0_, bf16[2,32,512]{2,1,0:T(8,128)(2,1)S(1)} %collective-permute-done.20.refs_1_, bf16[2,32,512]{2,1,0:T(8,128)(2,1)S(1)} %collective-permute-done.21.refs_2_, ...), custom_call_target="tpu_custom_call" | custom-call | tf_op jit(solution)/shard_map/finish/pallas_call | solution.py:409
  (82 shorter events, 7.6 us)
Async XLA Ops:
  1.1 8.0 %collective-permute-start = (bf16[32,512]{1,0:T(8,128)(2,1)S(1)}, bf16[32,512]{1,0:T(8,128)(2,1)S(1)}, u32[]{:S(2)}, u32[]{:S(2)}) collective-permute-start(bf16[32,512]{1,0:T(8,128)(2,1)S(1)} %get-tuple-element.55), channel_id=1, source_target_pairs={{4,8},{8,4},{5,9},{9,5},{6,10},{10,6},{7,11},{11,7},{20,24},{24,20... | collective-permute-start | bytes 98312 | tf_op jit(solution)/shard_map/ppermute | solution.py:430
  1.9 7.8 %collective-permute-start.1 = (bf16[32,512]{1,0:T(8,128)(2,1)S(1)}, bf16[32,512]{1,0:T(8,128)(2,1)S(1)}, u32[]{:S(2)}, u32[]{:S(2)}) collective-permute-start(bf16[32,512]{1,0:T(8,128)(2,1)S(1)} %get-tuple-element.56), channel_id=1, source_target_pairs={{0,4},{8,12},{4,0},{12,8},{1,5},{9,13},{5,1},{13,9},{2,6},{10,14},... | collective-permute-start | bytes 98312 | tf_op jit(solution)/shard_map/ppermute | solution.py:430
  9.9 4.1 %collective-permute-start.3 = (bf16[32,512]{1,0:T(8,128)(2,1)S(1)}, bf16[32,512]{1,0:T(8,128)(2,1)S(1)}, u32[]{:S(2)}, u32[]{:S(2)}) collective-permute-start(bf16[32,512]{1,0:T(8,128)(2,1)S(1)} %get-tuple-element.51), channel_id=1, source_target_pairs={{0,1},{2,3},{1,0},{3,2},{4,5},{6,7},{5,4},{7,6},{8,9},{10,11},{9,8... | collective-permute-start | bytes 98312 | tf_op jit(solution)/shard_map/ppermute | solution.py:430
  10.0 4.0 %collective-permute-start.2 = (bf16[32,512]{1,0:T(8,128)(2,1)S(1)}, bf16[32,512]{1,0:T(8,128)(2,1)S(1)}, u32[]{:S(2)}, u32[]{:S(2)}) collective-permute-start(bf16[32,512]{1,0:T(8,128)(2,1)S(1)} %get-tuple-element.52), channel_id=1, source_target_pairs={{1,2},{2,1},{5,6},{6,5},{9,10},{10,9},{13,14},{14,13},{17,18},{18,... | collective-permute-start | bytes 98312 | tf_op jit(solution)/shard_map/ppermute | solution.py:430
  19.9 9.8 %collective-permute-start.4 = (bf16[2,32,512]{2,1,0:T(8,128)(2,1)S(1)}, bf16[2,32,512]{2,1,0:T(8,128)(2,1)S(1)}, u32[]{:S(2)}, u32[]{:S(2)}) collective-permute-start(bf16[2,32,512]{2,1,0:T(8,128)(2,1)S(1)} %get-tuple-element.28), channel_id=1, source_target_pairs={{0,14},{1,15},{2,12},{3,13},{4,10},{5,11},{6,8},{7,9},{8,6},{9,7},... | collective-permute-start | bytes 196616 | tf_op jit(solution)/shard_map/ppermute | solution.py:452
  24.2 8.3 %collective-permute-start.5 = (bf16[2,32,512]{2,1,0:T(8,128)(2,1)S(1)}, bf16[2,32,512]{2,1,0:T(8,128)(2,1)S(1)}, u32[]{:S(2)}, u32[]{:S(2)}) collective-permute-start(bf16[2,32,512]{2,1,0:T(8,128)(2,1)S(1)} %get-tuple-element.29), channel_id=1, source_target_pairs={{0,12},{1,13},{2,14},{3,15},{4,8},{5,9},{6,10},{7,11},{8,4},{9,5},... | collective-permute-start | bytes 196616 | tf_op jit(solution)/shard_map/ppermute | solution.py:452
  26.7 5.9 %collective-permute-start.6 = (bf16[2,32,512]{2,1,0:T(8,128)(2,1)S(1)}, bf16[2,32,512]{2,1,0:T(8,128)(2,1)S(1)}, u32[]{:S(2)}, u32[]{:S(2)}) collective-permute-start(bf16[2,32,512]{2,1,0:T(8,128)(2,1)S(1)} %get-tuple-element.30), channel_id=1, source_target_pairs={{0,6},{1,7},{2,4},{3,5},{4,2},{5,3},{6,0},{7,1},{8,14},{9,15},{10,... | collective-permute-start | bytes 196616 | tf_op jit(solution)/shard_map/ppermute | solution.py:452
  26.7 8.2 %collective-permute-start.7 = (bf16[2,32,512]{2,1,0:T(8,128)(2,1)S(1)}, bf16[2,32,512]{2,1,0:T(8,128)(2,1)S(1)}, u32[]{:S(2)}, u32[]{:S(2)}) collective-permute-start(bf16[2,32,512]{2,1,0:T(8,128)(2,1)S(1)} %get-tuple-element.31), channel_id=1, source_target_pairs={{0,10},{1,11},{2,8},{3,9},{4,14},{5,15},{6,12},{7,13},{8,2},{9,3},... | collective-permute-start | bytes 196616 | tf_op jit(solution)/shard_map/ppermute | solution.py:452
  29.5 6.1 %collective-permute-start.8 = (bf16[2,32,512]{2,1,0:T(8,128)(2,1)S(1)}, bf16[2,32,512]{2,1,0:T(8,128)(2,1)S(1)}, u32[]{:S(2)}, u32[]{:S(2)}) collective-permute-start(bf16[2,32,512]{2,1,0:T(8,128)(2,1)S(1)} %get-tuple-element.32), channel_id=1, source_target_pairs={{0,4},{1,5},{2,6},{3,7},{4,0},{5,1},{6,2},{7,3},{8,12},{9,13},{10,... | collective-permute-start | bytes 196616 | tf_op jit(solution)/shard_map/ppermute | solution.py:452
  29.7 7.3 %collective-permute-start.9 = (bf16[2,32,512]{2,1,0:T(8,128)(2,1)S(1)}, bf16[2,32,512]{2,1,0:T(8,128)(2,1)S(1)}, u32[]{:S(2)}, u32[]{:S(2)}) collective-permute-start(bf16[2,32,512]{2,1,0:T(8,128)(2,1)S(1)} %get-tuple-element.33), channel_id=1, source_target_pairs={{0,8},{1,9},{2,10},{3,11},{4,12},{5,13},{6,14},{7,15},{8,0},{9,1},... | collective-permute-start | bytes 196616 | tf_op jit(solution)/shard_map/ppermute | solution.py:452
  32.5 4.4 %collective-permute-start.10 = (bf16[2,32,512]{2,1,0:T(8,128)(2,1)S(1)}, bf16[2,32,512]{2,1,0:T(8,128)(2,1)S(1)}, u32[]{:S(2)}, u32[]{:S(2)}) collective-permute-start(bf16[2,32,512]{2,1,0:T(8,128)(2,1)S(1)} %get-tuple-element.34), channel_id=1, source_target_pairs={{0,2},{1,3},{2,0},{3,1},{4,6},{5,7},{6,4},{7,5},{8,10},{9,11},{10,... | collective-permute-start | bytes 196616 | tf_op jit(solution)/shard_map/ppermute | solution.py:452
  32.6 4.9 %collective-permute-start.18 = (bf16[2,32,512]{2,1,0:T(8,128)(2,1)S(1)}, bf16[2,32,512]{2,1,0:T(8,128)(2,1)S(1)}, u32[]{:S(2)}, u32[]{:S(2)}) collective-permute-start(bf16[2,32,512]{2,1,0:T(8,128)(2,1)S(1)} %get-tuple-element.35.refs_7_), channel_id=1, source_target_pairs={{0,1},{1,0},{2,3},{3,2},{4,5},{5,4},{6,7},{7,6},{8,9},{9,8},{10,11... | collective-permute-start | bytes 196616 | tf_op jit(solution)/shard_map/ppermute | solution.py:452
  34.8 2.7 %collective-permute-start.11 = (bf16[2,32,512]{2,1,0:T(8,128)(2,1)S(1)}, bf16[2,32,512]{2,1,0:T(8,128)(2,1)S(1)}, u32[]{:S(2)}, u32[]{:S(2)}) collective-permute-start(bf16[2,32,512]{2,1,0:T(8,128)(2,1)S(1)} %collective-permute-done.4.refs_0_), channel_id=1, source_target_pairs={{0,1},{1,0},{2,3},{3,2},{4,5},{5,4},{6,7},{7,6},{8,9},{9,8},{10,11... | collective-permute-start | bytes 196616 | tf_op jit(solution)/shard_map/ppermute | solution.py:452
  35.6 2.4 %collective-permute-start.12 = (bf16[2,32,512]{2,1,0:T(8,128)(2,1)S(1)}, bf16[2,32,512]{2,1,0:T(8,128)(2,1)S(1)}, u32[]{:S(2)}, u32[]{:S(2)}) collective-permute-start(bf16[2,32,512]{2,1,0:T(8,128)(2,1)S(1)} %collective-permute-done.5.refs_1_), channel_id=1, source_target_pairs={{0,1},{1,0},{2,3},{3,2},{4,5},{5,4},{6,7},{7,6},{8,9},{9,8},{10,11... | collective-permute-start | bytes 196616 | tf_op jit(solution)/shard_map/ppermute | solution.py:452
  43.8 7.7 %collective-permute-start.19 = (bf16[2,32,512]{2,1,0:T(8,128)(2,1)S(1)}, bf16[2,32,512]{2,1,0:T(8,128)(2,1)S(1)}, u32[]{:S(2)}, u32[]{:S(2)}) collective-permute-start(bf16[2,32,512]{2,1,0:T(8,128)(2,1)S(1)} %get-tuple-element.36), channel_id=1, source_target_pairs={{0,14},{1,15},{2,12},{3,13},{4,10},{5,11},{6,8},{7,9},{8,6},{9,7},... | collective-permute-start | bytes 196616 | tf_op jit(solution)/shard_map/ppermute | solution.py:452
  46.2 7.9 %collective-permute-start.20 = (bf16[2,32,512]{2,1,0:T(8,128)(2,1)S(1)}, bf16[2,32,512]{2,1,0:T(8,128)(2,1)S(1)}, u32[]{:S(2)}, u32[]{:S(2)}) collective-permute-start(bf16[2,32,512]{2,1,0:T(8,128)(2,1)S(1)} %get-tuple-element.37), channel_id=1, source_target_pairs={{0,12},{1,13},{2,14},{3,15},{4,8},{5,9},{6,10},{7,11},{8,4},{9,5},... | collective-permute-start | bytes 196616 | tf_op jit(solution)/shard_map/ppermute | solution.py:452
  48.3 7.9 %collective-permute-start.21 = (bf16[2,32,512]{2,1,0:T(8,128)(2,1)S(1)}, bf16[2,32,512]{2,1,0:T(8,128)(2,1)S(1)}, u32[]{:S(2)}, u32[]{:S(2)}) collective-permute-start(bf16[2,32,512]{2,1,0:T(8,128)(2,1)S(1)} %get-tuple-element.38), channel_id=1, source_target_pairs={{0,6},{1,7},{2,4},{3,5},{4,2},{5,3},{6,0},{7,1},{8,14},{9,15},{10,... | collective-permute-start | bytes 196616 | tf_op jit(solution)/shard_map/ppermute | solution.py:452
  48.3 8.6 %collective-permute-start.22 = (bf16[2,32,512]{2,1,0:T(8,128)(2,1)S(1)}, bf16[2,32,512]{2,1,0:T(8,128)(2,1)S(1)}, u32[]{:S(2)}, u32[]{:S(2)}) collective-permute-start(bf16[2,32,512]{2,1,0:T(8,128)(2,1)S(1)} %get-tuple-element.39), channel_id=1, source_target_pairs={{0,10},{1,11},{2,8},{3,9},{4,14},{5,15},{6,12},{7,13},{8,2},{9,3},... | collective-permute-start | bytes 196616 | tf_op jit(solution)/shard_map/ppermute | solution.py:452
  51.5 6.1 %collective-permute-start.23 = (bf16[2,32,512]{2,1,0:T(8,128)(2,1)S(1)}, bf16[2,32,512]{2,1,0:T(8,128)(2,1)S(1)}, u32[]{:S(2)}, u32[]{:S(2)}) collective-permute-start(bf16[2,32,512]{2,1,0:T(8,128)(2,1)S(1)} %get-tuple-element.40), channel_id=1, source_target_pairs={{0,4},{1,5},{2,6},{3,7},{4,0},{5,1},{6,2},{7,3},{8,12},{9,13},{10,... | collective-permute-start | bytes 196616 | tf_op jit(solution)/shard_map/ppermute | solution.py:452
  51.5 6.1 %collective-permute-start.24 = (bf16[2,32,512]{2,1,0:T(8,128)(2,1)S(1)}, bf16[2,32,512]{2,1,0:T(8,128)(2,1)S(1)}, u32[]{:S(2)}, u32[]{:S(2)}) collective-permute-start(bf16[2,32,512]{2,1,0:T(8,128)(2,1)S(1)} %get-tuple-element.41), channel_id=1, source_target_pairs={{0,8},{1,9},{2,10},{3,11},{4,12},{5,13},{6,14},{7,15},{8,0},{9,1},... | collective-permute-start | bytes 196616 | tf_op jit(solution)/shard_map/ppermute | solution.py:452
  54.2 4.3 %collective-permute-start.25 = (bf16[2,32,512]{2,1,0:T(8,128)(2,1)S(1)}, bf16[2,32,512]{2,1,0:T(8,128)(2,1)S(1)}, u32[]{:S(2)}, u32[]{:S(2)}) collective-permute-start(bf16[2,32,512]{2,1,0:T(8,128)(2,1)S(1)} %get-tuple-element.42), channel_id=1, source_target_pairs={{0,2},{1,3},{2,0},{3,1},{4,6},{5,7},{6,4},{7,5},{8,10},{9,11},{10,... | collective-permute-start | bytes 196616 | tf_op jit(solution)/shard_map/ppermute | solution.py:452
  56.2 2.2 %collective-permute-start.33 = (bf16[2,32,512]{2,1,0:T(8,128)(2,1)S(1)}, bf16[2,32,512]{2,1,0:T(8,128)(2,1)S(1)}, u32[]{:S(2)}, u32[]{:S(2)}) collective-permute-start(bf16[2,32,512]{2,1,0:T(8,128)(2,1)S(1)} %get-tuple-element.43.refs_7_), channel_id=1, source_target_pairs={{0,1},{1,0},{2,3},{3,2},{4,5},{5,4},{6,7},{7,6},{8,9},{9,8},{10,11... | collective-permute-start | bytes 196616 | tf_op jit(solution)/shard_map/ppermute | solution.py:452
  56.9 2.1 %collective-permute-start.26 = (bf16[2,32,512]{2,1,0:T(8,128)(2,1)S(1)}, bf16[2,32,512]{2,1,0:T(8,128)(2,1)S(1)}, u32[]{:S(2)}, u32[]{:S(2)}) collective-permute-start(bf16[2,32,512]{2,1,0:T(8,128)(2,1)S(1)} %collective-permute-done.19.refs_0_), channel_id=1, source_target_pairs={{0,1},{1,0},{2,3},{3,2},{4,5},{5,4},{6,7},{7,6},{8,9},{9,8},{10,11... | collective-permute-start | bytes 196616 | tf_op jit(solution)/shard_map/ppermute | solution.py:452
  57.6 1.9 %collective-permute-start.28 = (bf16[2,32,512]{2,1,0:T(8,128)(2,1)S(1)}, bf16[2,32,512]{2,1,0:T(8,128)(2,1)S(1)}, u32[]{:S(2)}, u32[]{:S(2)}) collective-permute-start(bf16[2,32,512]{2,1,0:T(8,128)(2,1)S(1)} %collective-permute-done.21.refs_2_), channel_id=1, source_target_pairs={{0,1},{1,0},{2,3},{3,2},{4,5},{5,4},{6,7},{7,6},{8,9},{9,8},{10,11... | collective-permute-start | bytes 196616 | tf_op jit(solution)/shard_map/ppermute | solution.py:452
  (20 other events, 143.5 us)

commit v9 on v8

--- a/solution.py
+++ b/solution.py
@@ -125,12 +125,12 @@
 
 def mix_kernel(
     own_ref, expanded_ref, field_ref, up_ref, down_ref, left_ref, right_ref, w_expand_ref, depth_ref,
-    w_project_ref, perm_ref, mixed_ref, *refs, rows, cols, masks,
+    w_project_ref, perm_ref, mixed_ref, *refs, rows, cols, plan, size,
 ):
-    slab_refs = refs[: len(masks)]
-    total_ref, normed_ref, grouped_ref, even_ref, odd_ref, even_halo_ref, odd_halo_ref = refs[
-        len(masks) :
-    ]
+    masks, _, sides = plan
+    sent = len(outgoing_shapes(plan, size, 1))
+    slab_refs = refs[:sent]
+    total_ref, normed_ref, grouped_ref, even_ref, odd_ref, even_halo_ref, odd_halo_ref = refs[sent:]
     tokens = rows * cols
     width = w_expand_ref.shape[1]
     tile = even_ref.shape[1]
@@ -222,28 +222,30 @@
         mixed_ref[piece, :] = mixed
         normed_ref[piece, :] = layer_norm(mixed).astype(jnp.bfloat16)
     grouped_ref[...] = matmul(perm_ref[...], normed_ref[...]).astype(jnp.bfloat16)
-    size = slab_refs[0].shape[1]
-    for mask, slab_ref in zip(masks, slab_refs):
-        for side in range(slab_ref.shape[0]):
+    for index, mask in enumerate(masks):
+        for side in range(sides):
             start = pl.multiple_of((own_ref[0] ^ (mask | side)) * size, 16)
-            slab_ref[side] = grouped_ref[pl.ds(start, size), :]
+            write_block(
+                plan, slab_refs, index, side, slice(None), grouped_ref[pl.ds(start, size), :]
+            )
 
 
 def mix(
-    own, masks, slab, expanded, field, up, down, left, right, w_expand, depth_kernel, w_project, perm,
+    own, plan, size, expanded, field, up, down, left, right, w_expand, depth_kernel, w_project, perm,
     rows, cols,
 ):
     tokens, channels = field.shape
     width = w_expand.shape[1]
     tile = divisor(width // 2, 256, LANES)
     slot = left.shape[0]
+    sent = outgoing_shapes(plan, size, channels)
     halo = pltpu.VMEM((tile // LANES, 24 + 2 * cols + 2 * slot, LANES), jnp.float32)
     return pl.pallas_call(
-        functools.partial(mix_kernel, rows=rows, cols=cols, masks=masks),
+        functools.partial(mix_kernel, rows=rows, cols=cols, plan=plan, size=size),
         in_specs=[pl.BlockSpec(memory_space=pltpu.SMEM)] + [vmem()] * 10,
-        out_specs=[vmem()] * (1 + len(masks)),
+        out_specs=[vmem()] * (1 + len(sent)),
         out_shape=[jax.ShapeDtypeStruct((tokens, channels), jnp.float32)]
-        + [jax.ShapeDtypeStruct(slab, jnp.bfloat16)] * len(masks),
+        + [jax.ShapeDtypeStruct(shape, jnp.bfloat16) for shape in sent],
         scratch_shapes=[
             pltpu.VMEM((tokens, channels), jnp.float32),
             pltpu.VMEM((tokens, channels), jnp.bfloat16),
@@ -269,11 +271,12 @@
     return jnp.where(row == column, 1.0, 0.0).astype(jnp.bfloat16)
 
 
-def attend_kernel(*refs, slabs, sets):
-    mine, others, weight_ref = refs[:slabs], refs[slabs : 2 * slabs], refs[2 * slabs]
-    out_refs = refs[2 * slabs + 1 : 3 * slabs + 1]
-    query_ref, key_ref, value_ref, turned_ref, even_ref, odd_ref = refs[3 * slabs + 1 :]
-    sides, size, channels = mine[0].shape
+def attend_kernel(*refs, plan, sets, came):
+    masks, _, sides = plan
+    slabs = len(masks)
+    _, size, channels = refs[0].shape
+    in_refs, weight_ref, out_refs = refs[:came], refs[came], refs[came + 1 : -6]
+    query_ref, key_ref, value_ref, turned_ref, even_ref, odd_ref = refs[-6:]
     members = size // sets
     count = slabs * sides * members
     head_width = channels // HEADS
@@ -292,7 +295,7 @@
         piece = slice(s * members, (s + 1) * members)
         block = jnp.concatenate(
             [
-                (mine, others)[side][index][side, piece]
+                read_block(plan, in_refs, index, side, piece)
                 for index in range(slabs)
                 for side in range(sides)
             ],
@@ -343,23 +346,25 @@
         for index in range(slabs):
             for side in range(sides):
                 start = (index * sides + side) * members
-                out_refs[index][side, s * members : (s + 1) * members] = attended[
-                    start : start + members
-                ]
-
-
-def attend(mine, others, w_qkv, sets):
-    slabs = len(mine)
-    sides, size, channels = mine[0].shape
-    count = slabs * sides * size // sets
+                write_block(
+                    plan, out_refs, index, side, slice(s * members, (s + 1) * members),
+                    attended[start : start + members],
+                )
+
+
+def attend(plan, incoming, w_qkv, sets):
+    masks, _, sides = plan
+    _, size, channels = incoming[0].shape
+    count = len(masks) * sides * size // sets
+    sent = outgoing_shapes(plan, size, channels)
     head_width = channels // HEADS
     group_heads = LANES // head_width
     total = sets * channels // LANES
     return pl.pallas_call(
-        functools.partial(attend_kernel, slabs=slabs, sets=sets),
-        in_specs=[vmem()] * (2 * slabs + 1),
-        out_specs=[vmem()] * slabs,
-        out_shape=[jax.ShapeDtypeStruct(mine[0].shape, jnp.bfloat16)] * slabs,
+        functools.partial(attend_kernel, plan=plan, sets=sets, came=len(incoming)),
+        in_specs=[vmem()] * (len(incoming) + 1),
+        out_specs=[vmem()] * len(sent),
+        out_shape=[jax.ShapeDtypeStruct(shape, jnp.bfloat16) for shape in sent],
         scratch_shapes=[
             pltpu.VMEM((total, count, LANES), jnp.bfloat16),
             pltpu.VMEM((total, count, LANES), jnp.bfloat16),
@@ -375,19 +380,21 @@
             transcendentals=sets * HEADS * count * count,
         ),
         name="attend",
-    )(*mine, *others, w_qkv)
-
-
-def finish_kernel(own_ref, *refs, masks):
-    slabs = len(masks)
-    mine, others = refs[:slabs], refs[slabs : 2 * slabs]
-    back_ref, weight_ref, mixed_ref, out_ref, attended_ref, made_ref, sent = refs[2 * slabs :]
+    )(*incoming, w_qkv)
+
+
+def finish_kernel(own_ref, *refs, plan):
+    masks, _, sides = plan
+    in_refs, rest = refs[:-7], refs[-7:]
+    back_ref, weight_ref, mixed_ref, out_ref, attended_ref, made_ref, sent = rest
     tokens = mixed_ref.shape[0]
-    sides, size, _ = mine[0].shape
+    size = in_refs[0].shape[1]
     for index, mask in enumerate(masks):
         for side in range(sides):
             start = pl.multiple_of((own_ref[0] ^ (mask | side)) * size, 16)
-            attended_ref[pl.ds(start, size), :] = (mine, others)[side][index][side]
+            attended_ref[pl.ds(start, size), :] = read_block(
+                plan, in_refs, index, side, slice(None)
+            )
     step = made_ref.shape[1]
     copies = []
     for index, start in enumerate(range(0, tokens, step)):
@@ -403,12 +410,12 @@
         copy.wait()
 
 
-def finish(own, masks, mine, others, back, w_out, mixed):
+def finish(own, plan, incoming, back, w_out, mixed):
     tokens, channels = mixed.shape
     step = divisor(tokens, 128, 16)
     return pl.pallas_call(
-        functools.partial(finish_kernel, masks=masks),
-        in_specs=[pl.BlockSpec(memory_space=pltpu.SMEM)] + [vmem()] * (2 * len(masks) + 3),
+        functools.partial(finish_kernel, plan=plan),
+        in_specs=[pl.BlockSpec(memory_space=pltpu.SMEM)] + [vmem()] * (len(incoming) + 3),
         out_specs=pl.BlockSpec(memory_space=pltpu.HBM),
         out_shape=jax.ShapeDtypeStruct((tokens, channels), jnp.float32),
         scratch_shapes=[
@@ -418,7 +425,7 @@
         ],
         compiler_params=pltpu.CompilerParams(vmem_limit_bytes=16 * MIB),
         name="finish",
-    )(own, *mine, *others, back, w_out, mixed)
+    )(own, *incoming, back, w_out, mixed)
 
 
 def exchange(low_edge, high_edge, axis):
@@ -441,18 +448,76 @@
     masks = crossing[:1]
     for index, mask in enumerate(crossing[1:]):
         masks += [mask] + others[index : index + 1]
-    return masks + [0], 2
-
-
-def trade(masks, slabs):
-    axes = ("row", "col")
+    return masks + [0], min(2, len(masks)), 2
+
+
+def outgoing_shapes(plan, size, channels):
+    masks, late, sides = plan
+    if sides == 1:
+        return [(1, size, channels)]
+    early = len(masks) - 1 - late
+    return [(2, size, channels)] * late + [
+        (1, size, channels), (early + 1, size, channels), (early, size, channels)
+    ]
+
+
+def write_block(plan, refs, index, side, rows, value):
+    masks, late, sides = plan
+    if sides == 1:
+        refs[0][0, rows] = value
+    elif index < late:
+        refs[index][side, rows] = value
+    elif index == len(masks) - 1:
+        refs[late + side][0, rows] = value
+    elif side == 0:
+        refs[late + 2][index - late, rows] = value
+    else:
+        refs[late + 1][index - late + 1, rows] = value
+
+
+def read_block(plan, refs, index, side, rows):
+    masks, late, sides = plan
+    if sides == 1:
+        return refs[0][0, rows]
+    if index < late:
+        return refs[index + side * len(masks)][side, rows]
+    if index == len(masks) - 1:
+        return refs[index + side * (late + 1)][0, rows]
+    return refs[index][side, rows]
+
+
+def join_kernel(own_ref, swapped_ref, *out_refs):
+    for index, out_ref in enumerate(out_refs):
+        out_ref[0] = own_ref[index]
+        out_ref[1] = swapped_ref[index + 1]
+
+
+def join(own, swapped):
+    early, size, channels = own.shape
+    return pl.pallas_call(
+        join_kernel,
+        in_specs=[vmem()] * 2,
+        out_specs=[vmem()] * early,
+        out_shape=[jax.ShapeDtypeStruct((2, size, channels), own.dtype)] * early,
+        compiler_params=pltpu.CompilerParams(vmem_limit_bytes=8 * MIB),
+        name="join",
+    )(own, swapped)
+
+
+def trade(plan, outgoing):
+    masks, late, _ = plan
     devices = lax.axis_size("row") * lax.axis_size("col")
 
     def swap(slab, mask):
-        return lax.ppermute(slab, axes, [(i, i ^ mask) for i in range(devices)])
-
-    mine = [swap(slab, mask) if mask else slab for mask, slab in zip(masks, slabs)]
-    return mine, [swap(slab, 1) for slab in mine]
+        return lax.ppermute(slab, ("row", "col"), [(i, i ^ mask) for i in range(devices)])
+
+    slabs, (kept, passed, own) = outgoing[:late], outgoing[late:]
+    swapped = swap(passed, 1)
+    first = [swap(slab, mask) for slab, mask in zip(slabs, masks)]
+    rest = [swap(slab, mask) for slab, mask in zip(join(own, swapped), masks[late:-1])]
+    tie = min(1, len(rest) - 1)
+    *first, rest[tie] = lax.optimization_barrier((*first, rest[tie]))
+    return [*first, *rest, kept, *[swap(slab, 1) for slab in first], swapped]
 
 
 def trade_all(slabs, sets, members, outward):
@@ -466,8 +531,7 @@
     block = lax.all_to_all(block, axes, 0, 0, tiled=True)
     if outward:
         block = block.reshape(devices, sets, members, channels).transpose(1, 0, 2, 3)
-    block = [block.reshape(1, -1, channels)]
-    return block, block
+    return [block.reshape(1, -1, channels)]
 
 
 def grouping(rows, cols, blocks_rows, blocks_cols):
@@ -505,28 +569,26 @@
     normed, first, last = lax.optimization_barrier((normed, first, last))
     expanded = expand(normed, w_expand)
     left, right = exchange(first, last, "col")
-    pairwise = devices <= 16 and devices & (devices - 1) == 0 and col_devices % 2 == 0
+    pairwise = 8 <= devices <= 16 and devices & (devices - 1) == 0 and col_devices % 2 == 0
     if pairwise:
-        masks, sides = exchange_plan(row_devices, col_devices)
+        plan = exchange_plan(row_devices, col_devices)
         own = lax.axis_index(("row", "col")).reshape(1)
     else:
-        masks, sides = [0], 1
+        plan = [0], 0, 1
         own = jnp.zeros(1, jnp.int32)
-    slab = (sides, tokens // (sides * len(masks)), channels)
-    mixed, *slabs = mix(
-        own, masks, slab, expanded, flat, up, down, left, right, w_expand, depth_kernel, w_project,
+    size = tokens // (len(plan[0]) * plan[2])
+    mixed, *outgoing = mix(
+        own, plan, size, expanded, flat, up, down, left, right, w_expand, depth_kernel, w_project,
         perm, rows, cols,
     )
 
-    def route(slabs, outward):
+    def route(outgoing, outward):
         if pairwise:
-            return trade(masks, slabs)
-        return trade_all(slabs, sets_local, members, outward)
-
-    mine, others = route(slabs, True)
-    slabs = attend(mine, others, w_qkv, sets_local)
-    mine, others = route(slabs, False)
-    final = finish(own, masks, mine, others, back, w_out, mixed)
+            return trade(plan, outgoing)
+        return trade_all(outgoing, sets_local, members, outward)
+
+    outgoing = attend(plan, route(outgoing, True), w_qkv, sets_local)
+    final = finish(own, plan, route(outgoing, False), back, w_out, mixed)
     return final.reshape(rows, cols, channels)
 
 

time: 62.6 us -> 61.4 us (0.981)
  waiting for transfers between devices: 9.22 us -> 7.59 us
    ppermute x30 -> x20, waiting for transfers between devices: 8.61 us -> 6.98 us  [swap(): lax.ppermute(slab, ('row', 'col'), [(i, i ^ mask) for i in range(devices)])]
    ppermute x30 -> x20, starting transfers between devices: 27.3 us -> 27.8 us  [swap(): lax.ppermute(slab, ('row', 'col'), [(i, i ^ mask) for i in range(devices)])]
    pallas_call x3 -> x5, Pallas kernels: 12.3 us -> 12.3 us  [the longest x1 5.75 us: mix(): pl.pallas_call(functools.partial(mix_kernel, rows=rows, cols=cols, plan=p...]
  transfers between devices with their start and end apart: 34 -> 24, of which waited for: 16 -> 8; matrix products, arithmetic and copies ran while one was open for 0% -> 0% of each run, Pallas kernels for 4% -> 4%
where the time goes in v9:
time: 61.4 us; the launch traced here: 61.2 us
  starting transfers between devices  35.3 us (57%)
  Pallas kernels  15 us (24%)
  waiting for transfers between devices  7.59 us (12%)
  local copies, waits for them, and re-layouts  2.91 us (5%)
    ppermute x20, starting transfers between devices, swap(): lax.ppermute(slab, ('row', 'col'), [(i, i ^ mask) for i in range(devices)])  27.8 us
    ppermute x4, starting transfers between devices, swap(): return lax.ppermute(edge, axis, pairs + [(b, a) for a, b in pairs])  7.57 us
    ppermute x20, waiting for transfers between devices, swap(): lax.ppermute(slab, ('row', 'col'), [(i, i ^ mask) for i in range(devices)])  6.98 us
    pallas_call x1, Pallas kernels, mix(): pl.pallas_call(functools.partial(mix_kernel, rows=rows, cols=cols, plan=p...  5.75 us
    pallas_call x1, Pallas kernels, attend(): pl.pallas_call(functools.partial(attend_kernel, plan=plan, sets=sets, cam...  4.57 us
    pallas_call x1, Pallas kernels, expand(): pl.pallas_call(expand_kernel, in_specs=[vmem()] * 2, out_specs=vmem(), ou...  2.15 us
    pallas_call x1, Pallas kernels, finish(): pl.pallas_call(functools.partial(finish_kernel, plan=plan), in_specs=[pl....  1.94 us
    unnamed x20, local copies, waits for them, and re-layouts  1.87 us
  transfers between devices with their start and end apart: 24, of which 8 were waited for; matrix products, arithmetic and copies ran while one was open for 0% of the time, Pallas kernels for 4%

profile of v9, /device:TPU:0, one launch (start us, length us, event | category | flops | bytes accessed | tf_op | source)
XLA Modules:
  0.0 61.2 jit_solution(11168729100849131213)
XLA Ops:
  0.0 0.9 %slice_bitcast_fusion.1 = (f32[32,512]{1,0:T(8,128)S(1)}, f32[32,512]{1,0:T(8,128)S(1)}) fusion(f32[16,32,512]{2,1,0:T(8,128)} %param.8), kind=kLoop, calls=%fused_computation.2 | loop fusion | bytes 262144 | tf_op jit(solution)/shard_map/squeeze | solution.py:562
  1.1 0.8 %collective-permute-start = (bf16[32,512]{1,0:T(8,128)(2,1)S(1)}, bf16[32,512]{1,0:T(8,128)(2,1)S(1)}, u32[]{:S(2)}, u32[]{:S(2)}) collective-permute-start(bf16[32,512]{1,0:T(8,128)(2,1)S(1)} %get-tuple-element.75), channel_id=1, source_target_pairs={{4,8},{8,4},{5,9},{9,5},{6,10},{10,6},{7,11},{11,7},{20,24},{24,20... | collective-permute-start | bytes 98312 | tf_op jit(solution)/shard_map/ppermute | solution.py:437
  1.9 5.9 %collective-permute-start.1 = (bf16[32,512]{1,0:T(8,128)(2,1)S(1)}, bf16[32,512]{1,0:T(8,128)(2,1)S(1)}, u32[]{:S(2)}, u32[]{:S(2)}) collective-permute-start(bf16[32,512]{1,0:T(8,128)(2,1)S(1)} %get-tuple-element.76), channel_id=1, source_target_pairs={{0,4},{8,12},{4,0},{12,8},{1,5},{9,13},{5,1},{13,9},{2,6},{10,14},... | collective-permute-start | bytes 98312 | tf_op jit(solution)/shard_map/ppermute | solution.py:437
  10.0 0.8 %collective-permute-start.2 = (bf16[32,512]{1,0:T(8,128)(2,1)S(1)}, bf16[32,512]{1,0:T(8,128)(2,1)S(1)}, u32[]{:S(2)}, u32[]{:S(2)}) collective-permute-start(bf16[32,512]{1,0:T(8,128)(2,1)S(1)} %get-tuple-element.72), channel_id=1, source_target_pairs={{1,2},{2,1},{5,6},{6,5},{9,10},{10,9},{13,14},{14,13},{17,18},{18,... | collective-permute-start | bytes 98312 | tf_op jit(solution)/shard_map/ppermute | solution.py:437
  10.8 1.0 %copy-done.8 = bf16[512,512]{1,0:T(8,128)(2,1)S(1)} copy-done((bf16[512,512]{1,0:T(8,128)(2,1)S(1)}, bf16[512,512]{1,0:T(8,128)(2,1)}, u32[]{:S(2)}) %copy-start.8) | copy-done | bytes 524312
  11.8 2.2 %expand.1.expanded_ref = f32[8448,128]{1,0:T(8,128)S(1)} custom-call(bf16[512,512]{1,0:T(8,128)(2,1)S(1)} %copy-done.8, bf16[512,2048]{1,0:T(8,128)(2,1)S(1)} %copy-done), custom_call_target="tpu_custom_call" | custom-call | flops 10000000000 | bytes 6815744 | tf_op jit(solution)/shard_map/expand/pallas_call | solution.py:111
  14.1 5.7 %mix.1 = (f32[512,512]{1,0:T(8,128)S(1)}, bf16[2,32,512]{2,1,0:T(8,128)(2,1)S(1)}, bf16[2,32,512]{2,1,0:T(8,128)(2,1)S(1)}, bf16[1,32,512]{2,1,0:T(8,128)(2,1)S(...) custom-call(s32[1]{0:T(128)} %bitcast.own_ref, f32[8448,128]{1,0:T(8,128)S(1)} %expand.1.expanded_ref, ...), custom_call_target="tpu_custom_call" | custom-call | flops 1073741824 | bytes 11010048 | tf_op jit(solution)/shard_map/mix/pallas_call | solution.py:243
  19.8 3.1 %collective-permute-start.6 = (bf16[6,32,512]{2,1,0:T(8,128)(2,1)S(1)}, bf16[6,32,512]{2,1,0:T(8,128)(2,1)S(1)}, u32[]{:S(2)}, u32[]{:S(2)}) collective-permute-start(bf16[6,32,512]{2,1,0:T(8,128)(2,1)S(1)} %get-tuple-element.41), channel_id=1, source_target_pairs={{0,1},{1,0},{2,3},{3,2},{4,5},{5,4},{6,7},{7,6},{8,9},{9,8},{10,11... | collective-permute-start | bytes 589832 | tf_op jit(solution)/shard_map/ppermute | solution.py:512
  22.9 1.3 %collective-permute-start.4 = (bf16[2,32,512]{2,1,0:T(8,128)(2,1)S(1)}, bf16[2,32,512]{2,1,0:T(8,128)(2,1)S(1)}, u32[]{:S(2)}, u32[]{:S(2)}) collective-permute-start(bf16[2,32,512]{2,1,0:T(8,128)(2,1)S(1)} %get-tuple-element.38), channel_id=1, source_target_pairs={{0,14},{1,15},{2,12},{3,13},{4,10},{5,11},{6,8},{7,9},{8,6},{9,7},... | collective-permute-start | bytes 196616 | tf_op jit(solution)/shard_map/ppermute | solution.py:512
  24.2 2.5 %collective-permute-start.5 = (bf16[2,32,512]{2,1,0:T(8,128)(2,1)S(1)}, bf16[2,32,512]{2,1,0:T(8,128)(2,1)S(1)}, u32[]{:S(2)}, u32[]{:S(2)}) collective-permute-start(bf16[2,32,512]{2,1,0:T(8,128)(2,1)S(1)} %get-tuple-element.39), channel_id=1, source_target_pairs={{0,12},{1,13},{2,14},{3,15},{4,8},{5,9},{6,10},{7,11},{8,4},{9,5},... | collective-permute-start | bytes 196616 | tf_op jit(solution)/shard_map/ppermute | solution.py:512
  26.7 1.1 %collective-permute-start.7 = (bf16[2,32,512]{2,1,0:T(8,128)(2,1)S(1)}, bf16[2,32,512]{2,1,0:T(8,128)(2,1)S(1)}, u32[]{:S(2)}, u32[]{:S(2)}) collective-permute-start(bf16[2,32,512]{2,1,0:T(8,128)(2,1)S(1)} %get-tuple-element.42), channel_id=1, source_target_pairs={{0,10},{1,11},{2,8},{3,9},{4,14},{5,15},{6,12},{7,13},{8,2},{9,3},... | collective-permute-start | bytes 196616 | tf_op jit(solution)/shard_map/ppermute | solution.py:512
  27.8 1.8 %collective-permute-start.8 = (bf16[2,32,512]{2,1,0:T(8,128)(2,1)S(1)}, bf16[2,32,512]{2,1,0:T(8,128)(2,1)S(1)}, u32[]{:S(2)}, u32[]{:S(2)}) collective-permute-start(bf16[2,32,512]{2,1,0:T(8,128)(2,1)S(1)} %get-tuple-element.45), channel_id=1, source_target_pairs={{0,6},{1,7},{2,4},{3,5},{4,2},{5,3},{6,0},{7,1},{8,14},{9,15},{10,... | collective-permute-start | bytes 196616 | tf_op jit(solution)/shard_map/ppermute | solution.py:512
  30.4 4.4 %collective-permute-start.10 = (bf16[2,32,512]{2,1,0:T(8,128)(2,1)S(1)}, bf16[2,32,512]{2,1,0:T(8,128)(2,1)S(1)}, u32[]{:S(2)}, u32[]{:S(2)}) collective-permute-start(bf16[2,32,512]{2,1,0:T(8,128)(2,1)S(1)} %get-tuple-element.48), channel_id=1, source_target_pairs={{0,8},{1,9},{2,10},{3,11},{4,12},{5,13},{6,14},{7,15},{8,0},{9,1},... | collective-permute-start | bytes 196616 | tf_op jit(solution)/shard_map/ppermute | solution.py:512
  34.8 0.9 %collective-permute-start.11 = (bf16[2,32,512]{2,1,0:T(8,128)(2,1)S(1)}, bf16[2,32,512]{2,1,0:T(8,128)(2,1)S(1)}, u32[]{:S(2)}, u32[]{:S(2)}) collective-permute-start(bf16[2,32,512]{2,1,0:T(8,128)(2,1)S(1)} %get-tuple-element.49), channel_id=1, source_target_pairs={{0,2},{1,3},{2,0},{3,1},{4,6},{5,7},{6,4},{7,5},{8,10},{9,11},{10,... | collective-permute-start | bytes 196616 | tf_op jit(solution)/shard_map/ppermute | solution.py:512
  35.7 1.9 %collective-permute-done.7.refs_3_ = bf16[2,32,512]{2,1,0:T(8,128)(2,1)S(1)} collective-permute-done((bf16[2,32,512]{2,1,0:T(8,128)(2,1)S(1)}, bf16[2,32,512]{2,1,0:T(8,128)(2,1)S(1)}, u32[]{:S(2)}, u32[]{:S(2)}) %collective-permute-start.7) | collective-permute-done | bytes 65568 | tf_op jit(solution)/shard_map/ppermute | solution.py:512
  38.1 1.0 %collective-permute-done.11.refs_6_ = bf16[2,32,512]{2,1,0:T(8,128)(2,1)S(1)} collective-permute-done((bf16[2,32,512]{2,1,0:T(8,128)(2,1)S(1)}, bf16[2,32,512]{2,1,0:T(8,128)(2,1)S(1)}, u32[]{:S(2)}, u32[]{:S(2)}) %collective-permute-start.11) | collective-permute-done | bytes 65568 | tf_op jit(solution)/shard_map/ppermute | solution.py:512
  39.1 4.6 %attend.1 = (bf16[2,32,512]{2,1,0:T(8,128)(2,1)S(1)}, bf16[2,32,512]{2,1,0:T(8,128)(2,1)S(1)}, bf16[1,32,512]{2,1,0:T(8,128)(2,1)S(1)}, bf16[6,32,512]{2,1,0:T(8,128)(2,1)S(1)}, bf16[5,32,512]{2,1,0:T(8,128)(2,1)S(1)}) custom-call(bf16[2,32,512]{2,1,0:T(8,128)(2,1)S(1)} %collective-permute-done.4.refs_0_, ...), custom_call_target="tpu_custom_call" | custom-call | flops 1073741824 | bytes 2621440 | tf_op jit(solution)/shard_map/attend/pallas_call | solution.py:363
  44.0 2.9 %collective-permute-start.14 = (bf16[2,32,512]{2,1,0:T(8,128)(2,1)S(1)}, bf16[2,32,512]{2,1,0:T(8,128)(2,1)S(1)}, u32[]{:S(2)}, u32[]{:S(2)}) collective-permute-start(bf16[2,32,512]{2,1,0:T(8,128)(2,1)S(1)} %get-tuple-element.51), channel_id=1, source_target_pairs={{0,14},{1,15},{2,12},{3,13},{4,10},{5,11},{6,8},{7,9},{8,6},{9,7},... | collective-permute-start | bytes 196616 | tf_op jit(solution)/shard_map/ppermute | solution.py:512
  46.9 1.1 %collective-permute-start.15 = (bf16[2,32,512]{2,1,0:T(8,128)(2,1)S(1)}, bf16[2,32,512]{2,1,0:T(8,128)(2,1)S(1)}, u32[]{:S(2)}, u32[]{:S(2)}) collective-permute-start(bf16[2,32,512]{2,1,0:T(8,128)(2,1)S(1)} %get-tuple-element.52), channel_id=1, source_target_pairs={{0,12},{1,13},{2,14},{3,15},{4,8},{5,9},{6,10},{7,11},{8,4},{9,5},... | collective-permute-start | bytes 196616 | tf_op jit(solution)/shard_map/ppermute | solution.py:512
  48.1 4.2 %collective-permute-start.18 = (bf16[2,32,512]{2,1,0:T(8,128)(2,1)S(1)}, bf16[2,32,512]{2,1,0:T(8,128)(2,1)S(1)}, u32[]{:S(2)}, u32[]{:S(2)}) collective-permute-start(bf16[2,32,512]{2,1,0:T(8,128)(2,1)S(1)} %get-tuple-element.58), channel_id=1, source_target_pairs={{0,6},{1,7},{2,4},{3,5},{4,2},{5,3},{6,0},{7,1},{8,14},{9,15},{10,... | collective-permute-start | bytes 196616 | tf_op jit(solution)/shard_map/ppermute | solution.py:512
  52.3 1.6 %collective-permute-start.20 = (bf16[2,32,512]{2,1,0:T(8,128)(2,1)S(1)}, bf16[2,32,512]{2,1,0:T(8,128)(2,1)S(1)}, u32[]{:S(2)}, u32[]{:S(2)}) collective-permute-start(bf16[2,32,512]{2,1,0:T(8,128)(2,1)S(1)} %get-tuple-element.61), channel_id=1, source_target_pairs={{0,8},{1,9},{2,10},{3,11},{4,12},{5,13},{6,14},{7,15},{8,0},{9,1},... | collective-permute-start | bytes 196616 | tf_op jit(solution)/shard_map/ppermute | solution.py:512
  53.9 1.3 %collective-permute-start.21 = (bf16[2,32,512]{2,1,0:T(8,128)(2,1)S(1)}, bf16[2,32,512]{2,1,0:T(8,128)(2,1)S(1)}, u32[]{:S(2)}, u32[]{:S(2)}) collective-permute-start(bf16[2,32,512]{2,1,0:T(8,128)(2,1)S(1)} %get-tuple-element.62), channel_id=1, source_target_pairs={{0,2},{1,3},{2,0},{3,1},{4,6},{5,7},{6,4},{7,5},{8,10},{9,11},{10,... | collective-permute-start | bytes 196616 | tf_op jit(solution)/shard_map/ppermute | solution.py:512
  55.3 2.6 %collective-permute-done.17.refs_3_ = bf16[2,32,512]{2,1,0:T(8,128)(2,1)S(1)} collective-permute-done((bf16[2,32,512]{2,1,0:T(8,128)(2,1)S(1)}, bf16[2,32,512]{2,1,0:T(8,128)(2,1)S(1)}, u32[]{:S(2)}, u32[]{:S(2)}) %collective-permute-start.17) | collective-permute-done | bytes 65568 | tf_op jit(solution)/shard_map/ppermute | solution.py:512
  59.3 1.9 %finish.1 = f32[512,512]{1,0:T(8,128)} custom-call(s32[1]{0:T(128)} %bitcast.own_ref, bf16[2,32,512]{2,1,0:T(8,128)(2,1)S(1)} %collective-permute-done.14.refs_0_, bf16[2,32,512]{2,1,0:T(8,128)(2,1)S(1)} %collective-permute-done.15.refs_1_, bf16[2,32,512]{2,1,0:T(8,128)(2,1)S(1)} %collective-permute-done.18.refs_2_, ...), custom_call_target="tpu_custom_call" | custom-call | tf_op jit(solution)/shard_map/finish/pallas_call | solution.py:416
  (64 shorter events, 5.5 us)
Async XLA Ops:
  1.1 8.0 %collective-permute-start = (bf16[32,512]{1,0:T(8,128)(2,1)S(1)}, bf16[32,512]{1,0:T(8,128)(2,1)S(1)}, u32[]{:S(2)}, u32[]{:S(2)}) collective-permute-start(bf16[32,512]{1,0:T(8,128)(2,1)S(1)} %get-tuple-element.75), channel_id=1, source_target_pairs={{4,8},{8,4},{5,9},{9,5},{6,10},{10,6},{7,11},{11,7},{20,24},{24,20... | collective-permute-start | bytes 98312 | tf_op jit(solution)/shard_map/ppermute | solution.py:437
  1.9 7.8 %collective-permute-start.1 = (bf16[32,512]{1,0:T(8,128)(2,1)S(1)}, bf16[32,512]{1,0:T(8,128)(2,1)S(1)}, u32[]{:S(2)}, u32[]{:S(2)}) collective-permute-start(bf16[32,512]{1,0:T(8,128)(2,1)S(1)} %get-tuple-element.76), channel_id=1, source_target_pairs={{0,4},{8,12},{4,0},{12,8},{1,5},{9,13},{5,1},{13,9},{2,6},{10,14},... | collective-permute-start | bytes 98312 | tf_op jit(solution)/shard_map/ppermute | solution.py:437
  9.9 4.1 %collective-permute-start.3 = (bf16[32,512]{1,0:T(8,128)(2,1)S(1)}, bf16[32,512]{1,0:T(8,128)(2,1)S(1)}, u32[]{:S(2)}, u32[]{:S(2)}) collective-permute-start(bf16[32,512]{1,0:T(8,128)(2,1)S(1)} %get-tuple-element.71), channel_id=1, source_target_pairs={{0,1},{2,3},{1,0},{3,2},{4,5},{6,7},{5,4},{7,6},{8,9},{10,11},{9,8... | collective-permute-start | bytes 98312 | tf_op jit(solution)/shard_map/ppermute | solution.py:437
  10.0 4.0 %collective-permute-start.2 = (bf16[32,512]{1,0:T(8,128)(2,1)S(1)}, bf16[32,512]{1,0:T(8,128)(2,1)S(1)}, u32[]{:S(2)}, u32[]{:S(2)}) collective-permute-start(bf16[32,512]{1,0:T(8,128)(2,1)S(1)} %get-tuple-element.72), channel_id=1, source_target_pairs={{1,2},{2,1},{5,6},{6,5},{9,10},{10,9},{13,14},{14,13},{17,18},{18,... | collective-permute-start | bytes 98312 | tf_op jit(solution)/shard_map/ppermute | solution.py:437
  19.8 6.9 %collective-permute-start.6 = (bf16[6,32,512]{2,1,0:T(8,128)(2,1)S(1)}, bf16[6,32,512]{2,1,0:T(8,128)(2,1)S(1)}, u32[]{:S(2)}, u32[]{:S(2)}) collective-permute-start(bf16[6,32,512]{2,1,0:T(8,128)(2,1)S(1)} %get-tuple-element.41), channel_id=1, source_target_pairs={{0,1},{1,0},{2,3},{3,2},{4,5},{5,4},{6,7},{7,6},{8,9},{9,8},{10,11... | collective-permute-start | bytes 589832 | tf_op jit(solution)/shard_map/ppermute | solution.py:512
  22.9 7.5 %collective-permute-start.4 = (bf16[2,32,512]{2,1,0:T(8,128)(2,1)S(1)}, bf16[2,32,512]{2,1,0:T(8,128)(2,1)S(1)}, u32[]{:S(2)}, u32[]{:S(2)}) collective-permute-start(bf16[2,32,512]{2,1,0:T(8,128)(2,1)S(1)} %get-tuple-element.38), channel_id=1, source_target_pairs={{0,14},{1,15},{2,12},{3,13},{4,10},{5,11},{6,8},{7,9},{8,6},{9,7},... | collective-permute-start | bytes 196616 | tf_op jit(solution)/shard_map/ppermute | solution.py:512
  24.2 10.6 %collective-permute-start.5 = (bf16[2,32,512]{2,1,0:T(8,128)(2,1)S(1)}, bf16[2,32,512]{2,1,0:T(8,128)(2,1)S(1)}, u32[]{:S(2)}, u32[]{:S(2)}) collective-permute-start(bf16[2,32,512]{2,1,0:T(8,128)(2,1)S(1)} %get-tuple-element.39), channel_id=1, source_target_pairs={{0,12},{1,13},{2,14},{3,15},{4,8},{5,9},{6,10},{7,11},{8,4},{9,5},... | collective-permute-start | bytes 196616 | tf_op jit(solution)/shard_map/ppermute | solution.py:512
  26.7 10.9 %collective-permute-start.7 = (bf16[2,32,512]{2,1,0:T(8,128)(2,1)S(1)}, bf16[2,32,512]{2,1,0:T(8,128)(2,1)S(1)}, u32[]{:S(2)}, u32[]{:S(2)}) collective-permute-start(bf16[2,32,512]{2,1,0:T(8,128)(2,1)S(1)} %get-tuple-element.42), channel_id=1, source_target_pairs={{0,10},{1,11},{2,8},{3,9},{4,14},{5,15},{6,12},{7,13},{8,2},{9,3},... | collective-permute-start | bytes 196616 | tf_op jit(solution)/shard_map/ppermute | solution.py:512
  27.8 9.8 %collective-permute-start.8 = (bf16[2,32,512]{2,1,0:T(8,128)(2,1)S(1)}, bf16[2,32,512]{2,1,0:T(8,128)(2,1)S(1)}, u32[]{:S(2)}, u32[]{:S(2)}) collective-permute-start(bf16[2,32,512]{2,1,0:T(8,128)(2,1)S(1)} %get-tuple-element.45), channel_id=1, source_target_pairs={{0,6},{1,7},{2,4},{3,5},{4,2},{5,3},{6,0},{7,1},{8,14},{9,15},{10,... | collective-permute-start | bytes 196616 | tf_op jit(solution)/shard_map/ppermute | solution.py:512
  29.6 8.5 %collective-permute-start.9 = (bf16[2,32,512]{2,1,0:T(8,128)(2,1)S(1)}, bf16[2,32,512]{2,1,0:T(8,128)(2,1)S(1)}, u32[]{:S(2)}, u32[]{:S(2)}) collective-permute-start(bf16[2,32,512]{2,1,0:T(8,128)(2,1)S(1)} %get-tuple-element.47), channel_id=1, source_target_pairs={{0,4},{1,5},{2,6},{3,7},{4,0},{5,1},{6,2},{7,3},{8,12},{9,13},{10,... | collective-permute-start | bytes 196616 | tf_op jit(solution)/shard_map/ppermute | solution.py:512
  30.4 7.7 %collective-permute-start.10 = (bf16[2,32,512]{2,1,0:T(8,128)(2,1)S(1)}, bf16[2,32,512]{2,1,0:T(8,128)(2,1)S(1)}, u32[]{:S(2)}, u32[]{:S(2)}) collective-permute-start(bf16[2,32,512]{2,1,0:T(8,128)(2,1)S(1)} %get-tuple-element.48), channel_id=1, source_target_pairs={{0,8},{1,9},{2,10},{3,11},{4,12},{5,13},{6,14},{7,15},{8,0},{9,1},... | collective-permute-start | bytes 196616 | tf_op jit(solution)/shard_map/ppermute | solution.py:512
  34.8 4.3 %collective-permute-start.11 = (bf16[2,32,512]{2,1,0:T(8,128)(2,1)S(1)}, bf16[2,32,512]{2,1,0:T(8,128)(2,1)S(1)}, u32[]{:S(2)}, u32[]{:S(2)}) collective-permute-start(bf16[2,32,512]{2,1,0:T(8,128)(2,1)S(1)} %get-tuple-element.49), channel_id=1, source_target_pairs={{0,2},{1,3},{2,0},{3,1},{4,6},{5,7},{6,4},{7,5},{8,10},{9,11},{10,... | collective-permute-start | bytes 196616 | tf_op jit(solution)/shard_map/ppermute | solution.py:512
  37.6 1.5 %collective-permute-start.12 = (bf16[2,32,512]{2,1,0:T(8,128)(2,1)S(1)}, bf16[2,32,512]{2,1,0:T(8,128)(2,1)S(1)}, u32[]{:S(2)}, u32[]{:S(2)}) collective-permute-start(bf16[2,32,512]{2,1,0:T(8,128)(2,1)S(1)} %collective-permute-done.4.refs_0_), channel_id=1, source_target_pairs={{0,1},{1,0},{2,3},{3,2},{4,5},{5,4},{6,7},{7,6},{8,9},{9,8},{10,11... | collective-permute-start | bytes 196616 | tf_op jit(solution)/shard_map/ppermute | solution.py:512
  37.6 1.5 %collective-permute-start.13 = (bf16[2,32,512]{2,1,0:T(8,128)(2,1)S(1)}, bf16[2,32,512]{2,1,0:T(8,128)(2,1)S(1)}, u32[]{:S(2)}, u32[]{:S(2)}) collective-permute-start(bf16[2,32,512]{2,1,0:T(8,128)(2,1)S(1)} %collective-permute-done.5.refs_1_), channel_id=1, source_target_pairs={{0,1},{1,0},{2,3},{3,2},{4,5},{5,4},{6,7},{7,6},{8,9},{9,8},{10,11... | collective-permute-start | bytes 196616 | tf_op jit(solution)/shard_map/ppermute | solution.py:512
  43.7 4.3 %collective-permute-start.16 = (bf16[6,32,512]{2,1,0:T(8,128)(2,1)S(1)}, bf16[6,32,512]{2,1,0:T(8,128)(2,1)S(1)}, u32[]{:S(2)}, u32[]{:S(2)}) collective-permute-start(bf16[6,32,512]{2,1,0:T(8,128)(2,1)S(1)} %get-tuple-element.54), channel_id=1, source_target_pairs={{0,1},{1,0},{2,3},{3,2},{4,5},{5,4},{6,7},{7,6},{8,9},{9,8},{10,11... | collective-permute-start | bytes 589832 | tf_op jit(solution)/shard_map/ppermute | solution.py:512
  44.0 8.3 %collective-permute-start.14 = (bf16[2,32,512]{2,1,0:T(8,128)(2,1)S(1)}, bf16[2,32,512]{2,1,0:T(8,128)(2,1)S(1)}, u32[]{:S(2)}, u32[]{:S(2)}) collective-permute-start(bf16[2,32,512]{2,1,0:T(8,128)(2,1)S(1)} %get-tuple-element.51), channel_id=1, source_target_pairs={{0,14},{1,15},{2,12},{3,13},{4,10},{5,11},{6,8},{7,9},{8,6},{9,7},... | collective-permute-start | bytes 196616 | tf_op jit(solution)/shard_map/ppermute | solution.py:512
  46.9 7.0 %collective-permute-start.15 = (bf16[2,32,512]{2,1,0:T(8,128)(2,1)S(1)}, bf16[2,32,512]{2,1,0:T(8,128)(2,1)S(1)}, u32[]{:S(2)}, u32[]{:S(2)}) collective-permute-start(bf16[2,32,512]{2,1,0:T(8,128)(2,1)S(1)} %get-tuple-element.52), channel_id=1, source_target_pairs={{0,12},{1,13},{2,14},{3,15},{4,8},{5,9},{6,10},{7,11},{8,4},{9,5},... | collective-permute-start | bytes 196616 | tf_op jit(solution)/shard_map/ppermute | solution.py:512
  48.0 9.9 %collective-permute-start.17 = (bf16[2,32,512]{2,1,0:T(8,128)(2,1)S(1)}, bf16[2,32,512]{2,1,0:T(8,128)(2,1)S(1)}, u32[]{:S(2)}, u32[]{:S(2)}) collective-permute-start(bf16[2,32,512]{2,1,0:T(8,128)(2,1)S(1)} %get-tuple-element.55), channel_id=1, source_target_pairs={{0,10},{1,11},{2,8},{3,9},{4,14},{5,15},{6,12},{7,13},{8,2},{9,3},... | collective-permute-start | bytes 196616 | tf_op jit(solution)/shard_map/ppermute | solution.py:512
  48.1 9.8 %collective-permute-start.18 = (bf16[2,32,512]{2,1,0:T(8,128)(2,1)S(1)}, bf16[2,32,512]{2,1,0:T(8,128)(2,1)S(1)}, u32[]{:S(2)}, u32[]{:S(2)}) collective-permute-start(bf16[2,32,512]{2,1,0:T(8,128)(2,1)S(1)} %get-tuple-element.58), channel_id=1, source_target_pairs={{0,6},{1,7},{2,4},{3,5},{4,2},{5,3},{6,0},{7,1},{8,14},{9,15},{10,... | collective-permute-start | bytes 196616 | tf_op jit(solution)/shard_map/ppermute | solution.py:512
  52.3 6.3 %collective-permute-start.19 = (bf16[2,32,512]{2,1,0:T(8,128)(2,1)S(1)}, bf16[2,32,512]{2,1,0:T(8,128)(2,1)S(1)}, u32[]{:S(2)}, u32[]{:S(2)}) collective-permute-start(bf16[2,32,512]{2,1,0:T(8,128)(2,1)S(1)} %get-tuple-element.60), channel_id=1, source_target_pairs={{0,4},{1,5},{2,6},{3,7},{4,0},{5,1},{6,2},{7,3},{8,12},{9,13},{10,... | collective-permute-start | bytes 196616 | tf_op jit(solution)/shard_map/ppermute | solution.py:512
  52.3 6.9 %collective-permute-start.20 = (bf16[2,32,512]{2,1,0:T(8,128)(2,1)S(1)}, bf16[2,32,512]{2,1,0:T(8,128)(2,1)S(1)}, u32[]{:S(2)}, u32[]{:S(2)}) collective-permute-start(bf16[2,32,512]{2,1,0:T(8,128)(2,1)S(1)} %get-tuple-element.61), channel_id=1, source_target_pairs={{0,8},{1,9},{2,10},{3,11},{4,12},{5,13},{6,14},{7,15},{8,0},{9,1},... | collective-permute-start | bytes 196616 | tf_op jit(solution)/shard_map/ppermute | solution.py:512
  53.9 5.2 %collective-permute-start.21 = (bf16[2,32,512]{2,1,0:T(8,128)(2,1)S(1)}, bf16[2,32,512]{2,1,0:T(8,128)(2,1)S(1)}, u32[]{:S(2)}, u32[]{:S(2)}) collective-permute-start(bf16[2,32,512]{2,1,0:T(8,128)(2,1)S(1)} %get-tuple-element.62), channel_id=1, source_target_pairs={{0,2},{1,3},{2,0},{3,1},{4,6},{5,7},{6,4},{7,5},{8,10},{9,11},{10,... | collective-permute-start | bytes 196616 | tf_op jit(solution)/shard_map/ppermute | solution.py:512
  57.9 1.3 %collective-permute-start.22 = (bf16[2,32,512]{2,1,0:T(8,128)(2,1)S(1)}, bf16[2,32,512]{2,1,0:T(8,128)(2,1)S(1)}, u32[]{:S(2)}, u32[]{:S(2)}) collective-permute-start(bf16[2,32,512]{2,1,0:T(8,128)(2,1)S(1)} %collective-permute-done.14.refs_0_), channel_id=1, source_target_pairs={{0,1},{1,0},{2,3},{3,2},{4,5},{5,4},{6,7},{7,6},{8,9},{9,8},{10,11... | collective-permute-start | bytes 196616 | tf_op jit(solution)/shard_map/ppermute | solution.py:512
  57.9 1.4 %collective-permute-start.23 = (bf16[2,32,512]{2,1,0:T(8,128)(2,1)S(1)}, bf16[2,32,512]{2,1,0:T(8,128)(2,1)S(1)}, u32[]{:S(2)}, u32[]{:S(2)}) collective-permute-start(bf16[2,32,512]{2,1,0:T(8,128)(2,1)S(1)} %collective-permute-done.15.refs_1_), channel_id=1, source_target_pairs={{0,1},{1,0},{2,3},{3,2},{4,5},{5,4},{6,7},{7,6},{8,9},{9,8},{10,11... | collective-permute-start | bytes 196616 | tf_op jit(solution)/shard_map/ppermute | solution.py:512
  (10 other events, 89.4 us)

commit v10 on v9

--- a/solution.py
+++ b/solution.py
@@ -428,13 +428,20 @@
     )(own, *incoming, back, w_out, mixed)
 
 
-def exchange(low_edge, high_edge, axis):
-    count = lax.axis_size(axis)
-    even = lax.axis_index(axis) % 2 == 0
-
-    def swap(edge, start):
-        pairs = [(i, i + 1) for i in range(start, count - 1, 2)]
-        return lax.ppermute(edge, axis, pairs + [(b, a) for a, b in pairs])
+def exchange(low_edge, high_edge, shift):
+    counts = lax.axis_size("row"), lax.axis_size("col")
+    lead = 0 if shift[0] else 1
+    even = lax.axis_index(("row", "col")[lead]) % 2 == 0
+
+    def swap(edge, parity):
+        pairs = []
+        for row in range(counts[0]):
+            for col in range(counts[1]):
+                there = row + shift[0], col + shift[1]
+                inside = there[0] < counts[0] and 0 <= there[1] < counts[1]
+                if (row, col)[lead] % 2 == parity and inside:
+                    pairs.append((row * counts[1] + col, there[0] * counts[1] + there[1]))
+        return lax.ppermute(edge, ("row", "col"), pairs + [(b, a) for a, b in pairs])
 
     one = swap(jnp.where(even, high_edge, low_edge), 0)
     two = swap(jnp.where(even, low_edge, high_edge), 1)
@@ -443,12 +450,7 @@
 
 def exchange_plan(row_devices, col_devices):
     devices = row_devices * col_devices
-    crossing = list(range(devices - 2, devices // 2 - 1, -2))
-    others = list(range(devices // 2 - 2, 0, -2))
-    masks = crossing[:1]
-    for index, mask in enumerate(crossing[1:]):
-        masks += [mask] + others[index : index + 1]
-    return masks + [0], min(2, len(masks)), 2
+    return list(range(devices - 2, -1, -2)), 2, 2
 
 
 def outgoing_shapes(plan, size, channels):
@@ -515,8 +517,7 @@
     swapped = swap(passed, 1)
     first = [swap(slab, mask) for slab, mask in zip(slabs, masks)]
     rest = [swap(slab, mask) for slab, mask in zip(join(own, swapped), masks[late:-1])]
-    tie = min(1, len(rest) - 1)
-    *first, rest[tie] = lax.optimization_barrier((*first, rest[tie]))
+    *first, rest[0] = lax.optimization_barrier((*first, rest[0]))
     return [*first, *rest, kept, *[swap(slab, 1) for slab in first], swapped]
 
 
@@ -560,15 +561,19 @@
 
     flat = field.reshape(tokens, channels)
     edges = half_norm_of(jnp.concatenate([field[0], field[rows - 1]], axis=0), 10**10)
-    up, down = exchange(edges[:cols], edges[cols:], "row")
-    normed = half_norm_of(flat, 10**9)
+    top, bottom = edges[:cols], edges[cols:]
+    up, down = exchange(top, bottom, (1, 0))
+    ready, _ = lax.optimization_barrier((flat, edges))
+    normed = half_norm_of(ready, 10**9)
     tile = normed.reshape(rows, cols, channels)
+    left_side, right_side = exchange(tile[:, 0], tile[:, cols - 1], (0, 1))
+    up_left, down_right = exchange(top[:1], bottom[cols - 1 :], (1, 1))
+    up_right, down_left = exchange(top[cols - 1 :], bottom[:1], (1, -1))
+    ready, up_right, down_left, up_left, down_right = lax.optimization_barrier((normed, up_right, down_left, up_left, down_right))
+    expanded = expand(ready, w_expand)
     spare = jnp.zeros((round_up(rows + 2, 16) - rows - 2, channels), jnp.bfloat16)
-    first = jnp.concatenate([up[:1], tile[:, 0], down[:1], spare], axis=0)
-    last = jnp.concatenate([up[cols - 1 :], tile[:, cols - 1], down[cols - 1 :], spare], axis=0)
-    normed, first, last = lax.optimization_barrier((normed, first, last))
-    expanded = expand(normed, w_expand)
-    left, right = exchange(first, last, "col")
+    left = jnp.concatenate([up_left, left_side, down_left, spare], axis=0)
+    right = jnp.concatenate([up_right, right_side, down_right, spare], axis=0)
     pairwise = 8 <= devices <= 16 and devices & (devices - 1) == 0 and col_devices % 2 == 0
     if pairwise:
         plan = exchange_plan(row_devices, col_devices)

time: 61.4 us -> 72.1 us (1.17)
  starting transfers between devices: 35.3 us -> 46.2 us
    ppermute x4 -> x8, starting transfers between devices: 7.57 us -> 16.3 us  [swap(): lax.ppermute(edge, ('row', 'col'), pairs + [(b, a) for a, b in pairs])]
    ppermute x20, starting transfers between devices: 27.8 us -> 29.9 us  [swap(): lax.ppermute(slab, ('row', 'col'), [(i, i ^ mask) for i in range(devices)])]
  transfers between devices with their start and end apart: 24 -> 28, of which waited for: 8 -> 10; matrix products, arithmetic and copies ran while one was open for 0% -> 0% of each run, Pallas kernels for 4% -> 4%
where the time goes in v10:
time: 72.1 us; the launch traced here: 71.8 us
  starting transfers between devices  46.2 us (64%)
  Pallas kernels  15 us (21%)
  waiting for transfers between devices  7.19 us (10%)
  local copies, waits for them, and re-layouts  2.88 us (4%)
    ppermute x20, starting transfers between devices, swap(): lax.ppermute(slab, ('row', 'col'), [(i, i ^ mask) for i in range(devices)])  29.9 us
    ppermute x8, starting transfers between devices, swap(): lax.ppermute(edge, ('row', 'col'), pairs + [(b, a) for a, b in pairs])  16.3 us
    ppermute x20, waiting for transfers between devices, swap(): lax.ppermute(slab, ('row', 'col'), [(i, i ^ mask) for i in range(devices)])  7.17 us
    pallas_call x1, Pallas kernels, mix(): pl.pallas_call(functools.partial(mix_kernel, rows=rows, cols=cols, plan=p...  5.75 us
    pallas_call x1, Pallas kernels, attend(): pl.pallas_call(functools.partial(attend_kernel, plan=plan, sets=sets, cam...  4.56 us
    pallas_call x1, Pallas kernels, expand(): pl.pallas_call(expand_kernel, in_specs=[vmem()] * 2, out_specs=vmem(), ou...  2.15 us
    pallas_call x1, Pallas kernels, finish(): pl.pallas_call(functools.partial(finish_kernel, plan=plan), in_specs=[pl....  1.94 us
    unnamed x20, local copies, waits for them, and re-layouts  1.86 us
  transfers between devices with their start and end apart: 28, of which 10 were waited for; matrix products, arithmetic and copies ran while one was open for 0% of the time, Pallas kernels for 4%

profile of v10, /device:TPU:0, one launch (start us, length us, event | category | flops | bytes accessed | tf_op | source)
XLA Modules:
  0.0 71.8 jit_solution(7667808135115716499)
XLA Ops:
  0.0 0.9 %slice_bitcast_fusion.1 = (f32[32,512]{1,0:T(8,128)S(1)}, f32[32,512]{1,0:T(8,128)S(1)}) fusion(f32[16,32,512]{2,1,0:T(8,128)} %param.8), kind=kLoop, calls=%fused_computation.2 | loop fusion | bytes 262144 | tf_op jit(solution)/shard_map/squeeze | solution.py:563
  1.1 4.5 %collective-permute-start.3 = (bf16[1,512]{1,0:T(2,128)(2,1)S(1)}, bf16[1,512]{1,0:T(2,128)(2,1)S(1)}, u32[]{:S(2)}, u32[]{:S(2)}) collective-permute-start(bf16[1,512]{1,0:T(2,128)(2,1)S(1)} %get-tuple-element.81), channel_id=1, source_target_pairs={{0,5},{1,6},{2,7},{8,13},{9,14},{10,15},{5,0},{6,1},{7,2},{13,8},{... | collective-permute-start | bytes 3080 | tf_op jit(solution)/shard_map/ppermute | solution.py:444
  7.7 7.0 %collective-permute-start.5 = (bf16[32,512]{1,0:T(8,128)(2,1)S(1)}, bf16[32,512]{1,0:T(8,128)(2,1)S(1)}, u32[]{:S(2)}, u32[]{:S(2)}) collective-permute-start(bf16[32,512]{1,0:T(8,128)(2,1)S(1)} %get-tuple-element.79), channel_id=1, source_target_pairs={{0,4},{1,5},{2,6},{3,7},{8,12},{9,13},{10,14},{11,15},{4,0},{5,1},... | collective-permute-start | bytes 98312 | tf_op jit(solution)/shard_map/ppermute | solution.py:444
  16.6 1.5 %collective-permute-start.7 = (bf16[16,512]{1,0:T(8,128)(2,1)S(1)}, bf16[16,512]{1,0:T(8,128)(2,1)S(1)}, u32[]{:S(2)}, u32[]{:S(2)}) collective-permute-start(bf16[16,512]{1,0:T(8,128)(2,1)S(1)} %get-tuple-element.75), channel_id=1, source_target_pairs={{0,1},{2,3},{4,5},{6,7},{8,9},{10,11},{12,13},{14,15},{1,0},{3,2},... | collective-permute-start | bytes 49160 | tf_op jit(solution)/shard_map/ppermute | solution.py:444
  18.9 1.0 %copy-done.8 = bf16[512,512]{1,0:T(8,128)(2,1)S(1)} copy-done((bf16[512,512]{1,0:T(8,128)(2,1)S(1)}, bf16[512,512]{1,0:T(8,128)(2,1)}, u32[]{:S(2)}) %copy-start.8) | copy-done | bytes 524312
  19.9 2.1 %expand.1.expanded_ref = f32[8448,128]{1,0:T(8,128)S(1)} custom-call(bf16[512,512]{1,0:T(8,128)(2,1)S(1)} %copy-done.8, bf16[512,2048]{1,0:T(8,128)(2,1)S(1)} %copy-done), custom_call_target="tpu_custom_call" | custom-call | flops 10000000000 | bytes 6815744 | tf_op jit(solution)/shard_map/expand/pallas_call | solution.py:111
  22.3 5.8 %mix.1 = (f32[512,512]{1,0:T(8,128)S(1)}, bf16[2,32,512]{2,1,0:T(8,128)(2,1)S(1)}, bf16[2,32,512]{2,1,0:T(8,128)(2,1)S(1)}, bf16[1,32,512]{2,1,0:T(8,128)(2,1)S(...) custom-call(s32[1]{0:T(128)} %bitcast.own_ref, f32[8448,128]{1,0:T(8,128)S(1)} %expand.1.expanded_ref, ...), custom_call_target="tpu_custom_call" | custom-call | flops 1073741824 | bytes 11010048 | tf_op jit(solution)/shard_map/mix/pallas_call | solution.py:243
  28.1 3.3 %collective-permute-start.10 = (bf16[6,32,512]{2,1,0:T(8,128)(2,1)S(1)}, bf16[6,32,512]{2,1,0:T(8,128)(2,1)S(1)}, u32[]{:S(2)}, u32[]{:S(2)}) collective-permute-start(bf16[6,32,512]{2,1,0:T(8,128)(2,1)S(1)} %get-tuple-element.47), channel_id=1, source_target_pairs={{0,1},{1,0},{2,3},{3,2},{4,5},{5,4},{6,7},{7,6},{8,9},{9,8},{10,11... | collective-permute-start | bytes 589832 | tf_op jit(solution)/shard_map/ppermute | solution.py:514
  31.3 2.5 %collective-permute-start.8 = (bf16[2,32,512]{2,1,0:T(8,128)(2,1)S(1)}, bf16[2,32,512]{2,1,0:T(8,128)(2,1)S(1)}, u32[]{:S(2)}, u32[]{:S(2)}) collective-permute-start(bf16[2,32,512]{2,1,0:T(8,128)(2,1)S(1)} %get-tuple-element.44), channel_id=1, source_target_pairs={{0,14},{1,15},{2,12},{3,13},{4,10},{5,11},{6,8},{7,9},{8,6},{9,7},... | collective-permute-start | bytes 196616 | tf_op jit(solution)/shard_map/ppermute | solution.py:514
  34.6 2.5 %collective-permute-start.11 = (bf16[2,32,512]{2,1,0:T(8,128)(2,1)S(1)}, bf16[2,32,512]{2,1,0:T(8,128)(2,1)S(1)}, u32[]{:S(2)}, u32[]{:S(2)}) collective-permute-start(bf16[2,32,512]{2,1,0:T(8,128)(2,1)S(1)} %get-tuple-element.48), channel_id=1, source_target_pairs={{0,10},{1,11},{2,8},{3,9},{4,14},{5,15},{6,12},{7,13},{8,2},{9,3},... | collective-permute-start | bytes 196616 | tf_op jit(solution)/shard_map/ppermute | solution.py:514
  37.1 2.0 %collective-permute-start.12 = (bf16[2,32,512]{2,1,0:T(8,128)(2,1)S(1)}, bf16[2,32,512]{2,1,0:T(8,128)(2,1)S(1)}, u32[]{:S(2)}, u32[]{:S(2)}) collective-permute-start(bf16[2,32,512]{2,1,0:T(8,128)(2,1)S(1)} %get-tuple-element.52), channel_id=1, source_target_pairs={{0,8},{1,9},{2,10},{3,11},{4,12},{5,13},{6,14},{7,15},{8,0},{9,1},... | collective-permute-start | bytes 196616 | tf_op jit(solution)/shard_map/ppermute | solution.py:514
  39.1 1.1 %collective-permute-start.13 = (bf16[2,32,512]{2,1,0:T(8,128)(2,1)S(1)}, bf16[2,32,512]{2,1,0:T(8,128)(2,1)S(1)}, u32[]{:S(2)}, u32[]{:S(2)}) collective-permute-start(bf16[2,32,512]{2,1,0:T(8,128)(2,1)S(1)} %get-tuple-element.53), channel_id=1, source_target_pairs={{0,6},{1,7},{2,4},{3,5},{4,2},{5,3},{6,0},{7,1},{8,14},{9,15},{10,... | collective-permute-start | bytes 196616 | tf_op jit(solution)/shard_map/ppermute | solution.py:514
  40.1 3.5 %collective-permute-start.14 = (bf16[2,32,512]{2,1,0:T(8,128)(2,1)S(1)}, bf16[2,32,512]{2,1,0:T(8,128)(2,1)S(1)}, u32[]{:S(2)}, u32[]{:S(2)}) collective-permute-start(bf16[2,32,512]{2,1,0:T(8,128)(2,1)S(1)} %get-tuple-element.54), channel_id=1, source_target_pairs={{0,4},{1,5},{2,6},{3,7},{4,0},{5,1},{6,2},{7,3},{8,12},{9,13},{10,... | collective-permute-start | bytes 196616 | tf_op jit(solution)/shard_map/ppermute | solution.py:514
  43.6 0.9 %collective-permute-start.15 = (bf16[2,32,512]{2,1,0:T(8,128)(2,1)S(1)}, bf16[2,32,512]{2,1,0:T(8,128)(2,1)S(1)}, u32[]{:S(2)}, u32[]{:S(2)}) collective-permute-start(bf16[2,32,512]{2,1,0:T(8,128)(2,1)S(1)} %get-tuple-element.55), channel_id=1, source_target_pairs={{0,2},{1,3},{2,0},{3,1},{4,6},{5,7},{6,4},{7,5},{8,10},{9,11},{10,... | collective-permute-start | bytes 196616 | tf_op jit(solution)/shard_map/ppermute | solution.py:514
  44.6 2.1 %collective-permute-done.11.refs_2_ = bf16[2,32,512]{2,1,0:T(8,128)(2,1)S(1)} collective-permute-done((bf16[2,32,512]{2,1,0:T(8,128)(2,1)S(1)}, bf16[2,32,512]{2,1,0:T(8,128)(2,1)S(1)}, u32[]{:S(2)}, u32[]{:S(2)}) %collective-permute-start.11) | collective-permute-done | bytes 65568 | tf_op jit(solution)/shard_map/ppermute | solution.py:514
  48.2 4.6 %attend.1 = (bf16[2,32,512]{2,1,0:T(8,128)(2,1)S(1)}, bf16[2,32,512]{2,1,0:T(8,128)(2,1)S(1)}, bf16[1,32,512]{2,1,0:T(8,128)(2,1)S(1)}, bf16[6,32,512]{2,1,0:T(8,128)(2,1)S(1)}, bf16[5,32,512]{2,1,0:T(8,128)(2,1)S(1)}) custom-call(bf16[2,32,512]{2,1,0:T(8,128)(2,1)S(1)} %collective-permute-done.8.refs_0_, ...), custom_call_target="tpu_custom_call" | custom-call | flops 1073741824 | bytes 2621440 | tf_op jit(solution)/shard_map/attend/pallas_call | solution.py:363
  53.1 2.4 %collective-permute-start.18 = (bf16[2,32,512]{2,1,0:T(8,128)(2,1)S(1)}, bf16[2,32,512]{2,1,0:T(8,128)(2,1)S(1)}, u32[]{:S(2)}, u32[]{:S(2)}) collective-permute-start(bf16[2,32,512]{2,1,0:T(8,128)(2,1)S(1)} %get-tuple-element.57), channel_id=1, source_target_pairs={{0,14},{1,15},{2,12},{3,13},{4,10},{5,11},{6,8},{7,9},{8,6},{9,7},... | collective-permute-start | bytes 196616 | tf_op jit(solution)/shard_map/ppermute | solution.py:514
  55.5 1.8 %collective-permute-start.19 = (bf16[2,32,512]{2,1,0:T(8,128)(2,1)S(1)}, bf16[2,32,512]{2,1,0:T(8,128)(2,1)S(1)}, u32[]{:S(2)}, u32[]{:S(2)}) collective-permute-start(bf16[2,32,512]{2,1,0:T(8,128)(2,1)S(1)} %get-tuple-element.58), channel_id=1, source_target_pairs={{0,12},{1,13},{2,14},{3,15},{4,8},{5,9},{6,10},{7,11},{8,4},{9,5},... | collective-permute-start | bytes 196616 | tf_op jit(solution)/shard_map/ppermute | solution.py:514
  57.4 3.4 %collective-permute-start.22 = (bf16[2,32,512]{2,1,0:T(8,128)(2,1)S(1)}, bf16[2,32,512]{2,1,0:T(8,128)(2,1)S(1)}, u32[]{:S(2)}, u32[]{:S(2)}) collective-permute-start(bf16[2,32,512]{2,1,0:T(8,128)(2,1)S(1)} %get-tuple-element.65), channel_id=1, source_target_pairs={{0,8},{1,9},{2,10},{3,11},{4,12},{5,13},{6,14},{7,15},{8,0},{9,1},... | collective-permute-start | bytes 196616 | tf_op jit(solution)/shard_map/ppermute | solution.py:514
  60.9 3.0 %collective-permute-start.24 = (bf16[2,32,512]{2,1,0:T(8,128)(2,1)S(1)}, bf16[2,32,512]{2,1,0:T(8,128)(2,1)S(1)}, u32[]{:S(2)}, u32[]{:S(2)}) collective-permute-start(bf16[2,32,512]{2,1,0:T(8,128)(2,1)S(1)} %get-tuple-element.67), channel_id=1, source_target_pairs={{0,4},{1,5},{2,6},{3,7},{4,0},{5,1},{6,2},{7,3},{8,12},{9,13},{10,... | collective-permute-start | bytes 196616 | tf_op jit(solution)/shard_map/ppermute | solution.py:514
  63.8 2.2 %collective-permute-start.25 = (bf16[2,32,512]{2,1,0:T(8,128)(2,1)S(1)}, bf16[2,32,512]{2,1,0:T(8,128)(2,1)S(1)}, u32[]{:S(2)}, u32[]{:S(2)}) collective-permute-start(bf16[2,32,512]{2,1,0:T(8,128)(2,1)S(1)} %get-tuple-element.68), channel_id=1, source_target_pairs={{0,2},{1,3},{2,0},{3,1},{4,6},{5,7},{6,4},{7,5},{8,10},{9,11},{10,... | collective-permute-start | bytes 196616 | tf_op jit(solution)/shard_map/ppermute | solution.py:514
  66.0 1.6 %collective-permute-done.21.refs_2_ = bf16[2,32,512]{2,1,0:T(8,128)(2,1)S(1)} collective-permute-done((bf16[2,32,512]{2,1,0:T(8,128)(2,1)S(1)}, bf16[2,32,512]{2,1,0:T(8,128)(2,1)S(1)}, u32[]{:S(2)}, u32[]{:S(2)}) %collective-permute-start.21) | collective-permute-done | bytes 65568 | tf_op jit(solution)/shard_map/ppermute | solution.py:514
  67.6 1.0 %collective-permute-done.22.refs_3_ = bf16[2,32,512]{2,1,0:T(8,128)(2,1)S(1)} collective-permute-done((bf16[2,32,512]{2,1,0:T(8,128)(2,1)S(1)}, bf16[2,32,512]{2,1,0:T(8,128)(2,1)S(1)}, u32[]{:S(2)}, u32[]{:S(2)}) %collective-permute-start.22) | collective-permute-done | bytes 65568 | tf_op jit(solution)/shard_map/ppermute | solution.py:514
  69.8 1.9 %finish.1 = f32[512,512]{1,0:T(8,128)} custom-call(s32[1]{0:T(128)} %bitcast.own_ref, bf16[2,32,512]{2,1,0:T(8,128)(2,1)S(1)} %collective-permute-done.18.refs_0_, bf16[2,32,512]{2,1,0:T(8,128)(2,1)S(1)} %collective-permute-done.19.refs_1_, bf16[2,32,512]{2,1,0:T(8,128)(2,1)S(1)} %collective-permute-done.21.refs_2_, ...), custom_call_target="tpu_custom_call" | custom-call | tf_op jit(solution)/shard_map/finish/pallas_call | solution.py:416
  (73 shorter events, 9.0 us)
Async XLA Ops:
  1.1 14.8 %collective-permute-start.3 = (bf16[1,512]{1,0:T(2,128)(2,1)S(1)}, bf16[1,512]{1,0:T(2,128)(2,1)S(1)}, u32[]{:S(2)}, u32[]{:S(2)}) collective-permute-start(bf16[1,512]{1,0:T(2,128)(2,1)S(1)} %get-tuple-element.81), channel_id=1, source_target_pairs={{0,5},{1,6},{2,7},{8,13},{9,14},{10,15},{5,0},{6,1},{7,2},{13,8},{... | collective-permute-start | bytes 3080 | tf_op jit(solution)/shard_map/ppermute | solution.py:444
  5.7 12.5 %collective-permute-start.1 = (bf16[1,512]{1,0:T(2,128)(2,1)S(1)}, bf16[1,512]{1,0:T(2,128)(2,1)S(1)}, u32[]{:S(2)}, u32[]{:S(2)}) collective-permute-start(bf16[1,512]{1,0:T(2,128)(2,1)S(1)} %get-tuple-element.82), channel_id=1, source_target_pairs={{1,4},{2,5},{3,6},{9,12},{10,13},{11,14},{4,1},{5,2},{6,3},{12,9},... | collective-permute-start | bytes 3080 | tf_op jit(solution)/shard_map/ppermute | solution.py:444
  6.3 10.3 %collective-permute-start.2 = (bf16[1,512]{1,0:T(2,128)(2,1)S(1)}, bf16[1,512]{1,0:T(2,128)(2,1)S(1)}, u32[]{:S(2)}, u32[]{:S(2)}) collective-permute-start(bf16[1,512]{1,0:T(2,128)(2,1)S(1)} %get-tuple-element.83), channel_id=1, source_target_pairs={{4,9},{5,10},{6,11},{9,4},{10,5},{11,6},{20,25},{21,26},{22,27},{2... | collective-permute-start | bytes 3080 | tf_op jit(solution)/shard_map/ppermute | solution.py:444
  7.0 11.9 %collective-permute-start = (bf16[1,512]{1,0:T(2,128)(2,1)S(1)}, bf16[1,512]{1,0:T(2,128)(2,1)S(1)}, u32[]{:S(2)}, u32[]{:S(2)}) collective-permute-start(bf16[1,512]{1,0:T(2,128)(2,1)S(1)} %get-tuple-element.84), channel_id=1, source_target_pairs={{5,8},{6,9},{7,10},{8,5},{9,6},{10,7},{21,24},{22,25},{23,26},{24,... | collective-permute-start | bytes 3080 | tf_op jit(solution)/shard_map/ppermute | solution.py:444
  7.7 14.5 %collective-permute-start.5 = (bf16[32,512]{1,0:T(8,128)(2,1)S(1)}, bf16[32,512]{1,0:T(8,128)(2,1)S(1)}, u32[]{:S(2)}, u32[]{:S(2)}) collective-permute-start(bf16[32,512]{1,0:T(8,128)(2,1)S(1)} %get-tuple-element.79), channel_id=1, source_target_pairs={{0,4},{1,5},{2,6},{3,7},{8,12},{9,13},{10,14},{11,15},{4,0},{5,1},... | collective-permute-start | bytes 98312 | tf_op jit(solution)/shard_map/ppermute | solution.py:444
  15.9 6.3 %collective-permute-start.4 = (bf16[32,512]{1,0:T(8,128)(2,1)S(1)}, bf16[32,512]{1,0:T(8,128)(2,1)S(1)}, u32[]{:S(2)}, u32[]{:S(2)}) collective-permute-start(bf16[32,512]{1,0:T(8,128)(2,1)S(1)} %get-tuple-element.80), channel_id=1, source_target_pairs={{4,8},{5,9},{6,10},{7,11},{8,4},{9,5},{10,6},{11,7},{20,24},{21,25... | collective-permute-start | bytes 98312 | tf_op jit(solution)/shard_map/ppermute | solution.py:444
  16.6 5.5 %collective-permute-start.7 = (bf16[16,512]{1,0:T(8,128)(2,1)S(1)}, bf16[16,512]{1,0:T(8,128)(2,1)S(1)}, u32[]{:S(2)}, u32[]{:S(2)}) collective-permute-start(bf16[16,512]{1,0:T(8,128)(2,1)S(1)} %get-tuple-element.75), channel_id=1, source_target_pairs={{0,1},{2,3},{4,5},{6,7},{8,9},{10,11},{12,13},{14,15},{1,0},{3,2},... | collective-permute-start | bytes 49160 | tf_op jit(solution)/shard_map/ppermute | solution.py:444
  18.2 3.9 %collective-permute-start.6 = (bf16[16,512]{1,0:T(8,128)(2,1)S(1)}, bf16[16,512]{1,0:T(8,128)(2,1)S(1)}, u32[]{:S(2)}, u32[]{:S(2)}) collective-permute-start(bf16[16,512]{1,0:T(8,128)(2,1)S(1)} %get-tuple-element.76), channel_id=1, source_target_pairs={{1,2},{5,6},{9,10},{13,14},{2,1},{6,5},{10,9},{14,13},{17,18},{21,... | collective-permute-start | bytes 49160 | tf_op jit(solution)/shard_map/ppermute | solution.py:444
  28.1 6.5 %collective-permute-start.10 = (bf16[6,32,512]{2,1,0:T(8,128)(2,1)S(1)}, bf16[6,32,512]{2,1,0:T(8,128)(2,1)S(1)}, u32[]{:S(2)}, u32[]{:S(2)}) collective-permute-start(bf16[6,32,512]{2,1,0:T(8,128)(2,1)S(1)} %get-tuple-element.47), channel_id=1, source_target_pairs={{0,1},{1,0},{2,3},{3,2},{4,5},{5,4},{6,7},{7,6},{8,9},{9,8},{10,11... | collective-permute-start | bytes 589832 | tf_op jit(solution)/shard_map/ppermute | solution.py:514
  31.3 8.8 %collective-permute-start.8 = (bf16[2,32,512]{2,1,0:T(8,128)(2,1)S(1)}, bf16[2,32,512]{2,1,0:T(8,128)(2,1)S(1)}, u32[]{:S(2)}, u32[]{:S(2)}) collective-permute-start(bf16[2,32,512]{2,1,0:T(8,128)(2,1)S(1)} %get-tuple-element.44), channel_id=1, source_target_pairs={{0,14},{1,15},{2,12},{3,13},{4,10},{5,11},{6,8},{7,9},{8,6},{9,7},... | collective-permute-start | bytes 196616 | tf_op jit(solution)/shard_map/ppermute | solution.py:514
  33.8 9.8 %collective-permute-start.9 = (bf16[2,32,512]{2,1,0:T(8,128)(2,1)S(1)}, bf16[2,32,512]{2,1,0:T(8,128)(2,1)S(1)}, u32[]{:S(2)}, u32[]{:S(2)}) collective-permute-start(bf16[2,32,512]{2,1,0:T(8,128)(2,1)S(1)} %get-tuple-element.45), channel_id=1, source_target_pairs={{0,12},{1,13},{2,14},{3,15},{4,8},{5,9},{6,10},{7,11},{8,4},{9,5},... | collective-permute-start | bytes 196616 | tf_op jit(solution)/shard_map/ppermute | solution.py:514
  34.6 12.1 %collective-permute-start.11 = (bf16[2,32,512]{2,1,0:T(8,128)(2,1)S(1)}, bf16[2,32,512]{2,1,0:T(8,128)(2,1)S(1)}, u32[]{:S(2)}, u32[]{:S(2)}) collective-permute-start(bf16[2,32,512]{2,1,0:T(8,128)(2,1)S(1)} %get-tuple-element.48), channel_id=1, source_target_pairs={{0,10},{1,11},{2,8},{3,9},{4,14},{5,15},{6,12},{7,13},{8,2},{9,3},... | collective-permute-start | bytes 196616 | tf_op jit(solution)/shard_map/ppermute | solution.py:514
  37.1 9.8 %collective-permute-start.12 = (bf16[2,32,512]{2,1,0:T(8,128)(2,1)S(1)}, bf16[2,32,512]{2,1,0:T(8,128)(2,1)S(1)}, u32[]{:S(2)}, u32[]{:S(2)}) collective-permute-start(bf16[2,32,512]{2,1,0:T(8,128)(2,1)S(1)} %get-tuple-element.52), channel_id=1, source_target_pairs={{0,8},{1,9},{2,10},{3,11},{4,12},{5,13},{6,14},{7,15},{8,0},{9,1},... | collective-permute-start | bytes 196616 | tf_op jit(solution)/shard_map/ppermute | solution.py:514
  39.1 8.1 %collective-permute-start.13 = (bf16[2,32,512]{2,1,0:T(8,128)(2,1)S(1)}, bf16[2,32,512]{2,1,0:T(8,128)(2,1)S(1)}, u32[]{:S(2)}, u32[]{:S(2)}) collective-permute-start(bf16[2,32,512]{2,1,0:T(8,128)(2,1)S(1)} %get-tuple-element.53), channel_id=1, source_target_pairs={{0,6},{1,7},{2,4},{3,5},{4,2},{5,3},{6,0},{7,1},{8,14},{9,15},{10,... | collective-permute-start | bytes 196616 | tf_op jit(solution)/shard_map/ppermute | solution.py:514
  40.1 7.4 %collective-permute-start.14 = (bf16[2,32,512]{2,1,0:T(8,128)(2,1)S(1)}, bf16[2,32,512]{2,1,0:T(8,128)(2,1)S(1)}, u32[]{:S(2)}, u32[]{:S(2)}) collective-permute-start(bf16[2,32,512]{2,1,0:T(8,128)(2,1)S(1)} %get-tuple-element.54), channel_id=1, source_target_pairs={{0,4},{1,5},{2,6},{3,7},{4,0},{5,1},{6,2},{7,3},{8,12},{9,13},{10,... | collective-permute-start | bytes 196616 | tf_op jit(solution)/shard_map/ppermute | solution.py:514
  43.6 4.3 %collective-permute-start.15 = (bf16[2,32,512]{2,1,0:T(8,128)(2,1)S(1)}, bf16[2,32,512]{2,1,0:T(8,128)(2,1)S(1)}, u32[]{:S(2)}, u32[]{:S(2)}) collective-permute-start(bf16[2,32,512]{2,1,0:T(8,128)(2,1)S(1)} %get-tuple-element.55), channel_id=1, source_target_pairs={{0,2},{1,3},{2,0},{3,1},{4,6},{5,7},{6,4},{7,5},{8,10},{9,11},{10,... | collective-permute-start | bytes 196616 | tf_op jit(solution)/shard_map/ppermute | solution.py:514
  52.8 4.5 %collective-permute-start.20 = (bf16[6,32,512]{2,1,0:T(8,128)(2,1)S(1)}, bf16[6,32,512]{2,1,0:T(8,128)(2,1)S(1)}, u32[]{:S(2)}, u32[]{:S(2)}) collective-permute-start(bf16[6,32,512]{2,1,0:T(8,128)(2,1)S(1)} %get-tuple-element.60), channel_id=1, source_target_pairs={{0,1},{1,0},{2,3},{3,2},{4,5},{5,4},{6,7},{7,6},{8,9},{9,8},{10,11... | collective-permute-start | bytes 589832 | tf_op jit(solution)/shard_map/ppermute | solution.py:514
  53.1 7.8 %collective-permute-start.18 = (bf16[2,32,512]{2,1,0:T(8,128)(2,1)S(1)}, bf16[2,32,512]{2,1,0:T(8,128)(2,1)S(1)}, u32[]{:S(2)}, u32[]{:S(2)}) collective-permute-start(bf16[2,32,512]{2,1,0:T(8,128)(2,1)S(1)} %get-tuple-element.57), channel_id=1, source_target_pairs={{0,14},{1,15},{2,12},{3,13},{4,10},{5,11},{6,8},{7,9},{8,6},{9,7},... | collective-permute-start | bytes 196616 | tf_op jit(solution)/shard_map/ppermute | solution.py:514
  55.5 8.3 %collective-permute-start.19 = (bf16[2,32,512]{2,1,0:T(8,128)(2,1)S(1)}, bf16[2,32,512]{2,1,0:T(8,128)(2,1)S(1)}, u32[]{:S(2)}, u32[]{:S(2)}) collective-permute-start(bf16[2,32,512]{2,1,0:T(8,128)(2,1)S(1)} %get-tuple-element.58), channel_id=1, source_target_pairs={{0,12},{1,13},{2,14},{3,15},{4,8},{5,9},{6,10},{7,11},{8,4},{9,5},... | collective-permute-start | bytes 196616 | tf_op jit(solution)/shard_map/ppermute | solution.py:514
  57.3 10.3 %collective-permute-start.21 = (bf16[2,32,512]{2,1,0:T(8,128)(2,1)S(1)}, bf16[2,32,512]{2,1,0:T(8,128)(2,1)S(1)}, u32[]{:S(2)}, u32[]{:S(2)}) collective-permute-start(bf16[2,32,512]{2,1,0:T(8,128)(2,1)S(1)} %get-tuple-element.61), channel_id=1, source_target_pairs={{0,10},{1,11},{2,8},{3,9},{4,14},{5,15},{6,12},{7,13},{8,2},{9,3},... | collective-permute-start | bytes 196616 | tf_op jit(solution)/shard_map/ppermute | solution.py:514
  57.4 11.2 %collective-permute-start.22 = (bf16[2,32,512]{2,1,0:T(8,128)(2,1)S(1)}, bf16[2,32,512]{2,1,0:T(8,128)(2,1)S(1)}, u32[]{:S(2)}, u32[]{:S(2)}) collective-permute-start(bf16[2,32,512]{2,1,0:T(8,128)(2,1)S(1)} %get-tuple-element.65), channel_id=1, source_target_pairs={{0,8},{1,9},{2,10},{3,11},{4,12},{5,13},{6,14},{7,15},{8,0},{9,1},... | collective-permute-start | bytes 196616 | tf_op jit(solution)/shard_map/ppermute | solution.py:514
  60.8 7.8 %collective-permute-start.23 = (bf16[2,32,512]{2,1,0:T(8,128)(2,1)S(1)}, bf16[2,32,512]{2,1,0:T(8,128)(2,1)S(1)}, u32[]{:S(2)}, u32[]{:S(2)}) collective-permute-start(bf16[2,32,512]{2,1,0:T(8,128)(2,1)S(1)} %get-tuple-element.66), channel_id=1, source_target_pairs={{0,6},{1,7},{2,4},{3,5},{4,2},{5,3},{6,0},{7,1},{8,14},{9,15},{10,... | collective-permute-start | bytes 196616 | tf_op jit(solution)/shard_map/ppermute | solution.py:514
  60.9 8.1 %collective-permute-start.24 = (bf16[2,32,512]{2,1,0:T(8,128)(2,1)S(1)}, bf16[2,32,512]{2,1,0:T(8,128)(2,1)S(1)}, u32[]{:S(2)}, u32[]{:S(2)}) collective-permute-start(bf16[2,32,512]{2,1,0:T(8,128)(2,1)S(1)} %get-tuple-element.67), channel_id=1, source_target_pairs={{0,4},{1,5},{2,6},{3,7},{4,0},{5,1},{6,2},{7,3},{8,12},{9,13},{10,... | collective-permute-start | bytes 196616 | tf_op jit(solution)/shard_map/ppermute | solution.py:514
  63.8 5.2 %collective-permute-start.25 = (bf16[2,32,512]{2,1,0:T(8,128)(2,1)S(1)}, bf16[2,32,512]{2,1,0:T(8,128)(2,1)S(1)}, u32[]{:S(2)}, u32[]{:S(2)}) collective-permute-start(bf16[2,32,512]{2,1,0:T(8,128)(2,1)S(1)} %get-tuple-element.68), channel_id=1, source_target_pairs={{0,2},{1,3},{2,0},{3,1},{4,6},{5,7},{6,4},{7,5},{8,10},{9,11},{10,... | collective-permute-start | bytes 196616 | tf_op jit(solution)/shard_map/ppermute | solution.py:514
  (14 other events, 114.7 us)

commit v11 on v9

--- a/solution.py
+++ b/solution.py
@@ -70,7 +70,7 @@
         in_specs=[vmem()],
         out_specs=vmem(),
         out_shape=jax.ShapeDtypeStruct(inputs.shape, jnp.bfloat16),
-        compiler_params=pltpu.CompilerParams(vmem_limit_bytes=8 * MIB),
+        compiler_params=pltpu.CompilerParams(vmem_limit_bytes=2 * MIB),
         cost_estimate=pl.CostEstimate(
             flops=work, bytes_accessed=6 * inputs.size, transcendentals=inputs.shape[0]
         ),
@@ -113,7 +113,7 @@
         in_specs=[vmem()] * 2,
         out_specs=vmem(),
         out_shape=jax.ShapeDtypeStruct((width // LANES * padded_rows(tokens), LANES), jnp.float32),
-        compiler_params=pltpu.CompilerParams(vmem_limit_bytes=16 * MIB),
+        compiler_params=pltpu.CompilerParams(vmem_limit_bytes=4 * MIB),
         cost_estimate=pl.CostEstimate(
             flops=10**10,
             bytes_accessed=tokens * channels * 2 + channels * width * 2 + tokens * width * 4,
@@ -255,7 +255,7 @@
             halo,
             halo,
         ],
-        compiler_params=pltpu.CompilerParams(vmem_limit_bytes=16 * MIB),
+        compiler_params=pltpu.CompilerParams(vmem_limit_bytes=8 * MIB),
         cost_estimate=pl.CostEstimate(
             flops=2 * tokens * channels * width,
             bytes_accessed=tokens * channels * 10 + 4 * channels * width + tokens * width * 4,
@@ -373,7 +373,7 @@
             pltpu.VMEM((group_heads * count, count), jnp.float32),
             pltpu.VMEM((group_heads * count, count), jnp.float32),
         ],
-        compiler_params=pltpu.CompilerParams(vmem_limit_bytes=24 * MIB),
+        compiler_params=pltpu.CompilerParams(vmem_limit_bytes=10 * MIB),
         cost_estimate=pl.CostEstimate(
             flops=sets * (2 * count * channels * channels * 3 + 4 * count * count * channels),
             bytes_accessed=4 * sets * count * channels + 6 * channels * channels,
@@ -423,7 +423,7 @@
             pltpu.VMEM((tokens // step, step, channels), jnp.float32),
             pltpu.SemaphoreType.DMA((tokens // step,)),
         ],
-        compiler_params=pltpu.CompilerParams(vmem_limit_bytes=16 * MIB),
+        compiler_params=pltpu.CompilerParams(vmem_limit_bytes=6 * MIB),
         name="finish",
     )(own, *incoming, back, w_out, mixed)
 
@@ -499,7 +499,7 @@
         in_specs=[vmem()] * 2,
         out_specs=[vmem()] * early,
         out_shape=[jax.ShapeDtypeStruct((2, size, channels), own.dtype)] * early,
-        compiler_params=pltpu.CompilerParams(vmem_limit_bytes=8 * MIB),
+        compiler_params=pltpu.CompilerParams(vmem_limit_bytes=2 * MIB),
         name="join",
     )(own, swapped)
 
@@ -562,12 +562,12 @@
     edges = half_norm_of(jnp.concatenate([field[0], field[rows - 1]], axis=0), 10**10)
     up, down = exchange(edges[:cols], edges[cols:], "row")
     normed = half_norm_of(flat, 10**9)
+    expanded = expand(normed, w_expand)
+    up, down, normed, expanded = lax.optimization_barrier((up, down, normed, expanded))
     tile = normed.reshape(rows, cols, channels)
     spare = jnp.zeros((round_up(rows + 2, 16) - rows - 2, channels), jnp.bfloat16)
     first = jnp.concatenate([up[:1], tile[:, 0], down[:1], spare], axis=0)
     last = jnp.concatenate([up[cols - 1 :], tile[:, cols - 1], down[cols - 1 :], spare], axis=0)
-    normed, first, last = lax.optimization_barrier((normed, first, last))
-    expanded = expand(normed, w_expand)
     left, right = exchange(first, last, "col")
     pairwise = 8 <= devices <= 16 and devices & (devices - 1) == 0 and col_devices % 2 == 0
     if pairwise:

time: 61.4 us -> 68.7 us (1.12)
  local copies, waits for them, and re-layouts: 2.91 us -> 9.71 us
  starting transfers between devices: 35.3 us -> 37.3 us
  waiting for transfers between devices: 7.59 us -> 6.03 us
    unnamed x20 -> x22, local copies, waits for them, and re-layouts: 1.87 us -> 7.7 us
    ppermute x20, starting transfers between devices: 27.8 us -> 32.8 us  [swap(): lax.ppermute(slab, ('row', 'col'), [(i, i ^ mask) for i in range(devices)])]
    ppermute x4, starting transfers between devices: 7.57 us -> 4.47 us  [swap(): return lax.ppermute(edge, axis, pairs + [(b, a) for a, b in pairs])]
    ppermute x20, waiting for transfers between devices: 6.98 us -> 5.5 us  [swap(): lax.ppermute(slab, ('row', 'col'), [(i, i ^ mask) for i in range(devices)])]
    slice x2, local copies, waits for them, and re-layouts: 0.07 us -> 1.04 us  [shards(): first = jnp.concatenate([up[:1], tile[:, 0], down[:1], spare], axis=0)]
  transfers between devices with their start and end apart: 24 -> 24, of which waited for: 8 -> 6; matrix products, arithmetic and copies ran while one was open for 0% -> 0% of each run, Pallas kernels for 4% -> 4%
where the time goes in v11:
time: 68.7 us; the launch traced here: 68.4 us
  starting transfers between devices  37.3 us (54%)
  Pallas kernels  15 us (22%)
  local copies, waits for them, and re-layouts  9.71 us (14%)
  waiting for transfers between devices  6.03 us (9%)
    ppermute x20, starting transfers between devices, swap(): lax.ppermute(slab, ('row', 'col'), [(i, i ^ mask) for i in range(devices)])  32.8 us
    unnamed x22, local copies, waits for them, and re-layouts  7.7 us
    pallas_call x1, Pallas kernels, mix(): pl.pallas_call(functools.partial(mix_kernel, rows=rows, cols=cols, plan=p...  5.73 us
    ppermute x20, waiting for transfers between devices, swap(): lax.ppermute(slab, ('row', 'col'), [(i, i ^ mask) for i in range(devices)])  5.5 us
    pallas_call x1, Pallas kernels, attend(): pl.pallas_call(functools.partial(attend_kernel, plan=plan, sets=sets, cam...  4.58 us
    ppermute x4, starting transfers between devices, swap(): return lax.ppermute(edge, axis, pairs + [(b, a) for a, b in pairs])  4.47 us
    pallas_call x1, Pallas kernels, expand(): pl.pallas_call(expand_kernel, in_specs=[vmem()] * 2, out_specs=vmem(), ou...  2.16 us
    pallas_call x1, Pallas kernels, finish(): pl.pallas_call(functools.partial(finish_kernel, plan=plan), in_specs=[pl....  1.94 us
  transfers between devices with their start and end apart: 24, of which 6 were waited for; matrix products, arithmetic and copies ran while one was open for 0% of the time, Pallas kernels for 4%

profile of v11, /device:TPU:0, one launch (start us, length us, event | category | flops | bytes accessed | tf_op | source)
XLA Modules:
  0.0 68.4 jit_solution(16435889451531820205)
XLA Ops:
  1.1 3.1 %collective-permute-start.1 = (bf16[32,512]{1,0:T(8,128)(2,1)S(1)}, bf16[32,512]{1,0:T(8,128)(2,1)S(1)}, u32[]{:S(2)}, u32[]{:S(2)}) collective-permute-start(bf16[32,512]{1,0:T(8,128)(2,1)S(1)} %get-tuple-element.75), channel_id=1, source_target_pairs={{0,4},{8,12},{4,0},{12,8},{1,5},{9,13},{5,1},{13,9},{2,6},{10,14},... | collective-permute-start | bytes 98312 | tf_op jit(solution)/shard_map/ppermute | solution.py:437
  5.2 2.2 %expand.1.expanded_ref = f32[8448,128]{1,0:T(8,128)S(1)} custom-call(bf16[512,512]{1,0:T(8,128)(2,1)S(1)} %half_norm.3.normed_ref, bf16[512,2048]{1,0:T(8,128)(2,1)S(1)} %copy-done.2), custom_call_target="tpu_custom_call" | custom-call | flops 10000000000 | bytes 6815744 | tf_op jit(solution)/shard_map/expand/pallas_call | solution.py:111
  7.4 2.0 %copy-done = f32[8448,128]{1,0:T(8,128)} copy-done((f32[8448,128]{1,0:T(8,128)}, f32[8448,128]{1,0:T(8,128)S(1)}, u32[]{:S(2)}) %copy-start) | copy-done | bytes 4325400
  12.8 2.2 %copy-done.1 = f32[8448,128]{1,0:T(8,128)S(1)} copy-done((f32[8448,128]{1,0:T(8,128)S(1)}, f32[8448,128]{1,0:T(8,128)}, u32[]{:S(2)}) %copy-start.1) | copy-done | bytes 4325400
  15.0 1.6 %copy-done.3 = bf16[2048,512]{1,0:T(8,128)(2,1)S(1)} copy-done((bf16[2048,512]{1,0:T(8,128)(2,1)S(1)}, bf16[2048,512]{1,0:T(8,128)(2,1)}, u32[]{:S(2)}) %copy-start.3) | copy-done | bytes 2097176
  16.6 1.0 %copy-done.7 = bf16[512,512]{1,0:T(8,128)(2,1)S(1)} copy-done((bf16[512,512]{1,0:T(8,128)(2,1)S(1)}, bf16[512,512]{1,0:T(8,128)(2,1)}, u32[]{:S(2)}) %copy-start.7) | copy-done | bytes 524312
  17.7 5.7 %mix.1 = (f32[512,512]{1,0:T(8,128)S(1)}, bf16[2,32,512]{2,1,0:T(8,128)(2,1)S(1)}, bf16[2,32,512]{2,1,0:T(8,128)(2,1)S(1)}, bf16[1,32,512]{2,1,0:T(8,128)(2,1)S(...) custom-call(s32[1]{0:T(128)} %bitcast.own_ref, f32[8448,128]{1,0:T(8,128)S(1)} %copy-done.1, ...), custom_call_target="tpu_custom_call" | custom-call | flops 1073741824 | bytes 11010048 | tf_op jit(solution)/shard_map/mix/pallas_call | solution.py:243
  23.4 4.6 %collective-permute-start.6 = (bf16[6,32,512]{2,1,0:T(8,128)(2,1)S(1)}, bf16[6,32,512]{2,1,0:T(8,128)(2,1)S(1)}, u32[]{:S(2)}, u32[]{:S(2)}) collective-permute-start(bf16[6,32,512]{2,1,0:T(8,128)(2,1)S(1)} %get-tuple-element.43), channel_id=1, source_target_pairs={{0,1},{1,0},{2,3},{3,2},{4,5},{5,4},{6,7},{7,6},{8,9},{9,8},{10,11... | collective-permute-start | bytes 589832 | tf_op jit(solution)/shard_map/ppermute | solution.py:512
  28.0 3.2 %collective-permute-start.4 = (bf16[2,32,512]{2,1,0:T(8,128)(2,1)S(1)}, bf16[2,32,512]{2,1,0:T(8,128)(2,1)S(1)}, u32[]{:S(2)}, u32[]{:S(2)}) collective-permute-start(bf16[2,32,512]{2,1,0:T(8,128)(2,1)S(1)} %get-tuple-element.40), channel_id=1, source_target_pairs={{0,14},{1,15},{2,12},{3,13},{4,10},{5,11},{6,8},{7,9},{8,6},{9,7},... | collective-permute-start | bytes 196616 | tf_op jit(solution)/shard_map/ppermute | solution.py:512
  31.2 1.2 %collective-permute-start.5 = (bf16[2,32,512]{2,1,0:T(8,128)(2,1)S(1)}, bf16[2,32,512]{2,1,0:T(8,128)(2,1)S(1)}, u32[]{:S(2)}, u32[]{:S(2)}) collective-permute-start(bf16[2,32,512]{2,1,0:T(8,128)(2,1)S(1)} %get-tuple-element.41), channel_id=1, source_target_pairs={{0,12},{1,13},{2,14},{3,15},{4,8},{5,9},{6,10},{7,11},{8,4},{9,5},... | collective-permute-start | bytes 196616 | tf_op jit(solution)/shard_map/ppermute | solution.py:512
  32.4 2.5 %collective-permute-start.7 = (bf16[2,32,512]{2,1,0:T(8,128)(2,1)S(1)}, bf16[2,32,512]{2,1,0:T(8,128)(2,1)S(1)}, u32[]{:S(2)}, u32[]{:S(2)}) collective-permute-start(bf16[2,32,512]{2,1,0:T(8,128)(2,1)S(1)} %get-tuple-element.44), channel_id=1, source_target_pairs={{0,10},{1,11},{2,8},{3,9},{4,14},{5,15},{6,12},{7,13},{8,2},{9,3},... | collective-permute-start | bytes 196616 | tf_op jit(solution)/shard_map/ppermute | solution.py:512
  34.9 1.7 %collective-permute-start.8 = (bf16[2,32,512]{2,1,0:T(8,128)(2,1)S(1)}, bf16[2,32,512]{2,1,0:T(8,128)(2,1)S(1)}, u32[]{:S(2)}, u32[]{:S(2)}) collective-permute-start(bf16[2,32,512]{2,1,0:T(8,128)(2,1)S(1)} %get-tuple-element.47), channel_id=1, source_target_pairs={{0,6},{1,7},{2,4},{3,5},{4,2},{5,3},{6,0},{7,1},{8,14},{9,15},{10,... | collective-permute-start | bytes 196616 | tf_op jit(solution)/shard_map/ppermute | solution.py:512
  37.4 3.5 %collective-permute-start.10 = (bf16[2,32,512]{2,1,0:T(8,128)(2,1)S(1)}, bf16[2,32,512]{2,1,0:T(8,128)(2,1)S(1)}, u32[]{:S(2)}, u32[]{:S(2)}) collective-permute-start(bf16[2,32,512]{2,1,0:T(8,128)(2,1)S(1)} %get-tuple-element.50), channel_id=1, source_target_pairs={{0,8},{1,9},{2,10},{3,11},{4,12},{5,13},{6,14},{7,15},{8,0},{9,1},... | collective-permute-start | bytes 196616 | tf_op jit(solution)/shard_map/ppermute | solution.py:512
  40.9 2.6 %collective-permute-start.11 = (bf16[2,32,512]{2,1,0:T(8,128)(2,1)S(1)}, bf16[2,32,512]{2,1,0:T(8,128)(2,1)S(1)}, u32[]{:S(2)}, u32[]{:S(2)}) collective-permute-start(bf16[2,32,512]{2,1,0:T(8,128)(2,1)S(1)} %get-tuple-element.51), channel_id=1, source_target_pairs={{0,2},{1,3},{2,0},{3,1},{4,6},{5,7},{6,4},{7,5},{8,10},{9,11},{10,... | collective-permute-start | bytes 196616 | tf_op jit(solution)/shard_map/ppermute | solution.py:512
  44.0 1.3 %collective-permute-done.10.refs_5_ = bf16[2,32,512]{2,1,0:T(8,128)(2,1)S(1)} collective-permute-done((bf16[2,32,512]{2,1,0:T(8,128)(2,1)S(1)}, bf16[2,32,512]{2,1,0:T(8,128)(2,1)S(1)}, u32[]{:S(2)}, u32[]{:S(2)}) %collective-permute-start.10) | collective-permute-done | bytes 65568 | tf_op jit(solution)/shard_map/ppermute | solution.py:512
  45.7 4.6 %attend.1 = (bf16[2,32,512]{2,1,0:T(8,128)(2,1)S(1)}, bf16[2,32,512]{2,1,0:T(8,128)(2,1)S(1)}, bf16[1,32,512]{2,1,0:T(8,128)(2,1)S(1)}, bf16[6,32,512]{2,1,0:T(8,128)(2,1)S(1)}, bf16[5,32,512]{2,1,0:T(8,128)(2,1)S(1)}) custom-call(bf16[2,32,512]{2,1,0:T(8,128)(2,1)S(1)} %collective-permute-done.4.refs_0_, ...), custom_call_target="tpu_custom_call" | custom-call | flops 1073741824 | bytes 2621440 | tf_op jit(solution)/shard_map/attend/pallas_call | solution.py:363
  50.4 2.7 %collective-permute-start.14 = (bf16[2,32,512]{2,1,0:T(8,128)(2,1)S(1)}, bf16[2,32,512]{2,1,0:T(8,128)(2,1)S(1)}, u32[]{:S(2)}, u32[]{:S(2)}) collective-permute-start(bf16[2,32,512]{2,1,0:T(8,128)(2,1)S(1)} %get-tuple-element.53), channel_id=1, source_target_pairs={{0,14},{1,15},{2,12},{3,13},{4,10},{5,11},{6,8},{7,9},{8,6},{9,7},... | collective-permute-start | bytes 196616 | tf_op jit(solution)/shard_map/ppermute | solution.py:512
  53.1 2.6 %collective-permute-start.15 = (bf16[2,32,512]{2,1,0:T(8,128)(2,1)S(1)}, bf16[2,32,512]{2,1,0:T(8,128)(2,1)S(1)}, u32[]{:S(2)}, u32[]{:S(2)}) collective-permute-start(bf16[2,32,512]{2,1,0:T(8,128)(2,1)S(1)} %get-tuple-element.54), channel_id=1, source_target_pairs={{0,12},{1,13},{2,14},{3,15},{4,8},{5,9},{6,10},{7,11},{8,4},{9,5},... | collective-permute-start | bytes 196616 | tf_op jit(solution)/shard_map/ppermute | solution.py:512
  55.9 2.6 %collective-permute-start.18 = (bf16[2,32,512]{2,1,0:T(8,128)(2,1)S(1)}, bf16[2,32,512]{2,1,0:T(8,128)(2,1)S(1)}, u32[]{:S(2)}, u32[]{:S(2)}) collective-permute-start(bf16[2,32,512]{2,1,0:T(8,128)(2,1)S(1)} %get-tuple-element.60), channel_id=1, source_target_pairs={{0,6},{1,7},{2,4},{3,5},{4,2},{5,3},{6,0},{7,1},{8,14},{9,15},{10,... | collective-permute-start | bytes 196616 | tf_op jit(solution)/shard_map/ppermute | solution.py:512
  58.5 3.7 %collective-permute-start.20 = (bf16[2,32,512]{2,1,0:T(8,128)(2,1)S(1)}, bf16[2,32,512]{2,1,0:T(8,128)(2,1)S(1)}, u32[]{:S(2)}, u32[]{:S(2)}) collective-permute-start(bf16[2,32,512]{2,1,0:T(8,128)(2,1)S(1)} %get-tuple-element.63), channel_id=1, source_target_pairs={{0,8},{1,9},{2,10},{3,11},{4,12},{5,13},{6,14},{7,15},{8,0},{9,1},... | collective-permute-start | bytes 196616 | tf_op jit(solution)/shard_map/ppermute | solution.py:512
  62.2 1.5 %collective-permute-done.17.refs_3_ = bf16[2,32,512]{2,1,0:T(8,128)(2,1)S(1)} collective-permute-done((bf16[2,32,512]{2,1,0:T(8,128)(2,1)S(1)}, bf16[2,32,512]{2,1,0:T(8,128)(2,1)S(1)}, u32[]{:S(2)}, u32[]{:S(2)}) %collective-permute-start.17) | collective-permute-done | bytes 65568 | tf_op jit(solution)/shard_map/ppermute | solution.py:512
  64.2 1.1 %collective-permute-done.19.refs_4_ = bf16[2,32,512]{2,1,0:T(8,128)(2,1)S(1)} collective-permute-done((bf16[2,32,512]{2,1,0:T(8,128)(2,1)S(1)}, bf16[2,32,512]{2,1,0:T(8,128)(2,1)S(1)}, u32[]{:S(2)}, u32[]{:S(2)}) %collective-permute-start.19) | collective-permute-done | bytes 65568 | tf_op jit(solution)/shard_map/ppermute | solution.py:512
  65.3 1.1 %collective-permute-done.21.refs_6_ = bf16[2,32,512]{2,1,0:T(8,128)(2,1)S(1)} collective-permute-done((bf16[2,32,512]{2,1,0:T(8,128)(2,1)S(1)}, bf16[2,32,512]{2,1,0:T(8,128)(2,1)S(1)}, u32[]{:S(2)}, u32[]{:S(2)}) %collective-permute-start.21) | collective-permute-done | bytes 65568 | tf_op jit(solution)/shard_map/ppermute | solution.py:512
  66.5 1.9 %finish.1 = f32[512,512]{1,0:T(8,128)} custom-call(s32[1]{0:T(128)} %bitcast.own_ref, bf16[2,32,512]{2,1,0:T(8,128)(2,1)S(1)} %collective-permute-done.14.refs_0_, bf16[2,32,512]{2,1,0:T(8,128)(2,1)S(1)} %collective-permute-done.15.refs_1_, bf16[2,32,512]{2,1,0:T(8,128)(2,1)S(1)} %collective-permute-done.18.refs_2_, ...), custom_call_target="tpu_custom_call" | custom-call | tf_op jit(solution)/shard_map/finish/pallas_call | solution.py:416
  (65 shorter events, 7.9 us)
Async XLA Ops:
  1.1 9.2 %collective-permute-start.1 = (bf16[32,512]{1,0:T(8,128)(2,1)S(1)}, bf16[32,512]{1,0:T(8,128)(2,1)S(1)}, u32[]{:S(2)}, u32[]{:S(2)}) collective-permute-start(bf16[32,512]{1,0:T(8,128)(2,1)S(1)} %get-tuple-element.75), channel_id=1, source_target_pairs={{0,4},{8,12},{4,0},{12,8},{1,5},{9,13},{5,1},{13,9},{2,6},{10,14},... | collective-permute-start | bytes 98312 | tf_op jit(solution)/shard_map/ppermute | solution.py:437
  4.2 6.1 %collective-permute-start = (bf16[32,512]{1,0:T(8,128)(2,1)S(1)}, bf16[32,512]{1,0:T(8,128)(2,1)S(1)}, u32[]{:S(2)}, u32[]{:S(2)}) collective-permute-start(bf16[32,512]{1,0:T(8,128)(2,1)S(1)} %get-tuple-element.76), channel_id=1, source_target_pairs={{4,8},{8,4},{5,9},{9,5},{6,10},{10,6},{7,11},{11,7},{20,24},{24,20... | collective-permute-start | bytes 98312 | tf_op jit(solution)/shard_map/ppermute | solution.py:437
  11.5 1.3 %collective-permute-start.3 = (bf16[32,512]{1,0:T(8,128)(2,1)S(1)}, bf16[32,512]{1,0:T(8,128)(2,1)S(1)}, u32[]{:S(2)}, u32[]{:S(2)}) collective-permute-start(bf16[32,512]{1,0:T(8,128)(2,1)S(1)} %get-tuple-element.77), channel_id=1, source_target_pairs={{0,1},{2,3},{1,0},{3,2},{4,5},{6,7},{5,4},{7,6},{8,9},{10,11},{9,8... | collective-permute-start | bytes 98312 | tf_op jit(solution)/shard_map/ppermute | solution.py:437
  11.6 1.2 %collective-permute-start.2 = (bf16[32,512]{1,0:T(8,128)(2,1)S(1)}, bf16[32,512]{1,0:T(8,128)(2,1)S(1)}, u32[]{:S(2)}, u32[]{:S(2)}) collective-permute-start(bf16[32,512]{1,0:T(8,128)(2,1)S(1)} %get-tuple-element.78), channel_id=1, source_target_pairs={{1,2},{2,1},{5,6},{6,5},{9,10},{10,9},{13,14},{14,13},{17,18},{18,... | collective-permute-start | bytes 98312 | tf_op jit(solution)/shard_map/ppermute | solution.py:437
  23.4 9.0 %collective-permute-start.6 = (bf16[6,32,512]{2,1,0:T(8,128)(2,1)S(1)}, bf16[6,32,512]{2,1,0:T(8,128)(2,1)S(1)}, u32[]{:S(2)}, u32[]{:S(2)}) collective-permute-start(bf16[6,32,512]{2,1,0:T(8,128)(2,1)S(1)} %get-tuple-element.43), channel_id=1, source_target_pairs={{0,1},{1,0},{2,3},{3,2},{4,5},{5,4},{6,7},{7,6},{8,9},{9,8},{10,11... | collective-permute-start | bytes 589832 | tf_op jit(solution)/shard_map/ppermute | solution.py:512
  28.0 9.5 %collective-permute-start.4 = (bf16[2,32,512]{2,1,0:T(8,128)(2,1)S(1)}, bf16[2,32,512]{2,1,0:T(8,128)(2,1)S(1)}, u32[]{:S(2)}, u32[]{:S(2)}) collective-permute-start(bf16[2,32,512]{2,1,0:T(8,128)(2,1)S(1)} %get-tuple-element.40), channel_id=1, source_target_pairs={{0,14},{1,15},{2,12},{3,13},{4,10},{5,11},{6,8},{7,9},{8,6},{9,7},... | collective-permute-start | bytes 196616 | tf_op jit(solution)/shard_map/ppermute | solution.py:512
  31.2 9.7 %collective-permute-start.5 = (bf16[2,32,512]{2,1,0:T(8,128)(2,1)S(1)}, bf16[2,32,512]{2,1,0:T(8,128)(2,1)S(1)}, u32[]{:S(2)}, u32[]{:S(2)}) collective-permute-start(bf16[2,32,512]{2,1,0:T(8,128)(2,1)S(1)} %get-tuple-element.41), channel_id=1, source_target_pairs={{0,12},{1,13},{2,14},{3,15},{4,8},{5,9},{6,10},{7,11},{8,4},{9,5},... | collective-permute-start | bytes 196616 | tf_op jit(solution)/shard_map/ppermute | solution.py:512
  32.4 11.1 %collective-permute-start.7 = (bf16[2,32,512]{2,1,0:T(8,128)(2,1)S(1)}, bf16[2,32,512]{2,1,0:T(8,128)(2,1)S(1)}, u32[]{:S(2)}, u32[]{:S(2)}) collective-permute-start(bf16[2,32,512]{2,1,0:T(8,128)(2,1)S(1)} %get-tuple-element.44), channel_id=1, source_target_pairs={{0,10},{1,11},{2,8},{3,9},{4,14},{5,15},{6,12},{7,13},{8,2},{9,3},... | collective-permute-start | bytes 196616 | tf_op jit(solution)/shard_map/ppermute | solution.py:512
  34.9 8.6 %collective-permute-start.8 = (bf16[2,32,512]{2,1,0:T(8,128)(2,1)S(1)}, bf16[2,32,512]{2,1,0:T(8,128)(2,1)S(1)}, u32[]{:S(2)}, u32[]{:S(2)}) collective-permute-start(bf16[2,32,512]{2,1,0:T(8,128)(2,1)S(1)} %get-tuple-element.47), channel_id=1, source_target_pairs={{0,6},{1,7},{2,4},{3,5},{4,2},{5,3},{6,0},{7,1},{8,14},{9,15},{10,... | collective-permute-start | bytes 196616 | tf_op jit(solution)/shard_map/ppermute | solution.py:512
  36.6 7.4 %collective-permute-start.9 = (bf16[2,32,512]{2,1,0:T(8,128)(2,1)S(1)}, bf16[2,32,512]{2,1,0:T(8,128)(2,1)S(1)}, u32[]{:S(2)}, u32[]{:S(2)}) collective-permute-start(bf16[2,32,512]{2,1,0:T(8,128)(2,1)S(1)} %get-tuple-element.49), channel_id=1, source_target_pairs={{0,4},{1,5},{2,6},{3,7},{4,0},{5,1},{6,2},{7,3},{8,12},{9,13},{10,... | collective-permute-start | bytes 196616 | tf_op jit(solution)/shard_map/ppermute | solution.py:512
  37.4 7.8 %collective-permute-start.10 = (bf16[2,32,512]{2,1,0:T(8,128)(2,1)S(1)}, bf16[2,32,512]{2,1,0:T(8,128)(2,1)S(1)}, u32[]{:S(2)}, u32[]{:S(2)}) collective-permute-start(bf16[2,32,512]{2,1,0:T(8,128)(2,1)S(1)} %get-tuple-element.50), channel_id=1, source_target_pairs={{0,8},{1,9},{2,10},{3,11},{4,12},{5,13},{6,14},{7,15},{8,0},{9,1},... | collective-permute-start | bytes 196616 | tf_op jit(solution)/shard_map/ppermute | solution.py:512
  40.9 4.8 %collective-permute-start.11 = (bf16[2,32,512]{2,1,0:T(8,128)(2,1)S(1)}, bf16[2,32,512]{2,1,0:T(8,128)(2,1)S(1)}, u32[]{:S(2)}, u32[]{:S(2)}) collective-permute-start(bf16[2,32,512]{2,1,0:T(8,128)(2,1)S(1)} %get-tuple-element.51), channel_id=1, source_target_pairs={{0,2},{1,3},{2,0},{3,1},{4,6},{5,7},{6,4},{7,5},{8,10},{9,11},{10,... | collective-permute-start | bytes 196616 | tf_op jit(solution)/shard_map/ppermute | solution.py:512
  43.5 2.2 %collective-permute-start.12 = (bf16[2,32,512]{2,1,0:T(8,128)(2,1)S(1)}, bf16[2,32,512]{2,1,0:T(8,128)(2,1)S(1)}, u32[]{:S(2)}, u32[]{:S(2)}) collective-permute-start(bf16[2,32,512]{2,1,0:T(8,128)(2,1)S(1)} %collective-permute-done.4.refs_0_), channel_id=1, source_target_pairs={{0,1},{1,0},{2,3},{3,2},{4,5},{5,4},{6,7},{7,6},{8,9},{9,8},{10,11... | collective-permute-start | bytes 196616 | tf_op jit(solution)/shard_map/ppermute | solution.py:512
  43.5 2.2 %collective-permute-start.13 = (bf16[2,32,512]{2,1,0:T(8,128)(2,1)S(1)}, bf16[2,32,512]{2,1,0:T(8,128)(2,1)S(1)}, u32[]{:S(2)}, u32[]{:S(2)}) collective-permute-start(bf16[2,32,512]{2,1,0:T(8,128)(2,1)S(1)} %collective-permute-done.5.refs_1_), channel_id=1, source_target_pairs={{0,1},{1,0},{2,3},{3,2},{4,5},{5,4},{6,7},{7,6},{8,9},{9,8},{10,11... | collective-permute-start | bytes 196616 | tf_op jit(solution)/shard_map/ppermute | solution.py:512
  50.3 5.4 %collective-permute-start.16 = (bf16[6,32,512]{2,1,0:T(8,128)(2,1)S(1)}, bf16[6,32,512]{2,1,0:T(8,128)(2,1)S(1)}, u32[]{:S(2)}, u32[]{:S(2)}) collective-permute-start(bf16[6,32,512]{2,1,0:T(8,128)(2,1)S(1)} %get-tuple-element.56), channel_id=1, source_target_pairs={{0,1},{1,0},{2,3},{3,2},{4,5},{5,4},{6,7},{7,6},{8,9},{9,8},{10,11... | collective-permute-start | bytes 589832 | tf_op jit(solution)/shard_map/ppermute | solution.py:512
  50.4 8.1 %collective-permute-start.14 = (bf16[2,32,512]{2,1,0:T(8,128)(2,1)S(1)}, bf16[2,32,512]{2,1,0:T(8,128)(2,1)S(1)}, u32[]{:S(2)}, u32[]{:S(2)}) collective-permute-start(bf16[2,32,512]{2,1,0:T(8,128)(2,1)S(1)} %get-tuple-element.53), channel_id=1, source_target_pairs={{0,14},{1,15},{2,12},{3,13},{4,10},{5,11},{6,8},{7,9},{8,6},{9,7},... | collective-permute-start | bytes 196616 | tf_op jit(solution)/shard_map/ppermute | solution.py:512
  53.1 9.1 %collective-permute-start.15 = (bf16[2,32,512]{2,1,0:T(8,128)(2,1)S(1)}, bf16[2,32,512]{2,1,0:T(8,128)(2,1)S(1)}, u32[]{:S(2)}, u32[]{:S(2)}) collective-permute-start(bf16[2,32,512]{2,1,0:T(8,128)(2,1)S(1)} %get-tuple-element.54), channel_id=1, source_target_pairs={{0,12},{1,13},{2,14},{3,15},{4,8},{5,9},{6,10},{7,11},{8,4},{9,5},... | collective-permute-start | bytes 196616 | tf_op jit(solution)/shard_map/ppermute | solution.py:512
  55.8 7.9 %collective-permute-start.17 = (bf16[2,32,512]{2,1,0:T(8,128)(2,1)S(1)}, bf16[2,32,512]{2,1,0:T(8,128)(2,1)S(1)}, u32[]{:S(2)}, u32[]{:S(2)}) collective-permute-start(bf16[2,32,512]{2,1,0:T(8,128)(2,1)S(1)} %get-tuple-element.57), channel_id=1, source_target_pairs={{0,10},{1,11},{2,8},{3,9},{4,14},{5,15},{6,12},{7,13},{8,2},{9,3},... | collective-permute-start | bytes 196616 | tf_op jit(solution)/shard_map/ppermute | solution.py:512
  55.9 7.8 %collective-permute-start.18 = (bf16[2,32,512]{2,1,0:T(8,128)(2,1)S(1)}, bf16[2,32,512]{2,1,0:T(8,128)(2,1)S(1)}, u32[]{:S(2)}, u32[]{:S(2)}) collective-permute-start(bf16[2,32,512]{2,1,0:T(8,128)(2,1)S(1)} %get-tuple-element.60), channel_id=1, source_target_pairs={{0,6},{1,7},{2,4},{3,5},{4,2},{5,3},{6,0},{7,1},{8,14},{9,15},{10,... | collective-permute-start | bytes 196616 | tf_op jit(solution)/shard_map/ppermute | solution.py:512
  58.5 6.8 %collective-permute-start.19 = (bf16[2,32,512]{2,1,0:T(8,128)(2,1)S(1)}, bf16[2,32,512]{2,1,0:T(8,128)(2,1)S(1)}, u32[]{:S(2)}, u32[]{:S(2)}) collective-permute-start(bf16[2,32,512]{2,1,0:T(8,128)(2,1)S(1)} %get-tuple-element.62), channel_id=1, source_target_pairs={{0,4},{1,5},{2,6},{3,7},{4,0},{5,1},{6,2},{7,3},{8,12},{9,13},{10,... | collective-permute-start | bytes 196616 | tf_op jit(solution)/shard_map/ppermute | solution.py:512
  58.5 6.8 %collective-permute-start.20 = (bf16[2,32,512]{2,1,0:T(8,128)(2,1)S(1)}, bf16[2,32,512]{2,1,0:T(8,128)(2,1)S(1)}, u32[]{:S(2)}, u32[]{:S(2)}) collective-permute-start(bf16[2,32,512]{2,1,0:T(8,128)(2,1)S(1)} %get-tuple-element.63), channel_id=1, source_target_pairs={{0,8},{1,9},{2,10},{3,11},{4,12},{5,13},{6,14},{7,15},{8,0},{9,1},... | collective-permute-start | bytes 196616 | tf_op jit(solution)/shard_map/ppermute | solution.py:512
  62.2 4.3 %collective-permute-start.21 = (bf16[2,32,512]{2,1,0:T(8,128)(2,1)S(1)}, bf16[2,32,512]{2,1,0:T(8,128)(2,1)S(1)}, u32[]{:S(2)}, u32[]{:S(2)}) collective-permute-start(bf16[2,32,512]{2,1,0:T(8,128)(2,1)S(1)} %get-tuple-element.64), channel_id=1, source_target_pairs={{0,2},{1,3},{2,0},{3,1},{4,6},{5,7},{6,4},{7,5},{8,10},{9,11},{10,... | collective-permute-start | bytes 196616 | tf_op jit(solution)/shard_map/ppermute | solution.py:512
  63.7 2.8 %collective-permute-start.22 = (bf16[2,32,512]{2,1,0:T(8,128)(2,1)S(1)}, bf16[2,32,512]{2,1,0:T(8,128)(2,1)S(1)}, u32[]{:S(2)}, u32[]{:S(2)}) collective-permute-start(bf16[2,32,512]{2,1,0:T(8,128)(2,1)S(1)} %collective-permute-done.14.refs_0_), channel_id=1, source_target_pairs={{0,1},{1,0},{2,3},{3,2},{4,5},{5,4},{6,7},{7,6},{8,9},{9,8},{10,11... | collective-permute-start | bytes 196616 | tf_op jit(solution)/shard_map/ppermute | solution.py:512
  63.7 2.8 %collective-permute-start.23 = (bf16[2,32,512]{2,1,0:T(8,128)(2,1)S(1)}, bf16[2,32,512]{2,1,0:T(8,128)(2,1)S(1)}, u32[]{:S(2)}, u32[]{:S(2)}) collective-permute-start(bf16[2,32,512]{2,1,0:T(8,128)(2,1)S(1)} %collective-permute-done.15.refs_1_), channel_id=1, source_target_pairs={{0,1},{1,0},{2,3},{3,2},{4,5},{5,4},{6,7},{7,6},{8,9},{9,8},{10,11... | collective-permute-start | bytes 196616 | tf_op jit(solution)/shard_map/ppermute | solution.py:512
  (11 other events, 92.9 us)

commit v12 on v11

--- a/solution.py
+++ b/solution.py
@@ -67,10 +67,10 @@
 def half_norm_of(inputs, work):
     return pl.pallas_call(
         half_norm_kernel,
-        in_specs=[vmem()],
-        out_specs=vmem(),
+        in_specs=[pl.BlockSpec(inputs.shape, lambda: (0, 0))],
+        out_specs=pl.BlockSpec(inputs.shape, lambda: (0, 0)),
         out_shape=jax.ShapeDtypeStruct(inputs.shape, jnp.bfloat16),
-        compiler_params=pltpu.CompilerParams(vmem_limit_bytes=2 * MIB),
+        compiler_params=pltpu.CompilerParams(vmem_limit_bytes=8 * MIB),
         cost_estimate=pl.CostEstimate(
             flops=work, bytes_accessed=6 * inputs.size, transcendentals=inputs.shape[0]
         ),
@@ -84,36 +84,30 @@
 
 def expand_kernel(normed_ref, weight_ref, out_ref):
     tokens = normed_ref.shape[0]
-    width = weight_ref.shape[1]
-    tile = divisor(width, 512, LANES)
+    tile = weight_ref.shape[1]
     step = divisor(tokens, 128, 16)
-    starts = range(0, tokens, step)
-
-    def body(index, carry):
-        lanes = pl.ds(pl.multiple_of(index * tile, tile), tile)
-        for start in starts:
-            made = gelu_of_half(
-                matmul(normed_ref[start : start + step, :], weight_ref[:, lanes])
-            )
-            for sub in range(tile // LANES):
-                row = (index * (tile // LANES) + sub) * padded_rows(tokens) + 8 + start
-                out_ref[pl.ds(pl.multiple_of(row, 8), step), :] = made[
-                    :, sub * LANES : (sub + 1) * LANES
-                ]
-        return carry
-
-    lax.fori_loop(0, width // tile, body, 0)
+    for start in range(0, tokens, step):
+        made = gelu_of_half(matmul(normed_ref[start : start + step, :], weight_ref[...]))
+        for sub in range(tile // LANES):
+            row = sub * padded_rows(tokens) + 8 + start
+            out_ref[row : row + step, :] = made[:, sub * LANES : (sub + 1) * LANES]
 
 
 def expand(normed, w_expand):
     tokens, channels = normed.shape
     width = w_expand.shape[1]
+    tile = divisor(width, 512, LANES)
+    block = tile // LANES * padded_rows(tokens)
     return pl.pallas_call(
         expand_kernel,
-        in_specs=[vmem()] * 2,
-        out_specs=vmem(),
+        grid=(width // tile,),
+        in_specs=[
+            pl.BlockSpec((tokens, channels), lambda j: (0, 0)),
+            pl.BlockSpec((channels, tile), lambda j: (0, j)),
+        ],
+        out_specs=pl.BlockSpec((block, LANES), lambda j: (j, 0)),
         out_shape=jax.ShapeDtypeStruct((width // LANES * padded_rows(tokens), LANES), jnp.float32),
-        compiler_params=pltpu.CompilerParams(vmem_limit_bytes=4 * MIB),
+        compiler_params=pltpu.CompilerParams(vmem_limit_bytes=12 * MIB),
         cost_estimate=pl.CostEstimate(
             flops=10**10,
             bytes_accessed=tokens * channels * 2 + channels * width * 2 + tokens * width * 4,

time: 68.7 us -> 68.7 us (level)
  no operation moved by 1% of the time
where the time goes in v12:
time: 68.7 us; the launch traced here: 68.4 us
  starting transfers between devices  37.3 us (54%)
  Pallas kernels  15 us (22%)
  local copies, waits for them, and re-layouts  9.71 us (14%)
  waiting for transfers between devices  6.03 us (9%)
    ppermute x20, starting transfers between devices, swap(): lax.ppermute(slab, ('row', 'col'), [(i, i ^ mask) for i in range(devices)])  32.8 us
    unnamed x22, local copies, waits for them, and re-layouts  7.7 us
    pallas_call x1, Pallas kernels, mix(): pl.pallas_call(functools.partial(mix_kernel, rows=rows, cols=cols, plan=p...  5.73 us
    ppermute x20, waiting for transfers between devices, swap(): lax.ppermute(slab, ('row', 'col'), [(i, i ^ mask) for i in range(devices)])  5.5 us
    pallas_call x1, Pallas kernels, attend(): pl.pallas_call(functools.partial(attend_kernel, plan=plan, sets=sets, cam...  4.58 us
    ppermute x4, starting transfers between devices, swap(): return lax.ppermute(edge, axis, pairs + [(b, a) for a, b in pairs])  4.47 us
    pallas_call x1, Pallas kernels, expand(): pl.pallas_call(expand_kernel, grid=(width // tile,), in_specs=[pl.BlockSp...  2.15 us
    pallas_call x1, Pallas kernels, finish(): pl.pallas_call(functools.partial(finish_kernel, plan=plan), in_specs=[pl....  1.94 us
  transfers between devices with their start and end apart: 24, of which 6 were waited for; matrix products, arithmetic and copies ran while one was open for 0% of the time, Pallas kernels for 4%

profile of v12, /device:TPU:0, one launch (start us, length us, event | category | flops | bytes accessed | tf_op | source)
XLA Modules:
  0.0 68.4 jit_solution(16282710568262916999)
XLA Ops:
  1.1 3.1 %collective-permute-start.1 = (bf16[32,512]{1,0:T(8,128)(2,1)S(1)}, bf16[32,512]{1,0:T(8,128)(2,1)S(1)}, u32[]{:S(2)}, u32[]{:S(2)}) collective-permute-start(bf16[32,512]{1,0:T(8,128)(2,1)S(1)} %get-tuple-element.75), channel_id=1, source_target_pairs={{0,4},{8,12},{4,0},{12,8},{1,5},{9,13},{5,1},{13,9},{2,6},{10,14},... | collective-permute-start | bytes 98312 | tf_op jit(solution)/shard_map/ppermute | solution.py:431
  5.2 2.1 %expand.1.expanded_ref = f32[8448,128]{1,0:T(8,128)S(1)} custom-call(bf16[512,512]{1,0:T(8,128)(2,1)S(1)} %half_norm.3.normed_ref, bf16[512,2048]{1,0:T(8,128)(2,1)S(1)} %copy-done.2), custom_call_target="tpu_custom_call" | custom-call | flops 10000000000 | bytes 6815744 | tf_op jit(solution)/shard_map/expand/pallas_call | solution.py:101
  7.4 2.0 %copy-done = f32[8448,128]{1,0:T(8,128)} copy-done((f32[8448,128]{1,0:T(8,128)}, f32[8448,128]{1,0:T(8,128)S(1)}, u32[]{:S(2)}) %copy-start) | copy-done | bytes 4325400
  12.8 2.2 %copy-done.1 = f32[8448,128]{1,0:T(8,128)S(1)} copy-done((f32[8448,128]{1,0:T(8,128)S(1)}, f32[8448,128]{1,0:T(8,128)}, u32[]{:S(2)}) %copy-start.1) | copy-done | bytes 4325400
  15.0 1.6 %copy-done.3 = bf16[2048,512]{1,0:T(8,128)(2,1)S(1)} copy-done((bf16[2048,512]{1,0:T(8,128)(2,1)S(1)}, bf16[2048,512]{1,0:T(8,128)(2,1)}, u32[]{:S(2)}) %copy-start.3) | copy-done | bytes 2097176
  16.6 1.0 %copy-done.7 = bf16[512,512]{1,0:T(8,128)(2,1)S(1)} copy-done((bf16[512,512]{1,0:T(8,128)(2,1)S(1)}, bf16[512,512]{1,0:T(8,128)(2,1)}, u32[]{:S(2)}) %copy-start.7) | copy-done | bytes 524312
  17.6 5.7 %mix.1 = (f32[512,512]{1,0:T(8,128)S(1)}, bf16[2,32,512]{2,1,0:T(8,128)(2,1)S(1)}, bf16[2,32,512]{2,1,0:T(8,128)(2,1)S(1)}, bf16[1,32,512]{2,1,0:T(8,128)(2,1)S(...) custom-call(s32[1]{0:T(128)} %bitcast.own_ref, f32[8448,128]{1,0:T(8,128)S(1)} %copy-done.1, ...), custom_call_target="tpu_custom_call" | custom-call | flops 1073741824 | bytes 11010048 | tf_op jit(solution)/shard_map/mix/pallas_call | solution.py:237
  23.4 4.6 %collective-permute-start.6 = (bf16[6,32,512]{2,1,0:T(8,128)(2,1)S(1)}, bf16[6,32,512]{2,1,0:T(8,128)(2,1)S(1)}, u32[]{:S(2)}, u32[]{:S(2)}) collective-permute-start(bf16[6,32,512]{2,1,0:T(8,128)(2,1)S(1)} %get-tuple-element.43), channel_id=1, source_target_pairs={{0,1},{1,0},{2,3},{3,2},{4,5},{5,4},{6,7},{7,6},{8,9},{9,8},{10,11... | collective-permute-start | bytes 589832 | tf_op jit(solution)/shard_map/ppermute | solution.py:506
  28.0 3.2 %collective-permute-start.4 = (bf16[2,32,512]{2,1,0:T(8,128)(2,1)S(1)}, bf16[2,32,512]{2,1,0:T(8,128)(2,1)S(1)}, u32[]{:S(2)}, u32[]{:S(2)}) collective-permute-start(bf16[2,32,512]{2,1,0:T(8,128)(2,1)S(1)} %get-tuple-element.40), channel_id=1, source_target_pairs={{0,14},{1,15},{2,12},{3,13},{4,10},{5,11},{6,8},{7,9},{8,6},{9,7},... | collective-permute-start | bytes 196616 | tf_op jit(solution)/shard_map/ppermute | solution.py:506
  31.2 1.2 %collective-permute-start.5 = (bf16[2,32,512]{2,1,0:T(8,128)(2,1)S(1)}, bf16[2,32,512]{2,1,0:T(8,128)(2,1)S(1)}, u32[]{:S(2)}, u32[]{:S(2)}) collective-permute-start(bf16[2,32,512]{2,1,0:T(8,128)(2,1)S(1)} %get-tuple-element.41), channel_id=1, source_target_pairs={{0,12},{1,13},{2,14},{3,15},{4,8},{5,9},{6,10},{7,11},{8,4},{9,5},... | collective-permute-start | bytes 196616 | tf_op jit(solution)/shard_map/ppermute | solution.py:506
  32.4 2.5 %collective-permute-start.7 = (bf16[2,32,512]{2,1,0:T(8,128)(2,1)S(1)}, bf16[2,32,512]{2,1,0:T(8,128)(2,1)S(1)}, u32[]{:S(2)}, u32[]{:S(2)}) collective-permute-start(bf16[2,32,512]{2,1,0:T(8,128)(2,1)S(1)} %get-tuple-element.44), channel_id=1, source_target_pairs={{0,10},{1,11},{2,8},{3,9},{4,14},{5,15},{6,12},{7,13},{8,2},{9,3},... | collective-permute-start | bytes 196616 | tf_op jit(solution)/shard_map/ppermute | solution.py:506
  34.8 1.7 %collective-permute-start.8 = (bf16[2,32,512]{2,1,0:T(8,128)(2,1)S(1)}, bf16[2,32,512]{2,1,0:T(8,128)(2,1)S(1)}, u32[]{:S(2)}, u32[]{:S(2)}) collective-permute-start(bf16[2,32,512]{2,1,0:T(8,128)(2,1)S(1)} %get-tuple-element.47), channel_id=1, source_target_pairs={{0,6},{1,7},{2,4},{3,5},{4,2},{5,3},{6,0},{7,1},{8,14},{9,15},{10,... | collective-permute-start | bytes 196616 | tf_op jit(solution)/shard_map/ppermute | solution.py:506
  37.4 3.5 %collective-permute-start.10 = (bf16[2,32,512]{2,1,0:T(8,128)(2,1)S(1)}, bf16[2,32,512]{2,1,0:T(8,128)(2,1)S(1)}, u32[]{:S(2)}, u32[]{:S(2)}) collective-permute-start(bf16[2,32,512]{2,1,0:T(8,128)(2,1)S(1)} %get-tuple-element.50), channel_id=1, source_target_pairs={{0,8},{1,9},{2,10},{3,11},{4,12},{5,13},{6,14},{7,15},{8,0},{9,1},... | collective-permute-start | bytes 196616 | tf_op jit(solution)/shard_map/ppermute | solution.py:506
  40.9 2.5 %collective-permute-start.11 = (bf16[2,32,512]{2,1,0:T(8,128)(2,1)S(1)}, bf16[2,32,512]{2,1,0:T(8,128)(2,1)S(1)}, u32[]{:S(2)}, u32[]{:S(2)}) collective-permute-start(bf16[2,32,512]{2,1,0:T(8,128)(2,1)S(1)} %get-tuple-element.51), channel_id=1, source_target_pairs={{0,2},{1,3},{2,0},{3,1},{4,6},{5,7},{6,4},{7,5},{8,10},{9,11},{10,... | collective-permute-start | bytes 196616 | tf_op jit(solution)/shard_map/ppermute | solution.py:506
  44.0 1.3 %collective-permute-done.10.refs_5_ = bf16[2,32,512]{2,1,0:T(8,128)(2,1)S(1)} collective-permute-done((bf16[2,32,512]{2,1,0:T(8,128)(2,1)S(1)}, bf16[2,32,512]{2,1,0:T(8,128)(2,1)S(1)}, u32[]{:S(2)}, u32[]{:S(2)}) %collective-permute-start.10) | collective-permute-done | bytes 65568 | tf_op jit(solution)/shard_map/ppermute | solution.py:506
  45.7 4.6 %attend.1 = (bf16[2,32,512]{2,1,0:T(8,128)(2,1)S(1)}, bf16[2,32,512]{2,1,0:T(8,128)(2,1)S(1)}, bf16[1,32,512]{2,1,0:T(8,128)(2,1)S(1)}, bf16[6,32,512]{2,1,0:T(8,128)(2,1)S(1)}, bf16[5,32,512]{2,1,0:T(8,128)(2,1)S(1)}) custom-call(bf16[2,32,512]{2,1,0:T(8,128)(2,1)S(1)} %collective-permute-done.4.refs_0_, ...), custom_call_target="tpu_custom_call" | custom-call | flops 1073741824 | bytes 2621440 | tf_op jit(solution)/shard_map/attend/pallas_call | solution.py:357
  50.4 2.7 %collective-permute-start.14 = (bf16[2,32,512]{2,1,0:T(8,128)(2,1)S(1)}, bf16[2,32,512]{2,1,0:T(8,128)(2,1)S(1)}, u32[]{:S(2)}, u32[]{:S(2)}) collective-permute-start(bf16[2,32,512]{2,1,0:T(8,128)(2,1)S(1)} %get-tuple-element.53), channel_id=1, source_target_pairs={{0,14},{1,15},{2,12},{3,13},{4,10},{5,11},{6,8},{7,9},{8,6},{9,7},... | collective-permute-start | bytes 196616 | tf_op jit(solution)/shard_map/ppermute | solution.py:506
  53.1 2.6 %collective-permute-start.15 = (bf16[2,32,512]{2,1,0:T(8,128)(2,1)S(1)}, bf16[2,32,512]{2,1,0:T(8,128)(2,1)S(1)}, u32[]{:S(2)}, u32[]{:S(2)}) collective-permute-start(bf16[2,32,512]{2,1,0:T(8,128)(2,1)S(1)} %get-tuple-element.54), channel_id=1, source_target_pairs={{0,12},{1,13},{2,14},{3,15},{4,8},{5,9},{6,10},{7,11},{8,4},{9,5},... | collective-permute-start | bytes 196616 | tf_op jit(solution)/shard_map/ppermute | solution.py:506
  55.8 2.7 %collective-permute-start.18 = (bf16[2,32,512]{2,1,0:T(8,128)(2,1)S(1)}, bf16[2,32,512]{2,1,0:T(8,128)(2,1)S(1)}, u32[]{:S(2)}, u32[]{:S(2)}) collective-permute-start(bf16[2,32,512]{2,1,0:T(8,128)(2,1)S(1)} %get-tuple-element.60), channel_id=1, source_target_pairs={{0,6},{1,7},{2,4},{3,5},{4,2},{5,3},{6,0},{7,1},{8,14},{9,15},{10,... | collective-permute-start | bytes 196616 | tf_op jit(solution)/shard_map/ppermute | solution.py:506
  58.5 3.7 %collective-permute-start.20 = (bf16[2,32,512]{2,1,0:T(8,128)(2,1)S(1)}, bf16[2,32,512]{2,1,0:T(8,128)(2,1)S(1)}, u32[]{:S(2)}, u32[]{:S(2)}) collective-permute-start(bf16[2,32,512]{2,1,0:T(8,128)(2,1)S(1)} %get-tuple-element.63), channel_id=1, source_target_pairs={{0,8},{1,9},{2,10},{3,11},{4,12},{5,13},{6,14},{7,15},{8,0},{9,1},... | collective-permute-start | bytes 196616 | tf_op jit(solution)/shard_map/ppermute | solution.py:506
  62.2 1.5 %collective-permute-done.17.refs_3_ = bf16[2,32,512]{2,1,0:T(8,128)(2,1)S(1)} collective-permute-done((bf16[2,32,512]{2,1,0:T(8,128)(2,1)S(1)}, bf16[2,32,512]{2,1,0:T(8,128)(2,1)S(1)}, u32[]{:S(2)}, u32[]{:S(2)}) %collective-permute-start.17) | collective-permute-done | bytes 65568 | tf_op jit(solution)/shard_map/ppermute | solution.py:506
  64.2 1.1 %collective-permute-done.19.refs_4_ = bf16[2,32,512]{2,1,0:T(8,128)(2,1)S(1)} collective-permute-done((bf16[2,32,512]{2,1,0:T(8,128)(2,1)S(1)}, bf16[2,32,512]{2,1,0:T(8,128)(2,1)S(1)}, u32[]{:S(2)}, u32[]{:S(2)}) %collective-permute-start.19) | collective-permute-done | bytes 65568 | tf_op jit(solution)/shard_map/ppermute | solution.py:506
  65.3 1.2 %collective-permute-done.21.refs_6_ = bf16[2,32,512]{2,1,0:T(8,128)(2,1)S(1)} collective-permute-done((bf16[2,32,512]{2,1,0:T(8,128)(2,1)S(1)}, bf16[2,32,512]{2,1,0:T(8,128)(2,1)S(1)}, u32[]{:S(2)}, u32[]{:S(2)}) %collective-permute-start.21) | collective-permute-done | bytes 65568 | tf_op jit(solution)/shard_map/ppermute | solution.py:506
  66.5 1.9 %finish.1 = f32[512,512]{1,0:T(8,128)} custom-call(s32[1]{0:T(128)} %bitcast.own_ref, bf16[2,32,512]{2,1,0:T(8,128)(2,1)S(1)} %collective-permute-done.14.refs_0_, bf16[2,32,512]{2,1,0:T(8,128)(2,1)S(1)} %collective-permute-done.15.refs_1_, bf16[2,32,512]{2,1,0:T(8,128)(2,1)S(1)} %collective-permute-done.18.refs_2_, ...), custom_call_target="tpu_custom_call" | custom-call | tf_op jit(solution)/shard_map/finish/pallas_call | solution.py:410
  (65 shorter events, 7.9 us)
Async XLA Ops:
  1.1 9.2 %collective-permute-start.1 = (bf16[32,512]{1,0:T(8,128)(2,1)S(1)}, bf16[32,512]{1,0:T(8,128)(2,1)S(1)}, u32[]{:S(2)}, u32[]{:S(2)}) collective-permute-start(bf16[32,512]{1,0:T(8,128)(2,1)S(1)} %get-tuple-element.75), channel_id=1, source_target_pairs={{0,4},{8,12},{4,0},{12,8},{1,5},{9,13},{5,1},{13,9},{2,6},{10,14},... | collective-permute-start | bytes 98312 | tf_op jit(solution)/shard_map/ppermute | solution.py:431
  4.2 6.1 %collective-permute-start = (bf16[32,512]{1,0:T(8,128)(2,1)S(1)}, bf16[32,512]{1,0:T(8,128)(2,1)S(1)}, u32[]{:S(2)}, u32[]{:S(2)}) collective-permute-start(bf16[32,512]{1,0:T(8,128)(2,1)S(1)} %get-tuple-element.76), channel_id=1, source_target_pairs={{4,8},{8,4},{5,9},{9,5},{6,10},{10,6},{7,11},{11,7},{20,24},{24,20... | collective-permute-start | bytes 98312 | tf_op jit(solution)/shard_map/ppermute | solution.py:431
  11.5 1.3 %collective-permute-start.3 = (bf16[32,512]{1,0:T(8,128)(2,1)S(1)}, bf16[32,512]{1,0:T(8,128)(2,1)S(1)}, u32[]{:S(2)}, u32[]{:S(2)}) collective-permute-start(bf16[32,512]{1,0:T(8,128)(2,1)S(1)} %get-tuple-element.77), channel_id=1, source_target_pairs={{0,1},{2,3},{1,0},{3,2},{4,5},{6,7},{5,4},{7,6},{8,9},{10,11},{9,8... | collective-permute-start | bytes 98312 | tf_op jit(solution)/shard_map/ppermute | solution.py:431
  11.6 1.2 %collective-permute-start.2 = (bf16[32,512]{1,0:T(8,128)(2,1)S(1)}, bf16[32,512]{1,0:T(8,128)(2,1)S(1)}, u32[]{:S(2)}, u32[]{:S(2)}) collective-permute-start(bf16[32,512]{1,0:T(8,128)(2,1)S(1)} %get-tuple-element.78), channel_id=1, source_target_pairs={{1,2},{2,1},{5,6},{6,5},{9,10},{10,9},{13,14},{14,13},{17,18},{18,... | collective-permute-start | bytes 98312 | tf_op jit(solution)/shard_map/ppermute | solution.py:431
  23.4 9.0 %collective-permute-start.6 = (bf16[6,32,512]{2,1,0:T(8,128)(2,1)S(1)}, bf16[6,32,512]{2,1,0:T(8,128)(2,1)S(1)}, u32[]{:S(2)}, u32[]{:S(2)}) collective-permute-start(bf16[6,32,512]{2,1,0:T(8,128)(2,1)S(1)} %get-tuple-element.43), channel_id=1, source_target_pairs={{0,1},{1,0},{2,3},{3,2},{4,5},{5,4},{6,7},{7,6},{8,9},{9,8},{10,11... | collective-permute-start | bytes 589832 | tf_op jit(solution)/shard_map/ppermute | solution.py:506
  28.0 9.4 %collective-permute-start.4 = (bf16[2,32,512]{2,1,0:T(8,128)(2,1)S(1)}, bf16[2,32,512]{2,1,0:T(8,128)(2,1)S(1)}, u32[]{:S(2)}, u32[]{:S(2)}) collective-permute-start(bf16[2,32,512]{2,1,0:T(8,128)(2,1)S(1)} %get-tuple-element.40), channel_id=1, source_target_pairs={{0,14},{1,15},{2,12},{3,13},{4,10},{5,11},{6,8},{7,9},{8,6},{9,7},... | collective-permute-start | bytes 196616 | tf_op jit(solution)/shard_map/ppermute | solution.py:506
  31.2 9.7 %collective-permute-start.5 = (bf16[2,32,512]{2,1,0:T(8,128)(2,1)S(1)}, bf16[2,32,512]{2,1,0:T(8,128)(2,1)S(1)}, u32[]{:S(2)}, u32[]{:S(2)}) collective-permute-start(bf16[2,32,512]{2,1,0:T(8,128)(2,1)S(1)} %get-tuple-element.41), channel_id=1, source_target_pairs={{0,12},{1,13},{2,14},{3,15},{4,8},{5,9},{6,10},{7,11},{8,4},{9,5},... | collective-permute-start | bytes 196616 | tf_op jit(solution)/shard_map/ppermute | solution.py:506
  32.4 11.1 %collective-permute-start.7 = (bf16[2,32,512]{2,1,0:T(8,128)(2,1)S(1)}, bf16[2,32,512]{2,1,0:T(8,128)(2,1)S(1)}, u32[]{:S(2)}, u32[]{:S(2)}) collective-permute-start(bf16[2,32,512]{2,1,0:T(8,128)(2,1)S(1)} %get-tuple-element.44), channel_id=1, source_target_pairs={{0,10},{1,11},{2,8},{3,9},{4,14},{5,15},{6,12},{7,13},{8,2},{9,3},... | collective-permute-start | bytes 196616 | tf_op jit(solution)/shard_map/ppermute | solution.py:506
  34.8 8.6 %collective-permute-start.8 = (bf16[2,32,512]{2,1,0:T(8,128)(2,1)S(1)}, bf16[2,32,512]{2,1,0:T(8,128)(2,1)S(1)}, u32[]{:S(2)}, u32[]{:S(2)}) collective-permute-start(bf16[2,32,512]{2,1,0:T(8,128)(2,1)S(1)} %get-tuple-element.47), channel_id=1, source_target_pairs={{0,6},{1,7},{2,4},{3,5},{4,2},{5,3},{6,0},{7,1},{8,14},{9,15},{10,... | collective-permute-start | bytes 196616 | tf_op jit(solution)/shard_map/ppermute | solution.py:506
  36.6 7.4 %collective-permute-start.9 = (bf16[2,32,512]{2,1,0:T(8,128)(2,1)S(1)}, bf16[2,32,512]{2,1,0:T(8,128)(2,1)S(1)}, u32[]{:S(2)}, u32[]{:S(2)}) collective-permute-start(bf16[2,32,512]{2,1,0:T(8,128)(2,1)S(1)} %get-tuple-element.49), channel_id=1, source_target_pairs={{0,4},{1,5},{2,6},{3,7},{4,0},{5,1},{6,2},{7,3},{8,12},{9,13},{10,... | collective-permute-start | bytes 196616 | tf_op jit(solution)/shard_map/ppermute | solution.py:506
  37.4 7.8 %collective-permute-start.10 = (bf16[2,32,512]{2,1,0:T(8,128)(2,1)S(1)}, bf16[2,32,512]{2,1,0:T(8,128)(2,1)S(1)}, u32[]{:S(2)}, u32[]{:S(2)}) collective-permute-start(bf16[2,32,512]{2,1,0:T(8,128)(2,1)S(1)} %get-tuple-element.50), channel_id=1, source_target_pairs={{0,8},{1,9},{2,10},{3,11},{4,12},{5,13},{6,14},{7,15},{8,0},{9,1},... | collective-permute-start | bytes 196616 | tf_op jit(solution)/shard_map/ppermute | solution.py:506
  40.9 4.8 %collective-permute-start.11 = (bf16[2,32,512]{2,1,0:T(8,128)(2,1)S(1)}, bf16[2,32,512]{2,1,0:T(8,128)(2,1)S(1)}, u32[]{:S(2)}, u32[]{:S(2)}) collective-permute-start(bf16[2,32,512]{2,1,0:T(8,128)(2,1)S(1)} %get-tuple-element.51), channel_id=1, source_target_pairs={{0,2},{1,3},{2,0},{3,1},{4,6},{5,7},{6,4},{7,5},{8,10},{9,11},{10,... | collective-permute-start | bytes 196616 | tf_op jit(solution)/shard_map/ppermute | solution.py:506
  43.4 2.2 %collective-permute-start.12 = (bf16[2,32,512]{2,1,0:T(8,128)(2,1)S(1)}, bf16[2,32,512]{2,1,0:T(8,128)(2,1)S(1)}, u32[]{:S(2)}, u32[]{:S(2)}) collective-permute-start(bf16[2,32,512]{2,1,0:T(8,128)(2,1)S(1)} %collective-permute-done.4.refs_0_), channel_id=1, source_target_pairs={{0,1},{1,0},{2,3},{3,2},{4,5},{5,4},{6,7},{7,6},{8,9},{9,8},{10,11... | collective-permute-start | bytes 196616 | tf_op jit(solution)/shard_map/ppermute | solution.py:506
  43.4 2.2 %collective-permute-start.13 = (bf16[2,32,512]{2,1,0:T(8,128)(2,1)S(1)}, bf16[2,32,512]{2,1,0:T(8,128)(2,1)S(1)}, u32[]{:S(2)}, u32[]{:S(2)}) collective-permute-start(bf16[2,32,512]{2,1,0:T(8,128)(2,1)S(1)} %collective-permute-done.5.refs_1_), channel_id=1, source_target_pairs={{0,1},{1,0},{2,3},{3,2},{4,5},{5,4},{6,7},{7,6},{8,9},{9,8},{10,11... | collective-permute-start | bytes 196616 | tf_op jit(solution)/shard_map/ppermute | solution.py:506
  50.3 5.4 %collective-permute-start.16 = (bf16[6,32,512]{2,1,0:T(8,128)(2,1)S(1)}, bf16[6,32,512]{2,1,0:T(8,128)(2,1)S(1)}, u32[]{:S(2)}, u32[]{:S(2)}) collective-permute-start(bf16[6,32,512]{2,1,0:T(8,128)(2,1)S(1)} %get-tuple-element.56), channel_id=1, source_target_pairs={{0,1},{1,0},{2,3},{3,2},{4,5},{5,4},{6,7},{7,6},{8,9},{9,8},{10,11... | collective-permute-start | bytes 589832 | tf_op jit(solution)/shard_map/ppermute | solution.py:506
  50.4 8.1 %collective-permute-start.14 = (bf16[2,32,512]{2,1,0:T(8,128)(2,1)S(1)}, bf16[2,32,512]{2,1,0:T(8,128)(2,1)S(1)}, u32[]{:S(2)}, u32[]{:S(2)}) collective-permute-start(bf16[2,32,512]{2,1,0:T(8,128)(2,1)S(1)} %get-tuple-element.53), channel_id=1, source_target_pairs={{0,14},{1,15},{2,12},{3,13},{4,10},{5,11},{6,8},{7,9},{8,6},{9,7},... | collective-permute-start | bytes 196616 | tf_op jit(solution)/shard_map/ppermute | solution.py:506
  53.1 9.1 %collective-permute-start.15 = (bf16[2,32,512]{2,1,0:T(8,128)(2,1)S(1)}, bf16[2,32,512]{2,1,0:T(8,128)(2,1)S(1)}, u32[]{:S(2)}, u32[]{:S(2)}) collective-permute-start(bf16[2,32,512]{2,1,0:T(8,128)(2,1)S(1)} %get-tuple-element.54), channel_id=1, source_target_pairs={{0,12},{1,13},{2,14},{3,15},{4,8},{5,9},{6,10},{7,11},{8,4},{9,5},... | collective-permute-start | bytes 196616 | tf_op jit(solution)/shard_map/ppermute | solution.py:506
  55.8 7.9 %collective-permute-start.17 = (bf16[2,32,512]{2,1,0:T(8,128)(2,1)S(1)}, bf16[2,32,512]{2,1,0:T(8,128)(2,1)S(1)}, u32[]{:S(2)}, u32[]{:S(2)}) collective-permute-start(bf16[2,32,512]{2,1,0:T(8,128)(2,1)S(1)} %get-tuple-element.57), channel_id=1, source_target_pairs={{0,10},{1,11},{2,8},{3,9},{4,14},{5,15},{6,12},{7,13},{8,2},{9,3},... | collective-permute-start | bytes 196616 | tf_op jit(solution)/shard_map/ppermute | solution.py:506
  55.8 7.8 %collective-permute-start.18 = (bf16[2,32,512]{2,1,0:T(8,128)(2,1)S(1)}, bf16[2,32,512]{2,1,0:T(8,128)(2,1)S(1)}, u32[]{:S(2)}, u32[]{:S(2)}) collective-permute-start(bf16[2,32,512]{2,1,0:T(8,128)(2,1)S(1)} %get-tuple-element.60), channel_id=1, source_target_pairs={{0,6},{1,7},{2,4},{3,5},{4,2},{5,3},{6,0},{7,1},{8,14},{9,15},{10,... | collective-permute-start | bytes 196616 | tf_op jit(solution)/shard_map/ppermute | solution.py:506
  58.5 6.8 %collective-permute-start.19 = (bf16[2,32,512]{2,1,0:T(8,128)(2,1)S(1)}, bf16[2,32,512]{2,1,0:T(8,128)(2,1)S(1)}, u32[]{:S(2)}, u32[]{:S(2)}) collective-permute-start(bf16[2,32,512]{2,1,0:T(8,128)(2,1)S(1)} %get-tuple-element.62), channel_id=1, source_target_pairs={{0,4},{1,5},{2,6},{3,7},{4,0},{5,1},{6,2},{7,3},{8,12},{9,13},{10,... | collective-permute-start | bytes 196616 | tf_op jit(solution)/shard_map/ppermute | solution.py:506
  58.5 6.8 %collective-permute-start.20 = (bf16[2,32,512]{2,1,0:T(8,128)(2,1)S(1)}, bf16[2,32,512]{2,1,0:T(8,128)(2,1)S(1)}, u32[]{:S(2)}, u32[]{:S(2)}) collective-permute-start(bf16[2,32,512]{2,1,0:T(8,128)(2,1)S(1)} %get-tuple-element.63), channel_id=1, source_target_pairs={{0,8},{1,9},{2,10},{3,11},{4,12},{5,13},{6,14},{7,15},{8,0},{9,1},... | collective-permute-start | bytes 196616 | tf_op jit(solution)/shard_map/ppermute | solution.py:506
  62.2 4.3 %collective-permute-start.21 = (bf16[2,32,512]{2,1,0:T(8,128)(2,1)S(1)}, bf16[2,32,512]{2,1,0:T(8,128)(2,1)S(1)}, u32[]{:S(2)}, u32[]{:S(2)}) collective-permute-start(bf16[2,32,512]{2,1,0:T(8,128)(2,1)S(1)} %get-tuple-element.64), channel_id=1, source_target_pairs={{0,2},{1,3},{2,0},{3,1},{4,6},{5,7},{6,4},{7,5},{8,10},{9,11},{10,... | collective-permute-start | bytes 196616 | tf_op jit(solution)/shard_map/ppermute | solution.py:506
  63.7 2.8 %collective-permute-start.22 = (bf16[2,32,512]{2,1,0:T(8,128)(2,1)S(1)}, bf16[2,32,512]{2,1,0:T(8,128)(2,1)S(1)}, u32[]{:S(2)}, u32[]{:S(2)}) collective-permute-start(bf16[2,32,512]{2,1,0:T(8,128)(2,1)S(1)} %collective-permute-done.14.refs_0_), channel_id=1, source_target_pairs={{0,1},{1,0},{2,3},{3,2},{4,5},{5,4},{6,7},{7,6},{8,9},{9,8},{10,11... | collective-permute-start | bytes 196616 | tf_op jit(solution)/shard_map/ppermute | solution.py:506
  63.7 2.8 %collective-permute-start.23 = (bf16[2,32,512]{2,1,0:T(8,128)(2,1)S(1)}, bf16[2,32,512]{2,1,0:T(8,128)(2,1)S(1)}, u32[]{:S(2)}, u32[]{:S(2)}) collective-permute-start(bf16[2,32,512]{2,1,0:T(8,128)(2,1)S(1)} %collective-permute-done.15.refs_1_), channel_id=1, source_target_pairs={{0,1},{1,0},{2,3},{3,2},{4,5},{5,4},{6,7},{7,6},{8,9},{9,8},{10,11... | collective-permute-start | bytes 196616 | tf_op jit(solution)/shard_map/ppermute | solution.py:506
  (11 other events, 92.9 us)

commit v13 on v11

--- a/solution.py
+++ b/solution.py
@@ -565,9 +565,9 @@
     expanded = expand(normed, w_expand)
     up, down, normed, expanded = lax.optimization_barrier((up, down, normed, expanded))
     tile = normed.reshape(rows, cols, channels)
-    spare = jnp.zeros((round_up(rows + 2, 16) - rows - 2, channels), jnp.bfloat16)
-    first = jnp.concatenate([up[:1], tile[:, 0], down[:1], spare], axis=0)
-    last = jnp.concatenate([up[cols - 1 :], tile[:, cols - 1], down[cols - 1 :], spare], axis=0)
+    spare = round_up(rows + 2, 16) - rows - 2
+    first = jnp.concatenate([up[:1], tile[:, 0], down[:1], up[:spare]], axis=0)
+    last = jnp.concatenate([up[cols - 1 :], tile[:, cols - 1], down[cols - 1 :], up[:spare]], axis=0)
     left, right = exchange(first, last, "col")
     pairwise = 8 <= devices <= 16 and devices & (devices - 1) == 0 and col_devices % 2 == 0
     if pairwise:

time: 68.7 us -> 68.6 us (level)
  no operation moved by 1% of the time
where the time goes in v13:
time: 68.6 us; the launch traced here: 68.3 us
  starting transfers between devices  37.3 us (54%)
  Pallas kernels  15 us (22%)
  local copies, waits for them, and re-layouts  9.63 us (14%)
  waiting for transfers between devices  6.03 us (9%)
    ppermute x20, starting transfers between devices, swap(): lax.ppermute(slab, ('row', 'col'), [(i, i ^ mask) for i in range(devices)])  32.8 us
    unnamed x22, local copies, waits for them, and re-layouts  7.7 us
    pallas_call x1, Pallas kernels, mix(): pl.pallas_call(functools.partial(mix_kernel, rows=rows, cols=cols, plan=p...  5.73 us
    ppermute x20, waiting for transfers between devices, swap(): lax.ppermute(slab, ('row', 'col'), [(i, i ^ mask) for i in range(devices)])  5.5 us
    pallas_call x1, Pallas kernels, attend(): pl.pallas_call(functools.partial(attend_kernel, plan=plan, sets=sets, cam...  4.58 us
    ppermute x4, starting transfers between devices, swap(): return lax.ppermute(edge, axis, pairs + [(b, a) for a, b in pairs])  4.47 us
    pallas_call x1, Pallas kernels, expand(): pl.pallas_call(expand_kernel, in_specs=[vmem()] * 2, out_specs=vmem(), ou...  2.16 us
    pallas_call x1, Pallas kernels, finish(): pl.pallas_call(functools.partial(finish_kernel, plan=plan), in_specs=[pl....  1.94 us
  transfers between devices with their start and end apart: 24, of which 6 were waited for; matrix products, arithmetic and copies ran while one was open for 0% of the time, Pallas kernels for 4%

profile of v13, /device:TPU:0, one launch (start us, length us, event | category | flops | bytes accessed | tf_op | source)
XLA Modules:
  0.0 68.3 jit_solution(3591358870173480789)
XLA Ops:
  1.1 3.1 %collective-permute-start.1 = (bf16[32,512]{1,0:T(8,128)(2,1)S(1)}, bf16[32,512]{1,0:T(8,128)(2,1)S(1)}, u32[]{:S(2)}, u32[]{:S(2)}) collective-permute-start(bf16[32,512]{1,0:T(8,128)(2,1)S(1)} %get-tuple-element.75), channel_id=1, source_target_pairs={{0,4},{8,12},{4,0},{12,8},{1,5},{9,13},{5,1},{13,9},{2,6},{10,14},... | collective-permute-start | bytes 98312 | tf_op jit(solution)/shard_map/ppermute | solution.py:437
  5.2 2.2 %expand.1.expanded_ref = f32[8448,128]{1,0:T(8,128)S(1)} custom-call(bf16[512,512]{1,0:T(8,128)(2,1)S(1)} %half_norm.3.normed_ref, bf16[512,2048]{1,0:T(8,128)(2,1)S(1)} %copy-done.2), custom_call_target="tpu_custom_call" | custom-call | flops 10000000000 | bytes 6815744 | tf_op jit(solution)/shard_map/expand/pallas_call | solution.py:111
  7.4 2.0 %copy-done = f32[8448,128]{1,0:T(8,128)} copy-done((f32[8448,128]{1,0:T(8,128)}, f32[8448,128]{1,0:T(8,128)S(1)}, u32[]{:S(2)}) %copy-start) | copy-done | bytes 4325400
  12.7 2.2 %copy-done.1 = f32[8448,128]{1,0:T(8,128)S(1)} copy-done((f32[8448,128]{1,0:T(8,128)S(1)}, f32[8448,128]{1,0:T(8,128)}, u32[]{:S(2)}) %copy-start.1) | copy-done | bytes 4325400
  14.9 1.6 %copy-done.3 = bf16[2048,512]{1,0:T(8,128)(2,1)S(1)} copy-done((bf16[2048,512]{1,0:T(8,128)(2,1)S(1)}, bf16[2048,512]{1,0:T(8,128)(2,1)}, u32[]{:S(2)}) %copy-start.3) | copy-done | bytes 2097176
  16.5 1.0 %copy-done.7 = bf16[512,512]{1,0:T(8,128)(2,1)S(1)} copy-done((bf16[512,512]{1,0:T(8,128)(2,1)S(1)}, bf16[512,512]{1,0:T(8,128)(2,1)}, u32[]{:S(2)}) %copy-start.7) | copy-done | bytes 524312
  17.5 5.7 %mix.1 = (f32[512,512]{1,0:T(8,128)S(1)}, bf16[2,32,512]{2,1,0:T(8,128)(2,1)S(1)}, bf16[2,32,512]{2,1,0:T(8,128)(2,1)S(1)}, bf16[1,32,512]{2,1,0:T(8,128)(2,1)S(...) custom-call(s32[1]{0:T(128)} %bitcast.own_ref, f32[8448,128]{1,0:T(8,128)S(1)} %copy-done.1, ...), custom_call_target="tpu_custom_call" | custom-call | flops 1073741824 | bytes 11010048 | tf_op jit(solution)/shard_map/mix/pallas_call | solution.py:243
  23.3 4.6 %collective-permute-start.6 = (bf16[6,32,512]{2,1,0:T(8,128)(2,1)S(1)}, bf16[6,32,512]{2,1,0:T(8,128)(2,1)S(1)}, u32[]{:S(2)}, u32[]{:S(2)}) collective-permute-start(bf16[6,32,512]{2,1,0:T(8,128)(2,1)S(1)} %get-tuple-element.43), channel_id=1, source_target_pairs={{0,1},{1,0},{2,3},{3,2},{4,5},{5,4},{6,7},{7,6},{8,9},{9,8},{10,11... | collective-permute-start | bytes 589832 | tf_op jit(solution)/shard_map/ppermute | solution.py:512
  27.9 3.2 %collective-permute-start.4 = (bf16[2,32,512]{2,1,0:T(8,128)(2,1)S(1)}, bf16[2,32,512]{2,1,0:T(8,128)(2,1)S(1)}, u32[]{:S(2)}, u32[]{:S(2)}) collective-permute-start(bf16[2,32,512]{2,1,0:T(8,128)(2,1)S(1)} %get-tuple-element.40), channel_id=1, source_target_pairs={{0,14},{1,15},{2,12},{3,13},{4,10},{5,11},{6,8},{7,9},{8,6},{9,7},... | collective-permute-start | bytes 196616 | tf_op jit(solution)/shard_map/ppermute | solution.py:512
  31.1 1.2 %collective-permute-start.5 = (bf16[2,32,512]{2,1,0:T(8,128)(2,1)S(1)}, bf16[2,32,512]{2,1,0:T(8,128)(2,1)S(1)}, u32[]{:S(2)}, u32[]{:S(2)}) collective-permute-start(bf16[2,32,512]{2,1,0:T(8,128)(2,1)S(1)} %get-tuple-element.41), channel_id=1, source_target_pairs={{0,12},{1,13},{2,14},{3,15},{4,8},{5,9},{6,10},{7,11},{8,4},{9,5},... | collective-permute-start | bytes 196616 | tf_op jit(solution)/shard_map/ppermute | solution.py:512
  32.3 2.5 %collective-permute-start.7 = (bf16[2,32,512]{2,1,0:T(8,128)(2,1)S(1)}, bf16[2,32,512]{2,1,0:T(8,128)(2,1)S(1)}, u32[]{:S(2)}, u32[]{:S(2)}) collective-permute-start(bf16[2,32,512]{2,1,0:T(8,128)(2,1)S(1)} %get-tuple-element.44), channel_id=1, source_target_pairs={{0,10},{1,11},{2,8},{3,9},{4,14},{5,15},{6,12},{7,13},{8,2},{9,3},... | collective-permute-start | bytes 196616 | tf_op jit(solution)/shard_map/ppermute | solution.py:512
  34.8 1.7 %collective-permute-start.8 = (bf16[2,32,512]{2,1,0:T(8,128)(2,1)S(1)}, bf16[2,32,512]{2,1,0:T(8,128)(2,1)S(1)}, u32[]{:S(2)}, u32[]{:S(2)}) collective-permute-start(bf16[2,32,512]{2,1,0:T(8,128)(2,1)S(1)} %get-tuple-element.47), channel_id=1, source_target_pairs={{0,6},{1,7},{2,4},{3,5},{4,2},{5,3},{6,0},{7,1},{8,14},{9,15},{10,... | collective-permute-start | bytes 196616 | tf_op jit(solution)/shard_map/ppermute | solution.py:512
  37.3 3.5 %collective-permute-start.10 = (bf16[2,32,512]{2,1,0:T(8,128)(2,1)S(1)}, bf16[2,32,512]{2,1,0:T(8,128)(2,1)S(1)}, u32[]{:S(2)}, u32[]{:S(2)}) collective-permute-start(bf16[2,32,512]{2,1,0:T(8,128)(2,1)S(1)} %get-tuple-element.50), channel_id=1, source_target_pairs={{0,8},{1,9},{2,10},{3,11},{4,12},{5,13},{6,14},{7,15},{8,0},{9,1},... | collective-permute-start | bytes 196616 | tf_op jit(solution)/shard_map/ppermute | solution.py:512
  40.8 2.6 %collective-permute-start.11 = (bf16[2,32,512]{2,1,0:T(8,128)(2,1)S(1)}, bf16[2,32,512]{2,1,0:T(8,128)(2,1)S(1)}, u32[]{:S(2)}, u32[]{:S(2)}) collective-permute-start(bf16[2,32,512]{2,1,0:T(8,128)(2,1)S(1)} %get-tuple-element.51), channel_id=1, source_target_pairs={{0,2},{1,3},{2,0},{3,1},{4,6},{5,7},{6,4},{7,5},{8,10},{9,11},{10,... | collective-permute-start | bytes 196616 | tf_op jit(solution)/shard_map/ppermute | solution.py:512
  43.9 1.3 %collective-permute-done.10.refs_5_ = bf16[2,32,512]{2,1,0:T(8,128)(2,1)S(1)} collective-permute-done((bf16[2,32,512]{2,1,0:T(8,128)(2,1)S(1)}, bf16[2,32,512]{2,1,0:T(8,128)(2,1)S(1)}, u32[]{:S(2)}, u32[]{:S(2)}) %collective-permute-start.10) | collective-permute-done | bytes 65568 | tf_op jit(solution)/shard_map/ppermute | solution.py:512
  45.6 4.6 %attend.1 = (bf16[2,32,512]{2,1,0:T(8,128)(2,1)S(1)}, bf16[2,32,512]{2,1,0:T(8,128)(2,1)S(1)}, bf16[1,32,512]{2,1,0:T(8,128)(2,1)S(1)}, bf16[6,32,512]{2,1,0:T(8,128)(2,1)S(1)}, bf16[5,32,512]{2,1,0:T(8,128)(2,1)S(1)}) custom-call(bf16[2,32,512]{2,1,0:T(8,128)(2,1)S(1)} %collective-permute-done.4.refs_0_, ...), custom_call_target="tpu_custom_call" | custom-call | flops 1073741824 | bytes 2621440 | tf_op jit(solution)/shard_map/attend/pallas_call | solution.py:363
  50.3 2.7 %collective-permute-start.14 = (bf16[2,32,512]{2,1,0:T(8,128)(2,1)S(1)}, bf16[2,32,512]{2,1,0:T(8,128)(2,1)S(1)}, u32[]{:S(2)}, u32[]{:S(2)}) collective-permute-start(bf16[2,32,512]{2,1,0:T(8,128)(2,1)S(1)} %get-tuple-element.53), channel_id=1, source_target_pairs={{0,14},{1,15},{2,12},{3,13},{4,10},{5,11},{6,8},{7,9},{8,6},{9,7},... | collective-permute-start | bytes 196616 | tf_op jit(solution)/shard_map/ppermute | solution.py:512
  53.0 2.6 %collective-permute-start.15 = (bf16[2,32,512]{2,1,0:T(8,128)(2,1)S(1)}, bf16[2,32,512]{2,1,0:T(8,128)(2,1)S(1)}, u32[]{:S(2)}, u32[]{:S(2)}) collective-permute-start(bf16[2,32,512]{2,1,0:T(8,128)(2,1)S(1)} %get-tuple-element.54), channel_id=1, source_target_pairs={{0,12},{1,13},{2,14},{3,15},{4,8},{5,9},{6,10},{7,11},{8,4},{9,5},... | collective-permute-start | bytes 196616 | tf_op jit(solution)/shard_map/ppermute | solution.py:512
  55.7 2.6 %collective-permute-start.18 = (bf16[2,32,512]{2,1,0:T(8,128)(2,1)S(1)}, bf16[2,32,512]{2,1,0:T(8,128)(2,1)S(1)}, u32[]{:S(2)}, u32[]{:S(2)}) collective-permute-start(bf16[2,32,512]{2,1,0:T(8,128)(2,1)S(1)} %get-tuple-element.60), channel_id=1, source_target_pairs={{0,6},{1,7},{2,4},{3,5},{4,2},{5,3},{6,0},{7,1},{8,14},{9,15},{10,... | collective-permute-start | bytes 196616 | tf_op jit(solution)/shard_map/ppermute | solution.py:512
  58.4 3.7 %collective-permute-start.20 = (bf16[2,32,512]{2,1,0:T(8,128)(2,1)S(1)}, bf16[2,32,512]{2,1,0:T(8,128)(2,1)S(1)}, u32[]{:S(2)}, u32[]{:S(2)}) collective-permute-start(bf16[2,32,512]{2,1,0:T(8,128)(2,1)S(1)} %get-tuple-element.63), channel_id=1, source_target_pairs={{0,8},{1,9},{2,10},{3,11},{4,12},{5,13},{6,14},{7,15},{8,0},{9,1},... | collective-permute-start | bytes 196616 | tf_op jit(solution)/shard_map/ppermute | solution.py:512
  62.1 1.5 %collective-permute-done.17.refs_3_ = bf16[2,32,512]{2,1,0:T(8,128)(2,1)S(1)} collective-permute-done((bf16[2,32,512]{2,1,0:T(8,128)(2,1)S(1)}, bf16[2,32,512]{2,1,0:T(8,128)(2,1)S(1)}, u32[]{:S(2)}, u32[]{:S(2)}) %collective-permute-start.17) | collective-permute-done | bytes 65568 | tf_op jit(solution)/shard_map/ppermute | solution.py:512
  64.1 1.1 %collective-permute-done.19.refs_4_ = bf16[2,32,512]{2,1,0:T(8,128)(2,1)S(1)} collective-permute-done((bf16[2,32,512]{2,1,0:T(8,128)(2,1)S(1)}, bf16[2,32,512]{2,1,0:T(8,128)(2,1)S(1)}, u32[]{:S(2)}, u32[]{:S(2)}) %collective-permute-start.19) | collective-permute-done | bytes 65568 | tf_op jit(solution)/shard_map/ppermute | solution.py:512
  65.2 1.1 %collective-permute-done.21.refs_6_ = bf16[2,32,512]{2,1,0:T(8,128)(2,1)S(1)} collective-permute-done((bf16[2,32,512]{2,1,0:T(8,128)(2,1)S(1)}, bf16[2,32,512]{2,1,0:T(8,128)(2,1)S(1)}, u32[]{:S(2)}, u32[]{:S(2)}) %collective-permute-start.21) | collective-permute-done | bytes 65568 | tf_op jit(solution)/shard_map/ppermute | solution.py:512
  66.4 1.9 %finish.1 = f32[512,512]{1,0:T(8,128)} custom-call(s32[1]{0:T(128)} %bitcast.own_ref, bf16[2,32,512]{2,1,0:T(8,128)(2,1)S(1)} %collective-permute-done.14.refs_0_, bf16[2,32,512]{2,1,0:T(8,128)(2,1)S(1)} %collective-permute-done.15.refs_1_, bf16[2,32,512]{2,1,0:T(8,128)(2,1)S(1)} %collective-permute-done.18.refs_2_, ...), custom_call_target="tpu_custom_call" | custom-call | tf_op jit(solution)/shard_map/finish/pallas_call | solution.py:416
  (64 shorter events, 7.8 us)
Async XLA Ops:
  1.1 9.1 %collective-permute-start.1 = (bf16[32,512]{1,0:T(8,128)(2,1)S(1)}, bf16[32,512]{1,0:T(8,128)(2,1)S(1)}, u32[]{:S(2)}, u32[]{:S(2)}) collective-permute-start(bf16[32,512]{1,0:T(8,128)(2,1)S(1)} %get-tuple-element.75), channel_id=1, source_target_pairs={{0,4},{8,12},{4,0},{12,8},{1,5},{9,13},{5,1},{13,9},{2,6},{10,14},... | collective-permute-start | bytes 98312 | tf_op jit(solution)/shard_map/ppermute | solution.py:437
  4.2 6.0 %collective-permute-start = (bf16[32,512]{1,0:T(8,128)(2,1)S(1)}, bf16[32,512]{1,0:T(8,128)(2,1)S(1)}, u32[]{:S(2)}, u32[]{:S(2)}) collective-permute-start(bf16[32,512]{1,0:T(8,128)(2,1)S(1)} %get-tuple-element.76), channel_id=1, source_target_pairs={{4,8},{8,4},{5,9},{9,5},{6,10},{10,6},{7,11},{11,7},{20,24},{24,20... | collective-permute-start | bytes 98312 | tf_op jit(solution)/shard_map/ppermute | solution.py:437
  11.4 1.3 %collective-permute-start.3 = (bf16[32,512]{1,0:T(8,128)(2,1)S(1)}, bf16[32,512]{1,0:T(8,128)(2,1)S(1)}, u32[]{:S(2)}, u32[]{:S(2)}) collective-permute-start(bf16[32,512]{1,0:T(8,128)(2,1)S(1)} %get-tuple-element.77), channel_id=1, source_target_pairs={{0,1},{2,3},{1,0},{3,2},{4,5},{6,7},{5,4},{7,6},{8,9},{10,11},{9,8... | collective-permute-start | bytes 98312 | tf_op jit(solution)/shard_map/ppermute | solution.py:437
  11.5 1.2 %collective-permute-start.2 = (bf16[32,512]{1,0:T(8,128)(2,1)S(1)}, bf16[32,512]{1,0:T(8,128)(2,1)S(1)}, u32[]{:S(2)}, u32[]{:S(2)}) collective-permute-start(bf16[32,512]{1,0:T(8,128)(2,1)S(1)} %get-tuple-element.78), channel_id=1, source_target_pairs={{1,2},{2,1},{5,6},{6,5},{9,10},{10,9},{13,14},{14,13},{17,18},{18,... | collective-permute-start | bytes 98312 | tf_op jit(solution)/shard_map/ppermute | solution.py:437
  23.3 9.0 %collective-permute-start.6 = (bf16[6,32,512]{2,1,0:T(8,128)(2,1)S(1)}, bf16[6,32,512]{2,1,0:T(8,128)(2,1)S(1)}, u32[]{:S(2)}, u32[]{:S(2)}) collective-permute-start(bf16[6,32,512]{2,1,0:T(8,128)(2,1)S(1)} %get-tuple-element.43), channel_id=1, source_target_pairs={{0,1},{1,0},{2,3},{3,2},{4,5},{5,4},{6,7},{7,6},{8,9},{9,8},{10,11... | collective-permute-start | bytes 589832 | tf_op jit(solution)/shard_map/ppermute | solution.py:512
  27.9 9.5 %collective-permute-start.4 = (bf16[2,32,512]{2,1,0:T(8,128)(2,1)S(1)}, bf16[2,32,512]{2,1,0:T(8,128)(2,1)S(1)}, u32[]{:S(2)}, u32[]{:S(2)}) collective-permute-start(bf16[2,32,512]{2,1,0:T(8,128)(2,1)S(1)} %get-tuple-element.40), channel_id=1, source_target_pairs={{0,14},{1,15},{2,12},{3,13},{4,10},{5,11},{6,8},{7,9},{8,6},{9,7},... | collective-permute-start | bytes 196616 | tf_op jit(solution)/shard_map/ppermute | solution.py:512
  31.1 9.7 %collective-permute-start.5 = (bf16[2,32,512]{2,1,0:T(8,128)(2,1)S(1)}, bf16[2,32,512]{2,1,0:T(8,128)(2,1)S(1)}, u32[]{:S(2)}, u32[]{:S(2)}) collective-permute-start(bf16[2,32,512]{2,1,0:T(8,128)(2,1)S(1)} %get-tuple-element.41), channel_id=1, source_target_pairs={{0,12},{1,13},{2,14},{3,15},{4,8},{5,9},{6,10},{7,11},{8,4},{9,5},... | collective-permute-start | bytes 196616 | tf_op jit(solution)/shard_map/ppermute | solution.py:512
  32.3 11.1 %collective-permute-start.7 = (bf16[2,32,512]{2,1,0:T(8,128)(2,1)S(1)}, bf16[2,32,512]{2,1,0:T(8,128)(2,1)S(1)}, u32[]{:S(2)}, u32[]{:S(2)}) collective-permute-start(bf16[2,32,512]{2,1,0:T(8,128)(2,1)S(1)} %get-tuple-element.44), channel_id=1, source_target_pairs={{0,10},{1,11},{2,8},{3,9},{4,14},{5,15},{6,12},{7,13},{8,2},{9,3},... | collective-permute-start | bytes 196616 | tf_op jit(solution)/shard_map/ppermute | solution.py:512
  34.8 8.6 %collective-permute-start.8 = (bf16[2,32,512]{2,1,0:T(8,128)(2,1)S(1)}, bf16[2,32,512]{2,1,0:T(8,128)(2,1)S(1)}, u32[]{:S(2)}, u32[]{:S(2)}) collective-permute-start(bf16[2,32,512]{2,1,0:T(8,128)(2,1)S(1)} %get-tuple-element.47), channel_id=1, source_target_pairs={{0,6},{1,7},{2,4},{3,5},{4,2},{5,3},{6,0},{7,1},{8,14},{9,15},{10,... | collective-permute-start | bytes 196616 | tf_op jit(solution)/shard_map/ppermute | solution.py:512
  36.5 7.4 %collective-permute-start.9 = (bf16[2,32,512]{2,1,0:T(8,128)(2,1)S(1)}, bf16[2,32,512]{2,1,0:T(8,128)(2,1)S(1)}, u32[]{:S(2)}, u32[]{:S(2)}) collective-permute-start(bf16[2,32,512]{2,1,0:T(8,128)(2,1)S(1)} %get-tuple-element.49), channel_id=1, source_target_pairs={{0,4},{1,5},{2,6},{3,7},{4,0},{5,1},{6,2},{7,3},{8,12},{9,13},{10,... | collective-permute-start | bytes 196616 | tf_op jit(solution)/shard_map/ppermute | solution.py:512
  37.3 7.8 %collective-permute-start.10 = (bf16[2,32,512]{2,1,0:T(8,128)(2,1)S(1)}, bf16[2,32,512]{2,1,0:T(8,128)(2,1)S(1)}, u32[]{:S(2)}, u32[]{:S(2)}) collective-permute-start(bf16[2,32,512]{2,1,0:T(8,128)(2,1)S(1)} %get-tuple-element.50), channel_id=1, source_target_pairs={{0,8},{1,9},{2,10},{3,11},{4,12},{5,13},{6,14},{7,15},{8,0},{9,1},... | collective-permute-start | bytes 196616 | tf_op jit(solution)/shard_map/ppermute | solution.py:512
  40.8 4.8 %collective-permute-start.11 = (bf16[2,32,512]{2,1,0:T(8,128)(2,1)S(1)}, bf16[2,32,512]{2,1,0:T(8,128)(2,1)S(1)}, u32[]{:S(2)}, u32[]{:S(2)}) collective-permute-start(bf16[2,32,512]{2,1,0:T(8,128)(2,1)S(1)} %get-tuple-element.51), channel_id=1, source_target_pairs={{0,2},{1,3},{2,0},{3,1},{4,6},{5,7},{6,4},{7,5},{8,10},{9,11},{10,... | collective-permute-start | bytes 196616 | tf_op jit(solution)/shard_map/ppermute | solution.py:512
  43.3 2.2 %collective-permute-start.12 = (bf16[2,32,512]{2,1,0:T(8,128)(2,1)S(1)}, bf16[2,32,512]{2,1,0:T(8,128)(2,1)S(1)}, u32[]{:S(2)}, u32[]{:S(2)}) collective-permute-start(bf16[2,32,512]{2,1,0:T(8,128)(2,1)S(1)} %collective-permute-done.4.refs_0_), channel_id=1, source_target_pairs={{0,1},{1,0},{2,3},{3,2},{4,5},{5,4},{6,7},{7,6},{8,9},{9,8},{10,11... | collective-permute-start | bytes 196616 | tf_op jit(solution)/shard_map/ppermute | solution.py:512
  43.4 2.2 %collective-permute-start.13 = (bf16[2,32,512]{2,1,0:T(8,128)(2,1)S(1)}, bf16[2,32,512]{2,1,0:T(8,128)(2,1)S(1)}, u32[]{:S(2)}, u32[]{:S(2)}) collective-permute-start(bf16[2,32,512]{2,1,0:T(8,128)(2,1)S(1)} %collective-permute-done.5.refs_1_), channel_id=1, source_target_pairs={{0,1},{1,0},{2,3},{3,2},{4,5},{5,4},{6,7},{7,6},{8,9},{9,8},{10,11... | collective-permute-start | bytes 196616 | tf_op jit(solution)/shard_map/ppermute | solution.py:512
  50.2 5.4 %collective-permute-start.16 = (bf16[6,32,512]{2,1,0:T(8,128)(2,1)S(1)}, bf16[6,32,512]{2,1,0:T(8,128)(2,1)S(1)}, u32[]{:S(2)}, u32[]{:S(2)}) collective-permute-start(bf16[6,32,512]{2,1,0:T(8,128)(2,1)S(1)} %get-tuple-element.56), channel_id=1, source_target_pairs={{0,1},{1,0},{2,3},{3,2},{4,5},{5,4},{6,7},{7,6},{8,9},{9,8},{10,11... | collective-permute-start | bytes 589832 | tf_op jit(solution)/shard_map/ppermute | solution.py:512
  50.3 8.1 %collective-permute-start.14 = (bf16[2,32,512]{2,1,0:T(8,128)(2,1)S(1)}, bf16[2,32,512]{2,1,0:T(8,128)(2,1)S(1)}, u32[]{:S(2)}, u32[]{:S(2)}) collective-permute-start(bf16[2,32,512]{2,1,0:T(8,128)(2,1)S(1)} %get-tuple-element.53), channel_id=1, source_target_pairs={{0,14},{1,15},{2,12},{3,13},{4,10},{5,11},{6,8},{7,9},{8,6},{9,7},... | collective-permute-start | bytes 196616 | tf_op jit(solution)/shard_map/ppermute | solution.py:512
  53.0 9.1 %collective-permute-start.15 = (bf16[2,32,512]{2,1,0:T(8,128)(2,1)S(1)}, bf16[2,32,512]{2,1,0:T(8,128)(2,1)S(1)}, u32[]{:S(2)}, u32[]{:S(2)}) collective-permute-start(bf16[2,32,512]{2,1,0:T(8,128)(2,1)S(1)} %get-tuple-element.54), channel_id=1, source_target_pairs={{0,12},{1,13},{2,14},{3,15},{4,8},{5,9},{6,10},{7,11},{8,4},{9,5},... | collective-permute-start | bytes 196616 | tf_op jit(solution)/shard_map/ppermute | solution.py:512
  55.7 7.9 %collective-permute-start.17 = (bf16[2,32,512]{2,1,0:T(8,128)(2,1)S(1)}, bf16[2,32,512]{2,1,0:T(8,128)(2,1)S(1)}, u32[]{:S(2)}, u32[]{:S(2)}) collective-permute-start(bf16[2,32,512]{2,1,0:T(8,128)(2,1)S(1)} %get-tuple-element.57), channel_id=1, source_target_pairs={{0,10},{1,11},{2,8},{3,9},{4,14},{5,15},{6,12},{7,13},{8,2},{9,3},... | collective-permute-start | bytes 196616 | tf_op jit(solution)/shard_map/ppermute | solution.py:512
  55.7 7.8 %collective-permute-start.18 = (bf16[2,32,512]{2,1,0:T(8,128)(2,1)S(1)}, bf16[2,32,512]{2,1,0:T(8,128)(2,1)S(1)}, u32[]{:S(2)}, u32[]{:S(2)}) collective-permute-start(bf16[2,32,512]{2,1,0:T(8,128)(2,1)S(1)} %get-tuple-element.60), channel_id=1, source_target_pairs={{0,6},{1,7},{2,4},{3,5},{4,2},{5,3},{6,0},{7,1},{8,14},{9,15},{10,... | collective-permute-start | bytes 196616 | tf_op jit(solution)/shard_map/ppermute | solution.py:512
  58.4 6.8 %collective-permute-start.19 = (bf16[2,32,512]{2,1,0:T(8,128)(2,1)S(1)}, bf16[2,32,512]{2,1,0:T(8,128)(2,1)S(1)}, u32[]{:S(2)}, u32[]{:S(2)}) collective-permute-start(bf16[2,32,512]{2,1,0:T(8,128)(2,1)S(1)} %get-tuple-element.62), channel_id=1, source_target_pairs={{0,4},{1,5},{2,6},{3,7},{4,0},{5,1},{6,2},{7,3},{8,12},{9,13},{10,... | collective-permute-start | bytes 196616 | tf_op jit(solution)/shard_map/ppermute | solution.py:512
  58.4 6.8 %collective-permute-start.20 = (bf16[2,32,512]{2,1,0:T(8,128)(2,1)S(1)}, bf16[2,32,512]{2,1,0:T(8,128)(2,1)S(1)}, u32[]{:S(2)}, u32[]{:S(2)}) collective-permute-start(bf16[2,32,512]{2,1,0:T(8,128)(2,1)S(1)} %get-tuple-element.63), channel_id=1, source_target_pairs={{0,8},{1,9},{2,10},{3,11},{4,12},{5,13},{6,14},{7,15},{8,0},{9,1},... | collective-permute-start | bytes 196616 | tf_op jit(solution)/shard_map/ppermute | solution.py:512
  62.1 4.3 %collective-permute-start.21 = (bf16[2,32,512]{2,1,0:T(8,128)(2,1)S(1)}, bf16[2,32,512]{2,1,0:T(8,128)(2,1)S(1)}, u32[]{:S(2)}, u32[]{:S(2)}) collective-permute-start(bf16[2,32,512]{2,1,0:T(8,128)(2,1)S(1)} %get-tuple-element.64), channel_id=1, source_target_pairs={{0,2},{1,3},{2,0},{3,1},{4,6},{5,7},{6,4},{7,5},{8,10},{9,11},{10,... | collective-permute-start | bytes 196616 | tf_op jit(solution)/shard_map/ppermute | solution.py:512
  63.5 2.8 %collective-permute-start.22 = (bf16[2,32,512]{2,1,0:T(8,128)(2,1)S(1)}, bf16[2,32,512]{2,1,0:T(8,128)(2,1)S(1)}, u32[]{:S(2)}, u32[]{:S(2)}) collective-permute-start(bf16[2,32,512]{2,1,0:T(8,128)(2,1)S(1)} %collective-permute-done.14.refs_0_), channel_id=1, source_target_pairs={{0,1},{1,0},{2,3},{3,2},{4,5},{5,4},{6,7},{7,6},{8,9},{9,8},{10,11... | collective-permute-start | bytes 196616 | tf_op jit(solution)/shard_map/ppermute | solution.py:512
  63.6 2.8 %collective-permute-start.23 = (bf16[2,32,512]{2,1,0:T(8,128)(2,1)S(1)}, bf16[2,32,512]{2,1,0:T(8,128)(2,1)S(1)}, u32[]{:S(2)}, u32[]{:S(2)}) collective-permute-start(bf16[2,32,512]{2,1,0:T(8,128)(2,1)S(1)} %collective-permute-done.15.refs_1_), channel_id=1, source_target_pairs={{0,1},{1,0},{2,3},{3,2},{4,5},{5,4},{6,7},{7,6},{8,9},{9,8},{10,11... | collective-permute-start | bytes 196616 | tf_op jit(solution)/shard_map/ppermute | solution.py:512
  (11 other events, 92.8 us)

commit v14 on v13

--- a/solution.py
+++ b/solution.py
@@ -64,18 +64,86 @@
         out_ref[start : start + step, :] = half_norm(in_ref[start : start + step, :])
 
 
-def half_norm_of(inputs, work):
+def half_norm_of(inputs):
     return pl.pallas_call(
         half_norm_kernel,
         in_specs=[vmem()],
         out_specs=vmem(),
         out_shape=jax.ShapeDtypeStruct(inputs.shape, jnp.bfloat16),
-        compiler_params=pltpu.CompilerParams(vmem_limit_bytes=2 * MIB),
+        compiler_params=pltpu.CompilerParams(vmem_limit_bytes=4 * MIB),
         cost_estimate=pl.CostEstimate(
-            flops=work, bytes_accessed=6 * inputs.size, transcendentals=inputs.shape[0]
+            flops=10**9, bytes_accessed=6 * inputs.size, transcendentals=inputs.shape[0]
         ),
         name="half_norm",
     )(inputs)
+
+
+def choose(condition, one, two):
+    flags = jnp.full((one.shape[0], 1), condition, jnp.int32) == 1
+    return jnp.where(flags, one.astype(jnp.float32), two.astype(jnp.float32)).astype(one.dtype)
+
+
+def edges_kernel(place_ref, top_ref, bottom_ref, one_ref, two_ref):
+    odd = place_ref[1]
+    top, bottom = half_norm(top_ref[...]), half_norm(bottom_ref[...])
+    one_ref[...] = choose(odd, top, bottom)
+    two_ref[...] = choose(odd, bottom, top)
+
+
+def row_edges(place, top, bottom):
+    return pl.pallas_call(
+        edges_kernel,
+        in_specs=[pl.BlockSpec(memory_space=pltpu.SMEM)] + [vmem()] * 2,
+        out_specs=[vmem()] * 2,
+        out_shape=[jax.ShapeDtypeStruct(top.shape, jnp.bfloat16)] * 2,
+        compiler_params=pltpu.CompilerParams(vmem_limit_bytes=4 * MIB),
+        cost_estimate=pl.CostEstimate(
+            flops=10**10, bytes_accessed=12 * top.size, transcendentals=2 * top.shape[0]
+        ),
+        name="row_edges",
+    )(place, top, bottom)
+
+
+def picker(shape, pick):
+    row = lax.broadcasted_iota(jnp.int32, shape, 0)
+    column = lax.broadcasted_iota(jnp.int32, shape, 1)
+    return jnp.where(pick(row, column), 1.0, 0.0).astype(jnp.bfloat16)
+
+
+def strips_kernel(place_ref, normed_ref, row_one_ref, row_two_ref, up_ref, down_ref, one_ref, two_ref):
+    tokens = normed_ref.shape[0]
+    cols = up_ref.shape[0]
+    rows = tokens // cols
+    slot = one_ref.shape[0]
+    odd_row, odd_col = place_ref[1], place_ref[2]
+    up = choose(odd_row, row_one_ref[...], row_two_ref[...])
+    down = choose(odd_row, row_two_ref[...], row_one_ref[...])
+    up_ref[...] = up
+    down_ref[...] = down
+    strips = []
+    for x in (0, cols - 1):
+        body = picker(
+            (slot, tokens), lambda i, j: (i >= 1) & (i <= rows) & (j == (i - 1) * cols + x)
+        )
+        head = picker((slot, cols), lambda i, j: (i == 0) & (j == x))
+        foot = picker((slot, cols), lambda i, j: (i == rows + 1) & (j == x))
+        strip = matmul(body, normed_ref[...]) + matmul(head, up) + matmul(foot, down)
+        strips.append(strip.astype(jnp.bfloat16))
+    one_ref[...] = choose(odd_col, strips[0], strips[1])
+    two_ref[...] = choose(odd_col, strips[1], strips[0])
+
+
+def column_strips(place, normed, row_one, row_two, slot):
+    cols, channels = row_one.shape
+    shapes = [(cols, channels)] * 2 + [(slot, channels)] * 2
+    return pl.pallas_call(
+        strips_kernel,
+        in_specs=[pl.BlockSpec(memory_space=pltpu.SMEM)] + [vmem()] * 3,
+        out_specs=[vmem()] * 4,
+        out_shape=[jax.ShapeDtypeStruct(shape, jnp.bfloat16) for shape in shapes],
+        compiler_params=pltpu.CompilerParams(vmem_limit_bytes=4 * MIB),
+        name="column_strips",
+    )(place, normed, row_one, row_two)
 
 
 def padded_rows(tokens):
@@ -124,7 +192,7 @@
 
 
 def mix_kernel(
-    own_ref, expanded_ref, field_ref, up_ref, down_ref, left_ref, right_ref, w_expand_ref, depth_ref,
+    place_ref, expanded_ref, field_ref, up_ref, down_ref, one_ref, two_ref, w_expand_ref, depth_ref,
     w_project_ref, perm_ref, mixed_ref, *refs, rows, cols, plan, size,
 ):
     masks, _, sides = plan
@@ -134,13 +202,14 @@
     tokens = rows * cols
     width = w_expand_ref.shape[1]
     tile = even_ref.shape[1]
-    slot = left_ref.shape[0]
+    slot = one_ref.shape[0]
     up_start, down_start, left_start = 8, 16 + cols, 24 + 2 * cols
     right_start = left_start + slot
 
-    edges = jnp.concatenate(
-        [up_ref[...], down_ref[...], left_ref[...], right_ref[...]], axis=0
-    )
+    odd_col = place_ref[2]
+    left = choose(odd_col, one_ref[...], two_ref[...])
+    right = choose(odd_col, two_ref[...], one_ref[...])
+    edges = jnp.concatenate([up_ref[...], down_ref[...], left, right], axis=0)
 
     def expand_halo(index, out_ref):
         lanes = pl.ds(pl.multiple_of(index * tile, tile), tile)
@@ -224,20 +293,20 @@
     grouped_ref[...] = matmul(perm_ref[...], normed_ref[...]).astype(jnp.bfloat16)
     for index, mask in enumerate(masks):
         for side in range(sides):
-            start = pl.multiple_of((own_ref[0] ^ (mask | side)) * size, 16)
+            start = pl.multiple_of((place_ref[0] ^ (mask | side)) * size, 16)
             write_block(
                 plan, slab_refs, index, side, slice(None), grouped_ref[pl.ds(start, size), :]
             )
 
 
 def mix(
-    own, plan, size, expanded, field, up, down, left, right, w_expand, depth_kernel, w_project, perm,
+    place, plan, size, expanded, field, up, down, one, two, w_expand, depth_kernel, w_project, perm,
     rows, cols,
 ):
     tokens, channels = field.shape
     width = w_expand.shape[1]
     tile = divisor(width // 2, 256, LANES)
-    slot = left.shape[0]
+    slot = one.shape[0]
     sent = outgoing_shapes(plan, size, channels)
     halo = pltpu.VMEM((tile // LANES, 24 + 2 * cols + 2 * slot, LANES), jnp.float32)
     return pl.pallas_call(
@@ -262,7 +331,7 @@
             transcendentals=tokens * width,
         ),
         name="mix",
-    )(own, expanded, field, up, down, left, right, w_expand, depth_kernel, w_project, perm)
+    )(place, expanded, field, up, down, one, two, w_expand, depth_kernel, w_project, perm)
 
 
 def identity(size):
@@ -383,7 +452,7 @@
     )(*incoming, w_qkv)
 
 
-def finish_kernel(own_ref, *refs, plan):
+def finish_kernel(place_ref, *refs, plan):
     masks, _, sides = plan
     in_refs, rest = refs[:-7], refs[-7:]
     back_ref, weight_ref, mixed_ref, out_ref, attended_ref, made_ref, sent = rest
@@ -391,7 +460,7 @@
     size = in_refs[0].shape[1]
     for index, mask in enumerate(masks):
         for side in range(sides):
-            start = pl.multiple_of((own_ref[0] ^ (mask | side)) * size, 16)
+            start = pl.multiple_of((place_ref[0] ^ (mask | side)) * size, 16)
             attended_ref[pl.ds(start, size), :] = read_block(
                 plan, in_refs, index, side, slice(None)
             )
@@ -410,7 +479,7 @@
         copy.wait()
 
 
-def finish(own, plan, incoming, back, w_out, mixed):
+def finish(place, plan, incoming, back, w_out, mixed):
     tokens, channels = mixed.shape
     step = divisor(tokens, 128, 16)
     return pl.pallas_call(
@@ -425,20 +494,12 @@
         ],
         compiler_params=pltpu.CompilerParams(vmem_limit_bytes=6 * MIB),
         name="finish",
-    )(own, *incoming, back, w_out, mixed)
-
-
-def exchange(low_edge, high_edge, axis):
-    count = lax.axis_size(axis)
-    even = lax.axis_index(axis) % 2 == 0
-
-    def swap(edge, start):
-        pairs = [(i, i + 1) for i in range(start, count - 1, 2)]
-        return lax.ppermute(edge, axis, pairs + [(b, a) for a, b in pairs])
-
-    one = swap(jnp.where(even, high_edge, low_edge), 0)
-    two = swap(jnp.where(even, low_edge, high_edge), 1)
-    return jnp.where(even, two, one), jnp.where(even, one, two)
+    )(place, *incoming, back, w_out, mixed)
+
+
+def swap_pairs(edge, axis, start):
+    pairs = [(i, i + 1) for i in range(start, lax.axis_size(axis) - 1, 2)]
+    return lax.ppermute(edge, axis, pairs + [(b, a) for a, b in pairs])
 
 
 def exchange_plan(row_devices, col_devices):
@@ -559,26 +620,23 @@
     back = jnp.asarray(matrix.T, jnp.bfloat16)
 
     flat = field.reshape(tokens, channels)
-    edges = half_norm_of(jnp.concatenate([field[0], field[rows - 1]], axis=0), 10**10)
-    up, down = exchange(edges[:cols], edges[cols:], "row")
-    normed = half_norm_of(flat, 10**9)
+    pairwise = 8 <= devices <= 16 and devices & (devices - 1) == 0 and col_devices % 2 == 0
+    plan = exchange_plan(row_devices, col_devices) if pairwise else ([0], 0, 1)
+    row, col = lax.axis_index("row"), lax.axis_index("col")
+    own = row * col_devices + col if pairwise else row * 0
+    place = jnp.stack([own, row % 2, col % 2]).astype(jnp.int32)
+
+    one, two = row_edges(place, field[0], field[rows - 1])
+    one, two = swap_pairs(one, "row", 0), swap_pairs(two, "row", 1)
+    normed = half_norm_of(flat)
     expanded = expand(normed, w_expand)
-    up, down, normed, expanded = lax.optimization_barrier((up, down, normed, expanded))
-    tile = normed.reshape(rows, cols, channels)
-    spare = round_up(rows + 2, 16) - rows - 2
-    first = jnp.concatenate([up[:1], tile[:, 0], down[:1], up[:spare]], axis=0)
-    last = jnp.concatenate([up[cols - 1 :], tile[:, cols - 1], down[cols - 1 :], up[:spare]], axis=0)
-    left, right = exchange(first, last, "col")
-    pairwise = 8 <= devices <= 16 and devices & (devices - 1) == 0 and col_devices % 2 == 0
-    if pairwise:
-        plan = exchange_plan(row_devices, col_devices)
-        own = lax.axis_index(("row", "col")).reshape(1)
-    else:
-        plan = [0], 0, 1
-        own = jnp.zeros(1, jnp.int32)
+    one, two, normed, expanded = lax.optimization_barrier((one, two, normed, expanded))
+    up, down, one, two = column_strips(place, normed, one, two, round_up(rows + 2, 16))
+    one, two = swap_pairs(one, "col", 0), swap_pairs(two, "col", 1)
+
     size = tokens // (len(plan[0]) * plan[2])
     mixed, *outgoing = mix(
-        own, plan, size, expanded, flat, up, down, left, right, w_expand, depth_kernel, w_project,
+        place, plan, size, expanded, flat, up, down, one, two, w_expand, depth_kernel, w_project,
         perm, rows, cols,
     )
 
@@ -588,7 +646,7 @@
         return trade_all(outgoing, sets_local, members, outward)
 
     outgoing = attend(plan, route(outgoing, True), w_qkv, sets_local)
-    final = finish(own, plan, route(outgoing, False), back, w_out, mixed)
+    final = finish(place, plan, route(outgoing, False), back, w_out, mixed)
     return final.reshape(rows, cols, channels)
 
 

time: 68.6 us -> 61.7 us (0.90)
  local copies, waits for them, and re-layouts: 9.63 us -> 0.93 us
  Pallas kernels: 15 us -> 17.5 us
  starting transfers between devices: 37.3 us -> 35.9 us
  waiting for transfers between devices: 6.03 us -> 6.81 us
    unnamed x22 -> x16, local copies, waits for them, and re-layouts: 7.7 us -> 0.05 us
    pallas_call x0 -> x2, Pallas kernels: none -> 1.61 us  [the longest x1 0.88 us: column_strips(): pl.pallas_call(strips_kernel, in_specs=[pl.BlockSpec(memory_space=pltpu.S...]
    ppermute x20, starting transfers between devices: 32.8 us -> 31.5 us  [swap(): lax.ppermute(slab, ('row', 'col'), [(i, i ^ mask) for i in range(devices)])]
    slice x3 -> x0, local copies, waits for them, and re-layouts: 1.04 us -> none  [the longest x1 1.03 us: shards(): tile[:, cols - 1]]
    ppermute x20, waiting for transfers between devices: 5.5 us -> 6.28 us  [swap(): lax.ppermute(slab, ('row', 'col'), [(i, i ^ mask) for i in range(devices)])]
where the time goes in v14:
time: 61.7 us; the launch traced here: 61.5 us
  starting transfers between devices  35.9 us (58%)
  Pallas kernels  17.5 us (28%)
  waiting for transfers between devices  6.81 us (11%)
  local copies, waits for them, and re-layouts  0.93 us (2%)
    ppermute x20, starting transfers between devices, swap(): lax.ppermute(slab, ('row', 'col'), [(i, i ^ mask) for i in range(devices)])  31.5 us
    pallas_call x1, Pallas kernels, mix(): pl.pallas_call(functools.partial(mix_kernel, rows=rows, cols=cols, plan=p...  6.29 us
    ppermute x20, waiting for transfers between devices, swap(): lax.ppermute(slab, ('row', 'col'), [(i, i ^ mask) for i in range(devices)])  6.28 us
    pallas_call x1, Pallas kernels, attend(): pl.pallas_call(functools.partial(attend_kernel, plan=plan, sets=sets, cam...  4.58 us
    ppermute x4, starting transfers between devices, swap_pairs(): return lax.ppermute(edge, axis, pairs + [(b, a) for a, b in pairs])  4.47 us
    pallas_call x1, Pallas kernels, finish(): pl.pallas_call(functools.partial(finish_kernel, plan=plan), in_specs=[pl....  2.48 us
    pallas_call x1, Pallas kernels, expand(): pl.pallas_call(expand_kernel, in_specs=[vmem()] * 2, out_specs=vmem(), ou...  2.18 us
  transfers between devices with their start and end apart: 24, of which 6 were waited for; matrix products, arithmetic and copies ran while one was open for 0% of the time, Pallas kernels for 4%

profile of v14, /device:TPU:0, one launch (start us, length us, event | category | flops | bytes accessed | tf_op | source)
XLA Modules:
  0.0 61.5 jit_solution(11636601872385170646)
XLA Ops:
  0.0 0.9 %slice_bitcast_fusion = (f32[32,512]{1,0:T(8,128)S(1)}, f32[32,512]{1,0:T(8,128)S(1)}) fusion(f32[16,32,512]{2,1,0:T(8,128)} %param.8), kind=kLoop, calls=%fused_computation | loop fusion | bytes 262144 | tf_op jit(solution)/shard_map/squeeze | solution.py:629
  1.0 0.7 %row_edges.1 = (bf16[32,512]{1,0:T(8,128)(2,1)S(1)}, bf16[32,512]{1,0:T(8,128)(2,1)S(1)}) custom-call(s32[3]{0:T(128)S(1)} %pad_add_fusion.place_ref, f32[32,512]{1,0:T(8,128)S(1)} %get-tuple-element.80.top_ref, f32[32,512]{1,0:T(8,128)S(1)} %get-tuple-element.79.bottom_ref), custom_call_target="tpu_custom_call" | custom-call | flops 10000000000 | bytes 196608 | tf_op jit(solution)/shard_map/row_edges/pallas_call | solution.py:94
  1.7 3.1 %collective-permute-start = (bf16[32,512]{1,0:T(8,128)(2,1)S(1)}, bf16[32,512]{1,0:T(8,128)(2,1)S(1)}, u32[]{:S(2)}, u32[]{:S(2)}) collective-permute-start(bf16[32,512]{1,0:T(8,128)(2,1)S(1)} %get-tuple-element.42), channel_id=1, source_target_pairs={{0,4},{8,12},{4,0},{12,8},{1,5},{9,13},{5,1},{13,9},{2,6},{10,14},... | collective-permute-start | bytes 98312 | tf_op jit(solution)/shard_map/ppermute | solution.py:502
  4.8 0.7 %collective-permute-start.1 = (bf16[32,512]{1,0:T(8,128)(2,1)S(1)}, bf16[32,512]{1,0:T(8,128)(2,1)S(1)}, u32[]{:S(2)}, u32[]{:S(2)}) collective-permute-start(bf16[32,512]{1,0:T(8,128)(2,1)S(1)} %get-tuple-element.43), channel_id=1, source_target_pairs={{4,8},{8,4},{5,9},{9,5},{6,10},{10,6},{7,11},{11,7},{20,24},{24,20... | collective-permute-start | bytes 98312 | tf_op jit(solution)/shard_map/ppermute | solution.py:502
  5.9 2.2 %expand.1.expanded_ref = f32[8448,128]{1,0:T(8,128)S(1)} custom-call(bf16[512,512]{1,0:T(8,128)(2,1)S(1)} %half_norm.1.normed_ref, bf16[512,2048]{1,0:T(8,128)(2,1)S(1)} %copy-done), custom_call_target="tpu_custom_call" | custom-call | flops 10000000000 | bytes 6815744 | tf_op jit(solution)/shard_map/expand/pallas_call | solution.py:179
  8.1 0.9 %column_strips.1 = (bf16[32,512]{1,0:T(8,128)(2,1)S(1)}, bf16[32,512]{1,0:T(8,128)(2,1)S(1)}, bf16[32,512]{1,0:T(8,128)(2,1)S(1)}, bf16[32,512]{1,0:T(8,128)(2,1)S(1)}) custom-call(s32[3]{0:T(128)S(1)} %pad_add_fusion.place_ref, bf16[512,512]{1,0:T(8,128)(2,1)S(1)} %half_norm.1.normed_ref, bf16[32,512]{1,0:T(8,128)(2,1)S(1)} %collective-permute-done.row_one_ref, ...), custom_call_target="tpu_custom_call" | custom-call | tf_op jit(solution)/shard_map/column_strips/pallas_call | solution.py:139
  9.0 0.7 %collective-permute-start.3 = (bf16[32,512]{1,0:T(8,128)(2,1)S(1)}, bf16[32,512]{1,0:T(8,128)(2,1)S(1)}, u32[]{:S(2)}, u32[]{:S(2)}) collective-permute-start(bf16[32,512]{1,0:T(8,128)(2,1)S(1)} %get-tuple-element.51), channel_id=1, source_target_pairs={{1,2},{2,1},{5,6},{6,5},{9,10},{10,9},{13,14},{14,13},{17,18},{18,... | collective-permute-start | bytes 98312 | tf_op jit(solution)/shard_map/ppermute | solution.py:502
  10.3 6.3 %mix.1 = (f32[512,512]{1,0:T(8,128)S(1)}, bf16[2,32,512]{2,1,0:T(8,128)(2,1)S(1)}, bf16[2,32,512]{2,1,0:T(8,128)(2,1)S(1)}, bf16[1,32,512]{2,1,0:T(8,128)(2,1)S(...) custom-call(s32[3]{0:T(128)S(1)} %pad_add_fusion.place_ref, f32[8448,128]{1,0:T(8,128)S(1)} %expand.1.expanded_ref, ...), custom_call_target="tpu_custom_call" | custom-call | flops 1073741824 | bytes 11010048 | tf_op jit(solution)/shard_map/mix/pallas_call | solution.py:312
  16.6 4.6 %collective-permute-start.6 = (bf16[6,32,512]{2,1,0:T(8,128)(2,1)S(1)}, bf16[6,32,512]{2,1,0:T(8,128)(2,1)S(1)}, u32[]{:S(2)}, u32[]{:S(2)}) collective-permute-start(bf16[6,32,512]{2,1,0:T(8,128)(2,1)S(1)} %get-tuple-element.55), channel_id=1, source_target_pairs={{0,1},{1,0},{2,3},{3,2},{4,5},{5,4},{6,7},{7,6},{8,9},{9,8},{10,11... | collective-permute-start | bytes 589832 | tf_op jit(solution)/shard_map/ppermute | solution.py:573
  21.1 3.2 %collective-permute-start.4 = (bf16[2,32,512]{2,1,0:T(8,128)(2,1)S(1)}, bf16[2,32,512]{2,1,0:T(8,128)(2,1)S(1)}, u32[]{:S(2)}, u32[]{:S(2)}) collective-permute-start(bf16[2,32,512]{2,1,0:T(8,128)(2,1)S(1)} %get-tuple-element.52), channel_id=1, source_target_pairs={{0,14},{1,15},{2,12},{3,13},{4,10},{5,11},{6,8},{7,9},{8,6},{9,7},... | collective-permute-start | bytes 196616 | tf_op jit(solution)/shard_map/ppermute | solution.py:573
  24.4 1.2 %collective-permute-start.5 = (bf16[2,32,512]{2,1,0:T(8,128)(2,1)S(1)}, bf16[2,32,512]{2,1,0:T(8,128)(2,1)S(1)}, u32[]{:S(2)}, u32[]{:S(2)}) collective-permute-start(bf16[2,32,512]{2,1,0:T(8,128)(2,1)S(1)} %get-tuple-element.53), channel_id=1, source_target_pairs={{0,12},{1,13},{2,14},{3,15},{4,8},{5,9},{6,10},{7,11},{8,4},{9,5},... | collective-permute-start | bytes 196616 | tf_op jit(solution)/shard_map/ppermute | solution.py:573
  25.6 3.7 %collective-permute-start.7 = (bf16[2,32,512]{2,1,0:T(8,128)(2,1)S(1)}, bf16[2,32,512]{2,1,0:T(8,128)(2,1)S(1)}, u32[]{:S(2)}, u32[]{:S(2)}) collective-permute-start(bf16[2,32,512]{2,1,0:T(8,128)(2,1)S(1)} %get-tuple-element.56), channel_id=1, source_target_pairs={{0,10},{1,11},{2,8},{3,9},{4,14},{5,15},{6,12},{7,13},{8,2},{9,3},... | collective-permute-start | bytes 196616 | tf_op jit(solution)/shard_map/ppermute | solution.py:573
  29.8 2.1 %collective-permute-start.9 = (bf16[2,32,512]{2,1,0:T(8,128)(2,1)S(1)}, bf16[2,32,512]{2,1,0:T(8,128)(2,1)S(1)}, u32[]{:S(2)}, u32[]{:S(2)}) collective-permute-start(bf16[2,32,512]{2,1,0:T(8,128)(2,1)S(1)} %get-tuple-element.61), channel_id=1, source_target_pairs={{0,4},{1,5},{2,6},{3,7},{4,0},{5,1},{6,2},{7,3},{8,12},{9,13},{10,... | collective-permute-start | bytes 196616 | tf_op jit(solution)/shard_map/ppermute | solution.py:573
  31.9 0.9 %collective-permute-start.10 = (bf16[2,32,512]{2,1,0:T(8,128)(2,1)S(1)}, bf16[2,32,512]{2,1,0:T(8,128)(2,1)S(1)}, u32[]{:S(2)}, u32[]{:S(2)}) collective-permute-start(bf16[2,32,512]{2,1,0:T(8,128)(2,1)S(1)} %get-tuple-element.62), channel_id=1, source_target_pairs={{0,8},{1,9},{2,10},{3,11},{4,12},{5,13},{6,14},{7,15},{8,0},{9,1},... | collective-permute-start | bytes 196616 | tf_op jit(solution)/shard_map/ppermute | solution.py:573
  32.8 2.6 %collective-permute-start.11 = (bf16[2,32,512]{2,1,0:T(8,128)(2,1)S(1)}, bf16[2,32,512]{2,1,0:T(8,128)(2,1)S(1)}, u32[]{:S(2)}, u32[]{:S(2)}) collective-permute-start(bf16[2,32,512]{2,1,0:T(8,128)(2,1)S(1)} %get-tuple-element.63), channel_id=1, source_target_pairs={{0,2},{1,3},{2,0},{3,1},{4,6},{5,7},{6,4},{7,5},{8,10},{9,11},{10,... | collective-permute-start | bytes 196616 | tf_op jit(solution)/shard_map/ppermute | solution.py:573
  36.2 2.2 %collective-permute-done.10.refs_5_ = bf16[2,32,512]{2,1,0:T(8,128)(2,1)S(1)} collective-permute-done((bf16[2,32,512]{2,1,0:T(8,128)(2,1)S(1)}, bf16[2,32,512]{2,1,0:T(8,128)(2,1)S(1)}, u32[]{:S(2)}, u32[]{:S(2)}) %collective-permute-start.10) | collective-permute-done | bytes 65568 | tf_op jit(solution)/shard_map/ppermute | solution.py:573
  38.5 4.6 %attend.1 = (bf16[2,32,512]{2,1,0:T(8,128)(2,1)S(1)}, bf16[2,32,512]{2,1,0:T(8,128)(2,1)S(1)}, bf16[1,32,512]{2,1,0:T(8,128)(2,1)S(1)}, bf16[6,32,512]{2,1,0:T(8,128)(2,1)S(1)}, bf16[5,32,512]{2,1,0:T(8,128)(2,1)S(1)}) custom-call(bf16[2,32,512]{2,1,0:T(8,128)(2,1)S(1)} %collective-permute-done.4.refs_0_, ...), custom_call_target="tpu_custom_call" | custom-call | flops 1073741824 | bytes 2621440 | tf_op jit(solution)/shard_map/attend/pallas_call | solution.py:432
  43.1 2.6 %collective-permute-start.14 = (bf16[2,32,512]{2,1,0:T(8,128)(2,1)S(1)}, bf16[2,32,512]{2,1,0:T(8,128)(2,1)S(1)}, u32[]{:S(2)}, u32[]{:S(2)}) collective-permute-start(bf16[2,32,512]{2,1,0:T(8,128)(2,1)S(1)} %get-tuple-element.65), channel_id=1, source_target_pairs={{0,14},{1,15},{2,12},{3,13},{4,10},{5,11},{6,8},{7,9},{8,6},{9,7},... | collective-permute-start | bytes 196616 | tf_op jit(solution)/shard_map/ppermute | solution.py:573
  45.7 2.8 %collective-permute-start.15 = (bf16[2,32,512]{2,1,0:T(8,128)(2,1)S(1)}, bf16[2,32,512]{2,1,0:T(8,128)(2,1)S(1)}, u32[]{:S(2)}, u32[]{:S(2)}) collective-permute-start(bf16[2,32,512]{2,1,0:T(8,128)(2,1)S(1)} %get-tuple-element.66), channel_id=1, source_target_pairs={{0,12},{1,13},{2,14},{3,15},{4,8},{5,9},{6,10},{7,11},{8,4},{9,5},... | collective-permute-start | bytes 196616 | tf_op jit(solution)/shard_map/ppermute | solution.py:573
  48.6 2.5 %collective-permute-start.18 = (bf16[2,32,512]{2,1,0:T(8,128)(2,1)S(1)}, bf16[2,32,512]{2,1,0:T(8,128)(2,1)S(1)}, u32[]{:S(2)}, u32[]{:S(2)}) collective-permute-start(bf16[2,32,512]{2,1,0:T(8,128)(2,1)S(1)} %get-tuple-element.72), channel_id=1, source_target_pairs={{0,6},{1,7},{2,4},{3,5},{4,2},{5,3},{6,0},{7,1},{8,14},{9,15},{10,... | collective-permute-start | bytes 196616 | tf_op jit(solution)/shard_map/ppermute | solution.py:573
  51.1 3.6 %collective-permute-start.20 = (bf16[2,32,512]{2,1,0:T(8,128)(2,1)S(1)}, bf16[2,32,512]{2,1,0:T(8,128)(2,1)S(1)}, u32[]{:S(2)}, u32[]{:S(2)}) collective-permute-start(bf16[2,32,512]{2,1,0:T(8,128)(2,1)S(1)} %get-tuple-element.75), channel_id=1, source_target_pairs={{0,8},{1,9},{2,10},{3,11},{4,12},{5,13},{6,14},{7,15},{8,0},{9,1},... | collective-permute-start | bytes 196616 | tf_op jit(solution)/shard_map/ppermute | solution.py:573
  54.8 2.4 %collective-permute-done.17.refs_3_ = bf16[2,32,512]{2,1,0:T(8,128)(2,1)S(1)} collective-permute-done((bf16[2,32,512]{2,1,0:T(8,128)(2,1)S(1)}, bf16[2,32,512]{2,1,0:T(8,128)(2,1)S(1)}, u32[]{:S(2)}, u32[]{:S(2)}) %collective-permute-start.17) | collective-permute-done | bytes 65568 | tf_op jit(solution)/shard_map/ppermute | solution.py:573
  57.9 1.2 %collective-permute-done.21.refs_6_ = bf16[2,32,512]{2,1,0:T(8,128)(2,1)S(1)} collective-permute-done((bf16[2,32,512]{2,1,0:T(8,128)(2,1)S(1)}, bf16[2,32,512]{2,1,0:T(8,128)(2,1)S(1)}, u32[]{:S(2)}, u32[]{:S(2)}) %collective-permute-start.21) | collective-permute-done | bytes 65568 | tf_op jit(solution)/shard_map/ppermute | solution.py:573
  59.0 2.5 %finish.1 = f32[512,512]{1,0:T(8,128)} custom-call(s32[3]{0:T(128)S(1)} %pad_add_fusion.place_ref, bf16[2,32,512]{2,1,0:T(8,128)(2,1)S(1)} %collective-permute-done.14.refs_0_, bf16[2,32,512]{2,1,0:T(8,128)(2,1)S(1)} %collective-permute-done.15.refs_1_, bf16[2,32,512]{2,1,0:T(8,128)(2,1)S(1)} %collective-permute-done.18.refs_2_, ...), custom_call_target="tpu_custom_call" | custom-call | tf_op jit(solution)/shard_map/finish/pallas_call | solution.py:485
  (51 shorter events, 3.3 us)
Async XLA Ops:
  1.7 6.3 %collective-permute-start = (bf16[32,512]{1,0:T(8,128)(2,1)S(1)}, bf16[32,512]{1,0:T(8,128)(2,1)S(1)}, u32[]{:S(2)}, u32[]{:S(2)}) collective-permute-start(bf16[32,512]{1,0:T(8,128)(2,1)S(1)} %get-tuple-element.42), channel_id=1, source_target_pairs={{0,4},{8,12},{4,0},{12,8},{1,5},{9,13},{5,1},{13,9},{2,6},{10,14},... | collective-permute-start | bytes 98312 | tf_op jit(solution)/shard_map/ppermute | solution.py:502
  4.8 3.2 %collective-permute-start.1 = (bf16[32,512]{1,0:T(8,128)(2,1)S(1)}, bf16[32,512]{1,0:T(8,128)(2,1)S(1)}, u32[]{:S(2)}, u32[]{:S(2)}) collective-permute-start(bf16[32,512]{1,0:T(8,128)(2,1)S(1)} %get-tuple-element.43), channel_id=1, source_target_pairs={{4,8},{8,4},{5,9},{9,5},{6,10},{10,6},{7,11},{11,7},{20,24},{24,20... | collective-permute-start | bytes 98312 | tf_op jit(solution)/shard_map/ppermute | solution.py:502
  9.0 1.3 %collective-permute-start.2 = (bf16[32,512]{1,0:T(8,128)(2,1)S(1)}, bf16[32,512]{1,0:T(8,128)(2,1)S(1)}, u32[]{:S(2)}, u32[]{:S(2)}) collective-permute-start(bf16[32,512]{1,0:T(8,128)(2,1)S(1)} %get-tuple-element.50), channel_id=1, source_target_pairs={{0,1},{2,3},{1,0},{3,2},{4,5},{6,7},{5,4},{7,6},{8,9},{10,11},{9,8... | collective-permute-start | bytes 98312 | tf_op jit(solution)/shard_map/ppermute | solution.py:502
  9.0 1.2 %collective-permute-start.3 = (bf16[32,512]{1,0:T(8,128)(2,1)S(1)}, bf16[32,512]{1,0:T(8,128)(2,1)S(1)}, u32[]{:S(2)}, u32[]{:S(2)}) collective-permute-start(bf16[32,512]{1,0:T(8,128)(2,1)S(1)} %get-tuple-element.51), channel_id=1, source_target_pairs={{1,2},{2,1},{5,6},{6,5},{9,10},{10,9},{13,14},{14,13},{17,18},{18,... | collective-permute-start | bytes 98312 | tf_op jit(solution)/shard_map/ppermute | solution.py:502
  16.6 9.0 %collective-permute-start.6 = (bf16[6,32,512]{2,1,0:T(8,128)(2,1)S(1)}, bf16[6,32,512]{2,1,0:T(8,128)(2,1)S(1)}, u32[]{:S(2)}, u32[]{:S(2)}) collective-permute-start(bf16[6,32,512]{2,1,0:T(8,128)(2,1)S(1)} %get-tuple-element.55), channel_id=1, source_target_pairs={{0,1},{1,0},{2,3},{3,2},{4,5},{5,4},{6,7},{7,6},{8,9},{9,8},{10,11... | collective-permute-start | bytes 589832 | tf_op jit(solution)/shard_map/ppermute | solution.py:573
  21.1 10.7 %collective-permute-start.4 = (bf16[2,32,512]{2,1,0:T(8,128)(2,1)S(1)}, bf16[2,32,512]{2,1,0:T(8,128)(2,1)S(1)}, u32[]{:S(2)}, u32[]{:S(2)}) collective-permute-start(bf16[2,32,512]{2,1,0:T(8,128)(2,1)S(1)} %get-tuple-element.52), channel_id=1, source_target_pairs={{0,14},{1,15},{2,12},{3,13},{4,10},{5,11},{6,8},{7,9},{8,6},{9,7},... | collective-permute-start | bytes 196616 | tf_op jit(solution)/shard_map/ppermute | solution.py:573
  24.4 8.4 %collective-permute-start.5 = (bf16[2,32,512]{2,1,0:T(8,128)(2,1)S(1)}, bf16[2,32,512]{2,1,0:T(8,128)(2,1)S(1)}, u32[]{:S(2)}, u32[]{:S(2)}) collective-permute-start(bf16[2,32,512]{2,1,0:T(8,128)(2,1)S(1)} %get-tuple-element.53), channel_id=1, source_target_pairs={{0,12},{1,13},{2,14},{3,15},{4,8},{5,9},{6,10},{7,11},{8,4},{9,5},... | collective-permute-start | bytes 196616 | tf_op jit(solution)/shard_map/ppermute | solution.py:573
  25.6 10.2 %collective-permute-start.7 = (bf16[2,32,512]{2,1,0:T(8,128)(2,1)S(1)}, bf16[2,32,512]{2,1,0:T(8,128)(2,1)S(1)}, u32[]{:S(2)}, u32[]{:S(2)}) collective-permute-start(bf16[2,32,512]{2,1,0:T(8,128)(2,1)S(1)} %get-tuple-element.56), channel_id=1, source_target_pairs={{0,10},{1,11},{2,8},{3,9},{4,14},{5,15},{6,12},{7,13},{8,2},{9,3},... | collective-permute-start | bytes 196616 | tf_op jit(solution)/shard_map/ppermute | solution.py:573
  29.3 6.4 %collective-permute-start.8 = (bf16[2,32,512]{2,1,0:T(8,128)(2,1)S(1)}, bf16[2,32,512]{2,1,0:T(8,128)(2,1)S(1)}, u32[]{:S(2)}, u32[]{:S(2)}) collective-permute-start(bf16[2,32,512]{2,1,0:T(8,128)(2,1)S(1)} %get-tuple-element.59), channel_id=1, source_target_pairs={{0,6},{1,7},{2,4},{3,5},{4,2},{5,3},{6,0},{7,1},{8,14},{9,15},{10,... | collective-permute-start | bytes 196616 | tf_op jit(solution)/shard_map/ppermute | solution.py:573
  29.8 6.5 %collective-permute-start.9 = (bf16[2,32,512]{2,1,0:T(8,128)(2,1)S(1)}, bf16[2,32,512]{2,1,0:T(8,128)(2,1)S(1)}, u32[]{:S(2)}, u32[]{:S(2)}) collective-permute-start(bf16[2,32,512]{2,1,0:T(8,128)(2,1)S(1)} %get-tuple-element.61), channel_id=1, source_target_pairs={{0,4},{1,5},{2,6},{3,7},{4,0},{5,1},{6,2},{7,3},{8,12},{9,13},{10,... | collective-permute-start | bytes 196616 | tf_op jit(solution)/shard_map/ppermute | solution.py:573
  31.9 6.5 %collective-permute-start.10 = (bf16[2,32,512]{2,1,0:T(8,128)(2,1)S(1)}, bf16[2,32,512]{2,1,0:T(8,128)(2,1)S(1)}, u32[]{:S(2)}, u32[]{:S(2)}) collective-permute-start(bf16[2,32,512]{2,1,0:T(8,128)(2,1)S(1)} %get-tuple-element.62), channel_id=1, source_target_pairs={{0,8},{1,9},{2,10},{3,11},{4,12},{5,13},{6,14},{7,15},{8,0},{9,1},... | collective-permute-start | bytes 196616 | tf_op jit(solution)/shard_map/ppermute | solution.py:573
  32.8 5.7 %collective-permute-start.11 = (bf16[2,32,512]{2,1,0:T(8,128)(2,1)S(1)}, bf16[2,32,512]{2,1,0:T(8,128)(2,1)S(1)}, u32[]{:S(2)}, u32[]{:S(2)}) collective-permute-start(bf16[2,32,512]{2,1,0:T(8,128)(2,1)S(1)} %get-tuple-element.63), channel_id=1, source_target_pairs={{0,2},{1,3},{2,0},{3,1},{4,6},{5,7},{6,4},{7,5},{8,10},{9,11},{10,... | collective-permute-start | bytes 196616 | tf_op jit(solution)/shard_map/ppermute | solution.py:573
  35.7 2.7 %collective-permute-start.12 = (bf16[2,32,512]{2,1,0:T(8,128)(2,1)S(1)}, bf16[2,32,512]{2,1,0:T(8,128)(2,1)S(1)}, u32[]{:S(2)}, u32[]{:S(2)}) collective-permute-start(bf16[2,32,512]{2,1,0:T(8,128)(2,1)S(1)} %collective-permute-done.4.refs_0_), channel_id=1, source_target_pairs={{0,1},{1,0},{2,3},{3,2},{4,5},{5,4},{6,7},{7,6},{8,9},{9,8},{10,11... | collective-permute-start | bytes 196616 | tf_op jit(solution)/shard_map/ppermute | solution.py:573
  35.7 2.7 %collective-permute-start.13 = (bf16[2,32,512]{2,1,0:T(8,128)(2,1)S(1)}, bf16[2,32,512]{2,1,0:T(8,128)(2,1)S(1)}, u32[]{:S(2)}, u32[]{:S(2)}) collective-permute-start(bf16[2,32,512]{2,1,0:T(8,128)(2,1)S(1)} %collective-permute-done.5.refs_1_), channel_id=1, source_target_pairs={{0,1},{1,0},{2,3},{3,2},{4,5},{5,4},{6,7},{7,6},{8,9},{9,8},{10,11... | collective-permute-start | bytes 196616 | tf_op jit(solution)/shard_map/ppermute | solution.py:573
  43.0 5.5 %collective-permute-start.16 = (bf16[6,32,512]{2,1,0:T(8,128)(2,1)S(1)}, bf16[6,32,512]{2,1,0:T(8,128)(2,1)S(1)}, u32[]{:S(2)}, u32[]{:S(2)}) collective-permute-start(bf16[6,32,512]{2,1,0:T(8,128)(2,1)S(1)} %get-tuple-element.68), channel_id=1, source_target_pairs={{0,1},{1,0},{2,3},{3,2},{4,5},{5,4},{6,7},{7,6},{8,9},{9,8},{10,11... | collective-permute-start | bytes 589832 | tf_op jit(solution)/shard_map/ppermute | solution.py:573
  43.1 8.0 %collective-permute-start.14 = (bf16[2,32,512]{2,1,0:T(8,128)(2,1)S(1)}, bf16[2,32,512]{2,1,0:T(8,128)(2,1)S(1)}, u32[]{:S(2)}, u32[]{:S(2)}) collective-permute-start(bf16[2,32,512]{2,1,0:T(8,128)(2,1)S(1)} %get-tuple-element.65), channel_id=1, source_target_pairs={{0,14},{1,15},{2,12},{3,13},{4,10},{5,11},{6,8},{7,9},{8,6},{9,7},... | collective-permute-start | bytes 196616 | tf_op jit(solution)/shard_map/ppermute | solution.py:573
  45.7 9.0 %collective-permute-start.15 = (bf16[2,32,512]{2,1,0:T(8,128)(2,1)S(1)}, bf16[2,32,512]{2,1,0:T(8,128)(2,1)S(1)}, u32[]{:S(2)}, u32[]{:S(2)}) collective-permute-start(bf16[2,32,512]{2,1,0:T(8,128)(2,1)S(1)} %get-tuple-element.66), channel_id=1, source_target_pairs={{0,12},{1,13},{2,14},{3,15},{4,8},{5,9},{6,10},{7,11},{8,4},{9,5},... | collective-permute-start | bytes 196616 | tf_op jit(solution)/shard_map/ppermute | solution.py:573
  48.6 8.6 %collective-permute-start.17 = (bf16[2,32,512]{2,1,0:T(8,128)(2,1)S(1)}, bf16[2,32,512]{2,1,0:T(8,128)(2,1)S(1)}, u32[]{:S(2)}, u32[]{:S(2)}) collective-permute-start(bf16[2,32,512]{2,1,0:T(8,128)(2,1)S(1)} %get-tuple-element.69), channel_id=1, source_target_pairs={{0,10},{1,11},{2,8},{3,9},{4,14},{5,15},{6,12},{7,13},{8,2},{9,3},... | collective-permute-start | bytes 196616 | tf_op jit(solution)/shard_map/ppermute | solution.py:573
  48.6 8.5 %collective-permute-start.18 = (bf16[2,32,512]{2,1,0:T(8,128)(2,1)S(1)}, bf16[2,32,512]{2,1,0:T(8,128)(2,1)S(1)}, u32[]{:S(2)}, u32[]{:S(2)}) collective-permute-start(bf16[2,32,512]{2,1,0:T(8,128)(2,1)S(1)} %get-tuple-element.72), channel_id=1, source_target_pairs={{0,6},{1,7},{2,4},{3,5},{4,2},{5,3},{6,0},{7,1},{8,14},{9,15},{10,... | collective-permute-start | bytes 196616 | tf_op jit(solution)/shard_map/ppermute | solution.py:573
  51.1 6.7 %collective-permute-start.19 = (bf16[2,32,512]{2,1,0:T(8,128)(2,1)S(1)}, bf16[2,32,512]{2,1,0:T(8,128)(2,1)S(1)}, u32[]{:S(2)}, u32[]{:S(2)}) collective-permute-start(bf16[2,32,512]{2,1,0:T(8,128)(2,1)S(1)} %get-tuple-element.74), channel_id=1, source_target_pairs={{0,4},{1,5},{2,6},{3,7},{4,0},{5,1},{6,2},{7,3},{8,12},{9,13},{10,... | collective-permute-start | bytes 196616 | tf_op jit(solution)/shard_map/ppermute | solution.py:573
  51.1 6.7 %collective-permute-start.20 = (bf16[2,32,512]{2,1,0:T(8,128)(2,1)S(1)}, bf16[2,32,512]{2,1,0:T(8,128)(2,1)S(1)}, u32[]{:S(2)}, u32[]{:S(2)}) collective-permute-start(bf16[2,32,512]{2,1,0:T(8,128)(2,1)S(1)} %get-tuple-element.75), channel_id=1, source_target_pairs={{0,8},{1,9},{2,10},{3,11},{4,12},{5,13},{6,14},{7,15},{8,0},{9,1},... | collective-permute-start | bytes 196616 | tf_op jit(solution)/shard_map/ppermute | solution.py:573
  54.8 4.3 %collective-permute-start.21 = (bf16[2,32,512]{2,1,0:T(8,128)(2,1)S(1)}, bf16[2,32,512]{2,1,0:T(8,128)(2,1)S(1)}, u32[]{:S(2)}, u32[]{:S(2)}) collective-permute-start(bf16[2,32,512]{2,1,0:T(8,128)(2,1)S(1)} %get-tuple-element.76), channel_id=1, source_target_pairs={{0,2},{1,3},{2,0},{3,1},{4,6},{5,7},{6,4},{7,5},{8,10},{9,11},{10,... | collective-permute-start | bytes 196616 | tf_op jit(solution)/shard_map/ppermute | solution.py:573
  57.1 1.9 %collective-permute-start.22 = (bf16[2,32,512]{2,1,0:T(8,128)(2,1)S(1)}, bf16[2,32,512]{2,1,0:T(8,128)(2,1)S(1)}, u32[]{:S(2)}, u32[]{:S(2)}) collective-permute-start(bf16[2,32,512]{2,1,0:T(8,128)(2,1)S(1)} %collective-permute-done.14.refs_0_), channel_id=1, source_target_pairs={{0,1},{1,0},{2,3},{3,2},{4,5},{5,4},{6,7},{7,6},{8,9},{9,8},{10,11... | collective-permute-start | bytes 196616 | tf_op jit(solution)/shard_map/ppermute | solution.py:573
  57.1 1.9 %collective-permute-start.23 = (bf16[2,32,512]{2,1,0:T(8,128)(2,1)S(1)}, bf16[2,32,512]{2,1,0:T(8,128)(2,1)S(1)}, u32[]{:S(2)}, u32[]{:S(2)}) collective-permute-start(bf16[2,32,512]{2,1,0:T(8,128)(2,1)S(1)} %collective-permute-done.15.refs_1_), channel_id=1, source_target_pairs={{0,1},{1,0},{2,3},{3,2},{4,5},{5,4},{6,7},{7,6},{8,9},{9,8},{10,11... | collective-permute-start | bytes 196616 | tf_op jit(solution)/shard_map/ppermute | solution.py:573
  (8 other events, 91.2 us)

commit v15 on v14

--- a/solution.py
+++ b/solution.py
@@ -83,14 +83,14 @@
     return jnp.where(flags, one.astype(jnp.float32), two.astype(jnp.float32)).astype(one.dtype)
 
 
-def edges_kernel(place_ref, top_ref, bottom_ref, one_ref, two_ref):
-    odd = place_ref[1]
+def edges_kernel(odd_row_ref, top_ref, bottom_ref, one_ref, two_ref):
+    odd = odd_row_ref[0]
     top, bottom = half_norm(top_ref[...]), half_norm(bottom_ref[...])
     one_ref[...] = choose(odd, top, bottom)
     two_ref[...] = choose(odd, bottom, top)
 
 
-def row_edges(place, top, bottom):
+def row_edges(odd_row, top, bottom):
     return pl.pallas_call(
         edges_kernel,
         in_specs=[pl.BlockSpec(memory_space=pltpu.SMEM)] + [vmem()] * 2,
@@ -101,7 +101,7 @@
             flops=10**10, bytes_accessed=12 * top.size, transcendentals=2 * top.shape[0]
         ),
         name="row_edges",
-    )(place, top, bottom)
+    )(odd_row, top, bottom)
 
 
 def picker(shape, pick):
@@ -110,12 +110,14 @@
     return jnp.where(pick(row, column), 1.0, 0.0).astype(jnp.bfloat16)
 
 
-def strips_kernel(place_ref, normed_ref, row_one_ref, row_two_ref, up_ref, down_ref, one_ref, two_ref):
+def strips_kernel(
+    odd_row_ref, odd_col_ref, normed_ref, row_one_ref, row_two_ref, up_ref, down_ref, one_ref, two_ref
+):
     tokens = normed_ref.shape[0]
     cols = up_ref.shape[0]
     rows = tokens // cols
     slot = one_ref.shape[0]
-    odd_row, odd_col = place_ref[1], place_ref[2]
+    odd_row, odd_col = odd_row_ref[0], odd_col_ref[0]
     up = choose(odd_row, row_one_ref[...], row_two_ref[...])
     down = choose(odd_row, row_two_ref[...], row_one_ref[...])
     up_ref[...] = up
@@ -133,17 +135,17 @@
     two_ref[...] = choose(odd_col, strips[1], strips[0])
 
 
-def column_strips(place, normed, row_one, row_two, slot):
+def column_strips(odd_row, odd_col, normed, row_one, row_two, slot):
     cols, channels = row_one.shape
     shapes = [(cols, channels)] * 2 + [(slot, channels)] * 2
     return pl.pallas_call(
         strips_kernel,
-        in_specs=[pl.BlockSpec(memory_space=pltpu.SMEM)] + [vmem()] * 3,
+        in_specs=[pl.BlockSpec(memory_space=pltpu.SMEM)] * 2 + [vmem()] * 3,
         out_specs=[vmem()] * 4,
         out_shape=[jax.ShapeDtypeStruct(shape, jnp.bfloat16) for shape in shapes],
         compiler_params=pltpu.CompilerParams(vmem_limit_bytes=4 * MIB),
         name="column_strips",
-    )(place, normed, row_one, row_two)
+    )(odd_row, odd_col, normed, row_one, row_two)
 
 
 def padded_rows(tokens):
@@ -192,7 +194,7 @@
 
 
 def mix_kernel(
-    place_ref, expanded_ref, field_ref, up_ref, down_ref, one_ref, two_ref, w_expand_ref, depth_ref,
+    own_ref, odd_col_ref, expanded_ref, field_ref, up_ref, down_ref, one_ref, two_ref, w_expand_ref, depth_ref,
     w_project_ref, perm_ref, mixed_ref, *refs, rows, cols, plan, size,
 ):
     masks, _, sides = plan
@@ -206,7 +208,7 @@
     up_start, down_start, left_start = 8, 16 + cols, 24 + 2 * cols
     right_start = left_start + slot
 
-    odd_col = place_ref[2]
+    odd_col = odd_col_ref[0]
     left = choose(odd_col, one_ref[...], two_ref[...])
     right = choose(odd_col, two_ref[...], one_ref[...])
     edges = jnp.concatenate([up_ref[...], down_ref[...], left, right], axis=0)
@@ -293,15 +295,15 @@
     grouped_ref[...] = matmul(perm_ref[...], normed_ref[...]).astype(jnp.bfloat16)
     for index, mask in enumerate(masks):
         for side in range(sides):
-            start = pl.multiple_of((place_ref[0] ^ (mask | side)) * size, 16)
+            start = pl.multiple_of((own_ref[0] ^ (mask | side)) * size, 16)
             write_block(
                 plan, slab_refs, index, side, slice(None), grouped_ref[pl.ds(start, size), :]
             )
 
 
 def mix(
-    place, plan, size, expanded, field, up, down, one, two, w_expand, depth_kernel, w_project, perm,
-    rows, cols,
+    own, odd_col, plan, size, expanded, field, up, down, one, two, w_expand, depth_kernel, w_project,
+    perm, rows, cols,
 ):
     tokens, channels = field.shape
     width = w_expand.shape[1]
@@ -311,7 +313,7 @@
     halo = pltpu.VMEM((tile // LANES, 24 + 2 * cols + 2 * slot, LANES), jnp.float32)
     return pl.pallas_call(
         functools.partial(mix_kernel, rows=rows, cols=cols, plan=plan, size=size),
-        in_specs=[pl.BlockSpec(memory_space=pltpu.SMEM)] + [vmem()] * 10,
+        in_specs=[pl.BlockSpec(memory_space=pltpu.SMEM)] * 2 + [vmem()] * 10,
         out_specs=[vmem()] * (1 + len(sent)),
         out_shape=[jax.ShapeDtypeStruct((tokens, channels), jnp.float32)]
         + [jax.ShapeDtypeStruct(shape, jnp.bfloat16) for shape in sent],
@@ -331,7 +333,7 @@
             transcendentals=tokens * width,
         ),
         name="mix",
-    )(place, expanded, field, up, down, one, two, w_expand, depth_kernel, w_project, perm)
+    )(own, odd_col, expanded, field, up, down, one, two, w_expand, depth_kernel, w_project, perm)
 
 
 def identity(size):
@@ -452,7 +454,7 @@
     )(*incoming, w_qkv)
 
 
-def finish_kernel(place_ref, *refs, plan):
+def finish_kernel(own_ref, *refs, plan):
     masks, _, sides = plan
     in_refs, rest = refs[:-7], refs[-7:]
     back_ref, weight_ref, mixed_ref, out_ref, attended_ref, made_ref, sent = rest
@@ -460,7 +462,7 @@
     size = in_refs[0].shape[1]
     for index, mask in enumerate(masks):
         for side in range(sides):
-            start = pl.multiple_of((place_ref[0] ^ (mask | side)) * size, 16)
+            start = pl.multiple_of((own_ref[0] ^ (mask | side)) * size, 16)
             attended_ref[pl.ds(start, size), :] = read_block(
                 plan, in_refs, index, side, slice(None)
             )
@@ -479,7 +481,7 @@
         copy.wait()
 
 
-def finish(place, plan, incoming, back, w_out, mixed):
+def finish(own, plan, incoming, back, w_out, mixed):
     tokens, channels = mixed.shape
     step = divisor(tokens, 128, 16)
     return pl.pallas_call(
@@ -494,7 +496,7 @@
         ],
         compiler_params=pltpu.CompilerParams(vmem_limit_bytes=6 * MIB),
         name="finish",
-    )(place, *incoming, back, w_out, mixed)
+    )(own, *incoming, back, w_out, mixed)
 
 
 def swap_pairs(edge, axis, start):
@@ -623,20 +625,20 @@
     pairwise = 8 <= devices <= 16 and devices & (devices - 1) == 0 and col_devices % 2 == 0
     plan = exchange_plan(row_devices, col_devices) if pairwise else ([0], 0, 1)
     row, col = lax.axis_index("row"), lax.axis_index("col")
-    own = row * col_devices + col if pairwise else row * 0
-    place = jnp.stack([own, row % 2, col % 2]).astype(jnp.int32)
-
-    one, two = row_edges(place, field[0], field[rows - 1])
+    own = (row * col_devices + col if pairwise else row * 0).reshape(1)
+    odd_row, odd_col = (row % 2).reshape(1), (col % 2).reshape(1)
+
+    one, two = row_edges(odd_row, field[0], field[rows - 1])
     one, two = swap_pairs(one, "row", 0), swap_pairs(two, "row", 1)
     normed = half_norm_of(flat)
     expanded = expand(normed, w_expand)
     one, two, normed, expanded = lax.optimization_barrier((one, two, normed, expanded))
-    up, down, one, two = column_strips(place, normed, one, two, round_up(rows + 2, 16))
+    up, down, one, two = column_strips(odd_row, odd_col, normed, one, two, round_up(rows + 2, 16))
     one, two = swap_pairs(one, "col", 0), swap_pairs(two, "col", 1)
 
     size = tokens // (len(plan[0]) * plan[2])
     mixed, *outgoing = mix(
-        place, plan, size, expanded, flat, up, down, one, two, w_expand, depth_kernel, w_project,
+        own, odd_col, plan, size, expanded, flat, up, down, one, two, w_expand, depth_kernel, w_project,
         perm, rows, cols,
     )
 
@@ -646,7 +648,7 @@
         return trade_all(outgoing, sets_local, members, outward)
 
     outgoing = attend(plan, route(outgoing, True), w_qkv, sets_local)
-    final = finish(place, plan, route(outgoing, False), back, w_out, mixed)
+    final = finish(own, plan, route(outgoing, False), back, w_out, mixed)
     return final.reshape(rows, cols, channels)
 
 

time: 61.7 us -> 68.8 us (1.12)
  local copies, waits for them, and re-layouts: 0.93 us -> 9.6 us
  Pallas kernels: 17.5 us -> 15.3 us
  starting transfers between devices: 35.9 us -> 37.3 us
  waiting for transfers between devices: 6.81 us -> 6.03 us
    unnamed x16 -> x24, local copies, waits for them, and re-layouts: 0.05 us -> 8.72 us
    ppermute x20, starting transfers between devices: 31.5 us -> 32.9 us  [swap(): lax.ppermute(slab, ('row', 'col'), [(i, i ^ mask) for i in range(devices)])]
    ppermute x20, waiting for transfers between devices: 6.28 us -> 5.5 us  [swap(): lax.ppermute(slab, ('row', 'col'), [(i, i ^ mask) for i in range(devices)])]
where the time goes in v15:
time: 68.8 us; the launch traced here: 68.5 us
  starting transfers between devices  37.3 us (54%)
  Pallas kernels  15.3 us (22%)
  local copies, waits for them, and re-layouts  9.6 us (14%)
  waiting for transfers between devices  6.03 us (9%)
    ppermute x20, starting transfers between devices, swap(): lax.ppermute(slab, ('row', 'col'), [(i, i ^ mask) for i in range(devices)])  32.9 us
    unnamed x24, local copies, waits for them, and re-layouts  8.72 us
    pallas_call x1, Pallas kernels, mix(): pl.pallas_call(functools.partial(mix_kernel, rows=rows, cols=cols, plan=p...  5.74 us
    ppermute x20, waiting for transfers between devices, swap(): lax.ppermute(slab, ('row', 'col'), [(i, i ^ mask) for i in range(devices)])  5.5 us
    pallas_call x1, Pallas kernels, attend(): pl.pallas_call(functools.partial(attend_kernel, plan=plan, sets=sets, cam...  4.57 us
    ppermute x4, starting transfers between devices, swap_pairs(): return lax.ppermute(edge, axis, pairs + [(b, a) for a, b in pairs])  4.47 us
    pallas_call x1, Pallas kernels, expand(): pl.pallas_call(expand_kernel, in_specs=[vmem()] * 2, out_specs=vmem(), ou...  2.15 us
    pallas_call x1, Pallas kernels, finish(): pl.pallas_call(functools.partial(finish_kernel, plan=plan), in_specs=[pl....  1.94 us
  transfers between devices with their start and end apart: 24, of which 6 were waited for; matrix products, arithmetic and copies ran while one was open for 0% of the time, Pallas kernels for 4%

profile of v15, /device:TPU:0, one launch (start us, length us, event | category | flops | bytes accessed | tf_op | source)
XLA Modules:
  0.0 68.5 jit_solution(5907844416010363391)
XLA Ops:
  1.1 3.1 %collective-permute-start = (bf16[32,512]{1,0:T(8,128)(2,1)S(1)}, bf16[32,512]{1,0:T(8,128)(2,1)S(1)}, u32[]{:S(2)}, u32[]{:S(2)}) collective-permute-start(bf16[32,512]{1,0:T(8,128)(2,1)S(1)} %get-tuple-element.42), channel_id=1, source_target_pairs={{0,4},{8,12},{4,0},{12,8},{1,5},{9,13},{5,1},{13,9},{2,6},{10,14},... | collective-permute-start | bytes 98312 | tf_op jit(solution)/shard_map/ppermute | solution.py:504
  5.2 2.2 %expand.1.expanded_ref = f32[8448,128]{1,0:T(8,128)S(1)} custom-call(bf16[512,512]{1,0:T(8,128)(2,1)S(1)} %half_norm.1.normed_ref, bf16[512,2048]{1,0:T(8,128)(2,1)S(1)} %copy-done.2), custom_call_target="tpu_custom_call" | custom-call | flops 10000000000 | bytes 6815744 | tf_op jit(solution)/shard_map/expand/pallas_call | solution.py:181
  7.4 2.0 %copy-done = f32[8448,128]{1,0:T(8,128)} copy-done((f32[8448,128]{1,0:T(8,128)}, f32[8448,128]{1,0:T(8,128)S(1)}, u32[]{:S(2)}) %copy-start) | copy-done | bytes 4325400
  12.9 2.2 %copy-done.1 = f32[8448,128]{1,0:T(8,128)S(1)} copy-done((f32[8448,128]{1,0:T(8,128)S(1)}, f32[8448,128]{1,0:T(8,128)}, u32[]{:S(2)}) %copy-start.1) | copy-done | bytes 4325400
  15.1 1.6 %copy-done.3 = bf16[2048,512]{1,0:T(8,128)(2,1)S(1)} copy-done((bf16[2048,512]{1,0:T(8,128)(2,1)S(1)}, bf16[2048,512]{1,0:T(8,128)(2,1)}, u32[]{:S(2)}) %copy-start.3) | copy-done | bytes 2097176
  16.7 1.0 %copy-done.9 = bf16[512,512]{1,0:T(8,128)(2,1)S(1)} copy-done((bf16[512,512]{1,0:T(8,128)(2,1)S(1)}, bf16[512,512]{1,0:T(8,128)(2,1)}, u32[]{:S(2)}) %copy-start.9) | copy-done | bytes 524312
  17.7 5.7 %mix.1 = (f32[512,512]{1,0:T(8,128)S(1)}, bf16[2,32,512]{2,1,0:T(8,128)(2,1)S(1)}, bf16[2,32,512]{2,1,0:T(8,128)(2,1)S(1)}, bf16[1,32,512]{2,1,0:T(8,128)(2,1)S(...) custom-call(s32[1]{0:T(128)} %bitcast.own_ref, s32[1]{0:T(128)} %bitcast.1.odd_col_ref, ...), custom_call_target="tpu_custom_call" | custom-call | flops 1073741824 | bytes 11010048 | tf_op jit(solution)/shard_map/mix/pallas_call | solution.py:314
  23.5 4.6 %collective-permute-start.6 = (bf16[6,32,512]{2,1,0:T(8,128)(2,1)S(1)}, bf16[6,32,512]{2,1,0:T(8,128)(2,1)S(1)}, u32[]{:S(2)}, u32[]{:S(2)}) collective-permute-start(bf16[6,32,512]{2,1,0:T(8,128)(2,1)S(1)} %get-tuple-element.55), channel_id=1, source_target_pairs={{0,1},{1,0},{2,3},{3,2},{4,5},{5,4},{6,7},{7,6},{8,9},{9,8},{10,11... | collective-permute-start | bytes 589832 | tf_op jit(solution)/shard_map/ppermute | solution.py:575
  28.1 3.2 %collective-permute-start.4 = (bf16[2,32,512]{2,1,0:T(8,128)(2,1)S(1)}, bf16[2,32,512]{2,1,0:T(8,128)(2,1)S(1)}, u32[]{:S(2)}, u32[]{:S(2)}) collective-permute-start(bf16[2,32,512]{2,1,0:T(8,128)(2,1)S(1)} %get-tuple-element.52), channel_id=1, source_target_pairs={{0,14},{1,15},{2,12},{3,13},{4,10},{5,11},{6,8},{7,9},{8,6},{9,7},... | collective-permute-start | bytes 196616 | tf_op jit(solution)/shard_map/ppermute | solution.py:575
  31.3 1.1 %collective-permute-start.5 = (bf16[2,32,512]{2,1,0:T(8,128)(2,1)S(1)}, bf16[2,32,512]{2,1,0:T(8,128)(2,1)S(1)}, u32[]{:S(2)}, u32[]{:S(2)}) collective-permute-start(bf16[2,32,512]{2,1,0:T(8,128)(2,1)S(1)} %get-tuple-element.53), channel_id=1, source_target_pairs={{0,12},{1,13},{2,14},{3,15},{4,8},{5,9},{6,10},{7,11},{8,4},{9,5},... | collective-permute-start | bytes 196616 | tf_op jit(solution)/shard_map/ppermute | solution.py:575
  32.5 2.5 %collective-permute-start.7 = (bf16[2,32,512]{2,1,0:T(8,128)(2,1)S(1)}, bf16[2,32,512]{2,1,0:T(8,128)(2,1)S(1)}, u32[]{:S(2)}, u32[]{:S(2)}) collective-permute-start(bf16[2,32,512]{2,1,0:T(8,128)(2,1)S(1)} %get-tuple-element.56), channel_id=1, source_target_pairs={{0,10},{1,11},{2,8},{3,9},{4,14},{5,15},{6,12},{7,13},{8,2},{9,3},... | collective-permute-start | bytes 196616 | tf_op jit(solution)/shard_map/ppermute | solution.py:575
  34.9 1.8 %collective-permute-start.8 = (bf16[2,32,512]{2,1,0:T(8,128)(2,1)S(1)}, bf16[2,32,512]{2,1,0:T(8,128)(2,1)S(1)}, u32[]{:S(2)}, u32[]{:S(2)}) collective-permute-start(bf16[2,32,512]{2,1,0:T(8,128)(2,1)S(1)} %get-tuple-element.59), channel_id=1, source_target_pairs={{0,6},{1,7},{2,4},{3,5},{4,2},{5,3},{6,0},{7,1},{8,14},{9,15},{10,... | collective-permute-start | bytes 196616 | tf_op jit(solution)/shard_map/ppermute | solution.py:575
  37.5 3.5 %collective-permute-start.10 = (bf16[2,32,512]{2,1,0:T(8,128)(2,1)S(1)}, bf16[2,32,512]{2,1,0:T(8,128)(2,1)S(1)}, u32[]{:S(2)}, u32[]{:S(2)}) collective-permute-start(bf16[2,32,512]{2,1,0:T(8,128)(2,1)S(1)} %get-tuple-element.62), channel_id=1, source_target_pairs={{0,8},{1,9},{2,10},{3,11},{4,12},{5,13},{6,14},{7,15},{8,0},{9,1},... | collective-permute-start | bytes 196616 | tf_op jit(solution)/shard_map/ppermute | solution.py:575
  41.0 2.6 %collective-permute-start.11 = (bf16[2,32,512]{2,1,0:T(8,128)(2,1)S(1)}, bf16[2,32,512]{2,1,0:T(8,128)(2,1)S(1)}, u32[]{:S(2)}, u32[]{:S(2)}) collective-permute-start(bf16[2,32,512]{2,1,0:T(8,128)(2,1)S(1)} %get-tuple-element.63), channel_id=1, source_target_pairs={{0,2},{1,3},{2,0},{3,1},{4,6},{5,7},{6,4},{7,5},{8,10},{9,11},{10,... | collective-permute-start | bytes 196616 | tf_op jit(solution)/shard_map/ppermute | solution.py:575
  44.1 1.2 %collective-permute-done.10.refs_5_ = bf16[2,32,512]{2,1,0:T(8,128)(2,1)S(1)} collective-permute-done((bf16[2,32,512]{2,1,0:T(8,128)(2,1)S(1)}, bf16[2,32,512]{2,1,0:T(8,128)(2,1)S(1)}, u32[]{:S(2)}, u32[]{:S(2)}) %collective-permute-start.10) | collective-permute-done | bytes 65568 | tf_op jit(solution)/shard_map/ppermute | solution.py:575
  45.8 4.6 %attend.1 = (bf16[2,32,512]{2,1,0:T(8,128)(2,1)S(1)}, bf16[2,32,512]{2,1,0:T(8,128)(2,1)S(1)}, bf16[1,32,512]{2,1,0:T(8,128)(2,1)S(1)}, bf16[6,32,512]{2,1,0:T(8,128)(2,1)S(1)}, bf16[5,32,512]{2,1,0:T(8,128)(2,1)S(1)}) custom-call(bf16[2,32,512]{2,1,0:T(8,128)(2,1)S(1)} %collective-permute-done.4.refs_0_, ...), custom_call_target="tpu_custom_call" | custom-call | flops 1073741824 | bytes 2621440 | tf_op jit(solution)/shard_map/attend/pallas_call | solution.py:434
  50.5 2.7 %collective-permute-start.14 = (bf16[2,32,512]{2,1,0:T(8,128)(2,1)S(1)}, bf16[2,32,512]{2,1,0:T(8,128)(2,1)S(1)}, u32[]{:S(2)}, u32[]{:S(2)}) collective-permute-start(bf16[2,32,512]{2,1,0:T(8,128)(2,1)S(1)} %get-tuple-element.65), channel_id=1, source_target_pairs={{0,14},{1,15},{2,12},{3,13},{4,10},{5,11},{6,8},{7,9},{8,6},{9,7},... | collective-permute-start | bytes 196616 | tf_op jit(solution)/shard_map/ppermute | solution.py:575
  53.2 2.6 %collective-permute-start.15 = (bf16[2,32,512]{2,1,0:T(8,128)(2,1)S(1)}, bf16[2,32,512]{2,1,0:T(8,128)(2,1)S(1)}, u32[]{:S(2)}, u32[]{:S(2)}) collective-permute-start(bf16[2,32,512]{2,1,0:T(8,128)(2,1)S(1)} %get-tuple-element.66), channel_id=1, source_target_pairs={{0,12},{1,13},{2,14},{3,15},{4,8},{5,9},{6,10},{7,11},{8,4},{9,5},... | collective-permute-start | bytes 196616 | tf_op jit(solution)/shard_map/ppermute | solution.py:575
  55.9 2.7 %collective-permute-start.18 = (bf16[2,32,512]{2,1,0:T(8,128)(2,1)S(1)}, bf16[2,32,512]{2,1,0:T(8,128)(2,1)S(1)}, u32[]{:S(2)}, u32[]{:S(2)}) collective-permute-start(bf16[2,32,512]{2,1,0:T(8,128)(2,1)S(1)} %get-tuple-element.72), channel_id=1, source_target_pairs={{0,6},{1,7},{2,4},{3,5},{4,2},{5,3},{6,0},{7,1},{8,14},{9,15},{10,... | collective-permute-start | bytes 196616 | tf_op jit(solution)/shard_map/ppermute | solution.py:575
  58.6 3.7 %collective-permute-start.20 = (bf16[2,32,512]{2,1,0:T(8,128)(2,1)S(1)}, bf16[2,32,512]{2,1,0:T(8,128)(2,1)S(1)}, u32[]{:S(2)}, u32[]{:S(2)}) collective-permute-start(bf16[2,32,512]{2,1,0:T(8,128)(2,1)S(1)} %get-tuple-element.75), channel_id=1, source_target_pairs={{0,8},{1,9},{2,10},{3,11},{4,12},{5,13},{6,14},{7,15},{8,0},{9,1},... | collective-permute-start | bytes 196616 | tf_op jit(solution)/shard_map/ppermute | solution.py:575
  62.3 1.4 %collective-permute-done.17.refs_3_ = bf16[2,32,512]{2,1,0:T(8,128)(2,1)S(1)} collective-permute-done((bf16[2,32,512]{2,1,0:T(8,128)(2,1)S(1)}, bf16[2,32,512]{2,1,0:T(8,128)(2,1)S(1)}, u32[]{:S(2)}, u32[]{:S(2)}) %collective-permute-start.17) | collective-permute-done | bytes 65568 | tf_op jit(solution)/shard_map/ppermute | solution.py:575
  64.2 1.2 %collective-permute-done.19.refs_4_ = bf16[2,32,512]{2,1,0:T(8,128)(2,1)S(1)} collective-permute-done((bf16[2,32,512]{2,1,0:T(8,128)(2,1)S(1)}, bf16[2,32,512]{2,1,0:T(8,128)(2,1)S(1)}, u32[]{:S(2)}, u32[]{:S(2)}) %collective-permute-start.19) | collective-permute-done | bytes 65568 | tf_op jit(solution)/shard_map/ppermute | solution.py:575
  65.4 1.2 %collective-permute-done.21.refs_6_ = bf16[2,32,512]{2,1,0:T(8,128)(2,1)S(1)} collective-permute-done((bf16[2,32,512]{2,1,0:T(8,128)(2,1)S(1)}, bf16[2,32,512]{2,1,0:T(8,128)(2,1)S(1)}, u32[]{:S(2)}, u32[]{:S(2)}) %collective-permute-start.21) | collective-permute-done | bytes 65568 | tf_op jit(solution)/shard_map/ppermute | solution.py:575
  66.6 1.9 %finish.1 = f32[512,512]{1,0:T(8,128)} custom-call(s32[1]{0:T(128)} %bitcast.own_ref, bf16[2,32,512]{2,1,0:T(8,128)(2,1)S(1)} %collective-permute-done.14.refs_0_, bf16[2,32,512]{2,1,0:T(8,128)(2,1)S(1)} %collective-permute-done.15.refs_1_, bf16[2,32,512]{2,1,0:T(8,128)(2,1)S(1)} %collective-permute-done.18.refs_2_, ...), custom_call_target="tpu_custom_call" | custom-call | tf_op jit(solution)/shard_map/finish/pallas_call | solution.py:487
  (58 shorter events, 8.1 us)
Async XLA Ops:
  1.1 9.1 %collective-permute-start = (bf16[32,512]{1,0:T(8,128)(2,1)S(1)}, bf16[32,512]{1,0:T(8,128)(2,1)S(1)}, u32[]{:S(2)}, u32[]{:S(2)}) collective-permute-start(bf16[32,512]{1,0:T(8,128)(2,1)S(1)} %get-tuple-element.42), channel_id=1, source_target_pairs={{0,4},{8,12},{4,0},{12,8},{1,5},{9,13},{5,1},{13,9},{2,6},{10,14},... | collective-permute-start | bytes 98312 | tf_op jit(solution)/shard_map/ppermute | solution.py:504
  4.2 6.0 %collective-permute-start.1 = (bf16[32,512]{1,0:T(8,128)(2,1)S(1)}, bf16[32,512]{1,0:T(8,128)(2,1)S(1)}, u32[]{:S(2)}, u32[]{:S(2)}) collective-permute-start(bf16[32,512]{1,0:T(8,128)(2,1)S(1)} %get-tuple-element.43), channel_id=1, source_target_pairs={{4,8},{8,4},{5,9},{9,5},{6,10},{10,6},{7,11},{11,7},{20,24},{24,20... | collective-permute-start | bytes 98312 | tf_op jit(solution)/shard_map/ppermute | solution.py:504
  11.6 1.3 %collective-permute-start.2 = (bf16[32,512]{1,0:T(8,128)(2,1)S(1)}, bf16[32,512]{1,0:T(8,128)(2,1)S(1)}, u32[]{:S(2)}, u32[]{:S(2)}) collective-permute-start(bf16[32,512]{1,0:T(8,128)(2,1)S(1)} %get-tuple-element.50), channel_id=1, source_target_pairs={{0,1},{2,3},{1,0},{3,2},{4,5},{6,7},{5,4},{7,6},{8,9},{10,11},{9,8... | collective-permute-start | bytes 98312 | tf_op jit(solution)/shard_map/ppermute | solution.py:504
  11.7 1.2 %collective-permute-start.3 = (bf16[32,512]{1,0:T(8,128)(2,1)S(1)}, bf16[32,512]{1,0:T(8,128)(2,1)S(1)}, u32[]{:S(2)}, u32[]{:S(2)}) collective-permute-start(bf16[32,512]{1,0:T(8,128)(2,1)S(1)} %get-tuple-element.51), channel_id=1, source_target_pairs={{1,2},{2,1},{5,6},{6,5},{9,10},{10,9},{13,14},{14,13},{17,18},{18,... | collective-permute-start | bytes 98312 | tf_op jit(solution)/shard_map/ppermute | solution.py:504
  23.5 9.0 %collective-permute-start.6 = (bf16[6,32,512]{2,1,0:T(8,128)(2,1)S(1)}, bf16[6,32,512]{2,1,0:T(8,128)(2,1)S(1)}, u32[]{:S(2)}, u32[]{:S(2)}) collective-permute-start(bf16[6,32,512]{2,1,0:T(8,128)(2,1)S(1)} %get-tuple-element.55), channel_id=1, source_target_pairs={{0,1},{1,0},{2,3},{3,2},{4,5},{5,4},{6,7},{7,6},{8,9},{9,8},{10,11... | collective-permute-start | bytes 589832 | tf_op jit(solution)/shard_map/ppermute | solution.py:575
  28.1 9.4 %collective-permute-start.4 = (bf16[2,32,512]{2,1,0:T(8,128)(2,1)S(1)}, bf16[2,32,512]{2,1,0:T(8,128)(2,1)S(1)}, u32[]{:S(2)}, u32[]{:S(2)}) collective-permute-start(bf16[2,32,512]{2,1,0:T(8,128)(2,1)S(1)} %get-tuple-element.52), channel_id=1, source_target_pairs={{0,14},{1,15},{2,12},{3,13},{4,10},{5,11},{6,8},{7,9},{8,6},{9,7},... | collective-permute-start | bytes 196616 | tf_op jit(solution)/shard_map/ppermute | solution.py:575
  31.3 9.7 %collective-permute-start.5 = (bf16[2,32,512]{2,1,0:T(8,128)(2,1)S(1)}, bf16[2,32,512]{2,1,0:T(8,128)(2,1)S(1)}, u32[]{:S(2)}, u32[]{:S(2)}) collective-permute-start(bf16[2,32,512]{2,1,0:T(8,128)(2,1)S(1)} %get-tuple-element.53), channel_id=1, source_target_pairs={{0,12},{1,13},{2,14},{3,15},{4,8},{5,9},{6,10},{7,11},{8,4},{9,5},... | collective-permute-start | bytes 196616 | tf_op jit(solution)/shard_map/ppermute | solution.py:575
  32.5 11.1 %collective-permute-start.7 = (bf16[2,32,512]{2,1,0:T(8,128)(2,1)S(1)}, bf16[2,32,512]{2,1,0:T(8,128)(2,1)S(1)}, u32[]{:S(2)}, u32[]{:S(2)}) collective-permute-start(bf16[2,32,512]{2,1,0:T(8,128)(2,1)S(1)} %get-tuple-element.56), channel_id=1, source_target_pairs={{0,10},{1,11},{2,8},{3,9},{4,14},{5,15},{6,12},{7,13},{8,2},{9,3},... | collective-permute-start | bytes 196616 | tf_op jit(solution)/shard_map/ppermute | solution.py:575
  34.9 8.6 %collective-permute-start.8 = (bf16[2,32,512]{2,1,0:T(8,128)(2,1)S(1)}, bf16[2,32,512]{2,1,0:T(8,128)(2,1)S(1)}, u32[]{:S(2)}, u32[]{:S(2)}) collective-permute-start(bf16[2,32,512]{2,1,0:T(8,128)(2,1)S(1)} %get-tuple-element.59), channel_id=1, source_target_pairs={{0,6},{1,7},{2,4},{3,5},{4,2},{5,3},{6,0},{7,1},{8,14},{9,15},{10,... | collective-permute-start | bytes 196616 | tf_op jit(solution)/shard_map/ppermute | solution.py:575
  36.7 7.4 %collective-permute-start.9 = (bf16[2,32,512]{2,1,0:T(8,128)(2,1)S(1)}, bf16[2,32,512]{2,1,0:T(8,128)(2,1)S(1)}, u32[]{:S(2)}, u32[]{:S(2)}) collective-permute-start(bf16[2,32,512]{2,1,0:T(8,128)(2,1)S(1)} %get-tuple-element.61), channel_id=1, source_target_pairs={{0,4},{1,5},{2,6},{3,7},{4,0},{5,1},{6,2},{7,3},{8,12},{9,13},{10,... | collective-permute-start | bytes 196616 | tf_op jit(solution)/shard_map/ppermute | solution.py:575
  37.5 7.8 %collective-permute-start.10 = (bf16[2,32,512]{2,1,0:T(8,128)(2,1)S(1)}, bf16[2,32,512]{2,1,0:T(8,128)(2,1)S(1)}, u32[]{:S(2)}, u32[]{:S(2)}) collective-permute-start(bf16[2,32,512]{2,1,0:T(8,128)(2,1)S(1)} %get-tuple-element.62), channel_id=1, source_target_pairs={{0,8},{1,9},{2,10},{3,11},{4,12},{5,13},{6,14},{7,15},{8,0},{9,1},... | collective-permute-start | bytes 196616 | tf_op jit(solution)/shard_map/ppermute | solution.py:575
  41.0 4.8 %collective-permute-start.11 = (bf16[2,32,512]{2,1,0:T(8,128)(2,1)S(1)}, bf16[2,32,512]{2,1,0:T(8,128)(2,1)S(1)}, u32[]{:S(2)}, u32[]{:S(2)}) collective-permute-start(bf16[2,32,512]{2,1,0:T(8,128)(2,1)S(1)} %get-tuple-element.63), channel_id=1, source_target_pairs={{0,2},{1,3},{2,0},{3,1},{4,6},{5,7},{6,4},{7,5},{8,10},{9,11},{10,... | collective-permute-start | bytes 196616 | tf_op jit(solution)/shard_map/ppermute | solution.py:575
  43.6 2.2 %collective-permute-start.12 = (bf16[2,32,512]{2,1,0:T(8,128)(2,1)S(1)}, bf16[2,32,512]{2,1,0:T(8,128)(2,1)S(1)}, u32[]{:S(2)}, u32[]{:S(2)}) collective-permute-start(bf16[2,32,512]{2,1,0:T(8,128)(2,1)S(1)} %collective-permute-done.4.refs_0_), channel_id=1, source_target_pairs={{0,1},{1,0},{2,3},{3,2},{4,5},{5,4},{6,7},{7,6},{8,9},{9,8},{10,11... | collective-permute-start | bytes 196616 | tf_op jit(solution)/shard_map/ppermute | solution.py:575
  43.6 2.2 %collective-permute-start.13 = (bf16[2,32,512]{2,1,0:T(8,128)(2,1)S(1)}, bf16[2,32,512]{2,1,0:T(8,128)(2,1)S(1)}, u32[]{:S(2)}, u32[]{:S(2)}) collective-permute-start(bf16[2,32,512]{2,1,0:T(8,128)(2,1)S(1)} %collective-permute-done.5.refs_1_), channel_id=1, source_target_pairs={{0,1},{1,0},{2,3},{3,2},{4,5},{5,4},{6,7},{7,6},{8,9},{9,8},{10,11... | collective-permute-start | bytes 196616 | tf_op jit(solution)/shard_map/ppermute | solution.py:575
  50.4 5.4 %collective-permute-start.16 = (bf16[6,32,512]{2,1,0:T(8,128)(2,1)S(1)}, bf16[6,32,512]{2,1,0:T(8,128)(2,1)S(1)}, u32[]{:S(2)}, u32[]{:S(2)}) collective-permute-start(bf16[6,32,512]{2,1,0:T(8,128)(2,1)S(1)} %get-tuple-element.68), channel_id=1, source_target_pairs={{0,1},{1,0},{2,3},{3,2},{4,5},{5,4},{6,7},{7,6},{8,9},{9,8},{10,11... | collective-permute-start | bytes 589832 | tf_op jit(solution)/shard_map/ppermute | solution.py:575
  50.5 8.1 %collective-permute-start.14 = (bf16[2,32,512]{2,1,0:T(8,128)(2,1)S(1)}, bf16[2,32,512]{2,1,0:T(8,128)(2,1)S(1)}, u32[]{:S(2)}, u32[]{:S(2)}) collective-permute-start(bf16[2,32,512]{2,1,0:T(8,128)(2,1)S(1)} %get-tuple-element.65), channel_id=1, source_target_pairs={{0,14},{1,15},{2,12},{3,13},{4,10},{5,11},{6,8},{7,9},{8,6},{9,7},... | collective-permute-start | bytes 196616 | tf_op jit(solution)/shard_map/ppermute | solution.py:575
  53.2 9.1 %collective-permute-start.15 = (bf16[2,32,512]{2,1,0:T(8,128)(2,1)S(1)}, bf16[2,32,512]{2,1,0:T(8,128)(2,1)S(1)}, u32[]{:S(2)}, u32[]{:S(2)}) collective-permute-start(bf16[2,32,512]{2,1,0:T(8,128)(2,1)S(1)} %get-tuple-element.66), channel_id=1, source_target_pairs={{0,12},{1,13},{2,14},{3,15},{4,8},{5,9},{6,10},{7,11},{8,4},{9,5},... | collective-permute-start | bytes 196616 | tf_op jit(solution)/shard_map/ppermute | solution.py:575
  55.9 7.8 %collective-permute-start.17 = (bf16[2,32,512]{2,1,0:T(8,128)(2,1)S(1)}, bf16[2,32,512]{2,1,0:T(8,128)(2,1)S(1)}, u32[]{:S(2)}, u32[]{:S(2)}) collective-permute-start(bf16[2,32,512]{2,1,0:T(8,128)(2,1)S(1)} %get-tuple-element.69), channel_id=1, source_target_pairs={{0,10},{1,11},{2,8},{3,9},{4,14},{5,15},{6,12},{7,13},{8,2},{9,3},... | collective-permute-start | bytes 196616 | tf_op jit(solution)/shard_map/ppermute | solution.py:575
  55.9 7.8 %collective-permute-start.18 = (bf16[2,32,512]{2,1,0:T(8,128)(2,1)S(1)}, bf16[2,32,512]{2,1,0:T(8,128)(2,1)S(1)}, u32[]{:S(2)}, u32[]{:S(2)}) collective-permute-start(bf16[2,32,512]{2,1,0:T(8,128)(2,1)S(1)} %get-tuple-element.72), channel_id=1, source_target_pairs={{0,6},{1,7},{2,4},{3,5},{4,2},{5,3},{6,0},{7,1},{8,14},{9,15},{10,... | collective-permute-start | bytes 196616 | tf_op jit(solution)/shard_map/ppermute | solution.py:575
  58.6 6.8 %collective-permute-start.19 = (bf16[2,32,512]{2,1,0:T(8,128)(2,1)S(1)}, bf16[2,32,512]{2,1,0:T(8,128)(2,1)S(1)}, u32[]{:S(2)}, u32[]{:S(2)}) collective-permute-start(bf16[2,32,512]{2,1,0:T(8,128)(2,1)S(1)} %get-tuple-element.74), channel_id=1, source_target_pairs={{0,4},{1,5},{2,6},{3,7},{4,0},{5,1},{6,2},{7,3},{8,12},{9,13},{10,... | collective-permute-start | bytes 196616 | tf_op jit(solution)/shard_map/ppermute | solution.py:575
  58.6 6.8 %collective-permute-start.20 = (bf16[2,32,512]{2,1,0:T(8,128)(2,1)S(1)}, bf16[2,32,512]{2,1,0:T(8,128)(2,1)S(1)}, u32[]{:S(2)}, u32[]{:S(2)}) collective-permute-start(bf16[2,32,512]{2,1,0:T(8,128)(2,1)S(1)} %get-tuple-element.75), channel_id=1, source_target_pairs={{0,8},{1,9},{2,10},{3,11},{4,12},{5,13},{6,14},{7,15},{8,0},{9,1},... | collective-permute-start | bytes 196616 | tf_op jit(solution)/shard_map/ppermute | solution.py:575
  62.3 4.3 %collective-permute-start.21 = (bf16[2,32,512]{2,1,0:T(8,128)(2,1)S(1)}, bf16[2,32,512]{2,1,0:T(8,128)(2,1)S(1)}, u32[]{:S(2)}, u32[]{:S(2)}) collective-permute-start(bf16[2,32,512]{2,1,0:T(8,128)(2,1)S(1)} %get-tuple-element.76), channel_id=1, source_target_pairs={{0,2},{1,3},{2,0},{3,1},{4,6},{5,7},{6,4},{7,5},{8,10},{9,11},{10,... | collective-permute-start | bytes 196616 | tf_op jit(solution)/shard_map/ppermute | solution.py:575
  63.7 2.8 %collective-permute-start.22 = (bf16[2,32,512]{2,1,0:T(8,128)(2,1)S(1)}, bf16[2,32,512]{2,1,0:T(8,128)(2,1)S(1)}, u32[]{:S(2)}, u32[]{:S(2)}) collective-permute-start(bf16[2,32,512]{2,1,0:T(8,128)(2,1)S(1)} %collective-permute-done.14.refs_0_), channel_id=1, source_target_pairs={{0,1},{1,0},{2,3},{3,2},{4,5},{5,4},{6,7},{7,6},{8,9},{9,8},{10,11... | collective-permute-start | bytes 196616 | tf_op jit(solution)/shard_map/ppermute | solution.py:575
  63.7 2.8 %collective-permute-start.23 = (bf16[2,32,512]{2,1,0:T(8,128)(2,1)S(1)}, bf16[2,32,512]{2,1,0:T(8,128)(2,1)S(1)}, u32[]{:S(2)}, u32[]{:S(2)}) collective-permute-start(bf16[2,32,512]{2,1,0:T(8,128)(2,1)S(1)} %collective-permute-done.15.refs_1_), channel_id=1, source_target_pairs={{0,1},{1,0},{2,3},{3,2},{4,5},{5,4},{6,7},{7,6},{8,9},{9,8},{10,11... | collective-permute-start | bytes 196616 | tf_op jit(solution)/shard_map/ppermute | solution.py:575
  (12 other events, 94.0 us)

commit v16 on v15

--- a/solution.py
+++ b/solution.py
@@ -628,7 +628,10 @@
     own = (row * col_devices + col if pairwise else row * 0).reshape(1)
     odd_row, odd_col = (row % 2).reshape(1), (col % 2).reshape(1)
 
-    one, two = row_edges(odd_row, field[0], field[rows - 1])
+    own, odd_row, odd_col, top, bottom = lax.optimization_barrier(
+        (own, odd_row, odd_col, field[0], field[rows - 1])
+    )
+    one, two = row_edges(odd_row, top, bottom)
     one, two = swap_pairs(one, "row", 0), swap_pairs(two, "row", 1)
     normed = half_norm_of(flat)
     expanded = expand(normed, w_expand)

time: 68.8 us -> 59.5 us (0.86)
  local copies, waits for them, and re-layouts: 9.6 us -> 0.93 us
  starting transfers between devices: 37.3 us -> 35.9 us
  waiting for transfers between devices: 6.03 us -> 6.85 us
    unnamed x24 -> x16, local copies, waits for them, and re-layouts: 8.72 us -> 0.05 us
    ppermute x20, starting transfers between devices: 32.9 us -> 31.5 us  [swap(): lax.ppermute(slab, ('row', 'col'), [(i, i ^ mask) for i in range(devices)])]
    ppermute x20, waiting for transfers between devices: 5.5 us -> 6.32 us  [swap(): lax.ppermute(slab, ('row', 'col'), [(i, i ^ mask) for i in range(devices)])]
  transfers between devices with their start and end apart: 24 -> 24, of which waited for: 6 -> 7; matrix products, arithmetic and copies ran while one was open for 0% -> 0% of each run, Pallas kernels for 4% -> 4%
where the time goes in v16:
time: 59.5 us; the launch traced here: 59.3 us
  starting transfers between devices  35.9 us (60%)
  Pallas kernels  15.3 us (26%)
  waiting for transfers between devices  6.85 us (12%)
  local copies, waits for them, and re-layouts  0.93 us (2%)
    ppermute x20, starting transfers between devices, swap(): lax.ppermute(slab, ('row', 'col'), [(i, i ^ mask) for i in range(devices)])  31.5 us
    ppermute x20, waiting for transfers between devices, swap(): lax.ppermute(slab, ('row', 'col'), [(i, i ^ mask) for i in range(devices)])  6.32 us
    pallas_call x1, Pallas kernels, mix(): pl.pallas_call(functools.partial(mix_kernel, rows=rows, cols=cols, plan=p...  5.74 us
    pallas_call x1, Pallas kernels, attend(): pl.pallas_call(functools.partial(attend_kernel, plan=plan, sets=sets, cam...  4.57 us
    ppermute x4, starting transfers between devices, swap_pairs(): return lax.ppermute(edge, axis, pairs + [(b, a) for a, b in pairs])  4.47 us
    pallas_call x1, Pallas kernels, expand(): pl.pallas_call(expand_kernel, in_specs=[vmem()] * 2, out_specs=vmem(), ou...  2.15 us
    pallas_call x1, Pallas kernels, finish(): pl.pallas_call(functools.partial(finish_kernel, plan=plan), in_specs=[pl....  1.94 us
  transfers between devices with their start and end apart: 24, of which 7 were waited for; matrix products, arithmetic and copies ran while one was open for 0% of the time, Pallas kernels for 4%

profile of v16, /device:TPU:0, one launch (start us, length us, event | category | flops | bytes accessed | tf_op | source)
XLA Modules:
  0.0 59.3 jit_solution(16531444948444401318)
XLA Ops:
  0.0 0.9 %slice_bitcast_fusion = (f32[32,512]{1,0:T(8,128)S(1)}, f32[32,512]{1,0:T(8,128)S(1)}) fusion(f32[16,32,512]{2,1,0:T(8,128)} %param.8), kind=kLoop, calls=%fused_computation | loop fusion | bytes 262144 | tf_op jit(solution)/shard_map/squeeze | solution.py:632
  1.1 3.1 %collective-permute-start = (bf16[32,512]{1,0:T(8,128)(2,1)S(1)}, bf16[32,512]{1,0:T(8,128)(2,1)S(1)}, u32[]{:S(2)}, u32[]{:S(2)}) collective-permute-start(bf16[32,512]{1,0:T(8,128)(2,1)S(1)} %get-tuple-element.52), channel_id=1, source_target_pairs={{0,4},{8,12},{4,0},{12,8},{1,5},{9,13},{5,1},{13,9},{2,6},{10,14},... | collective-permute-start | bytes 98312 | tf_op jit(solution)/shard_map/ppermute | solution.py:504
  4.2 0.7 %collective-permute-start.1 = (bf16[32,512]{1,0:T(8,128)(2,1)S(1)}, bf16[32,512]{1,0:T(8,128)(2,1)S(1)}, u32[]{:S(2)}, u32[]{:S(2)}) collective-permute-start(bf16[32,512]{1,0:T(8,128)(2,1)S(1)} %get-tuple-element.53), channel_id=1, source_target_pairs={{4,8},{8,4},{5,9},{9,5},{6,10},{10,6},{7,11},{11,7},{20,24},{24,20... | collective-permute-start | bytes 98312 | tf_op jit(solution)/shard_map/ppermute | solution.py:504
  5.3 2.1 %expand.1.expanded_ref = f32[8448,128]{1,0:T(8,128)S(1)} custom-call(bf16[512,512]{1,0:T(8,128)(2,1)S(1)} %half_norm.1.normed_ref, bf16[512,2048]{1,0:T(8,128)(2,1)S(1)} %copy-done), custom_call_target="tpu_custom_call" | custom-call | flops 10000000000 | bytes 6815744 | tf_op jit(solution)/shard_map/expand/pallas_call | solution.py:181
  7.9 0.7 %collective-permute-start.3 = (bf16[32,512]{1,0:T(8,128)(2,1)S(1)}, bf16[32,512]{1,0:T(8,128)(2,1)S(1)}, u32[]{:S(2)}, u32[]{:S(2)}) collective-permute-start(bf16[32,512]{1,0:T(8,128)(2,1)S(1)} %get-tuple-element.61), channel_id=1, source_target_pairs={{1,2},{2,1},{5,6},{6,5},{9,10},{10,9},{13,14},{14,13},{17,18},{18,... | collective-permute-start | bytes 98312 | tf_op jit(solution)/shard_map/ppermute | solution.py:504
  8.5 0.5 collective-permute-done.2.one_ref
  9.1 5.7 %mix.1 = (f32[512,512]{1,0:T(8,128)S(1)}, bf16[2,32,512]{2,1,0:T(8,128)(2,1)S(1)}, bf16[2,32,512]{2,1,0:T(8,128)(2,1)S(1)}, bf16[1,32,512]{2,1,0:T(8,128)(2,1)S(...) custom-call(s32[1]{0:T(128)} %bitcast.own_ref, s32[1]{0:T(128)} %bitcast.2.odd_col_ref, ...), custom_call_target="tpu_custom_call" | custom-call | flops 1073741824 | bytes 11010048 | tf_op jit(solution)/shard_map/mix/pallas_call | solution.py:314
  14.8 4.6 %collective-permute-start.6 = (bf16[6,32,512]{2,1,0:T(8,128)(2,1)S(1)}, bf16[6,32,512]{2,1,0:T(8,128)(2,1)S(1)}, u32[]{:S(2)}, u32[]{:S(2)}) collective-permute-start(bf16[6,32,512]{2,1,0:T(8,128)(2,1)S(1)} %get-tuple-element.65), channel_id=1, source_target_pairs={{0,1},{1,0},{2,3},{3,2},{4,5},{5,4},{6,7},{7,6},{8,9},{9,8},{10,11... | collective-permute-start | bytes 589832 | tf_op jit(solution)/shard_map/ppermute | solution.py:575
  19.4 3.3 %collective-permute-start.4 = (bf16[2,32,512]{2,1,0:T(8,128)(2,1)S(1)}, bf16[2,32,512]{2,1,0:T(8,128)(2,1)S(1)}, u32[]{:S(2)}, u32[]{:S(2)}) collective-permute-start(bf16[2,32,512]{2,1,0:T(8,128)(2,1)S(1)} %get-tuple-element.62), channel_id=1, source_target_pairs={{0,14},{1,15},{2,12},{3,13},{4,10},{5,11},{6,8},{7,9},{8,6},{9,7},... | collective-permute-start | bytes 196616 | tf_op jit(solution)/shard_map/ppermute | solution.py:575
  22.7 1.1 %collective-permute-start.5 = (bf16[2,32,512]{2,1,0:T(8,128)(2,1)S(1)}, bf16[2,32,512]{2,1,0:T(8,128)(2,1)S(1)}, u32[]{:S(2)}, u32[]{:S(2)}) collective-permute-start(bf16[2,32,512]{2,1,0:T(8,128)(2,1)S(1)} %get-tuple-element.63), channel_id=1, source_target_pairs={{0,12},{1,13},{2,14},{3,15},{4,8},{5,9},{6,10},{7,11},{8,4},{9,5},... | collective-permute-start | bytes 196616 | tf_op jit(solution)/shard_map/ppermute | solution.py:575
  23.8 3.8 %collective-permute-start.7 = (bf16[2,32,512]{2,1,0:T(8,128)(2,1)S(1)}, bf16[2,32,512]{2,1,0:T(8,128)(2,1)S(1)}, u32[]{:S(2)}, u32[]{:S(2)}) collective-permute-start(bf16[2,32,512]{2,1,0:T(8,128)(2,1)S(1)} %get-tuple-element.66), channel_id=1, source_target_pairs={{0,10},{1,11},{2,8},{3,9},{4,14},{5,15},{6,12},{7,13},{8,2},{9,3},... | collective-permute-start | bytes 196616 | tf_op jit(solution)/shard_map/ppermute | solution.py:575
  28.1 2.1 %collective-permute-start.9 = (bf16[2,32,512]{2,1,0:T(8,128)(2,1)S(1)}, bf16[2,32,512]{2,1,0:T(8,128)(2,1)S(1)}, u32[]{:S(2)}, u32[]{:S(2)}) collective-permute-start(bf16[2,32,512]{2,1,0:T(8,128)(2,1)S(1)} %get-tuple-element.71), channel_id=1, source_target_pairs={{0,4},{1,5},{2,6},{3,7},{4,0},{5,1},{6,2},{7,3},{8,12},{9,13},{10,... | collective-permute-start | bytes 196616 | tf_op jit(solution)/shard_map/ppermute | solution.py:575
  30.2 0.9 %collective-permute-start.10 = (bf16[2,32,512]{2,1,0:T(8,128)(2,1)S(1)}, bf16[2,32,512]{2,1,0:T(8,128)(2,1)S(1)}, u32[]{:S(2)}, u32[]{:S(2)}) collective-permute-start(bf16[2,32,512]{2,1,0:T(8,128)(2,1)S(1)} %get-tuple-element.72), channel_id=1, source_target_pairs={{0,8},{1,9},{2,10},{3,11},{4,12},{5,13},{6,14},{7,15},{8,0},{9,1},... | collective-permute-start | bytes 196616 | tf_op jit(solution)/shard_map/ppermute | solution.py:575
  31.0 2.7 %collective-permute-start.11 = (bf16[2,32,512]{2,1,0:T(8,128)(2,1)S(1)}, bf16[2,32,512]{2,1,0:T(8,128)(2,1)S(1)}, u32[]{:S(2)}, u32[]{:S(2)}) collective-permute-start(bf16[2,32,512]{2,1,0:T(8,128)(2,1)S(1)} %get-tuple-element.73), channel_id=1, source_target_pairs={{0,2},{1,3},{2,0},{3,1},{4,6},{5,7},{6,4},{7,5},{8,10},{9,11},{10,... | collective-permute-start | bytes 196616 | tf_op jit(solution)/shard_map/ppermute | solution.py:575
  34.5 2.2 %collective-permute-done.10.refs_5_ = bf16[2,32,512]{2,1,0:T(8,128)(2,1)S(1)} collective-permute-done((bf16[2,32,512]{2,1,0:T(8,128)(2,1)S(1)}, bf16[2,32,512]{2,1,0:T(8,128)(2,1)S(1)}, u32[]{:S(2)}, u32[]{:S(2)}) %collective-permute-start.10) | collective-permute-done | bytes 65568 | tf_op jit(solution)/shard_map/ppermute | solution.py:575
  36.7 4.6 %attend.1 = (bf16[2,32,512]{2,1,0:T(8,128)(2,1)S(1)}, bf16[2,32,512]{2,1,0:T(8,128)(2,1)S(1)}, bf16[1,32,512]{2,1,0:T(8,128)(2,1)S(1)}, bf16[6,32,512]{2,1,0:T(8,128)(2,1)S(1)}, bf16[5,32,512]{2,1,0:T(8,128)(2,1)S(1)}) custom-call(bf16[2,32,512]{2,1,0:T(8,128)(2,1)S(1)} %collective-permute-done.4.refs_0_, ...), custom_call_target="tpu_custom_call" | custom-call | flops 1073741824 | bytes 2621440 | tf_op jit(solution)/shard_map/attend/pallas_call | solution.py:434
  41.4 2.6 %collective-permute-start.14 = (bf16[2,32,512]{2,1,0:T(8,128)(2,1)S(1)}, bf16[2,32,512]{2,1,0:T(8,128)(2,1)S(1)}, u32[]{:S(2)}, u32[]{:S(2)}) collective-permute-start(bf16[2,32,512]{2,1,0:T(8,128)(2,1)S(1)} %get-tuple-element.75), channel_id=1, source_target_pairs={{0,14},{1,15},{2,12},{3,13},{4,10},{5,11},{6,8},{7,9},{8,6},{9,7},... | collective-permute-start | bytes 196616 | tf_op jit(solution)/shard_map/ppermute | solution.py:575
  44.0 2.8 %collective-permute-start.15 = (bf16[2,32,512]{2,1,0:T(8,128)(2,1)S(1)}, bf16[2,32,512]{2,1,0:T(8,128)(2,1)S(1)}, u32[]{:S(2)}, u32[]{:S(2)}) collective-permute-start(bf16[2,32,512]{2,1,0:T(8,128)(2,1)S(1)} %get-tuple-element.76), channel_id=1, source_target_pairs={{0,12},{1,13},{2,14},{3,15},{4,8},{5,9},{6,10},{7,11},{8,4},{9,5},... | collective-permute-start | bytes 196616 | tf_op jit(solution)/shard_map/ppermute | solution.py:575
  46.9 2.5 %collective-permute-start.18 = (bf16[2,32,512]{2,1,0:T(8,128)(2,1)S(1)}, bf16[2,32,512]{2,1,0:T(8,128)(2,1)S(1)}, u32[]{:S(2)}, u32[]{:S(2)}) collective-permute-start(bf16[2,32,512]{2,1,0:T(8,128)(2,1)S(1)} %get-tuple-element.82), channel_id=1, source_target_pairs={{0,6},{1,7},{2,4},{3,5},{4,2},{5,3},{6,0},{7,1},{8,14},{9,15},{10,... | collective-permute-start | bytes 196616 | tf_op jit(solution)/shard_map/ppermute | solution.py:575
  49.4 3.7 %collective-permute-start.20 = (bf16[2,32,512]{2,1,0:T(8,128)(2,1)S(1)}, bf16[2,32,512]{2,1,0:T(8,128)(2,1)S(1)}, u32[]{:S(2)}, u32[]{:S(2)}) collective-permute-start(bf16[2,32,512]{2,1,0:T(8,128)(2,1)S(1)} %get-tuple-element.85), channel_id=1, source_target_pairs={{0,8},{1,9},{2,10},{3,11},{4,12},{5,13},{6,14},{7,15},{8,0},{9,1},... | collective-permute-start | bytes 196616 | tf_op jit(solution)/shard_map/ppermute | solution.py:575
  53.1 2.4 %collective-permute-done.17.refs_3_ = bf16[2,32,512]{2,1,0:T(8,128)(2,1)S(1)} collective-permute-done((bf16[2,32,512]{2,1,0:T(8,128)(2,1)S(1)}, bf16[2,32,512]{2,1,0:T(8,128)(2,1)S(1)}, u32[]{:S(2)}, u32[]{:S(2)}) %collective-permute-start.17) | collective-permute-done | bytes 65568 | tf_op jit(solution)/shard_map/ppermute | solution.py:575
  55.4 0.5 collective-permute-start.23
  56.1 1.2 %collective-permute-done.21.refs_6_ = bf16[2,32,512]{2,1,0:T(8,128)(2,1)S(1)} collective-permute-done((bf16[2,32,512]{2,1,0:T(8,128)(2,1)S(1)}, bf16[2,32,512]{2,1,0:T(8,128)(2,1)S(1)}, u32[]{:S(2)}, u32[]{:S(2)}) %collective-permute-start.21) | collective-permute-done | bytes 65568 | tf_op jit(solution)/shard_map/ppermute | solution.py:575
  57.3 1.9 %finish.1 = f32[512,512]{1,0:T(8,128)} custom-call(s32[1]{0:T(128)} %bitcast.own_ref, bf16[2,32,512]{2,1,0:T(8,128)(2,1)S(1)} %collective-permute-done.14.refs_0_, bf16[2,32,512]{2,1,0:T(8,128)(2,1)S(1)} %collective-permute-done.15.refs_1_, bf16[2,32,512]{2,1,0:T(8,128)(2,1)S(1)} %collective-permute-done.18.refs_2_, ...), custom_call_target="tpu_custom_call" | custom-call | tf_op jit(solution)/shard_map/finish/pallas_call | solution.py:487
  (50 shorter events, 2.7 us)
Async XLA Ops:
  1.1 6.3 %collective-permute-start = (bf16[32,512]{1,0:T(8,128)(2,1)S(1)}, bf16[32,512]{1,0:T(8,128)(2,1)S(1)}, u32[]{:S(2)}, u32[]{:S(2)}) collective-permute-start(bf16[32,512]{1,0:T(8,128)(2,1)S(1)} %get-tuple-element.52), channel_id=1, source_target_pairs={{0,4},{8,12},{4,0},{12,8},{1,5},{9,13},{5,1},{13,9},{2,6},{10,14},... | collective-permute-start | bytes 98312 | tf_op jit(solution)/shard_map/ppermute | solution.py:504
  4.2 3.2 %collective-permute-start.1 = (bf16[32,512]{1,0:T(8,128)(2,1)S(1)}, bf16[32,512]{1,0:T(8,128)(2,1)S(1)}, u32[]{:S(2)}, u32[]{:S(2)}) collective-permute-start(bf16[32,512]{1,0:T(8,128)(2,1)S(1)} %get-tuple-element.53), channel_id=1, source_target_pairs={{4,8},{8,4},{5,9},{9,5},{6,10},{10,6},{7,11},{11,7},{20,24},{24,20... | collective-permute-start | bytes 98312 | tf_op jit(solution)/shard_map/ppermute | solution.py:504
  7.8 1.3 %collective-permute-start.2 = (bf16[32,512]{1,0:T(8,128)(2,1)S(1)}, bf16[32,512]{1,0:T(8,128)(2,1)S(1)}, u32[]{:S(2)}, u32[]{:S(2)}) collective-permute-start(bf16[32,512]{1,0:T(8,128)(2,1)S(1)} %get-tuple-element.60), channel_id=1, source_target_pairs={{0,1},{2,3},{1,0},{3,2},{4,5},{6,7},{5,4},{7,6},{8,9},{10,11},{9,8... | collective-permute-start | bytes 98312 | tf_op jit(solution)/shard_map/ppermute | solution.py:504
  7.9 1.2 %collective-permute-start.3 = (bf16[32,512]{1,0:T(8,128)(2,1)S(1)}, bf16[32,512]{1,0:T(8,128)(2,1)S(1)}, u32[]{:S(2)}, u32[]{:S(2)}) collective-permute-start(bf16[32,512]{1,0:T(8,128)(2,1)S(1)} %get-tuple-element.61), channel_id=1, source_target_pairs={{1,2},{2,1},{5,6},{6,5},{9,10},{10,9},{13,14},{14,13},{17,18},{18,... | collective-permute-start | bytes 98312 | tf_op jit(solution)/shard_map/ppermute | solution.py:504
  14.8 9.0 %collective-permute-start.6 = (bf16[6,32,512]{2,1,0:T(8,128)(2,1)S(1)}, bf16[6,32,512]{2,1,0:T(8,128)(2,1)S(1)}, u32[]{:S(2)}, u32[]{:S(2)}) collective-permute-start(bf16[6,32,512]{2,1,0:T(8,128)(2,1)S(1)} %get-tuple-element.65), channel_id=1, source_target_pairs={{0,1},{1,0},{2,3},{3,2},{4,5},{5,4},{6,7},{7,6},{8,9},{9,8},{10,11... | collective-permute-start | bytes 589832 | tf_op jit(solution)/shard_map/ppermute | solution.py:575
  19.4 10.8 %collective-permute-start.4 = (bf16[2,32,512]{2,1,0:T(8,128)(2,1)S(1)}, bf16[2,32,512]{2,1,0:T(8,128)(2,1)S(1)}, u32[]{:S(2)}, u32[]{:S(2)}) collective-permute-start(bf16[2,32,512]{2,1,0:T(8,128)(2,1)S(1)} %get-tuple-element.62), channel_id=1, source_target_pairs={{0,14},{1,15},{2,12},{3,13},{4,10},{5,11},{6,8},{7,9},{8,6},{9,7},... | collective-permute-start | bytes 196616 | tf_op jit(solution)/shard_map/ppermute | solution.py:575
  22.7 8.3 %collective-permute-start.5 = (bf16[2,32,512]{2,1,0:T(8,128)(2,1)S(1)}, bf16[2,32,512]{2,1,0:T(8,128)(2,1)S(1)}, u32[]{:S(2)}, u32[]{:S(2)}) collective-permute-start(bf16[2,32,512]{2,1,0:T(8,128)(2,1)S(1)} %get-tuple-element.63), channel_id=1, source_target_pairs={{0,12},{1,13},{2,14},{3,15},{4,8},{5,9},{6,10},{7,11},{8,4},{9,5},... | collective-permute-start | bytes 196616 | tf_op jit(solution)/shard_map/ppermute | solution.py:575
  23.8 10.1 %collective-permute-start.7 = (bf16[2,32,512]{2,1,0:T(8,128)(2,1)S(1)}, bf16[2,32,512]{2,1,0:T(8,128)(2,1)S(1)}, u32[]{:S(2)}, u32[]{:S(2)}) collective-permute-start(bf16[2,32,512]{2,1,0:T(8,128)(2,1)S(1)} %get-tuple-element.66), channel_id=1, source_target_pairs={{0,10},{1,11},{2,8},{3,9},{4,14},{5,15},{6,12},{7,13},{8,2},{9,3},... | collective-permute-start | bytes 196616 | tf_op jit(solution)/shard_map/ppermute | solution.py:575
  27.6 6.4 %collective-permute-start.8 = (bf16[2,32,512]{2,1,0:T(8,128)(2,1)S(1)}, bf16[2,32,512]{2,1,0:T(8,128)(2,1)S(1)}, u32[]{:S(2)}, u32[]{:S(2)}) collective-permute-start(bf16[2,32,512]{2,1,0:T(8,128)(2,1)S(1)} %get-tuple-element.69), channel_id=1, source_target_pairs={{0,6},{1,7},{2,4},{3,5},{4,2},{5,3},{6,0},{7,1},{8,14},{9,15},{10,... | collective-permute-start | bytes 196616 | tf_op jit(solution)/shard_map/ppermute | solution.py:575
  28.1 6.4 %collective-permute-start.9 = (bf16[2,32,512]{2,1,0:T(8,128)(2,1)S(1)}, bf16[2,32,512]{2,1,0:T(8,128)(2,1)S(1)}, u32[]{:S(2)}, u32[]{:S(2)}) collective-permute-start(bf16[2,32,512]{2,1,0:T(8,128)(2,1)S(1)} %get-tuple-element.71), channel_id=1, source_target_pairs={{0,4},{1,5},{2,6},{3,7},{4,0},{5,1},{6,2},{7,3},{8,12},{9,13},{10,... | collective-permute-start | bytes 196616 | tf_op jit(solution)/shard_map/ppermute | solution.py:575
  30.2 6.5 %collective-permute-start.10 = (bf16[2,32,512]{2,1,0:T(8,128)(2,1)S(1)}, bf16[2,32,512]{2,1,0:T(8,128)(2,1)S(1)}, u32[]{:S(2)}, u32[]{:S(2)}) collective-permute-start(bf16[2,32,512]{2,1,0:T(8,128)(2,1)S(1)} %get-tuple-element.72), channel_id=1, source_target_pairs={{0,8},{1,9},{2,10},{3,11},{4,12},{5,13},{6,14},{7,15},{8,0},{9,1},... | collective-permute-start | bytes 196616 | tf_op jit(solution)/shard_map/ppermute | solution.py:575
  31.0 5.7 %collective-permute-start.11 = (bf16[2,32,512]{2,1,0:T(8,128)(2,1)S(1)}, bf16[2,32,512]{2,1,0:T(8,128)(2,1)S(1)}, u32[]{:S(2)}, u32[]{:S(2)}) collective-permute-start(bf16[2,32,512]{2,1,0:T(8,128)(2,1)S(1)} %get-tuple-element.73), channel_id=1, source_target_pairs={{0,2},{1,3},{2,0},{3,1},{4,6},{5,7},{6,4},{7,5},{8,10},{9,11},{10,... | collective-permute-start | bytes 196616 | tf_op jit(solution)/shard_map/ppermute | solution.py:575
  34.0 2.7 %collective-permute-start.12 = (bf16[2,32,512]{2,1,0:T(8,128)(2,1)S(1)}, bf16[2,32,512]{2,1,0:T(8,128)(2,1)S(1)}, u32[]{:S(2)}, u32[]{:S(2)}) collective-permute-start(bf16[2,32,512]{2,1,0:T(8,128)(2,1)S(1)} %collective-permute-done.4.refs_0_), channel_id=1, source_target_pairs={{0,1},{1,0},{2,3},{3,2},{4,5},{5,4},{6,7},{7,6},{8,9},{9,8},{10,11... | collective-permute-start | bytes 196616 | tf_op jit(solution)/shard_map/ppermute | solution.py:575
  34.0 2.7 %collective-permute-start.13 = (bf16[2,32,512]{2,1,0:T(8,128)(2,1)S(1)}, bf16[2,32,512]{2,1,0:T(8,128)(2,1)S(1)}, u32[]{:S(2)}, u32[]{:S(2)}) collective-permute-start(bf16[2,32,512]{2,1,0:T(8,128)(2,1)S(1)} %collective-permute-done.5.refs_1_), channel_id=1, source_target_pairs={{0,1},{1,0},{2,3},{3,2},{4,5},{5,4},{6,7},{7,6},{8,9},{9,8},{10,11... | collective-permute-start | bytes 196616 | tf_op jit(solution)/shard_map/ppermute | solution.py:575
  41.3 5.5 %collective-permute-start.16 = (bf16[6,32,512]{2,1,0:T(8,128)(2,1)S(1)}, bf16[6,32,512]{2,1,0:T(8,128)(2,1)S(1)}, u32[]{:S(2)}, u32[]{:S(2)}) collective-permute-start(bf16[6,32,512]{2,1,0:T(8,128)(2,1)S(1)} %get-tuple-element.78), channel_id=1, source_target_pairs={{0,1},{1,0},{2,3},{3,2},{4,5},{5,4},{6,7},{7,6},{8,9},{9,8},{10,11... | collective-permute-start | bytes 589832 | tf_op jit(solution)/shard_map/ppermute | solution.py:575
  41.4 8.0 %collective-permute-start.14 = (bf16[2,32,512]{2,1,0:T(8,128)(2,1)S(1)}, bf16[2,32,512]{2,1,0:T(8,128)(2,1)S(1)}, u32[]{:S(2)}, u32[]{:S(2)}) collective-permute-start(bf16[2,32,512]{2,1,0:T(8,128)(2,1)S(1)} %get-tuple-element.75), channel_id=1, source_target_pairs={{0,14},{1,15},{2,12},{3,13},{4,10},{5,11},{6,8},{7,9},{8,6},{9,7},... | collective-permute-start | bytes 196616 | tf_op jit(solution)/shard_map/ppermute | solution.py:575
  44.0 9.1 %collective-permute-start.15 = (bf16[2,32,512]{2,1,0:T(8,128)(2,1)S(1)}, bf16[2,32,512]{2,1,0:T(8,128)(2,1)S(1)}, u32[]{:S(2)}, u32[]{:S(2)}) collective-permute-start(bf16[2,32,512]{2,1,0:T(8,128)(2,1)S(1)} %get-tuple-element.76), channel_id=1, source_target_pairs={{0,12},{1,13},{2,14},{3,15},{4,8},{5,9},{6,10},{7,11},{8,4},{9,5},... | collective-permute-start | bytes 196616 | tf_op jit(solution)/shard_map/ppermute | solution.py:575
  46.9 8.6 %collective-permute-start.17 = (bf16[2,32,512]{2,1,0:T(8,128)(2,1)S(1)}, bf16[2,32,512]{2,1,0:T(8,128)(2,1)S(1)}, u32[]{:S(2)}, u32[]{:S(2)}) collective-permute-start(bf16[2,32,512]{2,1,0:T(8,128)(2,1)S(1)} %get-tuple-element.79), channel_id=1, source_target_pairs={{0,10},{1,11},{2,8},{3,9},{4,14},{5,15},{6,12},{7,13},{8,2},{9,3},... | collective-permute-start | bytes 196616 | tf_op jit(solution)/shard_map/ppermute | solution.py:575
  46.9 8.5 %collective-permute-start.18 = (bf16[2,32,512]{2,1,0:T(8,128)(2,1)S(1)}, bf16[2,32,512]{2,1,0:T(8,128)(2,1)S(1)}, u32[]{:S(2)}, u32[]{:S(2)}) collective-permute-start(bf16[2,32,512]{2,1,0:T(8,128)(2,1)S(1)} %get-tuple-element.82), channel_id=1, source_target_pairs={{0,6},{1,7},{2,4},{3,5},{4,2},{5,3},{6,0},{7,1},{8,14},{9,15},{10,... | collective-permute-start | bytes 196616 | tf_op jit(solution)/shard_map/ppermute | solution.py:575
  49.4 6.8 %collective-permute-start.19 = (bf16[2,32,512]{2,1,0:T(8,128)(2,1)S(1)}, bf16[2,32,512]{2,1,0:T(8,128)(2,1)S(1)}, u32[]{:S(2)}, u32[]{:S(2)}) collective-permute-start(bf16[2,32,512]{2,1,0:T(8,128)(2,1)S(1)} %get-tuple-element.84), channel_id=1, source_target_pairs={{0,4},{1,5},{2,6},{3,7},{4,0},{5,1},{6,2},{7,3},{8,12},{9,13},{10,... | collective-permute-start | bytes 196616 | tf_op jit(solution)/shard_map/ppermute | solution.py:575
  49.4 6.8 %collective-permute-start.20 = (bf16[2,32,512]{2,1,0:T(8,128)(2,1)S(1)}, bf16[2,32,512]{2,1,0:T(8,128)(2,1)S(1)}, u32[]{:S(2)}, u32[]{:S(2)}) collective-permute-start(bf16[2,32,512]{2,1,0:T(8,128)(2,1)S(1)} %get-tuple-element.85), channel_id=1, source_target_pairs={{0,8},{1,9},{2,10},{3,11},{4,12},{5,13},{6,14},{7,15},{8,0},{9,1},... | collective-permute-start | bytes 196616 | tf_op jit(solution)/shard_map/ppermute | solution.py:575
  53.1 4.3 %collective-permute-start.21 = (bf16[2,32,512]{2,1,0:T(8,128)(2,1)S(1)}, bf16[2,32,512]{2,1,0:T(8,128)(2,1)S(1)}, u32[]{:S(2)}, u32[]{:S(2)}) collective-permute-start(bf16[2,32,512]{2,1,0:T(8,128)(2,1)S(1)} %get-tuple-element.86), channel_id=1, source_target_pairs={{0,2},{1,3},{2,0},{3,1},{4,6},{5,7},{6,4},{7,5},{8,10},{9,11},{10,... | collective-permute-start | bytes 196616 | tf_op jit(solution)/shard_map/ppermute | solution.py:575
  55.4 1.9 %collective-permute-start.22 = (bf16[2,32,512]{2,1,0:T(8,128)(2,1)S(1)}, bf16[2,32,512]{2,1,0:T(8,128)(2,1)S(1)}, u32[]{:S(2)}, u32[]{:S(2)}) collective-permute-start(bf16[2,32,512]{2,1,0:T(8,128)(2,1)S(1)} %collective-permute-done.14.refs_0_), channel_id=1, source_target_pairs={{0,1},{1,0},{2,3},{3,2},{4,5},{5,4},{6,7},{7,6},{8,9},{9,8},{10,11... | collective-permute-start | bytes 196616 | tf_op jit(solution)/shard_map/ppermute | solution.py:575
  55.4 1.9 %collective-permute-start.23 = (bf16[2,32,512]{2,1,0:T(8,128)(2,1)S(1)}, bf16[2,32,512]{2,1,0:T(8,128)(2,1)S(1)}, u32[]{:S(2)}, u32[]{:S(2)}) collective-permute-start(bf16[2,32,512]{2,1,0:T(8,128)(2,1)S(1)} %collective-permute-done.15.refs_1_), channel_id=1, source_target_pairs={{0,1},{1,0},{2,3},{3,2},{4,5},{5,4},{6,7},{7,6},{8,9},{9,8},{10,11... | collective-permute-start | bytes 196616 | tf_op jit(solution)/shard_map/ppermute | solution.py:575
  (8 other events, 88.4 us)

commit v17 on v16

--- a/solution.py
+++ b/solution.py
@@ -193,105 +193,177 @@
     )(normed, w_expand)
 
 
-def mix_kernel(
-    own_ref, odd_col_ref, expanded_ref, field_ref, up_ref, down_ref, one_ref, two_ref, w_expand_ref, depth_ref,
-    w_project_ref, perm_ref, mixed_ref, *refs, rows, cols, plan, size,
+def inner_kernel(
+    expanded_ref, start_ref, depth_ref, w_project_ref, total_ref, rim_ref, even_ref, odd_ref,
+    *, rows, cols, first, count,
+):
+    tokens = rows * cols
+    tile = even_ref.shape[1]
+    subs = tile // LANES
+    position = lax.broadcasted_iota(jnp.int32, (8, LANES), 0)
+    at_first = position == 0
+    at_last = position == 7
+
+    def clear_ends(value, low, high):
+        head = jnp.where(at_first, 0.0, value[:8]) if low else value[:8]
+        foot = jnp.where(at_last, 0.0, value[-8:]) if high else value[-8:]
+        return jnp.concatenate([head, value[8:-8], foot], axis=0)
+
+    def convolve(index, out_ref):
+        for sub in range(subs):
+            chunk = (first + index) * subs + sub
+            lanes = pl.ds(pl.multiple_of(chunk * LANES, LANES), LANES)
+            base = chunk * padded_rows(tokens) + 8
+            here = index * subs + sub
+            taps = [[0.5 * depth_ref[p, q : q + 1, lanes] for q in range(3)] for p in range(3)]
+            spot = slice(sub * LANES, (sub + 1) * LANES)
+            sums = {}
+            for y in range(rows + 1):
+                if y < rows:
+                    parts = [
+                        expanded_ref[pl.ds(base + (y * cols + q), cols), :] for q in (-1, 0, 1)
+                    ]
+                    parts[0] = clear_ends(parts[0], True, False)
+                    parts[2] = clear_ends(parts[2], False, True)
+                    for p in range(3):
+                        target = y + 1 - p
+                        if 0 <= target < rows:
+                            for q in range(3):
+                                term = taps[p][q] * parts[q]
+                                sums[target] = sums[target] + term if target in sums else term
+                if y > 0:
+                    done = sums.pop(y - 1)
+                    rim_ref[here, 2 * cols + y - 1 : 2 * cols + y] = done[:1]
+                    rim_ref[here, 2 * cols + rows + y - 1 : 2 * cols + rows + y] = done[-1:]
+                    if y in (1, rows):
+                        start = 0 if y == 1 else cols
+                        rim_ref[here, start : start + cols] = done
+                        made = jnp.zeros_like(done)
+                    else:
+                        made = clear_ends(gelu_of_half(done), True, True)
+                    out_ref[(y - 1) * cols : y * cols, spot] = made.astype(jnp.bfloat16)
+
+    def project(index, in_ref, from_ref):
+        piece = pl.ds(pl.multiple_of((first + index) * tile, tile), tile)
+        total_ref[...] = from_ref[...] + matmul(in_ref[...], w_project_ref[piece, :])
+
+    convolve(0, even_ref)
+    project(0, even_ref, start_ref)
+    convolve(1, odd_ref)
+
+    def body(index, carry):
+        convolve(2 * index, even_ref)
+        project(2 * index - 1, odd_ref, total_ref)
+        convolve(2 * index + 1, odd_ref)
+        project(2 * index, even_ref, total_ref)
+        return carry
+
+    lax.fori_loop(1, count // 2, body, 0)
+    project(count - 1, odd_ref, total_ref)
+
+
+def inner(expanded, start, depth_kernel, w_project, rows, cols, first, count, tile):
+    tokens, channels = start.shape
+    rim = (count * tile // LANES, 2 * cols + 2 * rows, LANES)
+    return pl.pallas_call(
+        functools.partial(inner_kernel, rows=rows, cols=cols, first=first, count=count),
+        in_specs=[vmem()] * 4,
+        out_specs=[vmem()] * 2,
+        out_shape=[
+            jax.ShapeDtypeStruct((tokens, channels), jnp.float32),
+            jax.ShapeDtypeStruct(rim, jnp.float32),
+        ],
+        scratch_shapes=[pltpu.VMEM((tokens, tile), jnp.bfloat16)] * 2,
+        compiler_params=pltpu.CompilerParams(vmem_limit_bytes=6 * MIB),
+        cost_estimate=pl.CostEstimate(
+            flops=2 * 10**9 * count,
+            bytes_accessed=tokens * channels * 8 + tokens * count * tile * 4,
+            transcendentals=tokens * count * tile,
+        ),
+        name="inner",
+    )(expanded, start, depth_kernel, w_project)
+
+
+def rim_kernel(
+    own_ref, odd_col_ref, inner_ref, *refs, rows, cols, plan, size, pieces,
 ):
     masks, _, sides = plan
     sent = len(outgoing_shapes(plan, size, 1))
-    slab_refs = refs[:sent]
-    total_ref, normed_ref, grouped_ref, even_ref, odd_ref, even_halo_ref, odd_halo_ref = refs[sent:]
+    rim_refs, refs = refs[:pieces], refs[pieces:]
+    up_ref, down_ref, one_ref, two_ref, w_expand_ref, depth_ref, w_project_ref, perm_ref = refs[:8]
+    mixed_ref, slab_refs = refs[8], refs[9 : 9 + sent]
+    halo_ref, active_ref, normed_ref, grouped_ref = refs[9 + sent :]
     tokens = rows * cols
     width = w_expand_ref.shape[1]
-    tile = even_ref.shape[1]
+    tile = divisor(width, 512, LANES)
+    subs = tile // LANES
     slot = one_ref.shape[0]
-    up_start, down_start, left_start = 8, 16 + cols, 24 + 2 * cols
-    right_start = left_start + slot
+    left_start, right_start = 2 * cols, 2 * cols + slot
 
     odd_col = odd_col_ref[0]
     left = choose(odd_col, one_ref[...], two_ref[...])
     right = choose(odd_col, two_ref[...], one_ref[...])
     edges = jnp.concatenate([up_ref[...], down_ref[...], left, right], axis=0)
 
-    def expand_halo(index, out_ref):
+    def expand_halo(index, carry):
         lanes = pl.ds(pl.multiple_of(index * tile, tile), tile)
         made = gelu_of_half(matmul(edges, w_expand_ref[:, lanes]))
-        for sub in range(tile // LANES):
-            part = made[:, sub * LANES : (sub + 1) * LANES]
-            out_ref[sub, up_start : up_start + cols] = part[:cols]
-            out_ref[sub, down_start : down_start + cols] = part[cols : 2 * cols]
-            out_ref[sub, left_start : left_start + 2 * slot] = part[2 * cols :]
-
-    position = lax.broadcasted_iota(jnp.int32, (8, LANES), 0)
+        for sub in range(subs):
+            halo_ref[index * subs + sub] = made[:, sub * LANES : (sub + 1) * LANES]
+        return carry
+
+    lax.fori_loop(0, width // tile, expand_halo, 0)
+    mixed_ref[...] = inner_ref[...]
+    position = lax.broadcasted_iota(jnp.int32, (cols, LANES), 0)
     at_first = position == 0
-    at_last = position == 7
-
-    def convolve(index, out_ref, halo_ref):
-        for sub in range(tile // LANES):
-            lanes = pl.ds(pl.multiple_of(index * tile + sub * LANES, LANES), LANES)
-            base = (index * (tile // LANES) + sub) * padded_rows(tokens) + 8
-            taps = [[0.5 * depth_ref[p, q : q + 1, lanes] for q in range(3)] for p in range(3)]
-            sums = {}
-            for y in range(-1, rows + 1):
-                if y < 0:
-                    parts = [halo_ref[sub, up_start + q : up_start + q + cols] for q in (-1, 0, 1)]
-                elif y == rows:
-                    parts = [
-                        halo_ref[sub, down_start + q : down_start + q + cols] for q in (-1, 0, 1)
-                    ]
-                else:
-                    parts = [
-                        expanded_ref[pl.ds(base + (y * cols + q), cols), :] for q in (-1, 0, 1)
-                    ]
-                left = halo_ref[sub, left_start + y + 1 : left_start + y + 2]
-                right = halo_ref[sub, right_start + y + 1 : right_start + y + 2]
-                parts[0] = jnp.concatenate(
-                    [jnp.where(at_first, left, parts[0][:8]), parts[0][8:]], axis=0
-                )
-                parts[2] = jnp.concatenate(
-                    [parts[2][:-8], jnp.where(at_last, right, parts[2][-8:])], axis=0
-                )
-                for p in range(3):
-                    target = y + 1 - p
-                    if 0 <= target < rows:
-                        for q in range(3):
-                            term = taps[p][q] * parts[q]
-                            sums[target] = sums[target] + term if target in sums else term
-                if y > 0:
-                    out_ref[
-                        (y - 1) * cols : y * cols, sub * LANES : (sub + 1) * LANES
-                    ] = gelu_of_half(sums.pop(y - 1)).astype(jnp.bfloat16)
-
-    def project(index, in_ref):
-        piece = pl.ds(pl.multiple_of(index * tile, tile), tile)
-        total_ref[...] += matmul(in_ref[...], w_project_ref[piece, :])
-
-    total_ref[...] = field_ref[...]
-    expand_halo(0, even_halo_ref)
-    expand_halo(1, odd_halo_ref)
-    convolve(0, even_ref, even_halo_ref)
-
-    def body(index, carry):
-        project(2 * index, even_ref)
-        convolve(2 * index + 1, odd_ref, odd_halo_ref)
-        expand_halo(2 * index + 2, even_halo_ref)
-        project(2 * index + 1, odd_ref)
-        convolve(2 * index + 2, even_ref, even_halo_ref)
-        expand_halo(2 * index + 3, odd_halo_ref)
-        return carry
-
-    pairs = width // tile // 2
-    lax.fori_loop(0, pairs - 1, body, 0)
-    project(2 * pairs - 2, even_ref)
-    convolve(2 * pairs - 1, odd_ref, odd_halo_ref)
-    project(2 * pairs - 1, odd_ref)
+    at_last = position == cols - 1
+
+    def activate(chunk, here, sums_ref):
+        lanes = pl.ds(pl.multiple_of(chunk * LANES, LANES), LANES)
+        taps = [[0.5 * depth_ref[p, q : q + 1, lanes] for q in range(3)] for p in range(3)]
+        beside = []
+        for q, start in ((0, left_start), (2, right_start)):
+            beside.append(
+                sum(taps[p][q] * halo_ref[chunk, start + p : start + p + rows] for p in range(3))
+            )
+        made = []
+        for p, start, y in ((0, 0, 0), (2, cols, rows - 1)):
+            row = halo_ref[chunk, start : start + cols]
+            before = jnp.where(at_first, beside[0][y : y + 1], taps[p][0] * pltpu.roll(row, 1, 0))
+            after = jnp.where(
+                at_last, beside[1][y : y + 1], taps[p][2] * pltpu.roll(row, cols - 1, 0)
+            )
+            made.append(sums_ref[here, start : start + cols] + before + taps[p][1] * row + after)
+        for index in range(2):
+            start = 2 * cols + index * rows
+            made.append(sums_ref[here, start : start + rows] + beside[index])
+        active_ref[:, lanes] = gelu_of_half(jnp.concatenate(made, axis=0)).astype(jnp.bfloat16)
+
+    chunk = 0
+    for sums_ref in rim_refs:
+        offset = chunk
+
+        def body(index, carry, sums_ref=sums_ref, offset=offset):
+            activate(offset + 2 * index, 2 * index, sums_ref)
+            activate(offset + 2 * index + 1, 2 * index + 1, sums_ref)
+            return carry
+
+        lax.fori_loop(0, sums_ref.shape[0] // 2, body, 0)
+        chunk += sums_ref.shape[0]
+
+    branch = matmul(active_ref[...], w_project_ref[...])
+    mixed_ref[:cols, :] += branch[:cols]
+    mixed_ref[tokens - cols :, :] += branch[cols : 2 * cols]
+    for y in range(1, rows - 1):
+        for index, x in ((0, 0), (1, cols - 1)):
+            spot = y * cols + x
+            start = 2 * cols + index * rows + y
+            mixed_ref[spot : spot + 1, :] += branch[start : start + 1]
 
     step = divisor(tokens, 128, 16)
     for start in range(0, tokens, step):
         piece = slice(start, start + step)
-        mixed = total_ref[piece, :]
-        mixed_ref[piece, :] = mixed
-        normed_ref[piece, :] = layer_norm(mixed).astype(jnp.bfloat16)
+        normed_ref[piece, :] = layer_norm(mixed_ref[piece, :]).astype(jnp.bfloat16)
     grouped_ref[...] = matmul(perm_ref[...], normed_ref[...]).astype(jnp.bfloat16)
     for index, mask in enumerate(masks):
         for side in range(sides):
@@ -301,39 +373,36 @@
             )
 
 
-def mix(
-    own, odd_col, plan, size, expanded, field, up, down, one, two, w_expand, depth_kernel, w_project,
-    perm, rows, cols,
+def rim(
+    own, odd_col, plan, size, total, rims, up, down, one, two, w_expand, depth_kernel, w_project, perm,
+    rows, cols,
 ):
-    tokens, channels = field.shape
+    tokens, channels = total.shape
     width = w_expand.shape[1]
-    tile = divisor(width // 2, 256, LANES)
-    slot = one.shape[0]
+    halo_rows = 2 * cols + 2 * one.shape[0]
     sent = outgoing_shapes(plan, size, channels)
-    halo = pltpu.VMEM((tile // LANES, 24 + 2 * cols + 2 * slot, LANES), jnp.float32)
-    return pl.pallas_call(
-        functools.partial(mix_kernel, rows=rows, cols=cols, plan=plan, size=size),
-        in_specs=[pl.BlockSpec(memory_space=pltpu.SMEM)] * 2 + [vmem()] * 10,
+    return pl.pallas_call(
+        functools.partial(
+            rim_kernel, rows=rows, cols=cols, plan=plan, size=size, pieces=len(rims)
+        ),
+        in_specs=[pl.BlockSpec(memory_space=pltpu.SMEM)] * 2 + [vmem()] * (9 + len(rims)),
         out_specs=[vmem()] * (1 + len(sent)),
         out_shape=[jax.ShapeDtypeStruct((tokens, channels), jnp.float32)]
         + [jax.ShapeDtypeStruct(shape, jnp.bfloat16) for shape in sent],
         scratch_shapes=[
-            pltpu.VMEM((tokens, channels), jnp.float32),
+            pltpu.VMEM((width // LANES, halo_rows, LANES), jnp.float32),
+            pltpu.VMEM((2 * cols + 2 * rows, width), jnp.bfloat16),
             pltpu.VMEM((tokens, channels), jnp.bfloat16),
             pltpu.VMEM((tokens, channels), jnp.bfloat16),
-            pltpu.VMEM((tokens, tile), jnp.bfloat16),
-            pltpu.VMEM((tokens, tile), jnp.bfloat16),
-            halo,
-            halo,
         ],
         compiler_params=pltpu.CompilerParams(vmem_limit_bytes=8 * MIB),
         cost_estimate=pl.CostEstimate(
-            flops=2 * tokens * channels * width,
-            bytes_accessed=tokens * channels * 10 + 4 * channels * width + tokens * width * 4,
-            transcendentals=tokens * width,
+            flops=2 * halo_rows * channels * width * 2 + 2 * tokens * tokens * channels,
+            bytes_accessed=tokens * channels * 10 + 4 * channels * width,
+            transcendentals=2 * halo_rows * width,
         ),
-        name="mix",
-    )(own, odd_col, expanded, field, up, down, one, two, w_expand, depth_kernel, w_project, perm)
+        name="rim",
+    )(own, odd_col, total, *rims, up, down, one, two, w_expand, depth_kernel, w_project, perm)
 
 
 def identity(size):
@@ -635,14 +704,25 @@
     one, two = swap_pairs(one, "row", 0), swap_pairs(two, "row", 1)
     normed = half_norm_of(flat)
     expanded = expand(normed, w_expand)
-    one, two, normed, expanded = lax.optimization_barrier((one, two, normed, expanded))
+    tile = divisor(w_expand.shape[1] // 2, 256, LANES)
+    count = w_expand.shape[1] // tile
+    early = 2
+    total, rim_one = inner(
+        expanded, flat, depth_kernel, w_project, rows, cols, 0, early, tile
+    )
+    one, two, normed, expanded, total, rim_one = lax.optimization_barrier(
+        (one, two, normed, expanded, total, rim_one)
+    )
     up, down, one, two = column_strips(odd_row, odd_col, normed, one, two, round_up(rows + 2, 16))
     one, two = swap_pairs(one, "col", 0), swap_pairs(two, "col", 1)
+    total, rim_two = inner(
+        expanded, total, depth_kernel, w_project, rows, cols, early, count - early, tile
+    )
 
     size = tokens // (len(plan[0]) * plan[2])
-    mixed, *outgoing = mix(
-        own, odd_col, plan, size, expanded, flat, up, down, one, two, w_expand, depth_kernel, w_project,
-        perm, rows, cols,
+    mixed, *outgoing = rim(
+        own, odd_col, plan, size, total, [rim_one, rim_two], up, down, one, two, w_expand,
+        depth_kernel, w_project, perm, rows, cols,
     )
 
     def route(outgoing, outward):

time: 59.5 us -> 60.6 us (1.018)
  Pallas kernels: 15.3 us -> 17.5 us
  starting transfers between devices: 35.9 us -> 33.8 us
  waiting for transfers between devices: 6.85 us -> 7.94 us
    ppermute x20, starting transfers between devices: 31.5 us -> 29.2 us  [swap(): lax.ppermute(slab, ('row', 'col'), [(i, i ^ mask) for i in range(devices)])]
    pallas_call x1 -> x3, Pallas kernels: 5.74 us -> 7.94 us  [the longest x2 5.04 us: inner(): pl.pallas_call(functools.partial(inner_kernel, rows=rows, cols=cols, firs...]
    ppermute x20, waiting for transfers between devices: 6.32 us -> 7.93 us  [swap(): lax.ppermute(slab, ('row', 'col'), [(i, i ^ mask) for i in range(devices)])]
  transfers between devices with their start and end apart: 24 -> 24, of which waited for: 7 -> 8; matrix products, arithmetic and copies ran while one was open for 0% -> 0% of each run, Pallas kernels for 4% -> 13%
where the time goes in v17:
time: 60.6 us; the launch traced here: 60.4 us
  starting transfers between devices  33.8 us (56%)
  Pallas kernels  17.5 us (29%)
  waiting for transfers between devices  7.94 us (13%)
  local copies, waits for them, and re-layouts  0.93 us (2%)
    ppermute x20, starting transfers between devices, swap(): lax.ppermute(slab, ('row', 'col'), [(i, i ^ mask) for i in range(devices)])  29.2 us
    ppermute x20, waiting for transfers between devices, swap(): lax.ppermute(slab, ('row', 'col'), [(i, i ^ mask) for i in range(devices)])  7.93 us
    pallas_call x2, Pallas kernels, inner(): pl.pallas_call(functools.partial(inner_kernel, rows=rows, cols=cols, firs...  5.04 us
    ppermute x4, starting transfers between devices, swap_pairs(): return lax.ppermute(edge, axis, pairs + [(b, a) for a, b in pairs])  4.61 us
    pallas_call x1, Pallas kernels, attend(): pl.pallas_call(functools.partial(attend_kernel, plan=plan, sets=sets, cam...  4.57 us
    pallas_call x1, Pallas kernels, rim(): pl.pallas_call(functools.partial(rim_kernel, rows=rows, cols=cols, plan=p...  2.9 us
    pallas_call x1, Pallas kernels, expand(): pl.pallas_call(expand_kernel, in_specs=[vmem()] * 2, out_specs=vmem(), ou...  2.15 us
    pallas_call x1, Pallas kernels, finish(): pl.pallas_call(functools.partial(finish_kernel, plan=plan), in_specs=[pl....  1.94 us
  transfers between devices with their start and end apart: 24, of which 8 were waited for; matrix products, arithmetic and copies ran while one was open for 0% of the time, Pallas kernels for 13%

profile of v17, /device:TPU:0, one launch (start us, length us, event | category | flops | bytes accessed | tf_op | source)
XLA Modules:
  0.0 60.4 jit_solution(4725103473866151892)
XLA Ops:
  0.0 0.9 %slice_bitcast_fusion = (f32[32,512]{1,0:T(8,128)S(1)}, f32[32,512]{1,0:T(8,128)S(1)}) fusion(f32[16,32,512]{2,1,0:T(8,128)} %param.8), kind=kLoop, calls=%fused_computation | loop fusion | bytes 262144 | tf_op jit(solution)/shard_map/squeeze | solution.py:701
  1.1 3.1 %collective-permute-start = (bf16[32,512]{1,0:T(8,128)(2,1)S(1)}, bf16[32,512]{1,0:T(8,128)(2,1)S(1)}, u32[]{:S(2)}, u32[]{:S(2)}) collective-permute-start(bf16[32,512]{1,0:T(8,128)(2,1)S(1)} %get-tuple-element.58), channel_id=1, source_target_pairs={{0,4},{8,12},{4,0},{12,8},{1,5},{9,13},{5,1},{13,9},{2,6},{10,14},... | collective-permute-start | bytes 98312 | tf_op jit(solution)/shard_map/ppermute | solution.py:573
  5.2 2.2 %expand.1.expanded_ref = f32[8448,128]{1,0:T(8,128)S(1)} custom-call(bf16[512,512]{1,0:T(8,128)(2,1)S(1)} %half_norm.1.normed_ref, bf16[512,2048]{1,0:T(8,128)(2,1)S(1)} %copy-done), custom_call_target="tpu_custom_call" | custom-call | flops 10000000000 | bytes 6815744 | tf_op jit(solution)/shard_map/expand/pallas_call | solution.py:181
  7.4 1.2 %inner.2 = (f32[512,512]{1,0:T(8,128)S(1)}, f32[4,96,128]{2,1,0:T(8,128)S(1)}) custom-call(f32[8448,128]{1,0:T(8,128)S(1)} %expand.1.expanded_ref, f32[512,512]{1,0:T(8,128)S(1)} %bitcast.10, f32[3,3,2048]{2,1,0:T(4,128)S(1)} %copy-done.5, bf16[2048,512]{1,0:T(8,128)(2,1)S(1)} %copy-done.1), custom_call_target="tpu_custom_call" | custom-call | flops 4000000000 | bytes 3145728 | tf_op jit(solution)/shard_map/inner/pallas_call | solution.py:268
  9.9 3.8 %inner.3 = (f32[512,512]{1,0:T(8,128)S(1)}, f32[12,96,128]{2,1,0:T(8,128)S(1)}) custom-call(f32[8448,128]{1,0:T(8,128)S(1)} %expand.1.expanded_ref, f32[512,512]{1,0:T(8,128)S(1)} %get-tuple-element.63.start_ref, f32[3,3,2048]{2,1,0:T(4,128)S(1)} %copy-done.5, bf16[2048,512]{1,0:T(8,128)(2,1)S(1)} %copy-done.1), custom_call_target="tpu_custom_call" | custom-call | flops 12000000000 | bytes 5242880 | tf_op jit(solution)/shard_map/inner/pallas_call | solution.py:268
  13.8 2.9 %rim.1 = (f32[512,512]{1,0:T(8,128)S(1)}, bf16[2,32,512]{2,1,0:T(8,128)(2,1)S(1)}, bf16[2,32,512]{2,1,0:T(8,128)(2,1)S(1)}, bf16[1,32,512]{2,1,0:T(8,128)(2,1)S(...) custom-call(s32[1]{0:T(128)} %bitcast.own_ref, s32[1]{0:T(128)} %bitcast.2.odd_col_ref, ...), custom_call_target="tpu_custom_call" | custom-call | flops 805306368 | bytes 6815744 | tf_op jit(solution)/shard_map/rim/pallas_call | solution.py:384
  16.7 3.0 %collective-permute-start.6 = (bf16[6,32,512]{2,1,0:T(8,128)(2,1)S(1)}, bf16[6,32,512]{2,1,0:T(8,128)(2,1)S(1)}, u32[]{:S(2)}, u32[]{:S(2)}) collective-permute-start(bf16[6,32,512]{2,1,0:T(8,128)(2,1)S(1)} %get-tuple-element.77), channel_id=1, source_target_pairs={{0,1},{1,0},{2,3},{3,2},{4,5},{5,4},{6,7},{7,6},{8,9},{9,8},{10,11... | collective-permute-start | bytes 589832 | tf_op jit(solution)/shard_map/ppermute | solution.py:644
  19.7 2.7 %collective-permute-start.4 = (bf16[2,32,512]{2,1,0:T(8,128)(2,1)S(1)}, bf16[2,32,512]{2,1,0:T(8,128)(2,1)S(1)}, u32[]{:S(2)}, u32[]{:S(2)}) collective-permute-start(bf16[2,32,512]{2,1,0:T(8,128)(2,1)S(1)} %get-tuple-element.74), channel_id=1, source_target_pairs={{0,14},{1,15},{2,12},{3,13},{4,10},{5,11},{6,8},{7,9},{8,6},{9,7},... | collective-permute-start | bytes 196616 | tf_op jit(solution)/shard_map/ppermute | solution.py:644
  22.3 1.1 %collective-permute-start.5 = (bf16[2,32,512]{2,1,0:T(8,128)(2,1)S(1)}, bf16[2,32,512]{2,1,0:T(8,128)(2,1)S(1)}, u32[]{:S(2)}, u32[]{:S(2)}) collective-permute-start(bf16[2,32,512]{2,1,0:T(8,128)(2,1)S(1)} %get-tuple-element.75), channel_id=1, source_target_pairs={{0,12},{1,13},{2,14},{3,15},{4,8},{5,9},{6,10},{7,11},{8,4},{9,5},... | collective-permute-start | bytes 196616 | tf_op jit(solution)/shard_map/ppermute | solution.py:644
  23.5 3.1 %collective-permute-start.7 = (bf16[2,32,512]{2,1,0:T(8,128)(2,1)S(1)}, bf16[2,32,512]{2,1,0:T(8,128)(2,1)S(1)}, u32[]{:S(2)}, u32[]{:S(2)}) collective-permute-start(bf16[2,32,512]{2,1,0:T(8,128)(2,1)S(1)} %get-tuple-element.78), channel_id=1, source_target_pairs={{0,10},{1,11},{2,8},{3,9},{4,14},{5,15},{6,12},{7,13},{8,2},{9,3},... | collective-permute-start | bytes 196616 | tf_op jit(solution)/shard_map/ppermute | solution.py:644
  26.6 0.8 %collective-permute-start.10 = (bf16[2,32,512]{2,1,0:T(8,128)(2,1)S(1)}, bf16[2,32,512]{2,1,0:T(8,128)(2,1)S(1)}, u32[]{:S(2)}, u32[]{:S(2)}) collective-permute-start(bf16[2,32,512]{2,1,0:T(8,128)(2,1)S(1)} %get-tuple-element.84), channel_id=1, source_target_pairs={{0,8},{1,9},{2,10},{3,11},{4,12},{5,13},{6,14},{7,15},{8,0},{9,1},... | collective-permute-start | bytes 196616 | tf_op jit(solution)/shard_map/ppermute | solution.py:644
  27.9 6.0 %collective-permute-start.8 = (bf16[2,32,512]{2,1,0:T(8,128)(2,1)S(1)}, bf16[2,32,512]{2,1,0:T(8,128)(2,1)S(1)}, u32[]{:S(2)}, u32[]{:S(2)}) collective-permute-start(bf16[2,32,512]{2,1,0:T(8,128)(2,1)S(1)} %get-tuple-element.81), channel_id=1, source_target_pairs={{0,6},{1,7},{2,4},{3,5},{4,2},{5,3},{6,0},{7,1},{8,14},{9,15},{10,... | collective-permute-start | bytes 196616 | tf_op jit(solution)/shard_map/ppermute | solution.py:644
  34.5 1.5 %collective-permute-done.7.refs_3_ = bf16[2,32,512]{2,1,0:T(8,128)(2,1)S(1)} collective-permute-done((bf16[2,32,512]{2,1,0:T(8,128)(2,1)S(1)}, bf16[2,32,512]{2,1,0:T(8,128)(2,1)S(1)}, u32[]{:S(2)}, u32[]{:S(2)}) %collective-permute-start.7) | collective-permute-done | bytes 65568 | tf_op jit(solution)/shard_map/ppermute | solution.py:644
  36.5 1.8 %collective-permute-done.8.refs_2_ = bf16[2,32,512]{2,1,0:T(8,128)(2,1)S(1)} collective-permute-done((bf16[2,32,512]{2,1,0:T(8,128)(2,1)S(1)}, bf16[2,32,512]{2,1,0:T(8,128)(2,1)S(1)}, u32[]{:S(2)}, u32[]{:S(2)}) %collective-permute-start.8) | collective-permute-done | bytes 65568 | tf_op jit(solution)/shard_map/ppermute | solution.py:644
  38.5 4.6 %attend.1 = (bf16[2,32,512]{2,1,0:T(8,128)(2,1)S(1)}, bf16[2,32,512]{2,1,0:T(8,128)(2,1)S(1)}, bf16[1,32,512]{2,1,0:T(8,128)(2,1)S(1)}, bf16[6,32,512]{2,1,0:T(8,128)(2,1)S(1)}, bf16[5,32,512]{2,1,0:T(8,128)(2,1)S(1)}) custom-call(bf16[2,32,512]{2,1,0:T(8,128)(2,1)S(1)} %collective-permute-done.4.refs_0_, ...), custom_call_target="tpu_custom_call" | custom-call | flops 1073741824 | bytes 2621440 | tf_op jit(solution)/shard_map/attend/pallas_call | solution.py:503
  43.1 3.4 %collective-permute-start.14 = (bf16[2,32,512]{2,1,0:T(8,128)(2,1)S(1)}, bf16[2,32,512]{2,1,0:T(8,128)(2,1)S(1)}, u32[]{:S(2)}, u32[]{:S(2)}) collective-permute-start(bf16[2,32,512]{2,1,0:T(8,128)(2,1)S(1)} %get-tuple-element.87), channel_id=1, source_target_pairs={{0,14},{1,15},{2,12},{3,13},{4,10},{5,11},{6,8},{7,9},{8,6},{9,7},... | collective-permute-start | bytes 196616 | tf_op jit(solution)/shard_map/ppermute | solution.py:644
  46.5 1.1 %collective-permute-start.15 = (bf16[2,32,512]{2,1,0:T(8,128)(2,1)S(1)}, bf16[2,32,512]{2,1,0:T(8,128)(2,1)S(1)}, u32[]{:S(2)}, u32[]{:S(2)}) collective-permute-start(bf16[2,32,512]{2,1,0:T(8,128)(2,1)S(1)} %get-tuple-element.88), channel_id=1, source_target_pairs={{0,12},{1,13},{2,14},{3,15},{4,8},{5,9},{6,10},{7,11},{8,4},{9,5},... | collective-permute-start | bytes 196616 | tf_op jit(solution)/shard_map/ppermute | solution.py:644
  47.7 4.2 %collective-permute-start.18 = (bf16[2,32,512]{2,1,0:T(8,128)(2,1)S(1)}, bf16[2,32,512]{2,1,0:T(8,128)(2,1)S(1)}, u32[]{:S(2)}, u32[]{:S(2)}) collective-permute-start(bf16[2,32,512]{2,1,0:T(8,128)(2,1)S(1)} %get-tuple-element.94), channel_id=1, source_target_pairs={{0,6},{1,7},{2,4},{3,5},{4,2},{5,3},{6,0},{7,1},{8,14},{9,15},{10,... | collective-permute-start | bytes 196616 | tf_op jit(solution)/shard_map/ppermute | solution.py:644
  51.9 1.6 %collective-permute-start.20 = (bf16[2,32,512]{2,1,0:T(8,128)(2,1)S(1)}, bf16[2,32,512]{2,1,0:T(8,128)(2,1)S(1)}, u32[]{:S(2)}, u32[]{:S(2)}) collective-permute-start(bf16[2,32,512]{2,1,0:T(8,128)(2,1)S(1)} %get-tuple-element.97), channel_id=1, source_target_pairs={{0,8},{1,9},{2,10},{3,11},{4,12},{5,13},{6,14},{7,15},{8,0},{9,1},... | collective-permute-start | bytes 196616 | tf_op jit(solution)/shard_map/ppermute | solution.py:644
  53.5 0.9 %collective-permute-start.21 = (bf16[2,32,512]{2,1,0:T(8,128)(2,1)S(1)}, bf16[2,32,512]{2,1,0:T(8,128)(2,1)S(1)}, u32[]{:S(2)}, u32[]{:S(2)}) collective-permute-start(bf16[2,32,512]{2,1,0:T(8,128)(2,1)S(1)} %get-tuple-element.98), channel_id=1, source_target_pairs={{0,2},{1,3},{2,0},{3,1},{4,6},{5,7},{6,4},{7,5},{8,10},{9,11},{10,... | collective-permute-start | bytes 196616 | tf_op jit(solution)/shard_map/ppermute | solution.py:644
  54.4 1.3 %collective-permute-done.17.refs_3_ = bf16[2,32,512]{2,1,0:T(8,128)(2,1)S(1)} collective-permute-done((bf16[2,32,512]{2,1,0:T(8,128)(2,1)S(1)}, bf16[2,32,512]{2,1,0:T(8,128)(2,1)S(1)}, u32[]{:S(2)}, u32[]{:S(2)}) %collective-permute-start.17) | collective-permute-done | bytes 65568 | tf_op jit(solution)/shard_map/ppermute | solution.py:644
  55.7 1.5 %collective-permute-done.18.refs_2_ = bf16[2,32,512]{2,1,0:T(8,128)(2,1)S(1)} collective-permute-done((bf16[2,32,512]{2,1,0:T(8,128)(2,1)S(1)}, bf16[2,32,512]{2,1,0:T(8,128)(2,1)S(1)}, u32[]{:S(2)}, u32[]{:S(2)}) %collective-permute-start.18) | collective-permute-done | bytes 65568 | tf_op jit(solution)/shard_map/ppermute | solution.py:644
  57.2 0.8 %collective-permute-done.19.refs_4_ = bf16[2,32,512]{2,1,0:T(8,128)(2,1)S(1)} collective-permute-done((bf16[2,32,512]{2,1,0:T(8,128)(2,1)S(1)}, bf16[2,32,512]{2,1,0:T(8,128)(2,1)S(1)}, u32[]{:S(2)}, u32[]{:S(2)}) %collective-permute-start.19) | collective-permute-done | bytes 65568 | tf_op jit(solution)/shard_map/ppermute | solution.py:644
  58.5 1.9 %finish.1 = f32[512,512]{1,0:T(8,128)} custom-call(s32[1]{0:T(128)} %bitcast.own_ref, bf16[2,32,512]{2,1,0:T(8,128)(2,1)S(1)} %collective-permute-done.14.refs_0_, bf16[2,32,512]{2,1,0:T(8,128)(2,1)S(1)} %collective-permute-done.15.refs_1_, bf16[2,32,512]{2,1,0:T(8,128)(2,1)S(1)} %collective-permute-done.18.refs_2_, ...), custom_call_target="tpu_custom_call" | custom-call | tf_op jit(solution)/shard_map/finish/pallas_call | solution.py:556
  (52 shorter events, 4.8 us)
Async XLA Ops:
  1.1 7.5 %collective-permute-start = (bf16[32,512]{1,0:T(8,128)(2,1)S(1)}, bf16[32,512]{1,0:T(8,128)(2,1)S(1)}, u32[]{:S(2)}, u32[]{:S(2)}) collective-permute-start(bf16[32,512]{1,0:T(8,128)(2,1)S(1)} %get-tuple-element.58), channel_id=1, source_target_pairs={{0,4},{8,12},{4,0},{12,8},{1,5},{9,13},{5,1},{13,9},{2,6},{10,14},... | collective-permute-start | bytes 98312 | tf_op jit(solution)/shard_map/ppermute | solution.py:573
  4.2 4.5 %collective-permute-start.1 = (bf16[32,512]{1,0:T(8,128)(2,1)S(1)}, bf16[32,512]{1,0:T(8,128)(2,1)S(1)}, u32[]{:S(2)}, u32[]{:S(2)}) collective-permute-start(bf16[32,512]{1,0:T(8,128)(2,1)S(1)} %get-tuple-element.59), channel_id=1, source_target_pairs={{4,8},{8,4},{5,9},{9,5},{6,10},{10,6},{7,11},{11,7},{20,24},{24,20... | collective-permute-start | bytes 98312 | tf_op jit(solution)/shard_map/ppermute | solution.py:573
  9.0 4.7 %collective-permute-start.2 = (bf16[32,512]{1,0:T(8,128)(2,1)S(1)}, bf16[32,512]{1,0:T(8,128)(2,1)S(1)}, u32[]{:S(2)}, u32[]{:S(2)}) collective-permute-start(bf16[32,512]{1,0:T(8,128)(2,1)S(1)} %get-tuple-element.72), channel_id=1, source_target_pairs={{0,1},{2,3},{1,0},{3,2},{4,5},{6,7},{5,4},{7,6},{8,9},{10,11},{9,8... | collective-permute-start | bytes 98312 | tf_op jit(solution)/shard_map/ppermute | solution.py:573
  9.1 4.6 %collective-permute-start.3 = (bf16[32,512]{1,0:T(8,128)(2,1)S(1)}, bf16[32,512]{1,0:T(8,128)(2,1)S(1)}, u32[]{:S(2)}, u32[]{:S(2)}) collective-permute-start(bf16[32,512]{1,0:T(8,128)(2,1)S(1)} %get-tuple-element.73), channel_id=1, source_target_pairs={{1,2},{2,1},{5,6},{6,5},{9,10},{10,9},{13,14},{14,13},{17,18},{18,... | collective-permute-start | bytes 98312 | tf_op jit(solution)/shard_map/ppermute | solution.py:573
  16.7 6.8 %collective-permute-start.6 = (bf16[6,32,512]{2,1,0:T(8,128)(2,1)S(1)}, bf16[6,32,512]{2,1,0:T(8,128)(2,1)S(1)}, u32[]{:S(2)}, u32[]{:S(2)}) collective-permute-start(bf16[6,32,512]{2,1,0:T(8,128)(2,1)S(1)} %get-tuple-element.77), channel_id=1, source_target_pairs={{0,1},{1,0},{2,3},{3,2},{4,5},{5,4},{6,7},{7,6},{8,9},{9,8},{10,11... | collective-permute-start | bytes 589832 | tf_op jit(solution)/shard_map/ppermute | solution.py:644
  19.7 8.3 %collective-permute-start.4 = (bf16[2,32,512]{2,1,0:T(8,128)(2,1)S(1)}, bf16[2,32,512]{2,1,0:T(8,128)(2,1)S(1)}, u32[]{:S(2)}, u32[]{:S(2)}) collective-permute-start(bf16[2,32,512]{2,1,0:T(8,128)(2,1)S(1)} %get-tuple-element.74), channel_id=1, source_target_pairs={{0,14},{1,15},{2,12},{3,13},{4,10},{5,11},{6,8},{7,9},{8,6},{9,7},... | collective-permute-start | bytes 196616 | tf_op jit(solution)/shard_map/ppermute | solution.py:644
  22.3 11.7 %collective-permute-start.5 = (bf16[2,32,512]{2,1,0:T(8,128)(2,1)S(1)}, bf16[2,32,512]{2,1,0:T(8,128)(2,1)S(1)}, u32[]{:S(2)}, u32[]{:S(2)}) collective-permute-start(bf16[2,32,512]{2,1,0:T(8,128)(2,1)S(1)} %get-tuple-element.75), channel_id=1, source_target_pairs={{0,12},{1,13},{2,14},{3,15},{4,8},{5,9},{6,10},{7,11},{8,4},{9,5},... | collective-permute-start | bytes 196616 | tf_op jit(solution)/shard_map/ppermute | solution.py:644
  23.5 12.5 %collective-permute-start.7 = (bf16[2,32,512]{2,1,0:T(8,128)(2,1)S(1)}, bf16[2,32,512]{2,1,0:T(8,128)(2,1)S(1)}, u32[]{:S(2)}, u32[]{:S(2)}) collective-permute-start(bf16[2,32,512]{2,1,0:T(8,128)(2,1)S(1)} %get-tuple-element.78), channel_id=1, source_target_pairs={{0,10},{1,11},{2,8},{3,9},{4,14},{5,15},{6,12},{7,13},{8,2},{9,3},... | collective-permute-start | bytes 196616 | tf_op jit(solution)/shard_map/ppermute | solution.py:644
  26.6 9.9 %collective-permute-start.10 = (bf16[2,32,512]{2,1,0:T(8,128)(2,1)S(1)}, bf16[2,32,512]{2,1,0:T(8,128)(2,1)S(1)}, u32[]{:S(2)}, u32[]{:S(2)}) collective-permute-start(bf16[2,32,512]{2,1,0:T(8,128)(2,1)S(1)} %get-tuple-element.84), channel_id=1, source_target_pairs={{0,8},{1,9},{2,10},{3,11},{4,12},{5,13},{6,14},{7,15},{8,0},{9,1},... | collective-permute-start | bytes 196616 | tf_op jit(solution)/shard_map/ppermute | solution.py:644
  27.4 9.1 %collective-permute-start.11 = (bf16[2,32,512]{2,1,0:T(8,128)(2,1)S(1)}, bf16[2,32,512]{2,1,0:T(8,128)(2,1)S(1)}, u32[]{:S(2)}, u32[]{:S(2)}) collective-permute-start(bf16[2,32,512]{2,1,0:T(8,128)(2,1)S(1)} %get-tuple-element.85), channel_id=1, source_target_pairs={{0,2},{1,3},{2,0},{3,1},{4,6},{5,7},{6,4},{7,5},{8,10},{9,11},{10,... | collective-permute-start | bytes 196616 | tf_op jit(solution)/shard_map/ppermute | solution.py:644
  27.9 10.3 %collective-permute-start.8 = (bf16[2,32,512]{2,1,0:T(8,128)(2,1)S(1)}, bf16[2,32,512]{2,1,0:T(8,128)(2,1)S(1)}, u32[]{:S(2)}, u32[]{:S(2)}) collective-permute-start(bf16[2,32,512]{2,1,0:T(8,128)(2,1)S(1)} %get-tuple-element.81), channel_id=1, source_target_pairs={{0,6},{1,7},{2,4},{3,5},{4,2},{5,3},{6,0},{7,1},{8,14},{9,15},{10,... | collective-permute-start | bytes 196616 | tf_op jit(solution)/shard_map/ppermute | solution.py:644
  34.0 4.5 %collective-permute-start.9 = (bf16[2,32,512]{2,1,0:T(8,128)(2,1)S(1)}, bf16[2,32,512]{2,1,0:T(8,128)(2,1)S(1)}, u32[]{:S(2)}, u32[]{:S(2)}) collective-permute-start(bf16[2,32,512]{2,1,0:T(8,128)(2,1)S(1)} %get-tuple-element.83), channel_id=1, source_target_pairs={{0,4},{1,5},{2,6},{3,7},{4,0},{5,1},{6,2},{7,3},{8,12},{9,13},{10,... | collective-permute-start | bytes 196616 | tf_op jit(solution)/shard_map/ppermute | solution.py:644
  36.0 2.4 %collective-permute-start.12 = (bf16[2,32,512]{2,1,0:T(8,128)(2,1)S(1)}, bf16[2,32,512]{2,1,0:T(8,128)(2,1)S(1)}, u32[]{:S(2)}, u32[]{:S(2)}) collective-permute-start(bf16[2,32,512]{2,1,0:T(8,128)(2,1)S(1)} %collective-permute-done.4.refs_0_), channel_id=1, source_target_pairs={{0,1},{1,0},{2,3},{3,2},{4,5},{5,4},{6,7},{7,6},{8,9},{9,8},{10,11... | collective-permute-start | bytes 196616 | tf_op jit(solution)/shard_map/ppermute | solution.py:644
  36.4 2.0 %collective-permute-start.13 = (bf16[2,32,512]{2,1,0:T(8,128)(2,1)S(1)}, bf16[2,32,512]{2,1,0:T(8,128)(2,1)S(1)}, u32[]{:S(2)}, u32[]{:S(2)}) collective-permute-start(bf16[2,32,512]{2,1,0:T(8,128)(2,1)S(1)} %collective-permute-done.5.refs_1_), channel_id=1, source_target_pairs={{0,1},{1,0},{2,3},{3,2},{4,5},{5,4},{6,7},{7,6},{8,9},{9,8},{10,11... | collective-permute-start | bytes 196616 | tf_op jit(solution)/shard_map/ppermute | solution.py:644
  43.1 4.5 %collective-permute-start.16 = (bf16[6,32,512]{2,1,0:T(8,128)(2,1)S(1)}, bf16[6,32,512]{2,1,0:T(8,128)(2,1)S(1)}, u32[]{:S(2)}, u32[]{:S(2)}) collective-permute-start(bf16[6,32,512]{2,1,0:T(8,128)(2,1)S(1)} %get-tuple-element.90), channel_id=1, source_target_pairs={{0,1},{1,0},{2,3},{3,2},{4,5},{5,4},{6,7},{7,6},{8,9},{9,8},{10,11... | collective-permute-start | bytes 589832 | tf_op jit(solution)/shard_map/ppermute | solution.py:644
  43.1 8.8 %collective-permute-start.14 = (bf16[2,32,512]{2,1,0:T(8,128)(2,1)S(1)}, bf16[2,32,512]{2,1,0:T(8,128)(2,1)S(1)}, u32[]{:S(2)}, u32[]{:S(2)}) collective-permute-start(bf16[2,32,512]{2,1,0:T(8,128)(2,1)S(1)} %get-tuple-element.87), channel_id=1, source_target_pairs={{0,14},{1,15},{2,12},{3,13},{4,10},{5,11},{6,8},{7,9},{8,6},{9,7},... | collective-permute-start | bytes 196616 | tf_op jit(solution)/shard_map/ppermute | solution.py:644
  46.5 7.0 %collective-permute-start.15 = (bf16[2,32,512]{2,1,0:T(8,128)(2,1)S(1)}, bf16[2,32,512]{2,1,0:T(8,128)(2,1)S(1)}, u32[]{:S(2)}, u32[]{:S(2)}) collective-permute-start(bf16[2,32,512]{2,1,0:T(8,128)(2,1)S(1)} %get-tuple-element.88), channel_id=1, source_target_pairs={{0,12},{1,13},{2,14},{3,15},{4,8},{5,9},{6,10},{7,11},{8,4},{9,5},... | collective-permute-start | bytes 196616 | tf_op jit(solution)/shard_map/ppermute | solution.py:644
  47.6 8.1 %collective-permute-start.17 = (bf16[2,32,512]{2,1,0:T(8,128)(2,1)S(1)}, bf16[2,32,512]{2,1,0:T(8,128)(2,1)S(1)}, u32[]{:S(2)}, u32[]{:S(2)}) collective-permute-start(bf16[2,32,512]{2,1,0:T(8,128)(2,1)S(1)} %get-tuple-element.91), channel_id=1, source_target_pairs={{0,10},{1,11},{2,8},{3,9},{4,14},{5,15},{6,12},{7,13},{8,2},{9,3},... | collective-permute-start | bytes 196616 | tf_op jit(solution)/shard_map/ppermute | solution.py:644
  47.7 9.6 %collective-permute-start.18 = (bf16[2,32,512]{2,1,0:T(8,128)(2,1)S(1)}, bf16[2,32,512]{2,1,0:T(8,128)(2,1)S(1)}, u32[]{:S(2)}, u32[]{:S(2)}) collective-permute-start(bf16[2,32,512]{2,1,0:T(8,128)(2,1)S(1)} %get-tuple-element.94), channel_id=1, source_target_pairs={{0,6},{1,7},{2,4},{3,5},{4,2},{5,3},{6,0},{7,1},{8,14},{9,15},{10,... | collective-permute-start | bytes 196616 | tf_op jit(solution)/shard_map/ppermute | solution.py:644
  51.9 6.2 %collective-permute-start.19 = (bf16[2,32,512]{2,1,0:T(8,128)(2,1)S(1)}, bf16[2,32,512]{2,1,0:T(8,128)(2,1)S(1)}, u32[]{:S(2)}, u32[]{:S(2)}) collective-permute-start(bf16[2,32,512]{2,1,0:T(8,128)(2,1)S(1)} %get-tuple-element.96), channel_id=1, source_target_pairs={{0,4},{1,5},{2,6},{3,7},{4,0},{5,1},{6,2},{7,3},{8,12},{9,13},{10,... | collective-permute-start | bytes 196616 | tf_op jit(solution)/shard_map/ppermute | solution.py:644
  51.9 6.2 %collective-permute-start.20 = (bf16[2,32,512]{2,1,0:T(8,128)(2,1)S(1)}, bf16[2,32,512]{2,1,0:T(8,128)(2,1)S(1)}, u32[]{:S(2)}, u32[]{:S(2)}) collective-permute-start(bf16[2,32,512]{2,1,0:T(8,128)(2,1)S(1)} %get-tuple-element.97), channel_id=1, source_target_pairs={{0,8},{1,9},{2,10},{3,11},{4,12},{5,13},{6,14},{7,15},{8,0},{9,1},... | collective-permute-start | bytes 196616 | tf_op jit(solution)/shard_map/ppermute | solution.py:644
  53.5 4.6 %collective-permute-start.21 = (bf16[2,32,512]{2,1,0:T(8,128)(2,1)S(1)}, bf16[2,32,512]{2,1,0:T(8,128)(2,1)S(1)}, u32[]{:S(2)}, u32[]{:S(2)}) collective-permute-start(bf16[2,32,512]{2,1,0:T(8,128)(2,1)S(1)} %get-tuple-element.98), channel_id=1, source_target_pairs={{0,2},{1,3},{2,0},{3,1},{4,6},{5,7},{6,4},{7,5},{8,10},{9,11},{10,... | collective-permute-start | bytes 196616 | tf_op jit(solution)/shard_map/ppermute | solution.py:644
  55.7 2.4 %collective-permute-start.22 = (bf16[2,32,512]{2,1,0:T(8,128)(2,1)S(1)}, bf16[2,32,512]{2,1,0:T(8,128)(2,1)S(1)}, u32[]{:S(2)}, u32[]{:S(2)}) collective-permute-start(bf16[2,32,512]{2,1,0:T(8,128)(2,1)S(1)} %collective-permute-done.14.refs_0_), channel_id=1, source_target_pairs={{0,1},{1,0},{2,3},{3,2},{4,5},{5,4},{6,7},{7,6},{8,9},{9,8},{10,11... | collective-permute-start | bytes 196616 | tf_op jit(solution)/shard_map/ppermute | solution.py:644
  57.2 1.3 %collective-permute-start.23 = (bf16[2,32,512]{2,1,0:T(8,128)(2,1)S(1)}, bf16[2,32,512]{2,1,0:T(8,128)(2,1)S(1)}, u32[]{:S(2)}, u32[]{:S(2)}) collective-permute-start(bf16[2,32,512]{2,1,0:T(8,128)(2,1)S(1)} %collective-permute-done.15.refs_1_), channel_id=1, source_target_pairs={{0,1},{1,0},{2,3},{3,2},{4,5},{5,4},{6,7},{7,6},{8,9},{9,8},{10,11... | collective-permute-start | bytes 196616 | tf_op jit(solution)/shard_map/ppermute | solution.py:644
  (8 other events, 81.9 us)

commit v18 on v17

--- a/solution.py
+++ b/solution.py
@@ -577,10 +577,8 @@
     devices = row_devices * col_devices
     crossing = list(range(devices - 2, devices // 2 - 1, -2))
     others = list(range(devices // 2 - 2, 0, -2))
-    masks = crossing[:1]
-    for index, mask in enumerate(crossing[1:]):
-        masks += [mask] + others[index : index + 1]
-    return masks + [0], min(2, len(masks)), 2
+    masks = crossing[:-1] + others[:-1] + crossing[-1:] + others[-1:] + [0]
+    return masks, 2, 2
 
 
 def outgoing_shapes(plan, size, channels):
@@ -647,8 +645,8 @@
     swapped = swap(passed, 1)
     first = [swap(slab, mask) for slab, mask in zip(slabs, masks)]
     rest = [swap(slab, mask) for slab, mask in zip(join(own, swapped), masks[late:-1])]
-    tie = min(1, len(rest) - 1)
-    *first, rest[tie] = lax.optimization_barrier((*first, rest[tie]))
+    tied = lax.optimization_barrier((*first, *rest[:-late]))
+    first, rest = tied[:late], [*tied[late:], *rest[-late:]]
     return [*first, *rest, kept, *[swap(slab, 1) for slab in first], swapped]
 
 

time: 60.6 us -> 58.6 us (0.967)
  waiting for transfers between devices: 7.94 us -> 5.99 us
    ppermute x20, waiting for transfers between devices: 7.93 us -> 5.98 us  [swap(): lax.ppermute(slab, ('row', 'col'), [(i, i ^ mask) for i in range(devices)])]
  transfers between devices with their start and end apart: 24 -> 24, of which waited for: 8 -> 6; matrix products, arithmetic and copies ran while one was open for 0% -> 0% of each run, Pallas kernels for 13% -> 13%
where the time goes in v18:
time: 58.6 us; the launch traced here: 58.4 us
  starting transfers between devices  33.7 us (58%)
  Pallas kernels  17.5 us (30%)
  waiting for transfers between devices  5.99 us (10%)
  local copies, waits for them, and re-layouts  0.93 us (2%)
    ppermute x20, starting transfers between devices, swap(): lax.ppermute(slab, ('row', 'col'), [(i, i ^ mask) for i in range(devices)])  29.1 us
    ppermute x20, waiting for transfers between devices, swap(): lax.ppermute(slab, ('row', 'col'), [(i, i ^ mask) for i in range(devices)])  5.98 us
    pallas_call x2, Pallas kernels, inner(): pl.pallas_call(functools.partial(inner_kernel, rows=rows, cols=cols, firs...  5.04 us
    ppermute x4, starting transfers between devices, swap_pairs(): return lax.ppermute(edge, axis, pairs + [(b, a) for a, b in pairs])  4.61 us
    pallas_call x1, Pallas kernels, attend(): pl.pallas_call(functools.partial(attend_kernel, plan=plan, sets=sets, cam...  4.57 us
    pallas_call x1, Pallas kernels, rim(): pl.pallas_call(functools.partial(rim_kernel, rows=rows, cols=cols, plan=p...  2.9 us
    pallas_call x1, Pallas kernels, expand(): pl.pallas_call(expand_kernel, in_specs=[vmem()] * 2, out_specs=vmem(), ou...  2.15 us
    pallas_call x1, Pallas kernels, finish(): pl.pallas_call(functools.partial(finish_kernel, plan=plan), in_specs=[pl....  1.94 us
  transfers between devices with their start and end apart: 24, of which 6 were waited for; matrix products, arithmetic and copies ran while one was open for 0% of the time, Pallas kernels for 13%

profile of v18, /device:TPU:0, one launch (start us, length us, event | category | flops | bytes accessed | tf_op | source)
XLA Modules:
  0.0 58.4 jit_solution(15314412853654685363)
XLA Ops:
  0.0 0.9 %slice_bitcast_fusion = (f32[32,512]{1,0:T(8,128)S(1)}, f32[32,512]{1,0:T(8,128)S(1)}) fusion(f32[16,32,512]{2,1,0:T(8,128)} %param.8), kind=kLoop, calls=%fused_computation | loop fusion | bytes 262144 | tf_op jit(solution)/shard_map/squeeze | solution.py:699
  1.1 3.1 %collective-permute-start = (bf16[32,512]{1,0:T(8,128)(2,1)S(1)}, bf16[32,512]{1,0:T(8,128)(2,1)S(1)}, u32[]{:S(2)}, u32[]{:S(2)}) collective-permute-start(bf16[32,512]{1,0:T(8,128)(2,1)S(1)} %get-tuple-element.62), channel_id=1, source_target_pairs={{0,4},{8,12},{4,0},{12,8},{1,5},{9,13},{5,1},{13,9},{2,6},{10,14},... | collective-permute-start | bytes 98312 | tf_op jit(solution)/shard_map/ppermute | solution.py:573
  5.2 2.2 %expand.1.expanded_ref = f32[8448,128]{1,0:T(8,128)S(1)} custom-call(bf16[512,512]{1,0:T(8,128)(2,1)S(1)} %half_norm.1.normed_ref, bf16[512,2048]{1,0:T(8,128)(2,1)S(1)} %copy-done), custom_call_target="tpu_custom_call" | custom-call | flops 10000000000 | bytes 6815744 | tf_op jit(solution)/shard_map/expand/pallas_call | solution.py:181
  7.4 1.2 %inner.2 = (f32[512,512]{1,0:T(8,128)S(1)}, f32[4,96,128]{2,1,0:T(8,128)S(1)}) custom-call(f32[8448,128]{1,0:T(8,128)S(1)} %expand.1.expanded_ref, f32[512,512]{1,0:T(8,128)S(1)} %bitcast.10, f32[3,3,2048]{2,1,0:T(4,128)S(1)} %copy-done.5, bf16[2048,512]{1,0:T(8,128)(2,1)S(1)} %copy-done.1), custom_call_target="tpu_custom_call" | custom-call | flops 4000000000 | bytes 3145728 | tf_op jit(solution)/shard_map/inner/pallas_call | solution.py:268
  9.1 0.8 %collective-permute-start.3 = (bf16[32,512]{1,0:T(8,128)(2,1)S(1)}, bf16[32,512]{1,0:T(8,128)(2,1)S(1)}, u32[]{:S(2)}, u32[]{:S(2)}) collective-permute-start(bf16[32,512]{1,0:T(8,128)(2,1)S(1)} %get-tuple-element.77), channel_id=1, source_target_pairs={{1,2},{2,1},{5,6},{6,5},{9,10},{10,9},{13,14},{14,13},{17,18},{18,... | collective-permute-start | bytes 98312 | tf_op jit(solution)/shard_map/ppermute | solution.py:573
  9.9 3.8 %inner.3 = (f32[512,512]{1,0:T(8,128)S(1)}, f32[12,96,128]{2,1,0:T(8,128)S(1)}) custom-call(f32[8448,128]{1,0:T(8,128)S(1)} %expand.1.expanded_ref, f32[512,512]{1,0:T(8,128)S(1)} %get-tuple-element.67.start_ref, f32[3,3,2048]{2,1,0:T(4,128)S(1)} %copy-done.5, bf16[2048,512]{1,0:T(8,128)(2,1)S(1)} %copy-done.1), custom_call_target="tpu_custom_call" | custom-call | flops 12000000000 | bytes 5242880 | tf_op jit(solution)/shard_map/inner/pallas_call | solution.py:268
  13.8 2.9 %rim.1 = (f32[512,512]{1,0:T(8,128)S(1)}, bf16[2,32,512]{2,1,0:T(8,128)(2,1)S(1)}, bf16[2,32,512]{2,1,0:T(8,128)(2,1)S(1)}, bf16[1,32,512]{2,1,0:T(8,128)(2,1)S(...) custom-call(s32[1]{0:T(128)} %bitcast.own_ref, s32[1]{0:T(128)} %bitcast.2.odd_col_ref, ...), custom_call_target="tpu_custom_call" | custom-call | flops 805306368 | bytes 6815744 | tf_op jit(solution)/shard_map/rim/pallas_call | solution.py:384
  16.7 3.0 %collective-permute-start.6 = (bf16[6,32,512]{2,1,0:T(8,128)(2,1)S(1)}, bf16[6,32,512]{2,1,0:T(8,128)(2,1)S(1)}, u32[]{:S(2)}, u32[]{:S(2)}) collective-permute-start(bf16[6,32,512]{2,1,0:T(8,128)(2,1)S(1)} %get-tuple-element.81), channel_id=1, source_target_pairs={{0,1},{1,0},{2,3},{3,2},{4,5},{5,4},{6,7},{7,6},{8,9},{9,8},{10,11... | collective-permute-start | bytes 589832 | tf_op jit(solution)/shard_map/ppermute | solution.py:642
  19.7 2.7 %collective-permute-start.4 = (bf16[2,32,512]{2,1,0:T(8,128)(2,1)S(1)}, bf16[2,32,512]{2,1,0:T(8,128)(2,1)S(1)}, u32[]{:S(2)}, u32[]{:S(2)}) collective-permute-start(bf16[2,32,512]{2,1,0:T(8,128)(2,1)S(1)} %get-tuple-element.78), channel_id=1, source_target_pairs={{0,14},{1,15},{2,12},{3,13},{4,10},{5,11},{6,8},{7,9},{8,6},{9,7},... | collective-permute-start | bytes 196616 | tf_op jit(solution)/shard_map/ppermute | solution.py:642
  22.3 1.1 %collective-permute-start.5 = (bf16[2,32,512]{2,1,0:T(8,128)(2,1)S(1)}, bf16[2,32,512]{2,1,0:T(8,128)(2,1)S(1)}, u32[]{:S(2)}, u32[]{:S(2)}) collective-permute-start(bf16[2,32,512]{2,1,0:T(8,128)(2,1)S(1)} %get-tuple-element.79), channel_id=1, source_target_pairs={{0,12},{1,13},{2,14},{3,15},{4,8},{5,9},{6,10},{7,11},{8,4},{9,5},... | collective-permute-start | bytes 196616 | tf_op jit(solution)/shard_map/ppermute | solution.py:642
  23.5 3.1 %collective-permute-start.7 = (bf16[2,32,512]{2,1,0:T(8,128)(2,1)S(1)}, bf16[2,32,512]{2,1,0:T(8,128)(2,1)S(1)}, u32[]{:S(2)}, u32[]{:S(2)}) collective-permute-start(bf16[2,32,512]{2,1,0:T(8,128)(2,1)S(1)} %get-tuple-element.82), channel_id=1, source_target_pairs={{0,10},{1,11},{2,8},{3,9},{4,14},{5,15},{6,12},{7,13},{8,2},{9,3},... | collective-permute-start | bytes 196616 | tf_op jit(solution)/shard_map/ppermute | solution.py:642
  26.6 1.1 %collective-permute-start.8 = (bf16[2,32,512]{2,1,0:T(8,128)(2,1)S(1)}, bf16[2,32,512]{2,1,0:T(8,128)(2,1)S(1)}, u32[]{:S(2)}, u32[]{:S(2)}) collective-permute-start(bf16[2,32,512]{2,1,0:T(8,128)(2,1)S(1)} %get-tuple-element.83), channel_id=1, source_target_pairs={{0,6},{1,7},{2,4},{3,5},{4,2},{5,3},{6,0},{7,1},{8,14},{9,15},{10,... | collective-permute-start | bytes 196616 | tf_op jit(solution)/shard_map/ppermute | solution.py:642
  27.7 0.9 %collective-permute-start.9 = (bf16[2,32,512]{2,1,0:T(8,128)(2,1)S(1)}, bf16[2,32,512]{2,1,0:T(8,128)(2,1)S(1)}, u32[]{:S(2)}, u32[]{:S(2)}) collective-permute-start(bf16[2,32,512]{2,1,0:T(8,128)(2,1)S(1)} %get-tuple-element.84), channel_id=1, source_target_pairs={{0,4},{1,5},{2,6},{3,7},{4,0},{5,1},{6,2},{7,3},{8,12},{9,13},{10,... | collective-permute-start | bytes 196616 | tf_op jit(solution)/shard_map/ppermute | solution.py:642
  28.6 4.5 %collective-permute-start.10 = (bf16[2,32,512]{2,1,0:T(8,128)(2,1)S(1)}, bf16[2,32,512]{2,1,0:T(8,128)(2,1)S(1)}, u32[]{:S(2)}, u32[]{:S(2)}) collective-permute-start(bf16[2,32,512]{2,1,0:T(8,128)(2,1)S(1)} %get-tuple-element.90), channel_id=1, source_target_pairs={{0,8},{1,9},{2,10},{3,11},{4,12},{5,13},{6,14},{7,15},{8,0},{9,1},... | collective-permute-start | bytes 196616 | tf_op jit(solution)/shard_map/ppermute | solution.py:642
  33.4 1.9 %collective-permute-done.7.refs_2_ = bf16[2,32,512]{2,1,0:T(8,128)(2,1)S(1)} collective-permute-done((bf16[2,32,512]{2,1,0:T(8,128)(2,1)S(1)}, bf16[2,32,512]{2,1,0:T(8,128)(2,1)S(1)}, u32[]{:S(2)}, u32[]{:S(2)}) %collective-permute-start.7) | collective-permute-done | bytes 65568 | tf_op jit(solution)/shard_map/ppermute | solution.py:642
  35.8 1.7 %collective-permute-done.11.refs_6_ = bf16[2,32,512]{2,1,0:T(8,128)(2,1)S(1)} collective-permute-done((bf16[2,32,512]{2,1,0:T(8,128)(2,1)S(1)}, bf16[2,32,512]{2,1,0:T(8,128)(2,1)S(1)}, u32[]{:S(2)}, u32[]{:S(2)}) %collective-permute-start.11) | collective-permute-done | bytes 65568 | tf_op jit(solution)/shard_map/ppermute | solution.py:642
  37.4 4.6 %attend.1 = (bf16[2,32,512]{2,1,0:T(8,128)(2,1)S(1)}, bf16[2,32,512]{2,1,0:T(8,128)(2,1)S(1)}, bf16[1,32,512]{2,1,0:T(8,128)(2,1)S(1)}, bf16[6,32,512]{2,1,0:T(8,128)(2,1)S(1)}, bf16[5,32,512]{2,1,0:T(8,128)(2,1)S(1)}) custom-call(bf16[2,32,512]{2,1,0:T(8,128)(2,1)S(1)} %collective-permute-done.4.refs_0_, ...), custom_call_target="tpu_custom_call" | custom-call | flops 1073741824 | bytes 2621440 | tf_op jit(solution)/shard_map/attend/pallas_call | solution.py:503
  42.1 1.8 %collective-permute-start.14 = (bf16[2,32,512]{2,1,0:T(8,128)(2,1)S(1)}, bf16[2,32,512]{2,1,0:T(8,128)(2,1)S(1)}, u32[]{:S(2)}, u32[]{:S(2)}) collective-permute-start(bf16[2,32,512]{2,1,0:T(8,128)(2,1)S(1)} %get-tuple-element.93), channel_id=1, source_target_pairs={{0,14},{1,15},{2,12},{3,13},{4,10},{5,11},{6,8},{7,9},{8,6},{9,7},... | collective-permute-start | bytes 196616 | tf_op jit(solution)/shard_map/ppermute | solution.py:642
  43.9 1.8 %collective-permute-start.15 = (bf16[2,32,512]{2,1,0:T(8,128)(2,1)S(1)}, bf16[2,32,512]{2,1,0:T(8,128)(2,1)S(1)}, u32[]{:S(2)}, u32[]{:S(2)}) collective-permute-start(bf16[2,32,512]{2,1,0:T(8,128)(2,1)S(1)} %get-tuple-element.94), channel_id=1, source_target_pairs={{0,12},{1,13},{2,14},{3,15},{4,8},{5,9},{6,10},{7,11},{8,4},{9,5},... | collective-permute-start | bytes 196616 | tf_op jit(solution)/shard_map/ppermute | solution.py:642
  46.1 3.1 %collective-permute-start.18 = (bf16[2,32,512]{2,1,0:T(8,128)(2,1)S(1)}, bf16[2,32,512]{2,1,0:T(8,128)(2,1)S(1)}, u32[]{:S(2)}, u32[]{:S(2)}) collective-permute-start(bf16[2,32,512]{2,1,0:T(8,128)(2,1)S(1)} %get-tuple-element.98), channel_id=1, source_target_pairs={{0,6},{1,7},{2,4},{3,5},{4,2},{5,3},{6,0},{7,1},{8,14},{9,15},{10,... | collective-permute-start | bytes 196616 | tf_op jit(solution)/shard_map/ppermute | solution.py:642
  49.8 1.8 %collective-permute-start.20 = (bf16[2,32,512]{2,1,0:T(8,128)(2,1)S(1)}, bf16[2,32,512]{2,1,0:T(8,128)(2,1)S(1)}, u32[]{:S(2)}, u32[]{:S(2)}) collective-permute-start(bf16[2,32,512]{2,1,0:T(8,128)(2,1)S(1)} %get-tuple-element.105), channel_id=1, source_target_pairs={{0,8},{1,9},{2,10},{3,11},{4,12},{5,13},{6,14},{7,15},{8,0},{9,1},... | collective-permute-start | bytes 196616 | tf_op jit(solution)/shard_map/ppermute | solution.py:642
  51.6 2.5 %collective-permute-start.21 = (bf16[2,32,512]{2,1,0:T(8,128)(2,1)S(1)}, bf16[2,32,512]{2,1,0:T(8,128)(2,1)S(1)}, u32[]{:S(2)}, u32[]{:S(2)}) collective-permute-start(bf16[2,32,512]{2,1,0:T(8,128)(2,1)S(1)} %get-tuple-element.106), channel_id=1, source_target_pairs={{0,2},{1,3},{2,0},{3,1},{4,6},{5,7},{6,4},{7,5},{8,10},{9,11},{10,... | collective-permute-start | bytes 196616 | tf_op jit(solution)/shard_map/ppermute | solution.py:642
  55.1 1.3 %collective-permute-done.20.refs_5_ = bf16[2,32,512]{2,1,0:T(8,128)(2,1)S(1)} collective-permute-done((bf16[2,32,512]{2,1,0:T(8,128)(2,1)S(1)}, bf16[2,32,512]{2,1,0:T(8,128)(2,1)S(1)}, u32[]{:S(2)}, u32[]{:S(2)}) %collective-permute-start.20) | collective-permute-done | bytes 65568 | tf_op jit(solution)/shard_map/ppermute | solution.py:642
  56.4 1.9 %finish.1 = f32[512,512]{1,0:T(8,128)} custom-call(s32[1]{0:T(128)} %bitcast.own_ref, bf16[2,32,512]{2,1,0:T(8,128)(2,1)S(1)} %collective-permute-done.14.refs_0_, bf16[2,32,512]{2,1,0:T(8,128)(2,1)S(1)} %collective-permute-done.15.refs_1_, bf16[2,32,512]{2,1,0:T(8,128)(2,1)S(1)} %collective-permute-done.17.refs_2_, ...), custom_call_target="tpu_custom_call" | custom-call | tf_op jit(solution)/shard_map/finish/pallas_call | solution.py:556
  (52 shorter events, 4.6 us)
Async XLA Ops:
  1.1 7.5 %collective-permute-start = (bf16[32,512]{1,0:T(8,128)(2,1)S(1)}, bf16[32,512]{1,0:T(8,128)(2,1)S(1)}, u32[]{:S(2)}, u32[]{:S(2)}) collective-permute-start(bf16[32,512]{1,0:T(8,128)(2,1)S(1)} %get-tuple-element.62), channel_id=1, source_target_pairs={{0,4},{8,12},{4,0},{12,8},{1,5},{9,13},{5,1},{13,9},{2,6},{10,14},... | collective-permute-start | bytes 98312 | tf_op jit(solution)/shard_map/ppermute | solution.py:573
  4.2 4.5 %collective-permute-start.1 = (bf16[32,512]{1,0:T(8,128)(2,1)S(1)}, bf16[32,512]{1,0:T(8,128)(2,1)S(1)}, u32[]{:S(2)}, u32[]{:S(2)}) collective-permute-start(bf16[32,512]{1,0:T(8,128)(2,1)S(1)} %get-tuple-element.63), channel_id=1, source_target_pairs={{4,8},{8,4},{5,9},{9,5},{6,10},{10,6},{7,11},{11,7},{20,24},{24,20... | collective-permute-start | bytes 98312 | tf_op jit(solution)/shard_map/ppermute | solution.py:573
  9.0 4.7 %collective-permute-start.2 = (bf16[32,512]{1,0:T(8,128)(2,1)S(1)}, bf16[32,512]{1,0:T(8,128)(2,1)S(1)}, u32[]{:S(2)}, u32[]{:S(2)}) collective-permute-start(bf16[32,512]{1,0:T(8,128)(2,1)S(1)} %get-tuple-element.76), channel_id=1, source_target_pairs={{0,1},{2,3},{1,0},{3,2},{4,5},{6,7},{5,4},{7,6},{8,9},{10,11},{9,8... | collective-permute-start | bytes 98312 | tf_op jit(solution)/shard_map/ppermute | solution.py:573
  9.1 4.6 %collective-permute-start.3 = (bf16[32,512]{1,0:T(8,128)(2,1)S(1)}, bf16[32,512]{1,0:T(8,128)(2,1)S(1)}, u32[]{:S(2)}, u32[]{:S(2)}) collective-permute-start(bf16[32,512]{1,0:T(8,128)(2,1)S(1)} %get-tuple-element.77), channel_id=1, source_target_pairs={{1,2},{2,1},{5,6},{6,5},{9,10},{10,9},{13,14},{14,13},{17,18},{18,... | collective-permute-start | bytes 98312 | tf_op jit(solution)/shard_map/ppermute | solution.py:573
  16.7 6.8 %collective-permute-start.6 = (bf16[6,32,512]{2,1,0:T(8,128)(2,1)S(1)}, bf16[6,32,512]{2,1,0:T(8,128)(2,1)S(1)}, u32[]{:S(2)}, u32[]{:S(2)}) collective-permute-start(bf16[6,32,512]{2,1,0:T(8,128)(2,1)S(1)} %get-tuple-element.81), channel_id=1, source_target_pairs={{0,1},{1,0},{2,3},{3,2},{4,5},{5,4},{6,7},{7,6},{8,9},{9,8},{10,11... | collective-permute-start | bytes 589832 | tf_op jit(solution)/shard_map/ppermute | solution.py:642
  19.7 8.9 %collective-permute-start.4 = (bf16[2,32,512]{2,1,0:T(8,128)(2,1)S(1)}, bf16[2,32,512]{2,1,0:T(8,128)(2,1)S(1)}, u32[]{:S(2)}, u32[]{:S(2)}) collective-permute-start(bf16[2,32,512]{2,1,0:T(8,128)(2,1)S(1)} %get-tuple-element.78), channel_id=1, source_target_pairs={{0,14},{1,15},{2,12},{3,13},{4,10},{5,11},{6,8},{7,9},{8,6},{9,7},... | collective-permute-start | bytes 196616 | tf_op jit(solution)/shard_map/ppermute | solution.py:642
  22.3 10.8 %collective-permute-start.5 = (bf16[2,32,512]{2,1,0:T(8,128)(2,1)S(1)}, bf16[2,32,512]{2,1,0:T(8,128)(2,1)S(1)}, u32[]{:S(2)}, u32[]{:S(2)}) collective-permute-start(bf16[2,32,512]{2,1,0:T(8,128)(2,1)S(1)} %get-tuple-element.79), channel_id=1, source_target_pairs={{0,12},{1,13},{2,14},{3,15},{4,8},{5,9},{6,10},{7,11},{8,4},{9,5},... | collective-permute-start | bytes 196616 | tf_op jit(solution)/shard_map/ppermute | solution.py:642
  23.5 11.7 %collective-permute-start.7 = (bf16[2,32,512]{2,1,0:T(8,128)(2,1)S(1)}, bf16[2,32,512]{2,1,0:T(8,128)(2,1)S(1)}, u32[]{:S(2)}, u32[]{:S(2)}) collective-permute-start(bf16[2,32,512]{2,1,0:T(8,128)(2,1)S(1)} %get-tuple-element.82), channel_id=1, source_target_pairs={{0,10},{1,11},{2,8},{3,9},{4,14},{5,15},{6,12},{7,13},{8,2},{9,3},... | collective-permute-start | bytes 196616 | tf_op jit(solution)/shard_map/ppermute | solution.py:642
  26.6 8.6 %collective-permute-start.8 = (bf16[2,32,512]{2,1,0:T(8,128)(2,1)S(1)}, bf16[2,32,512]{2,1,0:T(8,128)(2,1)S(1)}, u32[]{:S(2)}, u32[]{:S(2)}) collective-permute-start(bf16[2,32,512]{2,1,0:T(8,128)(2,1)S(1)} %get-tuple-element.83), channel_id=1, source_target_pairs={{0,6},{1,7},{2,4},{3,5},{4,2},{5,3},{6,0},{7,1},{8,14},{9,15},{10,... | collective-permute-start | bytes 196616 | tf_op jit(solution)/shard_map/ppermute | solution.py:642
  27.7 7.5 %collective-permute-start.9 = (bf16[2,32,512]{2,1,0:T(8,128)(2,1)S(1)}, bf16[2,32,512]{2,1,0:T(8,128)(2,1)S(1)}, u32[]{:S(2)}, u32[]{:S(2)}) collective-permute-start(bf16[2,32,512]{2,1,0:T(8,128)(2,1)S(1)} %get-tuple-element.84), channel_id=1, source_target_pairs={{0,4},{1,5},{2,6},{3,7},{4,0},{5,1},{6,2},{7,3},{8,12},{9,13},{10,... | collective-permute-start | bytes 196616 | tf_op jit(solution)/shard_map/ppermute | solution.py:642
  28.6 7.2 %collective-permute-start.10 = (bf16[2,32,512]{2,1,0:T(8,128)(2,1)S(1)}, bf16[2,32,512]{2,1,0:T(8,128)(2,1)S(1)}, u32[]{:S(2)}, u32[]{:S(2)}) collective-permute-start(bf16[2,32,512]{2,1,0:T(8,128)(2,1)S(1)} %get-tuple-element.90), channel_id=1, source_target_pairs={{0,8},{1,9},{2,10},{3,11},{4,12},{5,13},{6,14},{7,15},{8,0},{9,1},... | collective-permute-start | bytes 196616 | tf_op jit(solution)/shard_map/ppermute | solution.py:642
  33.1 4.3 %collective-permute-start.11 = (bf16[2,32,512]{2,1,0:T(8,128)(2,1)S(1)}, bf16[2,32,512]{2,1,0:T(8,128)(2,1)S(1)}, u32[]{:S(2)}, u32[]{:S(2)}) collective-permute-start(bf16[2,32,512]{2,1,0:T(8,128)(2,1)S(1)} %get-tuple-element.91), channel_id=1, source_target_pairs={{0,2},{1,3},{2,0},{3,1},{4,6},{5,7},{6,4},{7,5},{8,10},{9,11},{10,... | collective-permute-start | bytes 196616 | tf_op jit(solution)/shard_map/ppermute | solution.py:642
  35.2 2.2 %collective-permute-start.12 = (bf16[2,32,512]{2,1,0:T(8,128)(2,1)S(1)}, bf16[2,32,512]{2,1,0:T(8,128)(2,1)S(1)}, u32[]{:S(2)}, u32[]{:S(2)}) collective-permute-start(bf16[2,32,512]{2,1,0:T(8,128)(2,1)S(1)} %collective-permute-done.4.refs_0_), channel_id=1, source_target_pairs={{0,1},{1,0},{2,3},{3,2},{4,5},{5,4},{6,7},{7,6},{8,9},{9,8},{10,11... | collective-permute-start | bytes 196616 | tf_op jit(solution)/shard_map/ppermute | solution.py:642
  35.2 2.2 %collective-permute-start.13 = (bf16[2,32,512]{2,1,0:T(8,128)(2,1)S(1)}, bf16[2,32,512]{2,1,0:T(8,128)(2,1)S(1)}, u32[]{:S(2)}, u32[]{:S(2)}) collective-permute-start(bf16[2,32,512]{2,1,0:T(8,128)(2,1)S(1)} %collective-permute-done.5.refs_1_), channel_id=1, source_target_pairs={{0,1},{1,0},{2,3},{3,2},{4,5},{5,4},{6,7},{7,6},{8,9},{9,8},{10,11... | collective-permute-start | bytes 196616 | tf_op jit(solution)/shard_map/ppermute | solution.py:642
  42.0 3.6 %collective-permute-start.16 = (bf16[6,32,512]{2,1,0:T(8,128)(2,1)S(1)}, bf16[6,32,512]{2,1,0:T(8,128)(2,1)S(1)}, u32[]{:S(2)}, u32[]{:S(2)}) collective-permute-start(bf16[6,32,512]{2,1,0:T(8,128)(2,1)S(1)} %get-tuple-element.96), channel_id=1, source_target_pairs={{0,1},{1,0},{2,3},{3,2},{4,5},{5,4},{6,7},{7,6},{8,9},{9,8},{10,11... | collective-permute-start | bytes 589832 | tf_op jit(solution)/shard_map/ppermute | solution.py:642
  42.1 7.7 %collective-permute-start.14 = (bf16[2,32,512]{2,1,0:T(8,128)(2,1)S(1)}, bf16[2,32,512]{2,1,0:T(8,128)(2,1)S(1)}, u32[]{:S(2)}, u32[]{:S(2)}) collective-permute-start(bf16[2,32,512]{2,1,0:T(8,128)(2,1)S(1)} %get-tuple-element.93), channel_id=1, source_target_pairs={{0,14},{1,15},{2,12},{3,13},{4,10},{5,11},{6,8},{7,9},{8,6},{9,7},... | collective-permute-start | bytes 196616 | tf_op jit(solution)/shard_map/ppermute | solution.py:642
  43.9 7.7 %collective-permute-start.15 = (bf16[2,32,512]{2,1,0:T(8,128)(2,1)S(1)}, bf16[2,32,512]{2,1,0:T(8,128)(2,1)S(1)}, u32[]{:S(2)}, u32[]{:S(2)}) collective-permute-start(bf16[2,32,512]{2,1,0:T(8,128)(2,1)S(1)} %get-tuple-element.94), channel_id=1, source_target_pairs={{0,12},{1,13},{2,14},{3,15},{4,8},{5,9},{6,10},{7,11},{8,4},{9,5},... | collective-permute-start | bytes 196616 | tf_op jit(solution)/shard_map/ppermute | solution.py:642
  45.7 8.8 %collective-permute-start.17 = (bf16[2,32,512]{2,1,0:T(8,128)(2,1)S(1)}, bf16[2,32,512]{2,1,0:T(8,128)(2,1)S(1)}, u32[]{:S(2)}, u32[]{:S(2)}) collective-permute-start(bf16[2,32,512]{2,1,0:T(8,128)(2,1)S(1)} %get-tuple-element.97), channel_id=1, source_target_pairs={{0,10},{1,11},{2,8},{3,9},{4,14},{5,15},{6,12},{7,13},{8,2},{9,3},... | collective-permute-start | bytes 196616 | tf_op jit(solution)/shard_map/ppermute | solution.py:642
  46.1 8.4 %collective-permute-start.18 = (bf16[2,32,512]{2,1,0:T(8,128)(2,1)S(1)}, bf16[2,32,512]{2,1,0:T(8,128)(2,1)S(1)}, u32[]{:S(2)}, u32[]{:S(2)}) collective-permute-start(bf16[2,32,512]{2,1,0:T(8,128)(2,1)S(1)} %get-tuple-element.98), channel_id=1, source_target_pairs={{0,6},{1,7},{2,4},{3,5},{4,2},{5,3},{6,0},{7,1},{8,14},{9,15},{10,... | collective-permute-start | bytes 196616 | tf_op jit(solution)/shard_map/ppermute | solution.py:642
  49.2 5.4 %collective-permute-start.19 = (bf16[2,32,512]{2,1,0:T(8,128)(2,1)S(1)}, bf16[2,32,512]{2,1,0:T(8,128)(2,1)S(1)}, u32[]{:S(2)}, u32[]{:S(2)}) collective-permute-start(bf16[2,32,512]{2,1,0:T(8,128)(2,1)S(1)} %get-tuple-element.99), channel_id=1, source_target_pairs={{0,4},{1,5},{2,6},{3,7},{4,0},{5,1},{6,2},{7,3},{8,12},{9,13},{10,... | collective-permute-start | bytes 196616 | tf_op jit(solution)/shard_map/ppermute | solution.py:642
  49.8 6.6 %collective-permute-start.20 = (bf16[2,32,512]{2,1,0:T(8,128)(2,1)S(1)}, bf16[2,32,512]{2,1,0:T(8,128)(2,1)S(1)}, u32[]{:S(2)}, u32[]{:S(2)}) collective-permute-start(bf16[2,32,512]{2,1,0:T(8,128)(2,1)S(1)} %get-tuple-element.105), channel_id=1, source_target_pairs={{0,8},{1,9},{2,10},{3,11},{4,12},{5,13},{6,14},{7,15},{8,0},{9,1},... | collective-permute-start | bytes 196616 | tf_op jit(solution)/shard_map/ppermute | solution.py:642
  51.6 4.8 %collective-permute-start.21 = (bf16[2,32,512]{2,1,0:T(8,128)(2,1)S(1)}, bf16[2,32,512]{2,1,0:T(8,128)(2,1)S(1)}, u32[]{:S(2)}, u32[]{:S(2)}) collective-permute-start(bf16[2,32,512]{2,1,0:T(8,128)(2,1)S(1)} %get-tuple-element.106), channel_id=1, source_target_pairs={{0,2},{1,3},{2,0},{3,1},{4,6},{5,7},{6,4},{7,5},{8,10},{9,11},{10,... | collective-permute-start | bytes 196616 | tf_op jit(solution)/shard_map/ppermute | solution.py:642
  54.6 1.8 %collective-permute-start.22 = (bf16[2,32,512]{2,1,0:T(8,128)(2,1)S(1)}, bf16[2,32,512]{2,1,0:T(8,128)(2,1)S(1)}, u32[]{:S(2)}, u32[]{:S(2)}) collective-permute-start(bf16[2,32,512]{2,1,0:T(8,128)(2,1)S(1)} %collective-permute-done.14.refs_0_), channel_id=1, source_target_pairs={{0,1},{1,0},{2,3},{3,2},{4,5},{5,4},{6,7},{7,6},{8,9},{9,8},{10,11... | collective-permute-start | bytes 196616 | tf_op jit(solution)/shard_map/ppermute | solution.py:642
  54.6 1.8 %collective-permute-start.23 = (bf16[2,32,512]{2,1,0:T(8,128)(2,1)S(1)}, bf16[2,32,512]{2,1,0:T(8,128)(2,1)S(1)}, u32[]{:S(2)}, u32[]{:S(2)}) collective-permute-start(bf16[2,32,512]{2,1,0:T(8,128)(2,1)S(1)} %collective-permute-done.15.refs_1_), channel_id=1, source_target_pairs={{0,1},{1,0},{2,3},{3,2},{4,5},{5,4},{6,7},{7,6},{8,9},{9,8},{10,11... | collective-permute-start | bytes 196616 | tf_op jit(solution)/shard_map/ppermute | solution.py:642
  (8 other events, 78.8 us)

commit v19 on v18

--- a/solution.py
+++ b/solution.py
@@ -209,7 +209,7 @@
         foot = jnp.where(at_last, 0.0, value[-8:]) if high else value[-8:]
         return jnp.concatenate([head, value[8:-8], foot], axis=0)
 
-    def convolve(index, out_ref):
+    def convolve(index, out_ref, between):
         for sub in range(subs):
             chunk = (first + index) * subs + sub
             lanes = pl.ds(pl.multiple_of(chunk * LANES, LANES), LANES)
@@ -242,24 +242,36 @@
                     else:
                         made = clear_ends(gelu_of_half(done), True, True)
                     out_ref[(y - 1) * cols : y * cols, spot] = made.astype(jnp.bfloat16)
+                    between(sub * rows + y - 1)
 
     def project(index, in_ref, from_ref):
         piece = pl.ds(pl.multiple_of((first + index) * tile, tile), tile)
-        total_ref[...] = from_ref[...] + matmul(in_ref[...], w_project_ref[piece, :])
-
-    convolve(0, even_ref)
-    project(0, even_ref, start_ref)
-    convolve(1, odd_ref)
+        step = divisor(tokens, tokens // rows * 2, 16)
+
+        def between(turn):
+            if turn % subs == 0 and turn // subs * step < tokens:
+                part = slice(turn // subs * step, (turn // subs + 1) * step)
+                total_ref[part, :] = from_ref[part, :] + matmul(
+                    in_ref[part, :], w_project_ref[piece, :]
+                )
+
+        return between
+
+    def nothing(turn):
+        return None
+
+    convolve(0, even_ref, nothing)
+    convolve(1, odd_ref, project(0, even_ref, start_ref))
 
     def body(index, carry):
-        convolve(2 * index, even_ref)
-        project(2 * index - 1, odd_ref, total_ref)
-        convolve(2 * index + 1, odd_ref)
-        project(2 * index, even_ref, total_ref)
+        convolve(2 * index, even_ref, project(2 * index - 1, odd_ref, total_ref))
+        convolve(2 * index + 1, odd_ref, project(2 * index, even_ref, total_ref))
         return carry
 
     lax.fori_loop(1, count // 2, body, 0)
-    project(count - 1, odd_ref, total_ref)
+    last = project(count - 1, odd_ref, total_ref)
+    for turn in range(subs * rows):
+        last(turn)
 
 
 def inner(expanded, start, depth_kernel, w_project, rows, cols, first, count, tile):
@@ -431,22 +443,23 @@
         for j in range(group_heads)
     ]
     turn_values = identity(channels)
+    block = jnp.concatenate(
+        [
+            read_block(plan, in_refs, index, side, slice(s * members, (s + 1) * members))
+            for s in range(sets)
+            for index in range(slabs)
+            for side in range(sides)
+        ],
+        axis=0,
+    )
+    qkv = matmul(block, weight_ref[...]).astype(jnp.bfloat16)
     for s in range(sets):
-        piece = slice(s * members, (s + 1) * members)
-        block = jnp.concatenate(
-            [
-                read_block(plan, in_refs, index, side, piece)
-                for index in range(slabs)
-                for side in range(sides)
-            ],
-            axis=0,
-        )
-        qkv = matmul(block, weight_ref[...]).astype(jnp.bfloat16)
-        values = matmul_nt(turn_values, qkv[:, 2 * channels :]).astype(jnp.bfloat16)
+        own_rows = slice(s * count, (s + 1) * count)
+        values = matmul_nt(turn_values, qkv[own_rows, 2 * channels :]).astype(jnp.bfloat16)
         for group in range(groups):
-            lanes = slice(group * LANES, (group + 1) * LANES)
-            query_ref[s * groups + group] = qkv[:, lanes]
-            key_ref[s * groups + group] = qkv[:, channels + group * LANES : channels + (group + 1) * LANES]
+            spot = group * LANES
+            query_ref[s * groups + group] = qkv[own_rows, spot : spot + LANES]
+            key_ref[s * groups + group] = qkv[own_rows, channels + spot : channels + spot + LANES]
             for j in range(group_heads):
                 head = (group * group_heads + j) * head_width
                 value_ref[s * groups + group, j, :head_width] = values[head : head + head_width]

time: 58.6 us -> 58.9 us (level)
  starting transfers between devices: 33.7 us -> 33 us
  waiting for transfers between devices: 5.99 us -> 6.61 us
    ppermute x20, starting transfers between devices: 29.1 us -> 28.4 us  [swap(): lax.ppermute(slab, ('row', 'col'), [(i, i ^ mask) for i in range(devices)])]
    ppermute x20, waiting for transfers between devices: 5.98 us -> 6.6 us  [swap(): lax.ppermute(slab, ('row', 'col'), [(i, i ^ mask) for i in range(devices)])]
  transfers between devices with their start and end apart: 24 -> 24, of which waited for: 6 -> 5; matrix products, arithmetic and copies ran while one was open for 0% -> 0% of each run, Pallas kernels for 13% -> 14%
where the time goes in v19:
time: 58.9 us; the launch traced here: 58.7 us
  starting transfers between devices  33 us (56%)
  Pallas kernels  17.8 us (30%)
  waiting for transfers between devices  6.61 us (11%)
  local copies, waits for them, and re-layouts  0.93 us (2%)
    ppermute x20, starting transfers between devices, swap(): lax.ppermute(slab, ('row', 'col'), [(i, i ^ mask) for i in range(devices)])  28.4 us
    ppermute x20, waiting for transfers between devices, swap(): lax.ppermute(slab, ('row', 'col'), [(i, i ^ mask) for i in range(devices)])  6.6 us
    pallas_call x2, Pallas kernels, inner(): pl.pallas_call(functools.partial(inner_kernel, rows=rows, cols=cols, firs...  5.43 us
    ppermute x4, starting transfers between devices, swap_pairs(): return lax.ppermute(edge, axis, pairs + [(b, a) for a, b in pairs])  4.61 us
    pallas_call x1, Pallas kernels, attend(): pl.pallas_call(functools.partial(attend_kernel, plan=plan, sets=sets, cam...  4.53 us
    pallas_call x1, Pallas kernels, rim(): pl.pallas_call(functools.partial(rim_kernel, rows=rows, cols=cols, plan=p...  2.9 us
    pallas_call x1, Pallas kernels, expand(): pl.pallas_call(expand_kernel, in_specs=[vmem()] * 2, out_specs=vmem(), ou...  2.15 us
    pallas_call x1, Pallas kernels, finish(): pl.pallas_call(functools.partial(finish_kernel, plan=plan), in_specs=[pl....  1.94 us
  transfers between devices with their start and end apart: 24, of which 5 were waited for; matrix products, arithmetic and copies ran while one was open for 0% of the time, Pallas kernels for 14%

profile of v19, /device:TPU:0, one launch (start us, length us, event | category | flops | bytes accessed | tf_op | source)
XLA Modules:
  0.0 58.7 jit_solution(8121338077984405169)
XLA Ops:
  0.0 0.9 %slice_bitcast_fusion = (f32[32,512]{1,0:T(8,128)S(1)}, f32[32,512]{1,0:T(8,128)S(1)}) fusion(f32[16,32,512]{2,1,0:T(8,128)} %param.8), kind=kLoop, calls=%fused_computation | loop fusion | bytes 262144 | tf_op jit(solution)/shard_map/squeeze | solution.py:712
  1.1 3.1 %collective-permute-start = (bf16[32,512]{1,0:T(8,128)(2,1)S(1)}, bf16[32,512]{1,0:T(8,128)(2,1)S(1)}, u32[]{:S(2)}, u32[]{:S(2)}) collective-permute-start(bf16[32,512]{1,0:T(8,128)(2,1)S(1)} %get-tuple-element.62), channel_id=1, source_target_pairs={{0,4},{8,12},{4,0},{12,8},{1,5},{9,13},{5,1},{13,9},{2,6},{10,14},... | collective-permute-start | bytes 98312 | tf_op jit(solution)/shard_map/ppermute | solution.py:586
  5.2 2.2 %expand.1.expanded_ref = f32[8448,128]{1,0:T(8,128)S(1)} custom-call(bf16[512,512]{1,0:T(8,128)(2,1)S(1)} %half_norm.1.normed_ref, bf16[512,2048]{1,0:T(8,128)(2,1)S(1)} %copy-done), custom_call_target="tpu_custom_call" | custom-call | flops 10000000000 | bytes 6815744 | tf_op jit(solution)/shard_map/expand/pallas_call | solution.py:181
  7.4 1.3 %inner.2 = (f32[512,512]{1,0:T(8,128)S(1)}, f32[4,96,128]{2,1,0:T(8,128)S(1)}) custom-call(f32[8448,128]{1,0:T(8,128)S(1)} %expand.1.expanded_ref, f32[512,512]{1,0:T(8,128)S(1)} %bitcast.10, f32[3,3,2048]{2,1,0:T(4,128)S(1)} %copy-done.5, bf16[2048,512]{1,0:T(8,128)(2,1)S(1)} %copy-done.1), custom_call_target="tpu_custom_call" | custom-call | flops 4000000000 | bytes 3145728 | tf_op jit(solution)/shard_map/inner/pallas_call | solution.py:280
  10.0 4.1 %inner.3 = (f32[512,512]{1,0:T(8,128)S(1)}, f32[12,96,128]{2,1,0:T(8,128)S(1)}) custom-call(f32[8448,128]{1,0:T(8,128)S(1)} %expand.1.expanded_ref, f32[512,512]{1,0:T(8,128)S(1)} %get-tuple-element.67.start_ref, f32[3,3,2048]{2,1,0:T(4,128)S(1)} %copy-done.5, bf16[2048,512]{1,0:T(8,128)(2,1)S(1)} %copy-done.1), custom_call_target="tpu_custom_call" | custom-call | flops 12000000000 | bytes 5242880 | tf_op jit(solution)/shard_map/inner/pallas_call | solution.py:280
  14.2 2.9 %rim.1 = (f32[512,512]{1,0:T(8,128)S(1)}, bf16[2,32,512]{2,1,0:T(8,128)(2,1)S(1)}, bf16[2,32,512]{2,1,0:T(8,128)(2,1)S(1)}, bf16[1,32,512]{2,1,0:T(8,128)(2,1)S(...) custom-call(s32[1]{0:T(128)} %bitcast.own_ref, s32[1]{0:T(128)} %bitcast.2.odd_col_ref, ...), custom_call_target="tpu_custom_call" | custom-call | flops 805306368 | bytes 6815744 | tf_op jit(solution)/shard_map/rim/pallas_call | solution.py:396
  17.1 2.9 %collective-permute-start.6 = (bf16[6,32,512]{2,1,0:T(8,128)(2,1)S(1)}, bf16[6,32,512]{2,1,0:T(8,128)(2,1)S(1)}, u32[]{:S(2)}, u32[]{:S(2)}) collective-permute-start(bf16[6,32,512]{2,1,0:T(8,128)(2,1)S(1)} %get-tuple-element.81), channel_id=1, source_target_pairs={{0,1},{1,0},{2,3},{3,2},{4,5},{5,4},{6,7},{7,6},{8,9},{9,8},{10,11... | collective-permute-start | bytes 589832 | tf_op jit(solution)/shard_map/ppermute | solution.py:655
  20.0 2.7 %collective-permute-start.4 = (bf16[2,32,512]{2,1,0:T(8,128)(2,1)S(1)}, bf16[2,32,512]{2,1,0:T(8,128)(2,1)S(1)}, u32[]{:S(2)}, u32[]{:S(2)}) collective-permute-start(bf16[2,32,512]{2,1,0:T(8,128)(2,1)S(1)} %get-tuple-element.78), channel_id=1, source_target_pairs={{0,14},{1,15},{2,12},{3,13},{4,10},{5,11},{6,8},{7,9},{8,6},{9,7},... | collective-permute-start | bytes 196616 | tf_op jit(solution)/shard_map/ppermute | solution.py:655
  22.7 1.1 %collective-permute-start.5 = (bf16[2,32,512]{2,1,0:T(8,128)(2,1)S(1)}, bf16[2,32,512]{2,1,0:T(8,128)(2,1)S(1)}, u32[]{:S(2)}, u32[]{:S(2)}) collective-permute-start(bf16[2,32,512]{2,1,0:T(8,128)(2,1)S(1)} %get-tuple-element.79), channel_id=1, source_target_pairs={{0,12},{1,13},{2,14},{3,15},{4,8},{5,9},{6,10},{7,11},{8,4},{9,5},... | collective-permute-start | bytes 196616 | tf_op jit(solution)/shard_map/ppermute | solution.py:655
  23.9 3.0 %collective-permute-start.7 = (bf16[2,32,512]{2,1,0:T(8,128)(2,1)S(1)}, bf16[2,32,512]{2,1,0:T(8,128)(2,1)S(1)}, u32[]{:S(2)}, u32[]{:S(2)}) collective-permute-start(bf16[2,32,512]{2,1,0:T(8,128)(2,1)S(1)} %get-tuple-element.82), channel_id=1, source_target_pairs={{0,10},{1,11},{2,8},{3,9},{4,14},{5,15},{6,12},{7,13},{8,2},{9,3},... | collective-permute-start | bytes 196616 | tf_op jit(solution)/shard_map/ppermute | solution.py:655
  26.9 1.2 %collective-permute-start.8 = (bf16[2,32,512]{2,1,0:T(8,128)(2,1)S(1)}, bf16[2,32,512]{2,1,0:T(8,128)(2,1)S(1)}, u32[]{:S(2)}, u32[]{:S(2)}) collective-permute-start(bf16[2,32,512]{2,1,0:T(8,128)(2,1)S(1)} %get-tuple-element.83), channel_id=1, source_target_pairs={{0,6},{1,7},{2,4},{3,5},{4,2},{5,3},{6,0},{7,1},{8,14},{9,15},{10,... | collective-permute-start | bytes 196616 | tf_op jit(solution)/shard_map/ppermute | solution.py:655
  28.1 0.8 %collective-permute-start.9 = (bf16[2,32,512]{2,1,0:T(8,128)(2,1)S(1)}, bf16[2,32,512]{2,1,0:T(8,128)(2,1)S(1)}, u32[]{:S(2)}, u32[]{:S(2)}) collective-permute-start(bf16[2,32,512]{2,1,0:T(8,128)(2,1)S(1)} %get-tuple-element.84), channel_id=1, source_target_pairs={{0,4},{1,5},{2,6},{3,7},{4,0},{5,1},{6,2},{7,3},{8,12},{9,13},{10,... | collective-permute-start | bytes 196616 | tf_op jit(solution)/shard_map/ppermute | solution.py:655
  28.9 4.6 %collective-permute-start.10 = (bf16[2,32,512]{2,1,0:T(8,128)(2,1)S(1)}, bf16[2,32,512]{2,1,0:T(8,128)(2,1)S(1)}, u32[]{:S(2)}, u32[]{:S(2)}) collective-permute-start(bf16[2,32,512]{2,1,0:T(8,128)(2,1)S(1)} %get-tuple-element.90), channel_id=1, source_target_pairs={{0,8},{1,9},{2,10},{3,11},{4,12},{5,13},{6,14},{7,15},{8,0},{9,1},... | collective-permute-start | bytes 196616 | tf_op jit(solution)/shard_map/ppermute | solution.py:655
  33.9 1.7 %collective-permute-done.7.refs_2_ = bf16[2,32,512]{2,1,0:T(8,128)(2,1)S(1)} collective-permute-done((bf16[2,32,512]{2,1,0:T(8,128)(2,1)S(1)}, bf16[2,32,512]{2,1,0:T(8,128)(2,1)S(1)}, u32[]{:S(2)}, u32[]{:S(2)}) %collective-permute-start.7) | collective-permute-done | bytes 65568 | tf_op jit(solution)/shard_map/ppermute | solution.py:655
  36.1 1.7 %collective-permute-done.11.refs_6_ = bf16[2,32,512]{2,1,0:T(8,128)(2,1)S(1)} collective-permute-done((bf16[2,32,512]{2,1,0:T(8,128)(2,1)S(1)}, bf16[2,32,512]{2,1,0:T(8,128)(2,1)S(1)}, u32[]{:S(2)}, u32[]{:S(2)}) %collective-permute-start.11) | collective-permute-done | bytes 65568 | tf_op jit(solution)/shard_map/ppermute | solution.py:655
  37.8 4.5 %attend.1 = (bf16[2,32,512]{2,1,0:T(8,128)(2,1)S(1)}, bf16[2,32,512]{2,1,0:T(8,128)(2,1)S(1)}, bf16[1,32,512]{2,1,0:T(8,128)(2,1)S(1)}, bf16[6,32,512]{2,1,0:T(8,128)(2,1)S(1)}, bf16[5,32,512]{2,1,0:T(8,128)(2,1)S(1)}) custom-call(bf16[2,32,512]{2,1,0:T(8,128)(2,1)S(1)} %collective-permute-done.4.refs_0_, ...), custom_call_target="tpu_custom_call" | custom-call | flops 1073741824 | bytes 2621440 | tf_op jit(solution)/shard_map/attend/pallas_call | solution.py:516
  42.4 1.7 %collective-permute-start.14 = (bf16[2,32,512]{2,1,0:T(8,128)(2,1)S(1)}, bf16[2,32,512]{2,1,0:T(8,128)(2,1)S(1)}, u32[]{:S(2)}, u32[]{:S(2)}) collective-permute-start(bf16[2,32,512]{2,1,0:T(8,128)(2,1)S(1)} %get-tuple-element.93), channel_id=1, source_target_pairs={{0,14},{1,15},{2,12},{3,13},{4,10},{5,11},{6,8},{7,9},{8,6},{9,7},... | collective-permute-start | bytes 196616 | tf_op jit(solution)/shard_map/ppermute | solution.py:655
  44.1 2.0 %collective-permute-start.15 = (bf16[2,32,512]{2,1,0:T(8,128)(2,1)S(1)}, bf16[2,32,512]{2,1,0:T(8,128)(2,1)S(1)}, u32[]{:S(2)}, u32[]{:S(2)}) collective-permute-start(bf16[2,32,512]{2,1,0:T(8,128)(2,1)S(1)} %get-tuple-element.94), channel_id=1, source_target_pairs={{0,12},{1,13},{2,14},{3,15},{4,8},{5,9},{6,10},{7,11},{8,4},{9,5},... | collective-permute-start | bytes 196616 | tf_op jit(solution)/shard_map/ppermute | solution.py:655
  46.4 3.1 %collective-permute-start.18 = (bf16[2,32,512]{2,1,0:T(8,128)(2,1)S(1)}, bf16[2,32,512]{2,1,0:T(8,128)(2,1)S(1)}, u32[]{:S(2)}, u32[]{:S(2)}) collective-permute-start(bf16[2,32,512]{2,1,0:T(8,128)(2,1)S(1)} %get-tuple-element.98), channel_id=1, source_target_pairs={{0,6},{1,7},{2,4},{3,5},{4,2},{5,3},{6,0},{7,1},{8,14},{9,15},{10,... | collective-permute-start | bytes 196616 | tf_op jit(solution)/shard_map/ppermute | solution.py:655
  50.2 1.9 %collective-permute-start.20 = (bf16[2,32,512]{2,1,0:T(8,128)(2,1)S(1)}, bf16[2,32,512]{2,1,0:T(8,128)(2,1)S(1)}, u32[]{:S(2)}, u32[]{:S(2)}) collective-permute-start(bf16[2,32,512]{2,1,0:T(8,128)(2,1)S(1)} %get-tuple-element.105), channel_id=1, source_target_pairs={{0,8},{1,9},{2,10},{3,11},{4,12},{5,13},{6,14},{7,15},{8,0},{9,1},... | collective-permute-start | bytes 196616 | tf_op jit(solution)/shard_map/ppermute | solution.py:655
  52.1 1.7 %collective-permute-start.21 = (bf16[2,32,512]{2,1,0:T(8,128)(2,1)S(1)}, bf16[2,32,512]{2,1,0:T(8,128)(2,1)S(1)}, u32[]{:S(2)}, u32[]{:S(2)}) collective-permute-start(bf16[2,32,512]{2,1,0:T(8,128)(2,1)S(1)} %get-tuple-element.106), channel_id=1, source_target_pairs={{0,2},{1,3},{2,0},{3,1},{4,6},{5,7},{6,4},{7,5},{8,10},{9,11},{10,... | collective-permute-start | bytes 196616 | tf_op jit(solution)/shard_map/ppermute | solution.py:655
  53.7 1.1 %collective-permute-done.17.refs_2_ = bf16[2,32,512]{2,1,0:T(8,128)(2,1)S(1)} collective-permute-done((bf16[2,32,512]{2,1,0:T(8,128)(2,1)S(1)}, bf16[2,32,512]{2,1,0:T(8,128)(2,1)S(1)}, u32[]{:S(2)}, u32[]{:S(2)}) %collective-permute-start.17) | collective-permute-done | bytes 65568 | tf_op jit(solution)/shard_map/ppermute | solution.py:655
  55.3 1.4 %collective-permute-done.20.refs_5_ = bf16[2,32,512]{2,1,0:T(8,128)(2,1)S(1)} collective-permute-done((bf16[2,32,512]{2,1,0:T(8,128)(2,1)S(1)}, bf16[2,32,512]{2,1,0:T(8,128)(2,1)S(1)}, u32[]{:S(2)}, u32[]{:S(2)}) %collective-permute-start.20) | collective-permute-done | bytes 65568 | tf_op jit(solution)/shard_map/ppermute | solution.py:655
  56.8 1.9 %finish.1 = f32[512,512]{1,0:T(8,128)} custom-call(s32[1]{0:T(128)} %bitcast.own_ref, bf16[2,32,512]{2,1,0:T(8,128)(2,1)S(1)} %collective-permute-done.14.refs_0_, bf16[2,32,512]{2,1,0:T(8,128)(2,1)S(1)} %collective-permute-done.15.refs_1_, bf16[2,32,512]{2,1,0:T(8,128)(2,1)S(1)} %collective-permute-done.17.refs_2_, ...), custom_call_target="tpu_custom_call" | custom-call | tf_op jit(solution)/shard_map/finish/pallas_call | solution.py:569
  (52 shorter events, 4.9 us)
Async XLA Ops:
  1.1 7.6 %collective-permute-start = (bf16[32,512]{1,0:T(8,128)(2,1)S(1)}, bf16[32,512]{1,0:T(8,128)(2,1)S(1)}, u32[]{:S(2)}, u32[]{:S(2)}) collective-permute-start(bf16[32,512]{1,0:T(8,128)(2,1)S(1)} %get-tuple-element.62), channel_id=1, source_target_pairs={{0,4},{8,12},{4,0},{12,8},{1,5},{9,13},{5,1},{13,9},{2,6},{10,14},... | collective-permute-start | bytes 98312 | tf_op jit(solution)/shard_map/ppermute | solution.py:586
  4.2 4.5 %collective-permute-start.1 = (bf16[32,512]{1,0:T(8,128)(2,1)S(1)}, bf16[32,512]{1,0:T(8,128)(2,1)S(1)}, u32[]{:S(2)}, u32[]{:S(2)}) collective-permute-start(bf16[32,512]{1,0:T(8,128)(2,1)S(1)} %get-tuple-element.63), channel_id=1, source_target_pairs={{4,8},{8,4},{5,9},{9,5},{6,10},{10,6},{7,11},{11,7},{20,24},{24,20... | collective-permute-start | bytes 98312 | tf_op jit(solution)/shard_map/ppermute | solution.py:586
  9.1 5.0 %collective-permute-start.2 = (bf16[32,512]{1,0:T(8,128)(2,1)S(1)}, bf16[32,512]{1,0:T(8,128)(2,1)S(1)}, u32[]{:S(2)}, u32[]{:S(2)}) collective-permute-start(bf16[32,512]{1,0:T(8,128)(2,1)S(1)} %get-tuple-element.76), channel_id=1, source_target_pairs={{0,1},{2,3},{1,0},{3,2},{4,5},{6,7},{5,4},{7,6},{8,9},{10,11},{9,8... | collective-permute-start | bytes 98312 | tf_op jit(solution)/shard_map/ppermute | solution.py:586
  9.2 5.0 %collective-permute-start.3 = (bf16[32,512]{1,0:T(8,128)(2,1)S(1)}, bf16[32,512]{1,0:T(8,128)(2,1)S(1)}, u32[]{:S(2)}, u32[]{:S(2)}) collective-permute-start(bf16[32,512]{1,0:T(8,128)(2,1)S(1)} %get-tuple-element.77), channel_id=1, source_target_pairs={{1,2},{2,1},{5,6},{6,5},{9,10},{10,9},{13,14},{14,13},{17,18},{18,... | collective-permute-start | bytes 98312 | tf_op jit(solution)/shard_map/ppermute | solution.py:586
  17.1 6.8 %collective-permute-start.6 = (bf16[6,32,512]{2,1,0:T(8,128)(2,1)S(1)}, bf16[6,32,512]{2,1,0:T(8,128)(2,1)S(1)}, u32[]{:S(2)}, u32[]{:S(2)}) collective-permute-start(bf16[6,32,512]{2,1,0:T(8,128)(2,1)S(1)} %get-tuple-element.81), channel_id=1, source_target_pairs={{0,1},{1,0},{2,3},{3,2},{4,5},{5,4},{6,7},{7,6},{8,9},{9,8},{10,11... | collective-permute-start | bytes 589832 | tf_op jit(solution)/shard_map/ppermute | solution.py:655
  20.0 8.9 %collective-permute-start.4 = (bf16[2,32,512]{2,1,0:T(8,128)(2,1)S(1)}, bf16[2,32,512]{2,1,0:T(8,128)(2,1)S(1)}, u32[]{:S(2)}, u32[]{:S(2)}) collective-permute-start(bf16[2,32,512]{2,1,0:T(8,128)(2,1)S(1)} %get-tuple-element.78), channel_id=1, source_target_pairs={{0,14},{1,15},{2,12},{3,13},{4,10},{5,11},{6,8},{7,9},{8,6},{9,7},... | collective-permute-start | bytes 196616 | tf_op jit(solution)/shard_map/ppermute | solution.py:655
  22.7 10.8 %collective-permute-start.5 = (bf16[2,32,512]{2,1,0:T(8,128)(2,1)S(1)}, bf16[2,32,512]{2,1,0:T(8,128)(2,1)S(1)}, u32[]{:S(2)}, u32[]{:S(2)}) collective-permute-start(bf16[2,32,512]{2,1,0:T(8,128)(2,1)S(1)} %get-tuple-element.79), channel_id=1, source_target_pairs={{0,12},{1,13},{2,14},{3,15},{4,8},{5,9},{6,10},{7,11},{8,4},{9,5},... | collective-permute-start | bytes 196616 | tf_op jit(solution)/shard_map/ppermute | solution.py:655
  23.9 11.7 %collective-permute-start.7 = (bf16[2,32,512]{2,1,0:T(8,128)(2,1)S(1)}, bf16[2,32,512]{2,1,0:T(8,128)(2,1)S(1)}, u32[]{:S(2)}, u32[]{:S(2)}) collective-permute-start(bf16[2,32,512]{2,1,0:T(8,128)(2,1)S(1)} %get-tuple-element.82), channel_id=1, source_target_pairs={{0,10},{1,11},{2,8},{3,9},{4,14},{5,15},{6,12},{7,13},{8,2},{9,3},... | collective-permute-start | bytes 196616 | tf_op jit(solution)/shard_map/ppermute | solution.py:655
  26.9 8.7 %collective-permute-start.8 = (bf16[2,32,512]{2,1,0:T(8,128)(2,1)S(1)}, bf16[2,32,512]{2,1,0:T(8,128)(2,1)S(1)}, u32[]{:S(2)}, u32[]{:S(2)}) collective-permute-start(bf16[2,32,512]{2,1,0:T(8,128)(2,1)S(1)} %get-tuple-element.83), channel_id=1, source_target_pairs={{0,6},{1,7},{2,4},{3,5},{4,2},{5,3},{6,0},{7,1},{8,14},{9,15},{10,... | collective-permute-start | bytes 196616 | tf_op jit(solution)/shard_map/ppermute | solution.py:655
  28.1 7.5 %collective-permute-start.9 = (bf16[2,32,512]{2,1,0:T(8,128)(2,1)S(1)}, bf16[2,32,512]{2,1,0:T(8,128)(2,1)S(1)}, u32[]{:S(2)}, u32[]{:S(2)}) collective-permute-start(bf16[2,32,512]{2,1,0:T(8,128)(2,1)S(1)} %get-tuple-element.84), channel_id=1, source_target_pairs={{0,4},{1,5},{2,6},{3,7},{4,0},{5,1},{6,2},{7,3},{8,12},{9,13},{10,... | collective-permute-start | bytes 196616 | tf_op jit(solution)/shard_map/ppermute | solution.py:655
  28.9 7.2 %collective-permute-start.10 = (bf16[2,32,512]{2,1,0:T(8,128)(2,1)S(1)}, bf16[2,32,512]{2,1,0:T(8,128)(2,1)S(1)}, u32[]{:S(2)}, u32[]{:S(2)}) collective-permute-start(bf16[2,32,512]{2,1,0:T(8,128)(2,1)S(1)} %get-tuple-element.90), channel_id=1, source_target_pairs={{0,8},{1,9},{2,10},{3,11},{4,12},{5,13},{6,14},{7,15},{8,0},{9,1},... | collective-permute-start | bytes 196616 | tf_op jit(solution)/shard_map/ppermute | solution.py:655
  33.5 4.3 %collective-permute-start.11 = (bf16[2,32,512]{2,1,0:T(8,128)(2,1)S(1)}, bf16[2,32,512]{2,1,0:T(8,128)(2,1)S(1)}, u32[]{:S(2)}, u32[]{:S(2)}) collective-permute-start(bf16[2,32,512]{2,1,0:T(8,128)(2,1)S(1)} %get-tuple-element.91), channel_id=1, source_target_pairs={{0,2},{1,3},{2,0},{3,1},{4,6},{5,7},{6,4},{7,5},{8,10},{9,11},{10,... | collective-permute-start | bytes 196616 | tf_op jit(solution)/shard_map/ppermute | solution.py:655
  35.6 2.2 %collective-permute-start.12 = (bf16[2,32,512]{2,1,0:T(8,128)(2,1)S(1)}, bf16[2,32,512]{2,1,0:T(8,128)(2,1)S(1)}, u32[]{:S(2)}, u32[]{:S(2)}) collective-permute-start(bf16[2,32,512]{2,1,0:T(8,128)(2,1)S(1)} %collective-permute-done.4.refs_0_), channel_id=1, source_target_pairs={{0,1},{1,0},{2,3},{3,2},{4,5},{5,4},{6,7},{7,6},{8,9},{9,8},{10,11... | collective-permute-start | bytes 196616 | tf_op jit(solution)/shard_map/ppermute | solution.py:655
  35.6 2.2 %collective-permute-start.13 = (bf16[2,32,512]{2,1,0:T(8,128)(2,1)S(1)}, bf16[2,32,512]{2,1,0:T(8,128)(2,1)S(1)}, u32[]{:S(2)}, u32[]{:S(2)}) collective-permute-start(bf16[2,32,512]{2,1,0:T(8,128)(2,1)S(1)} %collective-permute-done.5.refs_1_), channel_id=1, source_target_pairs={{0,1},{1,0},{2,3},{3,2},{4,5},{5,4},{6,7},{7,6},{8,9},{9,8},{10,11... | collective-permute-start | bytes 196616 | tf_op jit(solution)/shard_map/ppermute | solution.py:655
  42.4 3.8 %collective-permute-start.16 = (bf16[6,32,512]{2,1,0:T(8,128)(2,1)S(1)}, bf16[6,32,512]{2,1,0:T(8,128)(2,1)S(1)}, u32[]{:S(2)}, u32[]{:S(2)}) collective-permute-start(bf16[6,32,512]{2,1,0:T(8,128)(2,1)S(1)} %get-tuple-element.96), channel_id=1, source_target_pairs={{0,1},{1,0},{2,3},{3,2},{4,5},{5,4},{6,7},{7,6},{8,9},{9,8},{10,11... | collective-permute-start | bytes 589832 | tf_op jit(solution)/shard_map/ppermute | solution.py:655
  42.4 7.8 %collective-permute-start.14 = (bf16[2,32,512]{2,1,0:T(8,128)(2,1)S(1)}, bf16[2,32,512]{2,1,0:T(8,128)(2,1)S(1)}, u32[]{:S(2)}, u32[]{:S(2)}) collective-permute-start(bf16[2,32,512]{2,1,0:T(8,128)(2,1)S(1)} %get-tuple-element.93), channel_id=1, source_target_pairs={{0,14},{1,15},{2,12},{3,13},{4,10},{5,11},{6,8},{7,9},{8,6},{9,7},... | collective-permute-start | bytes 196616 | tf_op jit(solution)/shard_map/ppermute | solution.py:655
  44.1 8.0 %collective-permute-start.15 = (bf16[2,32,512]{2,1,0:T(8,128)(2,1)S(1)}, bf16[2,32,512]{2,1,0:T(8,128)(2,1)S(1)}, u32[]{:S(2)}, u32[]{:S(2)}) collective-permute-start(bf16[2,32,512]{2,1,0:T(8,128)(2,1)S(1)} %get-tuple-element.94), channel_id=1, source_target_pairs={{0,12},{1,13},{2,14},{3,15},{4,8},{5,9},{6,10},{7,11},{8,4},{9,5},... | collective-permute-start | bytes 196616 | tf_op jit(solution)/shard_map/ppermute | solution.py:655
  46.2 8.6 %collective-permute-start.17 = (bf16[2,32,512]{2,1,0:T(8,128)(2,1)S(1)}, bf16[2,32,512]{2,1,0:T(8,128)(2,1)S(1)}, u32[]{:S(2)}, u32[]{:S(2)}) collective-permute-start(bf16[2,32,512]{2,1,0:T(8,128)(2,1)S(1)} %get-tuple-element.97), channel_id=1, source_target_pairs={{0,10},{1,11},{2,8},{3,9},{4,14},{5,15},{6,12},{7,13},{8,2},{9,3},... | collective-permute-start | bytes 196616 | tf_op jit(solution)/shard_map/ppermute | solution.py:655
  46.4 8.4 %collective-permute-start.18 = (bf16[2,32,512]{2,1,0:T(8,128)(2,1)S(1)}, bf16[2,32,512]{2,1,0:T(8,128)(2,1)S(1)}, u32[]{:S(2)}, u32[]{:S(2)}) collective-permute-start(bf16[2,32,512]{2,1,0:T(8,128)(2,1)S(1)} %get-tuple-element.98), channel_id=1, source_target_pairs={{0,6},{1,7},{2,4},{3,5},{4,2},{5,3},{6,0},{7,1},{8,14},{9,15},{10,... | collective-permute-start | bytes 196616 | tf_op jit(solution)/shard_map/ppermute | solution.py:655
  49.5 5.3 %collective-permute-start.19 = (bf16[2,32,512]{2,1,0:T(8,128)(2,1)S(1)}, bf16[2,32,512]{2,1,0:T(8,128)(2,1)S(1)}, u32[]{:S(2)}, u32[]{:S(2)}) collective-permute-start(bf16[2,32,512]{2,1,0:T(8,128)(2,1)S(1)} %get-tuple-element.99), channel_id=1, source_target_pairs={{0,4},{1,5},{2,6},{3,7},{4,0},{5,1},{6,2},{7,3},{8,12},{9,13},{10,... | collective-permute-start | bytes 196616 | tf_op jit(solution)/shard_map/ppermute | solution.py:655
  50.2 6.6 %collective-permute-start.20 = (bf16[2,32,512]{2,1,0:T(8,128)(2,1)S(1)}, bf16[2,32,512]{2,1,0:T(8,128)(2,1)S(1)}, u32[]{:S(2)}, u32[]{:S(2)}) collective-permute-start(bf16[2,32,512]{2,1,0:T(8,128)(2,1)S(1)} %get-tuple-element.105), channel_id=1, source_target_pairs={{0,8},{1,9},{2,10},{3,11},{4,12},{5,13},{6,14},{7,15},{8,0},{9,1},... | collective-permute-start | bytes 196616 | tf_op jit(solution)/shard_map/ppermute | solution.py:655
  52.1 4.7 %collective-permute-start.21 = (bf16[2,32,512]{2,1,0:T(8,128)(2,1)S(1)}, bf16[2,32,512]{2,1,0:T(8,128)(2,1)S(1)}, u32[]{:S(2)}, u32[]{:S(2)}) collective-permute-start(bf16[2,32,512]{2,1,0:T(8,128)(2,1)S(1)} %get-tuple-element.106), channel_id=1, source_target_pairs={{0,2},{1,3},{2,0},{3,1},{4,6},{5,7},{6,4},{7,5},{8,10},{9,11},{10,... | collective-permute-start | bytes 196616 | tf_op jit(solution)/shard_map/ppermute | solution.py:655
  54.8 1.9 %collective-permute-start.22 = (bf16[2,32,512]{2,1,0:T(8,128)(2,1)S(1)}, bf16[2,32,512]{2,1,0:T(8,128)(2,1)S(1)}, u32[]{:S(2)}, u32[]{:S(2)}) collective-permute-start(bf16[2,32,512]{2,1,0:T(8,128)(2,1)S(1)} %collective-permute-done.14.refs_0_), channel_id=1, source_target_pairs={{0,1},{1,0},{2,3},{3,2},{4,5},{5,4},{6,7},{7,6},{8,9},{9,8},{10,11... | collective-permute-start | bytes 196616 | tf_op jit(solution)/shard_map/ppermute | solution.py:655
  54.8 1.9 %collective-permute-start.23 = (bf16[2,32,512]{2,1,0:T(8,128)(2,1)S(1)}, bf16[2,32,512]{2,1,0:T(8,128)(2,1)S(1)}, u32[]{:S(2)}, u32[]{:S(2)}) collective-permute-start(bf16[2,32,512]{2,1,0:T(8,128)(2,1)S(1)} %collective-permute-done.15.refs_1_), channel_id=1, source_target_pairs={{0,1},{1,0},{2,3},{3,2},{4,5},{5,4},{6,7},{7,6},{8,9},{9,8},{10,11... | collective-permute-start | bytes 196616 | tf_op jit(solution)/shard_map/ppermute | solution.py:655
  (8 other events, 79.0 us)

commit v20 on v19

--- a/solution.py
+++ b/solution.py
@@ -156,20 +156,15 @@
     tokens = normed_ref.shape[0]
     width = weight_ref.shape[1]
     tile = divisor(width, 512, LANES)
-    step = divisor(tokens, 128, 16)
-    starts = range(0, tokens, step)
 
     def body(index, carry):
         lanes = pl.ds(pl.multiple_of(index * tile, tile), tile)
-        for start in starts:
-            made = gelu_of_half(
-                matmul(normed_ref[start : start + step, :], weight_ref[:, lanes])
-            )
-            for sub in range(tile // LANES):
-                row = (index * (tile // LANES) + sub) * padded_rows(tokens) + 8 + start
-                out_ref[pl.ds(pl.multiple_of(row, 8), step), :] = made[
-                    :, sub * LANES : (sub + 1) * LANES
-                ]
+        made = gelu_of_half(matmul(normed_ref[...], weight_ref[:, lanes]))
+        for sub in range(tile // LANES):
+            row = (index * (tile // LANES) + sub) * padded_rows(tokens) + 8
+            out_ref[pl.ds(pl.multiple_of(row, 8), tokens), :] = made[
+                :, sub * LANES : (sub + 1) * LANES
+            ]
         return carry
 
     lax.fori_loop(0, width // tile, body, 0)
@@ -209,7 +204,7 @@
         foot = jnp.where(at_last, 0.0, value[-8:]) if high else value[-8:]
         return jnp.concatenate([head, value[8:-8], foot], axis=0)
 
-    def convolve(index, out_ref, between):
+    def convolve(index, out_ref):
         for sub in range(subs):
             chunk = (first + index) * subs + sub
             lanes = pl.ds(pl.multiple_of(chunk * LANES, LANES), LANES)
@@ -242,36 +237,24 @@
                     else:
                         made = clear_ends(gelu_of_half(done), True, True)
                     out_ref[(y - 1) * cols : y * cols, spot] = made.astype(jnp.bfloat16)
-                    between(sub * rows + y - 1)
 
     def project(index, in_ref, from_ref):
         piece = pl.ds(pl.multiple_of((first + index) * tile, tile), tile)
-        step = divisor(tokens, tokens // rows * 2, 16)
-
-        def between(turn):
-            if turn % subs == 0 and turn // subs * step < tokens:
-                part = slice(turn // subs * step, (turn // subs + 1) * step)
-                total_ref[part, :] = from_ref[part, :] + matmul(
-                    in_ref[part, :], w_project_ref[piece, :]
-                )
-
-        return between
-
-    def nothing(turn):
-        return None
-
-    convolve(0, even_ref, nothing)
-    convolve(1, odd_ref, project(0, even_ref, start_ref))
+        total_ref[...] = from_ref[...] + matmul(in_ref[...], w_project_ref[piece, :])
+
+    convolve(0, even_ref)
+    project(0, even_ref, start_ref)
+    convolve(1, odd_ref)
 
     def body(index, carry):
-        convolve(2 * index, even_ref, project(2 * index - 1, odd_ref, total_ref))
-        convolve(2 * index + 1, odd_ref, project(2 * index, even_ref, total_ref))
+        convolve(2 * index, even_ref)
+        project(2 * index - 1, odd_ref, total_ref)
+        convolve(2 * index + 1, odd_ref)
+        project(2 * index, even_ref, total_ref)
         return carry
 
     lax.fori_loop(1, count // 2, body, 0)
-    last = project(count - 1, odd_ref, total_ref)
-    for turn in range(subs * rows):
-        last(turn)
+    project(count - 1, odd_ref, total_ref)
 
 
 def inner(expanded, start, depth_kernel, w_project, rows, cols, first, count, tile):
@@ -565,7 +548,7 @@
 
 def finish(own, plan, incoming, back, w_out, mixed):
     tokens, channels = mixed.shape
-    step = divisor(tokens, 128, 16)
+    step = divisor(tokens, 256, 16)
     return pl.pallas_call(
         functools.partial(finish_kernel, plan=plan),
         in_specs=[pl.BlockSpec(memory_space=pltpu.SMEM)] + [vmem()] * (len(incoming) + 3),

time: 58.9 us -> 58.4 us (level)
  transfers between devices with their start and end apart: 24 -> 24, of which waited for: 5 -> 6; matrix products, arithmetic and copies ran while one was open for 0% -> 0% of each run, Pallas kernels for 14% -> 13%
where the time goes in v20:
time: 58.4 us; the launch traced here: 58.2 us
  starting transfers between devices  33.1 us (57%)
  Pallas kernels  17.3 us (30%)
  waiting for transfers between devices  6.53 us (11%)
  local copies, waits for them, and re-layouts  0.93 us (2%)
    ppermute x20, starting transfers between devices, swap(): lax.ppermute(slab, ('row', 'col'), [(i, i ^ mask) for i in range(devices)])  28.5 us
    ppermute x20, waiting for transfers between devices, swap(): lax.ppermute(slab, ('row', 'col'), [(i, i ^ mask) for i in range(devices)])  6.52 us
    pallas_call x2, Pallas kernels, inner(): pl.pallas_call(functools.partial(inner_kernel, rows=rows, cols=cols, firs...  5.04 us
    ppermute x4, starting transfers between devices, swap_pairs(): return lax.ppermute(edge, axis, pairs + [(b, a) for a, b in pairs])  4.61 us
    pallas_call x1, Pallas kernels, attend(): pl.pallas_call(functools.partial(attend_kernel, plan=plan, sets=sets, cam...  4.53 us
    pallas_call x1, Pallas kernels, rim(): pl.pallas_call(functools.partial(rim_kernel, rows=rows, cols=cols, plan=p...  2.9 us
    pallas_call x1, Pallas kernels, expand(): pl.pallas_call(expand_kernel, in_specs=[vmem()] * 2, out_specs=vmem(), ou...  2.21 us
    pallas_call x1, Pallas kernels, finish(): pl.pallas_call(functools.partial(finish_kernel, plan=plan), in_specs=[pl....  1.72 us
  transfers between devices with their start and end apart: 24, of which 6 were waited for; matrix products, arithmetic and copies ran while one was open for 0% of the time, Pallas kernels for 13%

profile of v20, /device:TPU:0, one launch (start us, length us, event | category | flops | bytes accessed | tf_op | source)
XLA Modules:
  0.0 58.2 jit_solution(10042259496396648257)
XLA Ops:
  0.0 0.9 %slice_bitcast_fusion = (f32[32,512]{1,0:T(8,128)S(1)}, f32[32,512]{1,0:T(8,128)S(1)}) fusion(f32[16,32,512]{2,1,0:T(8,128)} %param.8), kind=kLoop, calls=%fused_computation | loop fusion | bytes 262144 | tf_op jit(solution)/shard_map/squeeze | solution.py:695
  1.1 3.1 %collective-permute-start = (bf16[32,512]{1,0:T(8,128)(2,1)S(1)}, bf16[32,512]{1,0:T(8,128)(2,1)S(1)}, u32[]{:S(2)}, u32[]{:S(2)}) collective-permute-start(bf16[32,512]{1,0:T(8,128)(2,1)S(1)} %get-tuple-element.62), channel_id=1, source_target_pairs={{0,4},{8,12},{4,0},{12,8},{1,5},{9,13},{5,1},{13,9},{2,6},{10,14},... | collective-permute-start | bytes 98312 | tf_op jit(solution)/shard_map/ppermute | solution.py:569
  5.2 2.2 %expand.1.expanded_ref = f32[8448,128]{1,0:T(8,128)S(1)} custom-call(bf16[512,512]{1,0:T(8,128)(2,1)S(1)} %half_norm.1.normed_ref, bf16[512,2048]{1,0:T(8,128)(2,1)S(1)} %copy-done), custom_call_target="tpu_custom_call" | custom-call | flops 10000000000 | bytes 6815744 | tf_op jit(solution)/shard_map/expand/pallas_call | solution.py:176
  7.5 1.2 %inner.2 = (f32[512,512]{1,0:T(8,128)S(1)}, f32[4,96,128]{2,1,0:T(8,128)S(1)}) custom-call(f32[8448,128]{1,0:T(8,128)S(1)} %expand.1.expanded_ref, f32[512,512]{1,0:T(8,128)S(1)} %bitcast.10, f32[3,3,2048]{2,1,0:T(4,128)S(1)} %copy-done.5, bf16[2048,512]{1,0:T(8,128)(2,1)S(1)} %copy-done.1), custom_call_target="tpu_custom_call" | custom-call | flops 4000000000 | bytes 3145728 | tf_op jit(solution)/shard_map/inner/pallas_call | solution.py:263
  10.0 3.8 %inner.3 = (f32[512,512]{1,0:T(8,128)S(1)}, f32[12,96,128]{2,1,0:T(8,128)S(1)}) custom-call(f32[8448,128]{1,0:T(8,128)S(1)} %expand.1.expanded_ref, f32[512,512]{1,0:T(8,128)S(1)} %get-tuple-element.67.start_ref, f32[3,3,2048]{2,1,0:T(4,128)S(1)} %copy-done.5, bf16[2048,512]{1,0:T(8,128)(2,1)S(1)} %copy-done.1), custom_call_target="tpu_custom_call" | custom-call | flops 12000000000 | bytes 5242880 | tf_op jit(solution)/shard_map/inner/pallas_call | solution.py:263
  13.8 2.9 %rim.1 = (f32[512,512]{1,0:T(8,128)S(1)}, bf16[2,32,512]{2,1,0:T(8,128)(2,1)S(1)}, bf16[2,32,512]{2,1,0:T(8,128)(2,1)S(1)}, bf16[1,32,512]{2,1,0:T(8,128)(2,1)S(...) custom-call(s32[1]{0:T(128)} %bitcast.own_ref, s32[1]{0:T(128)} %bitcast.2.odd_col_ref, ...), custom_call_target="tpu_custom_call" | custom-call | flops 805306368 | bytes 6815744 | tf_op jit(solution)/shard_map/rim/pallas_call | solution.py:379
  16.8 2.9 %collective-permute-start.6 = (bf16[6,32,512]{2,1,0:T(8,128)(2,1)S(1)}, bf16[6,32,512]{2,1,0:T(8,128)(2,1)S(1)}, u32[]{:S(2)}, u32[]{:S(2)}) collective-permute-start(bf16[6,32,512]{2,1,0:T(8,128)(2,1)S(1)} %get-tuple-element.81), channel_id=1, source_target_pairs={{0,1},{1,0},{2,3},{3,2},{4,5},{5,4},{6,7},{7,6},{8,9},{9,8},{10,11... | collective-permute-start | bytes 589832 | tf_op jit(solution)/shard_map/ppermute | solution.py:638
  19.7 2.7 %collective-permute-start.4 = (bf16[2,32,512]{2,1,0:T(8,128)(2,1)S(1)}, bf16[2,32,512]{2,1,0:T(8,128)(2,1)S(1)}, u32[]{:S(2)}, u32[]{:S(2)}) collective-permute-start(bf16[2,32,512]{2,1,0:T(8,128)(2,1)S(1)} %get-tuple-element.78), channel_id=1, source_target_pairs={{0,14},{1,15},{2,12},{3,13},{4,10},{5,11},{6,8},{7,9},{8,6},{9,7},... | collective-permute-start | bytes 196616 | tf_op jit(solution)/shard_map/ppermute | solution.py:638
  22.4 1.1 %collective-permute-start.5 = (bf16[2,32,512]{2,1,0:T(8,128)(2,1)S(1)}, bf16[2,32,512]{2,1,0:T(8,128)(2,1)S(1)}, u32[]{:S(2)}, u32[]{:S(2)}) collective-permute-start(bf16[2,32,512]{2,1,0:T(8,128)(2,1)S(1)} %get-tuple-element.79), channel_id=1, source_target_pairs={{0,12},{1,13},{2,14},{3,15},{4,8},{5,9},{6,10},{7,11},{8,4},{9,5},... | collective-permute-start | bytes 196616 | tf_op jit(solution)/shard_map/ppermute | solution.py:638
  23.5 3.0 %collective-permute-start.7 = (bf16[2,32,512]{2,1,0:T(8,128)(2,1)S(1)}, bf16[2,32,512]{2,1,0:T(8,128)(2,1)S(1)}, u32[]{:S(2)}, u32[]{:S(2)}) collective-permute-start(bf16[2,32,512]{2,1,0:T(8,128)(2,1)S(1)} %get-tuple-element.82), channel_id=1, source_target_pairs={{0,10},{1,11},{2,8},{3,9},{4,14},{5,15},{6,12},{7,13},{8,2},{9,3},... | collective-permute-start | bytes 196616 | tf_op jit(solution)/shard_map/ppermute | solution.py:638
  26.6 1.2 %collective-permute-start.8 = (bf16[2,32,512]{2,1,0:T(8,128)(2,1)S(1)}, bf16[2,32,512]{2,1,0:T(8,128)(2,1)S(1)}, u32[]{:S(2)}, u32[]{:S(2)}) collective-permute-start(bf16[2,32,512]{2,1,0:T(8,128)(2,1)S(1)} %get-tuple-element.83), channel_id=1, source_target_pairs={{0,6},{1,7},{2,4},{3,5},{4,2},{5,3},{6,0},{7,1},{8,14},{9,15},{10,... | collective-permute-start | bytes 196616 | tf_op jit(solution)/shard_map/ppermute | solution.py:638
  27.8 0.8 %collective-permute-start.9 = (bf16[2,32,512]{2,1,0:T(8,128)(2,1)S(1)}, bf16[2,32,512]{2,1,0:T(8,128)(2,1)S(1)}, u32[]{:S(2)}, u32[]{:S(2)}) collective-permute-start(bf16[2,32,512]{2,1,0:T(8,128)(2,1)S(1)} %get-tuple-element.84), channel_id=1, source_target_pairs={{0,4},{1,5},{2,6},{3,7},{4,0},{5,1},{6,2},{7,3},{8,12},{9,13},{10,... | collective-permute-start | bytes 196616 | tf_op jit(solution)/shard_map/ppermute | solution.py:638
  28.6 4.6 %collective-permute-start.10 = (bf16[2,32,512]{2,1,0:T(8,128)(2,1)S(1)}, bf16[2,32,512]{2,1,0:T(8,128)(2,1)S(1)}, u32[]{:S(2)}, u32[]{:S(2)}) collective-permute-start(bf16[2,32,512]{2,1,0:T(8,128)(2,1)S(1)} %get-tuple-element.90), channel_id=1, source_target_pairs={{0,8},{1,9},{2,10},{3,11},{4,12},{5,13},{6,14},{7,15},{8,0},{9,1},... | collective-permute-start | bytes 196616 | tf_op jit(solution)/shard_map/ppermute | solution.py:638
  33.6 1.7 %collective-permute-done.7.refs_2_ = bf16[2,32,512]{2,1,0:T(8,128)(2,1)S(1)} collective-permute-done((bf16[2,32,512]{2,1,0:T(8,128)(2,1)S(1)}, bf16[2,32,512]{2,1,0:T(8,128)(2,1)S(1)}, u32[]{:S(2)}, u32[]{:S(2)}) %collective-permute-start.7) | collective-permute-done | bytes 65568 | tf_op jit(solution)/shard_map/ppermute | solution.py:638
  35.8 1.7 %collective-permute-done.11.refs_6_ = bf16[2,32,512]{2,1,0:T(8,128)(2,1)S(1)} collective-permute-done((bf16[2,32,512]{2,1,0:T(8,128)(2,1)S(1)}, bf16[2,32,512]{2,1,0:T(8,128)(2,1)S(1)}, u32[]{:S(2)}, u32[]{:S(2)}) %collective-permute-start.11) | collective-permute-done | bytes 65568 | tf_op jit(solution)/shard_map/ppermute | solution.py:638
  37.5 4.5 %attend.1 = (bf16[2,32,512]{2,1,0:T(8,128)(2,1)S(1)}, bf16[2,32,512]{2,1,0:T(8,128)(2,1)S(1)}, bf16[1,32,512]{2,1,0:T(8,128)(2,1)S(1)}, bf16[6,32,512]{2,1,0:T(8,128)(2,1)S(1)}, bf16[5,32,512]{2,1,0:T(8,128)(2,1)S(1)}) custom-call(bf16[2,32,512]{2,1,0:T(8,128)(2,1)S(1)} %collective-permute-done.4.refs_0_, ...), custom_call_target="tpu_custom_call" | custom-call | flops 1073741824 | bytes 2621440 | tf_op jit(solution)/shard_map/attend/pallas_call | solution.py:499
  42.1 1.8 %collective-permute-start.14 = (bf16[2,32,512]{2,1,0:T(8,128)(2,1)S(1)}, bf16[2,32,512]{2,1,0:T(8,128)(2,1)S(1)}, u32[]{:S(2)}, u32[]{:S(2)}) collective-permute-start(bf16[2,32,512]{2,1,0:T(8,128)(2,1)S(1)} %get-tuple-element.93), channel_id=1, source_target_pairs={{0,14},{1,15},{2,12},{3,13},{4,10},{5,11},{6,8},{7,9},{8,6},{9,7},... | collective-permute-start | bytes 196616 | tf_op jit(solution)/shard_map/ppermute | solution.py:638
  43.9 1.9 %collective-permute-start.15 = (bf16[2,32,512]{2,1,0:T(8,128)(2,1)S(1)}, bf16[2,32,512]{2,1,0:T(8,128)(2,1)S(1)}, u32[]{:S(2)}, u32[]{:S(2)}) collective-permute-start(bf16[2,32,512]{2,1,0:T(8,128)(2,1)S(1)} %get-tuple-element.94), channel_id=1, source_target_pairs={{0,12},{1,13},{2,14},{3,15},{4,8},{5,9},{6,10},{7,11},{8,4},{9,5},... | collective-permute-start | bytes 196616 | tf_op jit(solution)/shard_map/ppermute | solution.py:638
  46.1 3.2 %collective-permute-start.18 = (bf16[2,32,512]{2,1,0:T(8,128)(2,1)S(1)}, bf16[2,32,512]{2,1,0:T(8,128)(2,1)S(1)}, u32[]{:S(2)}, u32[]{:S(2)}) collective-permute-start(bf16[2,32,512]{2,1,0:T(8,128)(2,1)S(1)} %get-tuple-element.98), channel_id=1, source_target_pairs={{0,6},{1,7},{2,4},{3,5},{4,2},{5,3},{6,0},{7,1},{8,14},{9,15},{10,... | collective-permute-start | bytes 196616 | tf_op jit(solution)/shard_map/ppermute | solution.py:638
  49.9 1.9 %collective-permute-start.20 = (bf16[2,32,512]{2,1,0:T(8,128)(2,1)S(1)}, bf16[2,32,512]{2,1,0:T(8,128)(2,1)S(1)}, u32[]{:S(2)}, u32[]{:S(2)}) collective-permute-start(bf16[2,32,512]{2,1,0:T(8,128)(2,1)S(1)} %get-tuple-element.105), channel_id=1, source_target_pairs={{0,8},{1,9},{2,10},{3,11},{4,12},{5,13},{6,14},{7,15},{8,0},{9,1},... | collective-permute-start | bytes 196616 | tf_op jit(solution)/shard_map/ppermute | solution.py:638
  51.7 1.7 %collective-permute-start.21 = (bf16[2,32,512]{2,1,0:T(8,128)(2,1)S(1)}, bf16[2,32,512]{2,1,0:T(8,128)(2,1)S(1)}, u32[]{:S(2)}, u32[]{:S(2)}) collective-permute-start(bf16[2,32,512]{2,1,0:T(8,128)(2,1)S(1)} %get-tuple-element.106), channel_id=1, source_target_pairs={{0,2},{1,3},{2,0},{3,1},{4,6},{5,7},{6,4},{7,5},{8,10},{9,11},{10,... | collective-permute-start | bytes 196616 | tf_op jit(solution)/shard_map/ppermute | solution.py:638
  53.4 1.0 %collective-permute-done.17.refs_2_ = bf16[2,32,512]{2,1,0:T(8,128)(2,1)S(1)} collective-permute-done((bf16[2,32,512]{2,1,0:T(8,128)(2,1)S(1)}, bf16[2,32,512]{2,1,0:T(8,128)(2,1)S(1)}, u32[]{:S(2)}, u32[]{:S(2)}) %collective-permute-start.17) | collective-permute-done | bytes 65568 | tf_op jit(solution)/shard_map/ppermute | solution.py:638
  55.3 1.1 %collective-permute-done.20.refs_5_ = bf16[2,32,512]{2,1,0:T(8,128)(2,1)S(1)} collective-permute-done((bf16[2,32,512]{2,1,0:T(8,128)(2,1)S(1)}, bf16[2,32,512]{2,1,0:T(8,128)(2,1)S(1)}, u32[]{:S(2)}, u32[]{:S(2)}) %collective-permute-start.20) | collective-permute-done | bytes 65568 | tf_op jit(solution)/shard_map/ppermute | solution.py:638
  56.5 1.7 %finish.1 = f32[512,512]{1,0:T(8,128)} custom-call(s32[1]{0:T(128)} %bitcast.own_ref, bf16[2,32,512]{2,1,0:T(8,128)(2,1)S(1)} %collective-permute-done.14.refs_0_, bf16[2,32,512]{2,1,0:T(8,128)(2,1)S(1)} %collective-permute-done.15.refs_1_, bf16[2,32,512]{2,1,0:T(8,128)(2,1)S(1)} %collective-permute-done.17.refs_2_, ...), custom_call_target="tpu_custom_call" | custom-call | tf_op jit(solution)/shard_map/finish/pallas_call | solution.py:552
  (52 shorter events, 5.2 us)
Async XLA Ops:
  1.1 7.6 %collective-permute-start = (bf16[32,512]{1,0:T(8,128)(2,1)S(1)}, bf16[32,512]{1,0:T(8,128)(2,1)S(1)}, u32[]{:S(2)}, u32[]{:S(2)}) collective-permute-start(bf16[32,512]{1,0:T(8,128)(2,1)S(1)} %get-tuple-element.62), channel_id=1, source_target_pairs={{0,4},{8,12},{4,0},{12,8},{1,5},{9,13},{5,1},{13,9},{2,6},{10,14},... | collective-permute-start | bytes 98312 | tf_op jit(solution)/shard_map/ppermute | solution.py:569
  4.2 4.5 %collective-permute-start.1 = (bf16[32,512]{1,0:T(8,128)(2,1)S(1)}, bf16[32,512]{1,0:T(8,128)(2,1)S(1)}, u32[]{:S(2)}, u32[]{:S(2)}) collective-permute-start(bf16[32,512]{1,0:T(8,128)(2,1)S(1)} %get-tuple-element.63), channel_id=1, source_target_pairs={{4,8},{8,4},{5,9},{9,5},{6,10},{10,6},{7,11},{11,7},{20,24},{24,20... | collective-permute-start | bytes 98312 | tf_op jit(solution)/shard_map/ppermute | solution.py:569
  9.1 4.7 %collective-permute-start.2 = (bf16[32,512]{1,0:T(8,128)(2,1)S(1)}, bf16[32,512]{1,0:T(8,128)(2,1)S(1)}, u32[]{:S(2)}, u32[]{:S(2)}) collective-permute-start(bf16[32,512]{1,0:T(8,128)(2,1)S(1)} %get-tuple-element.76), channel_id=1, source_target_pairs={{0,1},{2,3},{1,0},{3,2},{4,5},{6,7},{5,4},{7,6},{8,9},{10,11},{9,8... | collective-permute-start | bytes 98312 | tf_op jit(solution)/shard_map/ppermute | solution.py:569
  9.2 4.6 %collective-permute-start.3 = (bf16[32,512]{1,0:T(8,128)(2,1)S(1)}, bf16[32,512]{1,0:T(8,128)(2,1)S(1)}, u32[]{:S(2)}, u32[]{:S(2)}) collective-permute-start(bf16[32,512]{1,0:T(8,128)(2,1)S(1)} %get-tuple-element.77), channel_id=1, source_target_pairs={{1,2},{2,1},{5,6},{6,5},{9,10},{10,9},{13,14},{14,13},{17,18},{18,... | collective-permute-start | bytes 98312 | tf_op jit(solution)/shard_map/ppermute | solution.py:569
  16.8 6.8 %collective-permute-start.6 = (bf16[6,32,512]{2,1,0:T(8,128)(2,1)S(1)}, bf16[6,32,512]{2,1,0:T(8,128)(2,1)S(1)}, u32[]{:S(2)}, u32[]{:S(2)}) collective-permute-start(bf16[6,32,512]{2,1,0:T(8,128)(2,1)S(1)} %get-tuple-element.81), channel_id=1, source_target_pairs={{0,1},{1,0},{2,3},{3,2},{4,5},{5,4},{6,7},{7,6},{8,9},{9,8},{10,11... | collective-permute-start | bytes 589832 | tf_op jit(solution)/shard_map/ppermute | solution.py:638
  19.7 8.9 %collective-permute-start.4 = (bf16[2,32,512]{2,1,0:T(8,128)(2,1)S(1)}, bf16[2,32,512]{2,1,0:T(8,128)(2,1)S(1)}, u32[]{:S(2)}, u32[]{:S(2)}) collective-permute-start(bf16[2,32,512]{2,1,0:T(8,128)(2,1)S(1)} %get-tuple-element.78), channel_id=1, source_target_pairs={{0,14},{1,15},{2,12},{3,13},{4,10},{5,11},{6,8},{7,9},{8,6},{9,7},... | collective-permute-start | bytes 196616 | tf_op jit(solution)/shard_map/ppermute | solution.py:638
  22.4 10.8 %collective-permute-start.5 = (bf16[2,32,512]{2,1,0:T(8,128)(2,1)S(1)}, bf16[2,32,512]{2,1,0:T(8,128)(2,1)S(1)}, u32[]{:S(2)}, u32[]{:S(2)}) collective-permute-start(bf16[2,32,512]{2,1,0:T(8,128)(2,1)S(1)} %get-tuple-element.79), channel_id=1, source_target_pairs={{0,12},{1,13},{2,14},{3,15},{4,8},{5,9},{6,10},{7,11},{8,4},{9,5},... | collective-permute-start | bytes 196616 | tf_op jit(solution)/shard_map/ppermute | solution.py:638
  23.5 11.7 %collective-permute-start.7 = (bf16[2,32,512]{2,1,0:T(8,128)(2,1)S(1)}, bf16[2,32,512]{2,1,0:T(8,128)(2,1)S(1)}, u32[]{:S(2)}, u32[]{:S(2)}) collective-permute-start(bf16[2,32,512]{2,1,0:T(8,128)(2,1)S(1)} %get-tuple-element.82), channel_id=1, source_target_pairs={{0,10},{1,11},{2,8},{3,9},{4,14},{5,15},{6,12},{7,13},{8,2},{9,3},... | collective-permute-start | bytes 196616 | tf_op jit(solution)/shard_map/ppermute | solution.py:638
  26.6 8.7 %collective-permute-start.8 = (bf16[2,32,512]{2,1,0:T(8,128)(2,1)S(1)}, bf16[2,32,512]{2,1,0:T(8,128)(2,1)S(1)}, u32[]{:S(2)}, u32[]{:S(2)}) collective-permute-start(bf16[2,32,512]{2,1,0:T(8,128)(2,1)S(1)} %get-tuple-element.83), channel_id=1, source_target_pairs={{0,6},{1,7},{2,4},{3,5},{4,2},{5,3},{6,0},{7,1},{8,14},{9,15},{10,... | collective-permute-start | bytes 196616 | tf_op jit(solution)/shard_map/ppermute | solution.py:638
  27.8 7.5 %collective-permute-start.9 = (bf16[2,32,512]{2,1,0:T(8,128)(2,1)S(1)}, bf16[2,32,512]{2,1,0:T(8,128)(2,1)S(1)}, u32[]{:S(2)}, u32[]{:S(2)}) collective-permute-start(bf16[2,32,512]{2,1,0:T(8,128)(2,1)S(1)} %get-tuple-element.84), channel_id=1, source_target_pairs={{0,4},{1,5},{2,6},{3,7},{4,0},{5,1},{6,2},{7,3},{8,12},{9,13},{10,... | collective-permute-start | bytes 196616 | tf_op jit(solution)/shard_map/ppermute | solution.py:638
  28.6 7.2 %collective-permute-start.10 = (bf16[2,32,512]{2,1,0:T(8,128)(2,1)S(1)}, bf16[2,32,512]{2,1,0:T(8,128)(2,1)S(1)}, u32[]{:S(2)}, u32[]{:S(2)}) collective-permute-start(bf16[2,32,512]{2,1,0:T(8,128)(2,1)S(1)} %get-tuple-element.90), channel_id=1, source_target_pairs={{0,8},{1,9},{2,10},{3,11},{4,12},{5,13},{6,14},{7,15},{8,0},{9,1},... | collective-permute-start | bytes 196616 | tf_op jit(solution)/shard_map/ppermute | solution.py:638
  33.2 4.3 %collective-permute-start.11 = (bf16[2,32,512]{2,1,0:T(8,128)(2,1)S(1)}, bf16[2,32,512]{2,1,0:T(8,128)(2,1)S(1)}, u32[]{:S(2)}, u32[]{:S(2)}) collective-permute-start(bf16[2,32,512]{2,1,0:T(8,128)(2,1)S(1)} %get-tuple-element.91), channel_id=1, source_target_pairs={{0,2},{1,3},{2,0},{3,1},{4,6},{5,7},{6,4},{7,5},{8,10},{9,11},{10,... | collective-permute-start | bytes 196616 | tf_op jit(solution)/shard_map/ppermute | solution.py:638
  35.3 2.2 %collective-permute-start.12 = (bf16[2,32,512]{2,1,0:T(8,128)(2,1)S(1)}, bf16[2,32,512]{2,1,0:T(8,128)(2,1)S(1)}, u32[]{:S(2)}, u32[]{:S(2)}) collective-permute-start(bf16[2,32,512]{2,1,0:T(8,128)(2,1)S(1)} %collective-permute-done.4.refs_0_), channel_id=1, source_target_pairs={{0,1},{1,0},{2,3},{3,2},{4,5},{5,4},{6,7},{7,6},{8,9},{9,8},{10,11... | collective-permute-start | bytes 196616 | tf_op jit(solution)/shard_map/ppermute | solution.py:638
  35.3 2.2 %collective-permute-start.13 = (bf16[2,32,512]{2,1,0:T(8,128)(2,1)S(1)}, bf16[2,32,512]{2,1,0:T(8,128)(2,1)S(1)}, u32[]{:S(2)}, u32[]{:S(2)}) collective-permute-start(bf16[2,32,512]{2,1,0:T(8,128)(2,1)S(1)} %collective-permute-done.5.refs_1_), channel_id=1, source_target_pairs={{0,1},{1,0},{2,3},{3,2},{4,5},{5,4},{6,7},{7,6},{8,9},{9,8},{10,11... | collective-permute-start | bytes 196616 | tf_op jit(solution)/shard_map/ppermute | solution.py:638
  42.1 3.7 %collective-permute-start.16 = (bf16[6,32,512]{2,1,0:T(8,128)(2,1)S(1)}, bf16[6,32,512]{2,1,0:T(8,128)(2,1)S(1)}, u32[]{:S(2)}, u32[]{:S(2)}) collective-permute-start(bf16[6,32,512]{2,1,0:T(8,128)(2,1)S(1)} %get-tuple-element.96), channel_id=1, source_target_pairs={{0,1},{1,0},{2,3},{3,2},{4,5},{5,4},{6,7},{7,6},{8,9},{9,8},{10,11... | collective-permute-start | bytes 589832 | tf_op jit(solution)/shard_map/ppermute | solution.py:638
  42.1 7.7 %collective-permute-start.14 = (bf16[2,32,512]{2,1,0:T(8,128)(2,1)S(1)}, bf16[2,32,512]{2,1,0:T(8,128)(2,1)S(1)}, u32[]{:S(2)}, u32[]{:S(2)}) collective-permute-start(bf16[2,32,512]{2,1,0:T(8,128)(2,1)S(1)} %get-tuple-element.93), channel_id=1, source_target_pairs={{0,14},{1,15},{2,12},{3,13},{4,10},{5,11},{6,8},{7,9},{8,6},{9,7},... | collective-permute-start | bytes 196616 | tf_op jit(solution)/shard_map/ppermute | solution.py:638
  43.9 7.9 %collective-permute-start.15 = (bf16[2,32,512]{2,1,0:T(8,128)(2,1)S(1)}, bf16[2,32,512]{2,1,0:T(8,128)(2,1)S(1)}, u32[]{:S(2)}, u32[]{:S(2)}) collective-permute-start(bf16[2,32,512]{2,1,0:T(8,128)(2,1)S(1)} %get-tuple-element.94), channel_id=1, source_target_pairs={{0,12},{1,13},{2,14},{3,15},{4,8},{5,9},{6,10},{7,11},{8,4},{9,5},... | collective-permute-start | bytes 196616 | tf_op jit(solution)/shard_map/ppermute | solution.py:638
  45.8 8.6 %collective-permute-start.17 = (bf16[2,32,512]{2,1,0:T(8,128)(2,1)S(1)}, bf16[2,32,512]{2,1,0:T(8,128)(2,1)S(1)}, u32[]{:S(2)}, u32[]{:S(2)}) collective-permute-start(bf16[2,32,512]{2,1,0:T(8,128)(2,1)S(1)} %get-tuple-element.97), channel_id=1, source_target_pairs={{0,10},{1,11},{2,8},{3,9},{4,14},{5,15},{6,12},{7,13},{8,2},{9,3},... | collective-permute-start | bytes 196616 | tf_op jit(solution)/shard_map/ppermute | solution.py:638
  46.1 8.3 %collective-permute-start.18 = (bf16[2,32,512]{2,1,0:T(8,128)(2,1)S(1)}, bf16[2,32,512]{2,1,0:T(8,128)(2,1)S(1)}, u32[]{:S(2)}, u32[]{:S(2)}) collective-permute-start(bf16[2,32,512]{2,1,0:T(8,128)(2,1)S(1)} %get-tuple-element.98), channel_id=1, source_target_pairs={{0,6},{1,7},{2,4},{3,5},{4,2},{5,3},{6,0},{7,1},{8,14},{9,15},{10,... | collective-permute-start | bytes 196616 | tf_op jit(solution)/shard_map/ppermute | solution.py:638
  49.3 5.5 %collective-permute-start.19 = (bf16[2,32,512]{2,1,0:T(8,128)(2,1)S(1)}, bf16[2,32,512]{2,1,0:T(8,128)(2,1)S(1)}, u32[]{:S(2)}, u32[]{:S(2)}) collective-permute-start(bf16[2,32,512]{2,1,0:T(8,128)(2,1)S(1)} %get-tuple-element.99), channel_id=1, source_target_pairs={{0,4},{1,5},{2,6},{3,7},{4,0},{5,1},{6,2},{7,3},{8,12},{9,13},{10,... | collective-permute-start | bytes 196616 | tf_op jit(solution)/shard_map/ppermute | solution.py:638
  49.9 6.5 %collective-permute-start.20 = (bf16[2,32,512]{2,1,0:T(8,128)(2,1)S(1)}, bf16[2,32,512]{2,1,0:T(8,128)(2,1)S(1)}, u32[]{:S(2)}, u32[]{:S(2)}) collective-permute-start(bf16[2,32,512]{2,1,0:T(8,128)(2,1)S(1)} %get-tuple-element.105), channel_id=1, source_target_pairs={{0,8},{1,9},{2,10},{3,11},{4,12},{5,13},{6,14},{7,15},{8,0},{9,1},... | collective-permute-start | bytes 196616 | tf_op jit(solution)/shard_map/ppermute | solution.py:638
  51.7 4.7 %collective-permute-start.21 = (bf16[2,32,512]{2,1,0:T(8,128)(2,1)S(1)}, bf16[2,32,512]{2,1,0:T(8,128)(2,1)S(1)}, u32[]{:S(2)}, u32[]{:S(2)}) collective-permute-start(bf16[2,32,512]{2,1,0:T(8,128)(2,1)S(1)} %get-tuple-element.106), channel_id=1, source_target_pairs={{0,2},{1,3},{2,0},{3,1},{4,6},{5,7},{6,4},{7,5},{8,10},{9,11},{10,... | collective-permute-start | bytes 196616 | tf_op jit(solution)/shard_map/ppermute | solution.py:638
  54.8 1.6 %collective-permute-start.22 = (bf16[2,32,512]{2,1,0:T(8,128)(2,1)S(1)}, bf16[2,32,512]{2,1,0:T(8,128)(2,1)S(1)}, u32[]{:S(2)}, u32[]{:S(2)}) collective-permute-start(bf16[2,32,512]{2,1,0:T(8,128)(2,1)S(1)} %collective-permute-done.14.refs_0_), channel_id=1, source_target_pairs={{0,1},{1,0},{2,3},{3,2},{4,5},{5,4},{6,7},{7,6},{8,9},{9,8},{10,11... | collective-permute-start | bytes 196616 | tf_op jit(solution)/shard_map/ppermute | solution.py:638
  54.8 1.6 %collective-permute-start.23 = (bf16[2,32,512]{2,1,0:T(8,128)(2,1)S(1)}, bf16[2,32,512]{2,1,0:T(8,128)(2,1)S(1)}, u32[]{:S(2)}, u32[]{:S(2)}) collective-permute-start(bf16[2,32,512]{2,1,0:T(8,128)(2,1)S(1)} %collective-permute-done.15.refs_1_), channel_id=1, source_target_pairs={{0,1},{1,0},{2,3},{3,2},{4,5},{5,4},{6,7},{7,6},{8,9},{9,8},{10,11... | collective-permute-start | bytes 196616 | tf_op jit(solution)/shard_map/ppermute | solution.py:638
  (8 other events, 78.8 us)

commit v21 on v20

--- a/solution.py
+++ b/solution.py
@@ -152,22 +152,35 @@
     return tokens + 16
 
 
-def expand_kernel(normed_ref, weight_ref, out_ref):
-    tokens = normed_ref.shape[0]
+def expand_kernel(normed_ref, weight_ref, out_ref, even_ref, odd_ref):
+    tokens, tile = even_ref.shape
     width = weight_ref.shape[1]
-    tile = divisor(width, 512, LANES)
+    subs = tile // LANES
+
+    def multiply(index, made_ref):
+        lanes = pl.ds(pl.multiple_of(index * tile, tile), tile)
+        made_ref[...] = matmul(normed_ref[...], weight_ref[:, lanes])
+
+    def activate(index, made_ref):
+        for sub in range(subs):
+            row = (index * subs + sub) * padded_rows(tokens) + 8
+            out_ref[pl.ds(pl.multiple_of(row, 8), tokens), :] = gelu_of_half(
+                made_ref[:, sub * LANES : (sub + 1) * LANES]
+            )
 
     def body(index, carry):
-        lanes = pl.ds(pl.multiple_of(index * tile, tile), tile)
-        made = gelu_of_half(matmul(normed_ref[...], weight_ref[:, lanes]))
-        for sub in range(tile // LANES):
-            row = (index * (tile // LANES) + sub) * padded_rows(tokens) + 8
-            out_ref[pl.ds(pl.multiple_of(row, 8), tokens), :] = made[
-                :, sub * LANES : (sub + 1) * LANES
-            ]
+        multiply(2 * index + 1, odd_ref)
+        activate(2 * index, even_ref)
+        multiply(2 * index + 2, even_ref)
+        activate(2 * index + 1, odd_ref)
         return carry
 
-    lax.fori_loop(0, width // tile, body, 0)
+    count = width // tile
+    multiply(0, even_ref)
+    lax.fori_loop(0, count // 2 - 1, body, 0)
+    multiply(count - 1, odd_ref)
+    activate(count - 2, even_ref)
+    activate(count - 1, odd_ref)
 
 
 def expand(normed, w_expand):
@@ -178,7 +191,10 @@
         in_specs=[vmem()] * 2,
         out_specs=vmem(),
         out_shape=jax.ShapeDtypeStruct((width // LANES * padded_rows(tokens), LANES), jnp.float32),
-        compiler_params=pltpu.CompilerParams(vmem_limit_bytes=4 * MIB),
+        scratch_shapes=[
+            pltpu.VMEM((tokens, divisor(width // 2, 256, LANES)), jnp.float32)
+        ] * 2,
+        compiler_params=pltpu.CompilerParams(vmem_limit_bytes=6 * MIB),
         cost_estimate=pl.CostEstimate(
             flops=10**10,
             bytes_accessed=tokens * channels * 2 + channels * width * 2 + tokens * width * 4,
@@ -300,21 +316,17 @@
     right = choose(odd_col, two_ref[...], one_ref[...])
     edges = jnp.concatenate([up_ref[...], down_ref[...], left, right], axis=0)
 
-    def expand_halo(index, carry):
-        lanes = pl.ds(pl.multiple_of(index * tile, tile), tile)
-        made = gelu_of_half(matmul(edges, w_expand_ref[:, lanes]))
+    def expand_halo(index):
+        made = gelu_of_half(matmul(edges, w_expand_ref[:, index * tile : (index + 1) * tile]))
         for sub in range(subs):
             halo_ref[index * subs + sub] = made[:, sub * LANES : (sub + 1) * LANES]
-        return carry
-
-    lax.fori_loop(0, width // tile, expand_halo, 0)
-    mixed_ref[...] = inner_ref[...]
+
     position = lax.broadcasted_iota(jnp.int32, (cols, LANES), 0)
     at_first = position == 0
     at_last = position == cols - 1
 
     def activate(chunk, here, sums_ref):
-        lanes = pl.ds(pl.multiple_of(chunk * LANES, LANES), LANES)
+        lanes = slice(chunk * LANES, (chunk + 1) * LANES)
         taps = [[0.5 * depth_ref[p, q : q + 1, lanes] for q in range(3)] for p in range(3)]
         beside = []
         for q, start in ((0, left_start), (2, right_start)):
@@ -334,18 +346,15 @@
             made.append(sums_ref[here, start : start + rows] + beside[index])
         active_ref[:, lanes] = gelu_of_half(jnp.concatenate(made, axis=0)).astype(jnp.bfloat16)
 
-    chunk = 0
-    for sums_ref in rim_refs:
-        offset = chunk
-
-        def body(index, carry, sums_ref=sums_ref, offset=offset):
-            activate(offset + 2 * index, 2 * index, sums_ref)
-            activate(offset + 2 * index + 1, 2 * index + 1, sums_ref)
-            return carry
-
-        lax.fori_loop(0, sums_ref.shape[0] // 2, body, 0)
-        chunk += sums_ref.shape[0]
-
+    spots = [(ref, here) for ref in rim_refs for here in range(ref.shape[0])]
+    expand_halo(0)
+    for index in range(width // tile):
+        if (index + 1) * tile < width:
+            expand_halo(index + 1)
+        for chunk in range(index * subs, (index + 1) * subs):
+            activate(chunk, spots[chunk][1], spots[chunk][0])
+
+    mixed_ref[...] = inner_ref[...]
     branch = matmul(active_ref[...], w_project_ref[...])
     mixed_ref[:cols, :] += branch[:cols]
     mixed_ref[tokens - cols :, :] += branch[cols : 2 * cols]

time: 58.4 us -> 57.6 us (0.986)
  Pallas kernels: 17.3 us -> 16.6 us
    pallas_call x1, Pallas kernels: 2.9 us -> 2.07 us  [rim(): pl.pallas_call(functools.partial(rim_kernel, rows=rows, cols=cols, plan=p...]
  transfers between devices with their start and end apart: 24 -> 24, of which waited for: 6 -> 5; matrix products, arithmetic and copies ran while one was open for 0% -> 0% of each run, Pallas kernels for 13% -> 13%
where the time goes in v21:
time: 57.6 us; the launch traced here: 57.4 us
  starting transfers between devices  33.2 us (58%)
  Pallas kernels  16.6 us (29%)
  waiting for transfers between devices  6.46 us (11%)
  local copies, waits for them, and re-layouts  0.93 us (2%)
    ppermute x20, starting transfers between devices, swap(): lax.ppermute(slab, ('row', 'col'), [(i, i ^ mask) for i in range(devices)])  28.6 us
    ppermute x20, waiting for transfers between devices, swap(): lax.ppermute(slab, ('row', 'col'), [(i, i ^ mask) for i in range(devices)])  6.45 us
    pallas_call x2, Pallas kernels, inner(): pl.pallas_call(functools.partial(inner_kernel, rows=rows, cols=cols, firs...  5.04 us
    ppermute x4, starting transfers between devices, swap_pairs(): return lax.ppermute(edge, axis, pairs + [(b, a) for a, b in pairs])  4.61 us
    pallas_call x1, Pallas kernels, attend(): pl.pallas_call(functools.partial(attend_kernel, plan=plan, sets=sets, cam...  4.53 us
    pallas_call x1, Pallas kernels, expand(): pl.pallas_call(expand_kernel, in_specs=[vmem()] * 2, out_specs=vmem(), ou...  2.31 us
    pallas_call x1, Pallas kernels, rim(): pl.pallas_call(functools.partial(rim_kernel, rows=rows, cols=cols, plan=p...  2.07 us
    pallas_call x1, Pallas kernels, finish(): pl.pallas_call(functools.partial(finish_kernel, plan=plan), in_specs=[pl....  1.72 us
  transfers between devices with their start and end apart: 24, of which 5 were waited for; matrix products, arithmetic and copies ran while one was open for 0% of the time, Pallas kernels for 13%

profile of v21, /device:TPU:0, one launch (start us, length us, event | category | flops | bytes accessed | tf_op | source)
XLA Modules:
  0.0 57.4 jit_solution(12981801732244354843)
XLA Ops:
  0.0 0.9 %slice_bitcast_fusion = (f32[32,512]{1,0:T(8,128)S(1)}, f32[32,512]{1,0:T(8,128)S(1)}) fusion(f32[16,32,512]{2,1,0:T(8,128)} %param.8), kind=kLoop, calls=%fused_computation | loop fusion | bytes 262144 | tf_op jit(solution)/shard_map/squeeze | solution.py:704
  1.1 3.1 %collective-permute-start = (bf16[32,512]{1,0:T(8,128)(2,1)S(1)}, bf16[32,512]{1,0:T(8,128)(2,1)S(1)}, u32[]{:S(2)}, u32[]{:S(2)}) collective-permute-start(bf16[32,512]{1,0:T(8,128)(2,1)S(1)} %get-tuple-element.62), channel_id=1, source_target_pairs={{0,4},{8,12},{4,0},{12,8},{1,5},{9,13},{5,1},{13,9},{2,6},{10,14},... | collective-permute-start | bytes 98312 | tf_op jit(solution)/shard_map/ppermute | solution.py:578
  5.2 2.3 %expand.1.expanded_ref = f32[8448,128]{1,0:T(8,128)S(1)} custom-call(bf16[512,512]{1,0:T(8,128)(2,1)S(1)} %half_norm.1.normed_ref, bf16[512,2048]{1,0:T(8,128)(2,1)S(1)} %copy-done), custom_call_target="tpu_custom_call" | custom-call | flops 10000000000 | bytes 6815744 | tf_op jit(solution)/shard_map/expand/pallas_call | solution.py:189
  7.6 1.2 %inner.2 = (f32[512,512]{1,0:T(8,128)S(1)}, f32[4,96,128]{2,1,0:T(8,128)S(1)}) custom-call(f32[8448,128]{1,0:T(8,128)S(1)} %expand.1.expanded_ref, f32[512,512]{1,0:T(8,128)S(1)} %bitcast.10, f32[3,3,2048]{2,1,0:T(4,128)S(1)} %copy-done.5, bf16[2048,512]{1,0:T(8,128)(2,1)S(1)} %copy-done.1), custom_call_target="tpu_custom_call" | custom-call | flops 4000000000 | bytes 3145728 | tf_op jit(solution)/shard_map/inner/pallas_call | solution.py:279
  10.1 3.8 %inner.3 = (f32[512,512]{1,0:T(8,128)S(1)}, f32[12,96,128]{2,1,0:T(8,128)S(1)}) custom-call(f32[8448,128]{1,0:T(8,128)S(1)} %expand.1.expanded_ref, f32[512,512]{1,0:T(8,128)S(1)} %get-tuple-element.67.start_ref, f32[3,3,2048]{2,1,0:T(4,128)S(1)} %copy-done.5, bf16[2048,512]{1,0:T(8,128)(2,1)S(1)} %copy-done.1), custom_call_target="tpu_custom_call" | custom-call | flops 12000000000 | bytes 5242880 | tf_op jit(solution)/shard_map/inner/pallas_call | solution.py:279
  13.9 2.1 %rim.1 = (f32[512,512]{1,0:T(8,128)S(1)}, bf16[2,32,512]{2,1,0:T(8,128)(2,1)S(1)}, bf16[2,32,512]{2,1,0:T(8,128)(2,1)S(1)}, bf16[1,32,512]{2,1,0:T(8,128)(2,1)S(...) custom-call(s32[1]{0:T(128)} %bitcast.own_ref, s32[1]{0:T(128)} %bitcast.2.odd_col_ref, ...), custom_call_target="tpu_custom_call" | custom-call | flops 805306368 | bytes 6815744 | tf_op jit(solution)/shard_map/rim/pallas_call | solution.py:388
  16.0 2.9 %collective-permute-start.6 = (bf16[6,32,512]{2,1,0:T(8,128)(2,1)S(1)}, bf16[6,32,512]{2,1,0:T(8,128)(2,1)S(1)}, u32[]{:S(2)}, u32[]{:S(2)}) collective-permute-start(bf16[6,32,512]{2,1,0:T(8,128)(2,1)S(1)} %get-tuple-element.81), channel_id=1, source_target_pairs={{0,1},{1,0},{2,3},{3,2},{4,5},{5,4},{6,7},{7,6},{8,9},{9,8},{10,11... | collective-permute-start | bytes 589832 | tf_op jit(solution)/shard_map/ppermute | solution.py:647
  19.0 2.7 %collective-permute-start.4 = (bf16[2,32,512]{2,1,0:T(8,128)(2,1)S(1)}, bf16[2,32,512]{2,1,0:T(8,128)(2,1)S(1)}, u32[]{:S(2)}, u32[]{:S(2)}) collective-permute-start(bf16[2,32,512]{2,1,0:T(8,128)(2,1)S(1)} %get-tuple-element.78), channel_id=1, source_target_pairs={{0,14},{1,15},{2,12},{3,13},{4,10},{5,11},{6,8},{7,9},{8,6},{9,7},... | collective-permute-start | bytes 196616 | tf_op jit(solution)/shard_map/ppermute | solution.py:647
  21.6 1.1 %collective-permute-start.5 = (bf16[2,32,512]{2,1,0:T(8,128)(2,1)S(1)}, bf16[2,32,512]{2,1,0:T(8,128)(2,1)S(1)}, u32[]{:S(2)}, u32[]{:S(2)}) collective-permute-start(bf16[2,32,512]{2,1,0:T(8,128)(2,1)S(1)} %get-tuple-element.79), channel_id=1, source_target_pairs={{0,12},{1,13},{2,14},{3,15},{4,8},{5,9},{6,10},{7,11},{8,4},{9,5},... | collective-permute-start | bytes 196616 | tf_op jit(solution)/shard_map/ppermute | solution.py:647
  22.8 3.0 %collective-permute-start.7 = (bf16[2,32,512]{2,1,0:T(8,128)(2,1)S(1)}, bf16[2,32,512]{2,1,0:T(8,128)(2,1)S(1)}, u32[]{:S(2)}, u32[]{:S(2)}) collective-permute-start(bf16[2,32,512]{2,1,0:T(8,128)(2,1)S(1)} %get-tuple-element.82), channel_id=1, source_target_pairs={{0,10},{1,11},{2,8},{3,9},{4,14},{5,15},{6,12},{7,13},{8,2},{9,3},... | collective-permute-start | bytes 196616 | tf_op jit(solution)/shard_map/ppermute | solution.py:647
  25.8 1.2 %collective-permute-start.8 = (bf16[2,32,512]{2,1,0:T(8,128)(2,1)S(1)}, bf16[2,32,512]{2,1,0:T(8,128)(2,1)S(1)}, u32[]{:S(2)}, u32[]{:S(2)}) collective-permute-start(bf16[2,32,512]{2,1,0:T(8,128)(2,1)S(1)} %get-tuple-element.83), channel_id=1, source_target_pairs={{0,6},{1,7},{2,4},{3,5},{4,2},{5,3},{6,0},{7,1},{8,14},{9,15},{10,... | collective-permute-start | bytes 196616 | tf_op jit(solution)/shard_map/ppermute | solution.py:647
  27.0 0.8 %collective-permute-start.9 = (bf16[2,32,512]{2,1,0:T(8,128)(2,1)S(1)}, bf16[2,32,512]{2,1,0:T(8,128)(2,1)S(1)}, u32[]{:S(2)}, u32[]{:S(2)}) collective-permute-start(bf16[2,32,512]{2,1,0:T(8,128)(2,1)S(1)} %get-tuple-element.84), channel_id=1, source_target_pairs={{0,4},{1,5},{2,6},{3,7},{4,0},{5,1},{6,2},{7,3},{8,12},{9,13},{10,... | collective-permute-start | bytes 196616 | tf_op jit(solution)/shard_map/ppermute | solution.py:647
  27.8 4.6 %collective-permute-start.10 = (bf16[2,32,512]{2,1,0:T(8,128)(2,1)S(1)}, bf16[2,32,512]{2,1,0:T(8,128)(2,1)S(1)}, u32[]{:S(2)}, u32[]{:S(2)}) collective-permute-start(bf16[2,32,512]{2,1,0:T(8,128)(2,1)S(1)} %get-tuple-element.90), channel_id=1, source_target_pairs={{0,8},{1,9},{2,10},{3,11},{4,12},{5,13},{6,14},{7,15},{8,0},{9,1},... | collective-permute-start | bytes 196616 | tf_op jit(solution)/shard_map/ppermute | solution.py:647
  32.9 1.7 %collective-permute-done.7.refs_2_ = bf16[2,32,512]{2,1,0:T(8,128)(2,1)S(1)} collective-permute-done((bf16[2,32,512]{2,1,0:T(8,128)(2,1)S(1)}, bf16[2,32,512]{2,1,0:T(8,128)(2,1)S(1)}, u32[]{:S(2)}, u32[]{:S(2)}) %collective-permute-start.7) | collective-permute-done | bytes 65568 | tf_op jit(solution)/shard_map/ppermute | solution.py:647
  35.1 1.6 %collective-permute-done.11.refs_6_ = bf16[2,32,512]{2,1,0:T(8,128)(2,1)S(1)} collective-permute-done((bf16[2,32,512]{2,1,0:T(8,128)(2,1)S(1)}, bf16[2,32,512]{2,1,0:T(8,128)(2,1)S(1)}, u32[]{:S(2)}, u32[]{:S(2)}) %collective-permute-start.11) | collective-permute-done | bytes 65568 | tf_op jit(solution)/shard_map/ppermute | solution.py:647
  36.7 4.5 %attend.1 = (bf16[2,32,512]{2,1,0:T(8,128)(2,1)S(1)}, bf16[2,32,512]{2,1,0:T(8,128)(2,1)S(1)}, bf16[1,32,512]{2,1,0:T(8,128)(2,1)S(1)}, bf16[6,32,512]{2,1,0:T(8,128)(2,1)S(1)}, bf16[5,32,512]{2,1,0:T(8,128)(2,1)S(1)}) custom-call(bf16[2,32,512]{2,1,0:T(8,128)(2,1)S(1)} %collective-permute-done.4.refs_0_, ...), custom_call_target="tpu_custom_call" | custom-call | flops 1073741824 | bytes 2621440 | tf_op jit(solution)/shard_map/attend/pallas_call | solution.py:508
  41.4 1.7 %collective-permute-start.14 = (bf16[2,32,512]{2,1,0:T(8,128)(2,1)S(1)}, bf16[2,32,512]{2,1,0:T(8,128)(2,1)S(1)}, u32[]{:S(2)}, u32[]{:S(2)}) collective-permute-start(bf16[2,32,512]{2,1,0:T(8,128)(2,1)S(1)} %get-tuple-element.93), channel_id=1, source_target_pairs={{0,14},{1,15},{2,12},{3,13},{4,10},{5,11},{6,8},{7,9},{8,6},{9,7},... | collective-permute-start | bytes 196616 | tf_op jit(solution)/shard_map/ppermute | solution.py:647
  43.1 2.0 %collective-permute-start.15 = (bf16[2,32,512]{2,1,0:T(8,128)(2,1)S(1)}, bf16[2,32,512]{2,1,0:T(8,128)(2,1)S(1)}, u32[]{:S(2)}, u32[]{:S(2)}) collective-permute-start(bf16[2,32,512]{2,1,0:T(8,128)(2,1)S(1)} %get-tuple-element.94), channel_id=1, source_target_pairs={{0,12},{1,13},{2,14},{3,15},{4,8},{5,9},{6,10},{7,11},{8,4},{9,5},... | collective-permute-start | bytes 196616 | tf_op jit(solution)/shard_map/ppermute | solution.py:647
  45.3 3.1 %collective-permute-start.18 = (bf16[2,32,512]{2,1,0:T(8,128)(2,1)S(1)}, bf16[2,32,512]{2,1,0:T(8,128)(2,1)S(1)}, u32[]{:S(2)}, u32[]{:S(2)}) collective-permute-start(bf16[2,32,512]{2,1,0:T(8,128)(2,1)S(1)} %get-tuple-element.98), channel_id=1, source_target_pairs={{0,6},{1,7},{2,4},{3,5},{4,2},{5,3},{6,0},{7,1},{8,14},{9,15},{10,... | collective-permute-start | bytes 196616 | tf_op jit(solution)/shard_map/ppermute | solution.py:647
  49.1 2.0 %collective-permute-start.20 = (bf16[2,32,512]{2,1,0:T(8,128)(2,1)S(1)}, bf16[2,32,512]{2,1,0:T(8,128)(2,1)S(1)}, u32[]{:S(2)}, u32[]{:S(2)}) collective-permute-start(bf16[2,32,512]{2,1,0:T(8,128)(2,1)S(1)} %get-tuple-element.105), channel_id=1, source_target_pairs={{0,8},{1,9},{2,10},{3,11},{4,12},{5,13},{6,14},{7,15},{8,0},{9,1},... | collective-permute-start | bytes 196616 | tf_op jit(solution)/shard_map/ppermute | solution.py:647
  51.1 1.6 %collective-permute-start.21 = (bf16[2,32,512]{2,1,0:T(8,128)(2,1)S(1)}, bf16[2,32,512]{2,1,0:T(8,128)(2,1)S(1)}, u32[]{:S(2)}, u32[]{:S(2)}) collective-permute-start(bf16[2,32,512]{2,1,0:T(8,128)(2,1)S(1)} %get-tuple-element.106), channel_id=1, source_target_pairs={{0,2},{1,3},{2,0},{3,1},{4,6},{5,7},{6,4},{7,5},{8,10},{9,11},{10,... | collective-permute-start | bytes 196616 | tf_op jit(solution)/shard_map/ppermute | solution.py:647
  52.7 1.2 %collective-permute-done.17.refs_2_ = bf16[2,32,512]{2,1,0:T(8,128)(2,1)S(1)} collective-permute-done((bf16[2,32,512]{2,1,0:T(8,128)(2,1)S(1)}, bf16[2,32,512]{2,1,0:T(8,128)(2,1)S(1)}, u32[]{:S(2)}, u32[]{:S(2)}) %collective-permute-start.17) | collective-permute-done | bytes 65568 | tf_op jit(solution)/shard_map/ppermute | solution.py:647
  54.4 1.3 %collective-permute-done.20.refs_5_ = bf16[2,32,512]{2,1,0:T(8,128)(2,1)S(1)} collective-permute-done((bf16[2,32,512]{2,1,0:T(8,128)(2,1)S(1)}, bf16[2,32,512]{2,1,0:T(8,128)(2,1)S(1)}, u32[]{:S(2)}, u32[]{:S(2)}) %collective-permute-start.20) | collective-permute-done | bytes 65568 | tf_op jit(solution)/shard_map/ppermute | solution.py:647
  55.7 1.7 %finish.1 = f32[512,512]{1,0:T(8,128)} custom-call(s32[1]{0:T(128)} %bitcast.own_ref, bf16[2,32,512]{2,1,0:T(8,128)(2,1)S(1)} %collective-permute-done.14.refs_0_, bf16[2,32,512]{2,1,0:T(8,128)(2,1)S(1)} %collective-permute-done.15.refs_1_, bf16[2,32,512]{2,1,0:T(8,128)(2,1)S(1)} %collective-permute-done.17.refs_2_, ...), custom_call_target="tpu_custom_call" | custom-call | tf_op jit(solution)/shard_map/finish/pallas_call | solution.py:561
  (52 shorter events, 4.9 us)
Async XLA Ops:
  1.1 7.7 %collective-permute-start = (bf16[32,512]{1,0:T(8,128)(2,1)S(1)}, bf16[32,512]{1,0:T(8,128)(2,1)S(1)}, u32[]{:S(2)}, u32[]{:S(2)}) collective-permute-start(bf16[32,512]{1,0:T(8,128)(2,1)S(1)} %get-tuple-element.62), channel_id=1, source_target_pairs={{0,4},{8,12},{4,0},{12,8},{1,5},{9,13},{5,1},{13,9},{2,6},{10,14},... | collective-permute-start | bytes 98312 | tf_op jit(solution)/shard_map/ppermute | solution.py:578
  4.2 4.6 %collective-permute-start.1 = (bf16[32,512]{1,0:T(8,128)(2,1)S(1)}, bf16[32,512]{1,0:T(8,128)(2,1)S(1)}, u32[]{:S(2)}, u32[]{:S(2)}) collective-permute-start(bf16[32,512]{1,0:T(8,128)(2,1)S(1)} %get-tuple-element.63), channel_id=1, source_target_pairs={{4,8},{8,4},{5,9},{9,5},{6,10},{10,6},{7,11},{11,7},{20,24},{24,20... | collective-permute-start | bytes 98312 | tf_op jit(solution)/shard_map/ppermute | solution.py:578
  9.2 4.7 %collective-permute-start.2 = (bf16[32,512]{1,0:T(8,128)(2,1)S(1)}, bf16[32,512]{1,0:T(8,128)(2,1)S(1)}, u32[]{:S(2)}, u32[]{:S(2)}) collective-permute-start(bf16[32,512]{1,0:T(8,128)(2,1)S(1)} %get-tuple-element.76), channel_id=1, source_target_pairs={{0,1},{2,3},{1,0},{3,2},{4,5},{6,7},{5,4},{7,6},{8,9},{10,11},{9,8... | collective-permute-start | bytes 98312 | tf_op jit(solution)/shard_map/ppermute | solution.py:578
  9.3 4.6 %collective-permute-start.3 = (bf16[32,512]{1,0:T(8,128)(2,1)S(1)}, bf16[32,512]{1,0:T(8,128)(2,1)S(1)}, u32[]{:S(2)}, u32[]{:S(2)}) collective-permute-start(bf16[32,512]{1,0:T(8,128)(2,1)S(1)} %get-tuple-element.77), channel_id=1, source_target_pairs={{1,2},{2,1},{5,6},{6,5},{9,10},{10,9},{13,14},{14,13},{17,18},{18,... | collective-permute-start | bytes 98312 | tf_op jit(solution)/shard_map/ppermute | solution.py:578
  16.0 6.8 %collective-permute-start.6 = (bf16[6,32,512]{2,1,0:T(8,128)(2,1)S(1)}, bf16[6,32,512]{2,1,0:T(8,128)(2,1)S(1)}, u32[]{:S(2)}, u32[]{:S(2)}) collective-permute-start(bf16[6,32,512]{2,1,0:T(8,128)(2,1)S(1)} %get-tuple-element.81), channel_id=1, source_target_pairs={{0,1},{1,0},{2,3},{3,2},{4,5},{5,4},{6,7},{7,6},{8,9},{9,8},{10,11... | collective-permute-start | bytes 589832 | tf_op jit(solution)/shard_map/ppermute | solution.py:647
  19.0 8.9 %collective-permute-start.4 = (bf16[2,32,512]{2,1,0:T(8,128)(2,1)S(1)}, bf16[2,32,512]{2,1,0:T(8,128)(2,1)S(1)}, u32[]{:S(2)}, u32[]{:S(2)}) collective-permute-start(bf16[2,32,512]{2,1,0:T(8,128)(2,1)S(1)} %get-tuple-element.78), channel_id=1, source_target_pairs={{0,14},{1,15},{2,12},{3,13},{4,10},{5,11},{6,8},{7,9},{8,6},{9,7},... | collective-permute-start | bytes 196616 | tf_op jit(solution)/shard_map/ppermute | solution.py:647
  21.6 10.8 %collective-permute-start.5 = (bf16[2,32,512]{2,1,0:T(8,128)(2,1)S(1)}, bf16[2,32,512]{2,1,0:T(8,128)(2,1)S(1)}, u32[]{:S(2)}, u32[]{:S(2)}) collective-permute-start(bf16[2,32,512]{2,1,0:T(8,128)(2,1)S(1)} %get-tuple-element.79), channel_id=1, source_target_pairs={{0,12},{1,13},{2,14},{3,15},{4,8},{5,9},{6,10},{7,11},{8,4},{9,5},... | collective-permute-start | bytes 196616 | tf_op jit(solution)/shard_map/ppermute | solution.py:647
  22.8 11.7 %collective-permute-start.7 = (bf16[2,32,512]{2,1,0:T(8,128)(2,1)S(1)}, bf16[2,32,512]{2,1,0:T(8,128)(2,1)S(1)}, u32[]{:S(2)}, u32[]{:S(2)}) collective-permute-start(bf16[2,32,512]{2,1,0:T(8,128)(2,1)S(1)} %get-tuple-element.82), channel_id=1, source_target_pairs={{0,10},{1,11},{2,8},{3,9},{4,14},{5,15},{6,12},{7,13},{8,2},{9,3},... | collective-permute-start | bytes 196616 | tf_op jit(solution)/shard_map/ppermute | solution.py:647
  25.8 8.7 %collective-permute-start.8 = (bf16[2,32,512]{2,1,0:T(8,128)(2,1)S(1)}, bf16[2,32,512]{2,1,0:T(8,128)(2,1)S(1)}, u32[]{:S(2)}, u32[]{:S(2)}) collective-permute-start(bf16[2,32,512]{2,1,0:T(8,128)(2,1)S(1)} %get-tuple-element.83), channel_id=1, source_target_pairs={{0,6},{1,7},{2,4},{3,5},{4,2},{5,3},{6,0},{7,1},{8,14},{9,15},{10,... | collective-permute-start | bytes 196616 | tf_op jit(solution)/shard_map/ppermute | solution.py:647
  27.0 7.5 %collective-permute-start.9 = (bf16[2,32,512]{2,1,0:T(8,128)(2,1)S(1)}, bf16[2,32,512]{2,1,0:T(8,128)(2,1)S(1)}, u32[]{:S(2)}, u32[]{:S(2)}) collective-permute-start(bf16[2,32,512]{2,1,0:T(8,128)(2,1)S(1)} %get-tuple-element.84), channel_id=1, source_target_pairs={{0,4},{1,5},{2,6},{3,7},{4,0},{5,1},{6,2},{7,3},{8,12},{9,13},{10,... | collective-permute-start | bytes 196616 | tf_op jit(solution)/shard_map/ppermute | solution.py:647
  27.8 7.2 %collective-permute-start.10 = (bf16[2,32,512]{2,1,0:T(8,128)(2,1)S(1)}, bf16[2,32,512]{2,1,0:T(8,128)(2,1)S(1)}, u32[]{:S(2)}, u32[]{:S(2)}) collective-permute-start(bf16[2,32,512]{2,1,0:T(8,128)(2,1)S(1)} %get-tuple-element.90), channel_id=1, source_target_pairs={{0,8},{1,9},{2,10},{3,11},{4,12},{5,13},{6,14},{7,15},{8,0},{9,1},... | collective-permute-start | bytes 196616 | tf_op jit(solution)/shard_map/ppermute | solution.py:647
  32.4 4.3 %collective-permute-start.11 = (bf16[2,32,512]{2,1,0:T(8,128)(2,1)S(1)}, bf16[2,32,512]{2,1,0:T(8,128)(2,1)S(1)}, u32[]{:S(2)}, u32[]{:S(2)}) collective-permute-start(bf16[2,32,512]{2,1,0:T(8,128)(2,1)S(1)} %get-tuple-element.91), channel_id=1, source_target_pairs={{0,2},{1,3},{2,0},{3,1},{4,6},{5,7},{6,4},{7,5},{8,10},{9,11},{10,... | collective-permute-start | bytes 196616 | tf_op jit(solution)/shard_map/ppermute | solution.py:647
  34.5 2.2 %collective-permute-start.12 = (bf16[2,32,512]{2,1,0:T(8,128)(2,1)S(1)}, bf16[2,32,512]{2,1,0:T(8,128)(2,1)S(1)}, u32[]{:S(2)}, u32[]{:S(2)}) collective-permute-start(bf16[2,32,512]{2,1,0:T(8,128)(2,1)S(1)} %collective-permute-done.4.refs_0_), channel_id=1, source_target_pairs={{0,1},{1,0},{2,3},{3,2},{4,5},{5,4},{6,7},{7,6},{8,9},{9,8},{10,11... | collective-permute-start | bytes 196616 | tf_op jit(solution)/shard_map/ppermute | solution.py:647
  34.6 2.2 %collective-permute-start.13 = (bf16[2,32,512]{2,1,0:T(8,128)(2,1)S(1)}, bf16[2,32,512]{2,1,0:T(8,128)(2,1)S(1)}, u32[]{:S(2)}, u32[]{:S(2)}) collective-permute-start(bf16[2,32,512]{2,1,0:T(8,128)(2,1)S(1)} %collective-permute-done.5.refs_1_), channel_id=1, source_target_pairs={{0,1},{1,0},{2,3},{3,2},{4,5},{5,4},{6,7},{7,6},{8,9},{9,8},{10,11... | collective-permute-start | bytes 196616 | tf_op jit(solution)/shard_map/ppermute | solution.py:647
  41.3 3.8 %collective-permute-start.16 = (bf16[6,32,512]{2,1,0:T(8,128)(2,1)S(1)}, bf16[6,32,512]{2,1,0:T(8,128)(2,1)S(1)}, u32[]{:S(2)}, u32[]{:S(2)}) collective-permute-start(bf16[6,32,512]{2,1,0:T(8,128)(2,1)S(1)} %get-tuple-element.96), channel_id=1, source_target_pairs={{0,1},{1,0},{2,3},{3,2},{4,5},{5,4},{6,7},{7,6},{8,9},{9,8},{10,11... | collective-permute-start | bytes 589832 | tf_op jit(solution)/shard_map/ppermute | solution.py:647
  41.4 7.7 %collective-permute-start.14 = (bf16[2,32,512]{2,1,0:T(8,128)(2,1)S(1)}, bf16[2,32,512]{2,1,0:T(8,128)(2,1)S(1)}, u32[]{:S(2)}, u32[]{:S(2)}) collective-permute-start(bf16[2,32,512]{2,1,0:T(8,128)(2,1)S(1)} %get-tuple-element.93), channel_id=1, source_target_pairs={{0,14},{1,15},{2,12},{3,13},{4,10},{5,11},{6,8},{7,9},{8,6},{9,7},... | collective-permute-start | bytes 196616 | tf_op jit(solution)/shard_map/ppermute | solution.py:647
  43.1 8.0 %collective-permute-start.15 = (bf16[2,32,512]{2,1,0:T(8,128)(2,1)S(1)}, bf16[2,32,512]{2,1,0:T(8,128)(2,1)S(1)}, u32[]{:S(2)}, u32[]{:S(2)}) collective-permute-start(bf16[2,32,512]{2,1,0:T(8,128)(2,1)S(1)} %get-tuple-element.94), channel_id=1, source_target_pairs={{0,12},{1,13},{2,14},{3,15},{4,8},{5,9},{6,10},{7,11},{8,4},{9,5},... | collective-permute-start | bytes 196616 | tf_op jit(solution)/shard_map/ppermute | solution.py:647
  45.2 8.7 %collective-permute-start.17 = (bf16[2,32,512]{2,1,0:T(8,128)(2,1)S(1)}, bf16[2,32,512]{2,1,0:T(8,128)(2,1)S(1)}, u32[]{:S(2)}, u32[]{:S(2)}) collective-permute-start(bf16[2,32,512]{2,1,0:T(8,128)(2,1)S(1)} %get-tuple-element.97), channel_id=1, source_target_pairs={{0,10},{1,11},{2,8},{3,9},{4,14},{5,15},{6,12},{7,13},{8,2},{9,3},... | collective-permute-start | bytes 196616 | tf_op jit(solution)/shard_map/ppermute | solution.py:647
  45.3 8.5 %collective-permute-start.18 = (bf16[2,32,512]{2,1,0:T(8,128)(2,1)S(1)}, bf16[2,32,512]{2,1,0:T(8,128)(2,1)S(1)}, u32[]{:S(2)}, u32[]{:S(2)}) collective-permute-start(bf16[2,32,512]{2,1,0:T(8,128)(2,1)S(1)} %get-tuple-element.98), channel_id=1, source_target_pairs={{0,6},{1,7},{2,4},{3,5},{4,2},{5,3},{6,0},{7,1},{8,14},{9,15},{10,... | collective-permute-start | bytes 196616 | tf_op jit(solution)/shard_map/ppermute | solution.py:647
  48.5 5.4 %collective-permute-start.19 = (bf16[2,32,512]{2,1,0:T(8,128)(2,1)S(1)}, bf16[2,32,512]{2,1,0:T(8,128)(2,1)S(1)}, u32[]{:S(2)}, u32[]{:S(2)}) collective-permute-start(bf16[2,32,512]{2,1,0:T(8,128)(2,1)S(1)} %get-tuple-element.99), channel_id=1, source_target_pairs={{0,4},{1,5},{2,6},{3,7},{4,0},{5,1},{6,2},{7,3},{8,12},{9,13},{10,... | collective-permute-start | bytes 196616 | tf_op jit(solution)/shard_map/ppermute | solution.py:647
  49.1 6.6 %collective-permute-start.20 = (bf16[2,32,512]{2,1,0:T(8,128)(2,1)S(1)}, bf16[2,32,512]{2,1,0:T(8,128)(2,1)S(1)}, u32[]{:S(2)}, u32[]{:S(2)}) collective-permute-start(bf16[2,32,512]{2,1,0:T(8,128)(2,1)S(1)} %get-tuple-element.105), channel_id=1, source_target_pairs={{0,8},{1,9},{2,10},{3,11},{4,12},{5,13},{6,14},{7,15},{8,0},{9,1},... | collective-permute-start | bytes 196616 | tf_op jit(solution)/shard_map/ppermute | solution.py:647
  51.1 4.6 %collective-permute-start.21 = (bf16[2,32,512]{2,1,0:T(8,128)(2,1)S(1)}, bf16[2,32,512]{2,1,0:T(8,128)(2,1)S(1)}, u32[]{:S(2)}, u32[]{:S(2)}) collective-permute-start(bf16[2,32,512]{2,1,0:T(8,128)(2,1)S(1)} %get-tuple-element.106), channel_id=1, source_target_pairs={{0,2},{1,3},{2,0},{3,1},{4,6},{5,7},{6,4},{7,5},{8,10},{9,11},{10,... | collective-permute-start | bytes 196616 | tf_op jit(solution)/shard_map/ppermute | solution.py:647
  53.8 1.8 %collective-permute-start.22 = (bf16[2,32,512]{2,1,0:T(8,128)(2,1)S(1)}, bf16[2,32,512]{2,1,0:T(8,128)(2,1)S(1)}, u32[]{:S(2)}, u32[]{:S(2)}) collective-permute-start(bf16[2,32,512]{2,1,0:T(8,128)(2,1)S(1)} %collective-permute-done.14.refs_0_), channel_id=1, source_target_pairs={{0,1},{1,0},{2,3},{3,2},{4,5},{5,4},{6,7},{7,6},{8,9},{9,8},{10,11... | collective-permute-start | bytes 196616 | tf_op jit(solution)/shard_map/ppermute | solution.py:647
  53.9 1.8 %collective-permute-start.23 = (bf16[2,32,512]{2,1,0:T(8,128)(2,1)S(1)}, bf16[2,32,512]{2,1,0:T(8,128)(2,1)S(1)}, u32[]{:S(2)}, u32[]{:S(2)}) collective-permute-start(bf16[2,32,512]{2,1,0:T(8,128)(2,1)S(1)} %collective-permute-done.15.refs_1_), channel_id=1, source_target_pairs={{0,1},{1,0},{2,3},{3,2},{4,5},{5,4},{6,7},{7,6},{8,9},{9,8},{10,11... | collective-permute-start | bytes 196616 | tf_op jit(solution)/shard_map/ppermute | solution.py:647
  (8 other events, 78.2 us)

commit v22 on v21

--- a/solution.py
+++ b/solution.py
@@ -26,7 +26,7 @@
 def gelu_of_half(half):
     scale = math.sqrt(2.0 / math.pi)
     inner = half * (2.0 * scale + (8.0 * scale * 0.044715) * (half * half))
-    return half + half * jnp.tanh(inner)
+    return half + half * jnp.tanh(inner.astype(jnp.bfloat16)).astype(jnp.float32)
 
 
 def matmul(a, b):
@@ -466,7 +466,7 @@
         for j in range(group_heads):
             part = scores_ref[j * count : (j + 1) * count]
             highest = jnp.max(part, axis=0, keepdims=True)
-            raised = jnp.exp2((part - highest) * factor).astype(jnp.bfloat16)
+            raised = jnp.exp2(((part - highest) * factor).astype(jnp.bfloat16))
             product = matmul(value_ref[index, j], raised)
             scale = 1.0 / product[head_width : head_width + 1]
             turned_ref[index, j * head_width : (j + 1) * head_width] = (

time: 57.6 us -> 58.1 us (level)
  transfers between devices with their start and end apart: 24 -> 24, of which waited for: 5 -> 5; matrix products, arithmetic and copies ran while one was open for 0% -> 0% of each run, Pallas kernels for 13% -> 14%
where the time goes in v22:
time: 58.1 us; the launch traced here: 57.9 us
  starting transfers between devices  33.1 us (57%)
  Pallas kernels  17 us (29%)
  waiting for transfers between devices  6.57 us (11%)
  local copies, waits for them, and re-layouts  0.93 us (2%)
    ppermute x20, starting transfers between devices, swap(): lax.ppermute(slab, ('row', 'col'), [(i, i ^ mask) for i in range(devices)])  28.5 us
    ppermute x20, waiting for transfers between devices, swap(): lax.ppermute(slab, ('row', 'col'), [(i, i ^ mask) for i in range(devices)])  6.56 us
    pallas_call x2, Pallas kernels, inner(): pl.pallas_call(functools.partial(inner_kernel, rows=rows, cols=cols, firs...  5.13 us
    pallas_call x1, Pallas kernels, attend(): pl.pallas_call(functools.partial(attend_kernel, plan=plan, sets=sets, cam...  4.63 us
    ppermute x4, starting transfers between devices, swap_pairs(): return lax.ppermute(edge, axis, pairs + [(b, a) for a, b in pairs])  4.61 us
    pallas_call x1, Pallas kernels, expand(): pl.pallas_call(expand_kernel, in_specs=[vmem()] * 2, out_specs=vmem(), ou...  2.51 us
    pallas_call x1, Pallas kernels, rim(): pl.pallas_call(functools.partial(rim_kernel, rows=rows, cols=cols, plan=p...  2.12 us
    pallas_call x1, Pallas kernels, finish(): pl.pallas_call(functools.partial(finish_kernel, plan=plan), in_specs=[pl....  1.72 us
  transfers between devices with their start and end apart: 24, of which 5 were waited for; matrix products, arithmetic and copies ran while one was open for 0% of the time, Pallas kernels for 14%

profile of v22, /device:TPU:0, one launch (start us, length us, event | category | flops | bytes accessed | tf_op | source)
XLA Modules:
  0.0 57.9 jit_solution(17416291696226058465)
XLA Ops:
  0.0 0.9 %slice_bitcast_fusion = (f32[32,512]{1,0:T(8,128)S(1)}, f32[32,512]{1,0:T(8,128)S(1)}) fusion(f32[16,32,512]{2,1,0:T(8,128)} %param.8), kind=kLoop, calls=%fused_computation | loop fusion | bytes 262144 | tf_op jit(solution)/shard_map/squeeze | solution.py:704
  1.1 3.1 %collective-permute-start = (bf16[32,512]{1,0:T(8,128)(2,1)S(1)}, bf16[32,512]{1,0:T(8,128)(2,1)S(1)}, u32[]{:S(2)}, u32[]{:S(2)}) collective-permute-start(bf16[32,512]{1,0:T(8,128)(2,1)S(1)} %get-tuple-element.62), channel_id=1, source_target_pairs={{0,4},{8,12},{4,0},{12,8},{1,5},{9,13},{5,1},{13,9},{2,6},{10,14},... | collective-permute-start | bytes 98312 | tf_op jit(solution)/shard_map/ppermute | solution.py:578
  5.2 2.5 %expand.1.expanded_ref = f32[8448,128]{1,0:T(8,128)S(1)} custom-call(bf16[512,512]{1,0:T(8,128)(2,1)S(1)} %half_norm.1.normed_ref, bf16[512,2048]{1,0:T(8,128)(2,1)S(1)} %copy-done), custom_call_target="tpu_custom_call" | custom-call | flops 10000000000 | bytes 6815744 | tf_op jit(solution)/shard_map/expand/pallas_call | solution.py:189
  7.8 1.2 %inner.2 = (f32[512,512]{1,0:T(8,128)S(1)}, f32[4,96,128]{2,1,0:T(8,128)S(1)}) custom-call(f32[8448,128]{1,0:T(8,128)S(1)} %expand.1.expanded_ref, f32[512,512]{1,0:T(8,128)S(1)} %bitcast.10, f32[3,3,2048]{2,1,0:T(4,128)S(1)} %copy-done.5, bf16[2048,512]{1,0:T(8,128)(2,1)S(1)} %copy-done.1), custom_call_target="tpu_custom_call" | custom-call | flops 4000000000 | bytes 3145728 | tf_op jit(solution)/shard_map/inner/pallas_call | solution.py:279
  10.3 3.9 %inner.3 = (f32[512,512]{1,0:T(8,128)S(1)}, f32[12,96,128]{2,1,0:T(8,128)S(1)}) custom-call(f32[8448,128]{1,0:T(8,128)S(1)} %expand.1.expanded_ref, f32[512,512]{1,0:T(8,128)S(1)} %get-tuple-element.67.start_ref, f32[3,3,2048]{2,1,0:T(4,128)S(1)} %copy-done.5, bf16[2048,512]{1,0:T(8,128)(2,1)S(1)} %copy-done.1), custom_call_target="tpu_custom_call" | custom-call | flops 12000000000 | bytes 5242880 | tf_op jit(solution)/shard_map/inner/pallas_call | solution.py:279
  14.2 2.1 %rim.1 = (f32[512,512]{1,0:T(8,128)S(1)}, bf16[2,32,512]{2,1,0:T(8,128)(2,1)S(1)}, bf16[2,32,512]{2,1,0:T(8,128)(2,1)S(1)}, bf16[1,32,512]{2,1,0:T(8,128)(2,1)S(...) custom-call(s32[1]{0:T(128)} %bitcast.own_ref, s32[1]{0:T(128)} %bitcast.2.odd_col_ref, ...), custom_call_target="tpu_custom_call" | custom-call | flops 805306368 | bytes 6815744 | tf_op jit(solution)/shard_map/rim/pallas_call | solution.py:388
  16.4 2.9 %collective-permute-start.6 = (bf16[6,32,512]{2,1,0:T(8,128)(2,1)S(1)}, bf16[6,32,512]{2,1,0:T(8,128)(2,1)S(1)}, u32[]{:S(2)}, u32[]{:S(2)}) collective-permute-start(bf16[6,32,512]{2,1,0:T(8,128)(2,1)S(1)} %get-tuple-element.81), channel_id=1, source_target_pairs={{0,1},{1,0},{2,3},{3,2},{4,5},{5,4},{6,7},{7,6},{8,9},{9,8},{10,11... | collective-permute-start | bytes 589832 | tf_op jit(solution)/shard_map/ppermute | solution.py:647
  19.3 2.7 %collective-permute-start.4 = (bf16[2,32,512]{2,1,0:T(8,128)(2,1)S(1)}, bf16[2,32,512]{2,1,0:T(8,128)(2,1)S(1)}, u32[]{:S(2)}, u32[]{:S(2)}) collective-permute-start(bf16[2,32,512]{2,1,0:T(8,128)(2,1)S(1)} %get-tuple-element.78), channel_id=1, source_target_pairs={{0,14},{1,15},{2,12},{3,13},{4,10},{5,11},{6,8},{7,9},{8,6},{9,7},... | collective-permute-start | bytes 196616 | tf_op jit(solution)/shard_map/ppermute | solution.py:647
  22.0 1.1 %collective-permute-start.5 = (bf16[2,32,512]{2,1,0:T(8,128)(2,1)S(1)}, bf16[2,32,512]{2,1,0:T(8,128)(2,1)S(1)}, u32[]{:S(2)}, u32[]{:S(2)}) collective-permute-start(bf16[2,32,512]{2,1,0:T(8,128)(2,1)S(1)} %get-tuple-element.79), channel_id=1, source_target_pairs={{0,12},{1,13},{2,14},{3,15},{4,8},{5,9},{6,10},{7,11},{8,4},{9,5},... | collective-permute-start | bytes 196616 | tf_op jit(solution)/shard_map/ppermute | solution.py:647
  23.1 3.0 %collective-permute-start.7 = (bf16[2,32,512]{2,1,0:T(8,128)(2,1)S(1)}, bf16[2,32,512]{2,1,0:T(8,128)(2,1)S(1)}, u32[]{:S(2)}, u32[]{:S(2)}) collective-permute-start(bf16[2,32,512]{2,1,0:T(8,128)(2,1)S(1)} %get-tuple-element.82), channel_id=1, source_target_pairs={{0,10},{1,11},{2,8},{3,9},{4,14},{5,15},{6,12},{7,13},{8,2},{9,3},... | collective-permute-start | bytes 196616 | tf_op jit(solution)/shard_map/ppermute | solution.py:647
  26.2 1.2 %collective-permute-start.8 = (bf16[2,32,512]{2,1,0:T(8,128)(2,1)S(1)}, bf16[2,32,512]{2,1,0:T(8,128)(2,1)S(1)}, u32[]{:S(2)}, u32[]{:S(2)}) collective-permute-start(bf16[2,32,512]{2,1,0:T(8,128)(2,1)S(1)} %get-tuple-element.83), channel_id=1, source_target_pairs={{0,6},{1,7},{2,4},{3,5},{4,2},{5,3},{6,0},{7,1},{8,14},{9,15},{10,... | collective-permute-start | bytes 196616 | tf_op jit(solution)/shard_map/ppermute | solution.py:647
  27.4 0.8 %collective-permute-start.9 = (bf16[2,32,512]{2,1,0:T(8,128)(2,1)S(1)}, bf16[2,32,512]{2,1,0:T(8,128)(2,1)S(1)}, u32[]{:S(2)}, u32[]{:S(2)}) collective-permute-start(bf16[2,32,512]{2,1,0:T(8,128)(2,1)S(1)} %get-tuple-element.84), channel_id=1, source_target_pairs={{0,4},{1,5},{2,6},{3,7},{4,0},{5,1},{6,2},{7,3},{8,12},{9,13},{10,... | collective-permute-start | bytes 196616 | tf_op jit(solution)/shard_map/ppermute | solution.py:647
  28.2 4.6 %collective-permute-start.10 = (bf16[2,32,512]{2,1,0:T(8,128)(2,1)S(1)}, bf16[2,32,512]{2,1,0:T(8,128)(2,1)S(1)}, u32[]{:S(2)}, u32[]{:S(2)}) collective-permute-start(bf16[2,32,512]{2,1,0:T(8,128)(2,1)S(1)} %get-tuple-element.90), channel_id=1, source_target_pairs={{0,8},{1,9},{2,10},{3,11},{4,12},{5,13},{6,14},{7,15},{8,0},{9,1},... | collective-permute-start | bytes 196616 | tf_op jit(solution)/shard_map/ppermute | solution.py:647
  33.2 1.7 %collective-permute-done.7.refs_2_ = bf16[2,32,512]{2,1,0:T(8,128)(2,1)S(1)} collective-permute-done((bf16[2,32,512]{2,1,0:T(8,128)(2,1)S(1)}, bf16[2,32,512]{2,1,0:T(8,128)(2,1)S(1)}, u32[]{:S(2)}, u32[]{:S(2)}) %collective-permute-start.7) | collective-permute-done | bytes 65568 | tf_op jit(solution)/shard_map/ppermute | solution.py:647
  35.4 1.7 %collective-permute-done.11.refs_6_ = bf16[2,32,512]{2,1,0:T(8,128)(2,1)S(1)} collective-permute-done((bf16[2,32,512]{2,1,0:T(8,128)(2,1)S(1)}, bf16[2,32,512]{2,1,0:T(8,128)(2,1)S(1)}, u32[]{:S(2)}, u32[]{:S(2)}) %collective-permute-start.11) | collective-permute-done | bytes 65568 | tf_op jit(solution)/shard_map/ppermute | solution.py:647
  37.1 4.6 %attend.1 = (bf16[2,32,512]{2,1,0:T(8,128)(2,1)S(1)}, bf16[2,32,512]{2,1,0:T(8,128)(2,1)S(1)}, bf16[1,32,512]{2,1,0:T(8,128)(2,1)S(1)}, bf16[6,32,512]{2,1,0:T(8,128)(2,1)S(1)}, bf16[5,32,512]{2,1,0:T(8,128)(2,1)S(1)}) custom-call(bf16[2,32,512]{2,1,0:T(8,128)(2,1)S(1)} %collective-permute-done.4.refs_0_, ...), custom_call_target="tpu_custom_call" | custom-call | flops 1073741824 | bytes 2621440 | tf_op jit(solution)/shard_map/attend/pallas_call | solution.py:508
  41.8 1.7 %collective-permute-start.14 = (bf16[2,32,512]{2,1,0:T(8,128)(2,1)S(1)}, bf16[2,32,512]{2,1,0:T(8,128)(2,1)S(1)}, u32[]{:S(2)}, u32[]{:S(2)}) collective-permute-start(bf16[2,32,512]{2,1,0:T(8,128)(2,1)S(1)} %get-tuple-element.93), channel_id=1, source_target_pairs={{0,14},{1,15},{2,12},{3,13},{4,10},{5,11},{6,8},{7,9},{8,6},{9,7},... | collective-permute-start | bytes 196616 | tf_op jit(solution)/shard_map/ppermute | solution.py:647
  43.5 2.1 %collective-permute-start.15 = (bf16[2,32,512]{2,1,0:T(8,128)(2,1)S(1)}, bf16[2,32,512]{2,1,0:T(8,128)(2,1)S(1)}, u32[]{:S(2)}, u32[]{:S(2)}) collective-permute-start(bf16[2,32,512]{2,1,0:T(8,128)(2,1)S(1)} %get-tuple-element.94), channel_id=1, source_target_pairs={{0,12},{1,13},{2,14},{3,15},{4,8},{5,9},{6,10},{7,11},{8,4},{9,5},... | collective-permute-start | bytes 196616 | tf_op jit(solution)/shard_map/ppermute | solution.py:647
  45.8 3.1 %collective-permute-start.18 = (bf16[2,32,512]{2,1,0:T(8,128)(2,1)S(1)}, bf16[2,32,512]{2,1,0:T(8,128)(2,1)S(1)}, u32[]{:S(2)}, u32[]{:S(2)}) collective-permute-start(bf16[2,32,512]{2,1,0:T(8,128)(2,1)S(1)} %get-tuple-element.98), channel_id=1, source_target_pairs={{0,6},{1,7},{2,4},{3,5},{4,2},{5,3},{6,0},{7,1},{8,14},{9,15},{10,... | collective-permute-start | bytes 196616 | tf_op jit(solution)/shard_map/ppermute | solution.py:647
  49.6 1.9 %collective-permute-start.20 = (bf16[2,32,512]{2,1,0:T(8,128)(2,1)S(1)}, bf16[2,32,512]{2,1,0:T(8,128)(2,1)S(1)}, u32[]{:S(2)}, u32[]{:S(2)}) collective-permute-start(bf16[2,32,512]{2,1,0:T(8,128)(2,1)S(1)} %get-tuple-element.105), channel_id=1, source_target_pairs={{0,8},{1,9},{2,10},{3,11},{4,12},{5,13},{6,14},{7,15},{8,0},{9,1},... | collective-permute-start | bytes 196616 | tf_op jit(solution)/shard_map/ppermute | solution.py:647
  51.5 1.6 %collective-permute-start.21 = (bf16[2,32,512]{2,1,0:T(8,128)(2,1)S(1)}, bf16[2,32,512]{2,1,0:T(8,128)(2,1)S(1)}, u32[]{:S(2)}, u32[]{:S(2)}) collective-permute-start(bf16[2,32,512]{2,1,0:T(8,128)(2,1)S(1)} %get-tuple-element.106), channel_id=1, source_target_pairs={{0,2},{1,3},{2,0},{3,1},{4,6},{5,7},{6,4},{7,5},{8,10},{9,11},{10,... | collective-permute-start | bytes 196616 | tf_op jit(solution)/shard_map/ppermute | solution.py:647
  53.1 1.1 %collective-permute-done.17.refs_2_ = bf16[2,32,512]{2,1,0:T(8,128)(2,1)S(1)} collective-permute-done((bf16[2,32,512]{2,1,0:T(8,128)(2,1)S(1)}, bf16[2,32,512]{2,1,0:T(8,128)(2,1)S(1)}, u32[]{:S(2)}, u32[]{:S(2)}) %collective-permute-start.17) | collective-permute-done | bytes 65568 | tf_op jit(solution)/shard_map/ppermute | solution.py:647
  54.7 1.4 %collective-permute-done.20.refs_5_ = bf16[2,32,512]{2,1,0:T(8,128)(2,1)S(1)} collective-permute-done((bf16[2,32,512]{2,1,0:T(8,128)(2,1)S(1)}, bf16[2,32,512]{2,1,0:T(8,128)(2,1)S(1)}, u32[]{:S(2)}, u32[]{:S(2)}) %collective-permute-start.20) | collective-permute-done | bytes 65568 | tf_op jit(solution)/shard_map/ppermute | solution.py:647
  56.2 1.7 %finish.1 = f32[512,512]{1,0:T(8,128)} custom-call(s32[1]{0:T(128)} %bitcast.own_ref, bf16[2,32,512]{2,1,0:T(8,128)(2,1)S(1)} %collective-permute-done.14.refs_0_, bf16[2,32,512]{2,1,0:T(8,128)(2,1)S(1)} %collective-permute-done.15.refs_1_, bf16[2,32,512]{2,1,0:T(8,128)(2,1)S(1)} %collective-permute-done.17.refs_2_, ...), custom_call_target="tpu_custom_call" | custom-call | tf_op jit(solution)/shard_map/finish/pallas_call | solution.py:561
  (52 shorter events, 4.9 us)
Async XLA Ops:
  1.1 7.9 %collective-permute-start = (bf16[32,512]{1,0:T(8,128)(2,1)S(1)}, bf16[32,512]{1,0:T(8,128)(2,1)S(1)}, u32[]{:S(2)}, u32[]{:S(2)}) collective-permute-start(bf16[32,512]{1,0:T(8,128)(2,1)S(1)} %get-tuple-element.62), channel_id=1, source_target_pairs={{0,4},{8,12},{4,0},{12,8},{1,5},{9,13},{5,1},{13,9},{2,6},{10,14},... | collective-permute-start | bytes 98312 | tf_op jit(solution)/shard_map/ppermute | solution.py:578
  4.2 4.8 %collective-permute-start.1 = (bf16[32,512]{1,0:T(8,128)(2,1)S(1)}, bf16[32,512]{1,0:T(8,128)(2,1)S(1)}, u32[]{:S(2)}, u32[]{:S(2)}) collective-permute-start(bf16[32,512]{1,0:T(8,128)(2,1)S(1)} %get-tuple-element.63), channel_id=1, source_target_pairs={{4,8},{8,4},{5,9},{9,5},{6,10},{10,6},{7,11},{11,7},{20,24},{24,20... | collective-permute-start | bytes 98312 | tf_op jit(solution)/shard_map/ppermute | solution.py:578
  9.4 4.8 %collective-permute-start.2 = (bf16[32,512]{1,0:T(8,128)(2,1)S(1)}, bf16[32,512]{1,0:T(8,128)(2,1)S(1)}, u32[]{:S(2)}, u32[]{:S(2)}) collective-permute-start(bf16[32,512]{1,0:T(8,128)(2,1)S(1)} %get-tuple-element.76), channel_id=1, source_target_pairs={{0,1},{2,3},{1,0},{3,2},{4,5},{6,7},{5,4},{7,6},{8,9},{10,11},{9,8... | collective-permute-start | bytes 98312 | tf_op jit(solution)/shard_map/ppermute | solution.py:578
  9.5 4.7 %collective-permute-start.3 = (bf16[32,512]{1,0:T(8,128)(2,1)S(1)}, bf16[32,512]{1,0:T(8,128)(2,1)S(1)}, u32[]{:S(2)}, u32[]{:S(2)}) collective-permute-start(bf16[32,512]{1,0:T(8,128)(2,1)S(1)} %get-tuple-element.77), channel_id=1, source_target_pairs={{1,2},{2,1},{5,6},{6,5},{9,10},{10,9},{13,14},{14,13},{17,18},{18,... | collective-permute-start | bytes 98312 | tf_op jit(solution)/shard_map/ppermute | solution.py:578
  16.4 6.8 %collective-permute-start.6 = (bf16[6,32,512]{2,1,0:T(8,128)(2,1)S(1)}, bf16[6,32,512]{2,1,0:T(8,128)(2,1)S(1)}, u32[]{:S(2)}, u32[]{:S(2)}) collective-permute-start(bf16[6,32,512]{2,1,0:T(8,128)(2,1)S(1)} %get-tuple-element.81), channel_id=1, source_target_pairs={{0,1},{1,0},{2,3},{3,2},{4,5},{5,4},{6,7},{7,6},{8,9},{9,8},{10,11... | collective-permute-start | bytes 589832 | tf_op jit(solution)/shard_map/ppermute | solution.py:647
  19.3 8.9 %collective-permute-start.4 = (bf16[2,32,512]{2,1,0:T(8,128)(2,1)S(1)}, bf16[2,32,512]{2,1,0:T(8,128)(2,1)S(1)}, u32[]{:S(2)}, u32[]{:S(2)}) collective-permute-start(bf16[2,32,512]{2,1,0:T(8,128)(2,1)S(1)} %get-tuple-element.78), channel_id=1, source_target_pairs={{0,14},{1,15},{2,12},{3,13},{4,10},{5,11},{6,8},{7,9},{8,6},{9,7},... | collective-permute-start | bytes 196616 | tf_op jit(solution)/shard_map/ppermute | solution.py:647
  22.0 10.8 %collective-permute-start.5 = (bf16[2,32,512]{2,1,0:T(8,128)(2,1)S(1)}, bf16[2,32,512]{2,1,0:T(8,128)(2,1)S(1)}, u32[]{:S(2)}, u32[]{:S(2)}) collective-permute-start(bf16[2,32,512]{2,1,0:T(8,128)(2,1)S(1)} %get-tuple-element.79), channel_id=1, source_target_pairs={{0,12},{1,13},{2,14},{3,15},{4,8},{5,9},{6,10},{7,11},{8,4},{9,5},... | collective-permute-start | bytes 196616 | tf_op jit(solution)/shard_map/ppermute | solution.py:647
  23.1 11.7 %collective-permute-start.7 = (bf16[2,32,512]{2,1,0:T(8,128)(2,1)S(1)}, bf16[2,32,512]{2,1,0:T(8,128)(2,1)S(1)}, u32[]{:S(2)}, u32[]{:S(2)}) collective-permute-start(bf16[2,32,512]{2,1,0:T(8,128)(2,1)S(1)} %get-tuple-element.82), channel_id=1, source_target_pairs={{0,10},{1,11},{2,8},{3,9},{4,14},{5,15},{6,12},{7,13},{8,2},{9,3},... | collective-permute-start | bytes 196616 | tf_op jit(solution)/shard_map/ppermute | solution.py:647
  26.2 8.7 %collective-permute-start.8 = (bf16[2,32,512]{2,1,0:T(8,128)(2,1)S(1)}, bf16[2,32,512]{2,1,0:T(8,128)(2,1)S(1)}, u32[]{:S(2)}, u32[]{:S(2)}) collective-permute-start(bf16[2,32,512]{2,1,0:T(8,128)(2,1)S(1)} %get-tuple-element.83), channel_id=1, source_target_pairs={{0,6},{1,7},{2,4},{3,5},{4,2},{5,3},{6,0},{7,1},{8,14},{9,15},{10,... | collective-permute-start | bytes 196616 | tf_op jit(solution)/shard_map/ppermute | solution.py:647
  27.4 7.5 %collective-permute-start.9 = (bf16[2,32,512]{2,1,0:T(8,128)(2,1)S(1)}, bf16[2,32,512]{2,1,0:T(8,128)(2,1)S(1)}, u32[]{:S(2)}, u32[]{:S(2)}) collective-permute-start(bf16[2,32,512]{2,1,0:T(8,128)(2,1)S(1)} %get-tuple-element.84), channel_id=1, source_target_pairs={{0,4},{1,5},{2,6},{3,7},{4,0},{5,1},{6,2},{7,3},{8,12},{9,13},{10,... | collective-permute-start | bytes 196616 | tf_op jit(solution)/shard_map/ppermute | solution.py:647
  28.2 7.2 %collective-permute-start.10 = (bf16[2,32,512]{2,1,0:T(8,128)(2,1)S(1)}, bf16[2,32,512]{2,1,0:T(8,128)(2,1)S(1)}, u32[]{:S(2)}, u32[]{:S(2)}) collective-permute-start(bf16[2,32,512]{2,1,0:T(8,128)(2,1)S(1)} %get-tuple-element.90), channel_id=1, source_target_pairs={{0,8},{1,9},{2,10},{3,11},{4,12},{5,13},{6,14},{7,15},{8,0},{9,1},... | collective-permute-start | bytes 196616 | tf_op jit(solution)/shard_map/ppermute | solution.py:647
  32.8 4.3 %collective-permute-start.11 = (bf16[2,32,512]{2,1,0:T(8,128)(2,1)S(1)}, bf16[2,32,512]{2,1,0:T(8,128)(2,1)S(1)}, u32[]{:S(2)}, u32[]{:S(2)}) collective-permute-start(bf16[2,32,512]{2,1,0:T(8,128)(2,1)S(1)} %get-tuple-element.91), channel_id=1, source_target_pairs={{0,2},{1,3},{2,0},{3,1},{4,6},{5,7},{6,4},{7,5},{8,10},{9,11},{10,... | collective-permute-start | bytes 196616 | tf_op jit(solution)/shard_map/ppermute | solution.py:647
  34.9 2.2 %collective-permute-start.12 = (bf16[2,32,512]{2,1,0:T(8,128)(2,1)S(1)}, bf16[2,32,512]{2,1,0:T(8,128)(2,1)S(1)}, u32[]{:S(2)}, u32[]{:S(2)}) collective-permute-start(bf16[2,32,512]{2,1,0:T(8,128)(2,1)S(1)} %collective-permute-done.4.refs_0_), channel_id=1, source_target_pairs={{0,1},{1,0},{2,3},{3,2},{4,5},{5,4},{6,7},{7,6},{8,9},{9,8},{10,11... | collective-permute-start | bytes 196616 | tf_op jit(solution)/shard_map/ppermute | solution.py:647
  34.9 2.2 %collective-permute-start.13 = (bf16[2,32,512]{2,1,0:T(8,128)(2,1)S(1)}, bf16[2,32,512]{2,1,0:T(8,128)(2,1)S(1)}, u32[]{:S(2)}, u32[]{:S(2)}) collective-permute-start(bf16[2,32,512]{2,1,0:T(8,128)(2,1)S(1)} %collective-permute-done.5.refs_1_), channel_id=1, source_target_pairs={{0,1},{1,0},{2,3},{3,2},{4,5},{5,4},{6,7},{7,6},{8,9},{9,8},{10,11... | collective-permute-start | bytes 196616 | tf_op jit(solution)/shard_map/ppermute | solution.py:647
  41.7 3.8 %collective-permute-start.16 = (bf16[6,32,512]{2,1,0:T(8,128)(2,1)S(1)}, bf16[6,32,512]{2,1,0:T(8,128)(2,1)S(1)}, u32[]{:S(2)}, u32[]{:S(2)}) collective-permute-start(bf16[6,32,512]{2,1,0:T(8,128)(2,1)S(1)} %get-tuple-element.96), channel_id=1, source_target_pairs={{0,1},{1,0},{2,3},{3,2},{4,5},{5,4},{6,7},{7,6},{8,9},{9,8},{10,11... | collective-permute-start | bytes 589832 | tf_op jit(solution)/shard_map/ppermute | solution.py:647
  41.8 7.8 %collective-permute-start.14 = (bf16[2,32,512]{2,1,0:T(8,128)(2,1)S(1)}, bf16[2,32,512]{2,1,0:T(8,128)(2,1)S(1)}, u32[]{:S(2)}, u32[]{:S(2)}) collective-permute-start(bf16[2,32,512]{2,1,0:T(8,128)(2,1)S(1)} %get-tuple-element.93), channel_id=1, source_target_pairs={{0,14},{1,15},{2,12},{3,13},{4,10},{5,11},{6,8},{7,9},{8,6},{9,7},... | collective-permute-start | bytes 196616 | tf_op jit(solution)/shard_map/ppermute | solution.py:647
  43.5 8.0 %collective-permute-start.15 = (bf16[2,32,512]{2,1,0:T(8,128)(2,1)S(1)}, bf16[2,32,512]{2,1,0:T(8,128)(2,1)S(1)}, u32[]{:S(2)}, u32[]{:S(2)}) collective-permute-start(bf16[2,32,512]{2,1,0:T(8,128)(2,1)S(1)} %get-tuple-element.94), channel_id=1, source_target_pairs={{0,12},{1,13},{2,14},{3,15},{4,8},{5,9},{6,10},{7,11},{8,4},{9,5},... | collective-permute-start | bytes 196616 | tf_op jit(solution)/shard_map/ppermute | solution.py:647
  45.6 8.6 %collective-permute-start.17 = (bf16[2,32,512]{2,1,0:T(8,128)(2,1)S(1)}, bf16[2,32,512]{2,1,0:T(8,128)(2,1)S(1)}, u32[]{:S(2)}, u32[]{:S(2)}) collective-permute-start(bf16[2,32,512]{2,1,0:T(8,128)(2,1)S(1)} %get-tuple-element.97), channel_id=1, source_target_pairs={{0,10},{1,11},{2,8},{3,9},{4,14},{5,15},{6,12},{7,13},{8,2},{9,3},... | collective-permute-start | bytes 196616 | tf_op jit(solution)/shard_map/ppermute | solution.py:647
  45.8 8.4 %collective-permute-start.18 = (bf16[2,32,512]{2,1,0:T(8,128)(2,1)S(1)}, bf16[2,32,512]{2,1,0:T(8,128)(2,1)S(1)}, u32[]{:S(2)}, u32[]{:S(2)}) collective-permute-start(bf16[2,32,512]{2,1,0:T(8,128)(2,1)S(1)} %get-tuple-element.98), channel_id=1, source_target_pairs={{0,6},{1,7},{2,4},{3,5},{4,2},{5,3},{6,0},{7,1},{8,14},{9,15},{10,... | collective-permute-start | bytes 196616 | tf_op jit(solution)/shard_map/ppermute | solution.py:647
  48.9 5.3 %collective-permute-start.19 = (bf16[2,32,512]{2,1,0:T(8,128)(2,1)S(1)}, bf16[2,32,512]{2,1,0:T(8,128)(2,1)S(1)}, u32[]{:S(2)}, u32[]{:S(2)}) collective-permute-start(bf16[2,32,512]{2,1,0:T(8,128)(2,1)S(1)} %get-tuple-element.99), channel_id=1, source_target_pairs={{0,4},{1,5},{2,6},{3,7},{4,0},{5,1},{6,2},{7,3},{8,12},{9,13},{10,... | collective-permute-start | bytes 196616 | tf_op jit(solution)/shard_map/ppermute | solution.py:647
  49.6 6.5 %collective-permute-start.20 = (bf16[2,32,512]{2,1,0:T(8,128)(2,1)S(1)}, bf16[2,32,512]{2,1,0:T(8,128)(2,1)S(1)}, u32[]{:S(2)}, u32[]{:S(2)}) collective-permute-start(bf16[2,32,512]{2,1,0:T(8,128)(2,1)S(1)} %get-tuple-element.105), channel_id=1, source_target_pairs={{0,8},{1,9},{2,10},{3,11},{4,12},{5,13},{6,14},{7,15},{8,0},{9,1},... | collective-permute-start | bytes 196616 | tf_op jit(solution)/shard_map/ppermute | solution.py:647
  51.5 4.6 %collective-permute-start.21 = (bf16[2,32,512]{2,1,0:T(8,128)(2,1)S(1)}, bf16[2,32,512]{2,1,0:T(8,128)(2,1)S(1)}, u32[]{:S(2)}, u32[]{:S(2)}) collective-permute-start(bf16[2,32,512]{2,1,0:T(8,128)(2,1)S(1)} %get-tuple-element.106), channel_id=1, source_target_pairs={{0,2},{1,3},{2,0},{3,1},{4,6},{5,7},{6,4},{7,5},{8,10},{9,11},{10,... | collective-permute-start | bytes 196616 | tf_op jit(solution)/shard_map/ppermute | solution.py:647
  54.2 1.9 %collective-permute-start.22 = (bf16[2,32,512]{2,1,0:T(8,128)(2,1)S(1)}, bf16[2,32,512]{2,1,0:T(8,128)(2,1)S(1)}, u32[]{:S(2)}, u32[]{:S(2)}) collective-permute-start(bf16[2,32,512]{2,1,0:T(8,128)(2,1)S(1)} %collective-permute-done.14.refs_0_), channel_id=1, source_target_pairs={{0,1},{1,0},{2,3},{3,2},{4,5},{5,4},{6,7},{7,6},{8,9},{9,8},{10,11... | collective-permute-start | bytes 196616 | tf_op jit(solution)/shard_map/ppermute | solution.py:647
  54.2 1.9 %collective-permute-start.23 = (bf16[2,32,512]{2,1,0:T(8,128)(2,1)S(1)}, bf16[2,32,512]{2,1,0:T(8,128)(2,1)S(1)}, u32[]{:S(2)}, u32[]{:S(2)}) collective-permute-start(bf16[2,32,512]{2,1,0:T(8,128)(2,1)S(1)} %collective-permute-done.15.refs_1_), channel_id=1, source_target_pairs={{0,1},{1,0},{2,3},{3,2},{4,5},{5,4},{6,7},{7,6},{8,9},{9,8},{10,11... | collective-permute-start | bytes 196616 | tf_op jit(solution)/shard_map/ppermute | solution.py:647
  (8 other events, 78.9 us)

commit v23 on v21

--- a/solution.py
+++ b/solution.py
@@ -415,11 +415,53 @@
     return jnp.where(row == column, 1.0, 0.0).astype(jnp.bfloat16)
 
 
+def gather_blocks(plan, refs, blocks, sets):
+    members = refs[0].shape[1] // sets
+    return jnp.concatenate(
+        [
+            read_block(plan, refs, index, side, slice(s * members, (s + 1) * members))
+            for s in range(sets)
+            for index, side in blocks
+        ],
+        axis=0,
+    )
+
+
+def project_kernel(*refs, plan, sets):
+    in_refs, weight_ref, out_ref = refs[:-2], refs[-2], refs[-1]
+    block = gather_blocks(plan, in_refs, split_blocks(plan)[0], sets)
+    out_ref[...] = matmul(block, weight_ref[...]).astype(jnp.bfloat16)
+
+
+def project(plan, incoming, w_qkv, sets):
+    soon = split_blocks(plan)[0]
+    _, size, channels = incoming[0].shape
+    masks, late, _ = plan
+    there = [*range(late, len(masks) - 1 - late), len(masks) - 1, len(masks) + late]
+    filled = [array if index in there else incoming[late] for index, array in enumerate(incoming)]
+    return pl.pallas_call(
+        functools.partial(project_kernel, plan=plan, sets=sets),
+        in_specs=[vmem()] * (len(filled) + 1),
+        out_specs=vmem(),
+        out_shape=jax.ShapeDtypeStruct((len(soon) * size, w_qkv.shape[1]), jnp.bfloat16),
+        compiler_params=pltpu.CompilerParams(vmem_limit_bytes=4 * MIB),
+        cost_estimate=pl.CostEstimate(
+            flops=2 * len(soon) * size * channels * w_qkv.shape[1],
+            bytes_accessed=2 * w_qkv.size + 8 * len(soon) * size * channels,
+            transcendentals=0,
+        ),
+        name="project",
+    )(*filled, w_qkv)
+
+
 def attend_kernel(*refs, plan, sets, came):
     masks, _, sides = plan
     slabs = len(masks)
     _, size, channels = refs[0].shape
+    soon, rest = split_blocks(plan)
     in_refs, weight_ref, out_refs = refs[:came], refs[came], refs[came + 1 : -6]
+    if soon:
+        soon_ref, out_refs = out_refs[0], out_refs[1:]
     query_ref, key_ref, value_ref, turned_ref, even_ref, odd_ref = refs[-6:]
     members = size // sets
     count = slabs * sides * members
@@ -435,23 +477,18 @@
         for j in range(group_heads)
     ]
     turn_values = identity(channels)
-    block = jnp.concatenate(
-        [
-            read_block(plan, in_refs, index, side, slice(s * members, (s + 1) * members))
-            for s in range(sets)
-            for index in range(slabs)
-            for side in range(sides)
-        ],
-        axis=0,
-    )
-    qkv = matmul(block, weight_ref[...]).astype(jnp.bfloat16)
+    block = gather_blocks(plan, in_refs, rest, sets)
+    projected = matmul(block, weight_ref[...]).astype(jnp.bfloat16)
     for s in range(sets):
-        own_rows = slice(s * count, (s + 1) * count)
-        values = matmul_nt(turn_values, qkv[own_rows, 2 * channels :]).astype(jnp.bfloat16)
+        near, far = len(soon) * members, len(rest) * members
+        qkv = projected[s * far : (s + 1) * far]
+        if soon:
+            qkv = jnp.concatenate([soon_ref[s * near : (s + 1) * near, :], qkv], axis=0)
+        values = matmul_nt(turn_values, qkv[:, 2 * channels :]).astype(jnp.bfloat16)
         for group in range(groups):
             spot = group * LANES
-            query_ref[s * groups + group] = qkv[own_rows, spot : spot + LANES]
-            key_ref[s * groups + group] = qkv[own_rows, channels + spot : channels + spot + LANES]
+            query_ref[s * groups + group] = qkv[:, spot : spot + LANES]
+            key_ref[s * groups + group] = qkv[:, channels + spot : channels + spot + LANES]
             for j in range(group_heads):
                 head = (group * group_heads + j) * head_width
                 value_ref[s * groups + group, j, :head_width] = values[head : head + head_width]
@@ -488,13 +525,11 @@
     for s in range(sets):
         turned = turned_ref[s * groups : (s + 1) * groups].reshape(channels, count)
         attended = matmul_nt(turn_tokens, turned).astype(jnp.bfloat16)
-        for index in range(slabs):
-            for side in range(sides):
-                start = (index * sides + side) * members
-                write_block(
-                    plan, out_refs, index, side, slice(s * members, (s + 1) * members),
-                    attended[start : start + members],
-                )
+        for number, (index, side) in enumerate(soon + rest):
+            write_block(
+                plan, out_refs, index, side, slice(s * members, (s + 1) * members),
+                attended[number * members : (number + 1) * members],
+            )
 
 
 def attend(plan, incoming, w_qkv, sets):
@@ -502,12 +537,13 @@
     _, size, channels = incoming[0].shape
     count = len(masks) * sides * size // sets
     sent = outgoing_shapes(plan, size, channels)
+    soon = [project(plan, incoming, w_qkv, sets)] if split_blocks(plan)[0] else []
     head_width = channels // HEADS
     group_heads = LANES // head_width
     total = sets * channels // LANES
     return pl.pallas_call(
         functools.partial(attend_kernel, plan=plan, sets=sets, came=len(incoming)),
-        in_specs=[vmem()] * (len(incoming) + 1),
+        in_specs=[vmem()] * (len(incoming) + 1 + len(soon)),
         out_specs=[vmem()] * len(sent),
         out_shape=[jax.ShapeDtypeStruct(shape, jnp.bfloat16) for shape in sent],
         scratch_shapes=[
@@ -525,7 +561,7 @@
             transcendentals=sets * HEADS * count * count,
         ),
         name="attend",
-    )(*incoming, w_qkv)
+    )(*incoming, w_qkv, *soon)
 
 
 def finish_kernel(own_ref, *refs, plan):
@@ -586,6 +622,15 @@
     return masks, 2, 2
 
 
+def split_blocks(plan):
+    masks, late, sides = plan
+    blocks = [(index, side) for index in range(len(masks)) for side in range(sides)]
+    if sides == 1:
+        return [], blocks
+    soon = [*range(late, len(masks) - 1 - late), len(masks) - 1]
+    return [b for b in blocks if b[0] in soon], [b for b in blocks if b[0] not in soon]
+
+
 def outgoing_shapes(plan, size, channels):
     masks, late, sides = plan
     if sides == 1:

time: 57.6 us -> 57.1 us (level)
  transfers between devices with their start and end apart: 24 -> 24, of which waited for: 5 -> 5; matrix products, arithmetic and copies ran while one was open for 0% -> 0% of each run, Pallas kernels for 13% -> 15%
where the time goes in v23:
time: 57.1 us; the launch traced here: 56.9 us
  starting transfers between devices  33.1 us (58%)
  Pallas kernels  16.6 us (29%)
  waiting for transfers between devices  5.92 us (10%)
  local copies, waits for them, and re-layouts  0.93 us (2%)
    ppermute x20, starting transfers between devices, swap(): lax.ppermute(slab, ('row', 'col'), [(i, i ^ mask) for i in range(devices)])  28.5 us
    ppermute x20, waiting for transfers between devices, swap(): lax.ppermute(slab, ('row', 'col'), [(i, i ^ mask) for i in range(devices)])  5.91 us
    pallas_call x2, Pallas kernels, inner(): pl.pallas_call(functools.partial(inner_kernel, rows=rows, cols=cols, firs...  5.06 us
    ppermute x4, starting transfers between devices, swap_pairs(): return lax.ppermute(edge, axis, pairs + [(b, a) for a, b in pairs])  4.61 us
    pallas_call x1, Pallas kernels, attend(): pl.pallas_call(functools.partial(attend_kernel, plan=plan, sets=sets, cam...  4.02 us
    pallas_call x1, Pallas kernels, expand(): pl.pallas_call(expand_kernel, in_specs=[vmem()] * 2, out_specs=vmem(), ou...  2.31 us
    pallas_call x1, Pallas kernels, rim(): pl.pallas_call(functools.partial(rim_kernel, rows=rows, cols=cols, plan=p...  2.07 us
    pallas_call x1, Pallas kernels, finish(): pl.pallas_call(functools.partial(finish_kernel, plan=plan), in_specs=[pl....  1.72 us
  transfers between devices with their start and end apart: 24, of which 5 were waited for; matrix products, arithmetic and copies ran while one was open for 0% of the time, Pallas kernels for 15%

profile of v23, /device:TPU:0, one launch (start us, length us, event | category | flops | bytes accessed | tf_op | source)
XLA Modules:
  0.0 56.9 jit_solution(10674750137661762311)
XLA Ops:
  0.0 0.9 %slice_bitcast_fusion = (f32[32,512]{1,0:T(8,128)S(1)}, f32[32,512]{1,0:T(8,128)S(1)}) fusion(f32[16,32,512]{2,1,0:T(8,128)} %param.8), kind=kLoop, calls=%fused_computation | loop fusion | bytes 262144 | tf_op jit(solution)/shard_map/squeeze | solution.py:749
  1.1 3.1 %collective-permute-start = (bf16[32,512]{1,0:T(8,128)(2,1)S(1)}, bf16[32,512]{1,0:T(8,128)(2,1)S(1)}, u32[]{:S(2)}, u32[]{:S(2)}) collective-permute-start(bf16[32,512]{1,0:T(8,128)(2,1)S(1)} %get-tuple-element.62), channel_id=1, source_target_pairs={{0,4},{8,12},{4,0},{12,8},{1,5},{9,13},{5,1},{13,9},{2,6},{10,14},... | collective-permute-start | bytes 98312 | tf_op jit(solution)/shard_map/ppermute | solution.py:614
  5.2 2.3 %expand.1.expanded_ref = f32[8448,128]{1,0:T(8,128)S(1)} custom-call(bf16[512,512]{1,0:T(8,128)(2,1)S(1)} %half_norm.1.normed_ref, bf16[512,2048]{1,0:T(8,128)(2,1)S(1)} %copy-done), custom_call_target="tpu_custom_call" | custom-call | flops 10000000000 | bytes 6815744 | tf_op jit(solution)/shard_map/expand/pallas_call | solution.py:189
  7.6 1.2 %inner.2 = (f32[512,512]{1,0:T(8,128)S(1)}, f32[4,96,128]{2,1,0:T(8,128)S(1)}) custom-call(f32[8448,128]{1,0:T(8,128)S(1)} %expand.1.expanded_ref, f32[512,512]{1,0:T(8,128)S(1)} %bitcast.10, f32[3,3,2048]{2,1,0:T(4,128)S(1)} %copy-done.6, bf16[2048,512]{1,0:T(8,128)(2,1)S(1)} %copy-done.1), custom_call_target="tpu_custom_call" | custom-call | flops 4000000000 | bytes 3145728 | tf_op jit(solution)/shard_map/inner/pallas_call | solution.py:279
  10.1 3.8 %inner.3 = (f32[512,512]{1,0:T(8,128)S(1)}, f32[12,96,128]{2,1,0:T(8,128)S(1)}) custom-call(f32[8448,128]{1,0:T(8,128)S(1)} %expand.1.expanded_ref, f32[512,512]{1,0:T(8,128)S(1)} %get-tuple-element.67.start_ref, f32[3,3,2048]{2,1,0:T(4,128)S(1)} %copy-done.6, bf16[2048,512]{1,0:T(8,128)(2,1)S(1)} %copy-done.1), custom_call_target="tpu_custom_call" | custom-call | flops 12000000000 | bytes 5242880 | tf_op jit(solution)/shard_map/inner/pallas_call | solution.py:279
  14.0 2.1 %rim.1 = (f32[512,512]{1,0:T(8,128)S(1)}, bf16[2,32,512]{2,1,0:T(8,128)(2,1)S(1)}, bf16[2,32,512]{2,1,0:T(8,128)(2,1)S(1)}, bf16[1,32,512]{2,1,0:T(8,128)(2,1)S(...) custom-call(s32[1]{0:T(128)} %bitcast.own_ref, s32[1]{0:T(128)} %bitcast.2.odd_col_ref, ...), custom_call_target="tpu_custom_call" | custom-call | flops 805306368 | bytes 6815744 | tf_op jit(solution)/shard_map/rim/pallas_call | solution.py:388
  16.0 3.0 %collective-permute-start.6 = (bf16[6,32,512]{2,1,0:T(8,128)(2,1)S(1)}, bf16[6,32,512]{2,1,0:T(8,128)(2,1)S(1)}, u32[]{:S(2)}, u32[]{:S(2)}) collective-permute-start(bf16[6,32,512]{2,1,0:T(8,128)(2,1)S(1)} %get-tuple-element.81), channel_id=1, source_target_pairs={{0,1},{1,0},{2,3},{3,2},{4,5},{5,4},{6,7},{7,6},{8,9},{9,8},{10,11... | collective-permute-start | bytes 589832 | tf_op jit(solution)/shard_map/ppermute | solution.py:692
  19.0 2.7 %collective-permute-start.4 = (bf16[2,32,512]{2,1,0:T(8,128)(2,1)S(1)}, bf16[2,32,512]{2,1,0:T(8,128)(2,1)S(1)}, u32[]{:S(2)}, u32[]{:S(2)}) collective-permute-start(bf16[2,32,512]{2,1,0:T(8,128)(2,1)S(1)} %get-tuple-element.78), channel_id=1, source_target_pairs={{0,14},{1,15},{2,12},{3,13},{4,10},{5,11},{6,8},{7,9},{8,6},{9,7},... | collective-permute-start | bytes 196616 | tf_op jit(solution)/shard_map/ppermute | solution.py:692
  21.7 1.1 %collective-permute-start.5 = (bf16[2,32,512]{2,1,0:T(8,128)(2,1)S(1)}, bf16[2,32,512]{2,1,0:T(8,128)(2,1)S(1)}, u32[]{:S(2)}, u32[]{:S(2)}) collective-permute-start(bf16[2,32,512]{2,1,0:T(8,128)(2,1)S(1)} %get-tuple-element.79), channel_id=1, source_target_pairs={{0,12},{1,13},{2,14},{3,15},{4,8},{5,9},{6,10},{7,11},{8,4},{9,5},... | collective-permute-start | bytes 196616 | tf_op jit(solution)/shard_map/ppermute | solution.py:692
  22.8 3.0 %collective-permute-start.7 = (bf16[2,32,512]{2,1,0:T(8,128)(2,1)S(1)}, bf16[2,32,512]{2,1,0:T(8,128)(2,1)S(1)}, u32[]{:S(2)}, u32[]{:S(2)}) collective-permute-start(bf16[2,32,512]{2,1,0:T(8,128)(2,1)S(1)} %get-tuple-element.82), channel_id=1, source_target_pairs={{0,10},{1,11},{2,8},{3,9},{4,14},{5,15},{6,12},{7,13},{8,2},{9,3},... | collective-permute-start | bytes 196616 | tf_op jit(solution)/shard_map/ppermute | solution.py:692
  25.8 1.2 %collective-permute-start.8 = (bf16[2,32,512]{2,1,0:T(8,128)(2,1)S(1)}, bf16[2,32,512]{2,1,0:T(8,128)(2,1)S(1)}, u32[]{:S(2)}, u32[]{:S(2)}) collective-permute-start(bf16[2,32,512]{2,1,0:T(8,128)(2,1)S(1)} %get-tuple-element.83), channel_id=1, source_target_pairs={{0,6},{1,7},{2,4},{3,5},{4,2},{5,3},{6,0},{7,1},{8,14},{9,15},{10,... | collective-permute-start | bytes 196616 | tf_op jit(solution)/shard_map/ppermute | solution.py:692
  27.0 0.8 %collective-permute-start.9 = (bf16[2,32,512]{2,1,0:T(8,128)(2,1)S(1)}, bf16[2,32,512]{2,1,0:T(8,128)(2,1)S(1)}, u32[]{:S(2)}, u32[]{:S(2)}) collective-permute-start(bf16[2,32,512]{2,1,0:T(8,128)(2,1)S(1)} %get-tuple-element.84), channel_id=1, source_target_pairs={{0,4},{1,5},{2,6},{3,7},{4,0},{5,1},{6,2},{7,3},{8,12},{9,13},{10,... | collective-permute-start | bytes 196616 | tf_op jit(solution)/shard_map/ppermute | solution.py:692
  27.9 4.6 %collective-permute-start.10 = (bf16[2,32,512]{2,1,0:T(8,128)(2,1)S(1)}, bf16[2,32,512]{2,1,0:T(8,128)(2,1)S(1)}, u32[]{:S(2)}, u32[]{:S(2)}) collective-permute-start(bf16[2,32,512]{2,1,0:T(8,128)(2,1)S(1)} %get-tuple-element.90), channel_id=1, source_target_pairs={{0,8},{1,9},{2,10},{3,11},{4,12},{5,13},{6,14},{7,15},{8,0},{9,1},... | collective-permute-start | bytes 196616 | tf_op jit(solution)/shard_map/ppermute | solution.py:692
  32.9 1.7 %collective-permute-done.7.refs_0_.refs_1_.refs_2_.refs_5_.refs_6_.refs_8_.refs_9_ = bf16[2,32,512]{2,1,0:T(8,128)(2,1)S(1)} collective-permute-done((bf16[2,32,512]{2,1,0:T(8,128)(2,1)S(1)}, bf16[2,32,512]{2,1,0:T(8,128)(2,1)S(1)}, u32[]{:S(2)}, u32[]{:S(2)}) %collective-permute-start.7) | collective-permute-done | bytes 65568 | tf_op jit(solution)/shard_map/ppermute | solution.py:692
  35.7 1.0 %collective-permute-done.11.refs_6_ = bf16[2,32,512]{2,1,0:T(8,128)(2,1)S(1)} collective-permute-done((bf16[2,32,512]{2,1,0:T(8,128)(2,1)S(1)}, bf16[2,32,512]{2,1,0:T(8,128)(2,1)S(1)}, u32[]{:S(2)}, u32[]{:S(2)}) %collective-permute-start.11) | collective-permute-done | bytes 65568 | tf_op jit(solution)/shard_map/ppermute | solution.py:692
  36.7 4.0 %attend.1 = (bf16[2,32,512]{2,1,0:T(8,128)(2,1)S(1)}, bf16[2,32,512]{2,1,0:T(8,128)(2,1)S(1)}, bf16[1,32,512]{2,1,0:T(8,128)(2,1)S(1)}, bf16[6,32,512]{2,1,0:T(8,128)(2,1)S(1)}, bf16[5,32,512]{2,1,0:T(8,128)(2,1)S(1)}) custom-call(bf16[2,32,512]{2,1,0:T(8,128)(2,1)S(1)} %collective-permute-done.4.refs_0_, ...), custom_call_target="tpu_custom_call" | custom-call | flops 1073741824 | bytes 2621440 | tf_op jit(solution)/shard_map/attend/pallas_call | solution.py:544
  40.9 1.7 %collective-permute-start.14 = (bf16[2,32,512]{2,1,0:T(8,128)(2,1)S(1)}, bf16[2,32,512]{2,1,0:T(8,128)(2,1)S(1)}, u32[]{:S(2)}, u32[]{:S(2)}) collective-permute-start(bf16[2,32,512]{2,1,0:T(8,128)(2,1)S(1)} %get-tuple-element.93), channel_id=1, source_target_pairs={{0,14},{1,15},{2,12},{3,13},{4,10},{5,11},{6,8},{7,9},{8,6},{9,7},... | collective-permute-start | bytes 196616 | tf_op jit(solution)/shard_map/ppermute | solution.py:692
  42.6 2.0 %collective-permute-start.15 = (bf16[2,32,512]{2,1,0:T(8,128)(2,1)S(1)}, bf16[2,32,512]{2,1,0:T(8,128)(2,1)S(1)}, u32[]{:S(2)}, u32[]{:S(2)}) collective-permute-start(bf16[2,32,512]{2,1,0:T(8,128)(2,1)S(1)} %get-tuple-element.94), channel_id=1, source_target_pairs={{0,12},{1,13},{2,14},{3,15},{4,8},{5,9},{6,10},{7,11},{8,4},{9,5},... | collective-permute-start | bytes 196616 | tf_op jit(solution)/shard_map/ppermute | solution.py:692
  44.8 3.1 %collective-permute-start.18 = (bf16[2,32,512]{2,1,0:T(8,128)(2,1)S(1)}, bf16[2,32,512]{2,1,0:T(8,128)(2,1)S(1)}, u32[]{:S(2)}, u32[]{:S(2)}) collective-permute-start(bf16[2,32,512]{2,1,0:T(8,128)(2,1)S(1)} %get-tuple-element.98), channel_id=1, source_target_pairs={{0,6},{1,7},{2,4},{3,5},{4,2},{5,3},{6,0},{7,1},{8,14},{9,15},{10,... | collective-permute-start | bytes 196616 | tf_op jit(solution)/shard_map/ppermute | solution.py:692
  48.6 1.9 %collective-permute-start.20 = (bf16[2,32,512]{2,1,0:T(8,128)(2,1)S(1)}, bf16[2,32,512]{2,1,0:T(8,128)(2,1)S(1)}, u32[]{:S(2)}, u32[]{:S(2)}) collective-permute-start(bf16[2,32,512]{2,1,0:T(8,128)(2,1)S(1)} %get-tuple-element.105), channel_id=1, source_target_pairs={{0,8},{1,9},{2,10},{3,11},{4,12},{5,13},{6,14},{7,15},{8,0},{9,1},... | collective-permute-start | bytes 196616 | tf_op jit(solution)/shard_map/ppermute | solution.py:692
  50.5 1.6 %collective-permute-start.21 = (bf16[2,32,512]{2,1,0:T(8,128)(2,1)S(1)}, bf16[2,32,512]{2,1,0:T(8,128)(2,1)S(1)}, u32[]{:S(2)}, u32[]{:S(2)}) collective-permute-start(bf16[2,32,512]{2,1,0:T(8,128)(2,1)S(1)} %get-tuple-element.106), channel_id=1, source_target_pairs={{0,2},{1,3},{2,0},{3,1},{4,6},{5,7},{6,4},{7,5},{8,10},{9,11},{10,... | collective-permute-start | bytes 196616 | tf_op jit(solution)/shard_map/ppermute | solution.py:692
  52.2 1.1 %collective-permute-done.17.refs_2_ = bf16[2,32,512]{2,1,0:T(8,128)(2,1)S(1)} collective-permute-done((bf16[2,32,512]{2,1,0:T(8,128)(2,1)S(1)}, bf16[2,32,512]{2,1,0:T(8,128)(2,1)S(1)}, u32[]{:S(2)}, u32[]{:S(2)}) %collective-permute-start.17) | collective-permute-done | bytes 65568 | tf_op jit(solution)/shard_map/ppermute | solution.py:692
  53.8 1.4 %collective-permute-done.20.refs_5_ = bf16[2,32,512]{2,1,0:T(8,128)(2,1)S(1)} collective-permute-done((bf16[2,32,512]{2,1,0:T(8,128)(2,1)S(1)}, bf16[2,32,512]{2,1,0:T(8,128)(2,1)S(1)}, u32[]{:S(2)}, u32[]{:S(2)}) %collective-permute-start.20) | collective-permute-done | bytes 65568 | tf_op jit(solution)/shard_map/ppermute | solution.py:692
  55.2 1.7 %finish.1 = f32[512,512]{1,0:T(8,128)} custom-call(s32[1]{0:T(128)} %bitcast.own_ref, bf16[2,32,512]{2,1,0:T(8,128)(2,1)S(1)} %collective-permute-done.14.refs_0_, bf16[2,32,512]{2,1,0:T(8,128)(2,1)S(1)} %collective-permute-done.15.refs_1_, bf16[2,32,512]{2,1,0:T(8,128)(2,1)S(1)} %collective-permute-done.17.refs_2_, ...), custom_call_target="tpu_custom_call" | custom-call | tf_op jit(solution)/shard_map/finish/pallas_call | solution.py:597
  (53 shorter events, 5.5 us)
Async XLA Ops:
  1.1 7.7 %collective-permute-start = (bf16[32,512]{1,0:T(8,128)(2,1)S(1)}, bf16[32,512]{1,0:T(8,128)(2,1)S(1)}, u32[]{:S(2)}, u32[]{:S(2)}) collective-permute-start(bf16[32,512]{1,0:T(8,128)(2,1)S(1)} %get-tuple-element.62), channel_id=1, source_target_pairs={{0,4},{8,12},{4,0},{12,8},{1,5},{9,13},{5,1},{13,9},{2,6},{10,14},... | collective-permute-start | bytes 98312 | tf_op jit(solution)/shard_map/ppermute | solution.py:614
  4.2 4.6 %collective-permute-start.1 = (bf16[32,512]{1,0:T(8,128)(2,1)S(1)}, bf16[32,512]{1,0:T(8,128)(2,1)S(1)}, u32[]{:S(2)}, u32[]{:S(2)}) collective-permute-start(bf16[32,512]{1,0:T(8,128)(2,1)S(1)} %get-tuple-element.63), channel_id=1, source_target_pairs={{4,8},{8,4},{5,9},{9,5},{6,10},{10,6},{7,11},{11,7},{20,24},{24,20... | collective-permute-start | bytes 98312 | tf_op jit(solution)/shard_map/ppermute | solution.py:614
  9.2 4.7 %collective-permute-start.2 = (bf16[32,512]{1,0:T(8,128)(2,1)S(1)}, bf16[32,512]{1,0:T(8,128)(2,1)S(1)}, u32[]{:S(2)}, u32[]{:S(2)}) collective-permute-start(bf16[32,512]{1,0:T(8,128)(2,1)S(1)} %get-tuple-element.76), channel_id=1, source_target_pairs={{0,1},{2,3},{1,0},{3,2},{4,5},{6,7},{5,4},{7,6},{8,9},{10,11},{9,8... | collective-permute-start | bytes 98312 | tf_op jit(solution)/shard_map/ppermute | solution.py:614
  9.3 4.6 %collective-permute-start.3 = (bf16[32,512]{1,0:T(8,128)(2,1)S(1)}, bf16[32,512]{1,0:T(8,128)(2,1)S(1)}, u32[]{:S(2)}, u32[]{:S(2)}) collective-permute-start(bf16[32,512]{1,0:T(8,128)(2,1)S(1)} %get-tuple-element.77), channel_id=1, source_target_pairs={{1,2},{2,1},{5,6},{6,5},{9,10},{10,9},{13,14},{14,13},{17,18},{18,... | collective-permute-start | bytes 98312 | tf_op jit(solution)/shard_map/ppermute | solution.py:614
  16.0 6.8 %collective-permute-start.6 = (bf16[6,32,512]{2,1,0:T(8,128)(2,1)S(1)}, bf16[6,32,512]{2,1,0:T(8,128)(2,1)S(1)}, u32[]{:S(2)}, u32[]{:S(2)}) collective-permute-start(bf16[6,32,512]{2,1,0:T(8,128)(2,1)S(1)} %get-tuple-element.81), channel_id=1, source_target_pairs={{0,1},{1,0},{2,3},{3,2},{4,5},{5,4},{6,7},{7,6},{8,9},{9,8},{10,11... | collective-permute-start | bytes 589832 | tf_op jit(solution)/shard_map/ppermute | solution.py:692
  19.0 8.9 %collective-permute-start.4 = (bf16[2,32,512]{2,1,0:T(8,128)(2,1)S(1)}, bf16[2,32,512]{2,1,0:T(8,128)(2,1)S(1)}, u32[]{:S(2)}, u32[]{:S(2)}) collective-permute-start(bf16[2,32,512]{2,1,0:T(8,128)(2,1)S(1)} %get-tuple-element.78), channel_id=1, source_target_pairs={{0,14},{1,15},{2,12},{3,13},{4,10},{5,11},{6,8},{7,9},{8,6},{9,7},... | collective-permute-start | bytes 196616 | tf_op jit(solution)/shard_map/ppermute | solution.py:692
  21.7 10.8 %collective-permute-start.5 = (bf16[2,32,512]{2,1,0:T(8,128)(2,1)S(1)}, bf16[2,32,512]{2,1,0:T(8,128)(2,1)S(1)}, u32[]{:S(2)}, u32[]{:S(2)}) collective-permute-start(bf16[2,32,512]{2,1,0:T(8,128)(2,1)S(1)} %get-tuple-element.79), channel_id=1, source_target_pairs={{0,12},{1,13},{2,14},{3,15},{4,8},{5,9},{6,10},{7,11},{8,4},{9,5},... | collective-permute-start | bytes 196616 | tf_op jit(solution)/shard_map/ppermute | solution.py:692
  22.8 11.7 %collective-permute-start.7 = (bf16[2,32,512]{2,1,0:T(8,128)(2,1)S(1)}, bf16[2,32,512]{2,1,0:T(8,128)(2,1)S(1)}, u32[]{:S(2)}, u32[]{:S(2)}) collective-permute-start(bf16[2,32,512]{2,1,0:T(8,128)(2,1)S(1)} %get-tuple-element.82), channel_id=1, source_target_pairs={{0,10},{1,11},{2,8},{3,9},{4,14},{5,15},{6,12},{7,13},{8,2},{9,3},... | collective-permute-start | bytes 196616 | tf_op jit(solution)/shard_map/ppermute | solution.py:692
  25.8 8.7 %collective-permute-start.8 = (bf16[2,32,512]{2,1,0:T(8,128)(2,1)S(1)}, bf16[2,32,512]{2,1,0:T(8,128)(2,1)S(1)}, u32[]{:S(2)}, u32[]{:S(2)}) collective-permute-start(bf16[2,32,512]{2,1,0:T(8,128)(2,1)S(1)} %get-tuple-element.83), channel_id=1, source_target_pairs={{0,6},{1,7},{2,4},{3,5},{4,2},{5,3},{6,0},{7,1},{8,14},{9,15},{10,... | collective-permute-start | bytes 196616 | tf_op jit(solution)/shard_map/ppermute | solution.py:692
  27.0 7.5 %collective-permute-start.9 = (bf16[2,32,512]{2,1,0:T(8,128)(2,1)S(1)}, bf16[2,32,512]{2,1,0:T(8,128)(2,1)S(1)}, u32[]{:S(2)}, u32[]{:S(2)}) collective-permute-start(bf16[2,32,512]{2,1,0:T(8,128)(2,1)S(1)} %get-tuple-element.84), channel_id=1, source_target_pairs={{0,4},{1,5},{2,6},{3,7},{4,0},{5,1},{6,2},{7,3},{8,12},{9,13},{10,... | collective-permute-start | bytes 196616 | tf_op jit(solution)/shard_map/ppermute | solution.py:692
  27.9 7.8 %collective-permute-start.10 = (bf16[2,32,512]{2,1,0:T(8,128)(2,1)S(1)}, bf16[2,32,512]{2,1,0:T(8,128)(2,1)S(1)}, u32[]{:S(2)}, u32[]{:S(2)}) collective-permute-start(bf16[2,32,512]{2,1,0:T(8,128)(2,1)S(1)} %get-tuple-element.90), channel_id=1, source_target_pairs={{0,8},{1,9},{2,10},{3,11},{4,12},{5,13},{6,14},{7,15},{8,0},{9,1},... | collective-permute-start | bytes 196616 | tf_op jit(solution)/shard_map/ppermute | solution.py:692
  32.5 4.3 %collective-permute-start.11 = (bf16[2,32,512]{2,1,0:T(8,128)(2,1)S(1)}, bf16[2,32,512]{2,1,0:T(8,128)(2,1)S(1)}, u32[]{:S(2)}, u32[]{:S(2)}) collective-permute-start(bf16[2,32,512]{2,1,0:T(8,128)(2,1)S(1)} %get-tuple-element.91), channel_id=1, source_target_pairs={{0,2},{1,3},{2,0},{3,1},{4,6},{5,7},{6,4},{7,5},{8,10},{9,11},{10,... | collective-permute-start | bytes 196616 | tf_op jit(solution)/shard_map/ppermute | solution.py:692
  34.6 2.2 %collective-permute-start.12 = (bf16[2,32,512]{2,1,0:T(8,128)(2,1)S(1)}, bf16[2,32,512]{2,1,0:T(8,128)(2,1)S(1)}, u32[]{:S(2)}, u32[]{:S(2)}) collective-permute-start(bf16[2,32,512]{2,1,0:T(8,128)(2,1)S(1)} %collective-permute-done.4.refs_0_), channel_id=1, source_target_pairs={{0,1},{1,0},{2,3},{3,2},{4,5},{5,4},{6,7},{7,6},{8,9},{9,8},{10,11... | collective-permute-start | bytes 196616 | tf_op jit(solution)/shard_map/ppermute | solution.py:692
  34.6 2.2 %collective-permute-start.13 = (bf16[2,32,512]{2,1,0:T(8,128)(2,1)S(1)}, bf16[2,32,512]{2,1,0:T(8,128)(2,1)S(1)}, u32[]{:S(2)}, u32[]{:S(2)}) collective-permute-start(bf16[2,32,512]{2,1,0:T(8,128)(2,1)S(1)} %collective-permute-done.5.refs_1_), channel_id=1, source_target_pairs={{0,1},{1,0},{2,3},{3,2},{4,5},{5,4},{6,7},{7,6},{8,9},{9,8},{10,11... | collective-permute-start | bytes 196616 | tf_op jit(solution)/shard_map/ppermute | solution.py:692
  40.8 3.8 %collective-permute-start.16 = (bf16[6,32,512]{2,1,0:T(8,128)(2,1)S(1)}, bf16[6,32,512]{2,1,0:T(8,128)(2,1)S(1)}, u32[]{:S(2)}, u32[]{:S(2)}) collective-permute-start(bf16[6,32,512]{2,1,0:T(8,128)(2,1)S(1)} %get-tuple-element.96), channel_id=1, source_target_pairs={{0,1},{1,0},{2,3},{3,2},{4,5},{5,4},{6,7},{7,6},{8,9},{9,8},{10,11... | collective-permute-start | bytes 589832 | tf_op jit(solution)/shard_map/ppermute | solution.py:692
  40.9 7.7 %collective-permute-start.14 = (bf16[2,32,512]{2,1,0:T(8,128)(2,1)S(1)}, bf16[2,32,512]{2,1,0:T(8,128)(2,1)S(1)}, u32[]{:S(2)}, u32[]{:S(2)}) collective-permute-start(bf16[2,32,512]{2,1,0:T(8,128)(2,1)S(1)} %get-tuple-element.93), channel_id=1, source_target_pairs={{0,14},{1,15},{2,12},{3,13},{4,10},{5,11},{6,8},{7,9},{8,6},{9,7},... | collective-permute-start | bytes 196616 | tf_op jit(solution)/shard_map/ppermute | solution.py:692
  42.6 8.0 %collective-permute-start.15 = (bf16[2,32,512]{2,1,0:T(8,128)(2,1)S(1)}, bf16[2,32,512]{2,1,0:T(8,128)(2,1)S(1)}, u32[]{:S(2)}, u32[]{:S(2)}) collective-permute-start(bf16[2,32,512]{2,1,0:T(8,128)(2,1)S(1)} %get-tuple-element.94), channel_id=1, source_target_pairs={{0,12},{1,13},{2,14},{3,15},{4,8},{5,9},{6,10},{7,11},{8,4},{9,5},... | collective-permute-start | bytes 196616 | tf_op jit(solution)/shard_map/ppermute | solution.py:692
  44.6 8.6 %collective-permute-start.17 = (bf16[2,32,512]{2,1,0:T(8,128)(2,1)S(1)}, bf16[2,32,512]{2,1,0:T(8,128)(2,1)S(1)}, u32[]{:S(2)}, u32[]{:S(2)}) collective-permute-start(bf16[2,32,512]{2,1,0:T(8,128)(2,1)S(1)} %get-tuple-element.97), channel_id=1, source_target_pairs={{0,10},{1,11},{2,8},{3,9},{4,14},{5,15},{6,12},{7,13},{8,2},{9,3},... | collective-permute-start | bytes 196616 | tf_op jit(solution)/shard_map/ppermute | solution.py:692
  44.8 8.4 %collective-permute-start.18 = (bf16[2,32,512]{2,1,0:T(8,128)(2,1)S(1)}, bf16[2,32,512]{2,1,0:T(8,128)(2,1)S(1)}, u32[]{:S(2)}, u32[]{:S(2)}) collective-permute-start(bf16[2,32,512]{2,1,0:T(8,128)(2,1)S(1)} %get-tuple-element.98), channel_id=1, source_target_pairs={{0,6},{1,7},{2,4},{3,5},{4,2},{5,3},{6,0},{7,1},{8,14},{9,15},{10,... | collective-permute-start | bytes 196616 | tf_op jit(solution)/shard_map/ppermute | solution.py:692
  48.0 5.3 %collective-permute-start.19 = (bf16[2,32,512]{2,1,0:T(8,128)(2,1)S(1)}, bf16[2,32,512]{2,1,0:T(8,128)(2,1)S(1)}, u32[]{:S(2)}, u32[]{:S(2)}) collective-permute-start(bf16[2,32,512]{2,1,0:T(8,128)(2,1)S(1)} %get-tuple-element.99), channel_id=1, source_target_pairs={{0,4},{1,5},{2,6},{3,7},{4,0},{5,1},{6,2},{7,3},{8,12},{9,13},{10,... | collective-permute-start | bytes 196616 | tf_op jit(solution)/shard_map/ppermute | solution.py:692
  48.6 6.6 %collective-permute-start.20 = (bf16[2,32,512]{2,1,0:T(8,128)(2,1)S(1)}, bf16[2,32,512]{2,1,0:T(8,128)(2,1)S(1)}, u32[]{:S(2)}, u32[]{:S(2)}) collective-permute-start(bf16[2,32,512]{2,1,0:T(8,128)(2,1)S(1)} %get-tuple-element.105), channel_id=1, source_target_pairs={{0,8},{1,9},{2,10},{3,11},{4,12},{5,13},{6,14},{7,15},{8,0},{9,1},... | collective-permute-start | bytes 196616 | tf_op jit(solution)/shard_map/ppermute | solution.py:692
  50.5 4.6 %collective-permute-start.21 = (bf16[2,32,512]{2,1,0:T(8,128)(2,1)S(1)}, bf16[2,32,512]{2,1,0:T(8,128)(2,1)S(1)}, u32[]{:S(2)}, u32[]{:S(2)}) collective-permute-start(bf16[2,32,512]{2,1,0:T(8,128)(2,1)S(1)} %get-tuple-element.106), channel_id=1, source_target_pairs={{0,2},{1,3},{2,0},{3,1},{4,6},{5,7},{6,4},{7,5},{8,10},{9,11},{10,... | collective-permute-start | bytes 196616 | tf_op jit(solution)/shard_map/ppermute | solution.py:692
  53.2 1.9 %collective-permute-start.22 = (bf16[2,32,512]{2,1,0:T(8,128)(2,1)S(1)}, bf16[2,32,512]{2,1,0:T(8,128)(2,1)S(1)}, u32[]{:S(2)}, u32[]{:S(2)}) collective-permute-start(bf16[2,32,512]{2,1,0:T(8,128)(2,1)S(1)} %collective-permute-done.14.refs_0_), channel_id=1, source_target_pairs={{0,1},{1,0},{2,3},{3,2},{4,5},{5,4},{6,7},{7,6},{8,9},{9,8},{10,11... | collective-permute-start | bytes 196616 | tf_op jit(solution)/shard_map/ppermute | solution.py:692
  53.3 1.9 %collective-permute-start.23 = (bf16[2,32,512]{2,1,0:T(8,128)(2,1)S(1)}, bf16[2,32,512]{2,1,0:T(8,128)(2,1)S(1)}, u32[]{:S(2)}, u32[]{:S(2)}) collective-permute-start(bf16[2,32,512]{2,1,0:T(8,128)(2,1)S(1)} %collective-permute-done.15.refs_1_), channel_id=1, source_target_pairs={{0,1},{1,0},{2,3},{3,2},{4,5},{5,4},{6,7},{7,6},{8,9},{9,8},{10,11... | collective-permute-start | bytes 196616 | tf_op jit(solution)/shard_map/ppermute | solution.py:692
  (8 other events, 77.6 us)

commit v24 on v23

--- a/solution.py
+++ b/solution.py
@@ -152,64 +152,15 @@
     return tokens + 16
 
 
-def expand_kernel(normed_ref, weight_ref, out_ref, even_ref, odd_ref):
-    tokens, tile = even_ref.shape
-    width = weight_ref.shape[1]
-    subs = tile // LANES
-
-    def multiply(index, made_ref):
-        lanes = pl.ds(pl.multiple_of(index * tile, tile), tile)
-        made_ref[...] = matmul(normed_ref[...], weight_ref[:, lanes])
-
-    def activate(index, made_ref):
-        for sub in range(subs):
-            row = (index * subs + sub) * padded_rows(tokens) + 8
-            out_ref[pl.ds(pl.multiple_of(row, 8), tokens), :] = gelu_of_half(
-                made_ref[:, sub * LANES : (sub + 1) * LANES]
-            )
-
-    def body(index, carry):
-        multiply(2 * index + 1, odd_ref)
-        activate(2 * index, even_ref)
-        multiply(2 * index + 2, even_ref)
-        activate(2 * index + 1, odd_ref)
-        return carry
-
-    count = width // tile
-    multiply(0, even_ref)
-    lax.fori_loop(0, count // 2 - 1, body, 0)
-    multiply(count - 1, odd_ref)
-    activate(count - 2, even_ref)
-    activate(count - 1, odd_ref)
-
-
-def expand(normed, w_expand):
-    tokens, channels = normed.shape
-    width = w_expand.shape[1]
-    return pl.pallas_call(
-        expand_kernel,
-        in_specs=[vmem()] * 2,
-        out_specs=vmem(),
-        out_shape=jax.ShapeDtypeStruct((width // LANES * padded_rows(tokens), LANES), jnp.float32),
-        scratch_shapes=[
-            pltpu.VMEM((tokens, divisor(width // 2, 256, LANES)), jnp.float32)
-        ] * 2,
-        compiler_params=pltpu.CompilerParams(vmem_limit_bytes=6 * MIB),
-        cost_estimate=pl.CostEstimate(
-            flops=10**10,
-            bytes_accessed=tokens * channels * 2 + channels * width * 2 + tokens * width * 4,
-            transcendentals=tokens * width,
-        ),
-        name="expand",
-    )(normed, w_expand)
-
-
 def inner_kernel(
-    expanded_ref, start_ref, depth_ref, w_project_ref, total_ref, rim_ref, even_ref, odd_ref,
-    *, rows, cols, first, count,
+    odd_col_ref, normed_ref, start_ref, w_expand_ref, depth_ref, w_project_ref, total_ref, rim_ref,
+    even_ref, odd_ref, even_grown_ref, odd_grown_ref, *, rows, cols, first, count,
 ):
     tokens = rows * cols
     tile = even_ref.shape[1]
+    origin = jnp.minimum(odd_col_ref[0], 0)
+    active_refs = even_ref, odd_ref
+    grown_refs = even_grown_ref, odd_grown_ref
     subs = tile // LANES
     position = lax.broadcasted_iota(jnp.int32, (8, LANES), 0)
     at_first = position == 0
@@ -220,11 +171,21 @@
         foot = jnp.where(at_last, 0.0, value[-8:]) if high else value[-8:]
         return jnp.concatenate([head, value[8:-8], foot], axis=0)
 
-    def convolve(index, out_ref):
+    def grow(index):
+        lanes = slice((first + index) * tile, (first + index + 1) * tile)
+        made = gelu_of_half(matmul(normed_ref[...], w_expand_ref[:, lanes]))
+        for sub in range(subs):
+            start = sub * padded_rows(tokens) + 8
+            grown_refs[index % 2][start : start + tokens, :] = made[
+                :, sub * LANES : (sub + 1) * LANES
+            ]
+
+    def convolve(index):
+        out_ref, grown_ref = active_refs[index % 2], grown_refs[index % 2]
         for sub in range(subs):
             chunk = (first + index) * subs + sub
-            lanes = pl.ds(pl.multiple_of(chunk * LANES, LANES), LANES)
-            base = chunk * padded_rows(tokens) + 8
+            lanes = slice(chunk * LANES, (chunk + 1) * LANES)
+            base = origin + sub * padded_rows(tokens) + 8
             here = index * subs + sub
             taps = [[0.5 * depth_ref[p, q : q + 1, lanes] for q in range(3)] for p in range(3)]
             spot = slice(sub * LANES, (sub + 1) * LANES)
@@ -232,7 +193,7 @@
             for y in range(rows + 1):
                 if y < rows:
                     parts = [
-                        expanded_ref[pl.ds(base + (y * cols + q), cols), :] for q in (-1, 0, 1)
+                        grown_ref[pl.ds(base + (y * cols + q), cols), :] for q in (-1, 0, 1)
                     ]
                     parts[0] = clear_ends(parts[0], True, False)
                     parts[2] = clear_ends(parts[2], False, True)
@@ -254,45 +215,42 @@
                         made = clear_ends(gelu_of_half(done), True, True)
                     out_ref[(y - 1) * cols : y * cols, spot] = made.astype(jnp.bfloat16)
 
-    def project(index, in_ref, from_ref):
-        piece = pl.ds(pl.multiple_of((first + index) * tile, tile), tile)
-        total_ref[...] = from_ref[...] + matmul(in_ref[...], w_project_ref[piece, :])
-
-    convolve(0, even_ref)
-    project(0, even_ref, start_ref)
-    convolve(1, odd_ref)
-
-    def body(index, carry):
-        convolve(2 * index, even_ref)
-        project(2 * index - 1, odd_ref, total_ref)
-        convolve(2 * index + 1, odd_ref)
-        project(2 * index, even_ref, total_ref)
-        return carry
-
-    lax.fori_loop(1, count // 2, body, 0)
-    project(count - 1, odd_ref, total_ref)
-
-
-def inner(expanded, start, depth_kernel, w_project, rows, cols, first, count, tile):
+    def add(index):
+        piece = slice((first + index) * tile, (first + index + 1) * tile)
+        from_ref = total_ref if index else start_ref
+        total_ref[...] = from_ref[...] + matmul(active_refs[index % 2][...], w_project_ref[piece, :])
+
+    grow(0)
+    for index in range(count):
+        if index + 1 < count:
+            grow(index + 1)
+        convolve(index)
+        if index:
+            add(index - 1)
+    add(count - 1)
+
+
+def inner(odd_col, normed, start, w_expand, depth_kernel, w_project, rows, cols, first, count, tile):
     tokens, channels = start.shape
     rim = (count * tile // LANES, 2 * cols + 2 * rows, LANES)
     return pl.pallas_call(
         functools.partial(inner_kernel, rows=rows, cols=cols, first=first, count=count),
-        in_specs=[vmem()] * 4,
+        in_specs=[pl.BlockSpec(memory_space=pltpu.SMEM)] + [vmem()] * 5,
         out_specs=[vmem()] * 2,
         out_shape=[
             jax.ShapeDtypeStruct((tokens, channels), jnp.float32),
             jax.ShapeDtypeStruct(rim, jnp.float32),
         ],
-        scratch_shapes=[pltpu.VMEM((tokens, tile), jnp.bfloat16)] * 2,
-        compiler_params=pltpu.CompilerParams(vmem_limit_bytes=6 * MIB),
+        scratch_shapes=[pltpu.VMEM((tokens, tile), jnp.bfloat16)] * 2
+        + [pltpu.VMEM((tile // LANES * padded_rows(tokens), LANES), jnp.float32)] * 2,
+        compiler_params=pltpu.CompilerParams(vmem_limit_bytes=8 * MIB),
         cost_estimate=pl.CostEstimate(
             flops=2 * 10**9 * count,
-            bytes_accessed=tokens * channels * 8 + tokens * count * tile * 4,
-            transcendentals=tokens * count * tile,
+            bytes_accessed=tokens * channels * 10 + 4 * count * tile * channels,
+            transcendentals=2 * tokens * count * tile,
         ),
         name="inner",
-    )(expanded, start, depth_kernel, w_project)
+    )(odd_col, normed, start, w_expand, depth_kernel, w_project)
 
 
 def rim_kernel(
@@ -751,20 +709,18 @@
     one, two = row_edges(odd_row, top, bottom)
     one, two = swap_pairs(one, "row", 0), swap_pairs(two, "row", 1)
     normed = half_norm_of(flat)
-    expanded = expand(normed, w_expand)
     tile = divisor(w_expand.shape[1] // 2, 256, LANES)
     count = w_expand.shape[1] // tile
-    early = 2
+    early = count // 2
     total, rim_one = inner(
-        expanded, flat, depth_kernel, w_project, rows, cols, 0, early, tile
+        odd_col, normed, flat, w_expand, depth_kernel, w_project, rows, cols, 0, early, tile
     )
-    one, two, normed, expanded, total, rim_one = lax.optimization_barrier(
-        (one, two, normed, expanded, total, rim_one)
-    )
+    one, two, normed, total, rim_one = lax.optimization_barrier((one, two, normed, total, rim_one))
     up, down, one, two = column_strips(odd_row, odd_col, normed, one, two, round_up(rows + 2, 16))
     one, two = swap_pairs(one, "col", 0), swap_pairs(two, "col", 1)
     total, rim_two = inner(
-        expanded, total, depth_kernel, w_project, rows, cols, early, count - early, tile
+        odd_col, normed, total, w_expand, depth_kernel, w_project, rows, cols, early,
+        count - early, tile
     )
 
     size = tokens // (len(plan[0]) * plan[2])

time: 57.1 us -> 58.1 us (1.018)
  starting transfers between devices: 33.1 us -> 34.6 us
  Pallas kernels: 16.6 us -> 15.6 us
    pallas_call x1 -> x0, Pallas kernels: 2.31 us -> none  [expand(): pl.pallas_call(expand_kernel, in_specs=[vmem()] * 2, out_specs=vmem(), ou...]
    ppermute x20, starting transfers between devices: 28.5 us -> 29.8 us  [swap(): lax.ppermute(slab, ('row', 'col'), [(i, i ^ mask) for i in range(devices)])]
    pallas_call x2, Pallas kernels: 5.06 us -> 6.27 us  [inner(): pl.pallas_call(functools.partial(inner_kernel, rows=rows, cols=cols, firs...]
  transfers between devices with their start and end apart: 24 -> 24, of which waited for: 5 -> 8; matrix products, arithmetic and copies ran while one was open for 0% -> 0% of each run, Pallas kernels for 15% -> 12%
where the time goes in v24:
time: 58.1 us; the launch traced here: 57.9 us
  starting transfers between devices  34.6 us (60%)
  Pallas kernels  15.6 us (27%)
  waiting for transfers between devices  6.35 us (11%)
  local copies, waits for them, and re-layouts  0.93 us (2%)
    ppermute x20, starting transfers between devices, swap(): lax.ppermute(slab, ('row', 'col'), [(i, i ^ mask) for i in range(devices)])  29.8 us
    ppermute x20, waiting for transfers between devices, swap(): lax.ppermute(slab, ('row', 'col'), [(i, i ^ mask) for i in range(devices)])  6.34 us
    pallas_call x2, Pallas kernels, inner(): pl.pallas_call(functools.partial(inner_kernel, rows=rows, cols=cols, firs...  6.27 us
    ppermute x4, starting transfers between devices, swap_pairs(): return lax.ppermute(edge, axis, pairs + [(b, a) for a, b in pairs])  4.79 us
    pallas_call x1, Pallas kernels, attend(): pl.pallas_call(functools.partial(attend_kernel, plan=plan, sets=sets, cam...  4.02 us
    pallas_call x1, Pallas kernels, rim(): pl.pallas_call(functools.partial(rim_kernel, rows=rows, cols=cols, plan=p...  2.11 us
    pallas_call x1, Pallas kernels, finish(): pl.pallas_call(functools.partial(finish_kernel, plan=plan), in_specs=[pl....  1.72 us
  transfers between devices with their start and end apart: 24, of which 8 were waited for; matrix products, arithmetic and copies ran while one was open for 0% of the time, Pallas kernels for 12%

profile of v24, /device:TPU:0, one launch (start us, length us, event | category | flops | bytes accessed | tf_op | source)
XLA Modules:
  0.0 57.9 jit_solution(6173835050404742062)
XLA Ops:
  0.0 0.9 %slice_bitcast_fusion = (f32[32,512]{1,0:T(8,128)S(1)}, f32[32,512]{1,0:T(8,128)S(1)}) fusion(f32[16,32,512]{2,1,0:T(8,128)} %param.8), kind=kLoop, calls=%fused_computation | loop fusion | bytes 262144 | tf_op jit(solution)/shard_map/squeeze | solution.py:707
  1.1 3.1 %collective-permute-start = (bf16[32,512]{1,0:T(8,128)(2,1)S(1)}, bf16[32,512]{1,0:T(8,128)(2,1)S(1)}, u32[]{:S(2)}, u32[]{:S(2)}) collective-permute-start(bf16[32,512]{1,0:T(8,128)(2,1)S(1)} %get-tuple-element.61), channel_id=1, source_target_pairs={{0,4},{8,12},{4,0},{12,8},{1,5},{9,13},{5,1},{13,9},{2,6},{10,14},... | collective-permute-start | bytes 98312 | tf_op jit(solution)/shard_map/ppermute | solution.py:572
  4.2 0.7 %collective-permute-start.1 = (bf16[32,512]{1,0:T(8,128)(2,1)S(1)}, bf16[32,512]{1,0:T(8,128)(2,1)S(1)}, u32[]{:S(2)}, u32[]{:S(2)}) collective-permute-start(bf16[32,512]{1,0:T(8,128)(2,1)S(1)} %get-tuple-element.62), channel_id=1, source_target_pairs={{4,8},{8,4},{5,9},{9,5},{6,10},{10,6},{7,11},{11,7},{20,24},{24,20... | collective-permute-start | bytes 98312 | tf_op jit(solution)/shard_map/ppermute | solution.py:572
  5.3 3.1 %inner.2 = (f32[512,512]{1,0:T(8,128)S(1)}, f32[8,96,128]{2,1,0:T(8,128)S(1)}) custom-call(s32[1]{0:T(128)} %bitcast.2.odd_col_ref, bf16[512,512]{1,0:T(8,128)(2,1)S(1)} %half_norm.1.normed_ref, f32[512,512]{1,0:T(8,128)S(1)} %bitcast.10, bf16[512,2048]{1,0:T(8,128)(2,1)S(1)} %copy-done, f32[3,3,2048]{2,1,0:T(4,128)S(1)} %copy-done.6, ...), custom_call_target="tpu_custom_call" | custom-call | flops 8000000000 | bytes 4718592 | tf_op jit(solution)/shard_map/inner/pallas_call | solution.py:236
  8.9 1.0 %collective-permute-start.3 = (bf16[32,512]{1,0:T(8,128)(2,1)S(1)}, bf16[32,512]{1,0:T(8,128)(2,1)S(1)}, u32[]{:S(2)}, u32[]{:S(2)}) collective-permute-start(bf16[32,512]{1,0:T(8,128)(2,1)S(1)} %get-tuple-element.75), channel_id=1, source_target_pairs={{1,2},{2,1},{5,6},{6,5},{9,10},{10,9},{13,14},{14,13},{17,18},{18,... | collective-permute-start | bytes 98312 | tf_op jit(solution)/shard_map/ppermute | solution.py:572
  9.9 3.1 %inner.3 = (f32[512,512]{1,0:T(8,128)S(1)}, f32[8,96,128]{2,1,0:T(8,128)S(1)}) custom-call(s32[1]{0:T(128)} %bitcast.2.odd_col_ref, bf16[512,512]{1,0:T(8,128)(2,1)S(1)} %half_norm.1.normed_ref, f32[512,512]{1,0:T(8,128)S(1)} %get-tuple-element.66.start_ref, bf16[512,2048]{1,0:T(8,128)(2,1)S(1)} %copy-done, f32[3,3,2048]{2,1,0:T(4,128)S(1)} %copy-done.6, ...), custom_call_target="tpu_custom_call" | custom-call | flops 8000000000 | bytes 4718592 | tf_op jit(solution)/shard_map/inner/pallas_call | solution.py:236
  13.0 2.1 %rim.1 = (f32[512,512]{1,0:T(8,128)S(1)}, bf16[2,32,512]{2,1,0:T(8,128)(2,1)S(1)}, bf16[2,32,512]{2,1,0:T(8,128)(2,1)S(1)}, bf16[1,32,512]{2,1,0:T(8,128)(2,1)S(...) custom-call(s32[1]{0:T(128)} %bitcast.own_ref, s32[1]{0:T(128)} %bitcast.2.odd_col_ref, ...), custom_call_target="tpu_custom_call" | custom-call | flops 805306368 | bytes 6815744 | tf_op jit(solution)/shard_map/rim/pallas_call | solution.py:346
  15.2 3.0 %collective-permute-start.6 = (bf16[6,32,512]{2,1,0:T(8,128)(2,1)S(1)}, bf16[6,32,512]{2,1,0:T(8,128)(2,1)S(1)}, u32[]{:S(2)}, u32[]{:S(2)}) collective-permute-start(bf16[6,32,512]{2,1,0:T(8,128)(2,1)S(1)} %get-tuple-element.79), channel_id=1, source_target_pairs={{0,1},{1,0},{2,3},{3,2},{4,5},{5,4},{6,7},{7,6},{8,9},{9,8},{10,11... | collective-permute-start | bytes 589832 | tf_op jit(solution)/shard_map/ppermute | solution.py:650
  18.1 3.3 %collective-permute-start.4 = (bf16[2,32,512]{2,1,0:T(8,128)(2,1)S(1)}, bf16[2,32,512]{2,1,0:T(8,128)(2,1)S(1)}, u32[]{:S(2)}, u32[]{:S(2)}) collective-permute-start(bf16[2,32,512]{2,1,0:T(8,128)(2,1)S(1)} %get-tuple-element.76), channel_id=1, source_target_pairs={{0,14},{1,15},{2,12},{3,13},{4,10},{5,11},{6,8},{7,9},{8,6},{9,7},... | collective-permute-start | bytes 196616 | tf_op jit(solution)/shard_map/ppermute | solution.py:650
  21.9 3.4 %collective-permute-start.7 = (bf16[2,32,512]{2,1,0:T(8,128)(2,1)S(1)}, bf16[2,32,512]{2,1,0:T(8,128)(2,1)S(1)}, u32[]{:S(2)}, u32[]{:S(2)}) collective-permute-start(bf16[2,32,512]{2,1,0:T(8,128)(2,1)S(1)} %get-tuple-element.80), channel_id=1, source_target_pairs={{0,10},{1,11},{2,8},{3,9},{4,14},{5,15},{6,12},{7,13},{8,2},{9,3},... | collective-permute-start | bytes 196616 | tf_op jit(solution)/shard_map/ppermute | solution.py:650
  25.3 1.5 %collective-permute-start.8 = (bf16[2,32,512]{2,1,0:T(8,128)(2,1)S(1)}, bf16[2,32,512]{2,1,0:T(8,128)(2,1)S(1)}, u32[]{:S(2)}, u32[]{:S(2)}) collective-permute-start(bf16[2,32,512]{2,1,0:T(8,128)(2,1)S(1)} %get-tuple-element.81), channel_id=1, source_target_pairs={{0,6},{1,7},{2,4},{3,5},{4,2},{5,3},{6,0},{7,1},{8,14},{9,15},{10,... | collective-permute-start | bytes 196616 | tf_op jit(solution)/shard_map/ppermute | solution.py:650
  27.3 5.3 %collective-permute-start.10 = (bf16[2,32,512]{2,1,0:T(8,128)(2,1)S(1)}, bf16[2,32,512]{2,1,0:T(8,128)(2,1)S(1)}, u32[]{:S(2)}, u32[]{:S(2)}) collective-permute-start(bf16[2,32,512]{2,1,0:T(8,128)(2,1)S(1)} %get-tuple-element.88), channel_id=1, source_target_pairs={{0,8},{1,9},{2,10},{3,11},{4,12},{5,13},{6,14},{7,15},{8,0},{9,1},... | collective-permute-start | bytes 196616 | tf_op jit(solution)/shard_map/ppermute | solution.py:650
  32.6 0.7 %collective-permute-start.11 = (bf16[2,32,512]{2,1,0:T(8,128)(2,1)S(1)}, bf16[2,32,512]{2,1,0:T(8,128)(2,1)S(1)}, u32[]{:S(2)}, u32[]{:S(2)}) collective-permute-start(bf16[2,32,512]{2,1,0:T(8,128)(2,1)S(1)} %get-tuple-element.89), channel_id=1, source_target_pairs={{0,2},{1,3},{2,0},{3,1},{4,6},{5,7},{6,4},{7,5},{8,10},{9,11},{10,... | collective-permute-start | bytes 196616 | tf_op jit(solution)/shard_map/ppermute | solution.py:650
  34.9 2.0 %collective-permute-done.11.refs_6_ = bf16[2,32,512]{2,1,0:T(8,128)(2,1)S(1)} collective-permute-done((bf16[2,32,512]{2,1,0:T(8,128)(2,1)S(1)}, bf16[2,32,512]{2,1,0:T(8,128)(2,1)S(1)}, u32[]{:S(2)}, u32[]{:S(2)}) %collective-permute-start.11) | collective-permute-done | bytes 65568 | tf_op jit(solution)/shard_map/ppermute | solution.py:650
  36.9 4.0 %attend.1 = (bf16[2,32,512]{2,1,0:T(8,128)(2,1)S(1)}, bf16[2,32,512]{2,1,0:T(8,128)(2,1)S(1)}, bf16[1,32,512]{2,1,0:T(8,128)(2,1)S(1)}, bf16[6,32,512]{2,1,0:T(8,128)(2,1)S(1)}, bf16[5,32,512]{2,1,0:T(8,128)(2,1)S(1)}) custom-call(bf16[2,32,512]{2,1,0:T(8,128)(2,1)S(1)} %collective-permute-done.4.refs_0_, ...), custom_call_target="tpu_custom_call" | custom-call | flops 1073741824 | bytes 2621440 | tf_op jit(solution)/shard_map/attend/pallas_call | solution.py:502
  41.0 1.1 %collective-permute-start.14 = (bf16[2,32,512]{2,1,0:T(8,128)(2,1)S(1)}, bf16[2,32,512]{2,1,0:T(8,128)(2,1)S(1)}, u32[]{:S(2)}, u32[]{:S(2)}) collective-permute-start(bf16[2,32,512]{2,1,0:T(8,128)(2,1)S(1)} %get-tuple-element.91), channel_id=1, source_target_pairs={{0,14},{1,15},{2,12},{3,13},{4,10},{5,11},{6,8},{7,9},{8,6},{9,7},... | collective-permute-start | bytes 196616 | tf_op jit(solution)/shard_map/ppermute | solution.py:650
  42.1 2.9 %collective-permute-start.15 = (bf16[2,32,512]{2,1,0:T(8,128)(2,1)S(1)}, bf16[2,32,512]{2,1,0:T(8,128)(2,1)S(1)}, u32[]{:S(2)}, u32[]{:S(2)}) collective-permute-start(bf16[2,32,512]{2,1,0:T(8,128)(2,1)S(1)} %get-tuple-element.92), channel_id=1, source_target_pairs={{0,12},{1,13},{2,14},{3,15},{4,8},{5,9},{6,10},{7,11},{8,4},{9,5},... | collective-permute-start | bytes 196616 | tf_op jit(solution)/shard_map/ppermute | solution.py:650
  45.2 2.3 %collective-permute-start.18 = (bf16[2,32,512]{2,1,0:T(8,128)(2,1)S(1)}, bf16[2,32,512]{2,1,0:T(8,128)(2,1)S(1)}, u32[]{:S(2)}, u32[]{:S(2)}) collective-permute-start(bf16[2,32,512]{2,1,0:T(8,128)(2,1)S(1)} %get-tuple-element.96), channel_id=1, source_target_pairs={{0,6},{1,7},{2,4},{3,5},{4,2},{5,3},{6,0},{7,1},{8,14},{9,15},{10,... | collective-permute-start | bytes 196616 | tf_op jit(solution)/shard_map/ppermute | solution.py:650
  48.0 0.8 %collective-permute-done.14.refs_0_ = bf16[2,32,512]{2,1,0:T(8,128)(2,1)S(1)} collective-permute-done((bf16[2,32,512]{2,1,0:T(8,128)(2,1)S(1)}, bf16[2,32,512]{2,1,0:T(8,128)(2,1)S(1)}, u32[]{:S(2)}, u32[]{:S(2)}) %collective-permute-start.14) | collective-permute-done | bytes 65568 | tf_op jit(solution)/shard_map/ppermute | solution.py:650
  48.8 2.2 %collective-permute-start.20 = (bf16[2,32,512]{2,1,0:T(8,128)(2,1)S(1)}, bf16[2,32,512]{2,1,0:T(8,128)(2,1)S(1)}, u32[]{:S(2)}, u32[]{:S(2)}) collective-permute-start(bf16[2,32,512]{2,1,0:T(8,128)(2,1)S(1)} %get-tuple-element.103), channel_id=1, source_target_pairs={{0,8},{1,9},{2,10},{3,11},{4,12},{5,13},{6,14},{7,15},{8,0},{9,1},... | collective-permute-start | bytes 196616 | tf_op jit(solution)/shard_map/ppermute | solution.py:650
  51.0 1.3 %collective-permute-start.21 = (bf16[2,32,512]{2,1,0:T(8,128)(2,1)S(1)}, bf16[2,32,512]{2,1,0:T(8,128)(2,1)S(1)}, u32[]{:S(2)}, u32[]{:S(2)}) collective-permute-start(bf16[2,32,512]{2,1,0:T(8,128)(2,1)S(1)} %get-tuple-element.104), channel_id=1, source_target_pairs={{0,2},{1,3},{2,0},{3,1},{4,6},{5,7},{6,4},{7,5},{8,10},{9,11},{10,... | collective-permute-start | bytes 196616 | tf_op jit(solution)/shard_map/ppermute | solution.py:650
  52.3 0.8 %collective-permute-done.17.refs_2_ = bf16[2,32,512]{2,1,0:T(8,128)(2,1)S(1)} collective-permute-done((bf16[2,32,512]{2,1,0:T(8,128)(2,1)S(1)}, bf16[2,32,512]{2,1,0:T(8,128)(2,1)S(1)}, u32[]{:S(2)}, u32[]{:S(2)}) %collective-permute-start.17) | collective-permute-done | bytes 65568 | tf_op jit(solution)/shard_map/ppermute | solution.py:650
  53.2 1.4 %collective-permute-done.19.refs_4_ = bf16[2,32,512]{2,1,0:T(8,128)(2,1)S(1)} collective-permute-done((bf16[2,32,512]{2,1,0:T(8,128)(2,1)S(1)}, bf16[2,32,512]{2,1,0:T(8,128)(2,1)S(1)}, u32[]{:S(2)}, u32[]{:S(2)}) %collective-permute-start.19) | collective-permute-done | bytes 65568 | tf_op jit(solution)/shard_map/ppermute | solution.py:650
  56.0 1.7 %finish.1 = f32[512,512]{1,0:T(8,128)} custom-call(s32[1]{0:T(128)} %bitcast.own_ref, bf16[2,32,512]{2,1,0:T(8,128)(2,1)S(1)} %collective-permute-done.14.refs_0_, bf16[2,32,512]{2,1,0:T(8,128)(2,1)S(1)} %collective-permute-done.15.refs_1_, bf16[2,32,512]{2,1,0:T(8,128)(2,1)S(1)} %collective-permute-done.17.refs_2_, ...), custom_call_target="tpu_custom_call" | custom-call | tf_op jit(solution)/shard_map/finish/pallas_call | solution.py:555
  (52 shorter events, 5.7 us)
Async XLA Ops:
  1.1 7.3 %collective-permute-start = (bf16[32,512]{1,0:T(8,128)(2,1)S(1)}, bf16[32,512]{1,0:T(8,128)(2,1)S(1)}, u32[]{:S(2)}, u32[]{:S(2)}) collective-permute-start(bf16[32,512]{1,0:T(8,128)(2,1)S(1)} %get-tuple-element.61), channel_id=1, source_target_pairs={{0,4},{8,12},{4,0},{12,8},{1,5},{9,13},{5,1},{13,9},{2,6},{10,14},... | collective-permute-start | bytes 98312 | tf_op jit(solution)/shard_map/ppermute | solution.py:572
  4.2 4.2 %collective-permute-start.1 = (bf16[32,512]{1,0:T(8,128)(2,1)S(1)}, bf16[32,512]{1,0:T(8,128)(2,1)S(1)}, u32[]{:S(2)}, u32[]{:S(2)}) collective-permute-start(bf16[32,512]{1,0:T(8,128)(2,1)S(1)} %get-tuple-element.62), channel_id=1, source_target_pairs={{4,8},{8,4},{5,9},{9,5},{6,10},{10,6},{7,11},{11,7},{20,24},{24,20... | collective-permute-start | bytes 98312 | tf_op jit(solution)/shard_map/ppermute | solution.py:572
  8.8 4.2 %collective-permute-start.2 = (bf16[32,512]{1,0:T(8,128)(2,1)S(1)}, bf16[32,512]{1,0:T(8,128)(2,1)S(1)}, u32[]{:S(2)}, u32[]{:S(2)}) collective-permute-start(bf16[32,512]{1,0:T(8,128)(2,1)S(1)} %get-tuple-element.74), channel_id=1, source_target_pairs={{0,1},{2,3},{1,0},{3,2},{4,5},{6,7},{5,4},{7,6},{8,9},{10,11},{9,8... | collective-permute-start | bytes 98312 | tf_op jit(solution)/shard_map/ppermute | solution.py:572
  8.9 4.1 %collective-permute-start.3 = (bf16[32,512]{1,0:T(8,128)(2,1)S(1)}, bf16[32,512]{1,0:T(8,128)(2,1)S(1)}, u32[]{:S(2)}, u32[]{:S(2)}) collective-permute-start(bf16[32,512]{1,0:T(8,128)(2,1)S(1)} %get-tuple-element.75), channel_id=1, source_target_pairs={{1,2},{2,1},{5,6},{6,5},{9,10},{10,9},{13,14},{14,13},{17,18},{18,... | collective-permute-start | bytes 98312 | tf_op jit(solution)/shard_map/ppermute | solution.py:572
  15.2 6.8 %collective-permute-start.6 = (bf16[6,32,512]{2,1,0:T(8,128)(2,1)S(1)}, bf16[6,32,512]{2,1,0:T(8,128)(2,1)S(1)}, u32[]{:S(2)}, u32[]{:S(2)}) collective-permute-start(bf16[6,32,512]{2,1,0:T(8,128)(2,1)S(1)} %get-tuple-element.79), channel_id=1, source_target_pairs={{0,1},{1,0},{2,3},{3,2},{4,5},{5,4},{6,7},{7,6},{8,9},{9,8},{10,11... | collective-permute-start | bytes 589832 | tf_op jit(solution)/shard_map/ppermute | solution.py:650
  18.1 9.2 %collective-permute-start.4 = (bf16[2,32,512]{2,1,0:T(8,128)(2,1)S(1)}, bf16[2,32,512]{2,1,0:T(8,128)(2,1)S(1)}, u32[]{:S(2)}, u32[]{:S(2)}) collective-permute-start(bf16[2,32,512]{2,1,0:T(8,128)(2,1)S(1)} %get-tuple-element.76), channel_id=1, source_target_pairs={{0,14},{1,15},{2,12},{3,13},{4,10},{5,11},{6,8},{7,9},{8,6},{9,7},... | collective-permute-start | bytes 196616 | tf_op jit(solution)/shard_map/ppermute | solution.py:650
  21.4 11.3 %collective-permute-start.5 = (bf16[2,32,512]{2,1,0:T(8,128)(2,1)S(1)}, bf16[2,32,512]{2,1,0:T(8,128)(2,1)S(1)}, u32[]{:S(2)}, u32[]{:S(2)}) collective-permute-start(bf16[2,32,512]{2,1,0:T(8,128)(2,1)S(1)} %get-tuple-element.77), channel_id=1, source_target_pairs={{0,12},{1,13},{2,14},{3,15},{4,8},{5,9},{6,10},{7,11},{8,4},{9,5},... | collective-permute-start | bytes 196616 | tf_op jit(solution)/shard_map/ppermute | solution.py:650
  21.9 11.4 %collective-permute-start.7 = (bf16[2,32,512]{2,1,0:T(8,128)(2,1)S(1)}, bf16[2,32,512]{2,1,0:T(8,128)(2,1)S(1)}, u32[]{:S(2)}, u32[]{:S(2)}) collective-permute-start(bf16[2,32,512]{2,1,0:T(8,128)(2,1)S(1)} %get-tuple-element.80), channel_id=1, source_target_pairs={{0,10},{1,11},{2,8},{3,9},{4,14},{5,15},{6,12},{7,13},{8,2},{9,3},... | collective-permute-start | bytes 196616 | tf_op jit(solution)/shard_map/ppermute | solution.py:650
  25.3 8.1 %collective-permute-start.8 = (bf16[2,32,512]{2,1,0:T(8,128)(2,1)S(1)}, bf16[2,32,512]{2,1,0:T(8,128)(2,1)S(1)}, u32[]{:S(2)}, u32[]{:S(2)}) collective-permute-start(bf16[2,32,512]{2,1,0:T(8,128)(2,1)S(1)} %get-tuple-element.81), channel_id=1, source_target_pairs={{0,6},{1,7},{2,4},{3,5},{4,2},{5,3},{6,0},{7,1},{8,14},{9,15},{10,... | collective-permute-start | bytes 196616 | tf_op jit(solution)/shard_map/ppermute | solution.py:650
  26.8 6.6 %collective-permute-start.9 = (bf16[2,32,512]{2,1,0:T(8,128)(2,1)S(1)}, bf16[2,32,512]{2,1,0:T(8,128)(2,1)S(1)}, u32[]{:S(2)}, u32[]{:S(2)}) collective-permute-start(bf16[2,32,512]{2,1,0:T(8,128)(2,1)S(1)} %get-tuple-element.82), channel_id=1, source_target_pairs={{0,4},{1,5},{2,6},{3,7},{4,0},{5,1},{6,2},{7,3},{8,12},{9,13},{10,... | collective-permute-start | bytes 196616 | tf_op jit(solution)/shard_map/ppermute | solution.py:650
  27.3 7.6 %collective-permute-start.10 = (bf16[2,32,512]{2,1,0:T(8,128)(2,1)S(1)}, bf16[2,32,512]{2,1,0:T(8,128)(2,1)S(1)}, u32[]{:S(2)}, u32[]{:S(2)}) collective-permute-start(bf16[2,32,512]{2,1,0:T(8,128)(2,1)S(1)} %get-tuple-element.88), channel_id=1, source_target_pairs={{0,8},{1,9},{2,10},{3,11},{4,12},{5,13},{6,14},{7,15},{8,0},{9,1},... | collective-permute-start | bytes 196616 | tf_op jit(solution)/shard_map/ppermute | solution.py:650
  32.6 4.3 %collective-permute-start.11 = (bf16[2,32,512]{2,1,0:T(8,128)(2,1)S(1)}, bf16[2,32,512]{2,1,0:T(8,128)(2,1)S(1)}, u32[]{:S(2)}, u32[]{:S(2)}) collective-permute-start(bf16[2,32,512]{2,1,0:T(8,128)(2,1)S(1)} %get-tuple-element.89), channel_id=1, source_target_pairs={{0,2},{1,3},{2,0},{3,1},{4,6},{5,7},{6,4},{7,5},{8,10},{9,11},{10,... | collective-permute-start | bytes 196616 | tf_op jit(solution)/shard_map/ppermute | solution.py:650
  33.4 3.5 %collective-permute-start.12 = (bf16[2,32,512]{2,1,0:T(8,128)(2,1)S(1)}, bf16[2,32,512]{2,1,0:T(8,128)(2,1)S(1)}, u32[]{:S(2)}, u32[]{:S(2)}) collective-permute-start(bf16[2,32,512]{2,1,0:T(8,128)(2,1)S(1)} %collective-permute-done.4.refs_0_), channel_id=1, source_target_pairs={{0,1},{1,0},{2,3},{3,2},{4,5},{5,4},{6,7},{7,6},{8,9},{9,8},{10,11... | collective-permute-start | bytes 196616 | tf_op jit(solution)/shard_map/ppermute | solution.py:650
  33.5 3.5 %collective-permute-start.13 = (bf16[2,32,512]{2,1,0:T(8,128)(2,1)S(1)}, bf16[2,32,512]{2,1,0:T(8,128)(2,1)S(1)}, u32[]{:S(2)}, u32[]{:S(2)}) collective-permute-start(bf16[2,32,512]{2,1,0:T(8,128)(2,1)S(1)} %collective-permute-done.5.refs_1_), channel_id=1, source_target_pairs={{0,1},{1,0},{2,3},{3,2},{4,5},{5,4},{6,7},{7,6},{8,9},{9,8},{10,11... | collective-permute-start | bytes 196616 | tf_op jit(solution)/shard_map/ppermute | solution.py:650
  40.9 4.1 %collective-permute-start.16 = (bf16[6,32,512]{2,1,0:T(8,128)(2,1)S(1)}, bf16[6,32,512]{2,1,0:T(8,128)(2,1)S(1)}, u32[]{:S(2)}, u32[]{:S(2)}) collective-permute-start(bf16[6,32,512]{2,1,0:T(8,128)(2,1)S(1)} %get-tuple-element.94), channel_id=1, source_target_pairs={{0,1},{1,0},{2,3},{3,2},{4,5},{5,4},{6,7},{7,6},{8,9},{9,8},{10,11... | collective-permute-start | bytes 589832 | tf_op jit(solution)/shard_map/ppermute | solution.py:650
  41.0 7.8 %collective-permute-start.14 = (bf16[2,32,512]{2,1,0:T(8,128)(2,1)S(1)}, bf16[2,32,512]{2,1,0:T(8,128)(2,1)S(1)}, u32[]{:S(2)}, u32[]{:S(2)}) collective-permute-start(bf16[2,32,512]{2,1,0:T(8,128)(2,1)S(1)} %get-tuple-element.91), channel_id=1, source_target_pairs={{0,14},{1,15},{2,12},{3,13},{4,10},{5,11},{6,8},{7,9},{8,6},{9,7},... | collective-permute-start | bytes 196616 | tf_op jit(solution)/shard_map/ppermute | solution.py:650
  42.1 8.9 %collective-permute-start.15 = (bf16[2,32,512]{2,1,0:T(8,128)(2,1)S(1)}, bf16[2,32,512]{2,1,0:T(8,128)(2,1)S(1)}, u32[]{:S(2)}, u32[]{:S(2)}) collective-permute-start(bf16[2,32,512]{2,1,0:T(8,128)(2,1)S(1)} %get-tuple-element.92), channel_id=1, source_target_pairs={{0,12},{1,13},{2,14},{3,15},{4,8},{5,9},{6,10},{7,11},{8,4},{9,5},... | collective-permute-start | bytes 196616 | tf_op jit(solution)/shard_map/ppermute | solution.py:650
  45.1 8.1 %collective-permute-start.17 = (bf16[2,32,512]{2,1,0:T(8,128)(2,1)S(1)}, bf16[2,32,512]{2,1,0:T(8,128)(2,1)S(1)}, u32[]{:S(2)}, u32[]{:S(2)}) collective-permute-start(bf16[2,32,512]{2,1,0:T(8,128)(2,1)S(1)} %get-tuple-element.95), channel_id=1, source_target_pairs={{0,10},{1,11},{2,8},{3,9},{4,14},{5,15},{6,12},{7,13},{8,2},{9,3},... | collective-permute-start | bytes 196616 | tf_op jit(solution)/shard_map/ppermute | solution.py:650
  45.2 8.0 %collective-permute-start.18 = (bf16[2,32,512]{2,1,0:T(8,128)(2,1)S(1)}, bf16[2,32,512]{2,1,0:T(8,128)(2,1)S(1)}, u32[]{:S(2)}, u32[]{:S(2)}) collective-permute-start(bf16[2,32,512]{2,1,0:T(8,128)(2,1)S(1)} %get-tuple-element.96), channel_id=1, source_target_pairs={{0,6},{1,7},{2,4},{3,5},{4,2},{5,3},{6,0},{7,1},{8,14},{9,15},{10,... | collective-permute-start | bytes 196616 | tf_op jit(solution)/shard_map/ppermute | solution.py:650
  47.5 7.1 %collective-permute-start.19 = (bf16[2,32,512]{2,1,0:T(8,128)(2,1)S(1)}, bf16[2,32,512]{2,1,0:T(8,128)(2,1)S(1)}, u32[]{:S(2)}, u32[]{:S(2)}) collective-permute-start(bf16[2,32,512]{2,1,0:T(8,128)(2,1)S(1)} %get-tuple-element.97), channel_id=1, source_target_pairs={{0,4},{1,5},{2,6},{3,7},{4,0},{5,1},{6,2},{7,3},{8,12},{9,13},{10,... | collective-permute-start | bytes 196616 | tf_op jit(solution)/shard_map/ppermute | solution.py:650
  48.8 6.3 %collective-permute-start.20 = (bf16[2,32,512]{2,1,0:T(8,128)(2,1)S(1)}, bf16[2,32,512]{2,1,0:T(8,128)(2,1)S(1)}, u32[]{:S(2)}, u32[]{:S(2)}) collective-permute-start(bf16[2,32,512]{2,1,0:T(8,128)(2,1)S(1)} %get-tuple-element.103), channel_id=1, source_target_pairs={{0,8},{1,9},{2,10},{3,11},{4,12},{5,13},{6,14},{7,15},{8,0},{9,1},... | collective-permute-start | bytes 196616 | tf_op jit(solution)/shard_map/ppermute | solution.py:650
  51.0 4.3 %collective-permute-start.21 = (bf16[2,32,512]{2,1,0:T(8,128)(2,1)S(1)}, bf16[2,32,512]{2,1,0:T(8,128)(2,1)S(1)}, u32[]{:S(2)}, u32[]{:S(2)}) collective-permute-start(bf16[2,32,512]{2,1,0:T(8,128)(2,1)S(1)} %get-tuple-element.104), channel_id=1, source_target_pairs={{0,2},{1,3},{2,0},{3,1},{4,6},{5,7},{6,4},{7,5},{8,10},{9,11},{10,... | collective-permute-start | bytes 196616 | tf_op jit(solution)/shard_map/ppermute | solution.py:650
  54.6 1.3 %collective-permute-start.22 = (bf16[2,32,512]{2,1,0:T(8,128)(2,1)S(1)}, bf16[2,32,512]{2,1,0:T(8,128)(2,1)S(1)}, u32[]{:S(2)}, u32[]{:S(2)}) collective-permute-start(bf16[2,32,512]{2,1,0:T(8,128)(2,1)S(1)} %collective-permute-done.14.refs_0_), channel_id=1, source_target_pairs={{0,1},{1,0},{2,3},{3,2},{4,5},{5,4},{6,7},{7,6},{8,9},{9,8},{10,11... | collective-permute-start | bytes 196616 | tf_op jit(solution)/shard_map/ppermute | solution.py:650
  54.6 1.4 %collective-permute-start.23 = (bf16[2,32,512]{2,1,0:T(8,128)(2,1)S(1)}, bf16[2,32,512]{2,1,0:T(8,128)(2,1)S(1)}, u32[]{:S(2)}, u32[]{:S(2)}) collective-permute-start(bf16[2,32,512]{2,1,0:T(8,128)(2,1)S(1)} %collective-permute-done.15.refs_1_), channel_id=1, source_target_pairs={{0,1},{1,0},{2,3},{3,2},{4,5},{5,4},{6,7},{7,6},{8,9},{9,8},{10,11... | collective-permute-start | bytes 196616 | tf_op jit(solution)/shard_map/ppermute | solution.py:650
  (8 other events, 84.7 us)

commit v25 on v24

--- a/solution.py
+++ b/solution.py
@@ -111,7 +111,7 @@
 
 
 def strips_kernel(
-    odd_row_ref, odd_col_ref, normed_ref, row_one_ref, row_two_ref, up_ref, down_ref, one_ref, two_ref
+    odd_row_ref, odd_col_ref, row_two_ref, row_one_ref, normed_ref, up_ref, down_ref, one_ref, two_ref
 ):
     tokens = normed_ref.shape[0]
     cols = up_ref.shape[0]
@@ -145,7 +145,7 @@
         out_shape=[jax.ShapeDtypeStruct(shape, jnp.bfloat16) for shape in shapes],
         compiler_params=pltpu.CompilerParams(vmem_limit_bytes=4 * MIB),
         name="column_strips",
-    )(odd_row, odd_col, normed, row_one, row_two)
+    )(odd_row, odd_col, row_two, row_one, normed)
 
 
 def padded_rows(tokens):
@@ -707,7 +707,7 @@
         (own, odd_row, odd_col, field[0], field[rows - 1])
     )
     one, two = row_edges(odd_row, top, bottom)
-    one, two = swap_pairs(one, "row", 0), swap_pairs(two, "row", 1)
+    two, one = swap_pairs(two, "row", 1), swap_pairs(one, "row", 0)
     normed = half_norm_of(flat)
     tile = divisor(w_expand.shape[1] // 2, 256, LANES)
     count = w_expand.shape[1] // tile
@@ -715,7 +715,7 @@
     total, rim_one = inner(
         odd_col, normed, flat, w_expand, depth_kernel, w_project, rows, cols, 0, early, tile
     )
-    one, two, normed, total, rim_one = lax.optimization_barrier((one, two, normed, total, rim_one))
+    two, one, normed, total, rim_one = lax.optimization_barrier((two, one, normed, total, rim_one))
     up, down, one, two = column_strips(odd_row, odd_col, normed, one, two, round_up(rows + 2, 16))
     one, two = swap_pairs(one, "col", 0), swap_pairs(two, "col", 1)
     total, rim_two = inner(

time: 58.1 us -> 58 us (level)
  starting transfers between devices: 34.6 us -> 34 us
    ppermute x20, starting transfers between devices: 29.8 us -> 26.1 us  [swap(): lax.ppermute(slab, ('row', 'col'), [(i, i ^ mask) for i in range(devices)])]
    ppermute x4, starting transfers between devices: 4.79 us -> 7.88 us  [swap_pairs(): return lax.ppermute(edge, axis, pairs + [(b, a) for a, b in pairs])]
  transfers between devices with their start and end apart: 24 -> 24, of which waited for: 8 -> 9; matrix products, arithmetic and copies ran while one was open for 0% -> 0% of each run, Pallas kernels for 12% -> 12%
where the time goes in v25:
time: 58 us; the launch traced here: 57.8 us
  starting transfers between devices  34 us (59%)
  Pallas kernels  15.6 us (27%)
  waiting for transfers between devices  6.83 us (12%)
  local copies, waits for them, and re-layouts  0.93 us (2%)
    ppermute x20, starting transfers between devices, swap(): lax.ppermute(slab, ('row', 'col'), [(i, i ^ mask) for i in range(devices)])  26.1 us
    ppermute x4, starting transfers between devices, swap_pairs(): return lax.ppermute(edge, axis, pairs + [(b, a) for a, b in pairs])  7.88 us
    ppermute x20, waiting for transfers between devices, swap(): lax.ppermute(slab, ('row', 'col'), [(i, i ^ mask) for i in range(devices)])  6.82 us
    pallas_call x2, Pallas kernels, inner(): pl.pallas_call(functools.partial(inner_kernel, rows=rows, cols=cols, firs...  6.27 us
    pallas_call x1, Pallas kernels, attend(): pl.pallas_call(functools.partial(attend_kernel, plan=plan, sets=sets, cam...  4.01 us
    pallas_call x1, Pallas kernels, rim(): pl.pallas_call(functools.partial(rim_kernel, rows=rows, cols=cols, plan=p...  2.12 us
    pallas_call x1, Pallas kernels, finish(): pl.pallas_call(functools.partial(finish_kernel, plan=plan), in_specs=[pl....  1.72 us
  transfers between devices with their start and end apart: 24, of which 9 were waited for; matrix products, arithmetic and copies ran while one was open for 0% of the time, Pallas kernels for 12%

profile of v25, /device:TPU:0, one launch (start us, length us, event | category | flops | bytes accessed | tf_op | source)
XLA Modules:
  0.0 57.8 jit_solution(10423373433812774590)
XLA Ops:
  0.0 0.9 %slice_bitcast_fusion = (f32[32,512]{1,0:T(8,128)S(1)}, f32[32,512]{1,0:T(8,128)S(1)}) fusion(f32[16,32,512]{2,1,0:T(8,128)} %param.8), kind=kLoop, calls=%fused_computation | loop fusion | bytes 262144 | tf_op jit(solution)/shard_map/squeeze | solution.py:707
  1.1 0.8 %collective-permute-start = (bf16[32,512]{1,0:T(8,128)(2,1)S(1)}, bf16[32,512]{1,0:T(8,128)(2,1)S(1)}, u32[]{:S(2)}, u32[]{:S(2)}) collective-permute-start(bf16[32,512]{1,0:T(8,128)(2,1)S(1)} %get-tuple-element.61), channel_id=1, source_target_pairs={{4,8},{8,4},{5,9},{9,5},{6,10},{10,6},{7,11},{11,7},{20,24},{24,20... | collective-permute-start | bytes 98312 | tf_op jit(solution)/shard_map/ppermute | solution.py:572
  1.9 6.0 %collective-permute-start.1 = (bf16[32,512]{1,0:T(8,128)(2,1)S(1)}, bf16[32,512]{1,0:T(8,128)(2,1)S(1)}, u32[]{:S(2)}, u32[]{:S(2)}) collective-permute-start(bf16[32,512]{1,0:T(8,128)(2,1)S(1)} %get-tuple-element.62), channel_id=1, source_target_pairs={{0,4},{8,12},{4,0},{12,8},{1,5},{9,13},{5,1},{13,9},{2,6},{10,14},... | collective-permute-start | bytes 98312 | tf_op jit(solution)/shard_map/ppermute | solution.py:572
  8.4 3.1 %inner.2 = (f32[512,512]{1,0:T(8,128)S(1)}, f32[8,96,128]{2,1,0:T(8,128)S(1)}) custom-call(s32[1]{0:T(128)} %bitcast.2.odd_col_ref, bf16[512,512]{1,0:T(8,128)(2,1)S(1)} %half_norm.1.normed_ref, f32[512,512]{1,0:T(8,128)S(1)} %bitcast.10, bf16[512,2048]{1,0:T(8,128)(2,1)S(1)} %copy-done, f32[3,3,2048]{2,1,0:T(4,128)S(1)} %copy-done.6, ...), custom_call_target="tpu_custom_call" | custom-call | flops 8000000000 | bytes 4718592 | tf_op jit(solution)/shard_map/inner/pallas_call | solution.py:236
  12.0 1.0 %collective-permute-start.3 = (bf16[32,512]{1,0:T(8,128)(2,1)S(1)}, bf16[32,512]{1,0:T(8,128)(2,1)S(1)}, u32[]{:S(2)}, u32[]{:S(2)}) collective-permute-start(bf16[32,512]{1,0:T(8,128)(2,1)S(1)} %get-tuple-element.75), channel_id=1, source_target_pairs={{1,2},{2,1},{5,6},{6,5},{9,10},{10,9},{13,14},{14,13},{17,18},{18,... | collective-permute-start | bytes 98312 | tf_op jit(solution)/shard_map/ppermute | solution.py:572
  12.9 3.1 %inner.3 = (f32[512,512]{1,0:T(8,128)S(1)}, f32[8,96,128]{2,1,0:T(8,128)S(1)}) custom-call(s32[1]{0:T(128)} %bitcast.2.odd_col_ref, bf16[512,512]{1,0:T(8,128)(2,1)S(1)} %half_norm.1.normed_ref, f32[512,512]{1,0:T(8,128)S(1)} %get-tuple-element.66.start_ref, bf16[512,2048]{1,0:T(8,128)(2,1)S(1)} %copy-done, f32[3,3,2048]{2,1,0:T(4,128)S(1)} %copy-done.6, ...), custom_call_target="tpu_custom_call" | custom-call | flops 8000000000 | bytes 4718592 | tf_op jit(solution)/shard_map/inner/pallas_call | solution.py:236
  16.1 2.1 %rim.1 = (f32[512,512]{1,0:T(8,128)S(1)}, bf16[2,32,512]{2,1,0:T(8,128)(2,1)S(1)}, bf16[2,32,512]{2,1,0:T(8,128)(2,1)S(1)}, bf16[1,32,512]{2,1,0:T(8,128)(2,1)S(...) custom-call(s32[1]{0:T(128)} %bitcast.own_ref, s32[1]{0:T(128)} %bitcast.2.odd_col_ref, ...), custom_call_target="tpu_custom_call" | custom-call | flops 805306368 | bytes 6815744 | tf_op jit(solution)/shard_map/rim/pallas_call | solution.py:346
  18.3 2.9 %collective-permute-start.6 = (bf16[6,32,512]{2,1,0:T(8,128)(2,1)S(1)}, bf16[6,32,512]{2,1,0:T(8,128)(2,1)S(1)}, u32[]{:S(2)}, u32[]{:S(2)}) collective-permute-start(bf16[6,32,512]{2,1,0:T(8,128)(2,1)S(1)} %get-tuple-element.79), channel_id=1, source_target_pairs={{0,1},{1,0},{2,3},{3,2},{4,5},{5,4},{6,7},{7,6},{8,9},{9,8},{10,11... | collective-permute-start | bytes 589832 | tf_op jit(solution)/shard_map/ppermute | solution.py:650
  21.2 1.3 %collective-permute-start.4 = (bf16[2,32,512]{2,1,0:T(8,128)(2,1)S(1)}, bf16[2,32,512]{2,1,0:T(8,128)(2,1)S(1)}, u32[]{:S(2)}, u32[]{:S(2)}) collective-permute-start(bf16[2,32,512]{2,1,0:T(8,128)(2,1)S(1)} %get-tuple-element.76), channel_id=1, source_target_pairs={{0,14},{1,15},{2,12},{3,13},{4,10},{5,11},{6,8},{7,9},{8,6},{9,7},... | collective-permute-start | bytes 196616 | tf_op jit(solution)/shard_map/ppermute | solution.py:650
  22.5 2.5 %collective-permute-start.5 = (bf16[2,32,512]{2,1,0:T(8,128)(2,1)S(1)}, bf16[2,32,512]{2,1,0:T(8,128)(2,1)S(1)}, u32[]{:S(2)}, u32[]{:S(2)}) collective-permute-start(bf16[2,32,512]{2,1,0:T(8,128)(2,1)S(1)} %get-tuple-element.77), channel_id=1, source_target_pairs={{0,12},{1,13},{2,14},{3,15},{4,8},{5,9},{6,10},{7,11},{8,4},{9,5},... | collective-permute-start | bytes 196616 | tf_op jit(solution)/shard_map/ppermute | solution.py:650
  25.1 2.8 %collective-permute-start.8 = (bf16[2,32,512]{2,1,0:T(8,128)(2,1)S(1)}, bf16[2,32,512]{2,1,0:T(8,128)(2,1)S(1)}, u32[]{:S(2)}, u32[]{:S(2)}) collective-permute-start(bf16[2,32,512]{2,1,0:T(8,128)(2,1)S(1)} %get-tuple-element.81), channel_id=1, source_target_pairs={{0,6},{1,7},{2,4},{3,5},{4,2},{5,3},{6,0},{7,1},{8,14},{9,15},{10,... | collective-permute-start | bytes 196616 | tf_op jit(solution)/shard_map/ppermute | solution.py:650
  28.8 2.2 %collective-permute-start.10 = (bf16[2,32,512]{2,1,0:T(8,128)(2,1)S(1)}, bf16[2,32,512]{2,1,0:T(8,128)(2,1)S(1)}, u32[]{:S(2)}, u32[]{:S(2)}) collective-permute-start(bf16[2,32,512]{2,1,0:T(8,128)(2,1)S(1)} %get-tuple-element.88), channel_id=1, source_target_pairs={{0,8},{1,9},{2,10},{3,11},{4,12},{5,13},{6,14},{7,15},{8,0},{9,1},... | collective-permute-start | bytes 196616 | tf_op jit(solution)/shard_map/ppermute | solution.py:650
  31.0 1.5 %collective-permute-start.11 = (bf16[2,32,512]{2,1,0:T(8,128)(2,1)S(1)}, bf16[2,32,512]{2,1,0:T(8,128)(2,1)S(1)}, u32[]{:S(2)}, u32[]{:S(2)}) collective-permute-start(bf16[2,32,512]{2,1,0:T(8,128)(2,1)S(1)} %get-tuple-element.89), channel_id=1, source_target_pairs={{0,2},{1,3},{2,0},{3,1},{4,6},{5,7},{6,4},{7,5},{8,10},{9,11},{10,... | collective-permute-start | bytes 196616 | tf_op jit(solution)/shard_map/ppermute | solution.py:650
  32.4 1.8 %collective-permute-done.7.refs_0_.refs_1_.refs_2_.refs_5_.refs_6_.refs_8_.refs_9_ = bf16[2,32,512]{2,1,0:T(8,128)(2,1)S(1)} collective-permute-done((bf16[2,32,512]{2,1,0:T(8,128)(2,1)S(1)}, bf16[2,32,512]{2,1,0:T(8,128)(2,1)S(1)}, u32[]{:S(2)}, u32[]{:S(2)}) %collective-permute-start.7) | collective-permute-done | bytes 65568 | tf_op jit(solution)/shard_map/ppermute | solution.py:650
  35.7 4.0 %attend.1 = (bf16[2,32,512]{2,1,0:T(8,128)(2,1)S(1)}, bf16[2,32,512]{2,1,0:T(8,128)(2,1)S(1)}, bf16[1,32,512]{2,1,0:T(8,128)(2,1)S(1)}, bf16[6,32,512]{2,1,0:T(8,128)(2,1)S(1)}, bf16[5,32,512]{2,1,0:T(8,128)(2,1)S(1)}) custom-call(bf16[2,32,512]{2,1,0:T(8,128)(2,1)S(1)} %collective-permute-done.4.refs_0_, ...), custom_call_target="tpu_custom_call" | custom-call | flops 1073741824 | bytes 2621440 | tf_op jit(solution)/shard_map/attend/pallas_call | solution.py:502
  40.1 2.9 %collective-permute-start.14 = (bf16[2,32,512]{2,1,0:T(8,128)(2,1)S(1)}, bf16[2,32,512]{2,1,0:T(8,128)(2,1)S(1)}, u32[]{:S(2)}, u32[]{:S(2)}) collective-permute-start(bf16[2,32,512]{2,1,0:T(8,128)(2,1)S(1)} %get-tuple-element.91), channel_id=1, source_target_pairs={{0,14},{1,15},{2,12},{3,13},{4,10},{5,11},{6,8},{7,9},{8,6},{9,7},... | collective-permute-start | bytes 196616 | tf_op jit(solution)/shard_map/ppermute | solution.py:650
  43.1 1.6 %collective-permute-start.15 = (bf16[2,32,512]{2,1,0:T(8,128)(2,1)S(1)}, bf16[2,32,512]{2,1,0:T(8,128)(2,1)S(1)}, u32[]{:S(2)}, u32[]{:S(2)}) collective-permute-start(bf16[2,32,512]{2,1,0:T(8,128)(2,1)S(1)} %get-tuple-element.92), channel_id=1, source_target_pairs={{0,12},{1,13},{2,14},{3,15},{4,8},{5,9},{6,10},{7,11},{8,4},{9,5},... | collective-permute-start | bytes 196616 | tf_op jit(solution)/shard_map/ppermute | solution.py:650
  44.8 3.7 %collective-permute-start.18 = (bf16[2,32,512]{2,1,0:T(8,128)(2,1)S(1)}, bf16[2,32,512]{2,1,0:T(8,128)(2,1)S(1)}, u32[]{:S(2)}, u32[]{:S(2)}) collective-permute-start(bf16[2,32,512]{2,1,0:T(8,128)(2,1)S(1)} %get-tuple-element.96), channel_id=1, source_target_pairs={{0,6},{1,7},{2,4},{3,5},{4,2},{5,3},{6,0},{7,1},{8,14},{9,15},{10,... | collective-permute-start | bytes 196616 | tf_op jit(solution)/shard_map/ppermute | solution.py:650
  48.5 2.1 %collective-permute-start.20 = (bf16[2,32,512]{2,1,0:T(8,128)(2,1)S(1)}, bf16[2,32,512]{2,1,0:T(8,128)(2,1)S(1)}, u32[]{:S(2)}, u32[]{:S(2)}) collective-permute-start(bf16[2,32,512]{2,1,0:T(8,128)(2,1)S(1)} %get-tuple-element.103), channel_id=1, source_target_pairs={{0,8},{1,9},{2,10},{3,11},{4,12},{5,13},{6,14},{7,15},{8,0},{9,1},... | collective-permute-start | bytes 196616 | tf_op jit(solution)/shard_map/ppermute | solution.py:650
  50.6 0.8 %collective-permute-start.21 = (bf16[2,32,512]{2,1,0:T(8,128)(2,1)S(1)}, bf16[2,32,512]{2,1,0:T(8,128)(2,1)S(1)}, u32[]{:S(2)}, u32[]{:S(2)}) collective-permute-start(bf16[2,32,512]{2,1,0:T(8,128)(2,1)S(1)} %get-tuple-element.104), channel_id=1, source_target_pairs={{0,2},{1,3},{2,0},{3,1},{4,6},{5,7},{6,4},{7,5},{8,10},{9,11},{10,... | collective-permute-start | bytes 196616 | tf_op jit(solution)/shard_map/ppermute | solution.py:650
  51.4 1.0 %collective-permute-done.17.refs_2_ = bf16[2,32,512]{2,1,0:T(8,128)(2,1)S(1)} collective-permute-done((bf16[2,32,512]{2,1,0:T(8,128)(2,1)S(1)}, bf16[2,32,512]{2,1,0:T(8,128)(2,1)S(1)}, u32[]{:S(2)}, u32[]{:S(2)}) %collective-permute-start.17) | collective-permute-done | bytes 65568 | tf_op jit(solution)/shard_map/ppermute | solution.py:650
  52.9 1.7 %collective-permute-done.19.refs_4_ = bf16[2,32,512]{2,1,0:T(8,128)(2,1)S(1)} collective-permute-done((bf16[2,32,512]{2,1,0:T(8,128)(2,1)S(1)}, bf16[2,32,512]{2,1,0:T(8,128)(2,1)S(1)}, u32[]{:S(2)}, u32[]{:S(2)}) %collective-permute-start.19) | collective-permute-done | bytes 65568 | tf_op jit(solution)/shard_map/ppermute | solution.py:650
  55.0 0.7 %collective-permute-done.22.refs_8_ = bf16[2,32,512]{2,1,0:T(8,128)(2,1)S(1)} collective-permute-done((bf16[2,32,512]{2,1,0:T(8,128)(2,1)S(1)}, bf16[2,32,512]{2,1,0:T(8,128)(2,1)S(1)}, u32[]{:S(2)}, u32[]{:S(2)}) %collective-permute-start.22) | collective-permute-done | bytes 65568 | tf_op jit(solution)/shard_map/ppermute | solution.py:650
  55.9 1.7 %finish.1 = f32[512,512]{1,0:T(8,128)} custom-call(s32[1]{0:T(128)} %bitcast.own_ref, bf16[2,32,512]{2,1,0:T(8,128)(2,1)S(1)} %collective-permute-done.14.refs_0_, bf16[2,32,512]{2,1,0:T(8,128)(2,1)S(1)} %collective-permute-done.15.refs_1_, bf16[2,32,512]{2,1,0:T(8,128)(2,1)S(1)} %collective-permute-done.17.refs_2_, ...), custom_call_target="tpu_custom_call" | custom-call | tf_op jit(solution)/shard_map/finish/pallas_call | solution.py:555
  (52 shorter events, 4.9 us)
Async XLA Ops:
  1.1 10.4 %collective-permute-start = (bf16[32,512]{1,0:T(8,128)(2,1)S(1)}, bf16[32,512]{1,0:T(8,128)(2,1)S(1)}, u32[]{:S(2)}, u32[]{:S(2)}) collective-permute-start(bf16[32,512]{1,0:T(8,128)(2,1)S(1)} %get-tuple-element.61), channel_id=1, source_target_pairs={{4,8},{8,4},{5,9},{9,5},{6,10},{10,6},{7,11},{11,7},{20,24},{24,20... | collective-permute-start | bytes 98312 | tf_op jit(solution)/shard_map/ppermute | solution.py:572
  1.9 9.6 %collective-permute-start.1 = (bf16[32,512]{1,0:T(8,128)(2,1)S(1)}, bf16[32,512]{1,0:T(8,128)(2,1)S(1)}, u32[]{:S(2)}, u32[]{:S(2)}) collective-permute-start(bf16[32,512]{1,0:T(8,128)(2,1)S(1)} %get-tuple-element.62), channel_id=1, source_target_pairs={{0,4},{8,12},{4,0},{12,8},{1,5},{9,13},{5,1},{13,9},{2,6},{10,14},... | collective-permute-start | bytes 98312 | tf_op jit(solution)/shard_map/ppermute | solution.py:572
  11.9 4.2 %collective-permute-start.2 = (bf16[32,512]{1,0:T(8,128)(2,1)S(1)}, bf16[32,512]{1,0:T(8,128)(2,1)S(1)}, u32[]{:S(2)}, u32[]{:S(2)}) collective-permute-start(bf16[32,512]{1,0:T(8,128)(2,1)S(1)} %get-tuple-element.74), channel_id=1, source_target_pairs={{0,1},{2,3},{1,0},{3,2},{4,5},{6,7},{5,4},{7,6},{8,9},{10,11},{9,8... | collective-permute-start | bytes 98312 | tf_op jit(solution)/shard_map/ppermute | solution.py:572
  12.0 4.1 %collective-permute-start.3 = (bf16[32,512]{1,0:T(8,128)(2,1)S(1)}, bf16[32,512]{1,0:T(8,128)(2,1)S(1)}, u32[]{:S(2)}, u32[]{:S(2)}) collective-permute-start(bf16[32,512]{1,0:T(8,128)(2,1)S(1)} %get-tuple-element.75), channel_id=1, source_target_pairs={{1,2},{2,1},{5,6},{6,5},{9,10},{10,9},{13,14},{14,13},{17,18},{18,... | collective-permute-start | bytes 98312 | tf_op jit(solution)/shard_map/ppermute | solution.py:572
  18.3 6.7 %collective-permute-start.6 = (bf16[6,32,512]{2,1,0:T(8,128)(2,1)S(1)}, bf16[6,32,512]{2,1,0:T(8,128)(2,1)S(1)}, u32[]{:S(2)}, u32[]{:S(2)}) collective-permute-start(bf16[6,32,512]{2,1,0:T(8,128)(2,1)S(1)} %get-tuple-element.79), channel_id=1, source_target_pairs={{0,1},{1,0},{2,3},{3,2},{4,5},{5,4},{6,7},{7,6},{8,9},{9,8},{10,11... | collective-permute-start | bytes 589832 | tf_op jit(solution)/shard_map/ppermute | solution.py:650
  21.2 7.6 %collective-permute-start.4 = (bf16[2,32,512]{2,1,0:T(8,128)(2,1)S(1)}, bf16[2,32,512]{2,1,0:T(8,128)(2,1)S(1)}, u32[]{:S(2)}, u32[]{:S(2)}) collective-permute-start(bf16[2,32,512]{2,1,0:T(8,128)(2,1)S(1)} %get-tuple-element.76), channel_id=1, source_target_pairs={{0,14},{1,15},{2,12},{3,13},{4,10},{5,11},{6,8},{7,9},{8,6},{9,7},... | collective-permute-start | bytes 196616 | tf_op jit(solution)/shard_map/ppermute | solution.py:650
  22.5 8.4 %collective-permute-start.5 = (bf16[2,32,512]{2,1,0:T(8,128)(2,1)S(1)}, bf16[2,32,512]{2,1,0:T(8,128)(2,1)S(1)}, u32[]{:S(2)}, u32[]{:S(2)}) collective-permute-start(bf16[2,32,512]{2,1,0:T(8,128)(2,1)S(1)} %get-tuple-element.77), channel_id=1, source_target_pairs={{0,12},{1,13},{2,14},{3,15},{4,8},{5,9},{6,10},{7,11},{8,4},{9,5},... | collective-permute-start | bytes 196616 | tf_op jit(solution)/shard_map/ppermute | solution.py:650
  25.0 9.2 %collective-permute-start.7 = (bf16[2,32,512]{2,1,0:T(8,128)(2,1)S(1)}, bf16[2,32,512]{2,1,0:T(8,128)(2,1)S(1)}, u32[]{:S(2)}, u32[]{:S(2)}) collective-permute-start(bf16[2,32,512]{2,1,0:T(8,128)(2,1)S(1)} %get-tuple-element.80), channel_id=1, source_target_pairs={{0,10},{1,11},{2,8},{3,9},{4,14},{5,15},{6,12},{7,13},{8,2},{9,3},... | collective-permute-start | bytes 196616 | tf_op jit(solution)/shard_map/ppermute | solution.py:650
  25.1 9.2 %collective-permute-start.8 = (bf16[2,32,512]{2,1,0:T(8,128)(2,1)S(1)}, bf16[2,32,512]{2,1,0:T(8,128)(2,1)S(1)}, u32[]{:S(2)}, u32[]{:S(2)}) collective-permute-start(bf16[2,32,512]{2,1,0:T(8,128)(2,1)S(1)} %get-tuple-element.81), channel_id=1, source_target_pairs={{0,6},{1,7},{2,4},{3,5},{4,2},{5,3},{6,0},{7,1},{8,14},{9,15},{10,... | collective-permute-start | bytes 196616 | tf_op jit(solution)/shard_map/ppermute | solution.py:650
  27.9 6.4 %collective-permute-start.9 = (bf16[2,32,512]{2,1,0:T(8,128)(2,1)S(1)}, bf16[2,32,512]{2,1,0:T(8,128)(2,1)S(1)}, u32[]{:S(2)}, u32[]{:S(2)}) collective-permute-start(bf16[2,32,512]{2,1,0:T(8,128)(2,1)S(1)} %get-tuple-element.82), channel_id=1, source_target_pairs={{0,4},{1,5},{2,6},{3,7},{4,0},{5,1},{6,2},{7,3},{8,12},{9,13},{10,... | collective-permute-start | bytes 196616 | tf_op jit(solution)/shard_map/ppermute | solution.py:650
  28.8 6.6 %collective-permute-start.10 = (bf16[2,32,512]{2,1,0:T(8,128)(2,1)S(1)}, bf16[2,32,512]{2,1,0:T(8,128)(2,1)S(1)}, u32[]{:S(2)}, u32[]{:S(2)}) collective-permute-start(bf16[2,32,512]{2,1,0:T(8,128)(2,1)S(1)} %get-tuple-element.88), channel_id=1, source_target_pairs={{0,8},{1,9},{2,10},{3,11},{4,12},{5,13},{6,14},{7,15},{8,0},{9,1},... | collective-permute-start | bytes 196616 | tf_op jit(solution)/shard_map/ppermute | solution.py:650
  31.0 4.5 %collective-permute-start.11 = (bf16[2,32,512]{2,1,0:T(8,128)(2,1)S(1)}, bf16[2,32,512]{2,1,0:T(8,128)(2,1)S(1)}, u32[]{:S(2)}, u32[]{:S(2)}) collective-permute-start(bf16[2,32,512]{2,1,0:T(8,128)(2,1)S(1)} %get-tuple-element.89), channel_id=1, source_target_pairs={{0,2},{1,3},{2,0},{3,1},{4,6},{5,7},{6,4},{7,5},{8,10},{9,11},{10,... | collective-permute-start | bytes 196616 | tf_op jit(solution)/shard_map/ppermute | solution.py:650
  34.3 1.3 %collective-permute-start.12 = (bf16[2,32,512]{2,1,0:T(8,128)(2,1)S(1)}, bf16[2,32,512]{2,1,0:T(8,128)(2,1)S(1)}, u32[]{:S(2)}, u32[]{:S(2)}) collective-permute-start(bf16[2,32,512]{2,1,0:T(8,128)(2,1)S(1)} %collective-permute-done.4.refs_0_), channel_id=1, source_target_pairs={{0,1},{1,0},{2,3},{3,2},{4,5},{5,4},{6,7},{7,6},{8,9},{9,8},{10,11... | collective-permute-start | bytes 196616 | tf_op jit(solution)/shard_map/ppermute | solution.py:650
  34.3 1.4 %collective-permute-start.13 = (bf16[2,32,512]{2,1,0:T(8,128)(2,1)S(1)}, bf16[2,32,512]{2,1,0:T(8,128)(2,1)S(1)}, u32[]{:S(2)}, u32[]{:S(2)}) collective-permute-start(bf16[2,32,512]{2,1,0:T(8,128)(2,1)S(1)} %collective-permute-done.5.refs_1_), channel_id=1, source_target_pairs={{0,1},{1,0},{2,3},{3,2},{4,5},{5,4},{6,7},{7,6},{8,9},{9,8},{10,11... | collective-permute-start | bytes 196616 | tf_op jit(solution)/shard_map/ppermute | solution.py:650
  39.7 4.9 %collective-permute-start.16 = (bf16[6,32,512]{2,1,0:T(8,128)(2,1)S(1)}, bf16[6,32,512]{2,1,0:T(8,128)(2,1)S(1)}, u32[]{:S(2)}, u32[]{:S(2)}) collective-permute-start(bf16[6,32,512]{2,1,0:T(8,128)(2,1)S(1)} %get-tuple-element.94), channel_id=1, source_target_pairs={{0,1},{1,0},{2,3},{3,2},{4,5},{5,4},{6,7},{7,6},{8,9},{9,8},{10,11... | collective-permute-start | bytes 589832 | tf_op jit(solution)/shard_map/ppermute | solution.py:650
  40.1 8.3 %collective-permute-start.14 = (bf16[2,32,512]{2,1,0:T(8,128)(2,1)S(1)}, bf16[2,32,512]{2,1,0:T(8,128)(2,1)S(1)}, u32[]{:S(2)}, u32[]{:S(2)}) collective-permute-start(bf16[2,32,512]{2,1,0:T(8,128)(2,1)S(1)} %get-tuple-element.91), channel_id=1, source_target_pairs={{0,14},{1,15},{2,12},{3,13},{4,10},{5,11},{6,8},{7,9},{8,6},{9,7},... | collective-permute-start | bytes 196616 | tf_op jit(solution)/shard_map/ppermute | solution.py:650
  43.1 7.5 %collective-permute-start.15 = (bf16[2,32,512]{2,1,0:T(8,128)(2,1)S(1)}, bf16[2,32,512]{2,1,0:T(8,128)(2,1)S(1)}, u32[]{:S(2)}, u32[]{:S(2)}) collective-permute-start(bf16[2,32,512]{2,1,0:T(8,128)(2,1)S(1)} %get-tuple-element.92), channel_id=1, source_target_pairs={{0,12},{1,13},{2,14},{3,15},{4,8},{5,9},{6,10},{7,11},{8,4},{9,5},... | collective-permute-start | bytes 196616 | tf_op jit(solution)/shard_map/ppermute | solution.py:650
  44.7 7.8 %collective-permute-start.17 = (bf16[2,32,512]{2,1,0:T(8,128)(2,1)S(1)}, bf16[2,32,512]{2,1,0:T(8,128)(2,1)S(1)}, u32[]{:S(2)}, u32[]{:S(2)}) collective-permute-start(bf16[2,32,512]{2,1,0:T(8,128)(2,1)S(1)} %get-tuple-element.95), channel_id=1, source_target_pairs={{0,10},{1,11},{2,8},{3,9},{4,14},{5,15},{6,12},{7,13},{8,2},{9,3},... | collective-permute-start | bytes 196616 | tf_op jit(solution)/shard_map/ppermute | solution.py:650
  44.8 8.1 %collective-permute-start.18 = (bf16[2,32,512]{2,1,0:T(8,128)(2,1)S(1)}, bf16[2,32,512]{2,1,0:T(8,128)(2,1)S(1)}, u32[]{:S(2)}, u32[]{:S(2)}) collective-permute-start(bf16[2,32,512]{2,1,0:T(8,128)(2,1)S(1)} %get-tuple-element.96), channel_id=1, source_target_pairs={{0,6},{1,7},{2,4},{3,5},{4,2},{5,3},{6,0},{7,1},{8,14},{9,15},{10,... | collective-permute-start | bytes 196616 | tf_op jit(solution)/shard_map/ppermute | solution.py:650
  48.5 6.1 %collective-permute-start.19 = (bf16[2,32,512]{2,1,0:T(8,128)(2,1)S(1)}, bf16[2,32,512]{2,1,0:T(8,128)(2,1)S(1)}, u32[]{:S(2)}, u32[]{:S(2)}) collective-permute-start(bf16[2,32,512]{2,1,0:T(8,128)(2,1)S(1)} %get-tuple-element.97), channel_id=1, source_target_pairs={{0,4},{1,5},{2,6},{3,7},{4,0},{5,1},{6,2},{7,3},{8,12},{9,13},{10,... | collective-permute-start | bytes 196616 | tf_op jit(solution)/shard_map/ppermute | solution.py:650
  48.5 6.6 %collective-permute-start.20 = (bf16[2,32,512]{2,1,0:T(8,128)(2,1)S(1)}, bf16[2,32,512]{2,1,0:T(8,128)(2,1)S(1)}, u32[]{:S(2)}, u32[]{:S(2)}) collective-permute-start(bf16[2,32,512]{2,1,0:T(8,128)(2,1)S(1)} %get-tuple-element.103), channel_id=1, source_target_pairs={{0,8},{1,9},{2,10},{3,11},{4,12},{5,13},{6,14},{7,15},{8,0},{9,1},... | collective-permute-start | bytes 196616 | tf_op jit(solution)/shard_map/ppermute | solution.py:650
  50.6 4.4 %collective-permute-start.21 = (bf16[2,32,512]{2,1,0:T(8,128)(2,1)S(1)}, bf16[2,32,512]{2,1,0:T(8,128)(2,1)S(1)}, u32[]{:S(2)}, u32[]{:S(2)}) collective-permute-start(bf16[2,32,512]{2,1,0:T(8,128)(2,1)S(1)} %get-tuple-element.104), channel_id=1, source_target_pairs={{0,2},{1,3},{2,0},{3,1},{4,6},{5,7},{6,4},{7,5},{8,10},{9,11},{10,... | collective-permute-start | bytes 196616 | tf_op jit(solution)/shard_map/ppermute | solution.py:650
  54.5 1.3 %collective-permute-start.22 = (bf16[2,32,512]{2,1,0:T(8,128)(2,1)S(1)}, bf16[2,32,512]{2,1,0:T(8,128)(2,1)S(1)}, u32[]{:S(2)}, u32[]{:S(2)}) collective-permute-start(bf16[2,32,512]{2,1,0:T(8,128)(2,1)S(1)} %collective-permute-done.14.refs_0_), channel_id=1, source_target_pairs={{0,1},{1,0},{2,3},{3,2},{4,5},{5,4},{6,7},{7,6},{8,9},{9,8},{10,11... | collective-permute-start | bytes 196616 | tf_op jit(solution)/shard_map/ppermute | solution.py:650
  54.5 1.4 %collective-permute-start.23 = (bf16[2,32,512]{2,1,0:T(8,128)(2,1)S(1)}, bf16[2,32,512]{2,1,0:T(8,128)(2,1)S(1)}, u32[]{:S(2)}, u32[]{:S(2)}) collective-permute-start(bf16[2,32,512]{2,1,0:T(8,128)(2,1)S(1)} %collective-permute-done.15.refs_1_), channel_id=1, source_target_pairs={{0,1},{1,0},{2,3},{3,2},{4,5},{5,4},{6,7},{7,6},{8,9},{9,8},{10,11... | collective-permute-start | bytes 196616 | tf_op jit(solution)/shard_map/ppermute | solution.py:650
  (8 other events, 92.9 us)

commit v26 on v23

--- a/solution.py
+++ b/solution.py
@@ -111,7 +111,7 @@
 
 
 def strips_kernel(
-    odd_row_ref, odd_col_ref, normed_ref, row_one_ref, row_two_ref, up_ref, down_ref, one_ref, two_ref
+    odd_row_ref, odd_col_ref, row_two_ref, row_one_ref, normed_ref, up_ref, down_ref, one_ref, two_ref
 ):
     tokens = normed_ref.shape[0]
     cols = up_ref.shape[0]
@@ -145,7 +145,7 @@
         out_shape=[jax.ShapeDtypeStruct(shape, jnp.bfloat16) for shape in shapes],
         compiler_params=pltpu.CompilerParams(vmem_limit_bytes=4 * MIB),
         name="column_strips",
-    )(odd_row, odd_col, normed, row_one, row_two)
+    )(odd_row, odd_col, row_two, row_one, normed)
 
 
 def padded_rows(tokens):
@@ -749,7 +749,7 @@
         (own, odd_row, odd_col, field[0], field[rows - 1])
     )
     one, two = row_edges(odd_row, top, bottom)
-    one, two = swap_pairs(one, "row", 0), swap_pairs(two, "row", 1)
+    two, one = swap_pairs(two, "row", 1), swap_pairs(one, "row", 0)
     normed = half_norm_of(flat)
     expanded = expand(normed, w_expand)
     tile = divisor(w_expand.shape[1] // 2, 256, LANES)
@@ -758,8 +758,8 @@
     total, rim_one = inner(
         expanded, flat, depth_kernel, w_project, rows, cols, 0, early, tile
     )
-    one, two, normed, expanded, total, rim_one = lax.optimization_barrier(
-        (one, two, normed, expanded, total, rim_one)
+    two, one, normed, expanded, total, rim_one = lax.optimization_barrier(
+        (two, one, normed, expanded, total, rim_one)
     )
     up, down, one, two = column_strips(odd_row, odd_col, normed, one, two, round_up(rows + 2, 16))
     one, two = swap_pairs(one, "col", 0), swap_pairs(two, "col", 1)

time: 57.1 us -> 58.5 us (1.025)
  waiting for transfers between devices: 5.92 us -> 6.79 us
  starting transfers between devices: 33.1 us -> 33.7 us
    ppermute x4, starting transfers between devices: 4.61 us -> 7.57 us  [swap_pairs(): return lax.ppermute(edge, axis, pairs + [(b, a) for a, b in pairs])]
    ppermute x20, starting transfers between devices: 28.5 us -> 26.2 us  [swap(): lax.ppermute(slab, ('row', 'col'), [(i, i ^ mask) for i in range(devices)])]
    ppermute x20, waiting for transfers between devices: 5.91 us -> 6.78 us  [swap(): lax.ppermute(slab, ('row', 'col'), [(i, i ^ mask) for i in range(devices)])]
  transfers between devices with their start and end apart: 24 -> 24, of which waited for: 5 -> 11; matrix products, arithmetic and copies ran while one was open for 0% -> 0% of each run, Pallas kernels for 15% -> 14%
where the time goes in v26:
time: 58.5 us; the launch traced here: 58.4 us
  starting transfers between devices  33.7 us (58%)
  Pallas kernels  16.6 us (28%)
  waiting for transfers between devices  6.79 us (12%)
  local copies, waits for them, and re-layouts  0.93 us (2%)
    ppermute x20, starting transfers between devices, swap(): lax.ppermute(slab, ('row', 'col'), [(i, i ^ mask) for i in range(devices)])  26.2 us
    ppermute x4, starting transfers between devices, swap_pairs(): return lax.ppermute(edge, axis, pairs + [(b, a) for a, b in pairs])  7.57 us
    ppermute x20, waiting for transfers between devices, swap(): lax.ppermute(slab, ('row', 'col'), [(i, i ^ mask) for i in range(devices)])  6.78 us
    pallas_call x2, Pallas kernels, inner(): pl.pallas_call(functools.partial(inner_kernel, rows=rows, cols=cols, firs...  5.06 us
    pallas_call x1, Pallas kernels, attend(): pl.pallas_call(functools.partial(attend_kernel, plan=plan, sets=sets, cam...  4.01 us
    pallas_call x1, Pallas kernels, expand(): pl.pallas_call(expand_kernel, in_specs=[vmem()] * 2, out_specs=vmem(), ou...  2.3 us
    pallas_call x1, Pallas kernels, rim(): pl.pallas_call(functools.partial(rim_kernel, rows=rows, cols=cols, plan=p...  2.07 us
    pallas_call x1, Pallas kernels, finish(): pl.pallas_call(functools.partial(finish_kernel, plan=plan), in_specs=[pl....  1.72 us
  transfers between devices with their start and end apart: 24, of which 11 were waited for; matrix products, arithmetic and copies ran while one was open for 0% of the time, Pallas kernels for 14%

profile of v26, /device:TPU:0, one launch (start us, length us, event | category | flops | bytes accessed | tf_op | source)
XLA Modules:
  0.0 58.4 jit_solution(9925718945690694894)
XLA Ops:
  0.0 0.9 %slice_bitcast_fusion = (f32[32,512]{1,0:T(8,128)S(1)}, f32[32,512]{1,0:T(8,128)S(1)}) fusion(f32[16,32,512]{2,1,0:T(8,128)} %param.8), kind=kLoop, calls=%fused_computation | loop fusion | bytes 262144 | tf_op jit(solution)/shard_map/squeeze | solution.py:749
  1.1 0.8 %collective-permute-start = (bf16[32,512]{1,0:T(8,128)(2,1)S(1)}, bf16[32,512]{1,0:T(8,128)(2,1)S(1)}, u32[]{:S(2)}, u32[]{:S(2)}) collective-permute-start(bf16[32,512]{1,0:T(8,128)(2,1)S(1)} %get-tuple-element.62), channel_id=1, source_target_pairs={{4,8},{8,4},{5,9},{9,5},{6,10},{10,6},{7,11},{11,7},{20,24},{24,20... | collective-permute-start | bytes 98312 | tf_op jit(solution)/shard_map/ppermute | solution.py:614
  1.9 5.9 %collective-permute-start.1 = (bf16[32,512]{1,0:T(8,128)(2,1)S(1)}, bf16[32,512]{1,0:T(8,128)(2,1)S(1)}, u32[]{:S(2)}, u32[]{:S(2)}) collective-permute-start(bf16[32,512]{1,0:T(8,128)(2,1)S(1)} %get-tuple-element.63), channel_id=1, source_target_pairs={{0,4},{8,12},{4,0},{12,8},{1,5},{9,13},{5,1},{13,9},{2,6},{10,14},... | collective-permute-start | bytes 98312 | tf_op jit(solution)/shard_map/ppermute | solution.py:614
  8.2 2.3 %expand.1.expanded_ref = f32[8448,128]{1,0:T(8,128)S(1)} custom-call(bf16[512,512]{1,0:T(8,128)(2,1)S(1)} %half_norm.1.normed_ref, bf16[512,2048]{1,0:T(8,128)(2,1)S(1)} %copy-done), custom_call_target="tpu_custom_call" | custom-call | flops 10000000000 | bytes 6815744 | tf_op jit(solution)/shard_map/expand/pallas_call | solution.py:189
  10.5 1.2 %inner.2 = (f32[512,512]{1,0:T(8,128)S(1)}, f32[4,96,128]{2,1,0:T(8,128)S(1)}) custom-call(f32[8448,128]{1,0:T(8,128)S(1)} %expand.1.expanded_ref, f32[512,512]{1,0:T(8,128)S(1)} %bitcast.10, f32[3,3,2048]{2,1,0:T(4,128)S(1)} %copy-done.6, bf16[2048,512]{1,0:T(8,128)(2,1)S(1)} %copy-done.1), custom_call_target="tpu_custom_call" | custom-call | flops 4000000000 | bytes 3145728 | tf_op jit(solution)/shard_map/inner/pallas_call | solution.py:279
  12.2 0.8 %collective-permute-start.3 = (bf16[32,512]{1,0:T(8,128)(2,1)S(1)}, bf16[32,512]{1,0:T(8,128)(2,1)S(1)}, u32[]{:S(2)}, u32[]{:S(2)}) collective-permute-start(bf16[32,512]{1,0:T(8,128)(2,1)S(1)} %get-tuple-element.77), channel_id=1, source_target_pairs={{1,2},{2,1},{5,6},{6,5},{9,10},{10,9},{13,14},{14,13},{17,18},{18,... | collective-permute-start | bytes 98312 | tf_op jit(solution)/shard_map/ppermute | solution.py:614
  13.0 3.8 %inner.3 = (f32[512,512]{1,0:T(8,128)S(1)}, f32[12,96,128]{2,1,0:T(8,128)S(1)}) custom-call(f32[8448,128]{1,0:T(8,128)S(1)} %expand.1.expanded_ref, f32[512,512]{1,0:T(8,128)S(1)} %get-tuple-element.67.start_ref, f32[3,3,2048]{2,1,0:T(4,128)S(1)} %copy-done.6, bf16[2048,512]{1,0:T(8,128)(2,1)S(1)} %copy-done.1), custom_call_target="tpu_custom_call" | custom-call | flops 12000000000 | bytes 5242880 | tf_op jit(solution)/shard_map/inner/pallas_call | solution.py:279
  16.9 2.1 %rim.1 = (f32[512,512]{1,0:T(8,128)S(1)}, bf16[2,32,512]{2,1,0:T(8,128)(2,1)S(1)}, bf16[2,32,512]{2,1,0:T(8,128)(2,1)S(1)}, bf16[1,32,512]{2,1,0:T(8,128)(2,1)S(...) custom-call(s32[1]{0:T(128)} %bitcast.own_ref, s32[1]{0:T(128)} %bitcast.2.odd_col_ref, ...), custom_call_target="tpu_custom_call" | custom-call | flops 805306368 | bytes 6815744 | tf_op jit(solution)/shard_map/rim/pallas_call | solution.py:388
  19.0 3.0 %collective-permute-start.6 = (bf16[6,32,512]{2,1,0:T(8,128)(2,1)S(1)}, bf16[6,32,512]{2,1,0:T(8,128)(2,1)S(1)}, u32[]{:S(2)}, u32[]{:S(2)}) collective-permute-start(bf16[6,32,512]{2,1,0:T(8,128)(2,1)S(1)} %get-tuple-element.81), channel_id=1, source_target_pairs={{0,1},{1,0},{2,3},{3,2},{4,5},{5,4},{6,7},{7,6},{8,9},{9,8},{10,11... | collective-permute-start | bytes 589832 | tf_op jit(solution)/shard_map/ppermute | solution.py:692
  21.9 1.3 %collective-permute-start.4 = (bf16[2,32,512]{2,1,0:T(8,128)(2,1)S(1)}, bf16[2,32,512]{2,1,0:T(8,128)(2,1)S(1)}, u32[]{:S(2)}, u32[]{:S(2)}) collective-permute-start(bf16[2,32,512]{2,1,0:T(8,128)(2,1)S(1)} %get-tuple-element.78), channel_id=1, source_target_pairs={{0,14},{1,15},{2,12},{3,13},{4,10},{5,11},{6,8},{7,9},{8,6},{9,7},... | collective-permute-start | bytes 196616 | tf_op jit(solution)/shard_map/ppermute | solution.py:692
  23.3 2.5 %collective-permute-start.5 = (bf16[2,32,512]{2,1,0:T(8,128)(2,1)S(1)}, bf16[2,32,512]{2,1,0:T(8,128)(2,1)S(1)}, u32[]{:S(2)}, u32[]{:S(2)}) collective-permute-start(bf16[2,32,512]{2,1,0:T(8,128)(2,1)S(1)} %get-tuple-element.79), channel_id=1, source_target_pairs={{0,12},{1,13},{2,14},{3,15},{4,8},{5,9},{6,10},{7,11},{8,4},{9,5},... | collective-permute-start | bytes 196616 | tf_op jit(solution)/shard_map/ppermute | solution.py:692
  25.9 2.8 %collective-permute-start.8 = (bf16[2,32,512]{2,1,0:T(8,128)(2,1)S(1)}, bf16[2,32,512]{2,1,0:T(8,128)(2,1)S(1)}, u32[]{:S(2)}, u32[]{:S(2)}) collective-permute-start(bf16[2,32,512]{2,1,0:T(8,128)(2,1)S(1)} %get-tuple-element.83), channel_id=1, source_target_pairs={{0,6},{1,7},{2,4},{3,5},{4,2},{5,3},{6,0},{7,1},{8,14},{9,15},{10,... | collective-permute-start | bytes 196616 | tf_op jit(solution)/shard_map/ppermute | solution.py:692
  29.5 2.2 %collective-permute-start.10 = (bf16[2,32,512]{2,1,0:T(8,128)(2,1)S(1)}, bf16[2,32,512]{2,1,0:T(8,128)(2,1)S(1)}, u32[]{:S(2)}, u32[]{:S(2)}) collective-permute-start(bf16[2,32,512]{2,1,0:T(8,128)(2,1)S(1)} %get-tuple-element.90), channel_id=1, source_target_pairs={{0,8},{1,9},{2,10},{3,11},{4,12},{5,13},{6,14},{7,15},{8,0},{9,1},... | collective-permute-start | bytes 196616 | tf_op jit(solution)/shard_map/ppermute | solution.py:692
  31.7 1.5 %collective-permute-start.11 = (bf16[2,32,512]{2,1,0:T(8,128)(2,1)S(1)}, bf16[2,32,512]{2,1,0:T(8,128)(2,1)S(1)}, u32[]{:S(2)}, u32[]{:S(2)}) collective-permute-start(bf16[2,32,512]{2,1,0:T(8,128)(2,1)S(1)} %get-tuple-element.91), channel_id=1, source_target_pairs={{0,2},{1,3},{2,0},{3,1},{4,6},{5,7},{6,4},{7,5},{8,10},{9,11},{10,... | collective-permute-start | bytes 196616 | tf_op jit(solution)/shard_map/ppermute | solution.py:692
  33.2 1.1 %collective-permute-done.7.refs_0_.refs_1_.refs_2_.refs_5_.refs_6_.refs_8_.refs_9_ = bf16[2,32,512]{2,1,0:T(8,128)(2,1)S(1)} collective-permute-done((bf16[2,32,512]{2,1,0:T(8,128)(2,1)S(1)}, bf16[2,32,512]{2,1,0:T(8,128)(2,1)S(1)}, u32[]{:S(2)}, u32[]{:S(2)}) %collective-permute-start.7) | collective-permute-done | bytes 65568 | tf_op jit(solution)/shard_map/ppermute | solution.py:692
  34.3 1.0 %collective-permute-done.9.refs_4_ = bf16[2,32,512]{2,1,0:T(8,128)(2,1)S(1)} collective-permute-done((bf16[2,32,512]{2,1,0:T(8,128)(2,1)S(1)}, bf16[2,32,512]{2,1,0:T(8,128)(2,1)S(1)}, u32[]{:S(2)}, u32[]{:S(2)}) %collective-permute-start.9) | collective-permute-done | bytes 65568 | tf_op jit(solution)/shard_map/ppermute | solution.py:692
  36.7 4.0 %attend.1 = (bf16[2,32,512]{2,1,0:T(8,128)(2,1)S(1)}, bf16[2,32,512]{2,1,0:T(8,128)(2,1)S(1)}, bf16[1,32,512]{2,1,0:T(8,128)(2,1)S(1)}, bf16[6,32,512]{2,1,0:T(8,128)(2,1)S(1)}, bf16[5,32,512]{2,1,0:T(8,128)(2,1)S(1)}) custom-call(bf16[2,32,512]{2,1,0:T(8,128)(2,1)S(1)} %collective-permute-done.4.refs_0_, ...), custom_call_target="tpu_custom_call" | custom-call | flops 1073741824 | bytes 2621440 | tf_op jit(solution)/shard_map/attend/pallas_call | solution.py:544
  41.1 2.6 %collective-permute-start.14 = (bf16[2,32,512]{2,1,0:T(8,128)(2,1)S(1)}, bf16[2,32,512]{2,1,0:T(8,128)(2,1)S(1)}, u32[]{:S(2)}, u32[]{:S(2)}) collective-permute-start(bf16[2,32,512]{2,1,0:T(8,128)(2,1)S(1)} %get-tuple-element.93), channel_id=1, source_target_pairs={{0,14},{1,15},{2,12},{3,13},{4,10},{5,11},{6,8},{7,9},{8,6},{9,7},... | collective-permute-start | bytes 196616 | tf_op jit(solution)/shard_map/ppermute | solution.py:692
  43.7 1.9 %collective-permute-start.15 = (bf16[2,32,512]{2,1,0:T(8,128)(2,1)S(1)}, bf16[2,32,512]{2,1,0:T(8,128)(2,1)S(1)}, u32[]{:S(2)}, u32[]{:S(2)}) collective-permute-start(bf16[2,32,512]{2,1,0:T(8,128)(2,1)S(1)} %get-tuple-element.94), channel_id=1, source_target_pairs={{0,12},{1,13},{2,14},{3,15},{4,8},{5,9},{6,10},{7,11},{8,4},{9,5},... | collective-permute-start | bytes 196616 | tf_op jit(solution)/shard_map/ppermute | solution.py:692
  45.8 3.4 %collective-permute-start.18 = (bf16[2,32,512]{2,1,0:T(8,128)(2,1)S(1)}, bf16[2,32,512]{2,1,0:T(8,128)(2,1)S(1)}, u32[]{:S(2)}, u32[]{:S(2)}) collective-permute-start(bf16[2,32,512]{2,1,0:T(8,128)(2,1)S(1)} %get-tuple-element.98), channel_id=1, source_target_pairs={{0,6},{1,7},{2,4},{3,5},{4,2},{5,3},{6,0},{7,1},{8,14},{9,15},{10,... | collective-permute-start | bytes 196616 | tf_op jit(solution)/shard_map/ppermute | solution.py:692
  49.1 2.5 %collective-permute-start.20 = (bf16[2,32,512]{2,1,0:T(8,128)(2,1)S(1)}, bf16[2,32,512]{2,1,0:T(8,128)(2,1)S(1)}, u32[]{:S(2)}, u32[]{:S(2)}) collective-permute-start(bf16[2,32,512]{2,1,0:T(8,128)(2,1)S(1)} %get-tuple-element.105), channel_id=1, source_target_pairs={{0,8},{1,9},{2,10},{3,11},{4,12},{5,13},{6,14},{7,15},{8,0},{9,1},... | collective-permute-start | bytes 196616 | tf_op jit(solution)/shard_map/ppermute | solution.py:692
  52.9 0.9 %collective-permute-done.18.refs_3_ = bf16[2,32,512]{2,1,0:T(8,128)(2,1)S(1)} collective-permute-done((bf16[2,32,512]{2,1,0:T(8,128)(2,1)S(1)}, bf16[2,32,512]{2,1,0:T(8,128)(2,1)S(1)}, u32[]{:S(2)}, u32[]{:S(2)}) %collective-permute-start.18) | collective-permute-done | bytes 65568 | tf_op jit(solution)/shard_map/ppermute | solution.py:692
  53.7 1.5 %collective-permute-done.19.refs_4_ = bf16[2,32,512]{2,1,0:T(8,128)(2,1)S(1)} collective-permute-done((bf16[2,32,512]{2,1,0:T(8,128)(2,1)S(1)}, bf16[2,32,512]{2,1,0:T(8,128)(2,1)S(1)}, u32[]{:S(2)}, u32[]{:S(2)}) %collective-permute-start.19) | collective-permute-done | bytes 65568 | tf_op jit(solution)/shard_map/ppermute | solution.py:692
  56.7 1.7 %finish.1 = f32[512,512]{1,0:T(8,128)} custom-call(s32[1]{0:T(128)} %bitcast.own_ref, bf16[2,32,512]{2,1,0:T(8,128)(2,1)S(1)} %collective-permute-done.14.refs_0_, bf16[2,32,512]{2,1,0:T(8,128)(2,1)S(1)} %collective-permute-done.15.refs_1_, bf16[2,32,512]{2,1,0:T(8,128)(2,1)S(1)} %collective-permute-done.17.refs_2_, ...), custom_call_target="tpu_custom_call" | custom-call | tf_op jit(solution)/shard_map/finish/pallas_call | solution.py:597
  (53 shorter events, 6.5 us)
Async XLA Ops:
  1.1 10.7 %collective-permute-start = (bf16[32,512]{1,0:T(8,128)(2,1)S(1)}, bf16[32,512]{1,0:T(8,128)(2,1)S(1)}, u32[]{:S(2)}, u32[]{:S(2)}) collective-permute-start(bf16[32,512]{1,0:T(8,128)(2,1)S(1)} %get-tuple-element.62), channel_id=1, source_target_pairs={{4,8},{8,4},{5,9},{9,5},{6,10},{10,6},{7,11},{11,7},{20,24},{24,20... | collective-permute-start | bytes 98312 | tf_op jit(solution)/shard_map/ppermute | solution.py:614
  1.9 9.9 %collective-permute-start.1 = (bf16[32,512]{1,0:T(8,128)(2,1)S(1)}, bf16[32,512]{1,0:T(8,128)(2,1)S(1)}, u32[]{:S(2)}, u32[]{:S(2)}) collective-permute-start(bf16[32,512]{1,0:T(8,128)(2,1)S(1)} %get-tuple-element.63), channel_id=1, source_target_pairs={{0,4},{8,12},{4,0},{12,8},{1,5},{9,13},{5,1},{13,9},{2,6},{10,14},... | collective-permute-start | bytes 98312 | tf_op jit(solution)/shard_map/ppermute | solution.py:614
  12.1 4.7 %collective-permute-start.2 = (bf16[32,512]{1,0:T(8,128)(2,1)S(1)}, bf16[32,512]{1,0:T(8,128)(2,1)S(1)}, u32[]{:S(2)}, u32[]{:S(2)}) collective-permute-start(bf16[32,512]{1,0:T(8,128)(2,1)S(1)} %get-tuple-element.76), channel_id=1, source_target_pairs={{0,1},{2,3},{1,0},{3,2},{4,5},{6,7},{5,4},{7,6},{8,9},{10,11},{9,8... | collective-permute-start | bytes 98312 | tf_op jit(solution)/shard_map/ppermute | solution.py:614
  12.2 4.6 %collective-permute-start.3 = (bf16[32,512]{1,0:T(8,128)(2,1)S(1)}, bf16[32,512]{1,0:T(8,128)(2,1)S(1)}, u32[]{:S(2)}, u32[]{:S(2)}) collective-permute-start(bf16[32,512]{1,0:T(8,128)(2,1)S(1)} %get-tuple-element.77), channel_id=1, source_target_pairs={{1,2},{2,1},{5,6},{6,5},{9,10},{10,9},{13,14},{14,13},{17,18},{18,... | collective-permute-start | bytes 98312 | tf_op jit(solution)/shard_map/ppermute | solution.py:614
  19.0 6.8 %collective-permute-start.6 = (bf16[6,32,512]{2,1,0:T(8,128)(2,1)S(1)}, bf16[6,32,512]{2,1,0:T(8,128)(2,1)S(1)}, u32[]{:S(2)}, u32[]{:S(2)}) collective-permute-start(bf16[6,32,512]{2,1,0:T(8,128)(2,1)S(1)} %get-tuple-element.81), channel_id=1, source_target_pairs={{0,1},{1,0},{2,3},{3,2},{4,5},{5,4},{6,7},{7,6},{8,9},{9,8},{10,11... | collective-permute-start | bytes 589832 | tf_op jit(solution)/shard_map/ppermute | solution.py:692
  21.9 7.6 %collective-permute-start.4 = (bf16[2,32,512]{2,1,0:T(8,128)(2,1)S(1)}, bf16[2,32,512]{2,1,0:T(8,128)(2,1)S(1)}, u32[]{:S(2)}, u32[]{:S(2)}) collective-permute-start(bf16[2,32,512]{2,1,0:T(8,128)(2,1)S(1)} %get-tuple-element.78), channel_id=1, source_target_pairs={{0,14},{1,15},{2,12},{3,13},{4,10},{5,11},{6,8},{7,9},{8,6},{9,7},... | collective-permute-start | bytes 196616 | tf_op jit(solution)/shard_map/ppermute | solution.py:692
  23.3 8.4 %collective-permute-start.5 = (bf16[2,32,512]{2,1,0:T(8,128)(2,1)S(1)}, bf16[2,32,512]{2,1,0:T(8,128)(2,1)S(1)}, u32[]{:S(2)}, u32[]{:S(2)}) collective-permute-start(bf16[2,32,512]{2,1,0:T(8,128)(2,1)S(1)} %get-tuple-element.79), channel_id=1, source_target_pairs={{0,12},{1,13},{2,14},{3,15},{4,8},{5,9},{6,10},{7,11},{8,4},{9,5},... | collective-permute-start | bytes 196616 | tf_op jit(solution)/shard_map/ppermute | solution.py:692
  25.8 8.5 %collective-permute-start.7 = (bf16[2,32,512]{2,1,0:T(8,128)(2,1)S(1)}, bf16[2,32,512]{2,1,0:T(8,128)(2,1)S(1)}, u32[]{:S(2)}, u32[]{:S(2)}) collective-permute-start(bf16[2,32,512]{2,1,0:T(8,128)(2,1)S(1)} %get-tuple-element.82), channel_id=1, source_target_pairs={{0,10},{1,11},{2,8},{3,9},{4,14},{5,15},{6,12},{7,13},{8,2},{9,3},... | collective-permute-start | bytes 196616 | tf_op jit(solution)/shard_map/ppermute | solution.py:692
  25.9 8.4 %collective-permute-start.8 = (bf16[2,32,512]{2,1,0:T(8,128)(2,1)S(1)}, bf16[2,32,512]{2,1,0:T(8,128)(2,1)S(1)}, u32[]{:S(2)}, u32[]{:S(2)}) collective-permute-start(bf16[2,32,512]{2,1,0:T(8,128)(2,1)S(1)} %get-tuple-element.83), channel_id=1, source_target_pairs={{0,6},{1,7},{2,4},{3,5},{4,2},{5,3},{6,0},{7,1},{8,14},{9,15},{10,... | collective-permute-start | bytes 196616 | tf_op jit(solution)/shard_map/ppermute | solution.py:692
  28.7 6.6 %collective-permute-start.9 = (bf16[2,32,512]{2,1,0:T(8,128)(2,1)S(1)}, bf16[2,32,512]{2,1,0:T(8,128)(2,1)S(1)}, u32[]{:S(2)}, u32[]{:S(2)}) collective-permute-start(bf16[2,32,512]{2,1,0:T(8,128)(2,1)S(1)} %get-tuple-element.84), channel_id=1, source_target_pairs={{0,4},{1,5},{2,6},{3,7},{4,0},{5,1},{6,2},{7,3},{8,12},{9,13},{10,... | collective-permute-start | bytes 196616 | tf_op jit(solution)/shard_map/ppermute | solution.py:692
  29.5 6.9 %collective-permute-start.10 = (bf16[2,32,512]{2,1,0:T(8,128)(2,1)S(1)}, bf16[2,32,512]{2,1,0:T(8,128)(2,1)S(1)}, u32[]{:S(2)}, u32[]{:S(2)}) collective-permute-start(bf16[2,32,512]{2,1,0:T(8,128)(2,1)S(1)} %get-tuple-element.90), channel_id=1, source_target_pairs={{0,8},{1,9},{2,10},{3,11},{4,12},{5,13},{6,14},{7,15},{8,0},{9,1},... | collective-permute-start | bytes 196616 | tf_op jit(solution)/shard_map/ppermute | solution.py:692
  31.7 4.7 %collective-permute-start.11 = (bf16[2,32,512]{2,1,0:T(8,128)(2,1)S(1)}, bf16[2,32,512]{2,1,0:T(8,128)(2,1)S(1)}, u32[]{:S(2)}, u32[]{:S(2)}) collective-permute-start(bf16[2,32,512]{2,1,0:T(8,128)(2,1)S(1)} %get-tuple-element.91), channel_id=1, source_target_pairs={{0,2},{1,3},{2,0},{3,1},{4,6},{5,7},{6,4},{7,5},{8,10},{9,11},{10,... | collective-permute-start | bytes 196616 | tf_op jit(solution)/shard_map/ppermute | solution.py:692
  35.3 1.3 %collective-permute-start.12 = (bf16[2,32,512]{2,1,0:T(8,128)(2,1)S(1)}, bf16[2,32,512]{2,1,0:T(8,128)(2,1)S(1)}, u32[]{:S(2)}, u32[]{:S(2)}) collective-permute-start(bf16[2,32,512]{2,1,0:T(8,128)(2,1)S(1)} %collective-permute-done.4.refs_0_), channel_id=1, source_target_pairs={{0,1},{1,0},{2,3},{3,2},{4,5},{5,4},{6,7},{7,6},{8,9},{9,8},{10,11... | collective-permute-start | bytes 196616 | tf_op jit(solution)/shard_map/ppermute | solution.py:692
  35.3 1.4 %collective-permute-start.13 = (bf16[2,32,512]{2,1,0:T(8,128)(2,1)S(1)}, bf16[2,32,512]{2,1,0:T(8,128)(2,1)S(1)}, u32[]{:S(2)}, u32[]{:S(2)}) collective-permute-start(bf16[2,32,512]{2,1,0:T(8,128)(2,1)S(1)} %collective-permute-done.5.refs_1_), channel_id=1, source_target_pairs={{0,1},{1,0},{2,3},{3,2},{4,5},{5,4},{6,7},{7,6},{8,9},{9,8},{10,11... | collective-permute-start | bytes 196616 | tf_op jit(solution)/shard_map/ppermute | solution.py:692
  40.7 5.0 %collective-permute-start.16 = (bf16[6,32,512]{2,1,0:T(8,128)(2,1)S(1)}, bf16[6,32,512]{2,1,0:T(8,128)(2,1)S(1)}, u32[]{:S(2)}, u32[]{:S(2)}) collective-permute-start(bf16[6,32,512]{2,1,0:T(8,128)(2,1)S(1)} %get-tuple-element.96), channel_id=1, source_target_pairs={{0,1},{1,0},{2,3},{3,2},{4,5},{5,4},{6,7},{7,6},{8,9},{9,8},{10,11... | collective-permute-start | bytes 589832 | tf_op jit(solution)/shard_map/ppermute | solution.py:692
  41.1 8.0 %collective-permute-start.14 = (bf16[2,32,512]{2,1,0:T(8,128)(2,1)S(1)}, bf16[2,32,512]{2,1,0:T(8,128)(2,1)S(1)}, u32[]{:S(2)}, u32[]{:S(2)}) collective-permute-start(bf16[2,32,512]{2,1,0:T(8,128)(2,1)S(1)} %get-tuple-element.93), channel_id=1, source_target_pairs={{0,14},{1,15},{2,12},{3,13},{4,10},{5,11},{6,8},{7,9},{8,6},{9,7},... | collective-permute-start | bytes 196616 | tf_op jit(solution)/shard_map/ppermute | solution.py:692
  43.7 7.9 %collective-permute-start.15 = (bf16[2,32,512]{2,1,0:T(8,128)(2,1)S(1)}, bf16[2,32,512]{2,1,0:T(8,128)(2,1)S(1)}, u32[]{:S(2)}, u32[]{:S(2)}) collective-permute-start(bf16[2,32,512]{2,1,0:T(8,128)(2,1)S(1)} %get-tuple-element.94), channel_id=1, source_target_pairs={{0,12},{1,13},{2,14},{3,15},{4,8},{5,9},{6,10},{7,11},{8,4},{9,5},... | collective-permute-start | bytes 196616 | tf_op jit(solution)/shard_map/ppermute | solution.py:692
  45.7 7.2 %collective-permute-start.17 = (bf16[2,32,512]{2,1,0:T(8,128)(2,1)S(1)}, bf16[2,32,512]{2,1,0:T(8,128)(2,1)S(1)}, u32[]{:S(2)}, u32[]{:S(2)}) collective-permute-start(bf16[2,32,512]{2,1,0:T(8,128)(2,1)S(1)} %get-tuple-element.97), channel_id=1, source_target_pairs={{0,10},{1,11},{2,8},{3,9},{4,14},{5,15},{6,12},{7,13},{8,2},{9,3},... | collective-permute-start | bytes 196616 | tf_op jit(solution)/shard_map/ppermute | solution.py:692
  45.8 8.0 %collective-permute-start.18 = (bf16[2,32,512]{2,1,0:T(8,128)(2,1)S(1)}, bf16[2,32,512]{2,1,0:T(8,128)(2,1)S(1)}, u32[]{:S(2)}, u32[]{:S(2)}) collective-permute-start(bf16[2,32,512]{2,1,0:T(8,128)(2,1)S(1)} %get-tuple-element.98), channel_id=1, source_target_pairs={{0,6},{1,7},{2,4},{3,5},{4,2},{5,3},{6,0},{7,1},{8,14},{9,15},{10,... | collective-permute-start | bytes 196616 | tf_op jit(solution)/shard_map/ppermute | solution.py:692
  49.1 6.1 %collective-permute-start.19 = (bf16[2,32,512]{2,1,0:T(8,128)(2,1)S(1)}, bf16[2,32,512]{2,1,0:T(8,128)(2,1)S(1)}, u32[]{:S(2)}, u32[]{:S(2)}) collective-permute-start(bf16[2,32,512]{2,1,0:T(8,128)(2,1)S(1)} %get-tuple-element.99), channel_id=1, source_target_pairs={{0,4},{1,5},{2,6},{3,7},{4,0},{5,1},{6,2},{7,3},{8,12},{9,13},{10,... | collective-permute-start | bytes 196616 | tf_op jit(solution)/shard_map/ppermute | solution.py:692
  49.1 6.6 %collective-permute-start.20 = (bf16[2,32,512]{2,1,0:T(8,128)(2,1)S(1)}, bf16[2,32,512]{2,1,0:T(8,128)(2,1)S(1)}, u32[]{:S(2)}, u32[]{:S(2)}) collective-permute-start(bf16[2,32,512]{2,1,0:T(8,128)(2,1)S(1)} %get-tuple-element.105), channel_id=1, source_target_pairs={{0,8},{1,9},{2,10},{3,11},{4,12},{5,13},{6,14},{7,15},{8,0},{9,1},... | collective-permute-start | bytes 196616 | tf_op jit(solution)/shard_map/ppermute | solution.py:692
  51.6 4.3 %collective-permute-start.21 = (bf16[2,32,512]{2,1,0:T(8,128)(2,1)S(1)}, bf16[2,32,512]{2,1,0:T(8,128)(2,1)S(1)}, u32[]{:S(2)}, u32[]{:S(2)}) collective-permute-start(bf16[2,32,512]{2,1,0:T(8,128)(2,1)S(1)} %get-tuple-element.106), channel_id=1, source_target_pairs={{0,2},{1,3},{2,0},{3,1},{4,6},{5,7},{6,4},{7,5},{8,10},{9,11},{10,... | collective-permute-start | bytes 196616 | tf_op jit(solution)/shard_map/ppermute | solution.py:692
  55.2 1.3 %collective-permute-start.22 = (bf16[2,32,512]{2,1,0:T(8,128)(2,1)S(1)}, bf16[2,32,512]{2,1,0:T(8,128)(2,1)S(1)}, u32[]{:S(2)}, u32[]{:S(2)}) collective-permute-start(bf16[2,32,512]{2,1,0:T(8,128)(2,1)S(1)} %collective-permute-done.14.refs_0_), channel_id=1, source_target_pairs={{0,1},{1,0},{2,3},{3,2},{4,5},{5,4},{6,7},{7,6},{8,9},{9,8},{10,11... | collective-permute-start | bytes 196616 | tf_op jit(solution)/shard_map/ppermute | solution.py:692
  55.2 1.4 %collective-permute-start.23 = (bf16[2,32,512]{2,1,0:T(8,128)(2,1)S(1)}, bf16[2,32,512]{2,1,0:T(8,128)(2,1)S(1)}, u32[]{:S(2)}, u32[]{:S(2)}) collective-permute-start(bf16[2,32,512]{2,1,0:T(8,128)(2,1)S(1)} %collective-permute-done.15.refs_1_), channel_id=1, source_target_pairs={{0,1},{1,0},{2,3},{3,2},{4,5},{5,4},{6,7},{7,6},{8,9},{9,8},{10,11... | collective-permute-start | bytes 196616 | tf_op jit(solution)/shard_map/ppermute | solution.py:692
  (8 other events, 82.8 us)

commit v27 on v23

--- a/solution.py
+++ b/solution.py
@@ -616,7 +616,7 @@
 
 def exchange_plan(row_devices, col_devices):
     devices = row_devices * col_devices
-    crossing = list(range(devices - 2, devices // 2 - 1, -2))
+    crossing = list(range(devices // 2, devices, 2))
     others = list(range(devices // 2 - 2, 0, -2))
     masks = crossing[:-1] + others[:-1] + crossing[-1:] + others[-1:] + [0]
     return masks, 2, 2

time: 57.1 us -> 59.8 us (1.047)
  starting transfers between devices: 33.1 us -> 35.7 us
    ppermute x20, starting transfers between devices: 28.5 us -> 31.1 us  [swap(): lax.ppermute(slab, ('row', 'col'), [(i, i ^ mask) for i in range(devices)])]
  transfers between devices with their start and end apart: 24 -> 24, of which waited for: 5 -> 12; matrix products, arithmetic and copies ran while one was open for 0% -> 0% of each run, Pallas kernels for 15% -> 14%
where the time goes in v27:
time: 59.8 us; the launch traced here: 59.6 us
  starting transfers between devices  35.7 us (60%)
  Pallas kernels  16.6 us (28%)
  waiting for transfers between devices  6.03 us (10%)
  local copies, waits for them, and re-layouts  0.93 us (2%)
    ppermute x20, starting transfers between devices, swap(): lax.ppermute(slab, ('row', 'col'), [(i, i ^ mask) for i in range(devices)])  31.1 us
    ppermute x20, waiting for transfers between devices, swap(): lax.ppermute(slab, ('row', 'col'), [(i, i ^ mask) for i in range(devices)])  6.02 us
    pallas_call x2, Pallas kernels, inner(): pl.pallas_call(functools.partial(inner_kernel, rows=rows, cols=cols, firs...  5.06 us
    ppermute x4, starting transfers between devices, swap_pairs(): return lax.ppermute(edge, axis, pairs + [(b, a) for a, b in pairs])  4.61 us
    pallas_call x1, Pallas kernels, attend(): pl.pallas_call(functools.partial(attend_kernel, plan=plan, sets=sets, cam...  4.02 us
    pallas_call x1, Pallas kernels, expand(): pl.pallas_call(expand_kernel, in_specs=[vmem()] * 2, out_specs=vmem(), ou...  2.31 us
    pallas_call x1, Pallas kernels, rim(): pl.pallas_call(functools.partial(rim_kernel, rows=rows, cols=cols, plan=p...  2.07 us
    pallas_call x1, Pallas kernels, finish(): pl.pallas_call(functools.partial(finish_kernel, plan=plan), in_specs=[pl....  1.72 us
  transfers between devices with their start and end apart: 24, of which 12 were waited for; matrix products, arithmetic and copies ran while one was open for 0% of the time, Pallas kernels for 14%

profile of v27, /device:TPU:0, one launch (start us, length us, event | category | flops | bytes accessed | tf_op | source)
XLA Modules:
  0.0 59.6 jit_solution(10300141553005270476)
XLA Ops:
  0.0 0.9 %slice_bitcast_fusion = (f32[32,512]{1,0:T(8,128)S(1)}, f32[32,512]{1,0:T(8,128)S(1)}) fusion(f32[16,32,512]{2,1,0:T(8,128)} %param.8), kind=kLoop, calls=%fused_computation | loop fusion | bytes 262144 | tf_op jit(solution)/shard_map/squeeze | solution.py:749
  1.1 3.1 %collective-permute-start = (bf16[32,512]{1,0:T(8,128)(2,1)S(1)}, bf16[32,512]{1,0:T(8,128)(2,1)S(1)}, u32[]{:S(2)}, u32[]{:S(2)}) collective-permute-start(bf16[32,512]{1,0:T(8,128)(2,1)S(1)} %get-tuple-element.62), channel_id=1, source_target_pairs={{0,4},{8,12},{4,0},{12,8},{1,5},{9,13},{5,1},{13,9},{2,6},{10,14},... | collective-permute-start | bytes 98312 | tf_op jit(solution)/shard_map/ppermute | solution.py:614
  4.2 0.7 %collective-permute-start.1 = (bf16[32,512]{1,0:T(8,128)(2,1)S(1)}, bf16[32,512]{1,0:T(8,128)(2,1)S(1)}, u32[]{:S(2)}, u32[]{:S(2)}) collective-permute-start(bf16[32,512]{1,0:T(8,128)(2,1)S(1)} %get-tuple-element.63), channel_id=1, source_target_pairs={{4,8},{8,4},{5,9},{9,5},{6,10},{10,6},{7,11},{11,7},{20,24},{24,20... | collective-permute-start | bytes 98312 | tf_op jit(solution)/shard_map/ppermute | solution.py:614
  5.2 2.3 %expand.1.expanded_ref = f32[8448,128]{1,0:T(8,128)S(1)} custom-call(bf16[512,512]{1,0:T(8,128)(2,1)S(1)} %half_norm.1.normed_ref, bf16[512,2048]{1,0:T(8,128)(2,1)S(1)} %copy-done), custom_call_target="tpu_custom_call" | custom-call | flops 10000000000 | bytes 6815744 | tf_op jit(solution)/shard_map/expand/pallas_call | solution.py:189
  7.6 1.2 %inner.2 = (f32[512,512]{1,0:T(8,128)S(1)}, f32[4,96,128]{2,1,0:T(8,128)S(1)}) custom-call(f32[8448,128]{1,0:T(8,128)S(1)} %expand.1.expanded_ref, f32[512,512]{1,0:T(8,128)S(1)} %bitcast.10, f32[3,3,2048]{2,1,0:T(4,128)S(1)} %copy-done.6, bf16[2048,512]{1,0:T(8,128)(2,1)S(1)} %copy-done.1), custom_call_target="tpu_custom_call" | custom-call | flops 4000000000 | bytes 3145728 | tf_op jit(solution)/shard_map/inner/pallas_call | solution.py:279
  9.3 0.8 %collective-permute-start.3 = (bf16[32,512]{1,0:T(8,128)(2,1)S(1)}, bf16[32,512]{1,0:T(8,128)(2,1)S(1)}, u32[]{:S(2)}, u32[]{:S(2)}) collective-permute-start(bf16[32,512]{1,0:T(8,128)(2,1)S(1)} %get-tuple-element.77), channel_id=1, source_target_pairs={{1,2},{2,1},{5,6},{6,5},{9,10},{10,9},{13,14},{14,13},{17,18},{18,... | collective-permute-start | bytes 98312 | tf_op jit(solution)/shard_map/ppermute | solution.py:614
  10.1 3.8 %inner.3 = (f32[512,512]{1,0:T(8,128)S(1)}, f32[12,96,128]{2,1,0:T(8,128)S(1)}) custom-call(f32[8448,128]{1,0:T(8,128)S(1)} %expand.1.expanded_ref, f32[512,512]{1,0:T(8,128)S(1)} %get-tuple-element.67.start_ref, f32[3,3,2048]{2,1,0:T(4,128)S(1)} %copy-done.6, bf16[2048,512]{1,0:T(8,128)(2,1)S(1)} %copy-done.1), custom_call_target="tpu_custom_call" | custom-call | flops 12000000000 | bytes 5242880 | tf_op jit(solution)/shard_map/inner/pallas_call | solution.py:279
  14.0 2.1 %rim.1 = (f32[512,512]{1,0:T(8,128)S(1)}, bf16[2,32,512]{2,1,0:T(8,128)(2,1)S(1)}, bf16[2,32,512]{2,1,0:T(8,128)(2,1)S(1)}, bf16[1,32,512]{2,1,0:T(8,128)(2,1)S(...) custom-call(s32[1]{0:T(128)} %bitcast.own_ref, s32[1]{0:T(128)} %bitcast.2.odd_col_ref, ...), custom_call_target="tpu_custom_call" | custom-call | flops 805306368 | bytes 6815744 | tf_op jit(solution)/shard_map/rim/pallas_call | solution.py:388
  16.0 3.0 %collective-permute-start.6 = (bf16[6,32,512]{2,1,0:T(8,128)(2,1)S(1)}, bf16[6,32,512]{2,1,0:T(8,128)(2,1)S(1)}, u32[]{:S(2)}, u32[]{:S(2)}) collective-permute-start(bf16[6,32,512]{2,1,0:T(8,128)(2,1)S(1)} %get-tuple-element.81), channel_id=1, source_target_pairs={{0,1},{1,0},{2,3},{3,2},{4,5},{5,4},{6,7},{7,6},{8,9},{9,8},{10,11... | collective-permute-start | bytes 589832 | tf_op jit(solution)/shard_map/ppermute | solution.py:692
  19.0 3.8 %collective-permute-start.4 = (bf16[2,32,512]{2,1,0:T(8,128)(2,1)S(1)}, bf16[2,32,512]{2,1,0:T(8,128)(2,1)S(1)}, u32[]{:S(2)}, u32[]{:S(2)}) collective-permute-start(bf16[2,32,512]{2,1,0:T(8,128)(2,1)S(1)} %get-tuple-element.78), channel_id=1, source_target_pairs={{0,8},{1,9},{2,10},{3,11},{4,12},{5,13},{6,14},{7,15},{8,0},{9,1},... | collective-permute-start | bytes 196616 | tf_op jit(solution)/shard_map/ppermute | solution.py:692
  22.9 3.0 %collective-permute-start.7 = (bf16[2,32,512]{2,1,0:T(8,128)(2,1)S(1)}, bf16[2,32,512]{2,1,0:T(8,128)(2,1)S(1)}, u32[]{:S(2)}, u32[]{:S(2)}) collective-permute-start(bf16[2,32,512]{2,1,0:T(8,128)(2,1)S(1)} %get-tuple-element.82), channel_id=1, source_target_pairs={{0,12},{1,13},{2,14},{3,15},{4,8},{5,9},{6,10},{7,11},{8,4},{9,5},... | collective-permute-start | bytes 196616 | tf_op jit(solution)/shard_map/ppermute | solution.py:692
  25.9 1.5 %collective-permute-start.8 = (bf16[2,32,512]{2,1,0:T(8,128)(2,1)S(1)}, bf16[2,32,512]{2,1,0:T(8,128)(2,1)S(1)}, u32[]{:S(2)}, u32[]{:S(2)}) collective-permute-start(bf16[2,32,512]{2,1,0:T(8,128)(2,1)S(1)} %get-tuple-element.83), channel_id=1, source_target_pairs={{0,6},{1,7},{2,4},{3,5},{4,2},{5,3},{6,0},{7,1},{8,14},{9,15},{10,... | collective-permute-start | bytes 196616 | tf_op jit(solution)/shard_map/ppermute | solution.py:692
  27.4 1.4 %collective-permute-start.9 = (bf16[2,32,512]{2,1,0:T(8,128)(2,1)S(1)}, bf16[2,32,512]{2,1,0:T(8,128)(2,1)S(1)}, u32[]{:S(2)}, u32[]{:S(2)}) collective-permute-start(bf16[2,32,512]{2,1,0:T(8,128)(2,1)S(1)} %get-tuple-element.84), channel_id=1, source_target_pairs={{0,4},{1,5},{2,6},{3,7},{4,0},{5,1},{6,2},{7,3},{8,12},{9,13},{10,... | collective-permute-start | bytes 196616 | tf_op jit(solution)/shard_map/ppermute | solution.py:692
  28.8 3.6 %collective-permute-start.10 = (bf16[2,32,512]{2,1,0:T(8,128)(2,1)S(1)}, bf16[2,32,512]{2,1,0:T(8,128)(2,1)S(1)}, u32[]{:S(2)}, u32[]{:S(2)}) collective-permute-start(bf16[2,32,512]{2,1,0:T(8,128)(2,1)S(1)} %get-tuple-element.90), channel_id=1, source_target_pairs={{0,14},{1,15},{2,12},{3,13},{4,10},{5,11},{6,8},{7,9},{8,6},{9,7},... | collective-permute-start | bytes 196616 | tf_op jit(solution)/shard_map/ppermute | solution.py:692
  32.5 1.9 %collective-permute-start.11 = (bf16[2,32,512]{2,1,0:T(8,128)(2,1)S(1)}, bf16[2,32,512]{2,1,0:T(8,128)(2,1)S(1)}, u32[]{:S(2)}, u32[]{:S(2)}) collective-permute-start(bf16[2,32,512]{2,1,0:T(8,128)(2,1)S(1)} %get-tuple-element.91), channel_id=1, source_target_pairs={{0,2},{1,3},{2,0},{3,1},{4,6},{5,7},{6,4},{7,5},{8,10},{9,11},{10,... | collective-permute-start | bytes 196616 | tf_op jit(solution)/shard_map/ppermute | solution.py:692
  34.6 1.0 %collective-permute-done.9.refs_4_ = bf16[2,32,512]{2,1,0:T(8,128)(2,1)S(1)} collective-permute-done((bf16[2,32,512]{2,1,0:T(8,128)(2,1)S(1)}, bf16[2,32,512]{2,1,0:T(8,128)(2,1)S(1)}, u32[]{:S(2)}, u32[]{:S(2)}) %collective-permute-start.9) | collective-permute-done | bytes 65568 | tf_op jit(solution)/shard_map/ppermute | solution.py:692
  37.1 4.0 %attend.1 = (bf16[2,32,512]{2,1,0:T(8,128)(2,1)S(1)}, bf16[2,32,512]{2,1,0:T(8,128)(2,1)S(1)}, bf16[1,32,512]{2,1,0:T(8,128)(2,1)S(1)}, bf16[6,32,512]{2,1,0:T(8,128)(2,1)S(1)}, bf16[5,32,512]{2,1,0:T(8,128)(2,1)S(1)}) custom-call(bf16[2,32,512]{2,1,0:T(8,128)(2,1)S(1)} %collective-permute-done.4.refs_0_, ...), custom_call_target="tpu_custom_call" | custom-call | flops 1073741824 | bytes 2621440 | tf_op jit(solution)/shard_map/attend/pallas_call | solution.py:544
  41.5 3.8 %collective-permute-start.15 = (bf16[2,32,512]{2,1,0:T(8,128)(2,1)S(1)}, bf16[2,32,512]{2,1,0:T(8,128)(2,1)S(1)}, u32[]{:S(2)}, u32[]{:S(2)}) collective-permute-start(bf16[2,32,512]{2,1,0:T(8,128)(2,1)S(1)} %get-tuple-element.94), channel_id=1, source_target_pairs={{0,10},{1,11},{2,8},{3,9},{4,14},{5,15},{6,12},{7,13},{8,2},{9,3},... | collective-permute-start | bytes 196616 | tf_op jit(solution)/shard_map/ppermute | solution.py:692
  45.2 2.0 %collective-permute-start.17 = (bf16[2,32,512]{2,1,0:T(8,128)(2,1)S(1)}, bf16[2,32,512]{2,1,0:T(8,128)(2,1)S(1)}, u32[]{:S(2)}, u32[]{:S(2)}) collective-permute-start(bf16[2,32,512]{2,1,0:T(8,128)(2,1)S(1)} %get-tuple-element.97), channel_id=1, source_target_pairs={{0,12},{1,13},{2,14},{3,15},{4,8},{5,9},{6,10},{7,11},{8,4},{9,5},... | collective-permute-start | bytes 196616 | tf_op jit(solution)/shard_map/ppermute | solution.py:692
  47.3 2.8 %collective-permute-start.19 = (bf16[2,32,512]{2,1,0:T(8,128)(2,1)S(1)}, bf16[2,32,512]{2,1,0:T(8,128)(2,1)S(1)}, u32[]{:S(2)}, u32[]{:S(2)}) collective-permute-start(bf16[2,32,512]{2,1,0:T(8,128)(2,1)S(1)} %get-tuple-element.99), channel_id=1, source_target_pairs={{0,4},{1,5},{2,6},{3,7},{4,0},{5,1},{6,2},{7,3},{8,12},{9,13},{10,... | collective-permute-start | bytes 196616 | tf_op jit(solution)/shard_map/ppermute | solution.py:692
  50.4 1.7 %collective-permute-start.20 = (bf16[2,32,512]{2,1,0:T(8,128)(2,1)S(1)}, bf16[2,32,512]{2,1,0:T(8,128)(2,1)S(1)}, u32[]{:S(2)}, u32[]{:S(2)}) collective-permute-start(bf16[2,32,512]{2,1,0:T(8,128)(2,1)S(1)} %get-tuple-element.105), channel_id=1, source_target_pairs={{0,14},{1,15},{2,12},{3,13},{4,10},{5,11},{6,8},{7,9},{8,6},{9,7},... | collective-permute-start | bytes 196616 | tf_op jit(solution)/shard_map/ppermute | solution.py:692
  52.6 1.3 %collective-permute-start.21 = (bf16[2,32,512]{2,1,0:T(8,128)(2,1)S(1)}, bf16[2,32,512]{2,1,0:T(8,128)(2,1)S(1)}, u32[]{:S(2)}, u32[]{:S(2)}) collective-permute-start(bf16[2,32,512]{2,1,0:T(8,128)(2,1)S(1)} %get-tuple-element.106), channel_id=1, source_target_pairs={{0,2},{1,3},{2,0},{3,1},{4,6},{5,7},{6,4},{7,5},{8,10},{9,11},{10,... | collective-permute-start | bytes 196616 | tf_op jit(solution)/shard_map/ppermute | solution.py:692
  54.0 2.4 %collective-permute-done.19.refs_4_ = bf16[2,32,512]{2,1,0:T(8,128)(2,1)S(1)} collective-permute-done((bf16[2,32,512]{2,1,0:T(8,128)(2,1)S(1)}, bf16[2,32,512]{2,1,0:T(8,128)(2,1)S(1)}, u32[]{:S(2)}, u32[]{:S(2)}) %collective-permute-start.19) | collective-permute-done | bytes 65568 | tf_op jit(solution)/shard_map/ppermute | solution.py:692
  57.9 1.7 %finish.1 = f32[512,512]{1,0:T(8,128)} custom-call(s32[1]{0:T(128)} %bitcast.own_ref, bf16[2,32,512]{2,1,0:T(8,128)(2,1)S(1)} %collective-permute-done.14.refs_0_, bf16[2,32,512]{2,1,0:T(8,128)(2,1)S(1)} %collective-permute-done.15.refs_1_, bf16[2,32,512]{2,1,0:T(8,128)(2,1)S(1)} %collective-permute-done.17.refs_2_, ...), custom_call_target="tpu_custom_call" | custom-call | tf_op jit(solution)/shard_map/finish/pallas_call | solution.py:597
  (53 shorter events, 5.6 us)
Async XLA Ops:
  1.1 7.7 %collective-permute-start = (bf16[32,512]{1,0:T(8,128)(2,1)S(1)}, bf16[32,512]{1,0:T(8,128)(2,1)S(1)}, u32[]{:S(2)}, u32[]{:S(2)}) collective-permute-start(bf16[32,512]{1,0:T(8,128)(2,1)S(1)} %get-tuple-element.62), channel_id=1, source_target_pairs={{0,4},{8,12},{4,0},{12,8},{1,5},{9,13},{5,1},{13,9},{2,6},{10,14},... | collective-permute-start | bytes 98312 | tf_op jit(solution)/shard_map/ppermute | solution.py:614
  4.2 4.6 %collective-permute-start.1 = (bf16[32,512]{1,0:T(8,128)(2,1)S(1)}, bf16[32,512]{1,0:T(8,128)(2,1)S(1)}, u32[]{:S(2)}, u32[]{:S(2)}) collective-permute-start(bf16[32,512]{1,0:T(8,128)(2,1)S(1)} %get-tuple-element.63), channel_id=1, source_target_pairs={{4,8},{8,4},{5,9},{9,5},{6,10},{10,6},{7,11},{11,7},{20,24},{24,20... | collective-permute-start | bytes 98312 | tf_op jit(solution)/shard_map/ppermute | solution.py:614
  9.2 4.7 %collective-permute-start.2 = (bf16[32,512]{1,0:T(8,128)(2,1)S(1)}, bf16[32,512]{1,0:T(8,128)(2,1)S(1)}, u32[]{:S(2)}, u32[]{:S(2)}) collective-permute-start(bf16[32,512]{1,0:T(8,128)(2,1)S(1)} %get-tuple-element.76), channel_id=1, source_target_pairs={{0,1},{2,3},{1,0},{3,2},{4,5},{6,7},{5,4},{7,6},{8,9},{10,11},{9,8... | collective-permute-start | bytes 98312 | tf_op jit(solution)/shard_map/ppermute | solution.py:614
  9.3 4.6 %collective-permute-start.3 = (bf16[32,512]{1,0:T(8,128)(2,1)S(1)}, bf16[32,512]{1,0:T(8,128)(2,1)S(1)}, u32[]{:S(2)}, u32[]{:S(2)}) collective-permute-start(bf16[32,512]{1,0:T(8,128)(2,1)S(1)} %get-tuple-element.77), channel_id=1, source_target_pairs={{1,2},{2,1},{5,6},{6,5},{9,10},{10,9},{13,14},{14,13},{17,18},{18,... | collective-permute-start | bytes 98312 | tf_op jit(solution)/shard_map/ppermute | solution.py:614
  16.0 6.9 %collective-permute-start.6 = (bf16[6,32,512]{2,1,0:T(8,128)(2,1)S(1)}, bf16[6,32,512]{2,1,0:T(8,128)(2,1)S(1)}, u32[]{:S(2)}, u32[]{:S(2)}) collective-permute-start(bf16[6,32,512]{2,1,0:T(8,128)(2,1)S(1)} %get-tuple-element.81), channel_id=1, source_target_pairs={{0,1},{1,0},{2,3},{3,2},{4,5},{5,4},{6,7},{7,6},{8,9},{9,8},{10,11... | collective-permute-start | bytes 589832 | tf_op jit(solution)/shard_map/ppermute | solution.py:692
  19.0 9.8 %collective-permute-start.4 = (bf16[2,32,512]{2,1,0:T(8,128)(2,1)S(1)}, bf16[2,32,512]{2,1,0:T(8,128)(2,1)S(1)}, u32[]{:S(2)}, u32[]{:S(2)}) collective-permute-start(bf16[2,32,512]{2,1,0:T(8,128)(2,1)S(1)} %get-tuple-element.78), channel_id=1, source_target_pairs={{0,8},{1,9},{2,10},{3,11},{4,12},{5,13},{6,14},{7,15},{8,0},{9,1},... | collective-permute-start | bytes 196616 | tf_op jit(solution)/shard_map/ppermute | solution.py:692
  22.8 9.7 %collective-permute-start.5 = (bf16[2,32,512]{2,1,0:T(8,128)(2,1)S(1)}, bf16[2,32,512]{2,1,0:T(8,128)(2,1)S(1)}, u32[]{:S(2)}, u32[]{:S(2)}) collective-permute-start(bf16[2,32,512]{2,1,0:T(8,128)(2,1)S(1)} %get-tuple-element.79), channel_id=1, source_target_pairs={{0,10},{1,11},{2,8},{3,9},{4,14},{5,15},{6,12},{7,13},{8,2},{9,3},... | collective-permute-start | bytes 196616 | tf_op jit(solution)/shard_map/ppermute | solution.py:692
  22.9 11.5 %collective-permute-start.7 = (bf16[2,32,512]{2,1,0:T(8,128)(2,1)S(1)}, bf16[2,32,512]{2,1,0:T(8,128)(2,1)S(1)}, u32[]{:S(2)}, u32[]{:S(2)}) collective-permute-start(bf16[2,32,512]{2,1,0:T(8,128)(2,1)S(1)} %get-tuple-element.82), channel_id=1, source_target_pairs={{0,12},{1,13},{2,14},{3,15},{4,8},{5,9},{6,10},{7,11},{8,4},{9,5},... | collective-permute-start | bytes 196616 | tf_op jit(solution)/shard_map/ppermute | solution.py:692
  25.9 8.7 %collective-permute-start.8 = (bf16[2,32,512]{2,1,0:T(8,128)(2,1)S(1)}, bf16[2,32,512]{2,1,0:T(8,128)(2,1)S(1)}, u32[]{:S(2)}, u32[]{:S(2)}) collective-permute-start(bf16[2,32,512]{2,1,0:T(8,128)(2,1)S(1)} %get-tuple-element.83), channel_id=1, source_target_pairs={{0,6},{1,7},{2,4},{3,5},{4,2},{5,3},{6,0},{7,1},{8,14},{9,15},{10,... | collective-permute-start | bytes 196616 | tf_op jit(solution)/shard_map/ppermute | solution.py:692
  27.4 8.2 %collective-permute-start.9 = (bf16[2,32,512]{2,1,0:T(8,128)(2,1)S(1)}, bf16[2,32,512]{2,1,0:T(8,128)(2,1)S(1)}, u32[]{:S(2)}, u32[]{:S(2)}) collective-permute-start(bf16[2,32,512]{2,1,0:T(8,128)(2,1)S(1)} %get-tuple-element.84), channel_id=1, source_target_pairs={{0,4},{1,5},{2,6},{3,7},{4,0},{5,1},{6,2},{7,3},{8,12},{9,13},{10,... | collective-permute-start | bytes 196616 | tf_op jit(solution)/shard_map/ppermute | solution.py:692
  28.8 7.9 %collective-permute-start.10 = (bf16[2,32,512]{2,1,0:T(8,128)(2,1)S(1)}, bf16[2,32,512]{2,1,0:T(8,128)(2,1)S(1)}, u32[]{:S(2)}, u32[]{:S(2)}) collective-permute-start(bf16[2,32,512]{2,1,0:T(8,128)(2,1)S(1)} %get-tuple-element.90), channel_id=1, source_target_pairs={{0,14},{1,15},{2,12},{3,13},{4,10},{5,11},{6,8},{7,9},{8,6},{9,7},... | collective-permute-start | bytes 196616 | tf_op jit(solution)/shard_map/ppermute | solution.py:692
  32.5 4.6 %collective-permute-start.11 = (bf16[2,32,512]{2,1,0:T(8,128)(2,1)S(1)}, bf16[2,32,512]{2,1,0:T(8,128)(2,1)S(1)}, u32[]{:S(2)}, u32[]{:S(2)}) collective-permute-start(bf16[2,32,512]{2,1,0:T(8,128)(2,1)S(1)} %get-tuple-element.91), channel_id=1, source_target_pairs={{0,2},{1,3},{2,0},{3,1},{4,6},{5,7},{6,4},{7,5},{8,10},{9,11},{10,... | collective-permute-start | bytes 196616 | tf_op jit(solution)/shard_map/ppermute | solution.py:692
  35.6 1.5 %collective-permute-start.12 = (bf16[2,32,512]{2,1,0:T(8,128)(2,1)S(1)}, bf16[2,32,512]{2,1,0:T(8,128)(2,1)S(1)}, u32[]{:S(2)}, u32[]{:S(2)}) collective-permute-start(bf16[2,32,512]{2,1,0:T(8,128)(2,1)S(1)} %collective-permute-done.4.refs_0_), channel_id=1, source_target_pairs={{0,1},{1,0},{2,3},{3,2},{4,5},{5,4},{6,7},{7,6},{8,9},{9,8},{10,11... | collective-permute-start | bytes 196616 | tf_op jit(solution)/shard_map/ppermute | solution.py:692
  35.6 1.5 %collective-permute-start.13 = (bf16[2,32,512]{2,1,0:T(8,128)(2,1)S(1)}, bf16[2,32,512]{2,1,0:T(8,128)(2,1)S(1)}, u32[]{:S(2)}, u32[]{:S(2)}) collective-permute-start(bf16[2,32,512]{2,1,0:T(8,128)(2,1)S(1)} %collective-permute-done.5.refs_1_), channel_id=1, source_target_pairs={{0,1},{1,0},{2,3},{3,2},{4,5},{5,4},{6,7},{7,6},{8,9},{9,8},{10,11... | collective-permute-start | bytes 196616 | tf_op jit(solution)/shard_map/ppermute | solution.py:692
  41.2 4.1 %collective-permute-start.16 = (bf16[6,32,512]{2,1,0:T(8,128)(2,1)S(1)}, bf16[6,32,512]{2,1,0:T(8,128)(2,1)S(1)}, u32[]{:S(2)}, u32[]{:S(2)}) collective-permute-start(bf16[6,32,512]{2,1,0:T(8,128)(2,1)S(1)} %get-tuple-element.96), channel_id=1, source_target_pairs={{0,1},{1,0},{2,3},{3,2},{4,5},{5,4},{6,7},{7,6},{8,9},{9,8},{10,11... | collective-permute-start | bytes 589832 | tf_op jit(solution)/shard_map/ppermute | solution.py:692
  41.5 8.9 %collective-permute-start.14 = (bf16[2,32,512]{2,1,0:T(8,128)(2,1)S(1)}, bf16[2,32,512]{2,1,0:T(8,128)(2,1)S(1)}, u32[]{:S(2)}, u32[]{:S(2)}) collective-permute-start(bf16[2,32,512]{2,1,0:T(8,128)(2,1)S(1)} %get-tuple-element.93), channel_id=1, source_target_pairs={{0,8},{1,9},{2,10},{3,11},{4,12},{5,13},{6,14},{7,15},{8,0},{9,1},... | collective-permute-start | bytes 196616 | tf_op jit(solution)/shard_map/ppermute | solution.py:692
  41.5 11.2 %collective-permute-start.15 = (bf16[2,32,512]{2,1,0:T(8,128)(2,1)S(1)}, bf16[2,32,512]{2,1,0:T(8,128)(2,1)S(1)}, u32[]{:S(2)}, u32[]{:S(2)}) collective-permute-start(bf16[2,32,512]{2,1,0:T(8,128)(2,1)S(1)} %get-tuple-element.94), channel_id=1, source_target_pairs={{0,10},{1,11},{2,8},{3,9},{4,14},{5,15},{6,12},{7,13},{8,2},{9,3},... | collective-permute-start | bytes 196616 | tf_op jit(solution)/shard_map/ppermute | solution.py:692
  45.2 8.7 %collective-permute-start.17 = (bf16[2,32,512]{2,1,0:T(8,128)(2,1)S(1)}, bf16[2,32,512]{2,1,0:T(8,128)(2,1)S(1)}, u32[]{:S(2)}, u32[]{:S(2)}) collective-permute-start(bf16[2,32,512]{2,1,0:T(8,128)(2,1)S(1)} %get-tuple-element.97), channel_id=1, source_target_pairs={{0,12},{1,13},{2,14},{3,15},{4,8},{5,9},{6,10},{7,11},{8,4},{9,5},... | collective-permute-start | bytes 196616 | tf_op jit(solution)/shard_map/ppermute | solution.py:692
  47.3 6.8 %collective-permute-start.18 = (bf16[2,32,512]{2,1,0:T(8,128)(2,1)S(1)}, bf16[2,32,512]{2,1,0:T(8,128)(2,1)S(1)}, u32[]{:S(2)}, u32[]{:S(2)}) collective-permute-start(bf16[2,32,512]{2,1,0:T(8,128)(2,1)S(1)} %get-tuple-element.98), channel_id=1, source_target_pairs={{0,6},{1,7},{2,4},{3,5},{4,2},{5,3},{6,0},{7,1},{8,14},{9,15},{10,... | collective-permute-start | bytes 196616 | tf_op jit(solution)/shard_map/ppermute | solution.py:692
  47.3 9.2 %collective-permute-start.19 = (bf16[2,32,512]{2,1,0:T(8,128)(2,1)S(1)}, bf16[2,32,512]{2,1,0:T(8,128)(2,1)S(1)}, u32[]{:S(2)}, u32[]{:S(2)}) collective-permute-start(bf16[2,32,512]{2,1,0:T(8,128)(2,1)S(1)} %get-tuple-element.99), channel_id=1, source_target_pairs={{0,4},{1,5},{2,6},{3,7},{4,0},{5,1},{6,2},{7,3},{8,12},{9,13},{10,... | collective-permute-start | bytes 196616 | tf_op jit(solution)/shard_map/ppermute | solution.py:692
  50.4 7.1 %collective-permute-start.20 = (bf16[2,32,512]{2,1,0:T(8,128)(2,1)S(1)}, bf16[2,32,512]{2,1,0:T(8,128)(2,1)S(1)}, u32[]{:S(2)}, u32[]{:S(2)}) collective-permute-start(bf16[2,32,512]{2,1,0:T(8,128)(2,1)S(1)} %get-tuple-element.105), channel_id=1, source_target_pairs={{0,14},{1,15},{2,12},{3,13},{4,10},{5,11},{6,8},{7,9},{8,6},{9,7},... | collective-permute-start | bytes 196616 | tf_op jit(solution)/shard_map/ppermute | solution.py:692
  52.6 5.0 %collective-permute-start.21 = (bf16[2,32,512]{2,1,0:T(8,128)(2,1)S(1)}, bf16[2,32,512]{2,1,0:T(8,128)(2,1)S(1)}, u32[]{:S(2)}, u32[]{:S(2)}) collective-permute-start(bf16[2,32,512]{2,1,0:T(8,128)(2,1)S(1)} %get-tuple-element.106), channel_id=1, source_target_pairs={{0,2},{1,3},{2,0},{3,1},{4,6},{5,7},{6,4},{7,5},{8,10},{9,11},{10,... | collective-permute-start | bytes 196616 | tf_op jit(solution)/shard_map/ppermute | solution.py:692
  56.5 1.3 %collective-permute-start.22 = (bf16[2,32,512]{2,1,0:T(8,128)(2,1)S(1)}, bf16[2,32,512]{2,1,0:T(8,128)(2,1)S(1)}, u32[]{:S(2)}, u32[]{:S(2)}) collective-permute-start(bf16[2,32,512]{2,1,0:T(8,128)(2,1)S(1)} %collective-permute-done.14.refs_0_), channel_id=1, source_target_pairs={{0,1},{1,0},{2,3},{3,2},{4,5},{5,4},{6,7},{7,6},{8,9},{9,8},{10,11... | collective-permute-start | bytes 196616 | tf_op jit(solution)/shard_map/ppermute | solution.py:692
  56.5 1.4 %collective-permute-start.23 = (bf16[2,32,512]{2,1,0:T(8,128)(2,1)S(1)}, bf16[2,32,512]{2,1,0:T(8,128)(2,1)S(1)}, u32[]{:S(2)}, u32[]{:S(2)}) collective-permute-start(bf16[2,32,512]{2,1,0:T(8,128)(2,1)S(1)} %collective-permute-done.15.refs_1_), channel_id=1, source_target_pairs={{0,1},{1,0},{2,3},{3,2},{4,5},{5,4},{6,7},{7,6},{8,9},{9,8},{10,11... | collective-permute-start | bytes 196616 | tf_op jit(solution)/shard_map/ppermute | solution.py:692
  (8 other events, 81.9 us)

commit v28 on v23

--- a/solution.py
+++ b/solution.py
@@ -754,7 +754,7 @@
     expanded = expand(normed, w_expand)
     tile = divisor(w_expand.shape[1] // 2, 256, LANES)
     count = w_expand.shape[1] // tile
-    early = 2
+    early = count // 4 * 2
     total, rim_one = inner(
         expanded, flat, depth_kernel, w_project, rows, cols, 0, early, tile
     )

time: 57.1 us -> 57.4 us (level)
  transfers between devices with their start and end apart: 24 -> 24, of which waited for: 5 -> 6; matrix products, arithmetic and copies ran while one was open for 0% -> 0% of each run, Pallas kernels for 15% -> 14%
where the time goes in v28:
time: 57.4 us; the launch traced here: 57.2 us
  starting transfers between devices  33.3 us (58%)
  Pallas kernels  16.6 us (29%)
  waiting for transfers between devices  5.92 us (10%)
  local copies, waits for them, and re-layouts  0.93 us (2%)
    ppermute x20, starting transfers between devices, swap(): lax.ppermute(slab, ('row', 'col'), [(i, i ^ mask) for i in range(devices)])  28.5 us
    ppermute x20, waiting for transfers between devices, swap(): lax.ppermute(slab, ('row', 'col'), [(i, i ^ mask) for i in range(devices)])  5.91 us
    pallas_call x2, Pallas kernels, inner(): pl.pallas_call(functools.partial(inner_kernel, rows=rows, cols=cols, firs...  5.03 us
    ppermute x4, starting transfers between devices, swap_pairs(): return lax.ppermute(edge, axis, pairs + [(b, a) for a, b in pairs])  4.79 us
    pallas_call x1, Pallas kernels, attend(): pl.pallas_call(functools.partial(attend_kernel, plan=plan, sets=sets, cam...  4.02 us
    pallas_call x1, Pallas kernels, expand(): pl.pallas_call(expand_kernel, in_specs=[vmem()] * 2, out_specs=vmem(), ou...  2.31 us
    pallas_call x1, Pallas kernels, rim(): pl.pallas_call(functools.partial(rim_kernel, rows=rows, cols=cols, plan=p...  2.09 us
    pallas_call x1, Pallas kernels, finish(): pl.pallas_call(functools.partial(finish_kernel, plan=plan), in_specs=[pl....  1.72 us
  transfers between devices with their start and end apart: 24, of which 6 were waited for; matrix products, arithmetic and copies ran while one was open for 0% of the time, Pallas kernels for 14%

profile of v28, /device:TPU:0, one launch (start us, length us, event | category | flops | bytes accessed | tf_op | source)
XLA Modules:
  0.0 57.2 jit_solution(14839405303733515983)
XLA Ops:
  0.0 0.9 %slice_bitcast_fusion = (f32[32,512]{1,0:T(8,128)S(1)}, f32[32,512]{1,0:T(8,128)S(1)}) fusion(f32[16,32,512]{2,1,0:T(8,128)} %param.8), kind=kLoop, calls=%fused_computation | loop fusion | bytes 262144 | tf_op jit(solution)/shard_map/squeeze | solution.py:749
  1.1 3.1 %collective-permute-start = (bf16[32,512]{1,0:T(8,128)(2,1)S(1)}, bf16[32,512]{1,0:T(8,128)(2,1)S(1)}, u32[]{:S(2)}, u32[]{:S(2)}) collective-permute-start(bf16[32,512]{1,0:T(8,128)(2,1)S(1)} %get-tuple-element.62), channel_id=1, source_target_pairs={{0,4},{8,12},{4,0},{12,8},{1,5},{9,13},{5,1},{13,9},{2,6},{10,14},... | collective-permute-start | bytes 98312 | tf_op jit(solution)/shard_map/ppermute | solution.py:614
  5.2 2.3 %expand.1.expanded_ref = f32[8448,128]{1,0:T(8,128)S(1)} custom-call(bf16[512,512]{1,0:T(8,128)(2,1)S(1)} %half_norm.1.normed_ref, bf16[512,2048]{1,0:T(8,128)(2,1)S(1)} %copy-done), custom_call_target="tpu_custom_call" | custom-call | flops 10000000000 | bytes 6815744 | tf_op jit(solution)/shard_map/expand/pallas_call | solution.py:189
  7.6 2.5 %inner.2 = (f32[512,512]{1,0:T(8,128)S(1)}, f32[8,96,128]{2,1,0:T(8,128)S(1)}) custom-call(f32[8448,128]{1,0:T(8,128)S(1)} %expand.1.expanded_ref, f32[512,512]{1,0:T(8,128)S(1)} %bitcast.10, f32[3,3,2048]{2,1,0:T(4,128)S(1)} %copy-done.6, bf16[2048,512]{1,0:T(8,128)(2,1)S(1)} %copy-done.1), custom_call_target="tpu_custom_call" | custom-call | flops 8000000000 | bytes 4194304 | tf_op jit(solution)/shard_map/inner/pallas_call | solution.py:279
  10.6 1.0 %collective-permute-start.3 = (bf16[32,512]{1,0:T(8,128)(2,1)S(1)}, bf16[32,512]{1,0:T(8,128)(2,1)S(1)}, u32[]{:S(2)}, u32[]{:S(2)}) collective-permute-start(bf16[32,512]{1,0:T(8,128)(2,1)S(1)} %get-tuple-element.77), channel_id=1, source_target_pairs={{1,2},{2,1},{5,6},{6,5},{9,10},{10,9},{13,14},{14,13},{17,18},{18,... | collective-permute-start | bytes 98312 | tf_op jit(solution)/shard_map/ppermute | solution.py:614
  11.6 2.5 %inner.3 = (f32[512,512]{1,0:T(8,128)S(1)}, f32[8,96,128]{2,1,0:T(8,128)S(1)}) custom-call(f32[8448,128]{1,0:T(8,128)S(1)} %expand.1.expanded_ref, f32[512,512]{1,0:T(8,128)S(1)} %get-tuple-element.67.start_ref, f32[3,3,2048]{2,1,0:T(4,128)S(1)} %copy-done.6, bf16[2048,512]{1,0:T(8,128)(2,1)S(1)} %copy-done.1), custom_call_target="tpu_custom_call" | custom-call | flops 8000000000 | bytes 4194304 | tf_op jit(solution)/shard_map/inner/pallas_call | solution.py:279
  14.1 2.1 %rim.1 = (f32[512,512]{1,0:T(8,128)S(1)}, bf16[2,32,512]{2,1,0:T(8,128)(2,1)S(1)}, bf16[2,32,512]{2,1,0:T(8,128)(2,1)S(1)}, bf16[1,32,512]{2,1,0:T(8,128)(2,1)S(...) custom-call(s32[1]{0:T(128)} %bitcast.own_ref, s32[1]{0:T(128)} %bitcast.2.odd_col_ref, ...), custom_call_target="tpu_custom_call" | custom-call | flops 805306368 | bytes 6815744 | tf_op jit(solution)/shard_map/rim/pallas_call | solution.py:388
  16.2 2.9 %collective-permute-start.6 = (bf16[6,32,512]{2,1,0:T(8,128)(2,1)S(1)}, bf16[6,32,512]{2,1,0:T(8,128)(2,1)S(1)}, u32[]{:S(2)}, u32[]{:S(2)}) collective-permute-start(bf16[6,32,512]{2,1,0:T(8,128)(2,1)S(1)} %get-tuple-element.81), channel_id=1, source_target_pairs={{0,1},{1,0},{2,3},{3,2},{4,5},{5,4},{6,7},{7,6},{8,9},{9,8},{10,11... | collective-permute-start | bytes 589832 | tf_op jit(solution)/shard_map/ppermute | solution.py:692
  19.1 2.7 %collective-permute-start.4 = (bf16[2,32,512]{2,1,0:T(8,128)(2,1)S(1)}, bf16[2,32,512]{2,1,0:T(8,128)(2,1)S(1)}, u32[]{:S(2)}, u32[]{:S(2)}) collective-permute-start(bf16[2,32,512]{2,1,0:T(8,128)(2,1)S(1)} %get-tuple-element.78), channel_id=1, source_target_pairs={{0,14},{1,15},{2,12},{3,13},{4,10},{5,11},{6,8},{7,9},{8,6},{9,7},... | collective-permute-start | bytes 196616 | tf_op jit(solution)/shard_map/ppermute | solution.py:692
  21.8 1.2 %collective-permute-start.5 = (bf16[2,32,512]{2,1,0:T(8,128)(2,1)S(1)}, bf16[2,32,512]{2,1,0:T(8,128)(2,1)S(1)}, u32[]{:S(2)}, u32[]{:S(2)}) collective-permute-start(bf16[2,32,512]{2,1,0:T(8,128)(2,1)S(1)} %get-tuple-element.79), channel_id=1, source_target_pairs={{0,12},{1,13},{2,14},{3,15},{4,8},{5,9},{6,10},{7,11},{8,4},{9,5},... | collective-permute-start | bytes 196616 | tf_op jit(solution)/shard_map/ppermute | solution.py:692
  23.0 3.0 %collective-permute-start.7 = (bf16[2,32,512]{2,1,0:T(8,128)(2,1)S(1)}, bf16[2,32,512]{2,1,0:T(8,128)(2,1)S(1)}, u32[]{:S(2)}, u32[]{:S(2)}) collective-permute-start(bf16[2,32,512]{2,1,0:T(8,128)(2,1)S(1)} %get-tuple-element.82), channel_id=1, source_target_pairs={{0,10},{1,11},{2,8},{3,9},{4,14},{5,15},{6,12},{7,13},{8,2},{9,3},... | collective-permute-start | bytes 196616 | tf_op jit(solution)/shard_map/ppermute | solution.py:692
  26.0 1.2 %collective-permute-start.8 = (bf16[2,32,512]{2,1,0:T(8,128)(2,1)S(1)}, bf16[2,32,512]{2,1,0:T(8,128)(2,1)S(1)}, u32[]{:S(2)}, u32[]{:S(2)}) collective-permute-start(bf16[2,32,512]{2,1,0:T(8,128)(2,1)S(1)} %get-tuple-element.83), channel_id=1, source_target_pairs={{0,6},{1,7},{2,4},{3,5},{4,2},{5,3},{6,0},{7,1},{8,14},{9,15},{10,... | collective-permute-start | bytes 196616 | tf_op jit(solution)/shard_map/ppermute | solution.py:692
  28.0 4.6 %collective-permute-start.10 = (bf16[2,32,512]{2,1,0:T(8,128)(2,1)S(1)}, bf16[2,32,512]{2,1,0:T(8,128)(2,1)S(1)}, u32[]{:S(2)}, u32[]{:S(2)}) collective-permute-start(bf16[2,32,512]{2,1,0:T(8,128)(2,1)S(1)} %get-tuple-element.90), channel_id=1, source_target_pairs={{0,8},{1,9},{2,10},{3,11},{4,12},{5,13},{6,14},{7,15},{8,0},{9,1},... | collective-permute-start | bytes 196616 | tf_op jit(solution)/shard_map/ppermute | solution.py:692
  33.0 1.7 %collective-permute-done.7.refs_0_.refs_1_.refs_2_.refs_5_.refs_6_.refs_8_.refs_9_ = bf16[2,32,512]{2,1,0:T(8,128)(2,1)S(1)} collective-permute-done((bf16[2,32,512]{2,1,0:T(8,128)(2,1)S(1)}, bf16[2,32,512]{2,1,0:T(8,128)(2,1)S(1)}, u32[]{:S(2)}, u32[]{:S(2)}) %collective-permute-start.7) | collective-permute-done | bytes 65568 | tf_op jit(solution)/shard_map/ppermute | solution.py:692
  35.9 1.1 %collective-permute-done.11.refs_6_ = bf16[2,32,512]{2,1,0:T(8,128)(2,1)S(1)} collective-permute-done((bf16[2,32,512]{2,1,0:T(8,128)(2,1)S(1)}, bf16[2,32,512]{2,1,0:T(8,128)(2,1)S(1)}, u32[]{:S(2)}, u32[]{:S(2)}) %collective-permute-start.11) | collective-permute-done | bytes 65568 | tf_op jit(solution)/shard_map/ppermute | solution.py:692
  36.9 4.0 %attend.1 = (bf16[2,32,512]{2,1,0:T(8,128)(2,1)S(1)}, bf16[2,32,512]{2,1,0:T(8,128)(2,1)S(1)}, bf16[1,32,512]{2,1,0:T(8,128)(2,1)S(1)}, bf16[6,32,512]{2,1,0:T(8,128)(2,1)S(1)}, bf16[5,32,512]{2,1,0:T(8,128)(2,1)S(1)}) custom-call(bf16[2,32,512]{2,1,0:T(8,128)(2,1)S(1)} %collective-permute-done.4.refs_0_, ...), custom_call_target="tpu_custom_call" | custom-call | flops 1073741824 | bytes 2621440 | tf_op jit(solution)/shard_map/attend/pallas_call | solution.py:544
  41.0 1.8 %collective-permute-start.14 = (bf16[2,32,512]{2,1,0:T(8,128)(2,1)S(1)}, bf16[2,32,512]{2,1,0:T(8,128)(2,1)S(1)}, u32[]{:S(2)}, u32[]{:S(2)}) collective-permute-start(bf16[2,32,512]{2,1,0:T(8,128)(2,1)S(1)} %get-tuple-element.93), channel_id=1, source_target_pairs={{0,14},{1,15},{2,12},{3,13},{4,10},{5,11},{6,8},{7,9},{8,6},{9,7},... | collective-permute-start | bytes 196616 | tf_op jit(solution)/shard_map/ppermute | solution.py:692
  42.8 1.9 %collective-permute-start.15 = (bf16[2,32,512]{2,1,0:T(8,128)(2,1)S(1)}, bf16[2,32,512]{2,1,0:T(8,128)(2,1)S(1)}, u32[]{:S(2)}, u32[]{:S(2)}) collective-permute-start(bf16[2,32,512]{2,1,0:T(8,128)(2,1)S(1)} %get-tuple-element.94), channel_id=1, source_target_pairs={{0,12},{1,13},{2,14},{3,15},{4,8},{5,9},{6,10},{7,11},{8,4},{9,5},... | collective-permute-start | bytes 196616 | tf_op jit(solution)/shard_map/ppermute | solution.py:692
  45.0 3.2 %collective-permute-start.18 = (bf16[2,32,512]{2,1,0:T(8,128)(2,1)S(1)}, bf16[2,32,512]{2,1,0:T(8,128)(2,1)S(1)}, u32[]{:S(2)}, u32[]{:S(2)}) collective-permute-start(bf16[2,32,512]{2,1,0:T(8,128)(2,1)S(1)} %get-tuple-element.98), channel_id=1, source_target_pairs={{0,6},{1,7},{2,4},{3,5},{4,2},{5,3},{6,0},{7,1},{8,14},{9,15},{10,... | collective-permute-start | bytes 196616 | tf_op jit(solution)/shard_map/ppermute | solution.py:692
  48.8 1.9 %collective-permute-start.20 = (bf16[2,32,512]{2,1,0:T(8,128)(2,1)S(1)}, bf16[2,32,512]{2,1,0:T(8,128)(2,1)S(1)}, u32[]{:S(2)}, u32[]{:S(2)}) collective-permute-start(bf16[2,32,512]{2,1,0:T(8,128)(2,1)S(1)} %get-tuple-element.105), channel_id=1, source_target_pairs={{0,8},{1,9},{2,10},{3,11},{4,12},{5,13},{6,14},{7,15},{8,0},{9,1},... | collective-permute-start | bytes 196616 | tf_op jit(solution)/shard_map/ppermute | solution.py:692
  50.6 1.7 %collective-permute-start.21 = (bf16[2,32,512]{2,1,0:T(8,128)(2,1)S(1)}, bf16[2,32,512]{2,1,0:T(8,128)(2,1)S(1)}, u32[]{:S(2)}, u32[]{:S(2)}) collective-permute-start(bf16[2,32,512]{2,1,0:T(8,128)(2,1)S(1)} %get-tuple-element.106), channel_id=1, source_target_pairs={{0,2},{1,3},{2,0},{3,1},{4,6},{5,7},{6,4},{7,5},{8,10},{9,11},{10,... | collective-permute-start | bytes 196616 | tf_op jit(solution)/shard_map/ppermute | solution.py:692
  52.3 1.0 %collective-permute-done.17.refs_2_ = bf16[2,32,512]{2,1,0:T(8,128)(2,1)S(1)} collective-permute-done((bf16[2,32,512]{2,1,0:T(8,128)(2,1)S(1)}, bf16[2,32,512]{2,1,0:T(8,128)(2,1)S(1)}, u32[]{:S(2)}, u32[]{:S(2)}) %collective-permute-start.17) | collective-permute-done | bytes 65568 | tf_op jit(solution)/shard_map/ppermute | solution.py:692
  54.0 1.3 %collective-permute-done.20.refs_5_ = bf16[2,32,512]{2,1,0:T(8,128)(2,1)S(1)} collective-permute-done((bf16[2,32,512]{2,1,0:T(8,128)(2,1)S(1)}, bf16[2,32,512]{2,1,0:T(8,128)(2,1)S(1)}, u32[]{:S(2)}, u32[]{:S(2)}) %collective-permute-start.20) | collective-permute-done | bytes 65568 | tf_op jit(solution)/shard_map/ppermute | solution.py:692
  55.4 1.7 %finish.1 = f32[512,512]{1,0:T(8,128)} custom-call(s32[1]{0:T(128)} %bitcast.own_ref, bf16[2,32,512]{2,1,0:T(8,128)(2,1)S(1)} %collective-permute-done.14.refs_0_, bf16[2,32,512]{2,1,0:T(8,128)(2,1)S(1)} %collective-permute-done.15.refs_1_, bf16[2,32,512]{2,1,0:T(8,128)(2,1)S(1)} %collective-permute-done.17.refs_2_, ...), custom_call_target="tpu_custom_call" | custom-call | tf_op jit(solution)/shard_map/finish/pallas_call | solution.py:597
  (53 shorter events, 5.6 us)
Async XLA Ops:
  1.1 9.0 %collective-permute-start = (bf16[32,512]{1,0:T(8,128)(2,1)S(1)}, bf16[32,512]{1,0:T(8,128)(2,1)S(1)}, u32[]{:S(2)}, u32[]{:S(2)}) collective-permute-start(bf16[32,512]{1,0:T(8,128)(2,1)S(1)} %get-tuple-element.62), channel_id=1, source_target_pairs={{0,4},{8,12},{4,0},{12,8},{1,5},{9,13},{5,1},{13,9},{2,6},{10,14},... | collective-permute-start | bytes 98312 | tf_op jit(solution)/shard_map/ppermute | solution.py:614
  4.2 5.9 %collective-permute-start.1 = (bf16[32,512]{1,0:T(8,128)(2,1)S(1)}, bf16[32,512]{1,0:T(8,128)(2,1)S(1)}, u32[]{:S(2)}, u32[]{:S(2)}) collective-permute-start(bf16[32,512]{1,0:T(8,128)(2,1)S(1)} %get-tuple-element.63), channel_id=1, source_target_pairs={{4,8},{8,4},{5,9},{9,5},{6,10},{10,6},{7,11},{11,7},{20,24},{24,20... | collective-permute-start | bytes 98312 | tf_op jit(solution)/shard_map/ppermute | solution.py:614
  10.5 3.6 %collective-permute-start.2 = (bf16[32,512]{1,0:T(8,128)(2,1)S(1)}, bf16[32,512]{1,0:T(8,128)(2,1)S(1)}, u32[]{:S(2)}, u32[]{:S(2)}) collective-permute-start(bf16[32,512]{1,0:T(8,128)(2,1)S(1)} %get-tuple-element.76), channel_id=1, source_target_pairs={{0,1},{2,3},{1,0},{3,2},{4,5},{6,7},{5,4},{7,6},{8,9},{10,11},{9,8... | collective-permute-start | bytes 98312 | tf_op jit(solution)/shard_map/ppermute | solution.py:614
  10.6 3.5 %collective-permute-start.3 = (bf16[32,512]{1,0:T(8,128)(2,1)S(1)}, bf16[32,512]{1,0:T(8,128)(2,1)S(1)}, u32[]{:S(2)}, u32[]{:S(2)}) collective-permute-start(bf16[32,512]{1,0:T(8,128)(2,1)S(1)} %get-tuple-element.77), channel_id=1, source_target_pairs={{1,2},{2,1},{5,6},{6,5},{9,10},{10,9},{13,14},{14,13},{17,18},{18,... | collective-permute-start | bytes 98312 | tf_op jit(solution)/shard_map/ppermute | solution.py:614
  16.2 6.8 %collective-permute-start.6 = (bf16[6,32,512]{2,1,0:T(8,128)(2,1)S(1)}, bf16[6,32,512]{2,1,0:T(8,128)(2,1)S(1)}, u32[]{:S(2)}, u32[]{:S(2)}) collective-permute-start(bf16[6,32,512]{2,1,0:T(8,128)(2,1)S(1)} %get-tuple-element.81), channel_id=1, source_target_pairs={{0,1},{1,0},{2,3},{3,2},{4,5},{5,4},{6,7},{7,6},{8,9},{9,8},{10,11... | collective-permute-start | bytes 589832 | tf_op jit(solution)/shard_map/ppermute | solution.py:692
  19.1 8.9 %collective-permute-start.4 = (bf16[2,32,512]{2,1,0:T(8,128)(2,1)S(1)}, bf16[2,32,512]{2,1,0:T(8,128)(2,1)S(1)}, u32[]{:S(2)}, u32[]{:S(2)}) collective-permute-start(bf16[2,32,512]{2,1,0:T(8,128)(2,1)S(1)} %get-tuple-element.78), channel_id=1, source_target_pairs={{0,14},{1,15},{2,12},{3,13},{4,10},{5,11},{6,8},{7,9},{8,6},{9,7},... | collective-permute-start | bytes 196616 | tf_op jit(solution)/shard_map/ppermute | solution.py:692
  21.8 10.8 %collective-permute-start.5 = (bf16[2,32,512]{2,1,0:T(8,128)(2,1)S(1)}, bf16[2,32,512]{2,1,0:T(8,128)(2,1)S(1)}, u32[]{:S(2)}, u32[]{:S(2)}) collective-permute-start(bf16[2,32,512]{2,1,0:T(8,128)(2,1)S(1)} %get-tuple-element.79), channel_id=1, source_target_pairs={{0,12},{1,13},{2,14},{3,15},{4,8},{5,9},{6,10},{7,11},{8,4},{9,5},... | collective-permute-start | bytes 196616 | tf_op jit(solution)/shard_map/ppermute | solution.py:692
  23.0 11.7 %collective-permute-start.7 = (bf16[2,32,512]{2,1,0:T(8,128)(2,1)S(1)}, bf16[2,32,512]{2,1,0:T(8,128)(2,1)S(1)}, u32[]{:S(2)}, u32[]{:S(2)}) collective-permute-start(bf16[2,32,512]{2,1,0:T(8,128)(2,1)S(1)} %get-tuple-element.82), channel_id=1, source_target_pairs={{0,10},{1,11},{2,8},{3,9},{4,14},{5,15},{6,12},{7,13},{8,2},{9,3},... | collective-permute-start | bytes 196616 | tf_op jit(solution)/shard_map/ppermute | solution.py:692
  26.0 8.7 %collective-permute-start.8 = (bf16[2,32,512]{2,1,0:T(8,128)(2,1)S(1)}, bf16[2,32,512]{2,1,0:T(8,128)(2,1)S(1)}, u32[]{:S(2)}, u32[]{:S(2)}) collective-permute-start(bf16[2,32,512]{2,1,0:T(8,128)(2,1)S(1)} %get-tuple-element.83), channel_id=1, source_target_pairs={{0,6},{1,7},{2,4},{3,5},{4,2},{5,3},{6,0},{7,1},{8,14},{9,15},{10,... | collective-permute-start | bytes 196616 | tf_op jit(solution)/shard_map/ppermute | solution.py:692
  27.2 7.5 %collective-permute-start.9 = (bf16[2,32,512]{2,1,0:T(8,128)(2,1)S(1)}, bf16[2,32,512]{2,1,0:T(8,128)(2,1)S(1)}, u32[]{:S(2)}, u32[]{:S(2)}) collective-permute-start(bf16[2,32,512]{2,1,0:T(8,128)(2,1)S(1)} %get-tuple-element.84), channel_id=1, source_target_pairs={{0,4},{1,5},{2,6},{3,7},{4,0},{5,1},{6,2},{7,3},{8,12},{9,13},{10,... | collective-permute-start | bytes 196616 | tf_op jit(solution)/shard_map/ppermute | solution.py:692
  28.0 7.8 %collective-permute-start.10 = (bf16[2,32,512]{2,1,0:T(8,128)(2,1)S(1)}, bf16[2,32,512]{2,1,0:T(8,128)(2,1)S(1)}, u32[]{:S(2)}, u32[]{:S(2)}) collective-permute-start(bf16[2,32,512]{2,1,0:T(8,128)(2,1)S(1)} %get-tuple-element.90), channel_id=1, source_target_pairs={{0,8},{1,9},{2,10},{3,11},{4,12},{5,13},{6,14},{7,15},{8,0},{9,1},... | collective-permute-start | bytes 196616 | tf_op jit(solution)/shard_map/ppermute | solution.py:692
  32.6 4.3 %collective-permute-start.11 = (bf16[2,32,512]{2,1,0:T(8,128)(2,1)S(1)}, bf16[2,32,512]{2,1,0:T(8,128)(2,1)S(1)}, u32[]{:S(2)}, u32[]{:S(2)}) collective-permute-start(bf16[2,32,512]{2,1,0:T(8,128)(2,1)S(1)} %get-tuple-element.91), channel_id=1, source_target_pairs={{0,2},{1,3},{2,0},{3,1},{4,6},{5,7},{6,4},{7,5},{8,10},{9,11},{10,... | collective-permute-start | bytes 196616 | tf_op jit(solution)/shard_map/ppermute | solution.py:692
  34.7 2.2 %collective-permute-start.12 = (bf16[2,32,512]{2,1,0:T(8,128)(2,1)S(1)}, bf16[2,32,512]{2,1,0:T(8,128)(2,1)S(1)}, u32[]{:S(2)}, u32[]{:S(2)}) collective-permute-start(bf16[2,32,512]{2,1,0:T(8,128)(2,1)S(1)} %collective-permute-done.4.refs_0_), channel_id=1, source_target_pairs={{0,1},{1,0},{2,3},{3,2},{4,5},{5,4},{6,7},{7,6},{8,9},{9,8},{10,11... | collective-permute-start | bytes 196616 | tf_op jit(solution)/shard_map/ppermute | solution.py:692
  34.7 2.2 %collective-permute-start.13 = (bf16[2,32,512]{2,1,0:T(8,128)(2,1)S(1)}, bf16[2,32,512]{2,1,0:T(8,128)(2,1)S(1)}, u32[]{:S(2)}, u32[]{:S(2)}) collective-permute-start(bf16[2,32,512]{2,1,0:T(8,128)(2,1)S(1)} %collective-permute-done.5.refs_1_), channel_id=1, source_target_pairs={{0,1},{1,0},{2,3},{3,2},{4,5},{5,4},{6,7},{7,6},{8,9},{9,8},{10,11... | collective-permute-start | bytes 196616 | tf_op jit(solution)/shard_map/ppermute | solution.py:692
  40.9 3.7 %collective-permute-start.16 = (bf16[6,32,512]{2,1,0:T(8,128)(2,1)S(1)}, bf16[6,32,512]{2,1,0:T(8,128)(2,1)S(1)}, u32[]{:S(2)}, u32[]{:S(2)}) collective-permute-start(bf16[6,32,512]{2,1,0:T(8,128)(2,1)S(1)} %get-tuple-element.96), channel_id=1, source_target_pairs={{0,1},{1,0},{2,3},{3,2},{4,5},{5,4},{6,7},{7,6},{8,9},{9,8},{10,11... | collective-permute-start | bytes 589832 | tf_op jit(solution)/shard_map/ppermute | solution.py:692
  41.0 7.7 %collective-permute-start.14 = (bf16[2,32,512]{2,1,0:T(8,128)(2,1)S(1)}, bf16[2,32,512]{2,1,0:T(8,128)(2,1)S(1)}, u32[]{:S(2)}, u32[]{:S(2)}) collective-permute-start(bf16[2,32,512]{2,1,0:T(8,128)(2,1)S(1)} %get-tuple-element.93), channel_id=1, source_target_pairs={{0,14},{1,15},{2,12},{3,13},{4,10},{5,11},{6,8},{7,9},{8,6},{9,7},... | collective-permute-start | bytes 196616 | tf_op jit(solution)/shard_map/ppermute | solution.py:692
  42.8 7.9 %collective-permute-start.15 = (bf16[2,32,512]{2,1,0:T(8,128)(2,1)S(1)}, bf16[2,32,512]{2,1,0:T(8,128)(2,1)S(1)}, u32[]{:S(2)}, u32[]{:S(2)}) collective-permute-start(bf16[2,32,512]{2,1,0:T(8,128)(2,1)S(1)} %get-tuple-element.94), channel_id=1, source_target_pairs={{0,12},{1,13},{2,14},{3,15},{4,8},{5,9},{6,10},{7,11},{8,4},{9,5},... | collective-permute-start | bytes 196616 | tf_op jit(solution)/shard_map/ppermute | solution.py:692
  44.7 8.6 %collective-permute-start.17 = (bf16[2,32,512]{2,1,0:T(8,128)(2,1)S(1)}, bf16[2,32,512]{2,1,0:T(8,128)(2,1)S(1)}, u32[]{:S(2)}, u32[]{:S(2)}) collective-permute-start(bf16[2,32,512]{2,1,0:T(8,128)(2,1)S(1)} %get-tuple-element.97), channel_id=1, source_target_pairs={{0,10},{1,11},{2,8},{3,9},{4,14},{5,15},{6,12},{7,13},{8,2},{9,3},... | collective-permute-start | bytes 196616 | tf_op jit(solution)/shard_map/ppermute | solution.py:692
  45.0 8.3 %collective-permute-start.18 = (bf16[2,32,512]{2,1,0:T(8,128)(2,1)S(1)}, bf16[2,32,512]{2,1,0:T(8,128)(2,1)S(1)}, u32[]{:S(2)}, u32[]{:S(2)}) collective-permute-start(bf16[2,32,512]{2,1,0:T(8,128)(2,1)S(1)} %get-tuple-element.98), channel_id=1, source_target_pairs={{0,6},{1,7},{2,4},{3,5},{4,2},{5,3},{6,0},{7,1},{8,14},{9,15},{10,... | collective-permute-start | bytes 196616 | tf_op jit(solution)/shard_map/ppermute | solution.py:692
  48.2 5.3 %collective-permute-start.19 = (bf16[2,32,512]{2,1,0:T(8,128)(2,1)S(1)}, bf16[2,32,512]{2,1,0:T(8,128)(2,1)S(1)}, u32[]{:S(2)}, u32[]{:S(2)}) collective-permute-start(bf16[2,32,512]{2,1,0:T(8,128)(2,1)S(1)} %get-tuple-element.99), channel_id=1, source_target_pairs={{0,4},{1,5},{2,6},{3,7},{4,0},{5,1},{6,2},{7,3},{8,12},{9,13},{10,... | collective-permute-start | bytes 196616 | tf_op jit(solution)/shard_map/ppermute | solution.py:692
  48.8 6.6 %collective-permute-start.20 = (bf16[2,32,512]{2,1,0:T(8,128)(2,1)S(1)}, bf16[2,32,512]{2,1,0:T(8,128)(2,1)S(1)}, u32[]{:S(2)}, u32[]{:S(2)}) collective-permute-start(bf16[2,32,512]{2,1,0:T(8,128)(2,1)S(1)} %get-tuple-element.105), channel_id=1, source_target_pairs={{0,8},{1,9},{2,10},{3,11},{4,12},{5,13},{6,14},{7,15},{8,0},{9,1},... | collective-permute-start | bytes 196616 | tf_op jit(solution)/shard_map/ppermute | solution.py:692
  50.6 4.7 %collective-permute-start.21 = (bf16[2,32,512]{2,1,0:T(8,128)(2,1)S(1)}, bf16[2,32,512]{2,1,0:T(8,128)(2,1)S(1)}, u32[]{:S(2)}, u32[]{:S(2)}) collective-permute-start(bf16[2,32,512]{2,1,0:T(8,128)(2,1)S(1)} %get-tuple-element.106), channel_id=1, source_target_pairs={{0,2},{1,3},{2,0},{3,1},{4,6},{5,7},{6,4},{7,5},{8,10},{9,11},{10,... | collective-permute-start | bytes 196616 | tf_op jit(solution)/shard_map/ppermute | solution.py:692
  53.5 1.8 %collective-permute-start.22 = (bf16[2,32,512]{2,1,0:T(8,128)(2,1)S(1)}, bf16[2,32,512]{2,1,0:T(8,128)(2,1)S(1)}, u32[]{:S(2)}, u32[]{:S(2)}) collective-permute-start(bf16[2,32,512]{2,1,0:T(8,128)(2,1)S(1)} %collective-permute-done.14.refs_0_), channel_id=1, source_target_pairs={{0,1},{1,0},{2,3},{3,2},{4,5},{5,4},{6,7},{7,6},{8,9},{9,8},{10,11... | collective-permute-start | bytes 196616 | tf_op jit(solution)/shard_map/ppermute | solution.py:692
  53.5 1.8 %collective-permute-start.23 = (bf16[2,32,512]{2,1,0:T(8,128)(2,1)S(1)}, bf16[2,32,512]{2,1,0:T(8,128)(2,1)S(1)}, u32[]{:S(2)}, u32[]{:S(2)}) collective-permute-start(bf16[2,32,512]{2,1,0:T(8,128)(2,1)S(1)} %collective-permute-done.15.refs_1_), channel_id=1, source_target_pairs={{0,1},{1,0},{2,3},{3,2},{4,5},{5,4},{6,7},{7,6},{8,9},{9,8},{10,11... | collective-permute-start | bytes 196616 | tf_op jit(solution)/shard_map/ppermute | solution.py:692
  (8 other events, 76.5 us)
